TPU v7x, 32 devices: a whole 2x2x4 slice. The times are simulated.
32 devices in a mesh: grp: 4 (over z), voc: 8 (over y, x, core).
Axes of the slice: x: 2, y: 2, z: 4, core: 2. Of those that a mesh axis runs over, the one named last changes fastest.
Arguments:
- hidden_states: bfloat16 [4096, 8192], P('grp', 'voc'), may hold values from -6 to 6
- target_logits: float32 [4096, 16384], P('grp', 'voc'), may hold values from -12 to 240
- labels: int32 [4096, 8], P('grp'), may hold values from 0 to 2047
- down_weight: bfloat16 [8192, 256], P('voc'), may hold values from -0.0625 to 0.0625
- up_weight: bfloat16 [256, 8192], P(None, 'grp'), may hold values from -0.75 to 0.75
- head_weight: bfloat16 [8192, 16384], P('grp', 'voc'), may hold values from -0.0625 to 0.0625
Outputs:
- frame_loss: float32 [8, 4, 1024], P('voc', 'grp')
- grad_a: float32 [8192, 256], P('voc')
- grad_b: float32 [256, 8192], P(None, 'grp')
All inputs are finite; a program needn't handle non-finite values.
Results may differ from a plain program's by a relative error of at most 0.0046.
Values may be sent and summed in bfloat16 or wider, within the bound.
No kernel may reach another device: no remote copies, remote signals or barrier semaphores. Data moves between devices by JAX's collectives and lax.ppermute only.
A program may use at most 64 MiB of HBM per device.

v0:
```python
import jax
import jax.numpy as jnp
from jax import lax
from jax.sharding import PartitionSpec as P

HEAD = 2


LAM = 0.1


def passed_along(block, axis, distance):
    devices = range(lax.axis_size(axis))
    route = [(i - distance, i) for i in devices if i - distance in devices]
    return lax.ppermute(block, axis, route)


def partner(value, axis, bit):
    mask = 2**bit
    pairs = [(source, source ^ mask) for source in range(lax.axis_size(axis))]
    return lax.ppermute(value, axis, pairs)


def as_sent(array):

    def short(part):
        return part.astype(jnp.bfloat16) if part.dtype == jnp.float32 else part

    return jax.tree.map(short, array)


def silu_slope(values):
    sigma = jax.nn.sigmoid(values)
    return sigma * (1.0 + values * (1.0 - sigma))


def log_normalize(values):
    top_value = jnp.max(values, -1, keepdims=True)
    return values - top_value - jnp.log(jnp.sum(jnp.exp(values - top_value), -1, keepdims=True))


def inner_rows(left, right):
    return lax.dot_general(
        left, right, (((0,), (0,)), ((), ())), preferred_element_type=jnp.float32
    )


def inner_cols(left, right):
    return lax.dot_general(
        left, right, (((1,), (1,)), ((), ())), preferred_element_type=jnp.float32
    )


def regroup(blocks, bit_total, swapper):
    position = lax.axis_index("voc")
    for bit_number in range(bit_total):
        leading = blocks.shape[:-3]
        slot_count = blocks.shape[-3]
        lower_count = 1 << bit_number
        upper_count = slot_count // (2 * lower_count)
        viewed = blocks.reshape(leading + (upper_count, 2, lower_count) + blocks.shape[-2:])
        bit_axis = len(leading) + 1
        own_bit = position // lower_count % 2
        zero_half = lax.index_in_dim(viewed, 0, bit_axis, keepdims=False)
        one_half = lax.index_in_dim(viewed, 1, bit_axis, keepdims=False)
        kept = jnp.where(own_bit == 0, zero_half, one_half)
        outgoing = jnp.where(own_bit == 0, one_half, zero_half)
        arrived = swapper(outgoing, bit_number)
        low_half = jnp.where(own_bit == 0, kept, arrived)
        high_half = jnp.where(own_bit == 0, arrived, kept)
        blocks = jnp.stack((low_half, high_half), bit_axis).reshape(blocks.shape)
    return blocks


def on_device(hidden_states, target_logits, labels, down_weight, up_weight, head_weight):
    row_count, slice_cols = target_logits.shape
    book_count = labels.shape[1]
    group_count = lax.axis_size("grp")
    per_book = lax.axis_size("voc") // book_count
    bit_total = per_book.bit_length() - 1
    book_width = slice_cols * per_book
    block_rows = row_count // per_book
    position = lax.axis_index("voc")
    book_index = position // per_book
    book_part = position % per_book
    pre_act = lax.psum(
        jnp.dot(hidden_states, down_weight, preferred_element_type=jnp.float32), "voc"
    )
    activation = jax.nn.silu(pre_act).astype(jnp.bfloat16)
    vocab_proj = lax.psum(
        jnp.dot(up_weight, head_weight, preferred_element_type=jnp.float32), "grp"
    ).astype(jnp.bfloat16)
    draft_logits = target_logits + jnp.dot(
        activation, vocab_proj, preferred_element_type=jnp.float32
    )
    incoming = passed_along(target_logits[:HEAD], "grp", -1)
    shifted = jnp.concatenate((target_logits[HEAD:], incoming), 0)
    frame_index = lax.axis_index("grp") * row_count + jnp.arange(row_count)
    live_mask = (frame_index < row_count * group_count - HEAD).astype(jnp.float32)
    paired = jnp.stack((shifted, draft_logits)).reshape(2, per_book, block_rows, slice_cols)
    regrouped = regroup(
        paired, bit_total, lambda piece_data, bit_number: partner(piece_data, "voc", bit_number)
    )
    regrouped = regrouped.transpose(0, 2, 1, 3).reshape(2, block_rows, book_width)
    log_target = log_normalize(regrouped[0])
    log_draft = log_normalize(regrouped[1])
    block_start = book_part * block_rows
    label_ids = lax.dynamic_slice(labels, (block_start, book_index), (block_rows, 1))[:, 0]
    live_rows = lax.dynamic_slice_in_dim(live_mask, block_start, block_rows)
    onehot = (jnp.arange(book_width)[None, :] == label_ids[:, None]).astype(jnp.float32)
    target_prob = jnp.exp(log_target)
    draft_prob = jnp.exp(log_draft)
    divergence = jnp.sum(target_prob * (log_target - log_draft), -1)
    picked = jnp.sum(onehot * log_draft, -1)
    frame_loss = (live_rows * divergence - LAM * picked).reshape(1, 1, block_rows)
    block_grad = (
        live_rows[:, None] * (draft_prob - target_prob) + LAM * (draft_prob - onehot)
    ).astype(jnp.bfloat16)
    returned = block_grad.reshape(block_rows, per_book, slice_cols).transpose(1, 0, 2)
    returned = regroup(
        returned,
        bit_total,
        lambda piece_data, bit_number: jax.tree.map(
            lambda part, own: part.astype(own.dtype),
            partner(as_sent(piece_data), "voc", bit_number),
            piece_data,
        ),
    )
    logit_grad = returned.reshape(row_count, slice_cols)
    act_part = inner_cols(logit_grad, vocab_proj)
    proj_grad = lax.psum(inner_rows(activation, logit_grad), "grp").astype(jnp.bfloat16)
    up_part = inner_cols(proj_grad, head_weight)
    act_grad = lax.psum(act_part, "voc")
    grad_b = lax.psum(up_part, "voc")
    pre_grad = (act_grad * silu_slope(pre_act)).astype(jnp.bfloat16)
    grad_a = lax.psum(inner_rows(hidden_states, pre_grad), "grp")
    return (frame_loss, grad_a, grad_b)


def solution(mesh):
    in_specs = (
        P("grp", "voc"),
        P("grp", "voc"),
        P("grp", None),
        P("voc", None),
        P(None, "grp"),
        P("grp", "voc"),
    )
    out_specs = (P("voc", "grp", None), P("voc", None), P(None, "grp"))
    return jax.shard_map(
        on_device, mesh=mesh, in_specs=in_specs, out_specs=out_specs, check_vma=False
    )
```

profile of v0, /device:TPU:0, one launch (start us, length us, event | category | flops | bytes accessed | tf_op | source)
XLA Modules:
  0.0 349.8 jit_solution(416178141001011604)
XLA Ops:
  7.2 0.0 copy-start
  7.2 0.0 all-reduce.7.cloned.1.call-start
  7.2 1.0 slice.7
  8.2 1.3 collective-permute-start
  9.5 0.0 copy-done
  9.5 2.7 fusion.12
  12.2 0.0 all-reduce.7.cloned.1.call-update
  12.3 0.0 all-reduce.11.cloned.1.call-start
  12.3 7.4 %fusion.13 = f32[256,2048]{1,0:T(8,128)} fusion(bf16[256,2048]{1,0:T(8,128)(2,1)} %param.10, bf16[2048,2048]{1,0:T(8,128)(2,1)} %param.11), kind=kOutput, calls=%fused_computation.30 | convolution fusion | flops 2147483648 | bytes 11534336 | tf_op jit(solution)/shard_map/dot_general | solution.py:91
  19.7 80.5 %all-reduce.12 = bf16[256,2048]{1,0:T(8,128)(2,1)S(1)} all-reduce(f32[256,2048]{1,0:T(8,128)} %fusion.13), channel_id=1, replica_groups=mesh['grp'=4,'voc'=8] {'grp'}, use_global_device_ids=true, to_apply=%region_3.4 | all-reduce | flops 524288 | bytes 3145728 | tf_op jit(solution)/shard_map/psum | solution.py:90
  100.3 0.8 constant_dynamic-slice_fusion
  101.0 4.3 %slice.6 = f32[1022,2048]{1,0:T(8,128)S(1)} slice(f32[1024,2048]{1,0:T(8,128)} %param.7), slice={[2:1024], [0:2048]} | slice | bytes 16744448 | tf_op jit(solution)/shard_map/slice | solution.py:97
  105.4 0.0 copy-start.1
  105.4 0.0 collective-permute-done
  105.4 0.5 fusion
  105.9 3.5 exponential_reduce_fusion.1
  109.3 0.0 copy-done.1
  109.3 0.0 all-reduce.7.cloned.1.call-done
  109.4 5.1 %fusion.11 = (f32[1024]{0:T(1024)S(1)}, f32[1024,2048]{1,0:T(8,128)S(1)}) fusion(f32[1024,2048]{1,0:T(8,128)} %param.7, bf16[256,2048]{1,0:T(8,128)(2,1)S(1)} %all-reduce.12, f32[1024,256]{1,0:T(8,128)} %all-reduce.7.cloned.1.call-done), kind=kOutput, calls=%fused_computation.28 | convolution fusion | flops 1079245824 | bytes 18878464 | tf_op jit(solution)/shard_map/dot_general | solution.py:93
  114.5 0.0 copy-start.2
  114.5 1.3 exponential_reduce_fusion
  115.8 2.1 copy-done.2
  117.9 0.0 copy-start.3
  117.9 9.2 %multiply_reduce_fusion = (f32[1024]{0:T(1024)S(1)}, f32[1024]{0:T(1024)S(1)}, bf16[1024,2048]{1,0:T(8,128)(2,1)S(1)}) fusion(f32[1024,2048]{1,0:T(8,128)S(1)} %get-tuple-element.12, f32[1024]{0:T(1024)S(1)} %log.17, f32[1024]{0:T(1024)S(1)} %get-tuple-element.11, f32[1024]{0:T(1024)S(1)} %log.16, f32[1024]{0:T(1024)S(1)} %fusion, ...), kind=kLoop, calls=%fused_computation.4 | loop fusion | flops 37746688 | bytes 21004288 | tf_op jit(solution)/shard_map/reduce_sum | solution.py:113
  127.1 2.3 fusion.15
  129.4 0.0 copy-done.3
  129.4 2.6 fusion.10
  132.0 72.9 %all-reduce.13 = bf16[256,2048]{1,0:T(8,128)(2,1)} all-reduce(f32[256,2048]{1,0:T(8,128)} %fusion.10), channel_id=1, replica_groups=mesh['grp'=4,'voc'=8] {'grp'}, use_global_device_ids=true, to_apply=%region_10.11 | all-reduce | flops 524288 | bytes 3145728 | tf_op jit(solution)/shard_map/psum | solution.py:131
  204.9 0.0 copy-start.4
  204.9 7.5 %fusion.14 = f32[256,2048]{1,0:T(8,128)} fusion(bf16[256,2048]{1,0:T(8,128)(2,1)} %all-reduce.13, bf16[2048,2048]{1,0:T(8,128)(2,1)} %param.11), kind=kOutput, calls=%fused_computation.31 | convolution fusion | flops 2147483648 | bytes 11534336 | tf_op jit(solution)/shard_map/dot_general | solution.py:49
  212.4 0.0 all-reduce.11.cloned.1.call-update
  212.4 0.0 all-reduce.9.cloned.1.call-start
  212.5 70.1 %all-reduce.11.cloned.1.call-done = (f32[1024,256]{1,0:T(8,128)}, f32[256,2048]{1,0:T(8,128)}) async-done(((f32[1024,256]{1,0:T(8,128)}, f32[256,2048]{1,0:T(8,128)}), (f32[1024,256]{1,0:T(8,128)}, f32[256,2048]{1,0:T(8,128)})) %all-reduce.11.cloned.1.call-update) | async-done | bytes 3145744 | tf_op jit(solution)/shard_map/psum | solution.py:133
  282.6 0.0 copy-done.4
  282.6 3.0 convolution_bitcast_fusion
  285.6 0.0 all-reduce.9.cloned.1.call-update
  285.6 0.6 fusion.7
  286.2 51.4 %all-reduce.9.cloned.1.call-done = f32[1024,256]{0,1:T(8,128)} async-done(((f32[1024,256]{0,1:T(8,128)}), f32[1024,256]{0,1:T(8,128)}) %all-reduce.9.cloned.1.call-update) | async-done | bytes 1048592 | tf_op jit(solution)/shard_map/psum | solution.py:136
  337.6 2.5 copy.9
  340.2 3.1 copy.18
  (4 shorter events, 0.0 us)
Async XLA Ops:
  7.2 2.3 copy-start
  7.2 102.2 %all-reduce.7.cloned.1.call-start = ((), (), s32[]{:S(2)}) async-start(), calls=%async_computation | async-start | bytes 2097152 | tf_op jit(solution)/shard_map/psum | solution.py:86
  8.2 97.2 %collective-permute-start = (f32[2,2048]{1,0:T(2,128)S(1)}, f32[2,2048]{1,0:T(2,128)S(1)}, u32[]{:S(2)}, u32[]{:S(2)}) collective-permute-start(f32[2,2048]{1,0:T(2,128)S(1)} %slice.7), channel_id=1, source_target_pairs={{8,0},{16,8},{24,16},{9,1},{17,9},{25,17},{10,2},{18,10},{26,18},{... | collective-permute-start | bytes 49160 | tf_op jit(solution)/shard_map/ppermute | solution.py:15
  12.3 270.3 %all-reduce.11.cloned.1.call-start = ((), (), s32[]{:S(2)}) async-start(), calls=%async_computation.2 | async-start | bytes 6291456 | tf_op jit(solution)/shard_map/psum | solution.py:133
  105.4 3.9 %copy-start.1 = (f32[1022,2048]{1,0:T(8,128)}, f32[1022,2048]{1,0:T(8,128)S(1)}, u32[]{:S(2)}) copy-start(f32[1022,2048]{1,0:T(8,128)S(1)} %slice.6) | copy-start | bytes 25116676
  114.5 3.4 copy-start.2
  117.9 11.5 %copy-start.3 = (f32[1024,256]{1,0:T(8,128)S(1)}, f32[1024,256]{1,0:T(8,128)}, u32[]{:S(2)}) copy-start(f32[1024,256]{1,0:T(8,128)} %all-reduce.7.cloned.1.call-done) | copy-start | bytes 3145732
  204.9 77.6 %copy-start.4 = (f32[1024,256]{1,0:T(8,128)S(1)}, f32[1024,256]{1,0:T(8,128)}, u32[]{:S(2)}) copy-start(f32[1024,256]{1,0:T(8,128)} %all-reduce.7.cloned.1.call-done) | copy-start | bytes 3145732
  212.4 125.2 %all-reduce.9.cloned.1.call-start = ((), (), s32[]{:S(2)}) async-start(), calls=%async_computation.1 | async-start | bytes 2097152 | tf_op jit(solution)/shard_map/psum | solution.py:136
Sparse Core Ops, SparseCore 0:
  12.4 60.3 all-reduce.6
  212.5 69.9 all-reduce.10
  285.7 51.8 all-reduce.8
where the time goes:
time: 350 us
  blocking collectives  153 us (44%)
  waiting for transfers between devices  122 us (35%)
  matrix products  30.7 us (9%)
  other arithmetic  14.9 us (4%)
  local copies, waits for them, and re-layouts  13.9 us (4%)
  between operations  13.9 us (4%)
    psum x1, blocking collectives, on_device(): lax.psum(jnp.dot(up_weight, head_weight, preferred_element_type=jnp.float...  80.5 us
    psum x1, blocking collectives, on_device(): lax.psum(inner_rows(activation, logit_grad), 'grp').astype(jnp.bfloat16)  72.9 us
    psum x1, waiting for transfers between devices, on_device(): act_grad = lax.psum(act_part, 'voc')  70.1 us
    psum x1, waiting for transfers between devices, on_device(): grad_a = lax.psum(inner_rows(hidden_states, pre_grad), 'grp')  51.4 us
    dot_general x2, matrix products, inner_cols(): lax.dot_general(left, right, (((1,), (1,)), ((), ())), preferred_element_...  9.77 us
    reduce_sum x1, other arithmetic, on_device(): divergence = jnp.sum(target_prob * (log_target - log_draft), -1)  9.16 us
    unnamed x12, local copies, waits for them, and re-layouts  7.79 us
    dot_general x1, matrix products, on_device(): jnp.dot(up_weight, head_weight, preferred_element_type=jnp.float32)  7.37 us
  transfers between devices with their start and end apart: 4, of which 2 were waited for; matrix products, arithmetic and copies ran while one was open for 6% of the time, Pallas kernels for 0%

commit v1 on v0

v1 whole, which is shorter than its diff:
```python
import jax
import jax.numpy as jnp
from jax import lax
from jax.sharding import PartitionSpec as P

HEAD = 2
LAM = 0.1
CHUNKS = 4


def swap(value, axis, bit):
    mask = 1 << bit
    pairs = [(i, i ^ mask) for i in range(lax.axis_size(axis))]
    return lax.ppermute(value, axis, pairs)


def own_bit(axis, bit):
    return (lax.axis_index(axis) >> bit) & 1


def half(value, which):
    rows = value.shape[0] // 2
    return lax.dynamic_slice_in_dim(value, which * rows, rows, 0)


def reduce_bits(part, axis, bits, wire):
    for bit in bits[:-1]:
        mine = own_bit(axis, bit)
        arrived = swap(half(part, 1 - mine).astype(wire), axis, bit)
        part = half(part, mine) + arrived.astype(jnp.float32)
    sent = part.astype(wire)
    return sent.astype(jnp.float32) + swap(sent, axis, bits[-1]).astype(jnp.float32)


def gather_bits(piece, axis, bits):
    for bit in reversed(bits[:-1]):
        mine = own_bit(axis, bit)
        other = swap(piece, axis, bit)
        low = jnp.where(mine == 0, piece, other)
        high = jnp.where(mine == 0, other, piece)
        piece = jnp.concatenate((low, high), 0)
    return piece


def owned_rows(value, axis, bits):
    for bit in bits[:-1]:
        value = half(value, own_bit(axis, bit))
    return value


def bit_orders(axis):
    count = lax.axis_size(axis).bit_length() - 1
    first = list(range(count))
    return [first, first[:1] + first[:0:-1]]


def silu_slope(values):
    sigma = jax.nn.sigmoid(values)
    return sigma * (1.0 + values * (1.0 - sigma))


def inner_rows(left, right):
    return lax.dot_general(
        left, right, (((0,), (0,)), ((), ())), preferred_element_type=jnp.float32
    )


def inner_cols(left, right):
    return lax.dot_general(
        left, right, (((1,), (1,)), ((), ())), preferred_element_type=jnp.float32
    )


def over_books(values, combine, per_book):
    bit = 0
    while (1 << bit) < per_book:
        values = combine(values, jax.tree.map(lambda v: swap(v, "voc", bit), values))
        bit += 1
    return values


def on_device(hidden_states, target_logits, labels, down_weight, up_weight, head_weight):
    row_count, slice_cols = target_logits.shape
    book_count = labels.shape[1]
    group_count = lax.axis_size("grp")
    per_book = lax.axis_size("voc") // book_count
    block_rows = row_count // per_book
    position = lax.axis_index("voc")
    book_index = position // per_book
    book_part = position % per_book
    width = slice_cols // CHUNKS
    z_bits = list(range(group_count.bit_length() - 1))
    orders = bit_orders("voc")

    devices = range(group_count)
    incoming = lax.ppermute(
        target_logits[:HEAD], "grp", [(i + 1, i) for i in devices if i + 1 in devices]
    )

    vocab_parts = [
        jnp.dot(
            up_weight,
            head_weight[:, c * width : (c + 1) * width],
            preferred_element_type=jnp.float32,
        )
        for c in range(CHUNKS)
    ]
    pre_part = jnp.dot(hidden_states, down_weight, preferred_element_type=jnp.float32)
    halves = (pre_part[: row_count // 2], pre_part[row_count // 2 :])
    pre_act = [reduce_bits(p, "voc", o, jnp.float32) for p, o in zip(halves, orders)]
    acts = jnp.concatenate(
        [
            gather_bits(jax.nn.silu(p).astype(jnp.bfloat16), "voc", o)
            for p, o in zip(pre_act, orders)
        ],
        0,
    )
    vocab_proj = [
        gather_bits(
            reduce_bits(p, "grp", z_bits, jnp.float16).astype(jnp.bfloat16), "grp", z_bits
        )
        for p in vocab_parts
    ]

    draft = jnp.concatenate(
        [
            target_logits[:, c * width : (c + 1) * width]
            + jnp.dot(acts, vocab_proj[c], preferred_element_type=jnp.float32)
            for c in range(CHUNKS)
        ],
        1,
    )
    shifted = jnp.concatenate((target_logits[HEAD:], incoming), 0)
    frame_index = lax.axis_index("grp") * row_count + jnp.arange(row_count)
    live = (frame_index < row_count * group_count - HEAD).astype(jnp.float32)

    def log_sum(values):
        def merge(a, b):
            top = jnp.maximum(a[0], b[0])
            return top, a[1] * jnp.exp(a[0] - top) + b[1] * jnp.exp(b[0] - top)

        top = jnp.max(values, -1, keepdims=True)
        total = jnp.sum(jnp.exp(values - top), -1, keepdims=True)
        top, total = over_books((top, total), merge, per_book)
        return top + jnp.log(total)

    log_target = shifted - log_sum(shifted)
    log_draft = draft - log_sum(draft)
    label_ids = lax.dynamic_slice_in_dim(labels, book_index, 1, 1)
    columns = book_part * slice_cols + jnp.arange(slice_cols)
    onehot = (columns[None, :] == label_ids).astype(jnp.float32)
    target_prob = jnp.exp(log_target)
    draft_prob = jnp.exp(log_draft)
    divergence = jnp.sum(target_prob * (log_target - log_draft), -1)
    picked = jnp.sum(onehot * log_draft, -1)
    loss = over_books(live * divergence - LAM * picked, jnp.add, per_book)
    frame_loss = lax.dynamic_slice_in_dim(loss, book_part * block_rows, block_rows)
    frame_loss = frame_loss.reshape(1, 1, block_rows)
    logit_grad = (
        live[:, None] * (draft_prob - target_prob) + LAM * (draft_prob - onehot)
    ).astype(jnp.bfloat16)

    proj_parts = [
        inner_rows(acts, logit_grad[:, c * width : (c + 1) * width]) for c in range(CHUNKS)
    ]
    act_part = inner_cols(logit_grad, jnp.concatenate(vocab_proj, 1))
    halves = (act_part[: row_count // 2], act_part[row_count // 2 :])
    pre_grad = jnp.concatenate(
        [
            gather_bits(
                (reduce_bits(p, "voc", o, jnp.float32) * silu_slope(a)).astype(jnp.bfloat16),
                "voc",
                o,
            )
            for p, o, a in zip(halves, orders, pre_act)
        ],
        0,
    )
    proj_grad = [
        gather_bits(
            reduce_bits(p, "grp", z_bits, jnp.float16).astype(jnp.bfloat16), "grp", z_bits
        )
        for p in proj_parts
    ]
    up_part = sum(
        inner_cols(proj_grad[c], head_weight[:, c * width : (c + 1) * width])
        for c in range(CHUNKS)
    )
    down_part = inner_rows(hidden_states, pre_grad)

    def finish(part, axis, bits):
        total = reduce_bits(part, axis, bits, jnp.float16)
        return gather_bits(total.astype(jnp.float16), axis, bits).astype(jnp.float32)

    rank = up_part.shape[0] // 2
    grad_b = jnp.concatenate(
        [finish(p, "voc", o) for p, o in zip((up_part[:rank], up_part[rank:]), orders)], 0
    )
    width_rows = down_part.shape[0] // 2
    grad_a = jnp.concatenate(
        [finish(p, "grp", z_bits) for p in (down_part[:width_rows], down_part[width_rows:])], 0
    )
    return frame_loss, grad_a, grad_b


def solution(mesh):
    in_specs = (
        P("grp", "voc"),
        P("grp", "voc"),
        P("grp", None),
        P("voc", None),
        P(None, "grp"),
        P("grp", "voc"),
    )
    out_specs = (P("voc", "grp", None), P("voc", None), P(None, "grp"))
    return jax.shard_map(
        on_device, mesh=mesh, in_specs=in_specs, out_specs=out_specs, check_vma=False
    )
```

time: 350 us -> 237 us (0.68)
  blocking collectives: 153 us -> 0 us
  starting transfers between devices: 1.4 us -> 64.5 us
  waiting for transfers between devices: 122 us -> 66.9 us
  local copies, waits for them, and re-layouts: 13.9 us -> 48.7 us
  other arithmetic: 14.9 us -> 35.4 us
  matrix products: 30.7 us -> 18.8 us
  between operations: 13.9 us -> 2.01 us
    psum x2 -> x0, blocking collectives: 153 us -> none  [the longest x1 80.5 us: on_device(): lax.psum(jnp.dot(up_weight, head_weight, preferred_element_type=jnp.float...]
    psum x3 -> x0, waiting for transfers between devices: 122 us -> none  [the longest x1 70.1 us: on_device(): act_grad = lax.psum(act_part, 'voc')]
    ppermute x1 -> x61, waiting for transfers between devices: 0.01 us -> 66.9 us  [the longest x60 66.9 us: swap(): return lax.ppermute(value, axis, pairs)]
    ppermute x1 -> x61, starting transfers between devices: 1.28 us -> 64.5 us  [the longest x60 63.3 us: swap(): return lax.ppermute(value, axis, pairs)]
    unnamed x12 -> x102, local copies, waits for them, and re-layouts: 7.79 us -> 28.5 us
    slice x1 -> x6, local copies, waits for them, and re-layouts: 0.99 us -> 9.05 us  [the longest x1 7.09 us: on_device(): target_logits[:, c * width:(c + 1) * width]]
    convert_element_type x1 -> x43, other arithmetic: 0.01 us -> 7.61 us  [the longest x12 3.24 us: reduce_bits(): sent = part.astype(wire)]
    slice x1, local copies, waits for them, and re-layouts: 4.35 us -> 8.51 us  [on_device(): shifted = jnp.concatenate((target_logits[HEAD:], incoming), 0)]
  transfers between devices with their start and end apart: 4 -> 61, of which waited for: 2 -> 28; matrix products, arithmetic and copies ran while one was open for 6% -> 31% of each run, Pallas kernels for 0% -> 0%
where the time goes in v1:
time: 237 us
  waiting for transfers between devices  66.9 us (28%)
  starting transfers between devices  64.5 us (27%)
  local copies, waits for them, and re-layouts  48.7 us (21%)
  other arithmetic  35.4 us (15%)
  matrix products  18.8 us (8%)
    ppermute x60, waiting for transfers between devices, swap(): return lax.ppermute(value, axis, pairs)  66.9 us
    ppermute x60, starting transfers between devices, swap(): return lax.ppermute(value, axis, pairs)  63.3 us
    unnamed x102, local copies, waits for them, and re-layouts  28.5 us
    reduce_sum x1, other arithmetic, on_device(): divergence = jnp.sum(target_prob * (log_target - log_draft), -1)  9.58 us
    slice x1, local copies, waits for them, and re-layouts, on_device(): shifted = jnp.concatenate((target_logits[HEAD:], incoming), 0)  8.51 us
    slice x1, local copies, waits for them, and re-layouts, on_device(): target_logits[:, c * width:(c + 1) * width]  7.09 us
    dot_general x5, matrix products, inner_cols(): lax.dot_general(left, right, (((1,), (1,)), ((), ())), preferred_element_...  6.96 us
    dot_general x4, matrix products, on_device(): jnp.dot(up_weight, head_weight[:, c * width:(c + 1) * width], preferred_e...  6.45 us
  transfers between devices with their start and end apart: 61, of which 28 were waited for; matrix products, arithmetic and copies ran while one was open for 31% of the time, Pallas kernels for 0%

profile of v1, /device:TPU:0, one launch (start us, length us, event | category | flops | bytes accessed | tf_op | source)
XLA Modules:
  0.0 236.5 jit_solution(10239634711570343030)
XLA Ops:
  3.6 2.8 %fusion.13 = f32[256,512]{1,0:T(8,128)S(1)} fusion(bf16[256,2048]{1,0:T(8,128)(2,1)} %param.10, bf16[2048,2048]{1,0:T(8,128)(2,1)} %param.11), kind=kOutput, calls=%fused_computation.22 | convolution fusion | flops 536870912 | bytes 3670016 | tf_op jit(solution)/shard_map/dot_general | solution.py:101
  7.2 3.7 %collective-permute-start.14 = (f16[128,512]{1,0:T(8,128)(2,1)}, f16[128,512]{1,0:T(8,128)(2,1)}, u32[]{:S(2)}, u32[]{:S(2)}) collective-permute-start(f16[128,512]{1,0:T(8,128)(2,1)} %dynamic-slice_convert_fusion.12), channel_id=1, source_target_pairs={{0,8},{8,0},{16,24},{24,16},{1,9},{9,1},{17,25},{25,17},{2,10},{10... | collective-permute-start | bytes 393224 | tf_op jit(solution)/shard_map/ppermute | solution.py:14
  10.8 2.3 fusion.16
  15.6 2.0 collective-permute-start.20
  19.8 7.1 %fusion.85 = (f32[1024,512]{1,0:T(8,128)}, f32[1024,512]{1,0:T(8,128)}, f32[1024,512]{1,0:T(8,128)}, f32[1024,512]{1,0:T(8,128)}) fusion(f32[1024,2048]{1,0:T(8,128)} %param.7), kind=kLoop, calls=%fused_computation.221 | loop fusion | bytes 16777216 | tf_op jit(solution)/shard_map/slice | solution.py:127
  30.6 8.5 %slice.70 = f32[1022,2048]{1,0:T(8,128)} slice(f32[1024,2048]{1,0:T(8,128)} %param.7), slice={[2:1024], [0:2048]} | slice | bytes 16744448 | tf_op jit(solution)/shard_map/slice | solution.py:133
  39.1 9.5 %copy.23 = f32[1022,2048]{0,1:T(8,128)} copy(f32[1022,2048]{1,0:T(8,128)} %slice.70) | data formatting | bytes 16744448
  48.6 2.9 %copy.25 = f32[1024,512]{0,1:T(8,128)} copy(f32[1024,512]{1,0:T(8,128)} %get-tuple-element.12) | data formatting | bytes 4194304
  51.5 2.9 %copy.26 = f32[1024,512]{0,1:T(8,128)} copy(f32[1024,512]{1,0:T(8,128)} %get-tuple-element.13) | data formatting | bytes 4194304
  54.4 2.9 %copy.24 = f32[1024,512]{0,1:T(8,128)} copy(f32[1024,512]{1,0:T(8,128)} %get-tuple-element.14) | data formatting | bytes 4194304
  57.3 2.9 %copy.27 = f32[1024,512]{0,1:T(8,128)} copy(f32[1024,512]{1,0:T(8,128)} %get-tuple-element.15) | data formatting | bytes 4194304
  60.6 4.2 %fusion.2 = f32[1024]{0:T(1024)S(1)} fusion(f32[2,2048]{0,1:T(8,128)S(1)} %copy.17, f32[1022,2048]{0,1:T(8,128)} %copy.23), kind=kLoop, calls=%fused_computation.11 | loop fusion | flops 4193280 | bytes 8392704 | tf_op jit(solution)/shard_map/reduce_max | solution.py:142
  64.8 4.6 %exponential_reduce_fusion.1 = f32[1024]{0:T(1024)S(1)} fusion(f32[1024]{0:T(1024)S(1)} %fusion.2, f32[2,2048]{0,1:T(8,128)S(1)} %copy.17, f32[1022,2048]{0,1:T(8,128)} %copy.23), kind=kLoop, calls=%fused_computation.7 | loop fusion | flops 6290432 | bytes 8396800 | tf_op jit(solution)/shard_map/reduce_sum | solution.py:143
  70.9 3.5 %collective-permute-start.15 = (f16[128,512]{1,0:T(8,128)(2,1)S(1)}, f16[128,512]{1,0:T(8,128)(2,1)S(1)}, u32[]{:S(2)}, u32[]{:S(2)}) collective-permute-start(f16[128,512]{1,0:T(8,128)(2,1)S(1)} %add_convert_fusion.22), channel_id=1, source_target_pairs={{0,16},{8,24},{16,0},{24,8},{1,17},{9,25},{17,1},{25,9},{2,18},{10... | collective-permute-start | bytes 393224 | tf_op jit(solution)/shard_map/ppermute | solution.py:14
  76.5 2.9 %collective-permute-start.21 = (f16[128,512]{1,0:T(8,128)(2,1)S(1)}, f16[128,512]{1,0:T(8,128)(2,1)S(1)}, u32[]{:S(2)}, u32[]{:S(2)}) collective-permute-start(f16[128,512]{1,0:T(8,128)(2,1)S(1)} %add_convert_fusion.18), channel_id=1, source_target_pairs={{0,16},{8,24},{16,0},{24,8},{1,17},{9,25},{17,1},{25,9},{2,18},{10... | collective-permute-start | bytes 393224 | tf_op jit(solution)/shard_map/ppermute | solution.py:14
  79.5 7.7 %collective-permute-done.15 = f16[128,512]{1,0:T(8,128)(2,1)S(1)} collective-permute-done((f16[128,512]{1,0:T(8,128)(2,1)S(1)}, f16[128,512]{1,0:T(8,128)(2,1)S(1)}, u32[]{:S(2)}, u32[]{:S(2)}) %collective-permute-start.15) | collective-permute-done | bytes 131104 | tf_op jit(solution)/shard_map/ppermute | solution.py:14
  87.2 2.8 %collective-permute-done.12 = f16[128,512]{1,0:T(8,128)(2,1)S(1)} collective-permute-done((f16[128,512]{1,0:T(8,128)(2,1)S(1)}, f16[128,512]{1,0:T(8,128)(2,1)S(1)}, u32[]{:S(2)}, u32[]{:S(2)}) %collective-permute-start.12) | collective-permute-done | bytes 131104 | tf_op jit(solution)/shard_map/ppermute | solution.py:14
  90.0 3.0 %collective-permute-start.16 = (bf16[128,512]{1,0:T(8,128)(2,1)S(1)}, bf16[128,512]{1,0:T(8,128)(2,1)S(1)}, u32[]{:S(2)}, u32[]{:S(2)}) collective-permute-start(bf16[128,512]{1,0:T(8,128)(2,1)S(1)} %add_convert_fusion.21), channel_id=1, source_target_pairs={{0,8},{8,0},{16,24},{24,16},{1,9},{9,1},{17,25},{25,17},{2,10},{10... | collective-permute-start | bytes 393224 | tf_op jit(solution)/shard_map/ppermute | solution.py:14
  93.1 2.6 %collective-permute-done.21 = f16[128,512]{1,0:T(8,128)(2,1)S(1)} collective-permute-done((f16[128,512]{1,0:T(8,128)(2,1)S(1)}, f16[128,512]{1,0:T(8,128)(2,1)S(1)}, u32[]{:S(2)}, u32[]{:S(2)}) %collective-permute-start.21) | collective-permute-done | bytes 131104 | tf_op jit(solution)/shard_map/ppermute | solution.py:14
  95.9 2.1 collective-permute-done.18
  102.8 3.4 %collective-permute-done.7 = f32[128,256]{1,0:T(8,128)S(1)} collective-permute-done((f32[128,256]{1,0:T(8,128)S(1)}, f32[128,256]{1,0:T(8,128)S(1)}, u32[]{:S(2)}, u32[]{:S(2)}) %collective-permute-start.7) | collective-permute-done | bytes 131104 | tf_op jit(solution)/shard_map/ppermute | solution.py:14
  107.7 3.6 %collective-permute-done.2 = f32[128,256]{1,0:T(8,128)S(1)} collective-permute-done((f32[128,256]{1,0:T(8,128)S(1)}, f32[128,256]{1,0:T(8,128)S(1)}, u32[]{:S(2)}, u32[]{:S(2)}) %collective-permute-start.2) | collective-permute-done | bytes 131104 | tf_op jit(solution)/shard_map/ppermute | solution.py:14
  114.7 1.6 collective-permute-done.8
  116.3 1.6 collective-permute-start.9
  118.0 2.2 collective-permute-start.4
  120.8 1.7 collective-permute-done.4
  132.2 9.6 %multiply_reduce_fusion = (f32[1024]{0:T(1024)S(1)}, f32[1024]{0:T(1024)S(1)}, bf16[1024,2048]{0,1:T(8,128)(2,1)}) fusion(f32[1024]{0:T(1024)S(1)} %log_add_fusion, f32[1024]{0:T(1024)S(1)} %log_add_fusion.1, f32[2,2048]{0,1:T(8,128)S(1)} %copy.17, f32[1022,2048]{0,1:T(8,128)S(1)} %bitcast.14, f32[1024,512]{0,1:T(8,128)} %copy-done.2, ...), kind=kLoop, calls=%fused_computation.5 | loop fusion | flops 39843840 | bytes 20996096 | tf_op jit(solution)/shard_map/reduce_sum | solution.py:154
  141.7 3.9 %fusion.26 = f32[1024,256]{1,0:T(8,128)S(1)} fusion(bf16[1024,2048]{0,1:T(8,128)(2,1)} %get-tuple-element.11, bf16[128,512]{1,0:T(8,128)(2,1)} %copy-done.25, bf16[128,512]{1,0:T(8,128)(2,1)} %copy-done.24, bf16[128,512]{1,0:T(8,128)(2,1)} %copy-done.27, bf16[128,512]{1,0:T(8,128)(2,1)} %copy-done.26, bf16[128,512]{1,0:T(8,128)(2,1)} %copy-done.21, ...), kind=kOutput, calls=%fused_computation.40 | convolution fusion | flops 1082130432 | bytes 6291456 | tf_op jit(solution)/shard_map/dot_general | solution.py:69
  148.9 1.7 collective-permute-start.45
  151.8 3.1 %collective-permute-done.48 = f16[128,512]{1,0:T(8,128)(2,1)S(1)} collective-permute-done((f16[128,512]{1,0:T(8,128)(2,1)S(1)}, f16[128,512]{1,0:T(8,128)(2,1)S(1)}, u32[]{:S(2)}, u32[]{:S(2)}) %collective-permute-start.48) | collective-permute-done | bytes 131104 | tf_op jit(solution)/shard_map/ppermute | solution.py:14
  155.3 2.3 collective-permute-done.45
  157.6 1.9 collective-permute-start.49
  159.5 2.3 collective-permute-done.42
  163.0 2.7 %collective-permute-done.39 = f16[128,512]{1,0:T(8,128)(2,1)S(1)} collective-permute-done((f16[128,512]{1,0:T(8,128)(2,1)S(1)}, f16[128,512]{1,0:T(8,128)(2,1)S(1)}, u32[]{:S(2)}, u32[]{:S(2)}) %collective-permute-start.39) | collective-permute-done | bytes 131104 | tf_op jit(solution)/shard_map/ppermute | solution.py:14
  165.8 3.0 %collective-permute-start.40 = (f16[128,512]{1,0:T(8,128)(2,1)S(1)}, f16[128,512]{1,0:T(8,128)(2,1)S(1)}, u32[]{:S(2)}, u32[]{:S(2)}) collective-permute-start(f16[128,512]{1,0:T(8,128)(2,1)S(1)} %add_convert_fusion.12), channel_id=1, source_target_pairs={{0,16},{8,24},{16,0},{24,8},{1,17},{9,25},{17,1},{25,9},{2,18},{10... | collective-permute-start | bytes 393224 | tf_op jit(solution)/shard_map/ppermute | solution.py:14
  170.5 5.4 %collective-permute-done.49 = f16[128,512]{1,0:T(8,128)(2,1)S(1)} collective-permute-done((f16[128,512]{1,0:T(8,128)(2,1)S(1)}, f16[128,512]{1,0:T(8,128)(2,1)S(1)}, u32[]{:S(2)}, u32[]{:S(2)}) %collective-permute-start.49) | collective-permute-done | bytes 131104 | tf_op jit(solution)/shard_map/ppermute | solution.py:14
  175.9 2.0 collective-permute-start.24
  178.7 2.9 %collective-permute-done.43 = f16[128,512]{1,0:T(8,128)(2,1)S(1)} collective-permute-done((f16[128,512]{1,0:T(8,128)(2,1)S(1)}, f16[128,512]{1,0:T(8,128)(2,1)S(1)}, u32[]{:S(2)}, u32[]{:S(2)}) %collective-permute-start.43) | collective-permute-done | bytes 131104 | tf_op jit(solution)/shard_map/ppermute | solution.py:14
  181.7 1.6 collective-permute-done.40
  183.8 1.6 collective-permute-start.41
  185.5 2.1 collective-permute-start.30
  187.6 4.2 %collective-permute-done.44 = bf16[128,512]{1,0:T(8,128)(2,1)S(1)} collective-permute-done((bf16[128,512]{1,0:T(8,128)(2,1)S(1)}, bf16[128,512]{1,0:T(8,128)(2,1)S(1)}, u32[]{:S(2)}, u32[]{:S(2)}) %collective-permute-start.44) | collective-permute-done | bytes 131104 | tf_op jit(solution)/shard_map/ppermute | solution.py:14
  198.2 2.1 collective-permute-start.26
  206.6 2.1 collective-permute-start.33
  208.8 2.1 collective-permute-start.58
  211.3 1.6 collective-permute-done.36
  218.5 5.6 %collective-permute-done.37 = f16[256,256]{0,1:T(8,128)(2,1)S(1)} collective-permute-done((f16[256,256]{0,1:T(8,128)(2,1)S(1)}, f16[256,256]{0,1:T(8,128)(2,1)S(1)}, u32[]{:S(2)}, u32[]{:S(2)}) %collective-permute-start.37) | collective-permute-done | bytes 131104 | tf_op jit(solution)/shard_map/ppermute | solution.py:14
  234.9 1.7 maximum_convert_fusion
  (306 shorter events, 74.2 us)
Async XLA Ops:
  2.3 57.9 %collective-permute-start = (f32[2,2048]{1,0:T(2,128)}, f32[2,2048]{1,0:T(2,128)S(1)}, u32[]{:S(2)}, u32[]{:S(2)}) collective-permute-start(f32[2,2048]{1,0:T(2,128)} %slice.71), channel_id=1, source_target_pairs={{8,0},{16,8},{24,16},{9,1},{17,9},{25,17},{10,2},{18,10},{26,18},{... | collective-permute-start | bytes 49160 | tf_op jit(solution)/shard_map/ppermute | solution.py:96
  7.2 62.2 %collective-permute-start.14 = (f16[128,512]{1,0:T(8,128)(2,1)}, f16[128,512]{1,0:T(8,128)(2,1)}, u32[]{:S(2)}, u32[]{:S(2)}) collective-permute-start(f16[128,512]{1,0:T(8,128)(2,1)} %dynamic-slice_convert_fusion.12), channel_id=1, source_target_pairs={{0,8},{8,0},{16,24},{24,16},{1,9},{9,1},{17,25},{25,17},{2,10},{10... | collective-permute-start | bytes 393224 | tf_op jit(solution)/shard_map/ppermute | solution.py:14
  14.0 56.9 %collective-permute-start.11 = (f16[128,512]{1,0:T(8,128)(2,1)}, f16[128,512]{1,0:T(8,128)(2,1)}, u32[]{:S(2)}, u32[]{:S(2)}) collective-permute-start(f16[128,512]{1,0:T(8,128)(2,1)} %dynamic-slice_convert_fusion.13), channel_id=1, source_target_pairs={{0,8},{8,0},{16,24},{24,16},{1,9},{9,1},{17,25},{25,17},{2,10},{10... | collective-permute-start | bytes 393224 | tf_op jit(solution)/shard_map/ppermute | solution.py:14
  15.6 59.8 %collective-permute-start.20 = (f16[128,512]{1,0:T(8,128)(2,1)}, f16[128,512]{1,0:T(8,128)(2,1)}, u32[]{:S(2)}, u32[]{:S(2)}) collective-permute-start(f16[128,512]{1,0:T(8,128)(2,1)} %dynamic-slice_convert_fusion.10), channel_id=1, source_target_pairs={{0,8},{8,0},{16,24},{24,16},{1,9},{9,1},{17,25},{25,17},{2,10},{10... | collective-permute-start | bytes 393224 | tf_op jit(solution)/shard_map/ppermute | solution.py:14
  19.8 56.7 %collective-permute-start.17 = (f16[128,512]{1,0:T(8,128)(2,1)}, f16[128,512]{1,0:T(8,128)(2,1)S(1)}, u32[]{:S(2)}, u32[]{:S(2)}) collective-permute-start(f16[128,512]{1,0:T(8,128)(2,1)} %dynamic-slice_convert_fusion.11), channel_id=1, source_target_pairs={{0,8},{8,0},{16,24},{24,16},{1,9},{9,1},{17,25},{25,17},{2,10},{10... | collective-permute-start | bytes 393224 | tf_op jit(solution)/shard_map/ppermute | solution.py:14
  60.2 38.5 %collective-permute-start.6 = (f32[256,256]{1,0:T(8,128)}, f32[256,256]{1,0:T(8,128)}, u32[]{:S(2)}, u32[]{:S(2)}) collective-permute-start(f32[256,256]{1,0:T(8,128)} %constant_dynamic-slice_fusion.6), channel_id=1, source_target_pairs={{0,1},{1,0},{2,3},{3,2},{4,5},{5,4},{6,7},{7,6},{8,9},{9,8},{10,11... | collective-permute-start | bytes 786440 | tf_op jit(solution)/shard_map/ppermute | solution.py:14
  69.4 31.7 %collective-permute-start.1 = (f32[256,256]{1,0:T(8,128)S(1)}, f32[256,256]{1,0:T(8,128)S(1)}, u32[]{:S(2)}, u32[]{:S(2)}) collective-permute-start(f32[256,256]{1,0:T(8,128)S(1)} %constant_dynamic-slice_fusion.8), channel_id=1, source_target_pairs={{0,1},{1,0},{2,3},{3,2},{4,5},{5,4},{6,7},{7,6},{8,9},{9,8},{10,11... | collective-permute-start | bytes 786440 | tf_op jit(solution)/shard_map/ppermute | solution.py:14
  70.9 16.3 %collective-permute-start.15 = (f16[128,512]{1,0:T(8,128)(2,1)S(1)}, f16[128,512]{1,0:T(8,128)(2,1)S(1)}, u32[]{:S(2)}, u32[]{:S(2)}) collective-permute-start(f16[128,512]{1,0:T(8,128)(2,1)S(1)} %add_convert_fusion.22), channel_id=1, source_target_pairs={{0,16},{8,24},{16,0},{24,8},{1,17},{9,25},{17,1},{25,9},{2,18},{10... | collective-permute-start | bytes 393224 | tf_op jit(solution)/shard_map/ppermute | solution.py:14
  75.4 14.6 %collective-permute-start.12 = (f16[128,512]{1,0:T(8,128)(2,1)S(1)}, f16[128,512]{1,0:T(8,128)(2,1)S(1)}, u32[]{:S(2)}, u32[]{:S(2)}) collective-permute-start(f16[128,512]{1,0:T(8,128)(2,1)S(1)} %add_convert_fusion.24), channel_id=1, source_target_pairs={{0,16},{8,24},{16,0},{24,8},{1,17},{9,25},{17,1},{25,9},{2,18},{10... | collective-permute-start | bytes 393224 | tf_op jit(solution)/shard_map/ppermute | solution.py:14
  76.5 19.2 %collective-permute-start.21 = (f16[128,512]{1,0:T(8,128)(2,1)S(1)}, f16[128,512]{1,0:T(8,128)(2,1)S(1)}, u32[]{:S(2)}, u32[]{:S(2)}) collective-permute-start(f16[128,512]{1,0:T(8,128)(2,1)S(1)} %add_convert_fusion.18), channel_id=1, source_target_pairs={{0,16},{8,24},{16,0},{24,8},{1,17},{9,25},{17,1},{25,9},{2,18},{10... | collective-permute-start | bytes 393224 | tf_op jit(solution)/shard_map/ppermute | solution.py:14
  87.2 10.8 %collective-permute-start.18 = (f16[128,512]{1,0:T(8,128)(2,1)S(1)}, f16[128,512]{1,0:T(8,128)(2,1)S(1)}, u32[]{:S(2)}, u32[]{:S(2)}) collective-permute-start(f16[128,512]{1,0:T(8,128)(2,1)S(1)} %add_convert_fusion.20), channel_id=1, source_target_pairs={{0,16},{8,24},{16,0},{24,8},{1,17},{9,25},{17,1},{25,9},{2,18},{10... | collective-permute-start | bytes 393224 | tf_op jit(solution)/shard_map/ppermute | solution.py:14
  90.0 22.8 %collective-permute-start.16 = (bf16[128,512]{1,0:T(8,128)(2,1)S(1)}, bf16[128,512]{1,0:T(8,128)(2,1)S(1)}, u32[]{:S(2)}, u32[]{:S(2)}) collective-permute-start(bf16[128,512]{1,0:T(8,128)(2,1)S(1)} %add_convert_fusion.21), channel_id=1, source_target_pairs={{0,8},{8,0},{16,24},{24,16},{1,9},{9,1},{17,25},{25,17},{2,10},{10... | collective-permute-start | bytes 393224 | tf_op jit(solution)/shard_map/ppermute | solution.py:14
  95.7 18.8 %collective-permute-start.13 = (bf16[128,512]{1,0:T(8,128)(2,1)S(1)}, bf16[128,512]{1,0:T(8,128)(2,1)S(1)}, u32[]{:S(2)}, u32[]{:S(2)}) collective-permute-start(bf16[128,512]{1,0:T(8,128)(2,1)S(1)} %add_convert_fusion.23), channel_id=1, source_target_pairs={{0,8},{8,0},{16,24},{24,16},{1,9},{9,1},{17,25},{25,17},{2,10},{10... | collective-permute-start | bytes 393224 | tf_op jit(solution)/shard_map/ppermute | solution.py:14
  98.0 16.6 %collective-permute-start.22 = (bf16[128,512]{1,0:T(8,128)(2,1)S(1)}, bf16[128,512]{1,0:T(8,128)(2,1)S(1)}, u32[]{:S(2)}, u32[]{:S(2)}) collective-permute-start(bf16[128,512]{1,0:T(8,128)(2,1)S(1)} %add_convert_fusion.17), channel_id=1, source_target_pairs={{0,8},{8,0},{16,24},{24,16},{1,9},{9,1},{17,25},{25,17},{2,10},{10... | collective-permute-start | bytes 393224 | tf_op jit(solution)/shard_map/ppermute | solution.py:14
  98.7 15.9 %collective-permute-start.19 = (bf16[128,512]{1,0:T(8,128)(2,1)S(1)}, bf16[128,512]{1,0:T(8,128)(2,1)S(1)}, u32[]{:S(2)}, u32[]{:S(2)}) collective-permute-start(bf16[128,512]{1,0:T(8,128)(2,1)S(1)} %add_convert_fusion.19), channel_id=1, source_target_pairs={{0,8},{8,0},{16,24},{24,16},{1,9},{9,1},{17,25},{25,17},{2,10},{10... | collective-permute-start | bytes 393224 | tf_op jit(solution)/shard_map/ppermute | solution.py:14
  147.8 18.0 %collective-permute-start.28 = (f32[256,256]{1,0:T(8,128)S(1)}, f32[256,256]{1,0:T(8,128)S(1)}, u32[]{:S(2)}, u32[]{:S(2)}) collective-permute-start(f32[256,256]{1,0:T(8,128)S(1)} %constant_dynamic-slice_fusion.1), channel_id=1, source_target_pairs={{0,1},{1,0},{2,3},{3,2},{4,5},{5,4},{6,7},{7,6},{8,9},{9,8},{10,11... | collective-permute-start | bytes 786440 | tf_op jit(solution)/shard_map/ppermute | solution.py:14
  148.0 20.8 %collective-permute-start.23 = (f32[256,256]{1,0:T(8,128)S(1)}, f32[256,256]{1,0:T(8,128)S(1)}, u32[]{:S(2)}, u32[]{:S(2)}) collective-permute-start(f32[256,256]{1,0:T(8,128)S(1)} %constant_dynamic-slice_fusion.3), channel_id=1, source_target_pairs={{0,1},{1,0},{2,3},{3,2},{4,5},{5,4},{6,7},{7,6},{8,9},{9,8},{10,11... | collective-permute-start | bytes 786440 | tf_op jit(solution)/shard_map/ppermute | solution.py:14
  148.4 6.4 %collective-permute-start.48 = (f16[128,512]{1,0:T(8,128)(2,1)S(1)}, f16[128,512]{1,0:T(8,128)(2,1)S(1)}, u32[]{:S(2)}, u32[]{:S(2)}) collective-permute-start(f16[128,512]{1,0:T(8,128)(2,1)S(1)} %dynamic-slice_convert_fusion.4), channel_id=1, source_target_pairs={{0,8},{8,0},{16,24},{24,16},{1,9},{9,1},{17,25},{25,17},{2,10},{10... | collective-permute-start | bytes 393224 | tf_op jit(solution)/shard_map/ppermute | solution.py:14
  148.9 8.7 %collective-permute-start.45 = (f16[128,512]{1,0:T(8,128)(2,1)S(1)}, f16[128,512]{1,0:T(8,128)(2,1)S(1)}, u32[]{:S(2)}, u32[]{:S(2)}) collective-permute-start(f16[128,512]{1,0:T(8,128)(2,1)S(1)} %dynamic-slice_convert_fusion.5), channel_id=1, source_target_pairs={{0,8},{8,0},{16,24},{24,16},{1,9},{9,1},{17,25},{25,17},{2,10},{10... | collective-permute-start | bytes 393224 | tf_op jit(solution)/shard_map/ppermute | solution.py:14
  150.6 11.2 %collective-permute-start.42 = (f16[128,512]{1,0:T(8,128)(2,1)S(1)}, f16[128,512]{1,0:T(8,128)(2,1)S(1)}, u32[]{:S(2)}, u32[]{:S(2)}) collective-permute-start(f16[128,512]{1,0:T(8,128)(2,1)S(1)} %dynamic-slice_convert_fusion.6), channel_id=1, source_target_pairs={{0,8},{8,0},{16,24},{24,16},{1,9},{9,1},{17,25},{25,17},{2,10},{10... | collective-permute-start | bytes 393224 | tf_op jit(solution)/shard_map/ppermute | solution.py:14
  154.8 10.9 %collective-permute-start.39 = (f16[128,512]{1,0:T(8,128)(2,1)S(1)}, f16[128,512]{1,0:T(8,128)(2,1)S(1)}, u32[]{:S(2)}, u32[]{:S(2)}) collective-permute-start(f16[128,512]{1,0:T(8,128)(2,1)S(1)} %dynamic-slice_convert_fusion.7), channel_id=1, source_target_pairs={{0,8},{8,0},{16,24},{24,16},{1,9},{9,1},{17,25},{25,17},{2,10},{10... | collective-permute-start | bytes 393224 | tf_op jit(solution)/shard_map/ppermute | solution.py:14
  157.6 18.3 %collective-permute-start.49 = (f16[128,512]{1,0:T(8,128)(2,1)S(1)}, f16[128,512]{1,0:T(8,128)(2,1)S(1)}, u32[]{:S(2)}, u32[]{:S(2)}) collective-permute-start(f16[128,512]{1,0:T(8,128)(2,1)S(1)} %add_convert_fusion.6), channel_id=1, source_target_pairs={{0,16},{8,24},{16,0},{24,8},{1,17},{9,25},{17,1},{25,9},{2,18},{10... | collective-permute-start | bytes 393224 | tf_op jit(solution)/shard_map/ppermute | solution.py:14
  161.8 16.9 %collective-permute-start.46 = (f16[128,512]{1,0:T(8,128)(2,1)S(1)}, f16[128,512]{1,0:T(8,128)(2,1)S(1)}, u32[]{:S(2)}, u32[]{:S(2)}) collective-permute-start(f16[128,512]{1,0:T(8,128)(2,1)S(1)} %add_convert_fusion.8), channel_id=1, source_target_pairs={{0,16},{8,24},{16,0},{24,8},{1,17},{9,25},{17,1},{25,9},{2,18},{10... | collective-permute-start | bytes 393224 | tf_op jit(solution)/shard_map/ppermute | solution.py:14
  165.7 15.9 %collective-permute-start.43 = (f16[128,512]{1,0:T(8,128)(2,1)S(1)}, f16[128,512]{1,0:T(8,128)(2,1)S(1)}, u32[]{:S(2)}, u32[]{:S(2)}) collective-permute-start(f16[128,512]{1,0:T(8,128)(2,1)S(1)} %add_convert_fusion.10), channel_id=1, source_target_pairs={{0,16},{8,24},{16,0},{24,8},{1,17},{9,25},{17,1},{25,9},{2,18},{10... | collective-permute-start | bytes 393224 | tf_op jit(solution)/shard_map/ppermute | solution.py:14
  165.8 17.5 %collective-permute-start.40 = (f16[128,512]{1,0:T(8,128)(2,1)S(1)}, f16[128,512]{1,0:T(8,128)(2,1)S(1)}, u32[]{:S(2)}, u32[]{:S(2)}) collective-permute-start(f16[128,512]{1,0:T(8,128)(2,1)S(1)} %add_convert_fusion.12), channel_id=1, source_target_pairs={{0,16},{8,24},{16,0},{24,8},{1,17},{9,25},{17,1},{25,9},{2,18},{10... | collective-permute-start | bytes 393224 | tf_op jit(solution)/shard_map/ppermute | solution.py:14
  168.9 14.9 %collective-permute-start.29 = (f32[128,256]{1,0:T(8,128)S(1)}, f32[128,256]{1,0:T(8,128)S(1)}, u32[]{:S(2)}, u32[]{:S(2)}) collective-permute-start(f32[128,256]{1,0:T(8,128)S(1)} %constant_dynamic-slice_fusion), channel_id=1, source_target_pairs={{0,4},{1,5},{2,6},{3,7},{4,0},{5,1},{6,2},{7,3},{8,12},{9,13},{10,... | collective-permute-start | bytes 393224 | tf_op jit(solution)/shard_map/ppermute | solution.py:14
  175.9 9.6 %collective-permute-start.24 = (f32[128,256]{1,0:T(8,128)S(1)}, f32[128,256]{1,0:T(8,128)S(1)}, u32[]{:S(2)}, u32[]{:S(2)}) collective-permute-start(f32[128,256]{1,0:T(8,128)S(1)} %constant_dynamic-slice_fusion.2), channel_id=1, source_target_pairs={{0,2},{1,3},{2,0},{3,1},{4,6},{5,7},{6,4},{7,5},{8,10},{9,11},{10,... | collective-permute-start | bytes 393224 | tf_op jit(solution)/shard_map/ppermute | solution.py:14
  178.7 15.9 %collective-permute-start.50 = (bf16[128,512]{1,0:T(8,128)(2,1)S(1)}, bf16[128,512]{1,0:T(8,128)(2,1)S(1)}, u32[]{:S(2)}, u32[]{:S(2)}) collective-permute-start(bf16[128,512]{1,0:T(8,128)(2,1)S(1)} %add_convert_fusion.5), channel_id=1, source_target_pairs={{0,8},{8,0},{16,24},{24,16},{1,9},{9,1},{17,25},{25,17},{2,10},{10... | collective-permute-start | bytes 393224 | tf_op jit(solution)/shard_map/ppermute | solution.py:14
  181.6 12.2 %collective-permute-start.47 = (bf16[128,512]{1,0:T(8,128)(2,1)S(1)}, bf16[128,512]{1,0:T(8,128)(2,1)S(1)}, u32[]{:S(2)}, u32[]{:S(2)}) collective-permute-start(bf16[128,512]{1,0:T(8,128)(2,1)S(1)} %add_convert_fusion.7), channel_id=1, source_target_pairs={{0,8},{8,0},{16,24},{24,16},{1,9},{9,1},{17,25},{25,17},{2,10},{10... | collective-permute-start | bytes 393224 | tf_op jit(solution)/shard_map/ppermute | solution.py:14
  183.3 8.4 %collective-permute-start.44 = (bf16[128,512]{1,0:T(8,128)(2,1)S(1)}, bf16[128,512]{1,0:T(8,128)(2,1)S(1)}, u32[]{:S(2)}, u32[]{:S(2)}) collective-permute-start(bf16[128,512]{1,0:T(8,128)(2,1)S(1)} %add_convert_fusion.9), channel_id=1, source_target_pairs={{0,8},{8,0},{16,24},{24,16},{1,9},{9,1},{17,25},{25,17},{2,10},{10... | collective-permute-start | bytes 393224 | tf_op jit(solution)/shard_map/ppermute | solution.py:14
  183.8 11.6 %collective-permute-start.41 = (bf16[128,512]{1,0:T(8,128)(2,1)S(1)}, bf16[128,512]{1,0:T(8,128)(2,1)S(1)}, u32[]{:S(2)}, u32[]{:S(2)}) collective-permute-start(bf16[128,512]{1,0:T(8,128)(2,1)S(1)} %add_convert_fusion.11), channel_id=1, source_target_pairs={{0,8},{8,0},{16,24},{24,16},{1,9},{9,1},{17,25},{25,17},{2,10},{10... | collective-permute-start | bytes 393224 | tf_op jit(solution)/shard_map/ppermute | solution.py:14
  185.5 11.7 %collective-permute-start.30 = (f32[128,256]{1,0:T(8,128)S(1)}, f32[128,256]{1,0:T(8,128)S(1)}, u32[]{:S(2)}, u32[]{:S(2)}) collective-permute-start(f32[128,256]{1,0:T(8,128)S(1)} %dynamic-slice_add_fusion.4), channel_id=1, source_target_pairs={{0,2},{1,3},{2,0},{3,1},{4,6},{5,7},{6,4},{7,5},{8,10},{9,11},{10,... | collective-permute-start | bytes 393224 | tf_op jit(solution)/shard_map/ppermute | solution.py:14
  191.7 6.4 %collective-permute-start.25 = (f32[128,256]{1,0:T(8,128)S(1)}, f32[128,256]{1,0:T(8,128)S(1)}, u32[]{:S(2)}, u32[]{:S(2)}) collective-permute-start(f32[128,256]{1,0:T(8,128)S(1)} %dynamic-slice_add_fusion.5), channel_id=1, source_target_pairs={{0,4},{1,5},{2,6},{3,7},{4,0},{5,1},{6,2},{7,3},{8,12},{9,13},{10,... | collective-permute-start | bytes 393224 | tf_op jit(solution)/shard_map/ppermute | solution.py:14
  196.5 6.1 %collective-permute-start.56 = (f16[64,2048]{1,0:T(8,128)(2,1)S(1)}, f16[64,2048]{1,0:T(8,128)(2,1)S(1)}, u32[]{:S(2)}, u32[]{:S(2)}) collective-permute-start(f16[64,2048]{1,0:T(8,128)(2,1)S(1)} %dynamic-slice_convert_fusion), channel_id=1, source_target_pairs={{0,1},{1,0},{2,3},{3,2},{4,5},{5,4},{6,7},{7,6},{8,9},{9,8},{10,11... | collective-permute-start | bytes 786440 | tf_op jit(solution)/shard_map/ppermute | solution.py:14
  196.7 7.5 %collective-permute-start.51 = (f16[64,2048]{1,0:T(8,128)(2,1)S(1)}, f16[64,2048]{1,0:T(8,128)(2,1)S(1)}, u32[]{:S(2)}, u32[]{:S(2)}) collective-permute-start(f16[64,2048]{1,0:T(8,128)(2,1)S(1)} %dynamic-slice_convert_fusion.1), channel_id=1, source_target_pairs={{0,1},{1,0},{2,3},{3,2},{4,5},{5,4},{6,7},{7,6},{8,9},{9,8},{10,11... | collective-permute-start | bytes 786440 | tf_op jit(solution)/shard_map/ppermute | solution.py:14
  202.8 6.0 %collective-permute-start.57 = (f16[32,2048]{1,0:T(8,128)(2,1)S(1)}, f16[32,2048]{1,0:T(8,128)(2,1)S(1)}, u32[]{:S(2)}, u32[]{:S(2)}) collective-permute-start(f16[32,2048]{1,0:T(8,128)(2,1)S(1)} %dynamic-slice_convert_fusion.2), channel_id=1, source_target_pairs={{0,4},{1,5},{2,6},{3,7},{4,0},{5,1},{6,2},{7,3},{8,12},{9,13},{10,... | collective-permute-start | bytes 393224 | tf_op jit(solution)/shard_map/ppermute | solution.py:14
  204.3 6.6 %collective-permute-start.52 = (f16[32,2048]{1,0:T(8,128)(2,1)S(1)}, f16[32,2048]{1,0:T(8,128)(2,1)S(1)}, u32[]{:S(2)}, u32[]{:S(2)}) collective-permute-start(f16[32,2048]{1,0:T(8,128)(2,1)S(1)} %dynamic-slice_convert_fusion.3), channel_id=1, source_target_pairs={{0,2},{1,3},{2,0},{3,1},{4,6},{5,7},{6,4},{7,5},{8,10},{9,11},{10,... | collective-permute-start | bytes 393224 | tf_op jit(solution)/shard_map/ppermute | solution.py:14
  206.4 6.5 %collective-permute-start.36 = (f16[256,256]{0,1:T(8,128)(2,1)S(1)}, f16[256,256]{0,1:T(8,128)(2,1)S(1)}, u32[]{:S(2)}, u32[]{:S(2)}) collective-permute-start(f16[256,256]{0,1:T(8,128)(2,1)S(1)} %dynamic-slice_convert_fusion.8), channel_id=1, source_target_pairs={{0,8},{8,0},{16,24},{24,16},{1,9},{9,1},{17,25},{25,17},{2,10},{10... | collective-permute-start | bytes 393224 | tf_op jit(solution)/shard_map/ppermute | solution.py:14
  206.6 8.7 %collective-permute-start.33 = (f16[256,256]{0,1:T(8,128)(2,1)S(1)}, f16[256,256]{0,1:T(8,128)(2,1)S(1)}, u32[]{:S(2)}, u32[]{:S(2)}) collective-permute-start(f16[256,256]{0,1:T(8,128)(2,1)S(1)} %dynamic-slice_convert_fusion.9), channel_id=1, source_target_pairs={{0,8},{8,0},{16,24},{24,16},{1,9},{9,1},{17,25},{25,17},{2,10},{10... | collective-permute-start | bytes 393224 | tf_op jit(solution)/shard_map/ppermute | solution.py:14
  208.8 8.0 %collective-permute-start.58 = (f16[32,2048]{1,0:T(8,128)(2,1)S(1)}, f16[32,2048]{1,0:T(8,128)(2,1)S(1)}, u32[]{:S(2)}, u32[]{:S(2)}) collective-permute-start(f16[32,2048]{1,0:T(8,128)(2,1)S(1)} %add_convert_fusion.2), channel_id=1, source_target_pairs={{0,2},{1,3},{2,0},{3,1},{4,6},{5,7},{6,4},{7,5},{8,10},{9,11},{10,... | collective-permute-start | bytes 393224 | tf_op jit(solution)/shard_map/ppermute | solution.py:14
  210.9 7.5 %collective-permute-start.53 = (f16[32,2048]{1,0:T(8,128)(2,1)S(1)}, f16[32,2048]{1,0:T(8,128)(2,1)S(1)}, u32[]{:S(2)}, u32[]{:S(2)}) collective-permute-start(f16[32,2048]{1,0:T(8,128)(2,1)S(1)} %add_convert_fusion.4), channel_id=1, source_target_pairs={{0,4},{1,5},{2,6},{3,7},{4,0},{5,1},{6,2},{7,3},{8,12},{9,13},{10,... | collective-permute-start | bytes 393224 | tf_op jit(solution)/shard_map/ppermute | solution.py:14
  213.0 11.2 %collective-permute-start.37 = (f16[256,256]{0,1:T(8,128)(2,1)S(1)}, f16[256,256]{0,1:T(8,128)(2,1)S(1)}, u32[]{:S(2)}, u32[]{:S(2)}) collective-permute-start(f16[256,256]{0,1:T(8,128)(2,1)S(1)} %add_convert_fusion.14), channel_id=1, source_target_pairs={{0,16},{8,24},{16,0},{24,8},{1,17},{9,25},{17,1},{25,9},{2,18},{10... | collective-permute-start | bytes 393224 | tf_op jit(solution)/shard_map/ppermute | solution.py:14
  215.3 10.3 %collective-permute-start.34 = (f16[256,256]{0,1:T(8,128)(2,1)S(1)}, f16[256,256]{0,1:T(8,128)(2,1)S(1)}, u32[]{:S(2)}, u32[]{:S(2)}) collective-permute-start(f16[256,256]{0,1:T(8,128)(2,1)S(1)} %add_convert_fusion.16), channel_id=1, source_target_pairs={{0,16},{8,24},{16,0},{24,8},{1,17},{9,25},{17,1},{25,9},{2,18},{10... | collective-permute-start | bytes 393224 | tf_op jit(solution)/shard_map/ppermute | solution.py:14
  216.9 9.5 %collective-permute-start.59 = (f16[32,2048]{1,0:T(8,128)(2,1)S(1)}, f16[32,2048]{1,0:T(8,128)(2,1)S(1)}, u32[]{:S(2)}, u32[]{:S(2)}) collective-permute-start(f16[32,2048]{1,0:T(8,128)(2,1)S(1)} %add_convert_fusion.1), channel_id=1, source_target_pairs={{0,4},{1,5},{2,6},{3,7},{4,0},{5,1},{6,2},{7,3},{8,12},{9,13},{10,... | collective-permute-start | bytes 393224 | tf_op jit(solution)/shard_map/ppermute | solution.py:14
  218.5 8.8 %collective-permute-start.54 = (f16[32,2048]{1,0:T(8,128)(2,1)S(1)}, f16[32,2048]{1,0:T(8,128)(2,1)S(1)}, u32[]{:S(2)}, u32[]{:S(2)}) collective-permute-start(f16[32,2048]{1,0:T(8,128)(2,1)S(1)} %add_convert_fusion.3), channel_id=1, source_target_pairs={{0,2},{1,3},{2,0},{3,1},{4,6},{5,7},{6,4},{7,5},{8,10},{9,11},{10,... | collective-permute-start | bytes 393224 | tf_op jit(solution)/shard_map/ppermute | solution.py:14
  224.2 5.5 %collective-permute-start.38 = (f16[256,256]{0,1:T(8,128)(2,1)S(1)}, f16[256,256]{0,1:T(8,128)(2,1)S(1)}, u32[]{:S(2)}, u32[]{:S(2)}) collective-permute-start(f16[256,256]{0,1:T(8,128)(2,1)S(1)} %add_convert_fusion.13), channel_id=1, source_target_pairs={{0,8},{8,0},{16,24},{24,16},{1,9},{9,1},{17,25},{25,17},{2,10},{10... | collective-permute-start | bytes 393224 | tf_op jit(solution)/shard_map/ppermute | solution.py:14
  225.6 5.5 %collective-permute-start.35 = (f16[256,256]{0,1:T(8,128)(2,1)S(1)}, f16[256,256]{0,1:T(8,128)(2,1)S(1)}, u32[]{:S(2)}, u32[]{:S(2)}) collective-permute-start(f16[256,256]{0,1:T(8,128)(2,1)S(1)} %add_convert_fusion.15), channel_id=1, source_target_pairs={{0,8},{8,0},{16,24},{24,16},{1,9},{9,1},{17,25},{25,17},{2,10},{10... | collective-permute-start | bytes 393224 | tf_op jit(solution)/shard_map/ppermute | solution.py:14
  228.1 5.6 %collective-permute-start.55 = (f16[64,2048]{1,0:T(8,128)(2,1)}, f16[64,2048]{1,0:T(8,128)(2,1)}, u32[]{:S(2)}, u32[]{:S(2)}) collective-permute-start(f16[64,2048]{1,0:T(8,128)(2,1)} %pad_maximum_fusion.3), channel_id=1, source_target_pairs={{0,1},{1,0},{2,3},{3,2},{4,5},{5,4},{6,7},{7,6},{8,9},{9,8},{10,11... | collective-permute-start | bytes 786440 | tf_op jit(solution)/shard_map/ppermute | solution.py:14
  (61 other events, 499.7 us)

commit v2 on v1

v2 whole, which is shorter than its diff:
```python
import jax
import jax.numpy as jnp
from jax import lax
from jax.experimental import pallas as pl
from jax.experimental.pallas import tpu as pltpu
from jax.sharding import PartitionSpec as P

HEAD = 2
LAM = 0.1
CHUNKS = 4
BLOCK = 256
VOCAB_SCALE = 128.0
F32 = jnp.float32
BF16 = jnp.bfloat16
F16 = jnp.float16


def swap(value, axis, bit):
    mask = 1 << bit
    pairs = [(i, i ^ mask) for i in range(lax.axis_size(axis))]
    return lax.ppermute(value, axis, pairs)


def own_bit(axis, bit):
    return (lax.axis_index(axis) >> bit) & 1


def half(value, which):
    rows = value.shape[0] // 2
    return lax.dynamic_slice_in_dim(value, which * rows, rows, 0)


def reduce_bits(part, axis, bits, wires):
    for bit, wire in zip(bits[:-1], wires):
        mine = own_bit(axis, bit)
        arrived = swap(half(part, 1 - mine).astype(wire), axis, bit)
        part = half(part, mine) + arrived.astype(F32)
    sent = part.astype(wires[-1])
    return sent.astype(F32) + swap(sent, axis, bits[-1]).astype(F32)


def gather_bits(piece, axis, bits):
    for bit in reversed(bits[:-1]):
        mine = own_bit(axis, bit)
        other = swap(piece, axis, bit)
        low = jnp.where(mine == 0, piece, other)
        high = jnp.where(mine == 0, other, piece)
        piece = jnp.concatenate((low, high), 0)
    return piece


def silu_slope(values):
    sigma = jax.nn.sigmoid(values)
    return sigma * (1.0 + values * (1.0 - sigma))


def inner_rows(left, right):
    return lax.dot_general(left, right, (((0,), (0,)), ((), ())), preferred_element_type=F32)


def inner_cols(left, right):
    return lax.dot_general(left, right, (((1,), (1,)), ((), ())), preferred_element_type=F32)


def over_books(values, combine, per_book):
    bit = 0
    while (1 << bit) < per_book:
        values = combine(values, jax.tree.map(lambda v: swap(v, "voc", bit), values))
        bit += 1
    return values


def merge_sums(a, b):
    top = jnp.maximum(a[0], b[0])
    return top, a[1] * jnp.exp(a[0] - top) + b[1] * jnp.exp(b[0] - top)


def params(megabytes):
    return pltpu.CompilerParams(
        dimension_semantics=("arbitrary",), vmem_limit_bytes=megabytes << 20
    )


def cost(flops, read, exps):
    return pl.CostEstimate(flops=flops, bytes_accessed=read, transcendentals=exps)


def row_spec(block, cols, column=0):
    return pl.BlockSpec((block, cols), lambda i: (i, column))


def whole_spec(rows, cols):
    return pl.BlockSpec((rows, cols), lambda i: (0, 0))


def shift_in(target_ref, next_ref, incoming_ref, window):
    block = target_ref.shape[0]
    last = pl.program_id(0) == pl.num_programs(0) - 1
    window[:block, :] = target_ref[...]
    window[block:, :] = jnp.where(last, incoming_ref[...], next_ref[...])
    return window[HEAD : HEAD + block, :]


def target_sums(target, incoming):
    rows, cols = target.shape
    block = min(BLOCK, rows)

    def body(target_ref, next_ref, incoming_ref, top_ref, sum_ref, window):
        shifted = shift_in(target_ref, next_ref, incoming_ref, window)
        top = jnp.max(shifted, -1, keepdims=True)
        top_ref[...] = top
        sum_ref[...] = jnp.sum(jnp.exp(shifted - top), -1, keepdims=True)

    per = block // 8
    return pl.pallas_call(
        body,
        grid=(rows // block,),
        in_specs=[
            row_spec(block, cols),
            pl.BlockSpec((8, cols), lambda i: (jnp.minimum((i + 1) * per, rows // 8 - 1), 0)),
            whole_spec(8, cols),
        ],
        out_specs=[row_spec(block, 1)] * 2,
        out_shape=[jax.ShapeDtypeStruct((rows, 1), F32)] * 2,
        scratch_shapes=[pltpu.VMEM((block + 8, cols), F32)],
        compiler_params=params(24),
        cost_estimate=cost(4 * rows * cols, 4 * rows * cols, rows * cols),
        name="target_sums",
    )(target, target, incoming)


def target_probs(target, incoming, top, total):
    rows, cols = target.shape
    block = min(BLOCK, rows)

    def body(target_ref, next_ref, incoming_ref, top_ref, sum_ref, prob_ref, entropy_ref, window):
        shifted = shift_in(target_ref, next_ref, incoming_ref, window)
        first = lax.axis_index("grp") * rows + pl.program_id(0) * block
        count = lax.axis_size("grp") * rows
        row = first + lax.broadcasted_iota(jnp.int32, (block, 1), 0)
        live = jnp.where(row < count - HEAD, 1.0, 0.0)
        log_target = shifted - (top_ref[...] + jnp.log(sum_ref[...]))
        prob = jnp.exp(log_target) * live
        prob_ref[...] = prob
        entropy_ref[...] = jnp.sum(prob * log_target, -1, keepdims=True)

    per = block // 8
    return pl.pallas_call(
        body,
        grid=(rows // block,),
        in_specs=[
            row_spec(block, cols),
            pl.BlockSpec((8, cols), lambda i: (jnp.minimum((i + 1) * per, rows // 8 - 1), 0)),
            whole_spec(8, cols),
            row_spec(block, 1),
            row_spec(block, 1),
        ],
        out_specs=[row_spec(block, cols), row_spec(block, 1)],
        out_shape=[
            jax.ShapeDtypeStruct((rows, cols), F32),
            jax.ShapeDtypeStruct((rows, 1), F32),
        ],
        scratch_shapes=[pltpu.VMEM((block + 8, cols), F32)],
        compiler_params=params(24),
        cost_estimate=cost(6 * rows * cols, 8 * rows * cols, rows * cols),
        name="target_probs",
    )(target, target, incoming, top, total)


def draft_chunk(target, acts, vocab_proj, column, sums):
    rows = target.shape[0]
    rank, width = vocab_proj.shape
    block = min(BLOCK, rows)

    def body(target_ref, acts_ref, proj_ref, *rest):
        draft_ref, top_ref, sum_ref = rest[-3:]
        draft = target_ref[...] + jnp.dot(
            acts_ref[...], proj_ref[...], preferred_element_type=F32
        )
        draft_ref[...] = draft
        top = jnp.max(draft, -1, keepdims=True)
        if sums is not None:
            top = jnp.maximum(top, rest[0][...])
        total = jnp.sum(jnp.exp(draft - top), -1, keepdims=True)
        if sums is not None:
            total = total + rest[1][...] * jnp.exp(rest[0][...] - top)
        top_ref[...] = top
        sum_ref[...] = total

    carried = () if sums is None else tuple(sums)
    draft, top, total = pl.pallas_call(
        body,
        grid=(rows // block,),
        in_specs=[
            row_spec(block, width, column),
            row_spec(block, rank),
            whole_spec(rank, width),
        ]
        + [row_spec(block, 1)] * len(carried),
        out_specs=[row_spec(block, width), row_spec(block, 1), row_spec(block, 1)],
        out_shape=[
            jax.ShapeDtypeStruct((rows, width), F32),
            jax.ShapeDtypeStruct((rows, 1), F32),
            jax.ShapeDtypeStruct((rows, 1), F32),
        ],
        compiler_params=params(16),
        cost_estimate=cost(2 * rows * rank * width, 8 * rows * width, rows * width),
        name="draft_chunk",
    )(target, acts, vocab_proj, *carried)
    return draft, (top, total)


def grad_chunk(draft, prob, label, acts, vocab_proj, column, sums, carried):
    rows, width = draft.shape
    rank = acts.shape[1]
    block = min(BLOCK, rows)

    def body(draft_ref, prob_ref, label_ref, acts_ref, proj_ref, top_ref, sum_ref, *rest):
        grad_ref, act_ref, loss_ref = rest[-3:]
        step = pl.program_id(0)
        first = lax.axis_index("grp") * rows + step * block
        count = lax.axis_size("grp") * rows
        row = first + lax.broadcasted_iota(jnp.int32, (block, 1), 0)
        live = jnp.where(row < count - HEAD, 1.0, 0.0)
        log_draft = draft_ref[...] - (top_ref[...] + jnp.log(sum_ref[...]))
        prob = prob_ref[...]
        place = lax.broadcasted_iota(jnp.int32, (block, width), 1) + column * width
        hit = jnp.where(place == label_ref[...], LAM, 0.0)
        loss = -jnp.sum((prob + hit) * log_draft, -1, keepdims=True)
        grad = ((live + LAM) * jnp.exp(log_draft) - prob - hit).astype(BF16)
        act = inner_cols(grad, proj_ref[...])
        if carried is not None:
            loss = loss + rest[1][...]
            act = act + rest[0][...]
        loss_ref[...] = loss
        act_ref[...] = act
        term = inner_rows(acts_ref[...], grad)

        @pl.when(step == 0)
        def _():
            grad_ref[...] = term

        @pl.when(step > 0)
        def _():
            grad_ref[...] += term

    extra = () if carried is None else tuple(carried)
    proj_grad, act, loss = pl.pallas_call(
        body,
        grid=(rows // block,),
        in_specs=[
            row_spec(block, width),
            row_spec(block, width, column),
            row_spec(block, 1),
            row_spec(block, rank),
            whole_spec(rank, width),
            row_spec(block, 1),
            row_spec(block, 1),
        ]
        + ([row_spec(block, rank), row_spec(block, 1)] if extra else []),
        out_specs=[whole_spec(rank, width), row_spec(block, rank), row_spec(block, 1)],
        out_shape=[
            jax.ShapeDtypeStruct((rank, width), F32),
            jax.ShapeDtypeStruct((rows, rank), F32),
            jax.ShapeDtypeStruct((rows, 1), F32),
        ],
        compiler_params=params(16),
        cost_estimate=cost(4 * rows * rank * width, 8 * rows * width, rows * width),
        name="grad_chunk",
    )(draft, prob, label, acts, vocab_proj, *sums, *extra)
    return proj_grad, (act, loss)


def on_device(hidden_states, target_logits, labels, down_weight, up_weight, head_weight):
    row_count, slice_cols = target_logits.shape
    book_count = labels.shape[1]
    group_count = lax.axis_size("grp")
    per_book = lax.axis_size("voc") // book_count
    block_rows = row_count // per_book
    position = lax.axis_index("voc")
    book_index = position // per_book
    book_part = position % per_book
    width = slice_cols // CHUNKS
    z_bits = list(range(group_count.bit_length() - 1))
    v_bits = list(range(lax.axis_size("voc").bit_length() - 1))
    v_other = v_bits[:1] + v_bits[:0:-1]

    def columns(c):
        return head_weight[:, c * width : (c + 1) * width]

    mine = own_bit("grp", 0)
    up_away, up_kept = half(up_weight, 1 - mine), half(up_weight, mine)
    away = [
        (jnp.dot(up_away, columns(c), preferred_element_type=F32) * VOCAB_SCALE).astype(F16)
        for c in range(CHUNKS)
    ]
    kept = [
        jnp.dot(up_kept, columns(c), preferred_element_type=F32) * VOCAB_SCALE
        for c in range(CHUNKS)
    ]
    vocab_proj = []
    for c in range(CHUNKS):
        part = kept[c] + swap(away[c], "grp", 0).astype(F32)
        total = reduce_bits(part, "grp", z_bits[1:], [F16] * len(z_bits))
        total = (total * (1.0 / VOCAB_SCALE)).astype(BF16)
        vocab_proj.append(gather_bits(total, "grp", z_bits))

    pre_part = jnp.dot(hidden_states, down_weight, preferred_element_type=F32)
    pre_act = reduce_bits(pre_part, "voc", v_bits, [F32] * len(v_bits))
    acts = gather_bits(jax.nn.silu(pre_act).astype(BF16), "voc", v_bits)

    bound = jnp.broadcast_to(jnp.max(jnp.abs(acts.astype(F32))), (8, 128))
    for bit in z_bits:
        bound = jnp.maximum(bound, swap(bound, "grp", bit))
    most = jnp.maximum(bound[0, 0] * (1.1 * group_count * row_count), 1e-30)
    grad_scale = jnp.exp2(jnp.floor(15.0 - jnp.log2(most)))

    devices = range(group_count)
    incoming = lax.ppermute(
        target_logits[:8], "grp", [(i + 1, i) for i in devices if i + 1 in devices]
    )
    top, total = over_books(tuple(target_sums(target_logits, incoming)), merge_sums, per_book)
    prob, entropy = target_probs(target_logits, incoming, top, total)
    label = lax.dynamic_slice_in_dim(labels, book_index, 1, 1) - book_part * slice_cols

    drafts, sums = [], None
    for c in range(CHUNKS):
        draft, sums = draft_chunk(target_logits, acts, vocab_proj[c], c, sums)
        drafts.append(draft)
    sums = over_books(tuple(sums), merge_sums, per_book)

    proj_parts, carried = [], None
    for c in range(CHUNKS):
        part, carried = grad_chunk(
            drafts[c], prob, label, acts, vocab_proj[c], c, sums, carried
        )
        proj_parts.append(part)
    act_part, loss = carried

    loss = over_books(loss + entropy, jnp.add, per_book)
    frame_loss = lax.dynamic_slice_in_dim(loss, book_part * block_rows, block_rows, 0)
    frame_loss = frame_loss.reshape(1, 1, block_rows)

    up_part = 0.0
    for c in range(CHUNKS):
        total = reduce_bits(proj_parts[c] * grad_scale, "grp", z_bits, [F16] * len(z_bits))
        total = (total * (1.0 / grad_scale)).astype(BF16)
        up_part = up_part + inner_cols(gather_bits(total, "grp", z_bits), columns(c))

    act_grad = reduce_bits(act_part, "voc", v_bits, [F32] * len(v_bits))
    pre_grad = gather_bits((act_grad * silu_slope(pre_act)).astype(BF16), "voc", v_bits)
    down_part = inner_rows(hidden_states, pre_grad)

    def finish(part, axis, bits, wires):
        total = reduce_bits(part, axis, bits, wires)
        return gather_bits(total.astype(BF16), axis, bits).astype(F32)

    rank = up_part.shape[0] // 2
    wires = [F32] + [BF16] * len(v_bits)
    grad_b = jnp.concatenate(
        [
            finish(p, "voc", o, wires)
            for p, o in zip((up_part[:rank], up_part[rank:]), (v_bits, v_other))
        ],
        0,
    )
    grad_a = finish(down_part, "grp", z_bits, [BF16] * len(z_bits))
    return frame_loss, grad_a, grad_b


def solution(mesh):
    in_specs = (
        P("grp", "voc"),
        P("grp", "voc"),
        P("grp", None),
        P("voc", None),
        P(None, "grp"),
        P("grp", "voc"),
    )
    out_specs = (P("voc", "grp", None), P("voc", None), P(None, "grp"))
    return jax.shard_map(
        on_device, mesh=mesh, in_specs=in_specs, out_specs=out_specs, check_vma=False
    )
```

time: 237 us -> 222 us (0.937)
  local copies, waits for them, and re-layouts: 48.7 us -> 14.1 us
  waiting for transfers between devices: 66.9 us -> 97.4 us
  other arithmetic: 35.4 us -> 11 us
  Pallas kernels: 0 us -> 24.1 us
  starting transfers between devices: 64.5 us -> 48.8 us
  matrix products: 18.8 us -> 23.4 us
    ppermute x60 -> x49, waiting for transfers between devices: 66.9 us -> 96.3 us  [swap(): return lax.ppermute(value, axis, pairs)]
    pallas_call x0 -> x10, Pallas kernels: none -> 24.1 us  [the longest x4 10.7 us: grad_chunk(): pl.pallas_call(body, grid=(rows // block,), in_specs=[row_spec(block, wid...]
    unnamed x102 -> x54, local copies, waits for them, and re-layouts: 28.5 us -> 9.28 us
    slice x6 -> x2, local copies, waits for them, and re-layouts: 17.4 us -> 1.36 us  [the longest x1 0.84 us: on_device(): target_logits[:8]]
    ppermute x60 -> x49, starting transfers between devices: 63.3 us -> 47.5 us  [swap(): return lax.ppermute(value, axis, pairs)]
    reduce_sum x3 -> x0, other arithmetic: 15.4 us -> none  [the longest x1 9.58 us: on_device(): divergence = jnp.sum(target_prob * (log_target - log_draft), -1)]
    dot_general x9, matrix products: 9.21 us -> 16.3 us  [the longest x4 10.9 us: on_device(): jnp.dot(up_away, columns(c), preferred_element_type=F32) * VOCAB_SCALE]
    reduce_max x2 -> x1, other arithmetic: 4.17 us -> 0.67 us  [on_device(): bound = jnp.broadcast_to(jnp.max(jnp.abs(acts.astype(F32))), (8, 128))]
  transfers between devices with their start and end apart: 61 -> 50, of which waited for: 28 -> 28; matrix products, arithmetic and copies ran while one was open for 31% -> 16% of each run, Pallas kernels for 0% -> 11%
where the time goes in v2:
time: 222 us; the launch traced here: 221 us
  waiting for transfers between devices  97.4 us (44%)
  starting transfers between devices  48.8 us (22%)
  Pallas kernels  24.1 us (11%)
  matrix products  23.4 us (11%)
  local copies, waits for them, and re-layouts  14.1 us (6%)
  other arithmetic  11 us (5%)
  between operations  2.36 us (1%)
    ppermute x49, waiting for transfers between devices, swap(): return lax.ppermute(value, axis, pairs)  96.3 us
    ppermute x49, starting transfers between devices, swap(): return lax.ppermute(value, axis, pairs)  47.5 us
    dot_general x4, matrix products, on_device(): jnp.dot(up_away, columns(c), preferred_element_type=F32) * VOCAB_SCALE  10.9 us
    pallas_call x4, Pallas kernels, grad_chunk(): pl.pallas_call(body, grid=(rows // block,), in_specs=[row_spec(block, wid...  10.7 us
    unnamed x54, local copies, waits for them, and re-layouts  9.28 us
    pallas_call x4, Pallas kernels, draft_chunk(): pl.pallas_call(body, grid=(rows // block,), in_specs=[row_spec(block, wid...  8.01 us
    dot_general x4, matrix products, inner_cols(): lax.dot_general(left, right, (((1,), (1,)), ((), ())), preferred_element_...  6.4 us
  transfers between devices with their start and end apart: 50, of which 28 were waited for; matrix products, arithmetic and copies ran while one was open for 16% of the time, Pallas kernels for 11%

profile of v2, /device:TPU:0, one launch (start us, length us, event | category | flops | bytes accessed | tf_op | source)
XLA Modules:
  0.0 221.2 jit_solution(4364784480160169448)
XLA Ops:
  2.2 1.8 fusion.117
  6.3 2.7 %fusion.49 = f16[128,512]{1,0:T(8,128)(2,1)} fusion(bf16[2048,2048]{1,0:T(8,128)(2,1)} %param.11, bf16[256,2048]{1,0:T(8,128)(2,1)S(1)} %copy-done.17, s32[]{:T(128)S(6)} %select_n.239), kind=kOutput, calls=%fused_computation.34 | convolution fusion | flops 268566528 | bytes 2752516 | tf_op jit(solution)/shard_map/dot_general | solution.py:294
  9.0 2.6 %collective-permute-start.14 = (f16[128,512]{1,0:T(8,128)(2,1)}, f16[128,512]{1,0:T(8,128)(2,1)}, u32[]{:S(2)}, u32[]{:S(2)}) collective-permute-start(f16[128,512]{1,0:T(8,128)(2,1)} %fusion.49), channel_id=1, source_target_pairs={{0,8},{8,0},{16,24},{24,16},{1,9},{9,1},{17,25},{25,17},{2,10},{10... | collective-permute-start | bytes 393224 | tf_op jit(solution)/shard_map/ppermute | solution.py:21
  11.6 2.7 %fusion.52 = f16[128,512]{1,0:T(8,128)(2,1)} fusion(bf16[2048,2048]{1,0:T(8,128)(2,1)} %param.11, bf16[256,2048]{1,0:T(8,128)(2,1)S(1)} %copy-done.17, s32[]{:T(128)S(6)} %select_n.239), kind=kOutput, calls=%fused_computation.35 | convolution fusion | flops 268566528 | bytes 2752516 | tf_op jit(solution)/shard_map/dot_general | solution.py:294
  14.3 2.8 %fusion.55 = f16[128,512]{1,0:T(8,128)(2,1)} fusion(bf16[2048,2048]{1,0:T(8,128)(2,1)} %param.11, bf16[256,2048]{1,0:T(8,128)(2,1)S(1)} %copy-done.17, s32[]{:T(128)S(6)} %select_n.239), kind=kOutput, calls=%fused_computation.36 | convolution fusion | flops 268566528 | bytes 2752516 | tf_op jit(solution)/shard_map/dot_general | solution.py:294
  17.1 1.9 collective-permute-start.8
  21.2 2.7 %fusion.58 = f16[128,512]{1,0:T(8,128)(2,1)} fusion(bf16[2048,2048]{1,0:T(8,128)(2,1)} %param.11, bf16[256,2048]{1,0:T(8,128)(2,1)S(1)} %copy-done.18, s32[]{:T(128)S(6)} %select_n.239), kind=kOutput, calls=%fused_computation.37 | convolution fusion | flops 268566528 | bytes 2752516 | tf_op jit(solution)/shard_map/dot_general | solution.py:294
  27.6 3.4 %copy-done.1 = f32[1024,2048]{1,0:T(8,128)S(1)} copy-done((f32[1024,2048]{1,0:T(8,128)S(1)}, f32[1024,2048]{1,0:T(8,128)}, u32[]{:S(2)}) %copy-start.1) | copy-done | bytes 8388632
  30.9 2.1 target_sums.1
  33.0 3.3 %target_probs.1 = (f32[1024,2048]{1,0:T(8,128)S(1)}, f32[1024,1]{1,0:T(8,128)S(1)}) custom-call(f32[1024,2048]{1,0:T(8,128)S(1)} %copy-done.1, f32[1024,2048]{1,0:T(8,128)S(1)} %copy-done.1, f32[8,2048]{1,0:T(8,128)S(1)} %collective-permute-done.17.incoming_ref, f32[1024,1]{1,0:T(8,128)S(1)} %get-tuple-element.38.top_ref, ...), custom_call_target="tpu_custom_call" | custom-call | flops 12582912 | bytes 16777216 | tf_op jit(solution)/shard_map/target_probs/pallas_call | solution.py:148
  37.7 2.7 %collective-permute-start.15 = (f16[128,512]{1,0:T(8,128)(2,1)S(1)}, f16[128,512]{1,0:T(8,128)(2,1)S(1)}, u32[]{:S(2)}, u32[]{:S(2)}) collective-permute-start(f16[128,512]{1,0:T(8,128)(2,1)S(1)} %add_convert_fusion.9), channel_id=1, source_target_pairs={{0,16},{8,24},{16,0},{24,8},{1,17},{9,25},{17,1},{25,9},{2,18},{10... | collective-permute-start | bytes 393224 | tf_op jit(solution)/shard_map/ppermute | solution.py:21
  42.6 2.7 %collective-permute-start.9 = (f16[128,512]{1,0:T(8,128)(2,1)S(1)}, f16[128,512]{1,0:T(8,128)(2,1)S(1)}, u32[]{:S(2)}, u32[]{:S(2)}) collective-permute-start(f16[128,512]{1,0:T(8,128)(2,1)S(1)} %add_convert_fusion.11), channel_id=1, source_target_pairs={{0,16},{8,24},{16,0},{24,8},{1,17},{9,25},{17,1},{25,9},{2,18},{10... | collective-permute-start | bytes 393224 | tf_op jit(solution)/shard_map/ppermute | solution.py:21
  46.1 8.8 %collective-permute-done.15 = f16[128,512]{1,0:T(8,128)(2,1)S(1)} collective-permute-done((f16[128,512]{1,0:T(8,128)(2,1)S(1)}, f16[128,512]{1,0:T(8,128)(2,1)S(1)}, u32[]{:S(2)}, u32[]{:S(2)}) %collective-permute-start.15) | collective-permute-done | bytes 131104 | tf_op jit(solution)/shard_map/ppermute | solution.py:21
  55.4 2.5 %collective-permute-done.12 = f16[128,512]{1,0:T(8,128)(2,1)S(1)} collective-permute-done((f16[128,512]{1,0:T(8,128)(2,1)S(1)}, f16[128,512]{1,0:T(8,128)(2,1)S(1)}, u32[]{:S(2)}, u32[]{:S(2)}) %collective-permute-start.12) | collective-permute-done | bytes 131104 | tf_op jit(solution)/shard_map/ppermute | solution.py:21
  58.2 2.4 %collective-permute-done.9 = f16[128,512]{1,0:T(8,128)(2,1)S(1)} collective-permute-done((f16[128,512]{1,0:T(8,128)(2,1)S(1)}, f16[128,512]{1,0:T(8,128)(2,1)S(1)}, u32[]{:S(2)}, u32[]{:S(2)}) %collective-permute-start.9) | collective-permute-done | bytes 131104 | tf_op jit(solution)/shard_map/ppermute | solution.py:21
  63.8 1.8 collective-permute-start.7
  65.7 3.1 %collective-permute-done.1 = f32[256,256]{1,0:T(8,128)S(1)} collective-permute-done((f32[256,256]{1,0:T(8,128)S(1)}, f32[256,256]{1,0:T(8,128)S(1)}, u32[]{:S(2)}, u32[]{:S(2)}) %collective-permute-start.1) | collective-permute-done | bytes 262176 | tf_op jit(solution)/shard_map/ppermute | solution.py:21
  71.2 4.1 %collective-permute-done.2 = f32[256,256]{1,0:T(8,128)S(1)} collective-permute-done((f32[256,256]{1,0:T(8,128)S(1)}, f32[256,256]{1,0:T(8,128)S(1)}, u32[]{:S(2)}, u32[]{:S(2)}) %collective-permute-start.2) | collective-permute-done | bytes 262176 | tf_op jit(solution)/shard_map/ppermute | solution.py:21
  76.9 3.4 %collective-permute-done.3 = bf16[256,256]{1,0:T(8,128)(2,1)S(1)} collective-permute-done((bf16[256,256]{1,0:T(8,128)(2,1)S(1)}, bf16[256,256]{1,0:T(8,128)(2,1)S(1)}, u32[]{:S(2)}, u32[]{:S(2)}) %collective-permute-start.3) | collective-permute-done | bytes 131104 | tf_op jit(solution)/shard_map/ppermute | solution.py:21
  83.5 1.8 collective-permute-start.26
  85.3 1.7 draft_chunk.4
  87.0 2.1 draft_chunk.5
  89.1 2.1 draft_chunk.6
  91.2 2.1 draft_chunk.7
  93.3 2.6 %grad_chunk.4 = (f32[256,512]{1,0:T(8,128)S(1)}, f32[1024,256]{1,0:T(8,128)S(1)}, f32[1024,1]{1,0:T(8,128)S(1)}) custom-call(f32[1024,512]{1,0:T(8,128)S(1)} %get-tuple-element.45.draft_ref, f32[1024,2048]{1,0:T(8,128)S(1)} %get-tuple-element.40.prob_ref, s32[1024,1]{1,0:T(8,128)S(1)} %copy.13.label_ref, bf16[1024,256]{1,0:T(8,128)(2,1)S(1)} %pad_maximum_fusion.acts_ref, ...), custom_call_target="tpu_custom_call" | custom-call | flops 536870912 | bytes 4194304 | tf_op jit(solution)/shard_map/grad_chunk/pallas_call | solution.py:248
  95.9 2.6 %grad_chunk.5 = (f32[256,512]{1,0:T(8,128)S(1)}, f32[1024,256]{1,0:T(8,128)S(1)}, f32[1024,1]{1,0:T(8,128)S(1)}) custom-call(f32[1024,512]{1,0:T(8,128)S(1)} %get-tuple-element.44.draft_ref, f32[1024,2048]{1,0:T(8,128)S(1)} %get-tuple-element.40.prob_ref, s32[1024,1]{1,0:T(8,128)S(1)} %copy.13.label_ref, bf16[1024,256]{1,0:T(8,128)(2,1)S(1)} %pad_maximum_fusion.acts_ref, ...), custom_call_target="tpu_custom_call" | custom-call | flops 536870912 | bytes 4194304 | tf_op jit(solution)/shard_map/grad_chunk/pallas_call | solution.py:248
  98.6 2.6 %grad_chunk.6 = (f32[256,512]{1,0:T(8,128)S(1)}, f32[1024,256]{1,0:T(8,128)S(1)}, f32[1024,1]{1,0:T(8,128)S(1)}) custom-call(f32[1024,512]{1,0:T(8,128)S(1)} %get-tuple-element.43.draft_ref, f32[1024,2048]{1,0:T(8,128)S(1)} %get-tuple-element.40.prob_ref, s32[1024,1]{1,0:T(8,128)S(1)} %copy.13.label_ref, bf16[1024,256]{1,0:T(8,128)(2,1)S(1)} %pad_maximum_fusion.acts_ref, ...), custom_call_target="tpu_custom_call" | custom-call | flops 536870912 | bytes 4194304 | tf_op jit(solution)/shard_map/grad_chunk/pallas_call | solution.py:248
  101.2 2.8 %grad_chunk.7 = (f32[256,512]{1,0:T(8,128)S(1)}, f32[1024,256]{1,0:T(8,128)S(1)}, f32[1024,1]{1,0:T(8,128)S(1)}) custom-call(f32[1024,512]{1,0:T(8,128)S(1)} %get-tuple-element.37.draft_ref, f32[1024,2048]{1,0:T(8,128)S(1)} %get-tuple-element.40.prob_ref, s32[1024,1]{1,0:T(8,128)S(1)} %copy.13.label_ref, bf16[1024,256]{1,0:T(8,128)(2,1)S(1)} %pad_maximum_fusion.acts_ref, ...), custom_call_target="tpu_custom_call" | custom-call | flops 536870912 | bytes 4194304 | tf_op jit(solution)/shard_map/grad_chunk/pallas_call | solution.py:248
  104.9 1.7 collective-permute-start.27
  107.5 2.0 collective-permute-done.27
  119.5 1.7 collective-permute-start.29
  121.2 5.3 %collective-permute-done.31 = f16[128,512]{1,0:T(8,128)(2,1)S(1)} collective-permute-done((f16[128,512]{1,0:T(8,128)(2,1)S(1)}, f16[128,512]{1,0:T(8,128)(2,1)S(1)}, u32[]{:S(2)}, u32[]{:S(2)}) %collective-permute-start.31) | collective-permute-done | bytes 131104 | tf_op jit(solution)/shard_map/ppermute | solution.py:21
  127.7 1.8 collective-permute-done.34
  131.0 1.7 collective-permute-start.38
  134.0 7.3 %collective-permute-done.32 = f16[128,512]{1,0:T(8,128)(2,1)S(1)} collective-permute-done((f16[128,512]{1,0:T(8,128)(2,1)S(1)}, f16[128,512]{1,0:T(8,128)(2,1)S(1)}, u32[]{:S(2)}, u32[]{:S(2)}) %collective-permute-start.32) | collective-permute-done | bytes 131104 | tf_op jit(solution)/shard_map/ppermute | solution.py:21
  141.4 1.8 collective-permute-done.35
  145.5 2.3 %collective-permute-done.33 = bf16[128,512]{1,0:T(8,128)(2,1)S(1)} collective-permute-done((bf16[128,512]{1,0:T(8,128)(2,1)S(1)}, bf16[128,512]{1,0:T(8,128)(2,1)S(1)}, u32[]{:S(2)}, u32[]{:S(2)}) %collective-permute-start.33) | collective-permute-done | bytes 131104 | tf_op jit(solution)/shard_map/ppermute | solution.py:21
  147.9 2.5 %fusion.7 = f32[256,2048]{1,0:T(8,128)S(1)} fusion(bf16[2048,2048]{1,0:T(8,128)(2,1)} %param.11, bf16[128,512]{1,0:T(8,128)(2,1)S(1)} %get-tuple-element.84, bf16[128,512]{1,0:T(8,128)(2,1)S(1)} %get-tuple-element.83), kind=kOutput, calls=%fused_computation.8 | convolution fusion | flops 537395200 | bytes 4456448 | tf_op jit(solution)/shard_map/dot_general | solution.py:62
  150.4 2.3 %fusion.13 = f32[256,2048]{1,0:T(8,128)S(1)} fusion(bf16[2048,2048]{1,0:T(8,128)(2,1)} %param.11, bf16[128,512]{1,0:T(8,128)(2,1)S(1)} %get-tuple-element.86, bf16[128,512]{1,0:T(8,128)(2,1)S(1)} %get-tuple-element.85), kind=kOutput, calls=%fused_computation.14 | convolution fusion | flops 537395200 | bytes 4456448 | tf_op jit(solution)/shard_map/dot_general | solution.py:62
  159.4 5.4 %collective-permute-done.19 = f32[256,256]{1,0:T(8,128)S(1)} collective-permute-done((f32[256,256]{1,0:T(8,128)S(1)}, f32[256,256]{1,0:T(8,128)S(1)}, u32[]{:S(2)}, u32[]{:S(2)}) %collective-permute-start.19) | collective-permute-done | bytes 262176 | tf_op jit(solution)/shard_map/ppermute | solution.py:21
  168.7 4.4 %collective-permute-done.20 = f32[256,256]{1,0:T(8,128)S(1)} collective-permute-done((f32[256,256]{1,0:T(8,128)S(1)}, f32[256,256]{1,0:T(8,128)S(1)}, u32[]{:S(2)}, u32[]{:S(2)}) %collective-permute-start.20) | collective-permute-done | bytes 262176 | tf_op jit(solution)/shard_map/ppermute | solution.py:21
  173.2 2.0 collective-permute-start.21
  178.4 1.9 collective-permute-done.42
  182.5 2.8 %collective-permute-done.43 = bf16[32,2048]{1,0:T(8,128)(2,1)S(1)} collective-permute-done((bf16[32,2048]{1,0:T(8,128)(2,1)S(1)}, bf16[32,2048]{1,0:T(8,128)(2,1)S(1)}, u32[]{:S(2)}, u32[]{:S(2)}) %collective-permute-start.43) | collective-permute-done | bytes 131104 | tf_op jit(solution)/shard_map/ppermute | solution.py:21
  185.5 1.6 collective-permute-done.48
  188.3 8.6 %collective-permute-done.23 = bf16[512,256]{0,1:T(8,128)(2,1)S(1)} collective-permute-done((bf16[512,256]{0,1:T(8,128)(2,1)S(1)}, bf16[512,256]{0,1:T(8,128)(2,1)S(1)}, u32[]{:S(2)}, u32[]{:S(2)}) %collective-permute-start.23) | collective-permute-done | bytes 262176 | tf_op jit(solution)/shard_map/ppermute | solution.py:21
  198.5 12.9 %collective-permute-done.24 = bf16[512,256]{0,1:T(8,128)(2,1)S(1)} collective-permute-done((bf16[512,256]{0,1:T(8,128)(2,1)S(1)}, bf16[512,256]{0,1:T(8,128)(2,1)S(1)}, u32[]{:S(2)}, u32[]{:S(2)}) %collective-permute-start.24) | collective-permute-done | bytes 262176 | tf_op jit(solution)/shard_map/ppermute | solution.py:21
  213.1 6.7 %collective-permute-done.25 = bf16[512,256]{0,1:T(8,128)(2,1)S(1)} collective-permute-done((bf16[512,256]{0,1:T(8,128)(2,1)S(1)}, bf16[512,256]{0,1:T(8,128)(2,1)S(1)}, u32[]{:S(2)}, u32[]{:S(2)}) %collective-permute-start.25) | collective-permute-done | bytes 262176 | tf_op jit(solution)/shard_map/ppermute | solution.py:21
  (213 shorter events, 64.4 us)
Async XLA Ops:
  5.9 55.2 %collective-permute-start = (f32[512,256]{1,0:T(8,128)}, f32[512,256]{1,0:T(8,128)}, u32[]{:S(2)}, u32[]{:S(2)}) collective-permute-start(f32[512,256]{1,0:T(8,128)} %constant_dynamic-slice_fusion.6), channel_id=1, source_target_pairs={{0,1},{1,0},{2,3},{3,2},{4,5},{5,4},{6,7},{7,6},{8,9},{9,8},{10,11... | collective-permute-start | bytes 1572872 | tf_op jit(solution)/shard_map/ppermute | solution.py:21
  9.0 27.3 %collective-permute-start.14 = (f16[128,512]{1,0:T(8,128)(2,1)}, f16[128,512]{1,0:T(8,128)(2,1)}, u32[]{:S(2)}, u32[]{:S(2)}) collective-permute-start(f16[128,512]{1,0:T(8,128)(2,1)} %fusion.49), channel_id=1, source_target_pairs={{0,8},{8,0},{16,24},{24,16},{1,9},{9,1},{17,25},{25,17},{2,10},{10... | collective-permute-start | bytes 393224 | tf_op jit(solution)/shard_map/ppermute | solution.py:21
  14.3 26.1 %collective-permute-start.11 = (f16[128,512]{1,0:T(8,128)(2,1)}, f16[128,512]{1,0:T(8,128)(2,1)}, u32[]{:S(2)}, u32[]{:S(2)}) collective-permute-start(f16[128,512]{1,0:T(8,128)(2,1)} %fusion.52), channel_id=1, source_target_pairs={{0,8},{8,0},{16,24},{24,16},{1,9},{9,1},{17,25},{25,17},{2,10},{10... | collective-permute-start | bytes 393224 | tf_op jit(solution)/shard_map/ppermute | solution.py:21
  17.1 25.1 %collective-permute-start.8 = (f16[128,512]{1,0:T(8,128)(2,1)}, f16[128,512]{1,0:T(8,128)(2,1)S(1)}, u32[]{:S(2)}, u32[]{:S(2)}) collective-permute-start(f16[128,512]{1,0:T(8,128)(2,1)} %fusion.55), channel_id=1, source_target_pairs={{0,8},{8,0},{16,24},{24,16},{1,9},{9,1},{17,25},{25,17},{2,10},{10... | collective-permute-start | bytes 393224 | tf_op jit(solution)/shard_map/ppermute | solution.py:21
  19.9 6.1 %collective-permute-start.17 = (f32[8,2048]{1,0:T(8,128)S(1)}, f32[8,2048]{1,0:T(8,128)S(1)}, u32[]{:S(2)}, u32[]{:S(2)}) collective-permute-start(f32[8,2048]{1,0:T(8,128)S(1)} %slice.36), channel_id=1, source_target_pairs={{8,0},{16,8},{24,16},{9,1},{17,9},{25,17},{10,2},{18,10},{26,18},{... | collective-permute-start | bytes 196616 | tf_op jit(solution)/shard_map/ppermute | solution.py:319
  26.0 19.3 %collective-permute-start.5 = (f16[128,512]{1,0:T(8,128)(2,1)}, f16[128,512]{1,0:T(8,128)(2,1)S(1)}, u32[]{:S(2)}, u32[]{:S(2)}) collective-permute-start(f16[128,512]{1,0:T(8,128)(2,1)} %fusion.58), channel_id=1, source_target_pairs={{0,8},{8,0},{16,24},{24,16},{1,9},{9,1},{17,25},{25,17},{2,10},{10... | collective-permute-start | bytes 393224 | tf_op jit(solution)/shard_map/ppermute | solution.py:21
  37.7 17.2 %collective-permute-start.15 = (f16[128,512]{1,0:T(8,128)(2,1)S(1)}, f16[128,512]{1,0:T(8,128)(2,1)S(1)}, u32[]{:S(2)}, u32[]{:S(2)}) collective-permute-start(f16[128,512]{1,0:T(8,128)(2,1)S(1)} %add_convert_fusion.9), channel_id=1, source_target_pairs={{0,16},{8,24},{16,0},{24,8},{1,17},{9,25},{17,1},{25,9},{2,18},{10... | collective-permute-start | bytes 393224 | tf_op jit(solution)/shard_map/ppermute | solution.py:21
  41.8 16.1 %collective-permute-start.12 = (f16[128,512]{1,0:T(8,128)(2,1)S(1)}, f16[128,512]{1,0:T(8,128)(2,1)S(1)}, u32[]{:S(2)}, u32[]{:S(2)}) collective-permute-start(f16[128,512]{1,0:T(8,128)(2,1)S(1)} %add_convert_fusion.10), channel_id=1, source_target_pairs={{0,16},{8,24},{16,0},{24,8},{1,17},{9,25},{17,1},{25,9},{2,18},{10... | collective-permute-start | bytes 393224 | tf_op jit(solution)/shard_map/ppermute | solution.py:21
  42.6 18.0 %collective-permute-start.9 = (f16[128,512]{1,0:T(8,128)(2,1)S(1)}, f16[128,512]{1,0:T(8,128)(2,1)S(1)}, u32[]{:S(2)}, u32[]{:S(2)}) collective-permute-start(f16[128,512]{1,0:T(8,128)(2,1)S(1)} %add_convert_fusion.11), channel_id=1, source_target_pairs={{0,16},{8,24},{16,0},{24,8},{1,17},{9,25},{17,1},{25,9},{2,18},{10... | collective-permute-start | bytes 393224 | tf_op jit(solution)/shard_map/ppermute | solution.py:21
  45.8 18.0 %collective-permute-start.6 = (f16[128,512]{1,0:T(8,128)(2,1)S(1)}, f16[128,512]{1,0:T(8,128)(2,1)S(1)}, u32[]{:S(2)}, u32[]{:S(2)}) collective-permute-start(f16[128,512]{1,0:T(8,128)(2,1)S(1)} %add_convert_fusion.12), channel_id=1, source_target_pairs={{0,16},{8,24},{16,0},{24,8},{1,17},{9,25},{17,1},{25,9},{2,18},{10... | collective-permute-start | bytes 393224 | tf_op jit(solution)/shard_map/ppermute | solution.py:21
  55.0 10.6 %collective-permute-start.16 = (bf16[128,512]{1,0:T(8,128)(2,1)S(1)}, bf16[128,512]{1,0:T(8,128)(2,1)S(1)}, u32[]{:S(2)}, u32[]{:S(2)}) collective-permute-start(bf16[128,512]{1,0:T(8,128)(2,1)S(1)} %multiply_convert_fusion.5), channel_id=1, source_target_pairs={{0,8},{8,0},{16,24},{24,16},{1,9},{9,1},{17,25},{25,17},{2,10},{10... | collective-permute-start | bytes 393224 | tf_op jit(solution)/shard_map/ppermute | solution.py:21
  57.9 12.5 %collective-permute-start.13 = (bf16[128,512]{1,0:T(8,128)(2,1)S(1)}, bf16[128,512]{1,0:T(8,128)(2,1)S(1)}, u32[]{:S(2)}, u32[]{:S(2)}) collective-permute-start(bf16[128,512]{1,0:T(8,128)(2,1)S(1)} %multiply_convert_fusion.6), channel_id=1, source_target_pairs={{0,8},{8,0},{16,24},{24,16},{1,9},{9,1},{17,25},{25,17},{2,10},{10... | collective-permute-start | bytes 393224 | tf_op jit(solution)/shard_map/ppermute | solution.py:21
  60.7 10.4 %collective-permute-start.10 = (bf16[128,512]{1,0:T(8,128)(2,1)S(1)}, bf16[128,512]{1,0:T(8,128)(2,1)S(1)}, u32[]{:S(2)}, u32[]{:S(2)}) collective-permute-start(bf16[128,512]{1,0:T(8,128)(2,1)S(1)} %multiply_convert_fusion.7), channel_id=1, source_target_pairs={{0,8},{8,0},{16,24},{24,16},{1,9},{9,1},{17,25},{25,17},{2,10},{10... | collective-permute-start | bytes 393224 | tf_op jit(solution)/shard_map/ppermute | solution.py:21
  62.2 6.5 %collective-permute-start.1 = (f32[256,256]{1,0:T(8,128)S(1)}, f32[256,256]{1,0:T(8,128)S(1)}, u32[]{:S(2)}, u32[]{:S(2)}) collective-permute-start(f32[256,256]{1,0:T(8,128)S(1)} %constant_dynamic-slice_fusion.5), channel_id=1, source_target_pairs={{0,2},{1,3},{2,0},{3,1},{4,6},{5,7},{6,4},{7,5},{8,10},{9,11},{10,... | collective-permute-start | bytes 786440 | tf_op jit(solution)/shard_map/ppermute | solution.py:21
  63.8 13.1 %collective-permute-start.7 = (bf16[128,512]{1,0:T(8,128)(2,1)S(1)}, bf16[128,512]{1,0:T(8,128)(2,1)S(1)}, u32[]{:S(2)}, u32[]{:S(2)}) collective-permute-start(bf16[128,512]{1,0:T(8,128)(2,1)S(1)} %multiply_convert_fusion.8), channel_id=1, source_target_pairs={{0,8},{8,0},{16,24},{24,16},{1,9},{9,1},{17,25},{25,17},{2,10},{10... | collective-permute-start | bytes 393224 | tf_op jit(solution)/shard_map/ppermute | solution.py:21
  68.8 6.4 %collective-permute-start.2 = (f32[256,256]{1,0:T(8,128)S(1)}, f32[256,256]{1,0:T(8,128)S(1)}, u32[]{:S(2)}, u32[]{:S(2)}) collective-permute-start(f32[256,256]{1,0:T(8,128)S(1)} %dynamic-slice_add_fusion.5), channel_id=1, source_target_pairs={{0,4},{1,5},{2,6},{3,7},{4,0},{5,1},{6,2},{7,3},{8,12},{9,13},{10,... | collective-permute-start | bytes 786440 | tf_op jit(solution)/shard_map/ppermute | solution.py:21
  75.3 5.0 %collective-permute-start.3 = (bf16[256,256]{1,0:T(8,128)(2,1)S(1)}, bf16[256,256]{1,0:T(8,128)(2,1)S(1)}, u32[]{:S(2)}, u32[]{:S(2)}) collective-permute-start(bf16[256,256]{1,0:T(8,128)(2,1)S(1)} %multiply_convert_fusion.9), channel_id=1, source_target_pairs={{0,2},{1,3},{2,0},{3,1},{4,6},{5,7},{6,4},{7,5},{8,10},{9,11},{10,... | collective-permute-start | bytes 393224 | tf_op jit(solution)/shard_map/ppermute | solution.py:21
  83.5 20.7 %collective-permute-start.26 = (f32[8,128]{1,0:T(8,128)S(1)}, f32[8,128]{1,0:T(8,128)S(1)}, u32[]{:S(2)}, u32[]{:S(2)}) collective-permute-start(f32[8,128]{1,0:T(8,128)S(1)} %broadcast_in_dim.3), channel_id=1, source_target_pairs={{0,8},{8,0},{16,24},{24,16},{1,9},{9,1},{17,25},{25,17},{2,10},{10... | collective-permute-start | bytes 12296 | tf_op jit(solution)/shard_map/ppermute | solution.py:21
  104.9 4.6 %collective-permute-start.27 = (f32[8,128]{1,0:T(8,128)S(1)}, f32[8,128]{1,0:T(8,128)S(1)}, u32[]{:S(2)}, u32[]{:S(2)}) collective-permute-start(f32[8,128]{1,0:T(8,128)S(1)} %broadcast_maximum_fusion), channel_id=1, source_target_pairs={{0,16},{8,24},{16,0},{24,8},{1,17},{9,25},{17,1},{25,9},{2,18},{10... | collective-permute-start | bytes 12296 | tf_op jit(solution)/shard_map/ppermute | solution.py:21
  107.5 47.3 %collective-permute-start.18 = (f32[512,256]{1,0:T(8,128)}, f32[512,256]{1,0:T(8,128)}, u32[]{:S(2)}, u32[]{:S(2)}) collective-permute-start(f32[512,256]{1,0:T(8,128)} %constant_dynamic-slice_fusion.3), channel_id=1, source_target_pairs={{0,1},{1,0},{2,3},{3,2},{4,5},{5,4},{6,7},{7,6},{8,9},{9,8},{10,11... | collective-permute-start | bytes 1572872 | tf_op jit(solution)/shard_map/ppermute | solution.py:21
  113.0 6.5 %collective-permute-start.28 = (f16[128,512]{1,0:T(8,128)(2,1)}, f16[128,512]{1,0:T(8,128)(2,1)S(1)}, u32[]{:S(2)}, u32[]{:S(2)}) collective-permute-start(f16[128,512]{1,0:T(8,128)(2,1)} %dynamic-slice_convert_fusion.6), channel_id=1, source_target_pairs={{0,8},{8,0},{16,24},{24,16},{1,9},{9,1},{17,25},{25,17},{2,10},{10... | collective-permute-start | bytes 393224 | tf_op jit(solution)/shard_map/ppermute | solution.py:21
  113.8 12.7 %collective-permute-start.31 = (f16[128,512]{1,0:T(8,128)(2,1)S(1)}, f16[128,512]{1,0:T(8,128)(2,1)S(1)}, u32[]{:S(2)}, u32[]{:S(2)}) collective-permute-start(f16[128,512]{1,0:T(8,128)(2,1)S(1)} %dynamic-slice_convert_fusion.5), channel_id=1, source_target_pairs={{0,8},{8,0},{16,24},{24,16},{1,9},{9,1},{17,25},{25,17},{2,10},{10... | collective-permute-start | bytes 393224 | tf_op jit(solution)/shard_map/ppermute | solution.py:21
  116.5 13.0 %collective-permute-start.34 = (f16[128,512]{1,0:T(8,128)(2,1)S(1)}, f16[128,512]{1,0:T(8,128)(2,1)S(1)}, u32[]{:S(2)}, u32[]{:S(2)}) collective-permute-start(f16[128,512]{1,0:T(8,128)(2,1)S(1)} %dynamic-slice_convert_fusion.4), channel_id=1, source_target_pairs={{0,8},{8,0},{16,24},{24,16},{1,9},{9,1},{17,25},{25,17},{2,10},{10... | collective-permute-start | bytes 393224 | tf_op jit(solution)/shard_map/ppermute | solution.py:21
  117.3 13.6 %collective-permute-start.37 = (f16[128,512]{1,0:T(8,128)(2,1)S(1)}, f16[128,512]{1,0:T(8,128)(2,1)S(1)}, u32[]{:S(2)}, u32[]{:S(2)}) collective-permute-start(f16[128,512]{1,0:T(8,128)(2,1)S(1)} %dynamic-slice_convert_fusion.3), channel_id=1, source_target_pairs={{0,8},{8,0},{16,24},{24,16},{1,9},{9,1},{17,25},{25,17},{2,10},{10... | collective-permute-start | bytes 393224 | tf_op jit(solution)/shard_map/ppermute | solution.py:21
  119.5 13.1 %collective-permute-start.29 = (f16[128,512]{1,0:T(8,128)(2,1)S(1)}, f16[128,512]{1,0:T(8,128)(2,1)S(1)}, u32[]{:S(2)}, u32[]{:S(2)}) collective-permute-start(f16[128,512]{1,0:T(8,128)(2,1)S(1)} %add_convert_fusion.8), channel_id=1, source_target_pairs={{0,16},{8,24},{16,0},{24,8},{1,17},{9,25},{17,1},{25,9},{2,18},{10... | collective-permute-start | bytes 393224 | tf_op jit(solution)/shard_map/ppermute | solution.py:21
  126.6 14.8 %collective-permute-start.32 = (f16[128,512]{1,0:T(8,128)(2,1)S(1)}, f16[128,512]{1,0:T(8,128)(2,1)S(1)}, u32[]{:S(2)}, u32[]{:S(2)}) collective-permute-start(f16[128,512]{1,0:T(8,128)(2,1)S(1)} %add_convert_fusion.7), channel_id=1, source_target_pairs={{0,16},{8,24},{16,0},{24,8},{1,17},{9,25},{17,1},{25,9},{2,18},{10... | collective-permute-start | bytes 393224 | tf_op jit(solution)/shard_map/ppermute | solution.py:21
  129.6 13.7 %collective-permute-start.35 = (f16[128,512]{1,0:T(8,128)(2,1)S(1)}, f16[128,512]{1,0:T(8,128)(2,1)S(1)}, u32[]{:S(2)}, u32[]{:S(2)}) collective-permute-start(f16[128,512]{1,0:T(8,128)(2,1)S(1)} %add_convert_fusion.6), channel_id=1, source_target_pairs={{0,16},{8,24},{16,0},{24,8},{1,17},{9,25},{17,1},{25,9},{2,18},{10... | collective-permute-start | bytes 393224 | tf_op jit(solution)/shard_map/ppermute | solution.py:21
  131.0 13.7 %collective-permute-start.38 = (f16[128,512]{1,0:T(8,128)(2,1)S(1)}, f16[128,512]{1,0:T(8,128)(2,1)S(1)}, u32[]{:S(2)}, u32[]{:S(2)}) collective-permute-start(f16[128,512]{1,0:T(8,128)(2,1)S(1)} %add_convert_fusion.5), channel_id=1, source_target_pairs={{0,16},{8,24},{16,0},{24,8},{1,17},{9,25},{17,1},{25,9},{2,18},{10... | collective-permute-start | bytes 393224 | tf_op jit(solution)/shard_map/ppermute | solution.py:21
  132.7 20.9 %collective-permute-start.30 = (bf16[128,512]{1,0:T(8,128)(2,1)S(1)}, bf16[128,512]{1,0:T(8,128)(2,1)S(1)}, u32[]{:S(2)}, u32[]{:S(2)}) collective-permute-start(bf16[128,512]{1,0:T(8,128)(2,1)S(1)} %multiply_convert_fusion.3), channel_id=1, source_target_pairs={{0,8},{8,0},{16,24},{24,16},{1,9},{9,1},{17,25},{25,17},{2,10},{10... | collective-permute-start | bytes 393224 | tf_op jit(solution)/shard_map/ppermute | solution.py:21
  141.4 6.5 %collective-permute-start.33 = (bf16[128,512]{1,0:T(8,128)(2,1)S(1)}, bf16[128,512]{1,0:T(8,128)(2,1)S(1)}, u32[]{:S(2)}, u32[]{:S(2)}) collective-permute-start(bf16[128,512]{1,0:T(8,128)(2,1)S(1)} %multiply_convert_fusion.2), channel_id=1, source_target_pairs={{0,8},{8,0},{16,24},{24,16},{1,9},{9,1},{17,25},{25,17},{2,10},{10... | collective-permute-start | bytes 393224 | tf_op jit(solution)/shard_map/ppermute | solution.py:21
  143.3 7.1 %collective-permute-start.36 = (bf16[128,512]{1,0:T(8,128)(2,1)S(1)}, bf16[128,512]{1,0:T(8,128)(2,1)S(1)}, u32[]{:S(2)}, u32[]{:S(2)}) collective-permute-start(bf16[128,512]{1,0:T(8,128)(2,1)S(1)} %multiply_convert_fusion.1), channel_id=1, source_target_pairs={{0,8},{8,0},{16,24},{24,16},{1,9},{9,1},{17,25},{25,17},{2,10},{10... | collective-permute-start | bytes 393224 | tf_op jit(solution)/shard_map/ppermute | solution.py:21
  144.7 8.1 %collective-permute-start.39 = (bf16[128,512]{1,0:T(8,128)(2,1)S(1)}, bf16[128,512]{1,0:T(8,128)(2,1)S(1)}, u32[]{:S(2)}, u32[]{:S(2)}) collective-permute-start(bf16[128,512]{1,0:T(8,128)(2,1)S(1)} %multiply_convert_fusion), channel_id=1, source_target_pairs={{0,8},{8,0},{16,24},{24,16},{1,9},{9,1},{17,25},{25,17},{2,10},{10... | collective-permute-start | bytes 393224 | tf_op jit(solution)/shard_map/ppermute | solution.py:21
  154.7 11.6 %collective-permute-start.40 = (f32[64,2048]{1,0:T(8,128)S(1)}, f32[64,2048]{1,0:T(8,128)S(1)}, u32[]{:S(2)}, u32[]{:S(2)}) collective-permute-start(f32[64,2048]{1,0:T(8,128)S(1)} %constant_dynamic-slice_fusion.1), channel_id=1, source_target_pairs={{0,1},{1,0},{2,3},{3,2},{4,5},{5,4},{6,7},{7,6},{8,9},{9,8},{10,11... | collective-permute-start | bytes 1572872 | tf_op jit(solution)/shard_map/ppermute | solution.py:21
  156.9 7.9 %collective-permute-start.19 = (f32[256,256]{1,0:T(8,128)S(1)}, f32[256,256]{1,0:T(8,128)S(1)}, u32[]{:S(2)}, u32[]{:S(2)}) collective-permute-start(f32[256,256]{1,0:T(8,128)S(1)} %constant_dynamic-slice_fusion.2), channel_id=1, source_target_pairs={{0,2},{1,3},{2,0},{3,1},{4,6},{5,7},{6,4},{7,5},{8,10},{9,11},{10,... | collective-permute-start | bytes 786440 | tf_op jit(solution)/shard_map/ppermute | solution.py:21
  159.3 8.7 %collective-permute-start.45 = (f32[64,2048]{1,0:T(8,128)S(1)}, f32[64,2048]{1,0:T(8,128)S(1)}, u32[]{:S(2)}, u32[]{:S(2)}) collective-permute-start(f32[64,2048]{1,0:T(8,128)S(1)} %constant_dynamic-slice_fusion), channel_id=1, source_target_pairs={{0,1},{1,0},{2,3},{3,2},{4,5},{5,4},{6,7},{7,6},{8,9},{9,8},{10,11... | collective-permute-start | bytes 1572872 | tf_op jit(solution)/shard_map/ppermute | solution.py:21
  164.8 8.3 %collective-permute-start.20 = (f32[256,256]{1,0:T(8,128)S(1)}, f32[256,256]{1,0:T(8,128)S(1)}, u32[]{:S(2)}, u32[]{:S(2)}) collective-permute-start(f32[256,256]{1,0:T(8,128)S(1)} %dynamic-slice_add_fusion.4), channel_id=1, source_target_pairs={{0,4},{1,5},{2,6},{3,7},{4,0},{5,1},{6,2},{7,3},{8,12},{9,13},{10,... | collective-permute-start | bytes 786440 | tf_op jit(solution)/shard_map/ppermute | solution.py:21
  166.4 8.8 %collective-permute-start.41 = (bf16[32,2048]{1,0:T(8,128)(2,1)S(1)}, bf16[32,2048]{1,0:T(8,128)(2,1)S(1)}, u32[]{:S(2)}, u32[]{:S(2)}) collective-permute-start(bf16[32,2048]{1,0:T(8,128)(2,1)S(1)} %dynamic-slice_convert_fusion.2), channel_id=1, source_target_pairs={{0,2},{1,3},{2,0},{3,1},{4,6},{5,7},{6,4},{7,5},{8,10},{9,11},{10,... | collective-permute-start | bytes 393224 | tf_op jit(solution)/shard_map/ppermute | solution.py:21
  168.1 8.8 %collective-permute-start.46 = (bf16[32,2048]{1,0:T(8,128)(2,1)S(1)}, bf16[32,2048]{1,0:T(8,128)(2,1)S(1)}, u32[]{:S(2)}, u32[]{:S(2)}) collective-permute-start(bf16[32,2048]{1,0:T(8,128)(2,1)S(1)} %dynamic-slice_convert_fusion.1), channel_id=1, source_target_pairs={{0,4},{1,5},{2,6},{3,7},{4,0},{5,1},{6,2},{7,3},{8,12},{9,13},{10,... | collective-permute-start | bytes 393224 | tf_op jit(solution)/shard_map/ppermute | solution.py:21
  173.2 5.0 %collective-permute-start.21 = (bf16[256,256]{1,0:T(8,128)(2,1)S(1)}, bf16[256,256]{1,0:T(8,128)(2,1)S(1)}, u32[]{:S(2)}, u32[]{:S(2)}) collective-permute-start(bf16[256,256]{1,0:T(8,128)(2,1)S(1)} %multiply_convert_fusion.4), channel_id=1, source_target_pairs={{0,2},{1,3},{2,0},{3,1},{4,6},{5,7},{6,4},{7,5},{8,10},{9,11},{10,... | collective-permute-start | bytes 393224 | tf_op jit(solution)/shard_map/ppermute | solution.py:21
  175.3 5.0 %collective-permute-start.42 = (bf16[32,2048]{1,0:T(8,128)(2,1)S(1)}, bf16[32,2048]{1,0:T(8,128)(2,1)S(1)}, u32[]{:S(2)}, u32[]{:S(2)}) collective-permute-start(bf16[32,2048]{1,0:T(8,128)(2,1)S(1)} %add_convert_fusion.4), channel_id=1, source_target_pairs={{0,4},{1,5},{2,6},{3,7},{4,0},{5,1},{6,2},{7,3},{8,12},{9,13},{10,... | collective-permute-start | bytes 393224 | tf_op jit(solution)/shard_map/ppermute | solution.py:21
  176.9 5.1 %collective-permute-start.47 = (bf16[32,2048]{1,0:T(8,128)(2,1)S(1)}, bf16[32,2048]{1,0:T(8,128)(2,1)S(1)}, u32[]{:S(2)}, u32[]{:S(2)}) collective-permute-start(bf16[32,2048]{1,0:T(8,128)(2,1)S(1)} %add_convert_fusion.2), channel_id=1, source_target_pairs={{0,2},{1,3},{2,0},{3,1},{4,6},{5,7},{6,4},{7,5},{8,10},{9,11},{10,... | collective-permute-start | bytes 393224 | tf_op jit(solution)/shard_map/ppermute | solution.py:21
  178.3 8.9 %collective-permute-start.22 = (bf16[512,256]{1,0:T(8,128)(2,1)S(1)}, bf16[512,256]{1,0:T(8,128)(2,1)S(1)}, u32[]{:S(2)}, u32[]{:S(2)}) collective-permute-start(bf16[512,256]{1,0:T(8,128)(2,1)S(1)} %pad_maximum_fusion.6), channel_id=1, source_target_pairs={{0,1},{1,0},{2,3},{3,2},{4,5},{5,4},{6,7},{7,6},{8,9},{9,8},{10,11... | collective-permute-start | bytes 786440 | tf_op jit(solution)/shard_map/ppermute | solution.py:21
  180.3 5.0 %collective-permute-start.43 = (bf16[32,2048]{1,0:T(8,128)(2,1)S(1)}, bf16[32,2048]{1,0:T(8,128)(2,1)S(1)}, u32[]{:S(2)}, u32[]{:S(2)}) collective-permute-start(bf16[32,2048]{1,0:T(8,128)(2,1)S(1)} %add_convert_fusion.3), channel_id=1, source_target_pairs={{0,2},{1,3},{2,0},{3,1},{4,6},{5,7},{6,4},{7,5},{8,10},{9,11},{10,... | collective-permute-start | bytes 393224 | tf_op jit(solution)/shard_map/ppermute | solution.py:21
  182.1 5.0 %collective-permute-start.48 = (bf16[32,2048]{1,0:T(8,128)(2,1)S(1)}, bf16[32,2048]{1,0:T(8,128)(2,1)S(1)}, u32[]{:S(2)}, u32[]{:S(2)}) collective-permute-start(bf16[32,2048]{1,0:T(8,128)(2,1)S(1)} %add_convert_fusion.1), channel_id=1, source_target_pairs={{0,4},{1,5},{2,6},{3,7},{4,0},{5,1},{6,2},{7,3},{8,12},{9,13},{10,... | collective-permute-start | bytes 393224 | tf_op jit(solution)/shard_map/ppermute | solution.py:21
  187.2 11.3 %collective-permute-start.49 = (bf16[64,2048]{1,0:T(8,128)(2,1)S(1)}, bf16[64,2048]{1,0:T(8,128)(2,1)S(1)}, u32[]{:S(2)}, u32[]{:S(2)}) collective-permute-start(bf16[64,2048]{1,0:T(8,128)(2,1)S(1)} %pad_maximum_fusion.8), channel_id=1, source_target_pairs={{0,1},{1,0},{2,3},{3,2},{4,5},{5,4},{6,7},{7,6},{8,9},{9,8},{10,11... | collective-permute-start | bytes 786440 | tf_op jit(solution)/shard_map/ppermute | solution.py:21
  188.1 8.8 %collective-permute-start.23 = (bf16[512,256]{0,1:T(8,128)(2,1)S(1)}, bf16[512,256]{0,1:T(8,128)(2,1)S(1)}, u32[]{:S(2)}, u32[]{:S(2)}) collective-permute-start(bf16[512,256]{0,1:T(8,128)(2,1)S(1)} %fusion.74), channel_id=1, source_target_pairs={{0,8},{8,0},{16,24},{24,16},{1,9},{9,1},{17,25},{25,17},{2,10},{10... | collective-permute-start | bytes 786440 | tf_op jit(solution)/shard_map/ppermute | solution.py:21
  197.0 14.4 %collective-permute-start.24 = (bf16[512,256]{0,1:T(8,128)(2,1)S(1)}, bf16[512,256]{0,1:T(8,128)(2,1)S(1)}, u32[]{:S(2)}, u32[]{:S(2)}) collective-permute-start(bf16[512,256]{0,1:T(8,128)(2,1)S(1)} %fusion.65), channel_id=1, source_target_pairs={{0,16},{8,24},{16,0},{24,8},{1,17},{9,25},{17,1},{25,9},{2,18},{10... | collective-permute-start | bytes 786440 | tf_op jit(solution)/shard_map/ppermute | solution.py:21
  211.5 8.3 %collective-permute-start.25 = (bf16[512,256]{0,1:T(8,128)(2,1)S(1)}, bf16[512,256]{0,1:T(8,128)(2,1)S(1)}, u32[]{:S(2)}, u32[]{:S(2)}) collective-permute-start(bf16[512,256]{0,1:T(8,128)(2,1)S(1)} %add_convert_fusion), channel_id=1, source_target_pairs={{0,8},{8,0},{16,24},{24,16},{1,9},{9,1},{17,25},{25,17},{2,10},{10... | collective-permute-start | bytes 786440 | tf_op jit(solution)/shard_map/ppermute | solution.py:21
  (28 other events, 209.1 us)

commit v3 on v2

--- a/solution.py
+++ b/solution.py
@@ -30,25 +30,6 @@
     return lax.dynamic_slice_in_dim(value, which * rows, rows, 0)
 
 
-def reduce_bits(part, axis, bits, wires):
-    for bit, wire in zip(bits[:-1], wires):
-        mine = own_bit(axis, bit)
-        arrived = swap(half(part, 1 - mine).astype(wire), axis, bit)
-        part = half(part, mine) + arrived.astype(F32)
-    sent = part.astype(wires[-1])
-    return sent.astype(F32) + swap(sent, axis, bits[-1]).astype(F32)
-
-
-def gather_bits(piece, axis, bits):
-    for bit in reversed(bits[:-1]):
-        mine = own_bit(axis, bit)
-        other = swap(piece, axis, bit)
-        low = jnp.where(mine == 0, piece, other)
-        high = jnp.where(mine == 0, other, piece)
-        piece = jnp.concatenate((low, high), 0)
-    return piece
-
-
 def silu_slope(values):
     sigma = jax.nn.sigmoid(values)
     return sigma * (1.0 + values * (1.0 - sigma))
@@ -82,7 +63,7 @@
 
 
 def cost(flops, read, exps):
-    return pl.CostEstimate(flops=flops, bytes_accessed=read, transcendentals=exps)
+    return pl.CostEstimate(flops=flops // 4096, bytes_accessed=read // 4096, transcendentals=0)
 
 
 def row_spec(block, cols, column=0):
@@ -123,9 +104,47 @@
         out_specs=[row_spec(block, 1)] * 2,
         out_shape=[jax.ShapeDtypeStruct((rows, 1), F32)] * 2,
         scratch_shapes=[pltpu.VMEM((block + 8, cols), F32)],
-        compiler_params=params(24),
+        compiler_params=params(50),
         cost_estimate=cost(4 * rows * cols, 4 * rows * cols, rows * cols),
         name="target_sums",
+    )(target, target, incoming)
+
+
+def target_pass(target, incoming):
+    rows, cols = target.shape
+    block = min(BLOCK, rows)
+
+    def body(target_ref, next_ref, incoming_ref, prob_ref, entropy_ref, window):
+        shifted = shift_in(target_ref, next_ref, incoming_ref, window)
+        first = lax.axis_index("grp") * rows + pl.program_id(0) * block
+        count = lax.axis_size("grp") * rows
+        row = first + lax.broadcasted_iota(jnp.int32, (block, 1), 0)
+        live = jnp.where(row < count - HEAD, 1.0, 0.0)
+        below = shifted - jnp.max(shifted, -1, keepdims=True)
+        raised = jnp.exp(below)
+        total = jnp.sum(raised, -1, keepdims=True)
+        scale = live / total
+        prob_ref[...] = raised * scale
+        entropy_ref[...] = scale * jnp.sum(raised * below, -1, keepdims=True) - live * jnp.log(total)
+
+    per = block // 8
+    return pl.pallas_call(
+        body,
+        grid=(rows // block,),
+        in_specs=[
+            row_spec(block, cols),
+            pl.BlockSpec((8, cols), lambda i: (jnp.minimum((i + 1) * per, rows // 8 - 1), 0)),
+            whole_spec(8, cols),
+        ],
+        out_specs=[row_spec(block, cols), row_spec(block, 1)],
+        out_shape=[
+            jax.ShapeDtypeStruct((rows, cols), F32),
+            jax.ShapeDtypeStruct((rows, 1), F32),
+        ],
+        scratch_shapes=[pltpu.VMEM((block + 8, cols), F32)],
+        compiler_params=params(50),
+        cost_estimate=cost(6 * rows * cols, 8 * rows * cols, rows * cols),
+        name="target_pass",
     )(target, target, incoming)
 
 
@@ -161,7 +180,7 @@
             jax.ShapeDtypeStruct((rows, 1), F32),
         ],
         scratch_shapes=[pltpu.VMEM((block + 8, cols), F32)],
-        compiler_params=params(24),
+        compiler_params=params(50),
         cost_estimate=cost(6 * rows * cols, 8 * rows * cols, rows * cols),
         name="target_probs",
     )(target, target, incoming, top, total)
@@ -213,10 +232,11 @@
 def grad_chunk(draft, prob, label, acts, vocab_proj, column, sums, carried):
     rows, width = draft.shape
     rank = acts.shape[1]
+    half_rank = rank // 2
     block = min(BLOCK, rows)
 
     def body(draft_ref, prob_ref, label_ref, acts_ref, proj_ref, top_ref, sum_ref, *rest):
-        grad_ref, act_ref, loss_ref = rest[-3:]
+        away_ref, kept_ref, act_ref, loss_ref, totals = rest[-5:]
         step = pl.program_id(0)
         first = lax.axis_index("grp") * rows + step * block
         count = lax.axis_size("grp") * rows
@@ -238,14 +258,20 @@
 
         @pl.when(step == 0)
         def _():
-            grad_ref[...] = term
+            totals[...] = term
 
         @pl.when(step > 0)
         def _():
-            grad_ref[...] += term
+            totals[...] += term
+
+        @pl.when(step == pl.num_programs(0) - 1)
+        def _():
+            mine = lax.axis_index("grp") & 1
+            away_ref[...] = totals[pl.ds(pl.multiple_of((1 - mine) * half_rank, half_rank), half_rank), :]
+            kept_ref[...] = totals[pl.ds(pl.multiple_of(mine * half_rank, half_rank), half_rank), :]
 
     extra = () if carried is None else tuple(carried)
-    proj_grad, act, loss = pl.pallas_call(
+    away, kept, act, loss = pl.pallas_call(
         body,
         grid=(rows // block,),
         in_specs=[
@@ -258,17 +284,145 @@
             row_spec(block, 1),
         ]
         + ([row_spec(block, rank), row_spec(block, 1)] if extra else []),
-        out_specs=[whole_spec(rank, width), row_spec(block, rank), row_spec(block, 1)],
+        out_specs=[whole_spec(half_rank, width)] * 2 + [row_spec(block, rank), row_spec(block, 1)],
         out_shape=[
-            jax.ShapeDtypeStruct((rank, width), F32),
+            jax.ShapeDtypeStruct((half_rank, width), F32),
+            jax.ShapeDtypeStruct((half_rank, width), F32),
             jax.ShapeDtypeStruct((rows, rank), F32),
             jax.ShapeDtypeStruct((rows, 1), F32),
         ],
+        scratch_shapes=[pltpu.VMEM((rank, width), F32)],
         compiler_params=params(16),
         cost_estimate=cost(4 * rows * rank * width, 8 * rows * width, rows * width),
         name="grad_chunk",
     )(draft, prob, label, acts, vocab_proj, *sums, *extra)
-    return proj_grad, (act, loss)
+    return (away, kept), (act, loss)
+
+
+def vocab_parts(up_weight, head_weight, width, first, end):
+    rank, depth = up_weight.shape
+    rows = rank // 2
+    block = min(512, depth)
+    count = end - first
+
+    def body(up_ref, *rest):
+        heads, outs, totals = rest[:count], rest[count:-1], rest[-1]
+        step = pl.program_id(0)
+        for c, head_ref in enumerate(heads):
+            term = jnp.dot(up_ref[...], head_ref[...], preferred_element_type=F32)
+
+            @pl.when(step == 0)
+            def _():
+                totals[c] = term
+
+            @pl.when(step > 0)
+            def _():
+                totals[c] += term
+
+        @pl.when(step == pl.num_programs(0) - 1)
+        def _():
+            mine = lax.axis_index("grp") & 1
+            for c in range(count):
+                outs[2 * c][...] = totals[c, pl.ds(pl.multiple_of((1 - mine) * rows, rows), rows), :]
+                outs[2 * c + 1][...] = totals[c, pl.ds(pl.multiple_of(mine * rows, rows), rows), :]
+
+    def column_spec(c):
+        return pl.BlockSpec((block, width), lambda k: (k, c))
+
+    outs = pl.pallas_call(
+        body,
+        grid=(depth // block,),
+        in_specs=[pl.BlockSpec((rank, block), lambda k: (0, k))]
+        + [column_spec(first + c) for c in range(count)],
+        out_specs=[pl.BlockSpec((rows, width), lambda k: (0, 0))] * (2 * count),
+        out_shape=[jax.ShapeDtypeStruct((rows, width), F32)] * (2 * count),
+        scratch_shapes=[pltpu.VMEM((count, rank, width), F32)],
+        compiler_params=params(56),
+        cost_estimate=cost(2 * rank * depth * width * count, 2 * depth * width * count, 0),
+        name="vocab_parts",
+    )(up_weight, *([head_weight] * count))
+    return [(outs[2 * c], outs[2 * c + 1]) for c in range(count)]
+
+
+class Line:
+    def __init__(self):
+        self.mark = None
+
+    def after(self, value):
+        if self.mark is None:
+            return value
+        return lax.optimization_barrier((value, self.mark))[0]
+
+    def put(self, value):
+        self.mark = jax.tree.leaves(value)[0]
+        return value
+
+
+class Chain:
+    def __init__(self, steps):
+        self.steps = steps
+        self.value = None
+
+    def step(self, times=1):
+        for _ in range(times):
+            if self.steps is not None:
+                try:
+                    next(self.steps)
+                except StopIteration as end:
+                    self.value = end.value
+                    self.steps = None
+
+    def result(self):
+        while self.steps is not None:
+            self.step()
+        return self.value
+
+
+def sent_over(line, value, axis, bit):
+    value = line.put(line.after(value))
+    arrived = swap(value, axis, bit)
+    yield
+    return line.after(arrived)
+
+
+def reduce_steps(line, pair, axis, bits, wires, scale=None):
+    away, part = pair
+    for index, (bit, wire) in enumerate(zip(bits[:-1], wires)):
+        mine = own_bit(axis, bit)
+        if index > 0:
+            away, part = half(part, 1 - mine), half(part, mine)
+        if scale is not None and index == 0:
+            away, part = away * scale, part * scale
+        arrived = yield from sent_over(line, away.astype(wire), axis, bit)
+        part = part + arrived.astype(F32)
+    sent = part.astype(wires[-1])
+    arrived = yield from sent_over(line, sent, axis, bits[-1])
+    total = sent.astype(F32) + arrived.astype(F32)
+    return total if scale is None else total * (1.0 / scale)
+
+
+def gather_steps(line, piece, axis, bits):
+    for bit in reversed(bits[:-1]):
+        mine = own_bit(axis, bit)
+        other = yield from sent_over(line, piece, axis, bit)
+        low = jnp.where(mine == 0, piece, other)
+        high = jnp.where(mine == 0, other, piece)
+        piece = jnp.concatenate((low, high), 0)
+    return piece
+
+
+def split_pair(part, axis, bits):
+    mine = own_bit(axis, bits[0])
+    return half(part, 1 - mine), half(part, mine)
+
+
+def summed(line, pair, axis, bits, wires, between, scale=None):
+    def steps():
+        total = yield from reduce_steps(line, pair, axis, bits, wires, scale)
+        piece = between(total)
+        return (yield from gather_steps(line, piece, axis, bits))
+
+    return Chain(steps())
 
 
 def on_device(hidden_states, target_logits, labels, down_weight, up_weight, head_weight):
@@ -284,87 +438,161 @@
     z_bits = list(range(group_count.bit_length() - 1))
     v_bits = list(range(lax.axis_size("voc").bit_length() - 1))
     v_other = v_bits[:1] + v_bits[:0:-1]
-
-    def columns(c):
-        return head_weight[:, c * width : (c + 1) * width]
-
-    mine = own_bit("grp", 0)
-    up_away, up_kept = half(up_weight, 1 - mine), half(up_weight, mine)
-    away = [
-        (jnp.dot(up_away, columns(c), preferred_element_type=F32) * VOCAB_SCALE).astype(F16)
-        for c in range(CHUNKS)
-    ]
-    kept = [
-        jnp.dot(up_kept, columns(c), preferred_element_type=F32) * VOCAB_SCALE
-        for c in range(CHUNKS)
-    ]
+    half_wires = [F16] * len(z_bits)
+    line = Line()
+
+    def to_bf16(total):
+        return total.astype(BF16)
+
+    vocab = []
+
+    def start_vocab(pairs):
+        for pair in pairs:
+            vocab.append(
+                summed(line, pair, "grp", z_bits, half_wires, to_bf16, VOCAB_SCALE)
+            )
+
+    start_vocab(vocab_parts(up_weight, head_weight, width, 0, 1))
+    vocab[0].step()
+    pre_part = line.put(
+        jnp.dot(line.after(hidden_states), down_weight, preferred_element_type=F32)
+    )
+    kept_pre = []
+
+    def activate(total):
+        kept_pre.append(total)
+        return jax.nn.silu(total).astype(BF16)
+
+    pre = summed(
+        line, split_pair(pre_part, "voc", v_bits), "voc", v_bits, [F32] * len(v_bits), activate
+    )
+    pre.step()
+    start_vocab(vocab_parts(line.after(up_weight), head_weight, width, 1, CHUNKS))
+    vocab[1].step()
+    vocab[0].step()
+    vocab[2].step()
+    pre.step()
+    vocab[1].step()
+    vocab[3].step()
+    devices = range(group_count)
+    top_rows = line.put(line.after(target_logits[:8]))
+    incoming = lax.ppermute(top_rows, "grp", [(i + 1, i) for i in devices if i + 1 in devices])
+    vocab[0].step()
+    pre.step()
+    vocab[2].step()
+    if per_book == 1:
+        prob, entropy = target_pass(target_logits, line.after(incoming))
+    else:
+        top, total = target_sums(target_logits, incoming)
+        top, total = over_books((top, total), merge_sums, per_book)
+        prob, entropy = target_probs(target_logits, incoming, top, total)
+    line.put(entropy)
+    label = lax.dynamic_slice_in_dim(labels, book_index, 1, 1) - book_part * slice_cols
+    pre.step()
+    vocab[1].step()
+    vocab[3].step()
+    pre.step()
+    vocab[2].step()
+    acts = line.put(pre.result())
+
+    bounds = [jnp.broadcast_to(jnp.max(jnp.abs(acts.astype(F32))), (8, 128))]
+
+    def bound_steps():
+        for bit in z_bits:
+            arrived = yield from sent_over(line, bounds[-1], "grp", bit)
+            bounds.append(jnp.maximum(bounds[-1], arrived))
+
+    bounding = Chain(bound_steps())
+    bounding.step()
+
+    drafts, sums = [], None
     vocab_proj = []
     for c in range(CHUNKS):
-        part = kept[c] + swap(away[c], "grp", 0).astype(F32)
-        total = reduce_bits(part, "grp", z_bits[1:], [F16] * len(z_bits))
-        total = (total * (1.0 / VOCAB_SCALE)).astype(BF16)
-        vocab_proj.append(gather_bits(total, "grp", z_bits))
-
-    pre_part = jnp.dot(hidden_states, down_weight, preferred_element_type=F32)
-    pre_act = reduce_bits(pre_part, "voc", v_bits, [F32] * len(v_bits))
-    acts = gather_bits(jax.nn.silu(pre_act).astype(BF16), "voc", v_bits)
-
-    bound = jnp.broadcast_to(jnp.max(jnp.abs(acts.astype(F32))), (8, 128))
-    for bit in z_bits:
-        bound = jnp.maximum(bound, swap(bound, "grp", bit))
-    most = jnp.maximum(bound[0, 0] * (1.1 * group_count * row_count), 1e-30)
+        vocab_proj.append(line.put(vocab[c].result()))
+        draft, sums = draft_chunk(target_logits, acts, vocab_proj[c], c, sums)
+        drafts.append(line.put(draft))
+        bounding.step()
+        if c == 1:
+            vocab[3].step()
+    bounding.result()
+    most = jnp.maximum(bounds[-1][0, 0] * (1.1 * group_count * row_count), 1e-30)
     grad_scale = jnp.exp2(jnp.floor(15.0 - jnp.log2(most)))
-
-    devices = range(group_count)
-    incoming = lax.ppermute(
-        target_logits[:8], "grp", [(i + 1, i) for i in devices if i + 1 in devices]
+    sums = over_books(tuple(sums), merge_sums, per_book)
+
+    grads, carried = [], None
+    for c in range(CHUNKS):
+        pair, carried = grad_chunk(
+            line.after(drafts[c]), prob, label, acts, vocab_proj[c], c, sums, carried
+        )
+        line.put(pair)
+        grads.append(summed(line, pair, "grp", z_bits, half_wires, to_bf16, grad_scale))
+        grads[c].step()
+        if c > 0:
+            grads[c - 1].step()
+    act_part, loss = carried
+    act = summed(
+        line,
+        split_pair(act_part, "voc", v_bits),
+        "voc",
+        v_bits,
+        [F32] * len(v_bits),
+        lambda total: (total * silu_slope(kept_pre[0])).astype(BF16),
     )
-    top, total = over_books(tuple(target_sums(target_logits, incoming)), merge_sums, per_book)
-    prob, entropy = target_probs(target_logits, incoming, top, total)
-    label = lax.dynamic_slice_in_dim(labels, book_index, 1, 1) - book_part * slice_cols
-
-    drafts, sums = [], None
-    for c in range(CHUNKS):
-        draft, sums = draft_chunk(target_logits, acts, vocab_proj[c], c, sums)
-        drafts.append(draft)
-    sums = over_books(tuple(sums), merge_sums, per_book)
-
-    proj_parts, carried = [], None
-    for c in range(CHUNKS):
-        part, carried = grad_chunk(
-            drafts[c], prob, label, acts, vocab_proj[c], c, sums, carried
-        )
-        proj_parts.append(part)
-    act_part, loss = carried
-
+    act.step()
     loss = over_books(loss + entropy, jnp.add, per_book)
     frame_loss = lax.dynamic_slice_in_dim(loss, book_part * block_rows, block_rows, 0)
     frame_loss = frame_loss.reshape(1, 1, block_rows)
 
+    def columns(c):
+        return head_weight[:, c * width : (c + 1) * width]
+
     up_part = 0.0
-    for c in range(CHUNKS):
-        total = reduce_bits(proj_parts[c] * grad_scale, "grp", z_bits, [F16] * len(z_bits))
-        total = (total * (1.0 / grad_scale)).astype(BF16)
-        up_part = up_part + inner_cols(gather_bits(total, "grp", z_bits), columns(c))
-
-    act_grad = reduce_bits(act_part, "voc", v_bits, [F32] * len(v_bits))
-    pre_grad = gather_bits((act_grad * silu_slope(pre_act)).astype(BF16), "voc", v_bits)
-    down_part = inner_rows(hidden_states, pre_grad)
+
+    def add_up(c):
+        return line.put(up_part + inner_cols(grads[c].result(), columns(c)))
+
+    grads[0].step()
+    act.step()
+    grads[CHUNKS - 1].step()
+    up_part = add_up(0)
+    grads[1].step()
+    act.step()
+    grads[2].step()
+    up_part = add_up(1)
+    act.step()
+    grads[3].step()
+    up_part = add_up(2)
+    act.step()
+    pre_grad = line.put(act.result())
+    down_part = line.put(inner_rows(line.after(hidden_states), pre_grad))
+
+    def final(total):
+        return total.astype(BF16)
 
     def finish(part, axis, bits, wires):
-        total = reduce_bits(part, axis, bits, wires)
-        return gather_bits(total.astype(BF16), axis, bits).astype(F32)
-
+        return summed(line, split_pair(part, axis, bits), axis, bits, wires, final)
+
+    rows = down_part.shape[0] // 2
+    downs = [
+        finish(p, "grp", z_bits, [BF16] * len(z_bits))
+        for p in (down_part[:rows], down_part[rows:])
+    ]
+    downs[0].step()
+    up_part = add_up(3)
     rank = up_part.shape[0] // 2
     wires = [F32] + [BF16] * len(v_bits)
-    grad_b = jnp.concatenate(
-        [
-            finish(p, "voc", o, wires)
-            for p, o in zip((up_part[:rank], up_part[rank:]), (v_bits, v_other))
-        ],
-        0,
-    )
-    grad_a = finish(down_part, "grp", z_bits, [BF16] * len(z_bits))
+    ups = [
+        finish(p, "voc", o, wires)
+        for p, o in zip((up_part[:rank], up_part[rank:]), (v_bits, v_other))
+    ]
+    ups[0].step()
+    ups[1].step()
+    downs[1].step()
+    while any(chain.steps is not None for chain in ups + downs):
+        for chain in (ups[0], ups[1], downs[0], downs[1]):
+            chain.step()
+    grad_b = jnp.concatenate([chain.result().astype(F32) for chain in ups], 0)
+    grad_a = jnp.concatenate([chain.result().astype(F32) for chain in downs], 0)
     return frame_loss, grad_a, grad_b
 
 

time: 222 us -> 192 us (0.86)
  waiting for transfers between devices: 97.4 us -> 42.5 us
  other arithmetic: 11 us -> 26.7 us
  Pallas kernels: 24.1 us -> 39.4 us
  matrix products: 23.4 us -> 13.2 us
  starting transfers between devices: 48.8 us -> 53.3 us
    ppermute x49 -> x52, waiting for transfers between devices: 96.3 us -> 42.5 us  [swap(): return lax.ppermute(value, axis, pairs)]
    pallas_call x2 -> x3, Pallas kernels: 5.39 us -> 20.8 us  [the longest x2 11.7 us: vocab_parts(): pl.pallas_call(body, grid=(depth // block,), in_specs=[pl.BlockSpec((rank...]
    dot_general x9 -> x1, matrix products: 16.3 us -> 1.74 us  [on_device(): jnp.dot(line.after(hidden_states), down_weight, preferred_element_type=F32)]
    convert_element_type x25 -> x33, other arithmetic: 1.85 us -> 15.2 us  [the longest x12 5.83 us: reduce_steps(): sent = part.astype(wires[-1])]
    ppermute x49 -> x52, starting transfers between devices: 47.5 us -> 52 us  [swap(): return lax.ppermute(value, axis, pairs)]
    dot_general x4, matrix products: 6.4 us -> 10.7 us  [inner_cols(): lax.dot_general(left, right, (((1,), (1,)), ((), ())), preferred_element_...]
    unnamed x54 -> x49, local copies, waits for them, and re-layouts: 9.28 us -> 5.66 us
  transfers between devices with their start and end apart: 50 -> 53, of which waited for: 28 -> 21; matrix products, arithmetic and copies ran while one was open for 16% -> 21% of each run, Pallas kernels for 11% -> 16%
where the time goes in v3:
time: 192 us; the launch traced here: 191 us
  starting transfers between devices  53.3 us (28%)
  waiting for transfers between devices  42.5 us (22%)
  Pallas kernels  39.4 us (21%)
  other arithmetic  26.7 us (14%)
  local copies, waits for them, and re-layouts  14 us (7%)
  matrix products  13.2 us (7%)
  between operations  2.26 us (1%)
    ppermute x52, starting transfers between devices, swap(): return lax.ppermute(value, axis, pairs)  52 us
    ppermute x52, waiting for transfers between devices, swap(): return lax.ppermute(value, axis, pairs)  42.5 us
    pallas_call x2, Pallas kernels, vocab_parts(): pl.pallas_call(body, grid=(depth // block,), in_specs=[pl.BlockSpec((rank...  11.7 us
    dot_general x4, matrix products, inner_cols(): lax.dot_general(left, right, (((1,), (1,)), ((), ())), preferred_element_...  10.7 us
    pallas_call x4, Pallas kernels, grad_chunk(): pl.pallas_call(body, grid=(rows // block,), in_specs=[row_spec(block, wid...  10.6 us
    pallas_call x1, Pallas kernels, target_pass(): pl.pallas_call(body, grid=(rows // block,), in_specs=[row_spec(block, col...  9.1 us
    pallas_call x4, Pallas kernels, draft_chunk(): pl.pallas_call(body, grid=(rows // block,), in_specs=[row_spec(block, wid...  8 us
    convert_element_type x12, other arithmetic, reduce_steps(): sent = part.astype(wires[-1])  5.83 us
  transfers between devices with their start and end apart: 53, of which 21 were waited for; matrix products, arithmetic and copies ran while one was open for 21% of the time, Pallas kernels for 16%

profile of v3, /device:TPU:0, one launch (start us, length us, event | category | flops | bytes accessed | tf_op | source)
XLA Modules:
  0.0 191.4 jit_solution(3433019338301459350)
XLA Ops:
  0.6 4.4 %vocab_parts.2 = (f32[128,512]{1,0:T(8,128)}, f32[128,512]{1,0:T(8,128)}) custom-call(bf16[256,2048]{1,0:T(8,128)(2,1)} %up_ref.2, bf16[2048,2048]{1,0:T(8,128)(2,1)} %rest_2_.1), custom_call_target="tpu_custom_call" | custom-call | flops 131072 | bytes 512 | tf_op jit(solution)/shard_map/vocab_parts/pallas_call | solution.py:332
  6.0 3.1 %collective-permute-start.1 = (f16[128,512]{1,0:T(8,128)(2,1)S(1)}, f16[128,512]{1,0:T(8,128)(2,1)S(1)}, u32[]{:S(2)}, u32[]{:S(2)}) collective-permute-start(f16[128,512]{1,0:T(8,128)(2,1)S(1)} %multiply_convert_fusion.17), channel_id=1, source_target_pairs={{0,8},{8,0},{16,24},{24,16},{1,9},{9,1},{17,25},{25,17},{2,10},{10... | collective-permute-start | bytes 393224 | tf_op jit(solution)/shard_map/ppermute | solution.py:21
  9.1 1.7 fusion.24
  11.7 7.3 %vocab_parts.3 = (f32[128,512]{1,0:T(8,128)}, f32[128,512]{1,0:T(8,128)}, f32[128,512]{1,0:T(8,128)}, f32[128,512]{1,0:T(8,128)}, f32[128,512]{1,0:T(8,128)}, /*index=5*/f32[128,512]{1,0:T(8,128)}) custom-call(bf16[256,2048]{1,0:T(8,128)(2,1)} %up_ref.2, bf16[2048,2048]{1,0:T(8,128)(2,1)} %rest_2_.1, bf16[2048,2048]{1,0:T(8,128)(2,1)} %rest_2_.1, ...), custom_call_target="tpu_custom_call" | custom-call | flops 393216 | bytes 1536 | tf_op jit(solution)/shard_map/vocab_parts/pallas_call | solution.py:332
  19.0 1.6 multiply_convert_fusion.15
  22.1 1.7 multiply_convert_fusion.16
  25.5 3.1 %collective-permute-start.3 = (f16[128,512]{1,0:T(8,128)(2,1)S(1)}, f16[128,512]{1,0:T(8,128)(2,1)S(1)}, u32[]{:S(2)}, u32[]{:S(2)}) collective-permute-start(f16[128,512]{1,0:T(8,128)(2,1)S(1)} %add_convert_fusion.15), channel_id=1, source_target_pairs={{0,16},{8,24},{16,0},{24,8},{1,17},{9,25},{17,1},{25,9},{2,18},{10... | collective-permute-start | bytes 393224 | tf_op jit(solution)/shard_map/ppermute | solution.py:21
  28.6 1.6 collective-permute-start.7
  33.6 1.8 collective-permute-done.3
  35.5 3.8 %collective-permute-done.2 = f32[256,256]{1,0:T(8,128)S(1)} collective-permute-done((f32[256,256]{1,0:T(8,128)S(1)}, f32[256,256]{1,0:T(8,128)S(1)}, u32[]{:S(2)}, u32[]{:S(2)}) %collective-permute-start.2) | collective-permute-done | bytes 262176 | tf_op jit(solution)/shard_map/ppermute | solution.py:21
  39.3 1.6 collective-permute-start.5
  42.2 2.6 %collective-permute-start.10 = (f16[128,512]{1,0:T(8,128)(2,1)S(1)}, f16[128,512]{1,0:T(8,128)(2,1)S(1)}, u32[]{:S(2)}, u32[]{:S(2)}) collective-permute-start(f16[128,512]{1,0:T(8,128)(2,1)S(1)} %get-tuple-element.169), channel_id=1, source_target_pairs={{0,16},{8,24},{16,0},{24,8},{1,17},{9,25},{17,1},{25,9},{2,18},{10... | collective-permute-start | bytes 393224 | tf_op jit(solution)/shard_map/ppermute | solution.py:21
  45.3 1.7 add_convert_fusion.13
  47.0 2.6 %collective-permute-start.12 = (f16[128,512]{1,0:T(8,128)(2,1)}, f16[128,512]{1,0:T(8,128)(2,1)}, u32[]{:S(2)}, u32[]{:S(2)}) collective-permute-start(f16[128,512]{1,0:T(8,128)(2,1)} %add_convert_fusion.13), channel_id=1, source_target_pairs={{0,16},{8,24},{16,0},{24,8},{1,17},{9,25},{17,1},{25,9},{2,18},{10... | collective-permute-start | bytes 393224 | tf_op jit(solution)/shard_map/ppermute | solution.py:21
  49.6 9.1 %target_pass.1 = (f32[1024,2048]{1,0:T(8,128)}, f32[1024,1]{1,0:T(8,128)S(1)}) custom-call(f32[1024,2048]{1,0:T(8,128)} %target_ref.9, f32[1024,2048]{1,0:T(8,128)} %target_ref.9, f32[8,2048]{1,0:T(8,128)S(1)} %collective-permute-done.6.incoming_ref), custom_call_target="tpu_custom_call" | custom-call | flops 3072 | bytes 4096 | tf_op jit(solution)/shard_map/target_pass/pallas_call | solution.py:131
  61.7 2.1 %collective-permute-done.8 = bf16[256,256]{1,0:T(8,128)(2,1)S(1)} collective-permute-done((bf16[256,256]{1,0:T(8,128)(2,1)S(1)}, bf16[256,256]{1,0:T(8,128)(2,1)S(1)}, u32[]{:S(2)}, u32[]{:S(2)}) %collective-permute-start.8) | collective-permute-done | bytes 131104 | tf_op jit(solution)/shard_map/ppermute | solution.py:21
  65.6 2.0 %collective-permute-start.14 = (bf16[128,512]{1,0:T(8,128)(2,1)}, bf16[128,512]{1,0:T(8,128)(2,1)S(1)}, u32[]{:S(2)}, u32[]{:S(2)}) collective-permute-start(bf16[128,512]{1,0:T(8,128)(2,1)} %multiply_convert_fusion.11), channel_id=1, source_target_pairs={{0,8},{8,0},{16,24},{24,16},{1,9},{9,1},{17,25},{25,17},{2,10},{10... | collective-permute-start | bytes 393224 | tf_op jit(solution)/shard_map/ppermute | solution.py:21
  71.4 1.6 collective-permute-start.15
  73.0 1.7 collective-permute-done.16
  74.8 3.4 %copy-done.1 = f32[1024,2048]{1,0:T(8,128)S(1)} copy-done((f32[1024,2048]{1,0:T(8,128)S(1)}, f32[1024,2048]{1,0:T(8,128)}, u32[]{:S(2)}) %copy-start.1) | copy-done | bytes 8388632
  78.2 1.7 draft_chunk.4
  80.6 1.9 %collective-permute-start.19 = (f32[8,128]{1,0:T(8,128)S(1)}, f32[8,128]{1,0:T(8,128)S(1)}, u32[]{:S(2)}, u32[]{:S(2)}) collective-permute-start(f32[8,128]{1,0:T(8,128)S(1)} %broadcast_maximum_fusion), channel_id=1, source_target_pairs={{0,16},{8,24},{16,0},{24,8},{1,17},{9,25},{17,1},{25,9},{2,18},{10... | collective-permute-start | bytes 12296 | tf_op jit(solution)/shard_map/ppermute | solution.py:21
  82.7 2.1 %draft_chunk.5 = (f32[1024,512]{1,0:T(8,128)S(1)}, f32[1024,1]{1,0:T(8,128)S(1)}, f32[1024,1]{1,0:T(8,128)S(1)}) custom-call(f32[1024,2048]{1,0:T(8,128)S(1)} %copy-done.1, bf16[1024,256]{1,0:T(8,128)(2,1)S(1)} %pad_maximum_fusion.acts_ref, bf16[256,512]{1,0:T(8,128)(2,1)S(1)} %pad_maximum_fusion.4.proj_ref, f32[1024,1]{1,0:T(8,128)S(1)} %get-tuple-element.199.rest_0_, ...), custom_call_target="tpu_custom_call" | custom-call | flops 65536 | bytes 1024 | tf_op jit(solution)/shard_map/draft_chunk/pallas_call | solution.py:210
  85.1 2.1 %draft_chunk.6 = (f32[1024,512]{1,0:T(8,128)S(1)}, f32[1024,1]{1,0:T(8,128)S(1)}, f32[1024,1]{1,0:T(8,128)S(1)}) custom-call(f32[1024,2048]{1,0:T(8,128)S(1)} %copy-done.1, bf16[1024,256]{1,0:T(8,128)(2,1)S(1)} %pad_maximum_fusion.acts_ref, bf16[256,512]{1,0:T(8,128)(2,1)S(1)} %pad_maximum_fusion.5.proj_ref, f32[1024,1]{1,0:T(8,128)S(1)} %get-tuple-element.205.rest_0_, ...), custom_call_target="tpu_custom_call" | custom-call | flops 65536 | bytes 1024 | tf_op jit(solution)/shard_map/draft_chunk/pallas_call | solution.py:210
  89.9 2.1 %draft_chunk.7 = (f32[1024,512]{1,0:T(8,128)S(1)}, f32[1024,1]{1,0:T(8,128)S(1)}, f32[1024,1]{1,0:T(8,128)S(1)}) custom-call(f32[1024,2048]{1,0:T(8,128)S(1)} %copy-done.1, bf16[1024,256]{1,0:T(8,128)(2,1)S(1)} %pad_maximum_fusion.acts_ref, bf16[256,512]{1,0:T(8,128)(2,1)S(1)} %pad_maximum_fusion.6.proj_ref, f32[1024,1]{1,0:T(8,128)S(1)} %get-tuple-element.209.rest_0_, ...), custom_call_target="tpu_custom_call" | custom-call | flops 65536 | bytes 1024 | tf_op jit(solution)/shard_map/draft_chunk/pallas_call | solution.py:210
  92.0 2.6 %grad_chunk.4 = (f32[128,512]{1,0:T(8,128)S(1)}, f32[128,512]{1,0:T(8,128)S(1)}, f32[1024,256]{1,0:T(8,128)S(1)}, f32[1024,1]{1,0:T(8,128)S(1)}) custom-call(f32[1024,512]{1,0:T(8,128)S(1)} %get-tuple-element.212.draft_ref, f32[1024,2048]{1,0:T(8,128)S(1)} %bitcast.6, s32[1024,1]{1,0:T(8,128)S(1)} %copy.11.label_ref, ...), custom_call_target="tpu_custom_call" | custom-call | flops 131072 | bytes 1024 | tf_op jit(solution)/shard_map/grad_chunk/pallas_call | solution.py:274
  95.9 2.6 %grad_chunk.5 = (f32[128,512]{1,0:T(8,128)S(1)}, f32[128,512]{1,0:T(8,128)S(1)}, f32[1024,256]{1,0:T(8,128)S(1)}, f32[1024,1]{1,0:T(8,128)S(1)}) custom-call(f32[1024,512]{1,0:T(8,128)S(1)} %get-tuple-element.219.draft_ref, f32[1024,2048]{1,0:T(8,128)S(1)} %bitcast.6, s32[1024,1]{1,0:T(8,128)S(1)} %copy.11.label_ref, ...), custom_call_target="tpu_custom_call" | custom-call | flops 131072 | bytes 1024 | tf_op jit(solution)/shard_map/grad_chunk/pallas_call | solution.py:274
  101.2 2.6 %grad_chunk.6 = (f32[128,512]{1,0:T(8,128)S(1)}, f32[128,512]{1,0:T(8,128)S(1)}, f32[1024,256]{1,0:T(8,128)S(1)}, f32[1024,1]{1,0:T(8,128)S(1)}) custom-call(f32[1024,512]{1,0:T(8,128)S(1)} %get-tuple-element.228.draft_ref, f32[1024,2048]{1,0:T(8,128)S(1)} %bitcast.6, s32[1024,1]{1,0:T(8,128)S(1)} %copy.11.label_ref, ...), custom_call_target="tpu_custom_call" | custom-call | flops 131072 | bytes 1024 | tf_op jit(solution)/shard_map/grad_chunk/pallas_call | solution.py:274
  103.8 1.7 collective-permute-start.22
  105.6 2.8 %grad_chunk.7 = (f32[128,512]{1,0:T(8,128)S(1)}, f32[128,512]{1,0:T(8,128)S(1)}, f32[1024,256]{1,0:T(8,128)S(1)}, f32[1024,1]{1,0:T(8,128)S(1)}) custom-call(f32[1024,512]{1,0:T(8,128)S(1)} %get-tuple-element.235.draft_ref, f32[1024,2048]{1,0:T(8,128)S(1)} %bitcast.6, s32[1024,1]{1,0:T(8,128)S(1)} %copy.11.label_ref, ...), custom_call_target="tpu_custom_call" | custom-call | flops 131072 | bytes 1024 | tf_op jit(solution)/shard_map/grad_chunk/pallas_call | solution.py:274
  114.2 1.6 collective-permute-start.31
  115.8 5.1 %collective-permute-done.24 = f16[128,512]{1,0:T(8,128)(2,1)} collective-permute-done((f16[128,512]{1,0:T(8,128)(2,1)}, f16[128,512]{1,0:T(8,128)(2,1)}, u32[]{:S(2)}, u32[]{:S(2)}) %collective-permute-start.24) | collective-permute-done | bytes 131104 | tf_op jit(solution)/shard_map/ppermute | solution.py:21
  123.3 1.6 collective-permute-start.25
  124.9 2.4 %collective-permute-start.34 = (f16[128,512]{1,0:T(8,128)(2,1)S(1)}, f16[128,512]{1,0:T(8,128)(2,1)S(1)}, u32[]{:S(2)}, u32[]{:S(2)}) collective-permute-start(f16[128,512]{1,0:T(8,128)(2,1)S(1)} %add_convert_fusion.8), channel_id=1, source_target_pairs={{0,16},{8,24},{16,0},{24,8},{1,17},{9,25},{17,1},{25,9},{2,18},{10... | collective-permute-start | bytes 393224 | tf_op jit(solution)/shard_map/ppermute | solution.py:21
  127.3 2.4 %collective-permute-done.27 = bf16[128,512]{1,0:T(8,128)(2,1)S(1)} collective-permute-done((bf16[128,512]{1,0:T(8,128)(2,1)S(1)}, bf16[128,512]{1,0:T(8,128)(2,1)S(1)}, u32[]{:S(2)}, u32[]{:S(2)}) %collective-permute-start.27) | collective-permute-done | bytes 131104 | tf_op jit(solution)/shard_map/ppermute | solution.py:21
  129.8 2.3 %fusion.3 = f32[256,2048]{1,0:T(8,128)S(1)} fusion(bf16[2048,2048]{1,0:T(8,128)(2,1)} %rest_2_.1, bf16[128,512]{1,0:T(8,128)(2,1)S(1)} %get-tuple-element.332, bf16[128,512]{1,0:T(8,128)(2,1)S(1)} %get-tuple-element.331), kind=kOutput, calls=%fused_computation.6 | convolution fusion | flops 537395200 | bytes 4456448 | tf_op jit(solution)/shard_map/dot_general | solution.py:43
  132.9 1.7 collective-permute-done.31
  135.9 3.9 %collective-permute-done.30 = bf16[128,512]{1,0:T(8,128)(2,1)S(1)} collective-permute-done((bf16[128,512]{1,0:T(8,128)(2,1)S(1)}, bf16[128,512]{1,0:T(8,128)(2,1)S(1)}, u32[]{:S(2)}, u32[]{:S(2)}) %collective-permute-start.30) | collective-permute-done | bytes 131104 | tf_op jit(solution)/shard_map/ppermute | solution.py:21
  139.9 2.4 %convolution_add_fusion.2 = f32[256,2048]{1,0:T(8,128)S(1)} fusion(f32[256,2048]{1,0:T(8,128)S(1)} %fusion.3, bf16[2048,2048]{1,0:T(8,128)(2,1)} %rest_2_.1, bf16[128,512]{1,0:T(8,128)(2,1)S(1)} %get-tuple-element.330, bf16[128,512]{1,0:T(8,128)(2,1)S(1)} %get-tuple-element.329), kind=kOutput, calls=%fused_computation.2 | convolution fusion | flops 537919488 | bytes 6553600 | tf_op jit(solution)/shard_map/dot_general | solution.py:43
  144.2 3.7 %convolution_add_fusion.1 = f32[256,2048]{1,0:T(8,128)} fusion(f32[256,2048]{1,0:T(8,128)S(1)} %convolution_add_fusion.2, bf16[2048,2048]{1,0:T(8,128)(2,1)} %rest_2_.1, bf16[128,512]{1,0:T(8,128)(2,1)S(1)} %get-tuple-element.328, bf16[128,512]{1,0:T(8,128)(2,1)S(1)} %get-tuple-element.327), kind=kOutput, calls=%fused_computation.1 | convolution fusion | flops 537919488 | bytes 6553600 | tf_op jit(solution)/shard_map/dot_general | solution.py:43
  151.3 2.6 %collective-permute-done.37 = bf16[128,512]{1,0:T(8,128)(2,1)S(1)} collective-permute-done((bf16[128,512]{1,0:T(8,128)(2,1)S(1)}, bf16[128,512]{1,0:T(8,128)(2,1)S(1)}, u32[]{:S(2)}, u32[]{:S(2)}) %collective-permute-start.37) | collective-permute-done | bytes 131104 | tf_op jit(solution)/shard_map/ppermute | solution.py:21
  154.0 2.3 %convolution_add_fusion = f32[256,2048]{1,0:T(8,128)S(1)} fusion(f32[256,2048]{1,0:T(8,128)S(1)} %copy-done.5, bf16[2048,2048]{1,0:T(8,128)(2,1)} %rest_2_.1, bf16[128,512]{1,0:T(8,128)(2,1)S(1)} %get-tuple-element.324, bf16[128,512]{1,0:T(8,128)(2,1)S(1)} %get-tuple-element.323), kind=kOutput, calls=%fused_computation | convolution fusion | flops 537919488 | bytes 6553600 | tf_op jit(solution)/shard_map/dot_general | solution.py:43
  161.8 1.8 collective-permute-start.43
  164.7 1.6 collective-permute-start.42
  172.4 5.9 %collective-permute-done.40 = bf16[256,256]{1,0:T(8,128)(2,1)S(1)} collective-permute-done((bf16[256,256]{1,0:T(8,128)(2,1)S(1)}, bf16[256,256]{1,0:T(8,128)(2,1)S(1)}, u32[]{:S(2)}, u32[]{:S(2)}) %collective-permute-start.40) | collective-permute-done | bytes 131104 | tf_op jit(solution)/shard_map/ppermute | solution.py:21
  178.4 2.6 %collective-permute-done.47 = bf16[256,256]{1,0:T(8,128)(2,1)S(1)} collective-permute-done((bf16[256,256]{1,0:T(8,128)(2,1)S(1)}, bf16[256,256]{1,0:T(8,128)(2,1)S(1)}, u32[]{:S(2)}, u32[]{:S(2)}) %collective-permute-start.47) | collective-permute-done | bytes 131104 | tf_op jit(solution)/shard_map/ppermute | solution.py:21
  183.9 2.8 %collective-permute-done.48 = bf16[256,256]{1,0:T(8,128)(2,1)S(1)} collective-permute-done((bf16[256,256]{1,0:T(8,128)(2,1)S(1)}, bf16[256,256]{1,0:T(8,128)(2,1)S(1)}, u32[]{:S(2)}, u32[]{:S(2)}) %collective-permute-start.48) | collective-permute-done | bytes 131104 | tf_op jit(solution)/shard_map/ppermute | solution.py:21
  189.8 1.6 maximum_convert_fusion
  (213 shorter events, 60.3 us)
Async XLA Ops:
  6.0 17.8 %collective-permute-start.1 = (f16[128,512]{1,0:T(8,128)(2,1)S(1)}, f16[128,512]{1,0:T(8,128)(2,1)S(1)}, u32[]{:S(2)}, u32[]{:S(2)}) collective-permute-start(f16[128,512]{1,0:T(8,128)(2,1)S(1)} %multiply_convert_fusion.17), channel_id=1, source_target_pairs={{0,8},{8,0},{16,24},{24,16},{1,9},{9,1},{17,25},{25,17},{2,10},{10... | collective-permute-start | bytes 393224 | tf_op jit(solution)/shard_map/ppermute | solution.py:21
  11.7 18.5 %collective-permute-start = (f32[512,256]{1,0:T(8,128)}, f32[512,256]{1,0:T(8,128)}, u32[]{:S(2)}, u32[]{:S(2)}) collective-permute-start(f32[512,256]{1,0:T(8,128)} %constant_dynamic-slice_fusion.6), channel_id=1, source_target_pairs={{0,1},{1,0},{2,3},{3,2},{4,5},{5,4},{6,7},{7,6},{8,9},{9,8},{10,11... | collective-permute-start | bytes 1572872 | tf_op jit(solution)/shard_map/ppermute | solution.py:21
  20.6 12.3 %collective-permute-start.4 = (f16[128,512]{1,0:T(8,128)(2,1)}, f16[128,512]{1,0:T(8,128)(2,1)S(1)}, u32[]{:S(2)}, u32[]{:S(2)}) collective-permute-start(f16[128,512]{1,0:T(8,128)(2,1)} %multiply_convert_fusion.15), channel_id=1, source_target_pairs={{0,8},{8,0},{16,24},{24,16},{1,9},{9,1},{17,25},{25,17},{2,10},{10... | collective-permute-start | bytes 393224 | tf_op jit(solution)/shard_map/ppermute | solution.py:21
  25.5 9.9 %collective-permute-start.3 = (f16[128,512]{1,0:T(8,128)(2,1)S(1)}, f16[128,512]{1,0:T(8,128)(2,1)S(1)}, u32[]{:S(2)}, u32[]{:S(2)}) collective-permute-start(f16[128,512]{1,0:T(8,128)(2,1)S(1)} %add_convert_fusion.15), channel_id=1, source_target_pairs={{0,16},{8,24},{16,0},{24,8},{1,17},{9,25},{17,1},{25,9},{2,18},{10... | collective-permute-start | bytes 393224 | tf_op jit(solution)/shard_map/ppermute | solution.py:21
  28.6 16.7 %collective-permute-start.7 = (f16[128,512]{1,0:T(8,128)(2,1)}, f16[128,512]{1,0:T(8,128)(2,1)}, u32[]{:S(2)}, u32[]{:S(2)}) collective-permute-start(f16[128,512]{1,0:T(8,128)(2,1)} %multiply_convert_fusion.16), channel_id=1, source_target_pairs={{0,8},{8,0},{16,24},{24,16},{1,9},{9,1},{17,25},{25,17},{2,10},{10... | collective-permute-start | bytes 393224 | tf_op jit(solution)/shard_map/ppermute | solution.py:21
  31.3 7.9 %collective-permute-start.2 = (f32[256,256]{1,0:T(8,128)S(1)}, f32[256,256]{1,0:T(8,128)S(1)}, u32[]{:S(2)}, u32[]{:S(2)}) collective-permute-start(f32[256,256]{1,0:T(8,128)S(1)} %constant_dynamic-slice_fusion.5), channel_id=1, source_target_pairs={{0,2},{1,3},{2,0},{3,1},{4,6},{5,7},{6,4},{7,5},{8,10},{9,11},{10,... | collective-permute-start | bytes 786440 | tf_op jit(solution)/shard_map/ppermute | solution.py:21
  39.3 19.3 %collective-permute-start.5 = (f32[256,256]{1,0:T(8,128)S(1)}, f32[256,256]{1,0:T(8,128)S(1)}, u32[]{:S(2)}, u32[]{:S(2)}) collective-permute-start(f32[256,256]{1,0:T(8,128)S(1)} %dynamic-slice_add_fusion.5), channel_id=1, source_target_pairs={{0,4},{1,5},{2,6},{3,7},{4,0},{5,1},{6,2},{7,3},{8,12},{9,13},{10,... | collective-permute-start | bytes 786440 | tf_op jit(solution)/shard_map/ppermute | solution.py:21
  40.9 8.6 %collective-permute-start.6 = (f32[8,2048]{1,0:T(8,128)}, f32[8,2048]{1,0:T(8,128)S(1)}, u32[]{:S(2)}, u32[]{:S(2)}) collective-permute-start(f32[8,2048]{1,0:T(8,128)} %slice.30), channel_id=1, source_target_pairs={{8,0},{16,8},{24,16},{9,1},{17,9},{25,17},{10,2},{18,10},{26,18},{... | collective-permute-start | bytes 196616 | tf_op jit(solution)/shard_map/ppermute | solution.py:479
  42.2 18.1 %collective-permute-start.10 = (f16[128,512]{1,0:T(8,128)(2,1)S(1)}, f16[128,512]{1,0:T(8,128)(2,1)S(1)}, u32[]{:S(2)}, u32[]{:S(2)}) collective-permute-start(f16[128,512]{1,0:T(8,128)(2,1)S(1)} %get-tuple-element.169), channel_id=1, source_target_pairs={{0,16},{8,24},{16,0},{24,8},{1,17},{9,25},{17,1},{25,9},{2,18},{10... | collective-permute-start | bytes 393224 | tf_op jit(solution)/shard_map/ppermute | solution.py:21
  44.8 16.2 %collective-permute-start.9 = (f16[128,512]{1,0:T(8,128)(2,1)}, f16[128,512]{1,0:T(8,128)(2,1)S(1)}, u32[]{:S(2)}, u32[]{:S(2)}) collective-permute-start(f16[128,512]{1,0:T(8,128)(2,1)} %get-tuple-element.170), channel_id=1, source_target_pairs={{0,8},{8,0},{16,24},{24,16},{1,9},{9,1},{17,25},{25,17},{2,10},{10... | collective-permute-start | bytes 393224 | tf_op jit(solution)/shard_map/ppermute | solution.py:21
  47.0 21.0 %collective-permute-start.12 = (f16[128,512]{1,0:T(8,128)(2,1)}, f16[128,512]{1,0:T(8,128)(2,1)}, u32[]{:S(2)}, u32[]{:S(2)}) collective-permute-start(f16[128,512]{1,0:T(8,128)(2,1)} %add_convert_fusion.13), channel_id=1, source_target_pairs={{0,16},{8,24},{16,0},{24,8},{1,17},{9,25},{17,1},{25,9},{2,18},{10... | collective-permute-start | bytes 393224 | tf_op jit(solution)/shard_map/ppermute | solution.py:21
  58.8 5.0 %collective-permute-start.8 = (bf16[256,256]{1,0:T(8,128)(2,1)S(1)}, bf16[256,256]{1,0:T(8,128)(2,1)S(1)}, u32[]{:S(2)}, u32[]{:S(2)}) collective-permute-start(bf16[256,256]{1,0:T(8,128)(2,1)S(1)} %multiply_convert_fusion.12), channel_id=1, source_target_pairs={{0,2},{1,3},{2,0},{3,1},{4,6},{5,7},{6,4},{7,5},{8,10},{9,11},{10,... | collective-permute-start | bytes 393224 | tf_op jit(solution)/shard_map/ppermute | solution.py:21
  65.5 9.2 %collective-permute-start.16 = (bf16[128,512]{1,0:T(8,128)(2,1)S(1)}, bf16[128,512]{1,0:T(8,128)(2,1)S(1)}, u32[]{:S(2)}, u32[]{:S(2)}) collective-permute-start(bf16[128,512]{1,0:T(8,128)(2,1)S(1)} %multiply_convert_fusion.13), channel_id=1, source_target_pairs={{0,8},{8,0},{16,24},{24,16},{1,9},{9,1},{17,25},{25,17},{2,10},{10... | collective-permute-start | bytes 393224 | tf_op jit(solution)/shard_map/ppermute | solution.py:21
  65.6 17.0 %collective-permute-start.14 = (bf16[128,512]{1,0:T(8,128)(2,1)}, bf16[128,512]{1,0:T(8,128)(2,1)S(1)}, u32[]{:S(2)}, u32[]{:S(2)}) collective-permute-start(bf16[128,512]{1,0:T(8,128)(2,1)} %multiply_convert_fusion.11), channel_id=1, source_target_pairs={{0,8},{8,0},{16,24},{24,16},{1,9},{9,1},{17,25},{25,17},{2,10},{10... | collective-permute-start | bytes 393224 | tf_op jit(solution)/shard_map/ppermute | solution.py:21
  67.6 17.1 %collective-permute-start.13 = (f16[128,512]{1,0:T(8,128)(2,1)}, f16[128,512]{1,0:T(8,128)(2,1)S(1)}, u32[]{:S(2)}, u32[]{:S(2)}) collective-permute-start(f16[128,512]{1,0:T(8,128)(2,1)} %add_convert_fusion.12), channel_id=1, source_target_pairs={{0,16},{8,24},{16,0},{24,8},{1,17},{9,25},{17,1},{25,9},{2,18},{10... | collective-permute-start | bytes 393224 | tf_op jit(solution)/shard_map/ppermute | solution.py:21
  71.4 8.5 %collective-permute-start.15 = (f32[8,128]{1,0:T(8,128)S(1)}, f32[8,128]{1,0:T(8,128)S(1)}, u32[]{:S(2)}, u32[]{:S(2)}) collective-permute-start(f32[8,128]{1,0:T(8,128)S(1)} %broadcast_in_dim.3), channel_id=1, source_target_pairs={{0,8},{8,0},{16,24},{24,16},{1,9},{9,1},{17,25},{25,17},{2,10},{10... | collective-permute-start | bytes 12296 | tf_op jit(solution)/shard_map/ppermute | solution.py:21
  74.8 10.3 %collective-permute-start.18 = (bf16[128,512]{1,0:T(8,128)(2,1)S(1)}, bf16[128,512]{1,0:T(8,128)(2,1)S(1)}, u32[]{:S(2)}, u32[]{:S(2)}) collective-permute-start(bf16[128,512]{1,0:T(8,128)(2,1)S(1)} %multiply_convert_fusion.10), channel_id=1, source_target_pairs={{0,8},{8,0},{16,24},{24,16},{1,9},{9,1},{17,25},{25,17},{2,10},{10... | collective-permute-start | bytes 393224 | tf_op jit(solution)/shard_map/ppermute | solution.py:21
  80.6 6.6 %collective-permute-start.19 = (f32[8,128]{1,0:T(8,128)S(1)}, f32[8,128]{1,0:T(8,128)S(1)}, u32[]{:S(2)}, u32[]{:S(2)}) collective-permute-start(f32[8,128]{1,0:T(8,128)S(1)} %broadcast_maximum_fusion), channel_id=1, source_target_pairs={{0,16},{8,24},{16,0},{24,8},{1,17},{9,25},{17,1},{25,9},{2,18},{10... | collective-permute-start | bytes 12296 | tf_op jit(solution)/shard_map/ppermute | solution.py:21
  84.8 5.0 %collective-permute-start.17 = (bf16[128,512]{1,0:T(8,128)(2,1)S(1)}, bf16[128,512]{1,0:T(8,128)(2,1)S(1)}, u32[]{:S(2)}, u32[]{:S(2)}) collective-permute-start(bf16[128,512]{1,0:T(8,128)(2,1)S(1)} %multiply_convert_fusion.9), channel_id=1, source_target_pairs={{0,8},{8,0},{16,24},{24,16},{1,9},{9,1},{17,25},{25,17},{2,10},{10... | collective-permute-start | bytes 393224 | tf_op jit(solution)/shard_map/ppermute | solution.py:21
  94.7 5.8 %collective-permute-start.21 = (f16[128,512]{1,0:T(8,128)(2,1)S(1)}, f16[128,512]{1,0:T(8,128)(2,1)S(1)}, u32[]{:S(2)}, u32[]{:S(2)}) collective-permute-start(f16[128,512]{1,0:T(8,128)(2,1)S(1)} %multiply_convert_fusion.8), channel_id=1, source_target_pairs={{0,8},{8,0},{16,24},{24,16},{1,9},{9,1},{17,25},{25,17},{2,10},{10... | collective-permute-start | bytes 393224 | tf_op jit(solution)/shard_map/ppermute | solution.py:21
  98.5 7.0 %collective-permute-start.20 = (f16[128,512]{1,0:T(8,128)(2,1)S(1)}, f16[128,512]{1,0:T(8,128)(2,1)S(1)}, u32[]{:S(2)}, u32[]{:S(2)}) collective-permute-start(f16[128,512]{1,0:T(8,128)(2,1)S(1)} %multiply_convert_fusion.7), channel_id=1, source_target_pairs={{0,8},{8,0},{16,24},{24,16},{1,9},{9,1},{17,25},{25,17},{2,10},{10... | collective-permute-start | bytes 393224 | tf_op jit(solution)/shard_map/ppermute | solution.py:21
  103.8 5.7 %collective-permute-start.22 = (f16[128,512]{1,0:T(8,128)(2,1)S(1)}, f16[128,512]{1,0:T(8,128)(2,1)S(1)}, u32[]{:S(2)}, u32[]{:S(2)}) collective-permute-start(f16[128,512]{1,0:T(8,128)(2,1)S(1)} %multiply_convert_fusion.6), channel_id=1, source_target_pairs={{0,8},{8,0},{16,24},{24,16},{1,9},{9,1},{17,25},{25,17},{2,10},{10... | collective-permute-start | bytes 393224 | tf_op jit(solution)/shard_map/ppermute | solution.py:21
  110.2 11.8 %collective-permute-start.23 = (f32[512,256]{1,0:T(8,128)S(1)}, f32[512,256]{1,0:T(8,128)}, u32[]{:S(2)}, u32[]{:S(2)}) collective-permute-start(f32[512,256]{1,0:T(8,128)S(1)} %constant_dynamic-slice_fusion.3), channel_id=1, source_target_pairs={{0,1},{1,0},{2,3},{3,2},{4,5},{5,4},{6,7},{7,6},{8,9},{9,8},{10,11... | collective-permute-start | bytes 1572872 | tf_op jit(solution)/shard_map/ppermute | solution.py:21
  110.3 10.7 %collective-permute-start.24 = (f16[128,512]{1,0:T(8,128)(2,1)}, f16[128,512]{1,0:T(8,128)(2,1)}, u32[]{:S(2)}, u32[]{:S(2)}) collective-permute-start(f16[128,512]{1,0:T(8,128)(2,1)} %add_convert_fusion.11), channel_id=1, source_target_pairs={{0,16},{8,24},{16,0},{24,8},{1,17},{9,25},{17,1},{25,9},{2,18},{10... | collective-permute-start | bytes 393224 | tf_op jit(solution)/shard_map/ppermute | solution.py:21
  111.9 13.0 %collective-permute-start.28 = (f16[128,512]{1,0:T(8,128)(2,1)}, f16[128,512]{1,0:T(8,128)(2,1)S(1)}, u32[]{:S(2)}, u32[]{:S(2)}) collective-permute-start(f16[128,512]{1,0:T(8,128)(2,1)} %multiply_convert_fusion.5), channel_id=1, source_target_pairs={{0,8},{8,0},{16,24},{24,16},{1,9},{9,1},{17,25},{25,17},{2,10},{10... | collective-permute-start | bytes 393224 | tf_op jit(solution)/shard_map/ppermute | solution.py:21
  112.9 19.3 %collective-permute-start.26 = (f16[128,512]{1,0:T(8,128)(2,1)S(1)}, f16[128,512]{1,0:T(8,128)(2,1)S(1)}, u32[]{:S(2)}, u32[]{:S(2)}) collective-permute-start(f16[128,512]{1,0:T(8,128)(2,1)S(1)} %add_convert_fusion.10), channel_id=1, source_target_pairs={{0,16},{8,24},{16,0},{24,8},{1,17},{9,25},{17,1},{25,9},{2,18},{10... | collective-permute-start | bytes 393224 | tf_op jit(solution)/shard_map/ppermute | solution.py:21
  114.2 20.4 %collective-permute-start.31 = (f16[128,512]{1,0:T(8,128)(2,1)}, f16[128,512]{1,0:T(8,128)(2,1)S(1)}, u32[]{:S(2)}, u32[]{:S(2)}) collective-permute-start(f16[128,512]{1,0:T(8,128)(2,1)} %add_convert_fusion.9), channel_id=1, source_target_pairs={{0,16},{8,24},{16,0},{24,8},{1,17},{9,25},{17,1},{25,9},{2,18},{10... | collective-permute-start | bytes 393224 | tf_op jit(solution)/shard_map/ppermute | solution.py:21
  121.9 7.8 %collective-permute-start.27 = (bf16[128,512]{1,0:T(8,128)(2,1)S(1)}, bf16[128,512]{1,0:T(8,128)(2,1)S(1)}, u32[]{:S(2)}, u32[]{:S(2)}) collective-permute-start(bf16[128,512]{1,0:T(8,128)(2,1)S(1)} %multiply_convert_fusion.4), channel_id=1, source_target_pairs={{0,8},{8,0},{16,24},{24,16},{1,9},{9,1},{17,25},{25,17},{2,10},{10... | collective-permute-start | bytes 393224 | tf_op jit(solution)/shard_map/ppermute | solution.py:21
  123.3 9.0 %collective-permute-start.25 = (f32[256,256]{1,0:T(8,128)S(1)}, f32[256,256]{1,0:T(8,128)S(1)}, u32[]{:S(2)}, u32[]{:S(2)}) collective-permute-start(f32[256,256]{1,0:T(8,128)S(1)} %constant_dynamic-slice_fusion.2), channel_id=1, source_target_pairs={{0,2},{1,3},{2,0},{3,1},{4,6},{5,7},{6,4},{7,5},{8,10},{9,11},{10,... | collective-permute-start | bytes 786440 | tf_op jit(solution)/shard_map/ppermute | solution.py:21
  124.9 19.1 %collective-permute-start.34 = (f16[128,512]{1,0:T(8,128)(2,1)S(1)}, f16[128,512]{1,0:T(8,128)(2,1)S(1)}, u32[]{:S(2)}, u32[]{:S(2)}) collective-permute-start(f16[128,512]{1,0:T(8,128)(2,1)S(1)} %add_convert_fusion.8), channel_id=1, source_target_pairs={{0,16},{8,24},{16,0},{24,8},{1,17},{9,25},{17,1},{25,9},{2,18},{10... | collective-permute-start | bytes 393224 | tf_op jit(solution)/shard_map/ppermute | solution.py:21
  132.2 7.7 %collective-permute-start.30 = (bf16[128,512]{1,0:T(8,128)(2,1)S(1)}, bf16[128,512]{1,0:T(8,128)(2,1)S(1)}, u32[]{:S(2)}, u32[]{:S(2)}) collective-permute-start(bf16[128,512]{1,0:T(8,128)(2,1)S(1)} %multiply_convert_fusion.3), channel_id=1, source_target_pairs={{0,8},{8,0},{16,24},{24,16},{1,9},{9,1},{17,25},{25,17},{2,10},{10... | collective-permute-start | bytes 393224 | tf_op jit(solution)/shard_map/ppermute | solution.py:21
  132.4 10.0 %collective-permute-start.29 = (f32[256,256]{1,0:T(8,128)S(1)}, f32[256,256]{1,0:T(8,128)S(1)}, u32[]{:S(2)}, u32[]{:S(2)}) collective-permute-start(f32[256,256]{1,0:T(8,128)S(1)} %dynamic-slice_add_fusion.4), channel_id=1, source_target_pairs={{0,4},{1,5},{2,6},{3,7},{4,0},{5,1},{6,2},{7,3},{8,12},{9,13},{10,... | collective-permute-start | bytes 786440 | tf_op jit(solution)/shard_map/ppermute | solution.py:21
  135.6 8.5 %collective-permute-start.33 = (bf16[128,512]{1,0:T(8,128)(2,1)S(1)}, bf16[128,512]{1,0:T(8,128)(2,1)S(1)}, u32[]{:S(2)}, u32[]{:S(2)}) collective-permute-start(bf16[128,512]{1,0:T(8,128)(2,1)S(1)} %multiply_convert_fusion.2), channel_id=1, source_target_pairs={{0,8},{8,0},{16,24},{24,16},{1,9},{9,1},{17,25},{25,17},{2,10},{10... | collective-permute-start | bytes 393224 | tf_op jit(solution)/shard_map/ppermute | solution.py:21
  142.5 5.4 %collective-permute-start.32 = (bf16[256,256]{1,0:T(8,128)(2,1)S(1)}, bf16[256,256]{1,0:T(8,128)(2,1)S(1)}, u32[]{:S(2)}, u32[]{:S(2)}) collective-permute-start(bf16[256,256]{1,0:T(8,128)(2,1)S(1)} %multiply_convert_fusion.1), channel_id=1, source_target_pairs={{0,2},{1,3},{2,0},{3,1},{4,6},{5,7},{6,4},{7,5},{8,10},{9,11},{10,... | collective-permute-start | bytes 393224 | tf_op jit(solution)/shard_map/ppermute | solution.py:21
  148.0 5.9 %collective-permute-start.37 = (bf16[128,512]{1,0:T(8,128)(2,1)S(1)}, bf16[128,512]{1,0:T(8,128)(2,1)S(1)}, u32[]{:S(2)}, u32[]{:S(2)}) collective-permute-start(bf16[128,512]{1,0:T(8,128)(2,1)S(1)} %multiply_convert_fusion), channel_id=1, source_target_pairs={{0,8},{8,0},{16,24},{24,16},{1,9},{9,1},{17,25},{25,17},{2,10},{10... | collective-permute-start | bytes 393224 | tf_op jit(solution)/shard_map/ppermute | solution.py:21
  160.1 6.9 %collective-permute-start.36 = (bf16[256,256]{1,0:T(8,128)(2,1)S(1)}, bf16[256,256]{1,0:T(8,128)(2,1)S(1)}, u32[]{:S(2)}, u32[]{:S(2)}) collective-permute-start(bf16[256,256]{1,0:T(8,128)(2,1)S(1)} %dynamic-slice_convert_fusion.3), channel_id=1, source_target_pairs={{0,8},{8,0},{16,24},{24,16},{1,9},{9,1},{17,25},{25,17},{2,10},{10... | collective-permute-start | bytes 393224 | tf_op jit(solution)/shard_map/ppermute | solution.py:21
  161.5 4.8 %collective-permute-start.38 = (f32[64,2048]{1,0:T(8,128)S(1)}, f32[64,2048]{1,0:T(8,128)S(1)}, u32[]{:S(2)}, u32[]{:S(2)}) collective-permute-start(f32[64,2048]{1,0:T(8,128)S(1)} %constant_dynamic-slice_fusion.1), channel_id=1, source_target_pairs={{0,1},{1,0},{2,3},{3,2},{4,5},{5,4},{6,7},{7,6},{8,9},{9,8},{10,11... | collective-permute-start | bytes 1572872 | tf_op jit(solution)/shard_map/ppermute | solution.py:21
  161.8 7.0 %collective-permute-start.43 = (bf16[256,256]{1,0:T(8,128)(2,1)S(1)}, bf16[256,256]{1,0:T(8,128)(2,1)S(1)}, u32[]{:S(2)}, u32[]{:S(2)}) collective-permute-start(bf16[256,256]{1,0:T(8,128)(2,1)S(1)} %dynamic-slice_convert_fusion.2), channel_id=1, source_target_pairs={{0,8},{8,0},{16,24},{24,16},{1,9},{9,1},{17,25},{25,17},{2,10},{10... | collective-permute-start | bytes 393224 | tf_op jit(solution)/shard_map/ppermute | solution.py:21
  164.7 5.5 %collective-permute-start.42 = (bf16[32,2048]{1,0:T(8,128)(2,1)S(1)}, bf16[32,2048]{1,0:T(8,128)(2,1)S(1)}, u32[]{:S(2)}, u32[]{:S(2)}) collective-permute-start(bf16[32,2048]{1,0:T(8,128)(2,1)S(1)} %dynamic-slice_convert_fusion.1), channel_id=1, source_target_pairs={{0,2},{1,3},{2,0},{3,1},{4,6},{5,7},{6,4},{7,5},{8,10},{9,11},{10,... | collective-permute-start | bytes 393224 | tf_op jit(solution)/shard_map/ppermute | solution.py:21
  166.4 5.3 %collective-permute-start.41 = (bf16[32,2048]{1,0:T(8,128)(2,1)S(1)}, bf16[32,2048]{1,0:T(8,128)(2,1)S(1)}, u32[]{:S(2)}, u32[]{:S(2)}) collective-permute-start(bf16[32,2048]{1,0:T(8,128)(2,1)S(1)} %dynamic-slice_convert_fusion), channel_id=1, source_target_pairs={{0,4},{1,5},{2,6},{3,7},{4,0},{5,1},{6,2},{7,3},{8,12},{9,13},{10,... | collective-permute-start | bytes 393224 | tf_op jit(solution)/shard_map/ppermute | solution.py:21
  167.0 11.3 %collective-permute-start.40 = (bf16[256,256]{1,0:T(8,128)(2,1)S(1)}, bf16[256,256]{1,0:T(8,128)(2,1)S(1)}, u32[]{:S(2)}, u32[]{:S(2)}) collective-permute-start(bf16[256,256]{1,0:T(8,128)(2,1)S(1)} %add_convert_fusion.7), channel_id=1, source_target_pairs={{0,16},{8,24},{16,0},{24,8},{1,17},{9,25},{17,1},{25,9},{2,18},{10... | collective-permute-start | bytes 393224 | tf_op jit(solution)/shard_map/ppermute | solution.py:21
  168.8 12.2 %collective-permute-start.47 = (bf16[256,256]{1,0:T(8,128)(2,1)S(1)}, bf16[256,256]{1,0:T(8,128)(2,1)S(1)}, u32[]{:S(2)}, u32[]{:S(2)}) collective-permute-start(bf16[256,256]{1,0:T(8,128)(2,1)S(1)} %add_convert_fusion.6), channel_id=1, source_target_pairs={{0,16},{8,24},{16,0},{24,8},{1,17},{9,25},{17,1},{25,9},{2,18},{10... | collective-permute-start | bytes 393224 | tf_op jit(solution)/shard_map/ppermute | solution.py:21
  170.3 10.9 %collective-permute-start.46 = (bf16[32,2048]{1,0:T(8,128)(2,1)S(1)}, bf16[32,2048]{1,0:T(8,128)(2,1)S(1)}, u32[]{:S(2)}, u32[]{:S(2)}) collective-permute-start(bf16[32,2048]{1,0:T(8,128)(2,1)S(1)} %add_convert_fusion.5), channel_id=1, source_target_pairs={{0,4},{1,5},{2,6},{3,7},{4,0},{5,1},{6,2},{7,3},{8,12},{9,13},{10,... | collective-permute-start | bytes 393224 | tf_op jit(solution)/shard_map/ppermute | solution.py:21
  171.8 10.4 %collective-permute-start.45 = (bf16[32,2048]{1,0:T(8,128)(2,1)S(1)}, bf16[32,2048]{1,0:T(8,128)(2,1)S(1)}, u32[]{:S(2)}, u32[]{:S(2)}) collective-permute-start(bf16[32,2048]{1,0:T(8,128)(2,1)S(1)} %add_convert_fusion.4), channel_id=1, source_target_pairs={{0,2},{1,3},{2,0},{3,1},{4,6},{5,7},{6,4},{7,5},{8,10},{9,11},{10,... | collective-permute-start | bytes 393224 | tf_op jit(solution)/shard_map/ppermute | solution.py:21
  178.3 5.5 %collective-permute-start.44 = (bf16[256,256]{1,0:T(8,128)(2,1)S(1)}, bf16[256,256]{1,0:T(8,128)(2,1)S(1)}, u32[]{:S(2)}, u32[]{:S(2)}) collective-permute-start(bf16[256,256]{1,0:T(8,128)(2,1)S(1)} %add_convert_fusion.3), channel_id=1, source_target_pairs={{0,8},{8,0},{16,24},{24,16},{1,9},{9,1},{17,25},{25,17},{2,10},{10... | collective-permute-start | bytes 393224 | tf_op jit(solution)/shard_map/ppermute | solution.py:21
  181.0 5.6 %collective-permute-start.48 = (bf16[256,256]{1,0:T(8,128)(2,1)S(1)}, bf16[256,256]{1,0:T(8,128)(2,1)S(1)}, u32[]{:S(2)}, u32[]{:S(2)}) collective-permute-start(bf16[256,256]{1,0:T(8,128)(2,1)S(1)} %add_convert_fusion.2), channel_id=1, source_target_pairs={{0,8},{8,0},{16,24},{24,16},{1,9},{9,1},{17,25},{25,17},{2,10},{10... | collective-permute-start | bytes 393224 | tf_op jit(solution)/shard_map/ppermute | solution.py:21
  181.2 6.5 %collective-permute-start.49 = (bf16[32,2048]{1,0:T(8,128)(2,1)S(1)}, bf16[32,2048]{1,0:T(8,128)(2,1)S(1)}, u32[]{:S(2)}, u32[]{:S(2)}) collective-permute-start(bf16[32,2048]{1,0:T(8,128)(2,1)S(1)} %add_convert_fusion.1), channel_id=1, source_target_pairs={{0,2},{1,3},{2,0},{3,1},{4,6},{5,7},{6,4},{7,5},{8,10},{9,11},{10,... | collective-permute-start | bytes 393224 | tf_op jit(solution)/shard_map/ppermute | solution.py:21
  182.2 5.6 %collective-permute-start.51 = (bf16[32,2048]{1,0:T(8,128)(2,1)S(1)}, bf16[32,2048]{1,0:T(8,128)(2,1)S(1)}, u32[]{:S(2)}, u32[]{:S(2)}) collective-permute-start(bf16[32,2048]{1,0:T(8,128)(2,1)S(1)} %add_convert_fusion), channel_id=1, source_target_pairs={{0,4},{1,5},{2,6},{3,7},{4,0},{5,1},{6,2},{7,3},{8,12},{9,13},{10,... | collective-permute-start | bytes 393224 | tf_op jit(solution)/shard_map/ppermute | solution.py:21
  (29 other events, 140.0 us)

commit v4 on v2

v4 whole, which is shorter than its diff:
```python
import jax
import jax.numpy as jnp
from jax import lax
from jax.experimental import pallas as pl
from jax.experimental.pallas import tpu as pltpu
from jax.sharding import PartitionSpec as P

HEAD = 2
LAM = 0.1
CHUNKS = 2
PARTS = 4
BLOCK = 256
VOCAB_SCALE = 128.0
F32 = jnp.float32
BF16 = jnp.bfloat16
F16 = jnp.float16


def swap(value, axis, bit):
    mask = 1 << bit
    pairs = [(i, i ^ mask) for i in range(lax.axis_size(axis))]
    return lax.ppermute(value, axis, pairs)


def own_bit(axis, bit):
    return (lax.axis_index(axis) >> bit) & 1


def half(value, which):
    rows = value.shape[0] // 2
    return lax.dynamic_slice_in_dim(value, which * rows, rows, 0)


def silu_slope(values):
    sigma = jax.nn.sigmoid(values)
    return sigma * (1.0 + values * (1.0 - sigma))


def inner_rows(left, right):
    return lax.dot_general(left, right, (((0,), (0,)), ((), ())), preferred_element_type=F32)


def inner_cols(left, right):
    return lax.dot_general(left, right, (((1,), (1,)), ((), ())), preferred_element_type=F32)


def over_books(values, combine, per_book):
    bit = 0
    while (1 << bit) < per_book:
        values = combine(values, jax.tree.map(lambda v: swap(v, "voc", bit), values))
        bit += 1
    return values


def merge_sums(a, b):
    top = jnp.maximum(a[0], b[0])
    return top, a[1] * jnp.exp(a[0] - top) + b[1] * jnp.exp(b[0] - top)


def params(megabytes):
    return pltpu.CompilerParams(
        dimension_semantics=("arbitrary",), vmem_limit_bytes=megabytes << 20
    )


def cost(flops, read, exps):
    return pl.CostEstimate(flops=flops // 4096, bytes_accessed=read // 4096, transcendentals=0)


def row_spec(block, cols, column=0):
    return pl.BlockSpec((block, cols), lambda i: (i, column))


def whole_spec(rows, cols):
    return pl.BlockSpec((rows, cols), lambda i: (0, 0))


def shift_in(target_ref, next_ref, incoming_ref, window):
    block = target_ref.shape[0]
    last = pl.program_id(0) == pl.num_programs(0) - 1
    window[:block, :] = target_ref[...]
    window[block:, :] = jnp.where(last, incoming_ref[...], next_ref[...])
    return window[HEAD : HEAD + block, :]


def target_sums(target, incoming):
    rows, cols = target.shape
    block = min(BLOCK, rows)

    def body(target_ref, next_ref, incoming_ref, top_ref, sum_ref, window):
        shifted = shift_in(target_ref, next_ref, incoming_ref, window)
        top = jnp.max(shifted, -1, keepdims=True)
        top_ref[...] = top
        sum_ref[...] = jnp.sum(jnp.exp(shifted - top), -1, keepdims=True)

    per = block // 8
    return pl.pallas_call(
        body,
        grid=(rows // block,),
        in_specs=[
            row_spec(block, cols),
            pl.BlockSpec((8, cols), lambda i: (jnp.minimum((i + 1) * per, rows // 8 - 1), 0)),
            whole_spec(8, cols),
        ],
        out_specs=[row_spec(block, 1)] * 2,
        out_shape=[jax.ShapeDtypeStruct((rows, 1), F32)] * 2,
        scratch_shapes=[pltpu.VMEM((block + 8, cols), F32)],
        compiler_params=params(50),
        cost_estimate=cost(4 * rows * cols, 4 * rows * cols, rows * cols),
        name="target_sums",
    )(target, target, incoming)


def vocab_parts(up_weight, head_weight, width):
    rank, depth = up_weight.shape
    cols = head_weight.shape[1]
    rows = rank // 2
    block = depth // PARTS
    count = cols // width

    def body(up_ref, head_ref, *rest):
        outs, (buffer, totals, arrived) = rest[: 2 * count], rest[2 * count :]
        copies = [
            pltpu.make_async_copy(
                head_ref.at[pl.ds(k * block, block), :], buffer.at[k], arrived.at[k]
            )
            for k in range(PARTS)
        ]
        for copy in copies:
            copy.start()
        tile = min(512, cols)
        for k in range(PARTS):
            copies[k].wait()
            left = up_ref[:, k * block : (k + 1) * block]

            @pl.loop(0, cols // tile)
            def _(t):
                place = pl.ds(pl.multiple_of(t * tile, tile), tile)
                term = jnp.dot(left, buffer[k, :, place], preferred_element_type=F32)
                if k == 0:
                    totals[:, place] = term
                else:
                    totals[:, place] += term

        mine = lax.axis_index("grp") & 1
        for c in range(count):
            here = slice(c * width, (c + 1) * width)
            away = totals[pl.ds(pl.multiple_of((1 - mine) * rows, rows), rows), here]
            kept = totals[pl.ds(pl.multiple_of(mine * rows, rows), rows), here]
            outs[2 * c][...] = away * VOCAB_SCALE
            outs[2 * c + 1][...] = kept * VOCAB_SCALE

    outs = pl.pallas_call(
        body,
        in_specs=[pl.BlockSpec(memory_space=pltpu.VMEM), pl.BlockSpec(memory_space=pltpu.HBM)],
        out_specs=[pl.BlockSpec(memory_space=pltpu.VMEM)] * (2 * count),
        out_shape=[jax.ShapeDtypeStruct((rows, width), F32)] * (2 * count),
        scratch_shapes=[
            pltpu.VMEM((PARTS, block, cols), BF16),
            pltpu.VMEM((rank, cols), F32),
            pltpu.SemaphoreType.DMA((PARTS,)),
        ],
        compiler_params=pltpu.CompilerParams(vmem_limit_bytes=24 << 20),
        cost_estimate=cost(2 * rank * depth * cols, 2 * depth * cols, 0),
        name="vocab_parts",
    )(up_weight, head_weight)
    return [(outs[2 * c], outs[2 * c + 1]) for c in range(count)]


def draft_chunk(target, acts, pieces, column, sums):
    rows, rank = acts.shape
    half_rank, width = pieces[0].shape
    block = min(BLOCK, rows)

    def body(target_ref, acts_ref, own_ref, other_ref, *rest):
        draft_ref, proj_ref, most_ref, top_ref, sum_ref = rest[-5:]

        @pl.when(pl.program_id(0) == 0)
        def _():
            mine = lax.axis_index("grp") & 1
            proj_ref[pl.ds(pl.multiple_of(mine * half_rank, half_rank), half_rank), :] = own_ref[...]
            proj_ref[
                pl.ds(pl.multiple_of((1 - mine) * half_rank, half_rank), half_rank), :
            ] = other_ref[...]
            most_ref[...] = jnp.zeros_like(most_ref)

        size = jnp.max(jnp.abs(acts_ref[...].astype(F32)), 0, keepdims=True)
        most_ref[...] = jnp.maximum(most_ref[...], jnp.max(size, -1, keepdims=True))
        draft = target_ref[...] + jnp.dot(
            acts_ref[...], proj_ref[...], preferred_element_type=F32
        )
        draft_ref[...] = draft
        top = jnp.max(draft, -1, keepdims=True)
        if sums is not None:
            top = jnp.maximum(top, rest[0][...])
        total = jnp.sum(jnp.exp(draft - top), -1, keepdims=True)
        if sums is not None:
            total = total + rest[1][...] * jnp.exp(rest[0][...] - top)
        top_ref[...] = top
        sum_ref[...] = total

    carried = () if sums is None else tuple(sums)
    draft, proj, most, top, total = pl.pallas_call(
        body,
        grid=(rows // block,),
        in_specs=[
            row_spec(block, width, column),
            row_spec(block, rank),
            whole_spec(half_rank, width),
            whole_spec(half_rank, width),
        ]
        + [row_spec(block, 1)] * len(carried),
        out_specs=[
            row_spec(block, width),
            whole_spec(rank, width),
            whole_spec(8, 128),
            row_spec(block, 1),
            row_spec(block, 1),
        ],
        out_shape=[
            jax.ShapeDtypeStruct((rows, width), F32),
            jax.ShapeDtypeStruct((rank, width), BF16),
            jax.ShapeDtypeStruct((8, 128), F32),
            jax.ShapeDtypeStruct((rows, 1), F32),
            jax.ShapeDtypeStruct((rows, 1), F32),
        ],
        compiler_params=params(24),
        cost_estimate=cost(2 * rows * rank * width, 8 * rows * width, rows * width),
        name="draft_chunk",
    )(target, acts, *pieces, *carried)
    return draft, proj, most, (top, total)


def grad_chunk(draft, target, incoming, label, acts, vocab_proj, column, sums, sizes, carried):
    rows, width = draft.shape
    rank = acts.shape[1]
    half_rank = rank // 2
    block = min(BLOCK, rows)
    bounds = sizes.shape[0]

    def body(
        draft_ref, target_ref, next_ref, incoming_ref, label_ref, acts_ref, proj_ref,
        top_ref, sum_ref, target_top_ref, target_sum_ref, sizes_ref, *rest
    ):
        away_ref, kept_ref, scale_ref, act_ref, loss_ref, totals, window = rest[-7:]
        step = pl.program_id(0)
        count = lax.axis_size("grp") * rows
        row = lax.axis_index("grp") * rows + step * block
        row = row + lax.broadcasted_iota(jnp.int32, (block, 1), 0)
        live = jnp.where(row < count - HEAD, 1.0, 0.0)
        shifted = shift_in(target_ref, next_ref, incoming_ref, window)
        log_target = shifted - (target_top_ref[...] + jnp.log(target_sum_ref[...]))
        log_draft = draft_ref[...] - (top_ref[...] + jnp.log(sum_ref[...]))
        prob = live * jnp.exp(log_target)
        place = lax.broadcasted_iota(jnp.int32, (block, width), 1) + column * width
        hit = jnp.where(place == label_ref[...], LAM, 0.0)
        loss = jnp.sum(prob * (log_target - log_draft) - hit * log_draft, -1, keepdims=True)
        grad = ((live + LAM) * jnp.exp(log_draft) - prob - hit).astype(BF16)
        act = inner_cols(grad, proj_ref[...])
        if carried is not None:
            loss = loss + rest[1][...]
            act = act + rest[0][...]
        loss_ref[...] = loss
        act_ref[...] = act
        term = inner_rows(acts_ref[...], grad)

        @pl.when(step == 0)
        def _():
            totals[...] = term

        @pl.when(step > 0)
        def _():
            totals[...] += term

        @pl.when(step == pl.num_programs(0) - 1)
        def _():
            size = jnp.max(jnp.max(sizes_ref[...], 0), (0, 1), keepdims=True)
            most = jnp.maximum(size * (1.1 * count), 1e-30)
            scale = jnp.exp2(jnp.floor(15.0 - jnp.log(most) * 1.4426950408889634))
            scale_ref[...] = jnp.broadcast_to(scale, (8, 128))
            mine = lax.axis_index("grp") & 1
            away = totals[pl.ds(pl.multiple_of((1 - mine) * half_rank, half_rank), half_rank), :]
            kept = totals[pl.ds(pl.multiple_of(mine * half_rank, half_rank), half_rank), :]
            away_ref[...] = away * scale
            kept_ref[...] = kept * scale

    per = block // 8
    extra = () if carried is None else tuple(carried)
    away, kept, scale, act, loss = pl.pallas_call(
        body,
        grid=(rows // block,),
        in_specs=[
            row_spec(block, width),
            row_spec(block, width, column),
            pl.BlockSpec(
                (8, width), lambda i: (jnp.minimum((i + 1) * per, rows // 8 - 1), column)
            ),
            pl.BlockSpec((8, width), lambda i: (0, column)),
            row_spec(block, 1),
            row_spec(block, rank),
            whole_spec(rank, width),
        ]
        + [row_spec(block, 1)] * 4
        + [pl.BlockSpec((bounds, 8, 128), lambda i: (0, 0, 0))]
        + ([row_spec(block, rank), row_spec(block, 1)] if extra else []),
        out_specs=[whole_spec(half_rank, width)] * 2
        + [whole_spec(8, 128), row_spec(block, rank), row_spec(block, 1)],
        out_shape=[
            jax.ShapeDtypeStruct((half_rank, width), F32),
            jax.ShapeDtypeStruct((half_rank, width), F32),
            jax.ShapeDtypeStruct((8, 128), F32),
            jax.ShapeDtypeStruct((rows, rank), F32),
            jax.ShapeDtypeStruct((rows, 1), F32),
        ],
        scratch_shapes=[pltpu.VMEM((rank, width), F32), pltpu.VMEM((block + 8, width), F32)],
        compiler_params=params(24),
        cost_estimate=cost(4 * rows * rank * width, 8 * rows * width, rows * width),
        name="grad_chunk",
    )(draft, target, target, incoming, label, acts, vocab_proj, *sums, sizes, *extra)
    return (away, kept), scale[0, 0], (act, loss)


class Line:
    def __init__(self):
        self.mark = None

    def after(self, value):
        if self.mark is None:
            return value
        return lax.optimization_barrier((value, self.mark))[0]

    def put(self, value):
        self.mark = jax.tree.leaves(value)[0]
        return value


class Chain:
    def __init__(self, steps):
        self.steps = steps
        self.value = None

    def step(self, times=1):
        for _ in range(times):
            if self.steps is not None:
                try:
                    next(self.steps)
                except StopIteration as end:
                    self.value = end.value
                    self.steps = None

    def result(self):
        while self.steps is not None:
            self.step()
        return self.value


def sent_over(line, value, axis, bit):
    value = line.put(line.after(value))
    arrived = swap(value, axis, bit)
    yield
    return line.after(arrived)


def reduce_steps(line, pair, axis, bits, wires):
    away, part = pair
    for index, (bit, wire) in enumerate(zip(bits[:-1], wires)):
        mine = own_bit(axis, bit)
        if index > 0:
            away, part = half(part, 1 - mine), half(part, mine)
        arrived = yield from sent_over(line, away.astype(wire), axis, bit)
        part = part + arrived.astype(F32)
    sent = part.astype(wires[-1])
    arrived = yield from sent_over(line, sent, axis, bits[-1])
    return sent.astype(F32) + arrived.astype(F32)


def joined(axis, bit, own, other):
    mine = own_bit(axis, bit)
    low = jnp.where(mine == 0, own, other)
    high = jnp.where(mine == 0, other, own)
    return jnp.concatenate((low, high), 0)


def gather_steps(line, piece, axis, bits):
    for bit in reversed(bits[1:-1]):
        other = yield from sent_over(line, piece, axis, bit)
        piece = joined(axis, bit, piece, other)
    return piece


def split_pair(part, axis, bits):
    mine = own_bit(axis, bits[0])
    return half(part, 1 - mine), half(part, mine)


def summed(line, pair, axis, bits, wires, between, pieces):
    def steps():
        total = yield from reduce_steps(line, pair, axis, bits, wires)
        own = yield from gather_steps(line, between(total), axis, bits)
        pieces.append(own)
        other = yield from sent_over(line, own, axis, bits[0])
        pieces.append(other)

    return Chain(steps())


def first_of(chain, pieces):
    while not pieces:
        chain.step()
    return pieces[0]


def scattered(line, part, wire):
    count = lax.axis_size("voc")
    blocks = part.astype(wire).reshape(count, part.shape[0] // count, part.shape[1])
    blocks = line.put(line.after(blocks))
    arrived = lax.all_to_all(blocks, "voc", 0, 0)
    yield
    return jnp.sum(line.after(arrived).astype(F32), 0)


def over_voc(line, part, wire, between):
    def steps():
        total = yield from scattered(line, part, wire)
        rows = line.put(line.after(between(total)))
        whole = lax.all_gather(rows, "voc", axis=0, tiled=True)
        yield
        return line.after(whole)

    return Chain(steps())


def on_device(hidden_states, target_logits, labels, down_weight, up_weight, head_weight):
    row_count, slice_cols = target_logits.shape
    book_count = labels.shape[1]
    group_count = lax.axis_size("grp")
    per_book = lax.axis_size("voc") // book_count
    block_rows = row_count // per_book
    position = lax.axis_index("voc")
    book_index = position // per_book
    book_part = position % per_book
    width = slice_cols // CHUNKS
    chunks = range(CHUNKS)
    z_bits = list(range(group_count.bit_length() - 1))
    half_wires = [F16] * len(z_bits)
    line = Line()

    vocab_pieces = [[] for c in chunks]
    vocab = [
        summed(
            line, pair, "grp", z_bits, half_wires,
            lambda total: (total * (1.0 / VOCAB_SCALE)).astype(BF16), vocab_pieces[c],
        )
        for c, pair in enumerate(vocab_parts(up_weight, head_weight, width))
    ]
    for c in chunks:
        vocab[c].step()
    pre_part = line.put(
        jnp.dot(line.after(hidden_states), down_weight, preferred_element_type=F32)
    )
    kept_pre = []

    def activate(total):
        kept_pre.append(total)
        return jax.nn.silu(total).astype(BF16)

    pre = over_voc(line, pre_part, F32, activate)
    devices = range(group_count)
    top_rows = line.put(line.after(target_logits[:8]))
    incoming = lax.ppermute(top_rows, "grp", [(i + 1, i) for i in devices if i + 1 in devices])
    vocab[0].step()
    pre.step()
    target = tuple(target_sums(target_logits, line.after(incoming)))
    line.put(target[0])
    target = over_books(target, merge_sums, per_book)
    label = lax.dynamic_slice_in_dim(labels, book_index, 1, 1) - book_part * slice_cols
    vocab[1].step()
    pre.step()
    vocab[0].step()
    vocab[1].step()
    acts = line.put(pre.result())

    drafts, vocab_proj, sums = [], [], None
    for c in chunks:
        vocab[c].result()
        pieces = vocab_pieces[c]
        line.put(pieces[1])
        draft, proj, size, sums = draft_chunk(target_logits, acts, pieces, c, sums)
        drafts.append(line.put(draft))
        vocab_proj.append(proj)
        if c == 0:
            sizes = lax.all_gather(size, "grp", axis=0)
    sums = over_books(tuple(sums), merge_sums, per_book)

    grads, carried, grad_pieces = [], None, [[] for c in chunks]
    for c in chunks:
        pair, scale, carried = grad_chunk(
            line.after(drafts[c]), target_logits, incoming, label, acts, vocab_proj[c], c,
            (*sums, *target), sizes, carried,
        )
        line.put(pair)
        unscale = 1.0 / scale
        grads.append(
            summed(
                line, pair, "grp", z_bits, half_wires,
                lambda total, unscale=unscale: (total * unscale).astype(BF16), grad_pieces[c],
            )
        )
        grads[c].step()
    act_part, loss = carried
    act = over_voc(
        line, act_part, F32, lambda total: (total * silu_slope(kept_pre[0])).astype(BF16)
    )
    grads[0].step()
    act.step()
    grads[1].step()
    loss = over_books(loss, jnp.add, per_book)
    frame_loss = lax.dynamic_slice_in_dim(loss, book_part * block_rows, block_rows, 0)
    frame_loss = frame_loss.reshape(1, 1, block_rows)

    def columns(c):
        return head_weight[:, c * width : (c + 1) * width]

    def times_head(before, piece, c):
        return line.put(before + inner_cols(line.after(piece), columns(c)))

    act.step()
    grads[0].step()
    own_up = times_head(0.0, first_of(grads[0], grad_pieces[0]), 0)
    pre_grad = line.put(act.result())
    down_part = line.put(inner_rows(line.after(hidden_states), pre_grad))
    grads[0].result()
    other_up = times_head(0.0, grad_pieces[0][1], 0)
    grads[1].step()
    rows = down_part.shape[0] // 2
    down_pieces = [[], []]
    downs = [
        summed(
            line, split_pair(part, "grp", z_bits), "grp", z_bits, [BF16] * len(z_bits),
            lambda total: total.astype(BF16), down_pieces[i],
        )
        for i, part in enumerate((down_part[:rows], down_part[rows:]))
    ]
    downs[0].step()
    downs[1].step()
    own_up = times_head(own_up, first_of(grads[1], grad_pieces[1]), 1)
    grads[1].result()
    other_up = times_head(other_up, grad_pieces[1][1], 1)
    up_part = joined("grp", 0, own_up, other_up)
    ups = over_voc(line, up_part, BF16, lambda total: total.astype(BF16))
    ups.step()
    downs[0].step()
    downs[1].step()
    ups.step()
    downs[0].step()
    downs[1].step()
    grad_b = ups.result().astype(F32)
    for chain in downs:
        chain.result()
    grad_a = jnp.concatenate(
        [joined("grp", z_bits[0], *pieces).astype(F32) for pieces in down_pieces], 0
    )
    return frame_loss, grad_a, grad_b


def solution(mesh):
    in_specs = (
        P("grp", "voc"),
        P("grp", "voc"),
        P("grp", None),
        P("voc", None),
        P(None, "grp"),
        P("grp", "voc"),
    )
    out_specs = (P("voc", "grp", None), P("voc", None), P(None, "grp"))
    return jax.shard_map(
        on_device, mesh=mesh, in_specs=in_specs, out_specs=out_specs, check_vma=False
    )
```

time: 222 us -> 223 us (level)
  waiting for transfers between devices: 97.4 us -> 63.8 us
  blocking collectives: 0 us -> 31.8 us
  starting transfers between devices: 48.8 us -> 35 us
  between operations: 2.36 us -> 15.8 us
  matrix products: 23.4 us -> 10.7 us
  other arithmetic: 11 us -> 18.3 us
  Pallas kernels: 24.1 us -> 30.6 us
    ppermute x49 -> x18, waiting for transfers between devices: 96.3 us -> 43.7 us  [swap(): return lax.ppermute(value, axis, pairs)]
    all_gather x0 -> x3, blocking collectives: none -> 31.8 us  [the longest x2 18.7 us: steps(): whole = lax.all_gather(rows, 'voc', axis=0, tiled=True)]
    ppermute x49 -> x18, starting transfers between devices: 47.5 us -> 20.9 us  [swap(): return lax.ppermute(value, axis, pairs)]
    dot_general x9 -> x1, matrix products: 16.3 us -> 1.68 us  [on_device(): jnp.dot(line.after(hidden_states), down_weight, preferred_element_type=F32)]
    all_to_all x0 -> x3, starting transfers between devices: none -> 12.7 us  [scattered(): arrived = lax.all_to_all(blocks, 'voc', 0, 0)]
    all_to_all x0 -> x3, waiting for transfers between devices: none -> 9.38 us  [scattered(): arrived = lax.all_to_all(blocks, 'voc', 0, 0)]
    convert_element_type x25 -> x19, other arithmetic: 1.85 us -> 10.7 us  [the longest x6 3.03 us: reduce_steps(): sent = part.astype(wires[-1])]
    ppermute x1, waiting for transfers between devices: 1.16 us -> 7.71 us  [on_device(): lax.ppermute(top_rows, 'grp', [(i + 1, i) for i in devices if i + 1 in de...]
  transfers between devices with their start and end apart: 50 -> 23, of which waited for: 28 -> 15; matrix products, arithmetic and copies ran while one was open for 16% -> 11% of each run, Pallas kernels for 11% -> 7%
where the time goes in v4:
time: 223 us; the launch traced here: 222 us
  waiting for transfers between devices  63.8 us (29%)
  starting transfers between devices  35 us (16%)
  blocking collectives  31.8 us (14%)
  Pallas kernels  30.6 us (14%)
  other arithmetic  18.3 us (8%)
  local copies, waits for them, and re-layouts  15.9 us (7%)
  between operations  15.8 us (7%)
  matrix products  10.7 us (5%)
    ppermute x18, waiting for transfers between devices, swap(): return lax.ppermute(value, axis, pairs)  43.7 us
    ppermute x18, starting transfers between devices, swap(): return lax.ppermute(value, axis, pairs)  20.9 us
    all_gather x2, blocking collectives, steps(): whole = lax.all_gather(rows, 'voc', axis=0, tiled=True)  18.7 us
    all_gather x1, blocking collectives, on_device(): sizes = lax.all_gather(size, 'grp', axis=0)  13.1 us
    all_to_all x3, starting transfers between devices, scattered(): arrived = lax.all_to_all(blocks, 'voc', 0, 0)  12.7 us
    unnamed x37, local copies, waits for them, and re-layouts  12.4 us
    pallas_call x2, Pallas kernels, grad_chunk(): pl.pallas_call(body, grid=(rows // block,), in_specs=[row_spec(block, wid...  12.2 us
    all_to_all x3, waiting for transfers between devices, scattered(): arrived = lax.all_to_all(blocks, 'voc', 0, 0)  9.38 us
  transfers between devices with their start and end apart: 23, of which 15 were waited for; matrix products, arithmetic and copies ran while one was open for 11% of the time, Pallas kernels for 7%

profile of v4, /device:TPU:0, one launch (start us, length us, event | category | flops | bytes accessed | tf_op | source)
XLA Modules:
  0.0 221.9 jit_solution(9352947024982454543)
XLA Ops:
  7.2 3.5 %copy-done.2 = bf16[2048,2048]{1,0:T(8,128)(2,1)S(1)} copy-done((bf16[2048,2048]{1,0:T(8,128)(2,1)S(1)}, bf16[2048,2048]{1,0:T(8,128)(2,1)}, u32[]{:S(2)}) %copy-start.2) | copy-done | bytes 8388632
  10.7 1.2 copy-done.5
  11.9 5.7 %vocab_parts.1 = (f32[128,1024]{1,0:T(8,128)S(1)}, f32[128,1024]{1,0:T(8,128)S(1)}, f32[128,1024]{1,0:T(8,128)S(1)}, f32[128,1024]{1,0:T(8,128)S(1)}) custom-call(bf16[256,2048]{1,0:T(8,128)(2,1)S(1)} %copy-done.5, bf16[2048,2048]{1,0:T(8,128)(2,1)S(1)} %copy-done.2), custom_call_target="tpu_custom_call" | custom-call | flops 524288 | bytes 2048 | tf_op jit(solution)/shard_map/vocab_parts/pallas_call | solution.py:153
  17.7 3.1 %collective-permute-start = (f16[128,1024]{1,0:T(8,128)(2,1)S(1)}, f16[128,1024]{1,0:T(8,128)(2,1)S(1)}, u32[]{:S(2)}, u32[]{:S(2)}) collective-permute-start(f16[128,1024]{1,0:T(8,128)(2,1)S(1)} %convert_element_type.127), channel_id=1, source_target_pairs={{0,8},{8,0},{16,24},{24,16},{1,9},{9,1},{17,25},{25,17},{2,10},{10... | collective-permute-start | bytes 786440 | tf_op jit(solution)/shard_map/ppermute | solution.py:22
  22.4 1.7 fusion.15
  24.1 3.0 %collective-permute-done = f16[128,1024]{1,0:T(8,128)(2,1)S(1)} collective-permute-done((f16[128,1024]{1,0:T(8,128)(2,1)S(1)}, f16[128,1024]{1,0:T(8,128)(2,1)S(1)}, u32[]{:S(2)}, u32[]{:S(2)}) %collective-permute-start) | collective-permute-done | bytes 262176 | tf_op jit(solution)/shard_map/ppermute | solution.py:22
  27.2 4.3 %all-to-all-start = ((f32[8,128,256]{2,1,0:T(8,128)}), f32[8,128,256]{2,1,0:T(8,128)}, u32[]{:S(2)}, u32[]{:S(2)}) async-start(f32[8,128,256]{2,1,0:T(8,128)} %bitcast.21), calls=%async_computation | async-start | bytes 2097152 | tf_op jit(solution)/shard_map/all_to_all | solution.py:417
  31.5 1.8 collective-permute-start.1
  33.3 1.3 collective-permute-start.2
  34.6 3.3 %collective-permute-start.4 = (f16[128,1024]{1,0:T(8,128)(2,1)S(1)}, f16[128,1024]{1,0:T(8,128)(2,1)}, u32[]{:S(2)}, u32[]{:S(2)}) collective-permute-start(f16[128,1024]{1,0:T(8,128)(2,1)S(1)} %add_convert_fusion.3), channel_id=1, source_target_pairs={{0,16},{8,24},{16,0},{24,8},{1,17},{9,25},{17,1},{25,9},{2,18},{10... | collective-permute-start | bytes 786440 | tf_op jit(solution)/shard_map/ppermute | solution.py:22
  37.8 7.7 %collective-permute-done.2.incoming_ref = f32[8,2048]{1,0:T(8,128)S(1)} collective-permute-done((f32[8,2048]{1,0:T(8,128)S(1)}, f32[8,2048]{1,0:T(8,128)S(1)}, u32[]{:S(2)}, u32[]{:S(2)}) %collective-permute-start.2) | collective-permute-done | bytes 65568 | tf_op jit(solution)/shard_map/ppermute | solution.py:470
  45.5 5.0 %target_sums.1 = (f32[1024,1]{1,0:T(8,128)S(1)}, f32[1024,1]{1,0:T(8,128)S(1)}) custom-call(f32[1024,2048]{1,0:T(8,128)} %next_ref.5, f32[1024,2048]{1,0:T(8,128)} %next_ref.5, f32[8,2048]{1,0:T(8,128)S(1)} %collective-permute-done.2.incoming_ref), custom_call_target="tpu_custom_call" | custom-call | flops 2048 | bytes 2048 | tf_op jit(solution)/shard_map/target_sums/pallas_call | solution.py:97
  52.2 1.3 reduce_sum.30
  53.5 1.7 multiply_convert_fusion.3.own_ref
  55.3 10.3 %collective-permute-done.3 = f16[128,1024]{1,0:T(8,128)(2,1)S(1)} collective-permute-done((f16[128,1024]{1,0:T(8,128)(2,1)}, f16[128,1024]{1,0:T(8,128)(2,1)S(1)}, u32[]{:S(2)}, u32[]{:S(2)}) %collective-permute-start.3) | collective-permute-done | bytes 262176 | tf_op jit(solution)/shard_map/ppermute | solution.py:22
  67.8 9.4 %all_gather.15.acts_ref = bf16[1024,256]{1,0:T(8,128)(2,1)S(1)} all-gather(bf16[128,256]{1,0:T(8,128)(2,1)S(1)} %multiply_convert_fusion.5), channel_id=1, replica_groups=mesh['grp'=4,'voc'=8] {'voc'}, dimensions={0}, use_global_device_ids=true | all-gather | bytes 589824 | tf_op jit(solution)/shard_map/all_gather | solution.py:426
  77.2 3.4 %copy-done.1 = f32[1024,2048]{1,0:T(8,128)S(1)} copy-done((f32[1024,2048]{1,0:T(8,128)S(1)}, f32[1024,2048]{1,0:T(8,128)}, u32[]{:S(2)}) %copy-start.1) | copy-done | bytes 8388632
  80.6 3.5 %draft_chunk.2 = (f32[1024,1024]{1,0:T(8,128)S(1)}, bf16[256,1024]{1,0:T(8,128)(2,1)S(1)}, f32[8,128]{1,0:T(8,128)S(1)}, f32[1024,1]{1,0:T(8,128)S(1)}, f32[1024,1]{1,0:T(8,128)S(1)}) custom-call(f32[1024,2048]{1,0:T(8,128)S(1)} %copy-done.1, bf16[1024,256]{1,0:T(8,128)(2,1)S(1)} %all_gather.15.acts_ref, bf16[128,1024]{1,0:T(8,128)(2,1)} %multiply_convert_fusion.3.own_ref, ...), custom_call_target="tpu_custom_call" | custom-call | flops 131072 | bytes 2048 | tf_op jit(solution)/shard_map/draft_chunk/pallas_call | solution.py:203
  84.0 4.1 %draft_chunk.3 = (f32[1024,1024]{1,0:T(8,128)S(1)}, bf16[256,1024]{1,0:T(8,128)(2,1)S(1)}, f32[8,128]{1,0:T(8,128)}, f32[1024,1]{1,0:T(8,128)S(1)}, f32[1024,1]{1,0:T(8,128)S(1)}) custom-call(f32[1024,2048]{1,0:T(8,128)S(1)} %copy-done.1, bf16[1024,256]{1,0:T(8,128)(2,1)S(1)} %all_gather.15.acts_ref, bf16[128,1024]{1,0:T(8,128)(2,1)S(1)} %multiply_convert_fusion.2.own_ref, ...), custom_call_target="tpu_custom_call" | custom-call | flops 131072 | bytes 2048 | tf_op jit(solution)/shard_map/draft_chunk/pallas_call | solution.py:203
  88.2 13.1 %all-gather = f32[32,128]{1,0:T(8,128)S(1)} all-gather(f32[8,128]{1,0:T(8,128)S(1)} %get-tuple-element.117), channel_id=2, replica_groups=mesh['grp'=4,'voc'=8] {'grp'}, dimensions={0}, use_global_device_ids=true | all-gather | bytes 20480 | tf_op jit(solution)/shard_map/all_gather | solution.py:492
  101.3 6.1 %grad_chunk.2 = (f32[128,1024]{1,0:T(8,128)S(1)}, f32[128,1024]{1,0:T(8,128)S(1)}, f32[8,128]{1,0:T(8,128)S(1)}, f32[1024,256]{1,0:T(8,128)S(1)}, f32[1024,1]{1,0:T(8,128)S(1)}) custom-call(f32[1024,1024]{1,0:T(8,128)S(1)} %get-tuple-element.112.draft_ref, f32[1024,2048]{1,0:T(8,128)S(1)} %copy-done.1, f32[1024,2048]{1,0:T(8,128)S(1)} %copy-done.1, ...), custom_call_target="tpu_custom_call" | custom-call | flops 262144 | bytes 2048 | tf_op jit(solution)/shard_map/grad_chunk/pallas_call | solution.py:289
  107.7 6.1 %grad_chunk.3 = (f32[128,1024]{1,0:T(8,128)S(1)}, f32[128,1024]{1,0:T(8,128)S(1)}, f32[8,128]{1,0:T(8,128)S(1)}, f32[1024,256]{1,0:T(8,128)S(1)}, f32[1024,1]{1,0:T(8,128)S(1)}) custom-call(f32[1024,1024]{1,0:T(8,128)S(1)} %get-tuple-element.120.draft_ref, f32[1024,2048]{1,0:T(8,128)S(1)} %copy-done.1, f32[1024,2048]{1,0:T(8,128)S(1)} %copy-done.1, ...), custom_call_target="tpu_custom_call" | custom-call | flops 262144 | bytes 2048 | tf_op jit(solution)/shard_map/grad_chunk/pallas_call | solution.py:289
  116.4 4.2 %all-to-all-start.1 = ((f32[8,128,256]{2,1,0:T(8,128)}), f32[8,128,256]{2,1,0:T(8,128)}, u32[]{:S(2)}, u32[]{:S(2)}) async-start(f32[8,128,256]{2,1,0:T(8,128)} %bitcast.17), calls=%async_computation.1 | async-start | bytes 2097152 | tf_op jit(solution)/shard_map/all_to_all | solution.py:417
  120.7 1.9 collective-permute-start.8
  125.6 6.3 %collective-permute-done.8 = f16[128,1024]{1,0:T(8,128)(2,1)} collective-permute-done((f16[128,1024]{1,0:T(8,128)(2,1)S(1)}, f16[128,1024]{1,0:T(8,128)(2,1)}, u32[]{:S(2)}, u32[]{:S(2)}) %collective-permute-start.8) | collective-permute-done | bytes 262176 | tf_op jit(solution)/shard_map/ppermute | solution.py:22
  133.4 2.7 %all-to-all-done.1 = f32[8,128,256]{2,1,0:T(8,128)} async-done(((f32[8,128,256]{2,1,0:T(8,128)}), f32[8,128,256]{2,1,0:T(8,128)}, u32[]{:S(2)}, u32[]{:S(2)}) %all-to-all-start.1) | async-done | bytes 1048608 | tf_op jit(solution)/shard_map/all_to_all | solution.py:417
  136.1 1.3 reduce_sum.31
  137.5 9.3 %all_gather.18 = bf16[1024,256]{1,0:T(8,128)(2,1)S(1)} all-gather(bf16[128,256]{1,0:T(8,128)(2,1)S(1)} %multiply_convert_fusion.4), channel_id=1, replica_groups=mesh['grp'=4,'voc'=8] {'voc'}, dimensions={0}, use_global_device_ids=true | all-gather | bytes 589824 | tf_op jit(solution)/shard_map/all_gather | solution.py:426
  147.9 1.9 collective-permute-start.11
  149.8 3.7 %fusion.6 = f32[128,2048]{1,0:T(8,128)S(1)} fusion(bf16[128,1024]{1,0:T(8,128)(2,1)S(1)} %multiply_convert_fusion.1, bf16[2048,2048]{1,0:T(8,128)(2,1)} %head_ref.1), kind=kOutput, calls=%fused_computation.6 | convolution fusion | flops 536870912 | bytes 5505024 | tf_op jit(solution)/shard_map/dot_general | solution.py:44
  156.7 1.5 fusion.4
  158.4 1.7 collective-permute-start.13
  160.0 1.5 fusion.8
  161.6 4.9 %collective-permute-done.13 = bf16[128,1024]{1,0:T(8,128)(2,1)S(1)} collective-permute-done((bf16[128,1024]{1,0:T(8,128)(2,1)S(1)}, bf16[128,1024]{1,0:T(8,128)(2,1)S(1)}, u32[]{:S(2)}, u32[]{:S(2)}) %collective-permute-start.13) | collective-permute-done | bytes 262176 | tf_op jit(solution)/shard_map/ppermute | solution.py:22
  166.4 1.5 select_convert_fusion.1
  169.0 4.2 %all-to-all-start.2 = ((bf16[8,32,2048]{2,1,0:T(8,128)(2,1)}), bf16[8,32,2048]{2,1,0:T(8,128)(2,1)}, u32[]{:S(2)}, u32[]{:S(2)}) async-start(bf16[8,32,2048]{2,1,0:T(8,128)(2,1)} %bitcast.20), calls=%async_computation.2 | async-start | bytes 2097152 | tf_op jit(solution)/shard_map/all_to_all | solution.py:417
  173.3 1.4 collective-permute-start.12
  175.4 4.4 %collective-permute-done.12 = bf16[256,256]{1,0:T(8,128)(2,1)} collective-permute-done((bf16[256,256]{1,0:T(8,128)(2,1)S(1)}, bf16[256,256]{1,0:T(8,128)(2,1)}, u32[]{:S(2)}, u32[]{:S(2)}) %collective-permute-start.12) | collective-permute-done | bytes 131104 | tf_op jit(solution)/shard_map/ppermute | solution.py:22
  180.9 1.1 collective-permute-done.15
  182.0 6.7 %all-to-all-done.2 = bf16[8,32,2048]{2,1,0:T(8,128)(2,1)} async-done(((bf16[8,32,2048]{2,1,0:T(8,128)(2,1)}), bf16[8,32,2048]{2,1,0:T(8,128)(2,1)}, u32[]{:S(2)}, u32[]{:S(2)}) %all-to-all-start.2) | async-done | bytes 1048608 | tf_op jit(solution)/shard_map/all_to_all | solution.py:417
  188.7 2.0 reduce_sum.32
  190.8 1.9 collective-permute-start.14
  193.8 7.3 %collective-permute-done.14 = bf16[256,256]{1,0:T(8,128)(2,1)S(1)} collective-permute-done((bf16[256,256]{1,0:T(8,128)(2,1)S(1)}, bf16[256,256]{1,0:T(8,128)(2,1)S(1)}, u32[]{:S(2)}, u32[]{:S(2)}) %collective-permute-start.14) | collective-permute-done | bytes 131104 | tf_op jit(solution)/shard_map/ppermute | solution.py:22
  201.2 1.3 collective-permute-done.17
  204.1 2.6 %collective-permute-done.16 = bf16[256,256]{1,0:T(8,128)(2,1)S(1)} collective-permute-done((bf16[256,256]{1,0:T(8,128)(2,1)S(1)}, bf16[256,256]{1,0:T(8,128)(2,1)S(1)}, u32[]{:S(2)}, u32[]{:S(2)}) %collective-permute-start.16) | collective-permute-done | bytes 131104 | tf_op jit(solution)/shard_map/ppermute | solution.py:22
  206.7 1.4 collective-permute-done.18
  209.2 3.1 %all-gather.3.cloned.1.call-done = bf16[256,2048]{1,0:T(8,128)(2,1)} async-done(((bf16[32,2048]{1,0:T(8,128)(2,1)}), bf16[256,2048]{1,0:T(8,128)(2,1)}) %all-gather.3.cloned.1.call-update) | async-done | bytes 1048592 | tf_op jit(solution)/shard_map/all_gather | solution.py:426
  212.3 2.8 %convert_element_type.165 = f32[256,2048]{1,0:T(8,128)} convert(bf16[256,2048]{1,0:T(8,128)(2,1)} %all-gather.3.cloned.1.call-done) | non-fusion elementwise | flops 524288 | bytes 3145728 | tf_op jit(solution)/shard_map/convert_element_type | solution.py:557
  (85 shorter events, 22.6 us)
Async XLA Ops:
  7.2 15.2 %copy-start = (bf16[1024,1024]{1,0:T(8,128)(2,1)S(1)}, bf16[1024,1024]{1,0:T(8,128)(2,1)}, u32[]{:S(2)}) copy-start(bf16[1024,1024]{1,0:T(8,128)(2,1)} %param.6) | copy-start | bytes 6291460
  7.2 3.5 %copy-start.2 = (bf16[2048,2048]{1,0:T(8,128)(2,1)S(1)}, bf16[2048,2048]{1,0:T(8,128)(2,1)}, u32[]{:S(2)}) copy-start(bf16[2048,2048]{1,0:T(8,128)(2,1)} %head_ref.1) | copy-start | bytes 25165828
  10.7 1.2 copy-start.5
  11.9 10.5 %copy-start.15 = (bf16[1024,256]{1,0:T(8,128)(2,1)S(1)}, bf16[1024,256]{1,0:T(8,128)(2,1)}, u32[]{:S(2)}) copy-start(bf16[1024,256]{1,0:T(8,128)(2,1)} %param.9) | copy-start | bytes 1572868
  17.7 9.4 %collective-permute-start = (f16[128,1024]{1,0:T(8,128)(2,1)S(1)}, f16[128,1024]{1,0:T(8,128)(2,1)S(1)}, u32[]{:S(2)}, u32[]{:S(2)}) collective-permute-start(f16[128,1024]{1,0:T(8,128)(2,1)S(1)} %convert_element_type.127), channel_id=1, source_target_pairs={{0,8},{8,0},{16,24},{24,16},{1,9},{9,1},{17,25},{25,17},{2,10},{10... | collective-permute-start | bytes 786440 | tf_op jit(solution)/shard_map/ppermute | solution.py:22
  27.2 25.0 %all-to-all-start = ((f32[8,128,256]{2,1,0:T(8,128)}), f32[8,128,256]{2,1,0:T(8,128)}, u32[]{:S(2)}, u32[]{:S(2)}) async-start(f32[8,128,256]{2,1,0:T(8,128)} %bitcast.21), calls=%async_computation | async-start | bytes 2097152 | tf_op jit(solution)/shard_map/all_to_all | solution.py:417
  31.5 19.9 %collective-permute-start.1 = (f16[128,1024]{1,0:T(8,128)(2,1)}, f16[128,1024]{1,0:T(8,128)(2,1)S(1)}, u32[]{:S(2)}, u32[]{:S(2)}) collective-permute-start(f16[128,1024]{1,0:T(8,128)(2,1)} %convert_element_type.126), channel_id=1, source_target_pairs={{0,8},{8,0},{16,24},{24,16},{1,9},{9,1},{17,25},{25,17},{2,10},{10... | collective-permute-start | bytes 786440 | tf_op jit(solution)/shard_map/ppermute | solution.py:22
  33.3 12.3 %collective-permute-start.2 = (f32[8,2048]{1,0:T(8,128)S(1)}, f32[8,2048]{1,0:T(8,128)S(1)}, u32[]{:S(2)}, u32[]{:S(2)}) collective-permute-start(f32[8,2048]{1,0:T(8,128)S(1)} %slice.23), channel_id=1, source_target_pairs={{8,0},{16,8},{24,16},{9,1},{17,9},{25,17},{10,2},{18,10},{26,18},{... | collective-permute-start | bytes 196616 | tf_op jit(solution)/shard_map/ppermute | solution.py:470
  34.6 19.0 %collective-permute-start.4 = (f16[128,1024]{1,0:T(8,128)(2,1)S(1)}, f16[128,1024]{1,0:T(8,128)(2,1)}, u32[]{:S(2)}, u32[]{:S(2)}) collective-permute-start(f16[128,1024]{1,0:T(8,128)(2,1)S(1)} %add_convert_fusion.3), channel_id=1, source_target_pairs={{0,16},{8,24},{16,0},{24,8},{1,17},{9,25},{17,1},{25,9},{2,18},{10... | collective-permute-start | bytes 786440 | tf_op jit(solution)/shard_map/ppermute | solution.py:22
  50.6 0.8 copy-start.3
  52.2 13.5 %collective-permute-start.3 = (f16[128,1024]{1,0:T(8,128)(2,1)}, f16[128,1024]{1,0:T(8,128)(2,1)S(1)}, u32[]{:S(2)}, u32[]{:S(2)}) collective-permute-start(f16[128,1024]{1,0:T(8,128)(2,1)} %add_convert_fusion.2), channel_id=1, source_target_pairs={{0,16},{8,24},{16,0},{24,8},{1,17},{9,25},{17,1},{25,9},{2,18},{10... | collective-permute-start | bytes 786440 | tf_op jit(solution)/shard_map/ppermute | solution.py:22
  53.5 13.3 %copy-start.12 = (f32[128,256]{1,0:T(8,128)}, f32[128,256]{1,0:T(8,128)S(1)}, u32[]{:S(2)}) copy-start(f32[128,256]{1,0:T(8,128)S(1)} %reduce_sum.30) | copy-start | bytes 393220
  55.3 21.9 %collective-permute-start.6 = (bf16[128,1024]{1,0:T(8,128)(2,1)}, bf16[128,1024]{1,0:T(8,128)(2,1)}, u32[]{:S(2)}, u32[]{:S(2)}) collective-permute-start(bf16[128,1024]{1,0:T(8,128)(2,1)} %multiply_convert_fusion.3.own_ref), channel_id=1, source_target_pairs={{0,8},{8,0},{16,24},{24,16},{1,9},{9,1},{17,25},{25,17},{2,10},{10... | collective-permute-start | bytes 786440 | tf_op jit(solution)/shard_map/ppermute | solution.py:22
  66.7 17.3 %collective-permute-start.5 = (bf16[128,1024]{1,0:T(8,128)(2,1)S(1)}, bf16[128,1024]{1,0:T(8,128)(2,1)}, u32[]{:S(2)}, u32[]{:S(2)}) collective-permute-start(bf16[128,1024]{1,0:T(8,128)(2,1)S(1)} %multiply_convert_fusion.2.own_ref), channel_id=1, source_target_pairs={{0,8},{8,0},{16,24},{24,16},{1,9},{9,1},{17,25},{25,17},{2,10},{10... | collective-permute-start | bytes 786440 | tf_op jit(solution)/shard_map/ppermute | solution.py:22
  77.2 3.4 %copy-start.1 = (f32[1024,2048]{1,0:T(8,128)S(1)}, f32[1024,2048]{1,0:T(8,128)}, u32[]{:S(2)}) copy-start(f32[1024,2048]{1,0:T(8,128)} %next_ref.5) | copy-start | bytes 25165828
  84.0 17.3 %copy-start.4 = (f32[1024,1]{1,0:T(8,128)S(1)}, f32[1024,1]{1,0:T(8,128)}, u32[]{:S(2)}) copy-start(f32[1024,1]{1,0:T(8,128)} %copy-done.3) | copy-start | bytes 12292
  107.5 8.0 %collective-permute-start.7 = (f16[128,1024]{1,0:T(8,128)(2,1)S(1)}, f16[128,1024]{1,0:T(8,128)(2,1)S(1)}, u32[]{:S(2)}, u32[]{:S(2)}) collective-permute-start(f16[128,1024]{1,0:T(8,128)(2,1)S(1)} %convert_element_type.139), channel_id=1, source_target_pairs={{0,8},{8,0},{16,24},{24,16},{1,9},{9,1},{17,25},{25,17},{2,10},{10... | collective-permute-start | bytes 786440 | tf_op jit(solution)/shard_map/ppermute | solution.py:22
  113.9 0.8 copy-start.7
  114.7 0.8 copy-start.9
  115.5 1.0 copy-start.6
  115.5 21.9 %copy-start.13 = (f32[128,256]{1,0:T(8,128)S(1)}, f32[128,256]{1,0:T(8,128)}, u32[]{:S(2)}) copy-start(f32[128,256]{1,0:T(8,128)} %copy-done.12) | copy-start | bytes 393220
  115.5 16.5 %copy-start.10 = (f32[128,1024]{1,0:T(8,128)S(1)}, f32[128,1024]{1,0:T(8,128)}, u32[]{:S(2)}) copy-start(f32[128,1024]{1,0:T(8,128)} %copy-done.9) | copy-start | bytes 1572868
  116.4 19.7 %all-to-all-start.1 = ((f32[8,128,256]{2,1,0:T(8,128)}), f32[8,128,256]{2,1,0:T(8,128)}, u32[]{:S(2)}, u32[]{:S(2)}) async-start(f32[8,128,256]{2,1,0:T(8,128)} %bitcast.17), calls=%async_computation.1 | async-start | bytes 2097152 | tf_op jit(solution)/shard_map/all_to_all | solution.py:417
  120.7 11.3 %collective-permute-start.8 = (f16[128,1024]{1,0:T(8,128)(2,1)S(1)}, f16[128,1024]{1,0:T(8,128)(2,1)}, u32[]{:S(2)}, u32[]{:S(2)}) collective-permute-start(f16[128,1024]{1,0:T(8,128)(2,1)S(1)} %convert_element_type.140), channel_id=1, source_target_pairs={{0,8},{8,0},{16,24},{24,16},{1,9},{9,1},{17,25},{25,17},{2,10},{10... | collective-permute-start | bytes 786440 | tf_op jit(solution)/shard_map/ppermute | solution.py:22
  125.0 21.8 %collective-permute-start.9 = (f16[128,1024]{1,0:T(8,128)(2,1)S(1)}, f16[128,1024]{1,0:T(8,128)(2,1)}, u32[]{:S(2)}, u32[]{:S(2)}) collective-permute-start(f16[128,1024]{1,0:T(8,128)(2,1)S(1)} %add_convert_fusion.1), channel_id=1, source_target_pairs={{0,16},{8,24},{16,0},{24,8},{1,17},{9,25},{17,1},{25,9},{2,18},{10... | collective-permute-start | bytes 786440 | tf_op jit(solution)/shard_map/ppermute | solution.py:22
  133.0 25.2 %collective-permute-start.10 = (f16[128,1024]{1,0:T(8,128)(2,1)S(1)}, f16[128,1024]{1,0:T(8,128)(2,1)S(1)}, u32[]{:S(2)}, u32[]{:S(2)}) collective-permute-start(f16[128,1024]{1,0:T(8,128)(2,1)S(1)} %add_convert_fusion), channel_id=1, source_target_pairs={{0,16},{8,24},{16,0},{24,8},{1,17},{9,25},{17,1},{25,9},{2,18},{10... | collective-permute-start | bytes 786440 | tf_op jit(solution)/shard_map/ppermute | solution.py:22
  137.5 19.3 %slice-start = ((s8[8388608]{0:T(1024)(128)(4,1)}), s8[4194304]{0:T(1024)(128)(4,1)S(1)}, s32[]{:S(2)}) async-start(s8[8388608]{0:T(1024)(128)(4,1)} %bitcast.15), calls=%async_computation.4 | async-start | bytes 8388608
  147.9 8.9 %collective-permute-start.11 = (bf16[128,1024]{1,0:T(8,128)(2,1)S(1)}, bf16[128,1024]{1,0:T(8,128)(2,1)S(1)}, u32[]{:S(2)}, u32[]{:S(2)}) collective-permute-start(bf16[128,1024]{1,0:T(8,128)(2,1)S(1)} %multiply_convert_fusion.1), channel_id=1, source_target_pairs={{0,8},{8,0},{16,24},{24,16},{1,9},{9,1},{17,25},{25,17},{2,10},{10... | collective-permute-start | bytes 786440 | tf_op jit(solution)/shard_map/ppermute | solution.py:22
  153.5 3.3 %slice-start.1 = ((s8[8388608]{0:T(1024)(128)(4,1)}), s8[4194304]{0:T(1024)(128)(4,1)S(1)}, s32[]{:S(2)}) async-start(s8[8388608]{0:T(1024)(128)(4,1)} %bitcast.15), calls=%async_computation.5 | async-start | bytes 8388608
  154.3 0.8 copy-start.11
  158.4 8.1 %collective-permute-start.13 = (bf16[128,1024]{1,0:T(8,128)(2,1)S(1)}, bf16[128,1024]{1,0:T(8,128)(2,1)S(1)}, u32[]{:S(2)}, u32[]{:S(2)}) collective-permute-start(bf16[128,1024]{1,0:T(8,128)(2,1)S(1)} %multiply_convert_fusion), channel_id=1, source_target_pairs={{0,8},{8,0},{16,24},{24,16},{1,9},{9,1},{17,25},{25,17},{2,10},{10... | collective-permute-start | bytes 786440 | tf_op jit(solution)/shard_map/ppermute | solution.py:22
  161.6 11.8 %copy-start.14 = (bf16[256,256]{1,0:T(8,128)(2,1)S(1)}, bf16[256,256]{1,0:T(8,128)(2,1)}, u32[]{:S(2)}) copy-start(bf16[256,256]{1,0:T(8,128)(2,1)} %get-tuple-element.148) | copy-start | bytes 393220
  168.0 35.3 %copy-start.8 = (f32[1024,1]{1,0:T(8,128)S(1)}, f32[1024,1]{1,0:T(8,128)}, u32[]{:S(2)}) copy-start(f32[1024,1]{1,0:T(8,128)} %copy-done.7) | copy-start | bytes 12292
  169.0 19.7 %all-to-all-start.2 = ((bf16[8,32,2048]{2,1,0:T(8,128)(2,1)}), bf16[8,32,2048]{2,1,0:T(8,128)(2,1)}, u32[]{:S(2)}, u32[]{:S(2)}) async-start(bf16[8,32,2048]{2,1,0:T(8,128)(2,1)} %bitcast.20), calls=%async_computation.2 | async-start | bytes 2097152 | tf_op jit(solution)/shard_map/all_to_all | solution.py:417
  173.3 39.0 %all-gather.3.cloned.1.call-start = ((), (), s32[]{:S(2)}) async-start(), calls=%async_computation.3 | async-start | bytes 1179648 | tf_op jit(solution)/shard_map/all_gather | solution.py:426
  173.3 6.5 %collective-permute-start.12 = (bf16[256,256]{1,0:T(8,128)(2,1)S(1)}, bf16[256,256]{1,0:T(8,128)(2,1)}, u32[]{:S(2)}, u32[]{:S(2)}) collective-permute-start(bf16[256,256]{1,0:T(8,128)(2,1)S(1)} %copy-done.14), channel_id=1, source_target_pairs={{0,8},{8,0},{16,24},{24,16},{1,9},{9,1},{17,25},{25,17},{2,10},{10... | collective-permute-start | bytes 393224 | tf_op jit(solution)/shard_map/ppermute | solution.py:22
  174.7 7.2 %collective-permute-start.15 = (bf16[256,256]{1,0:T(8,128)(2,1)S(1)}, bf16[256,256]{1,0:T(8,128)(2,1)S(1)}, u32[]{:S(2)}, u32[]{:S(2)}) collective-permute-start(bf16[256,256]{1,0:T(8,128)(2,1)S(1)} %get-tuple-element.149), channel_id=1, source_target_pairs={{0,8},{8,0},{16,24},{24,16},{1,9},{9,1},{17,25},{25,17},{2,10},{10... | collective-permute-start | bytes 393224 | tf_op jit(solution)/shard_map/ppermute | solution.py:22
  190.8 10.3 %collective-permute-start.14 = (bf16[256,256]{1,0:T(8,128)(2,1)S(1)}, bf16[256,256]{1,0:T(8,128)(2,1)S(1)}, u32[]{:S(2)}, u32[]{:S(2)}) collective-permute-start(bf16[256,256]{1,0:T(8,128)(2,1)S(1)} %add_convert_fusion.7), channel_id=1, source_target_pairs={{0,16},{8,24},{16,0},{24,8},{1,17},{9,25},{17,1},{25,9},{2,18},{10... | collective-permute-start | bytes 393224 | tf_op jit(solution)/shard_map/ppermute | solution.py:22
  192.7 9.8 %collective-permute-start.17 = (bf16[256,256]{1,0:T(8,128)(2,1)S(1)}, bf16[256,256]{1,0:T(8,128)(2,1)S(1)}, u32[]{:S(2)}, u32[]{:S(2)}) collective-permute-start(bf16[256,256]{1,0:T(8,128)(2,1)S(1)} %add_convert_fusion.6), channel_id=1, source_target_pairs={{0,16},{8,24},{16,0},{24,8},{1,17},{9,25},{17,1},{25,9},{2,18},{10... | collective-permute-start | bytes 393224 | tf_op jit(solution)/shard_map/ppermute | solution.py:22
  201.1 5.6 %collective-permute-start.16 = (bf16[256,256]{1,0:T(8,128)(2,1)S(1)}, bf16[256,256]{1,0:T(8,128)(2,1)S(1)}, u32[]{:S(2)}, u32[]{:S(2)}) collective-permute-start(bf16[256,256]{1,0:T(8,128)(2,1)S(1)} %add_convert_fusion.5), channel_id=1, source_target_pairs={{0,8},{8,0},{16,24},{24,16},{1,9},{9,1},{17,25},{25,17},{2,10},{10... | collective-permute-start | bytes 393224 | tf_op jit(solution)/shard_map/ppermute | solution.py:22
  202.6 5.6 %collective-permute-start.18 = (bf16[256,256]{1,0:T(8,128)(2,1)S(1)}, bf16[256,256]{1,0:T(8,128)(2,1)S(1)}, u32[]{:S(2)}, u32[]{:S(2)}) collective-permute-start(bf16[256,256]{1,0:T(8,128)(2,1)S(1)} %add_convert_fusion.4), channel_id=1, source_target_pairs={{0,8},{8,0},{16,24},{24,16},{1,9},{9,1},{17,25},{25,17},{2,10},{10... | collective-permute-start | bytes 393224 | tf_op jit(solution)/shard_map/ppermute | solution.py:22
Sparse Core Ops, SparseCore 0:
  190.9 21.3 all-gather.2

commit v5 on v4

v5 whole, which is shorter than its diff:
```python
import jax
import jax.numpy as jnp
from jax import lax
from jax.experimental import pallas as pl
from jax.experimental.pallas import tpu as pltpu
from jax.sharding import PartitionSpec as P

HEAD = 2
LAM = 0.1
CHUNKS = 4
PARTS = 4
BLOCK = 256
GROUP = 16
VOCAB_SCALE = 128.0
F32 = jnp.float32
BF16 = jnp.bfloat16
F16 = jnp.float16


def swap(value, axis, bit):
    mask = 1 << bit
    pairs = [(i, i ^ mask) for i in range(lax.axis_size(axis))]
    return lax.ppermute(value, axis, pairs)


def own_bit(axis, bit):
    return (lax.axis_index(axis) >> bit) & 1


def half(value, which):
    rows = value.shape[0] // 2
    return lax.dynamic_slice_in_dim(value, which * rows, rows, 0)


def silu_slope(values):
    sigma = jax.nn.sigmoid(values)
    return sigma * (1.0 + values * (1.0 - sigma))


def inner_rows(left, right):
    return lax.dot_general(left, right, (((0,), (0,)), ((), ())), preferred_element_type=F32)


def inner_cols(left, right):
    return lax.dot_general(left, right, (((1,), (1,)), ((), ())), preferred_element_type=F32)


def over_books(values, combine, per_book):
    bit = 0
    while (1 << bit) < per_book:
        values = combine(values, jax.tree.map(lambda v: swap(v, "voc", bit), values))
        bit += 1
    return values


def merge_sums(a, b):
    top = jnp.maximum(a[0], b[0])
    return top, a[1] * jnp.exp(a[0] - top) + b[1] * jnp.exp(b[0] - top)


def params(megabytes):
    return pltpu.CompilerParams(
        dimension_semantics=("arbitrary",), vmem_limit_bytes=megabytes << 20
    )


def cost(flops, read, exps):
    return pl.CostEstimate(flops=flops // 4096, bytes_accessed=read // 4096, transcendentals=0)


def row_spec(block, cols, column=0):
    return pl.BlockSpec((block, cols), lambda i: (i, column))


def whole_spec(rows, cols):
    return pl.BlockSpec((rows, cols), lambda i: (0, 0))


def shift_in(target_ref, next_ref, incoming_ref, window):
    block = target_ref.shape[0]
    last = pl.program_id(0) == pl.num_programs(0) - 1
    window[:block, :] = target_ref[...]
    window[block:, :] = jnp.where(last, incoming_ref[...], next_ref[...])
    return window[HEAD : HEAD + block, :]


def target_sums(target, incoming):
    rows, cols = target.shape
    block = min(BLOCK, rows)

    def body(target_ref, next_ref, incoming_ref, top_ref, sum_ref, window):
        shifted = shift_in(target_ref, next_ref, incoming_ref, window)
        top = jnp.max(shifted, -1, keepdims=True)
        top_ref[...] = top
        sum_ref[...] = jnp.sum(jnp.exp(shifted - top), -1, keepdims=True)

    per = block // 8
    return pl.pallas_call(
        body,
        grid=(rows // block,),
        in_specs=[
            row_spec(block, cols),
            pl.BlockSpec((8, cols), lambda i: (jnp.minimum((i + 1) * per, rows // 8 - 1), 0)),
            whole_spec(8, cols),
        ],
        out_specs=[row_spec(block, 1)] * 2,
        out_shape=[jax.ShapeDtypeStruct((rows, 1), F32)] * 2,
        scratch_shapes=[pltpu.VMEM((block + 8, cols), F32)],
        compiler_params=params(50),
        cost_estimate=cost(4 * rows * cols, 4 * rows * cols, rows * cols),
        name="target_sums",
    )(target, target, incoming)


def vocab_parts(up_weight, head_weight, count):
    rank, depth = up_weight.shape
    cols = head_weight.shape[1]
    chunk = rank // count
    rows = chunk // 2
    block = depth // PARTS

    def body(up_ref, head_ref, *rest):
        outs, (buffer, totals, arrived) = rest[: 2 * count], rest[2 * count :]
        copies = [
            pltpu.make_async_copy(
                head_ref.at[pl.ds(k * block, block), :], buffer.at[k], arrived.at[k]
            )
            for k in range(PARTS)
        ]
        for copy in copies:
            copy.start()
        tile = min(512, cols)
        for k in range(PARTS):
            copies[k].wait()
            left = up_ref[:, k * block : (k + 1) * block]

            @pl.loop(0, cols // tile)
            def _(t):
                place = pl.ds(pl.multiple_of(t * tile, tile), tile)
                term = jnp.dot(left, buffer[k, :, place], preferred_element_type=F32)
                if k == 0:
                    totals[:, place] = term
                else:
                    totals[:, place] += term

        mine = lax.axis_index("grp") & 1
        for c in range(count):
            away = totals[pl.ds(pl.multiple_of(c * chunk + (1 - mine) * rows, rows), rows), :]
            kept = totals[pl.ds(pl.multiple_of(c * chunk + mine * rows, rows), rows), :]
            outs[2 * c][...] = away * VOCAB_SCALE
            outs[2 * c + 1][...] = kept * VOCAB_SCALE

    outs = pl.pallas_call(
        body,
        in_specs=[pl.BlockSpec(memory_space=pltpu.VMEM), pl.BlockSpec(memory_space=pltpu.HBM)],
        out_specs=[pl.BlockSpec(memory_space=pltpu.VMEM)] * (2 * count),
        out_shape=[jax.ShapeDtypeStruct((rows, cols), F32)] * (2 * count),
        scratch_shapes=[
            pltpu.VMEM((PARTS, block, cols), BF16),
            pltpu.VMEM((rank, cols), F32),
            pltpu.SemaphoreType.DMA((PARTS,)),
        ],
        compiler_params=pltpu.CompilerParams(vmem_limit_bytes=24 << 20),
        cost_estimate=cost(2 * rank * depth * cols, 2 * depth * cols, 0),
        name="vocab_parts",
    )(up_weight, head_weight)
    return [(outs[2 * c], outs[2 * c + 1]) for c in range(count)]


def lane_parts(values, combine):
    parts = values[:, :128]
    for first in range(128, values.shape[1], 128):
        parts = combine(parts, values[:, first : first + 128])
    return parts


def draft_sums(target, acts, pieces):
    vocab_proj = jnp.concatenate([joined("grp", 0, *pair) for pair in pieces], 0)
    draft = target + jnp.dot(acts, vocab_proj, preferred_element_type=F32)
    top = jnp.max(draft, -1, keepdims=True)
    return top, jnp.sum(jnp.exp(draft - top), -1, keepdims=True)


def middle(target, incoming, label, acts, pieces, target_sum, sizes, draft_sum):
    rows, cols = target.shape
    rank = acts.shape[1]
    count = len(pieces)
    chunk = rank // count
    half_rows = chunk // 2
    block = min(BLOCK, rows)
    flat = [piece for pair in pieces for piece in pair]
    given = () if draft_sum is None else tuple(draft_sum)

    def body(target_ref, next_ref, incoming_ref, label_ref, acts_ref, *rest):
        target_top_ref, target_sum_ref, sizes_ref = rest[: 3]
        piece_refs = rest[3 : 3 + 2 * count]
        given_refs = rest[3 + 2 * count : 3 + 2 * count + len(given)]
        outs = rest[3 + 2 * count + len(given) :]
        parts, (scale_ref, act_ref, loss_ref) = outs[: 2 * count], outs[2 * count : 2 * count + 3]
        proj, totals, window, draft, grad, lanes, wide, wider = outs[2 * count + 3 :]
        step = pl.program_id(0)
        mine = lax.axis_index("grp") & 1

        @pl.when(step == 0)
        def _():
            for c in range(count):
                first = pl.multiple_of(c * chunk + mine * half_rows, half_rows)
                proj[pl.ds(first, half_rows), :] = piece_refs[2 * c][...]
                first = pl.multiple_of(c * chunk + (1 - mine) * half_rows, half_rows)
                proj[pl.ds(first, half_rows), :] = piece_refs[2 * c + 1][...]

        total_rows = lax.axis_size("grp") * rows
        row = lax.axis_index("grp") * rows + step * block
        row = row + lax.broadcasted_iota(jnp.int32, (block, 1), 0)
        live = row < total_rows - HEAD
        last = step == pl.num_programs(0) - 1
        window[:block, :] = target_ref[...]
        window[block:, :] = jnp.where(last, incoming_ref[...], next_ref[...])
        draft[...] = jnp.dot(acts_ref[...], proj[...], preferred_element_type=F32)

        def group(i):
            return pl.ds(pl.multiple_of(i * GROUP, GROUP), GROUP)

        if not given:

            @pl.loop(0, block // GROUP)
            def _(i):
                here = group(i)
                value = draft[here, :] + target_ref[here, :]
                draft[here, :] = value
                lanes[here, :] = lane_parts(value, jnp.maximum)

            wide[...] = jnp.broadcast_to(jnp.max(lanes[...], -1, keepdims=True), (block, 128))

            @pl.loop(0, block // GROUP)
            def _(i):
                here = group(i)
                raised = jnp.exp(draft[here, :] - wide[here, :1])
                lanes[here, :] = lane_parts(raised, jnp.add)

            sums = jnp.sum(lanes[...], -1, keepdims=True)
            wide[...] = jnp.broadcast_to(wide[:, :1] + jnp.log(sums), (block, 128))
        else:
            draft[...] += target_ref[...]
            wide[...] = jnp.broadcast_to(
                given_refs[0][...] + jnp.log(given_refs[1][...]), (block, 128)
            )
        below = target_top_ref[...] + jnp.log(target_sum_ref[...])
        wider[...] = jnp.broadcast_to(jnp.where(live, below, 1e6), (block, 128))
        lanes[...] = jnp.broadcast_to(jnp.where(live, 1.0 + LAM, LAM), (block, 128))
        shifted = window
        place = lax.broadcasted_iota(jnp.int32, (GROUP, cols), 1)

        @pl.loop(0, block // GROUP)
        def _(i):
            here = group(i)
            log_draft = draft[here, :] - wide[here, :1]
            there = window[pl.ds(pl.multiple_of(i * GROUP, GROUP), GROUP + 8), :]
            log_target = there[HEAD : HEAD + GROUP, :] - wider[here, :1]
            prob = jnp.exp(log_target)
            marked = prob + jnp.where(place == label_ref[here, :], LAM, 0.0)
            loss = prob * log_target - marked * log_draft
            grad[here, :] = (lanes[here, :1] * jnp.exp(log_draft) - marked).astype(BF16)
            lanes[here, :] = lane_parts(loss, jnp.add)

        loss_ref[...] = jnp.sum(lanes[...], -1, keepdims=True)
        act_ref[...] = inner_cols(grad[...], proj[...])
        term = inner_rows(acts_ref[...], grad[...])

        @pl.when(step == 0)
        def _():
            totals[...] = term

        @pl.when(step > 0)
        def _():
            totals[...] += term

        @pl.when(last)
        def _():
            size = jnp.max(sizes_ref[...], (0, 1), keepdims=True)
            most = jnp.maximum(size * (1.1 * total_rows), 1e-30)
            scale = jnp.exp2(jnp.floor(15.0 - jnp.log(most) * 1.4426950408889634))
            scale_ref[...] = jnp.broadcast_to(scale, (8, 128))
            for c in range(count):
                first = pl.multiple_of(c * chunk + (1 - mine) * half_rows, half_rows)
                parts[2 * c][...] = totals[pl.ds(first, half_rows), :] * scale
                first = pl.multiple_of(c * chunk + mine * half_rows, half_rows)
                parts[2 * c + 1][...] = totals[pl.ds(first, half_rows), :] * scale

    per = block // 8
    outs = pl.pallas_call(
        body,
        grid=(rows // block,),
        in_specs=[
            row_spec(block, cols),
            pl.BlockSpec((8, cols), lambda i: (jnp.minimum((i + 1) * per, rows // 8 - 1), 0)),
            whole_spec(8, cols),
            row_spec(block, 1),
            row_spec(block, rank),
            row_spec(block, 1),
            row_spec(block, 1),
            whole_spec(8, 128),
        ]
        + [whole_spec(half_rows, cols)] * (2 * count)
        + [row_spec(block, 1)] * len(given),
        out_specs=[whole_spec(half_rows, cols)] * (2 * count)
        + [whole_spec(8, 128), row_spec(block, rank), row_spec(block, 1)],
        out_shape=[jax.ShapeDtypeStruct((half_rows, cols), F32)] * (2 * count)
        + [
            jax.ShapeDtypeStruct((8, 128), F32),
            jax.ShapeDtypeStruct((rows, rank), F32),
            jax.ShapeDtypeStruct((rows, 1), F32),
        ],
        scratch_shapes=[
            pltpu.VMEM((rank, cols), BF16),
            pltpu.VMEM((rank, cols), F32),
            pltpu.VMEM((block + 8, cols), F32),
            pltpu.VMEM((block, cols), F32),
            pltpu.VMEM((block, cols), BF16),
            pltpu.VMEM((block, 128), F32),
            pltpu.VMEM((block, 128), F32),
            pltpu.VMEM((block, 128), F32),
        ],
        compiler_params=params(48),
        cost_estimate=cost(6 * rows * rank * cols, 4 * rows * cols, 2 * rows * cols),
        name="middle",
    )(target, target, incoming, label, acts, *target_sum, sizes, *flat, *given)
    pairs = [(outs[2 * c], outs[2 * c + 1]) for c in range(count)]
    return pairs, outs[2 * count][0, 0], outs[2 * count + 1], outs[2 * count + 2]


class Line:
    def __init__(self):
        self.mark = None

    def after(self, value):
        if self.mark is None:
            return value
        return lax.optimization_barrier((value, self.mark))[0]

    def put(self, value):
        self.mark = jax.tree.leaves(value)[0]
        return value


class Chain:
    def __init__(self, steps):
        self.steps = steps
        self.value = None

    def step(self, times=1):
        for _ in range(times):
            if self.steps is not None:
                try:
                    next(self.steps)
                except StopIteration as end:
                    self.value = end.value
                    self.steps = None

    def result(self):
        while self.steps is not None:
            self.step()
        return self.value


def sent_over(line, value, axis, bit):
    value = line.put(line.after(value))
    arrived = swap(value, axis, bit)
    yield
    return line.after(arrived)


def reduce_steps(line, pair, axis, bits, wires):
    away, part = pair
    for index, (bit, wire) in enumerate(zip(bits[:-1], wires)):
        mine = own_bit(axis, bit)
        if index > 0:
            away, part = half(part, 1 - mine), half(part, mine)
        arrived = yield from sent_over(line, away.astype(wire), axis, bit)
        part = part + arrived.astype(F32)
    sent = part.astype(wires[-1])
    arrived = yield from sent_over(line, sent, axis, bits[-1])
    return sent.astype(F32) + arrived.astype(F32)


def joined(axis, bit, own, other):
    mine = own_bit(axis, bit)
    low = jnp.where(mine == 0, own, other)
    high = jnp.where(mine == 0, other, own)
    return jnp.concatenate((low, high), 0)


def gather_steps(line, piece, axis, bits):
    for bit in reversed(bits[1:-1]):
        other = yield from sent_over(line, piece, axis, bit)
        piece = joined(axis, bit, piece, other)
    return piece


def split_pair(part, axis, bits):
    mine = own_bit(axis, bits[0])
    return half(part, 1 - mine), half(part, mine)


def summed(line, pair, axis, bits, wires, between, pieces):
    def steps():
        total = yield from reduce_steps(line, pair, axis, bits, wires)
        own = yield from gather_steps(line, between(total), axis, bits)
        pieces.append(own)
        other = yield from sent_over(line, own, axis, bits[0])
        pieces.append(other)

    return Chain(steps())


def over_voc(line, part, wire, between):
    def steps():
        count = lax.axis_size("voc")
        blocks = part.astype(wire).reshape(count, part.shape[0] // count, part.shape[1])
        blocks = line.put(line.after(blocks))
        arrived = lax.all_to_all(blocks, "voc", 0, 0)
        yield
        total = jnp.sum(line.after(arrived).astype(F32), 0)
        own = line.put(line.after(between(total)))
        copies = jnp.broadcast_to(own[None], (count, *own.shape))
        arrived = lax.all_to_all(copies, "voc", 0, 0)
        yield
        return line.after(arrived).reshape(part.shape)

    return Chain(steps())


def on_device(hidden_states, target_logits, labels, down_weight, up_weight, head_weight):
    row_count, slice_cols = target_logits.shape
    book_count = labels.shape[1]
    group_count = lax.axis_size("grp")
    per_book = lax.axis_size("voc") // book_count
    block_rows = row_count // per_book
    position = lax.axis_index("voc")
    book_index = position // per_book
    book_part = position % per_book
    rank = up_weight.shape[0]
    z_bits = list(range(group_count.bit_length() - 1))
    count = max(1, min(CHUNKS, rank // (32 << max(0, len(z_bits) - 2))))
    chunks = range(count)
    half_wires = [F16] * len(z_bits)
    line = Line()

    vocab_pieces = [[] for c in chunks]
    vocab = [
        summed(
            line, pair, "grp", z_bits, half_wires,
            lambda total: (total * (1.0 / VOCAB_SCALE)).astype(BF16), vocab_pieces[c],
        )
        for c, pair in enumerate(vocab_parts(up_weight, head_weight, count))
    ]
    vocab[0].step()
    devices = range(group_count)
    top_rows = line.put(line.after(target_logits[:8]))
    incoming = lax.ppermute(top_rows, "grp", [(i + 1, i) for i in devices if i + 1 in devices])
    for c in chunks[1:]:
        vocab[c].step()
    pre_part = line.put(
        jnp.dot(line.after(hidden_states), down_weight, preferred_element_type=F32)
    )
    kept_pre = []

    def activate(total):
        kept_pre.append(total)
        return jax.nn.silu(total).astype(BF16)

    pre = over_voc(line, pre_part, F32, activate)
    vocab[0].step()
    pre.step()
    for c in chunks[1:]:
        vocab[c].step()
    target = tuple(target_sums(target_logits, line.after(incoming)))
    line.put(target[0])
    target = over_books(target, merge_sums, per_book)
    label = lax.dynamic_slice_in_dim(labels, book_index, 1, 1) - book_part * slice_cols
    pre.step()
    vocab[0].step()
    acts = line.put(pre.result())
    bounds = [jnp.broadcast_to(jnp.max(jnp.abs(acts.astype(F32))), (8, 128))]

    def bound_steps():
        for bit in z_bits:
            arrived = yield from sent_over(line, bounds[-1], "grp", bit)
            bounds.append(jnp.maximum(bounds[-1], arrived))

    bounding = Chain(bound_steps())
    bounding.step()
    if count > 1:
        vocab[1].step()
    bounding.step()
    for c in chunks[2:]:
        vocab[c].step()
    bounding.result()
    for c in chunks:
        vocab[c].result()
    draft_sum = None
    if per_book > 1:
        draft_sum = over_books(
            draft_sums(target_logits, acts, vocab_pieces), merge_sums, per_book
        )
    pairs, scale, act_part, loss = middle(
        target_logits, incoming, label, acts, vocab_pieces, target, bounds[-1], draft_sum
    )
    line.put(pairs[0])

    unscale = 1.0 / scale
    grad_pieces = [[] for c in chunks]
    grads = [
        summed(
            line, pair, "grp", z_bits, half_wires,
            lambda total: (total * unscale).astype(BF16), grad_pieces[c],
        )
        for c, pair in enumerate(pairs)
    ]
    for c in chunks:
        grads[c].step()
    act = over_voc(
        line, act_part, F32, lambda total: (total * silu_slope(kept_pre[0])).astype(BF16)
    )
    grads[0].step()
    act.step()
    for c in chunks[1:]:
        grads[c].step()
    loss = over_books(loss, jnp.add, per_book)
    frame_loss = lax.dynamic_slice_in_dim(loss, book_part * block_rows, block_rows, 0)
    frame_loss = frame_loss.reshape(1, 1, block_rows)
    act.step()
    grads[0].step()
    pre_grad = line.put(act.result())
    down_part = line.put(inner_rows(line.after(hidden_states), pre_grad))
    rows = down_part.shape[0] // 2
    down_pieces = [[], []]
    downs = [
        summed(
            line, split_pair(part, "grp", z_bits), "grp", z_bits, [BF16] * len(z_bits),
            lambda total: total.astype(BF16), down_pieces[i],
        )
        for i, part in enumerate((down_part[:rows], down_part[rows:]))
    ]
    for c in chunks[1:2]:
        grads[c].step()
    downs[0].step()
    downs[1].step()

    split = 2 if count % 2 == 0 and rank // 2 >= 16 * lax.axis_size("voc") else 1
    ups = []

    def start_up(part):
        taken = chunks[part * count // split : (part + 1) * count // split]
        for c in taken:
            grads[c].result()
        grad = jnp.concatenate([joined("grp", 0, *grad_pieces[c]) for c in taken], 0)
        up_part = inner_cols(line.after(grad), head_weight)
        ups.append(over_voc(line, up_part, BF16, lambda total: total.astype(BF16)))
        ups[-1].step()

    start_up(0)
    for c in chunks[2:]:
        grads[c].step()
    downs[0].step()
    downs[1].step()
    if split > 1:
        start_up(1)
    for chain in ups:
        chain.step()
    downs[0].step()
    downs[1].step()
    grad_b = jnp.concatenate([chain.result().astype(F32) for chain in ups], 0)
    for chain in downs:
        chain.result()
    grad_a = jnp.concatenate(
        [joined("grp", z_bits[0], *pieces).astype(F32) for pieces in down_pieces], 0
    )
    return frame_loss, grad_a, grad_b


def solution(mesh):
    in_specs = (
        P("grp", "voc"),
        P("grp", "voc"),
        P("grp", None),
        P("voc", None),
        P(None, "grp"),
        P("grp", "voc"),
    )
    out_specs = (P("voc", "grp", None), P("voc", None), P(None, "grp"))
    return jax.shard_map(
        on_device, mesh=mesh, in_specs=in_specs, out_specs=out_specs, check_vma=False
    )
```

time: 223 us -> 256 us (1.15)
  starting transfers between devices: 35 us -> 68.3 us
  blocking collectives: 31.8 us -> 0 us
  other arithmetic: 18.3 us -> 37.5 us
  between operations: 15.8 us -> 1.83 us
  Pallas kernels: 30.6 us -> 42.1 us
  local copies, waits for them, and re-layouts: 15.9 us -> 22.6 us
  matrix products: 10.7 us -> 16.7 us
    all_gather x3 -> x0, blocking collectives: 31.8 us -> none  [the longest x2 18.7 us: steps(): whole = lax.all_gather(rows, 'voc', axis=0, tiled=True)]
    all_to_all x3 -> x8, waiting for transfers between devices: 9.38 us -> 36.7 us  [the longest x4 22.4 us: steps(): arrived = lax.all_to_all(blocks, 'voc', 0, 0)]
    all_to_all x3 -> x8, starting transfers between devices: 12.7 us -> 30.6 us  [the longest x4 16.7 us: steps(): arrived = lax.all_to_all(blocks, 'voc', 0, 0)]
    ppermute x18 -> x32, starting transfers between devices: 20.9 us -> 36.4 us  [swap(): return lax.ppermute(value, axis, pairs)]
    ppermute x18 -> x32, waiting for transfers between devices: 43.7 us -> 28.4 us  [swap(): return lax.ppermute(value, axis, pairs)]
    pallas_call x4 -> x1, Pallas kernels: 19.8 us -> 31.3 us  [middle(): pl.pallas_call(body, grid=(rows // block,), in_specs=[row_spec(block, col...]
    convert_element_type x6 -> x10, other arithmetic: 3.03 us -> 11.5 us  [reduce_steps(): sent = part.astype(wires[-1])]
    ppermute x1, waiting for transfers between devices: 7.71 us -> 0.01 us  [on_device(): lax.ppermute(top_rows, 'grp', [(i + 1, i) for i in devices if i + 1 in de...]
  transfers between devices with their start and end apart: 23 -> 41, of which waited for: 15 -> 16; matrix products, arithmetic and copies ran while one was open for 11% -> 24% of each run, Pallas kernels for 7% -> 2%
where the time goes in v5:
time: 256 us; the launch traced here: 254 us
  starting transfers between devices  68.3 us (27%)
  waiting for transfers between devices  65.2 us (25%)
  Pallas kernels  42.1 us (16%)
  other arithmetic  37.5 us (15%)
  local copies, waits for them, and re-layouts  22.6 us (9%)
  matrix products  16.7 us (7%)
    ppermute x32, starting transfers between devices, swap(): return lax.ppermute(value, axis, pairs)  36.4 us
    pallas_call x1, Pallas kernels, middle(): pl.pallas_call(body, grid=(rows // block,), in_specs=[row_spec(block, col...  31.3 us
    ppermute x32, waiting for transfers between devices, swap(): return lax.ppermute(value, axis, pairs)  28.4 us
    all_to_all x4, waiting for transfers between devices, steps(): arrived = lax.all_to_all(blocks, 'voc', 0, 0)  22.4 us
    all_to_all x4, starting transfers between devices, steps(): arrived = lax.all_to_all(blocks, 'voc', 0, 0)  16.7 us
    unnamed x53, local copies, waits for them, and re-layouts  15.7 us
    all_to_all x4, waiting for transfers between devices, steps(): arrived = lax.all_to_all(copies, 'voc', 0, 0)  14.3 us
    dot_general x2, matrix products, inner_cols(): lax.dot_general(left, right, (((1,), (1,)), ((), ())), preferred_element_...  14.3 us
  transfers between devices with their start and end apart: 41, of which 16 were waited for; matrix products, arithmetic and copies ran while one was open for 24% of the time, Pallas kernels for 2%

profile of v5, /device:TPU:0, one launch (start us, length us, event | category | flops | bytes accessed | tf_op | source)
XLA Modules:
  0.0 254.2 jit_solution(9651591319110945735)
XLA Ops:
  0.7 3.5 %copy-done.1 = bf16[2048,2048]{1,0:T(8,128)(2,1)S(1)} copy-done((bf16[2048,2048]{1,0:T(8,128)(2,1)S(1)}, bf16[2048,2048]{1,0:T(8,128)(2,1)}, u32[]{:S(2)}) %copy-start.1) | copy-done | bytes 8388632
  5.4 5.7 %vocab_parts.1 = (f32[32,2048]{1,0:T(8,128)S(1)}, f32[32,2048]{1,0:T(8,128)S(1)}, f32[32,2048]{1,0:T(8,128)S(1)}, f32[32,2048]{1,0:T(8,128)S(1)}, f32[32,2048]{1...) custom-call(bf16[256,2048]{1,0:T(8,128)(2,1)S(1)} %copy-done.2, ...), custom_call_target="tpu_custom_call" | custom-call | flops 524288 | bytes 2048 | tf_op jit(solution)/shard_map/vocab_parts/pallas_call | solution.py:153
  11.2 3.1 %collective-permute-start.1 = (f16[32,2048]{1,0:T(8,128)(2,1)S(1)}, f16[32,2048]{1,0:T(8,128)(2,1)}, u32[]{:S(2)}, u32[]{:S(2)}) collective-permute-start(f16[32,2048]{1,0:T(8,128)(2,1)S(1)} %convert_element_type.210), channel_id=1, source_target_pairs={{0,8},{8,0},{16,24},{24,16},{1,9},{9,1},{17,25},{25,17},{2,10},{10... | collective-permute-start | bytes 393224 | tf_op jit(solution)/shard_map/ppermute | solution.py:23
  17.1 2.6 %collective-permute-start.4 = (f16[32,2048]{1,0:T(8,128)(2,1)}, f16[32,2048]{1,0:T(8,128)(2,1)}, u32[]{:S(2)}, u32[]{:S(2)}) collective-permute-start(f16[32,2048]{1,0:T(8,128)(2,1)} %convert_element_type.213), channel_id=1, source_target_pairs={{0,8},{8,0},{16,24},{24,16},{1,9},{9,1},{17,25},{25,17},{2,10},{10... | collective-permute-start | bytes 393224 | tf_op jit(solution)/shard_map/ppermute | solution.py:23
  20.4 2.1 collective-permute-start.2
  22.5 1.7 fusion.1
  25.1 2.7 %collective-permute-start.5 = (f16[32,2048]{1,0:T(8,128)(2,1)S(1)}, f16[32,2048]{1,0:T(8,128)(2,1)}, u32[]{:S(2)}, u32[]{:S(2)}) collective-permute-start(f16[32,2048]{1,0:T(8,128)(2,1)S(1)} %add_convert_fusion.11), channel_id=1, source_target_pairs={{0,16},{8,24},{16,0},{24,8},{1,17},{9,25},{17,1},{25,9},{2,18},{10... | collective-permute-start | bytes 393224 | tf_op jit(solution)/shard_map/ppermute | solution.py:23
  27.8 4.2 %all-to-all-start = ((f32[8,128,256]{2,1,0:T(8,128)}), f32[8,128,256]{2,1,0:T(8,128)}, u32[]{:S(2)}, u32[]{:S(2)}) async-start(f32[8,128,256]{2,1,0:T(8,128)} %bitcast.22), calls=%async_computation | async-start | bytes 2097152 | tf_op jit(solution)/shard_map/all_to_all | solution.py:421
  32.0 1.6 add_convert_fusion.10
  33.6 1.6 add_convert_fusion.9
  35.2 1.6 add_convert_fusion.8
  36.8 5.0 %target_sums.1 = (f32[1024,1]{1,0:T(8,128)S(1)}, f32[1024,1]{1,0:T(8,128)S(1)}) custom-call(f32[1024,2048]{1,0:T(8,128)} %next_ref.3, f32[1024,2048]{1,0:T(8,128)} %next_ref.3, f32[8,2048]{1,0:T(8,128)S(1)} %collective-permute-done.incoming_ref), custom_call_target="tpu_custom_call" | custom-call | flops 2048 | bytes 2048 | tf_op jit(solution)/shard_map/target_sums/pallas_call | solution.py:98
  43.4 4.0 %all-to-all-done = f32[8,128,256]{2,1,0:T(8,128)} async-done(((f32[8,128,256]{2,1,0:T(8,128)}), f32[8,128,256]{2,1,0:T(8,128)}, u32[]{:S(2)}, u32[]{:S(2)}) %all-to-all-start) | async-done | bytes 1048608 | tf_op jit(solution)/shard_map/all_to_all | solution.py:421
  47.4 1.3 reduce_sum.42
  49.6 3.5 %all-to-all-start.1 = ((bf16[8,128,256]{2,1,0:T(8,128)(2,1)}), bf16[8,128,256]{2,1,0:T(8,128)(2,1)S(1)}, u32[]{:S(2)}, u32[]{:S(2)}) async-start(bf16[8,128,256]{2,1,0:T(8,128)(2,1)} %broadcast_in_dim.10), calls=%async_computation.1 | async-start | bytes 1048576 | tf_op jit(solution)/shard_map/all_to_all | solution.py:426
  54.5 2.6 %collective-permute-start.10 = (f16[32,2048]{1,0:T(8,128)(2,1)}, f16[32,2048]{1,0:T(8,128)(2,1)}, u32[]{:S(2)}, u32[]{:S(2)}) collective-permute-start(f16[32,2048]{1,0:T(8,128)(2,1)} %add_convert_fusion.9), channel_id=1, source_target_pairs={{0,16},{8,24},{16,0},{24,8},{1,17},{9,25},{17,1},{25,9},{2,18},{10... | collective-permute-start | bytes 393224 | tf_op jit(solution)/shard_map/ppermute | solution.py:23
  58.5 4.3 %all-to-all-done.1 = bf16[8,128,256]{2,1,0:T(8,128)(2,1)S(1)} async-done(((bf16[8,128,256]{2,1,0:T(8,128)(2,1)}), bf16[8,128,256]{2,1,0:T(8,128)(2,1)S(1)}, u32[]{:S(2)}, u32[]{:S(2)}) %all-to-all-start.1) | async-done | bytes 524320 | tf_op jit(solution)/shard_map/all_to_all | solution.py:426
  64.2 5.0 %collective-permute-done.7 = f16[32,2048]{1,0:T(8,128)(2,1)} collective-permute-done((f16[32,2048]{1,0:T(8,128)(2,1)}, f16[32,2048]{1,0:T(8,128)(2,1)}, u32[]{:S(2)}, u32[]{:S(2)}) %collective-permute-start.7) | collective-permute-done | bytes 131104 | tf_op jit(solution)/shard_map/ppermute | solution.py:23
  71.0 1.3 collective-permute-start.8
  77.7 5.6 %collective-permute-done.14.rest_10_ = bf16[32,2048]{1,0:T(8,128)(2,1)S(1)} collective-permute-done((bf16[32,2048]{1,0:T(8,128)(2,1)S(1)}, bf16[32,2048]{1,0:T(8,128)(2,1)S(1)}, u32[]{:S(2)}, u32[]{:S(2)}) %collective-permute-start.14) | collective-permute-done | bytes 131104 | tf_op jit(solution)/shard_map/ppermute | solution.py:23
  85.3 31.3 %middle.1 = (f32[32,2048]{1,0:T(8,128)S(1)}, f32[32,2048]{1,0:T(8,128)S(1)}, f32[32,2048]{1,0:T(8,128)S(1)}, f32[32,2048]{1,0:T(8,128)S(1)}, f32[32,2048]{1,0:T(...) custom-call(f32[1024,2048]{1,0:T(8,128)} %next_ref.3, ...), custom_call_target="tpu_custom_call" | custom-call | flops 786432 | bytes 2048 | tf_op jit(solution)/shard_map/middle/pallas_call | solution.py:291
  123.4 2.1 collective-permute-start.18
  126.4 1.7 convert_element_type.237
  128.1 2.0 collective-permute-start.16
  132.4 4.4 %all-to-all-start.2 = ((f32[8,128,256]{2,1,0:T(8,128)}), f32[8,128,256]{2,1,0:T(8,128)}, u32[]{:S(2)}, u32[]{:S(2)}) async-start(f32[8,128,256]{2,1,0:T(8,128)} %bitcast.21), calls=%async_computation.2 | async-start | bytes 2097152 | tf_op jit(solution)/shard_map/all_to_all | solution.py:421
  139.7 12.5 %all-to-all-done.2 = f32[8,128,256]{2,1,0:T(8,128)} async-done(((f32[8,128,256]{2,1,0:T(8,128)}), f32[8,128,256]{2,1,0:T(8,128)}, u32[]{:S(2)}, u32[]{:S(2)}) %all-to-all-start.2) | async-done | bytes 1048608 | tf_op jit(solution)/shard_map/all_to_all | solution.py:421
  152.2 1.3 reduce_sum.43
  154.4 3.5 %all-to-all-start.3 = ((bf16[8,128,256]{2,1,0:T(8,128)(2,1)}), bf16[8,128,256]{2,1,0:T(8,128)(2,1)S(1)}, u32[]{:S(2)}, u32[]{:S(2)}) async-start(bf16[8,128,256]{2,1,0:T(8,128)(2,1)} %broadcast_in_dim.12), calls=%async_computation.3 | async-start | bytes 1048576 | tf_op jit(solution)/shard_map/all_to_all | solution.py:426
  158.6 3.0 %collective-permute-start.20 = (f16[32,2048]{1,0:T(8,128)(2,1)S(1)}, f16[32,2048]{1,0:T(8,128)(2,1)S(1)}, u32[]{:S(2)}, u32[]{:S(2)}) collective-permute-start(f16[32,2048]{1,0:T(8,128)(2,1)S(1)} %add_convert_fusion.6), channel_id=1, source_target_pairs={{0,16},{8,24},{16,0},{24,8},{1,17},{9,25},{17,1},{25,9},{2,18},{10... | collective-permute-start | bytes 393224 | tf_op jit(solution)/shard_map/ppermute | solution.py:23
  161.7 2.8 %collective-permute-start.22 = (f16[32,2048]{1,0:T(8,128)(2,1)S(1)}, f16[32,2048]{1,0:T(8,128)(2,1)}, u32[]{:S(2)}, u32[]{:S(2)}) collective-permute-start(f16[32,2048]{1,0:T(8,128)(2,1)S(1)} %add_convert_fusion.4), channel_id=1, source_target_pairs={{0,16},{8,24},{16,0},{24,8},{1,17},{9,25},{17,1},{25,9},{2,18},{10... | collective-permute-start | bytes 393224 | tf_op jit(solution)/shard_map/ppermute | solution.py:23
  165.6 2.1 all-to-all-done.3
  168.4 6.0 %collective-permute-done.20 = f16[32,2048]{1,0:T(8,128)(2,1)S(1)} collective-permute-done((f16[32,2048]{1,0:T(8,128)(2,1)S(1)}, f16[32,2048]{1,0:T(8,128)(2,1)S(1)}, u32[]{:S(2)}, u32[]{:S(2)}) %collective-permute-start.20) | collective-permute-done | bytes 131104 | tf_op jit(solution)/shard_map/ppermute | solution.py:23
  175.4 2.0 collective-permute-start.21
  179.0 3.6 %collective-permute-done.25 = bf16[32,2048]{1,0:T(8,128)(2,1)S(1)} collective-permute-done((bf16[32,2048]{1,0:T(8,128)(2,1)S(1)}, bf16[32,2048]{1,0:T(8,128)(2,1)S(1)}, u32[]{:S(2)}, u32[]{:S(2)}) %collective-permute-start.25) | collective-permute-done | bytes 131104 | tf_op jit(solution)/shard_map/ppermute | solution.py:23
  182.7 7.1 %convolution_convert_fusion.1 = bf16[128,2048]{1,0:T(8,128)(2,1)} fusion(bf16[128,2048]{1,0:T(8,128)(2,1)S(1)} %pad_maximum_fusion, bf16[2048,2048]{1,0:T(8,128)(2,1)} %head_ref.1), kind=kOutput, calls=%fused_computation.1 | convolution fusion | flops 1074003968 | bytes 9437184 | tf_op jit(solution)/shard_map/dot_general | solution.py:45
  189.8 3.9 %all-to-all-start.5 = ((bf16[8,16,2048]{2,1,0:T(8,128)(2,1)}), bf16[8,16,2048]{2,1,0:T(8,128)(2,1)S(1)}, u32[]{:S(2)}, u32[]{:S(2)}) async-start(bf16[8,16,2048]{2,1,0:T(8,128)(2,1)} %bitcast.5), calls=%async_computation.5 | async-start | bytes 1048576 | tf_op jit(solution)/shard_map/all_to_all | solution.py:421
  195.7 2.1 collective-permute-start.29
  201.0 2.4 collective-permute-done.29
  203.5 7.2 %convolution_convert_fusion = bf16[128,2048]{1,0:T(8,128)(2,1)} fusion(bf16[128,2048]{1,0:T(8,128)(2,1)S(1)} %pad_maximum_fusion.1, bf16[2048,2048]{1,0:T(8,128)(2,1)} %head_ref.1), kind=kOutput, calls=%fused_computation | convolution fusion | flops 1074003968 | bytes 9437184 | tf_op jit(solution)/shard_map/dot_general | solution.py:45
  210.7 4.1 %all-to-all-start.4 = ((bf16[8,16,2048]{2,1,0:T(8,128)(2,1)}), bf16[8,16,2048]{2,1,0:T(8,128)(2,1)}, u32[]{:S(2)}, u32[]{:S(2)}) async-start(bf16[8,16,2048]{2,1,0:T(8,128)(2,1)} %bitcast.6), calls=%async_computation.4 | async-start | bytes 1048576 | tf_op jit(solution)/shard_map/all_to_all | solution.py:421
  216.6 2.0 collective-permute-start.31
  218.7 5.9 %all-to-all-done.4 = bf16[8,16,2048]{2,1,0:T(8,128)(2,1)} async-done(((bf16[8,16,2048]{2,1,0:T(8,128)(2,1)}), bf16[8,16,2048]{2,1,0:T(8,128)(2,1)}, u32[]{:S(2)}, u32[]{:S(2)}) %all-to-all-start.4) | async-done | bytes 524320 | tf_op jit(solution)/shard_map/all_to_all | solution.py:421
  225.4 3.5 %all-to-all-start.6 = ((bf16[8,16,2048]{2,1,0:T(8,128)(2,1)}), bf16[8,16,2048]{2,1,0:T(8,128)(2,1)S(1)}, u32[]{:S(2)}, u32[]{:S(2)}) async-start(bf16[8,16,2048]{2,1,0:T(8,128)(2,1)} %broadcast_in_dim.13), calls=%async_computation.6 | async-start | bytes 1048576 | tf_op jit(solution)/shard_map/all_to_all | solution.py:426
  232.3 1.8 collective-permute-start.32
  234.1 3.3 %collective-permute-done.30 = bf16[256,256]{1,0:T(8,128)(2,1)S(1)} collective-permute-done((bf16[256,256]{1,0:T(8,128)(2,1)S(1)}, bf16[256,256]{1,0:T(8,128)(2,1)S(1)}, u32[]{:S(2)}, u32[]{:S(2)}) %collective-permute-start.30) | collective-permute-done | bytes 131104 | tf_op jit(solution)/shard_map/ppermute | solution.py:23
  239.4 3.5 %all-to-all-start.7 = ((bf16[8,16,2048]{2,1,0:T(8,128)(2,1)}), bf16[8,16,2048]{2,1,0:T(8,128)(2,1)S(1)}, u32[]{:S(2)}, u32[]{:S(2)}) async-start(bf16[8,16,2048]{2,1,0:T(8,128)(2,1)} %broadcast_in_dim.14), calls=%async_computation.7 | async-start | bytes 1048576 | tf_op jit(solution)/shard_map/all_to_all | solution.py:426
  245.9 6.8 %all-to-all-done.7 = bf16[8,16,2048]{2,1,0:T(8,128)(2,1)S(1)} async-done(((bf16[8,16,2048]{2,1,0:T(8,128)(2,1)}), bf16[8,16,2048]{2,1,0:T(8,128)(2,1)S(1)}, u32[]{:S(2)}, u32[]{:S(2)}) %all-to-all-start.7) | async-done | bytes 524320 | tf_op jit(solution)/shard_map/all_to_all | solution.py:426
  252.6 1.6 maximum_convert_fusion
  (152 shorter events, 56.0 us)
Async XLA Ops:
  0.6 21.9 %copy-start = (bf16[1024,1024]{1,0:T(8,128)(2,1)S(1)}, bf16[1024,1024]{1,0:T(8,128)(2,1)}, u32[]{:S(2)}) copy-start(bf16[1024,1024]{1,0:T(8,128)(2,1)} %param.6) | copy-start | bytes 6291460
  5.4 17.1 %copy-start.25 = (bf16[1024,256]{1,0:T(8,128)(2,1)S(1)}, bf16[1024,256]{1,0:T(8,128)(2,1)}, u32[]{:S(2)}) copy-start(bf16[1024,256]{1,0:T(8,128)(2,1)} %param.9) | copy-start | bytes 1572868
  11.2 13.0 %collective-permute-start.1 = (f16[32,2048]{1,0:T(8,128)(2,1)S(1)}, f16[32,2048]{1,0:T(8,128)(2,1)}, u32[]{:S(2)}, u32[]{:S(2)}) collective-permute-start(f16[32,2048]{1,0:T(8,128)(2,1)S(1)} %convert_element_type.210), channel_id=1, source_target_pairs={{0,8},{8,0},{16,24},{24,16},{1,9},{9,1},{17,25},{25,17},{2,10},{10... | collective-permute-start | bytes 393224 | tf_op jit(solution)/shard_map/ppermute | solution.py:23
  15.1 21.7 %collective-permute-start = (f32[8,2048]{1,0:T(8,128)S(1)}, f32[8,2048]{1,0:T(8,128)S(1)}, u32[]{:S(2)}, u32[]{:S(2)}) collective-permute-start(f32[8,2048]{1,0:T(8,128)S(1)} %slice.12), channel_id=1, source_target_pairs={{8,0},{16,8},{24,16},{9,1},{17,9},{25,17},{10,2},{18,10},{26,18},{... | collective-permute-start | bytes 196616 | tf_op jit(solution)/shard_map/ppermute | solution.py:460
  17.1 15.0 %collective-permute-start.4 = (f16[32,2048]{1,0:T(8,128)(2,1)}, f16[32,2048]{1,0:T(8,128)(2,1)}, u32[]{:S(2)}, u32[]{:S(2)}) collective-permute-start(f16[32,2048]{1,0:T(8,128)(2,1)} %convert_element_type.213), channel_id=1, source_target_pairs={{0,8},{8,0},{16,24},{24,16},{1,9},{9,1},{17,25},{25,17},{2,10},{10... | collective-permute-start | bytes 393224 | tf_op jit(solution)/shard_map/ppermute | solution.py:23
  20.4 13.2 %collective-permute-start.3 = (f16[32,2048]{1,0:T(8,128)(2,1)}, f16[32,2048]{1,0:T(8,128)(2,1)}, u32[]{:S(2)}, u32[]{:S(2)}) collective-permute-start(f16[32,2048]{1,0:T(8,128)(2,1)} %convert_element_type.212), channel_id=1, source_target_pairs={{0,8},{8,0},{16,24},{24,16},{1,9},{9,1},{17,25},{25,17},{2,10},{10... | collective-permute-start | bytes 393224 | tf_op jit(solution)/shard_map/ppermute | solution.py:23
  20.4 14.8 %collective-permute-start.2 = (f16[32,2048]{1,0:T(8,128)(2,1)S(1)}, f16[32,2048]{1,0:T(8,128)(2,1)}, u32[]{:S(2)}, u32[]{:S(2)}) collective-permute-start(f16[32,2048]{1,0:T(8,128)(2,1)S(1)} %convert_element_type.211), channel_id=1, source_target_pairs={{0,8},{8,0},{16,24},{24,16},{1,9},{9,1},{17,25},{25,17},{2,10},{10... | collective-permute-start | bytes 393224 | tf_op jit(solution)/shard_map/ppermute | solution.py:23
  25.1 32.4 %collective-permute-start.5 = (f16[32,2048]{1,0:T(8,128)(2,1)S(1)}, f16[32,2048]{1,0:T(8,128)(2,1)}, u32[]{:S(2)}, u32[]{:S(2)}) collective-permute-start(f16[32,2048]{1,0:T(8,128)(2,1)S(1)} %add_convert_fusion.11), channel_id=1, source_target_pairs={{0,16},{8,24},{16,0},{24,8},{1,17},{9,25},{17,1},{25,9},{2,18},{10... | collective-permute-start | bytes 393224 | tf_op jit(solution)/shard_map/ppermute | solution.py:23
  27.8 19.7 %all-to-all-start = ((f32[8,128,256]{2,1,0:T(8,128)}), f32[8,128,256]{2,1,0:T(8,128)}, u32[]{:S(2)}, u32[]{:S(2)}) async-start(f32[8,128,256]{2,1,0:T(8,128)} %bitcast.22), calls=%async_computation | async-start | bytes 2097152 | tf_op jit(solution)/shard_map/all_to_all | solution.py:421
  49.6 13.2 %all-to-all-start.1 = ((bf16[8,128,256]{2,1,0:T(8,128)(2,1)}), bf16[8,128,256]{2,1,0:T(8,128)(2,1)S(1)}, u32[]{:S(2)}, u32[]{:S(2)}) async-start(bf16[8,128,256]{2,1,0:T(8,128)(2,1)} %broadcast_in_dim.10), calls=%async_computation.1 | async-start | bytes 1048576 | tf_op jit(solution)/shard_map/all_to_all | solution.py:426
  54.1 15.1 %collective-permute-start.7 = (f16[32,2048]{1,0:T(8,128)(2,1)}, f16[32,2048]{1,0:T(8,128)(2,1)}, u32[]{:S(2)}, u32[]{:S(2)}) collective-permute-start(f16[32,2048]{1,0:T(8,128)(2,1)} %add_convert_fusion.10), channel_id=1, source_target_pairs={{0,16},{8,24},{16,0},{24,8},{1,17},{9,25},{17,1},{25,9},{2,18},{10... | collective-permute-start | bytes 393224 | tf_op jit(solution)/shard_map/ppermute | solution.py:23
  54.5 17.8 %collective-permute-start.10 = (f16[32,2048]{1,0:T(8,128)(2,1)}, f16[32,2048]{1,0:T(8,128)(2,1)}, u32[]{:S(2)}, u32[]{:S(2)}) collective-permute-start(f16[32,2048]{1,0:T(8,128)(2,1)} %add_convert_fusion.9), channel_id=1, source_target_pairs={{0,16},{8,24},{16,0},{24,8},{1,17},{9,25},{17,1},{25,9},{2,18},{10... | collective-permute-start | bytes 393224 | tf_op jit(solution)/shard_map/ppermute | solution.py:23
  57.1 17.8 %collective-permute-start.9 = (f16[32,2048]{1,0:T(8,128)(2,1)}, f16[32,2048]{1,0:T(8,128)(2,1)}, u32[]{:S(2)}, u32[]{:S(2)}) collective-permute-start(f16[32,2048]{1,0:T(8,128)(2,1)} %add_convert_fusion.8), channel_id=1, source_target_pairs={{0,16},{8,24},{16,0},{24,8},{1,17},{9,25},{17,1},{25,9},{2,18},{10... | collective-permute-start | bytes 393224 | tf_op jit(solution)/shard_map/ppermute | solution.py:23
  58.4 18.1 %collective-permute-start.11 = (bf16[32,2048]{1,0:T(8,128)(2,1)S(1)}, bf16[32,2048]{1,0:T(8,128)(2,1)S(1)}, u32[]{:S(2)}, u32[]{:S(2)}) collective-permute-start(bf16[32,2048]{1,0:T(8,128)(2,1)S(1)} %multiply_convert_fusion.7.rest_3_), channel_id=1, source_target_pairs={{0,8},{8,0},{16,24},{24,16},{1,9},{9,1},{17,25},{25,17},{2,10},{10... | collective-permute-start | bytes 393224 | tf_op jit(solution)/shard_map/ppermute | solution.py:23
  64.1 6.2 %collective-permute-start.6 = (f32[8,128]{1,0:T(8,128)S(1)}, f32[8,128]{1,0:T(8,128)S(1)}, u32[]{:S(2)}, u32[]{:S(2)}) collective-permute-start(f32[8,128]{1,0:T(8,128)S(1)} %broadcast_in_dim.11), channel_id=1, source_target_pairs={{0,8},{8,0},{16,24},{24,16},{1,9},{9,1},{17,25},{25,17},{2,10},{10... | collective-permute-start | bytes 12296 | tf_op jit(solution)/shard_map/ppermute | solution.py:23
  70.3 7.4 %collective-permute-start.12 = (bf16[32,2048]{1,0:T(8,128)(2,1)S(1)}, bf16[32,2048]{1,0:T(8,128)(2,1)S(1)}, u32[]{:S(2)}, u32[]{:S(2)}) collective-permute-start(bf16[32,2048]{1,0:T(8,128)(2,1)S(1)} %multiply_convert_fusion.6.rest_5_), channel_id=1, source_target_pairs={{0,8},{8,0},{16,24},{24,16},{1,9},{9,1},{17,25},{25,17},{2,10},{10... | collective-permute-start | bytes 393224 | tf_op jit(solution)/shard_map/ppermute | solution.py:23
  71.0 5.5 %collective-permute-start.8 = (f32[8,128]{1,0:T(8,128)S(1)}, f32[8,128]{1,0:T(8,128)S(1)}, u32[]{:S(2)}, u32[]{:S(2)}) collective-permute-start(f32[8,128]{1,0:T(8,128)S(1)} %broadcast_maximum_fusion), channel_id=1, source_target_pairs={{0,16},{8,24},{16,0},{24,8},{1,17},{9,25},{17,1},{25,9},{2,18},{10... | collective-permute-start | bytes 12296 | tf_op jit(solution)/shard_map/ppermute | solution.py:23
  73.3 9.9 %collective-permute-start.13 = (bf16[32,2048]{1,0:T(8,128)(2,1)S(1)}, bf16[32,2048]{1,0:T(8,128)(2,1)S(1)}, u32[]{:S(2)}, u32[]{:S(2)}) collective-permute-start(bf16[32,2048]{1,0:T(8,128)(2,1)S(1)} %multiply_convert_fusion.5.rest_7_), channel_id=1, source_target_pairs={{0,8},{8,0},{16,24},{24,16},{1,9},{9,1},{17,25},{25,17},{2,10},{10... | collective-permute-start | bytes 393224 | tf_op jit(solution)/shard_map/ppermute | solution.py:23
  75.9 7.3 %collective-permute-start.14 = (bf16[32,2048]{1,0:T(8,128)(2,1)S(1)}, bf16[32,2048]{1,0:T(8,128)(2,1)S(1)}, u32[]{:S(2)}, u32[]{:S(2)}) collective-permute-start(bf16[32,2048]{1,0:T(8,128)(2,1)S(1)} %multiply_convert_fusion.4.rest_9_), channel_id=1, source_target_pairs={{0,8},{8,0},{16,24},{24,16},{1,9},{9,1},{17,25},{25,17},{2,10},{10... | collective-permute-start | bytes 393224 | tf_op jit(solution)/shard_map/ppermute | solution.py:23
  121.7 15.2 %copy-start.17 = (f32[32,2048]{1,0:T(8,128)S(1)}, f32[32,2048]{1,0:T(8,128)}, u32[]{:S(2)}) copy-start(f32[32,2048]{1,0:T(8,128)} %copy-done.16) | copy-start | bytes 786436
  122.4 8.3 %collective-permute-start.15 = (f16[32,2048]{1,0:T(8,128)(2,1)S(1)}, f16[32,2048]{1,0:T(8,128)(2,1)S(1)}, u32[]{:S(2)}, u32[]{:S(2)}) collective-permute-start(f16[32,2048]{1,0:T(8,128)(2,1)S(1)} %convert_element_type.236), channel_id=1, source_target_pairs={{0,8},{8,0},{16,24},{24,16},{1,9},{9,1},{17,25},{25,17},{2,10},{10... | collective-permute-start | bytes 393224 | tf_op jit(solution)/shard_map/ppermute | solution.py:23
  122.4 15.4 %copy-start.15 = (f32[32,2048]{1,0:T(8,128)S(1)}, f32[32,2048]{1,0:T(8,128)}, u32[]{:S(2)}) copy-start(f32[32,2048]{1,0:T(8,128)} %copy-done.14) | copy-start | bytes 786436
  123.4 13.4 %collective-permute-start.18 = (f16[32,2048]{1,0:T(8,128)(2,1)S(1)}, f16[32,2048]{1,0:T(8,128)(2,1)}, u32[]{:S(2)}, u32[]{:S(2)}) collective-permute-start(f16[32,2048]{1,0:T(8,128)(2,1)S(1)} %convert_element_type.239), channel_id=1, source_target_pairs={{0,8},{8,0},{16,24},{24,16},{1,9},{9,1},{17,25},{25,17},{2,10},{10... | collective-permute-start | bytes 393224 | tf_op jit(solution)/shard_map/ppermute | solution.py:23
  126.4 12.3 %copy-start.13 = (f32[32,2048]{1,0:T(8,128)S(1)}, f32[32,2048]{1,0:T(8,128)}, u32[]{:S(2)}) copy-start(f32[32,2048]{1,0:T(8,128)} %copy-done.12) | copy-start | bytes 786436
  128.1 9.7 %collective-permute-start.17 = (f16[32,2048]{1,0:T(8,128)(2,1)S(1)}, f16[32,2048]{1,0:T(8,128)(2,1)}, u32[]{:S(2)}, u32[]{:S(2)}) collective-permute-start(f16[32,2048]{1,0:T(8,128)(2,1)S(1)} %convert_element_type.238), channel_id=1, source_target_pairs={{0,8},{8,0},{16,24},{24,16},{1,9},{9,1},{17,25},{25,17},{2,10},{10... | collective-permute-start | bytes 393224 | tf_op jit(solution)/shard_map/ppermute | solution.py:23
  128.1 10.6 %collective-permute-start.16 = (f16[32,2048]{1,0:T(8,128)(2,1)}, f16[32,2048]{1,0:T(8,128)(2,1)}, u32[]{:S(2)}, u32[]{:S(2)}) collective-permute-start(f16[32,2048]{1,0:T(8,128)(2,1)} %convert_element_type.237), channel_id=1, source_target_pairs={{0,8},{8,0},{16,24},{24,16},{1,9},{9,1},{17,25},{25,17},{2,10},{10... | collective-permute-start | bytes 393224 | tf_op jit(solution)/shard_map/ppermute | solution.py:23
  132.3 32.2 %collective-permute-start.19 = (f16[32,2048]{1,0:T(8,128)(2,1)S(1)}, f16[32,2048]{1,0:T(8,128)(2,1)}, u32[]{:S(2)}, u32[]{:S(2)}) collective-permute-start(f16[32,2048]{1,0:T(8,128)(2,1)S(1)} %add_convert_fusion.7), channel_id=1, source_target_pairs={{0,16},{8,24},{16,0},{24,8},{1,17},{9,25},{17,1},{25,9},{2,18},{10... | collective-permute-start | bytes 393224 | tf_op jit(solution)/shard_map/ppermute | solution.py:23
  132.4 21.1 %copy-start.21 = (f32[128,256]{1,0:T(8,128)S(1)}, f32[128,256]{1,0:T(8,128)}, u32[]{:S(2)}) copy-start(f32[128,256]{1,0:T(8,128)} %copy-done.20) | copy-start | bytes 393220
  132.4 19.8 %all-to-all-start.2 = ((f32[8,128,256]{2,1,0:T(8,128)}), f32[8,128,256]{2,1,0:T(8,128)}, u32[]{:S(2)}, u32[]{:S(2)}) async-start(f32[8,128,256]{2,1,0:T(8,128)} %bitcast.21), calls=%async_computation.2 | async-start | bytes 2097152 | tf_op jit(solution)/shard_map/all_to_all | solution.py:421
  154.4 13.2 %all-to-all-start.3 = ((bf16[8,128,256]{2,1,0:T(8,128)(2,1)}), bf16[8,128,256]{2,1,0:T(8,128)(2,1)S(1)}, u32[]{:S(2)}, u32[]{:S(2)}) async-start(bf16[8,128,256]{2,1,0:T(8,128)(2,1)} %broadcast_in_dim.12), calls=%async_computation.3 | async-start | bytes 1048576 | tf_op jit(solution)/shard_map/all_to_all | solution.py:426
  158.6 15.8 %collective-permute-start.20 = (f16[32,2048]{1,0:T(8,128)(2,1)S(1)}, f16[32,2048]{1,0:T(8,128)(2,1)S(1)}, u32[]{:S(2)}, u32[]{:S(2)}) collective-permute-start(f16[32,2048]{1,0:T(8,128)(2,1)S(1)} %add_convert_fusion.6), channel_id=1, source_target_pairs={{0,16},{8,24},{16,0},{24,8},{1,17},{9,25},{17,1},{25,9},{2,18},{10... | collective-permute-start | bytes 393224 | tf_op jit(solution)/shard_map/ppermute | solution.py:23
  161.6 32.1 %collective-permute-start.23 = (f16[32,2048]{1,0:T(8,128)(2,1)S(1)}, f16[32,2048]{1,0:T(8,128)(2,1)}, u32[]{:S(2)}, u32[]{:S(2)}) collective-permute-start(f16[32,2048]{1,0:T(8,128)(2,1)S(1)} %add_convert_fusion.5), channel_id=1, source_target_pairs={{0,16},{8,24},{16,0},{24,8},{1,17},{9,25},{17,1},{25,9},{2,18},{10... | collective-permute-start | bytes 393224 | tf_op jit(solution)/shard_map/ppermute | solution.py:23
  161.7 33.1 %collective-permute-start.22 = (f16[32,2048]{1,0:T(8,128)(2,1)S(1)}, f16[32,2048]{1,0:T(8,128)(2,1)}, u32[]{:S(2)}, u32[]{:S(2)}) collective-permute-start(f16[32,2048]{1,0:T(8,128)(2,1)S(1)} %add_convert_fusion.4), channel_id=1, source_target_pairs={{0,16},{8,24},{16,0},{24,8},{1,17},{9,25},{17,1},{25,9},{2,18},{10... | collective-permute-start | bytes 393224 | tf_op jit(solution)/shard_map/ppermute | solution.py:23
  165.5 11.8 %collective-permute-start.24 = (bf16[32,2048]{1,0:T(8,128)(2,1)S(1)}, bf16[32,2048]{1,0:T(8,128)(2,1)S(1)}, u32[]{:S(2)}, u32[]{:S(2)}) collective-permute-start(bf16[32,2048]{1,0:T(8,128)(2,1)S(1)} %multiply_convert_fusion.3), channel_id=1, source_target_pairs={{0,8},{8,0},{16,24},{24,16},{1,9},{9,1},{17,25},{25,17},{2,10},{10... | collective-permute-start | bytes 393224 | tf_op jit(solution)/shard_map/ppermute | solution.py:23
  174.5 8.1 %collective-permute-start.25 = (bf16[32,2048]{1,0:T(8,128)(2,1)S(1)}, bf16[32,2048]{1,0:T(8,128)(2,1)S(1)}, u32[]{:S(2)}, u32[]{:S(2)}) collective-permute-start(bf16[32,2048]{1,0:T(8,128)(2,1)S(1)} %multiply_convert_fusion.2), channel_id=1, source_target_pairs={{0,8},{8,0},{16,24},{24,16},{1,9},{9,1},{17,25},{25,17},{2,10},{10... | collective-permute-start | bytes 393224 | tf_op jit(solution)/shard_map/ppermute | solution.py:23
  175.4 22.4 %collective-permute-start.21 = (bf16[256,256]{1,0:T(8,128)(2,1)}, bf16[256,256]{1,0:T(8,128)(2,1)}, u32[]{:S(2)}, u32[]{:S(2)}) collective-permute-start(bf16[256,256]{1,0:T(8,128)(2,1)} %get-tuple-element.185), channel_id=1, source_target_pairs={{0,8},{8,0},{16,24},{24,16},{1,9},{9,1},{17,25},{25,17},{2,10},{10... | collective-permute-start | bytes 393224 | tf_op jit(solution)/shard_map/ppermute | solution.py:23
  178.0 20.8 %collective-permute-start.28 = (bf16[256,256]{1,0:T(8,128)(2,1)S(1)}, bf16[256,256]{1,0:T(8,128)(2,1)}, u32[]{:S(2)}, u32[]{:S(2)}) collective-permute-start(bf16[256,256]{1,0:T(8,128)(2,1)S(1)} %get-tuple-element.186), channel_id=1, source_target_pairs={{0,8},{8,0},{16,24},{24,16},{1,9},{9,1},{17,25},{25,17},{2,10},{10... | collective-permute-start | bytes 393224 | tf_op jit(solution)/shard_map/ppermute | solution.py:23
  189.8 20.9 %all-to-all-start.5 = ((bf16[8,16,2048]{2,1,0:T(8,128)(2,1)}), bf16[8,16,2048]{2,1,0:T(8,128)(2,1)S(1)}, u32[]{:S(2)}, u32[]{:S(2)}) async-start(bf16[8,16,2048]{2,1,0:T(8,128)(2,1)} %bitcast.5), calls=%async_computation.5 | async-start | bytes 1048576 | tf_op jit(solution)/shard_map/all_to_all | solution.py:421
  194.6 6.4 %collective-permute-start.27 = (bf16[32,2048]{1,0:T(8,128)(2,1)S(1)}, bf16[32,2048]{1,0:T(8,128)(2,1)S(1)}, u32[]{:S(2)}, u32[]{:S(2)}) collective-permute-start(bf16[32,2048]{1,0:T(8,128)(2,1)S(1)} %multiply_convert_fusion.1), channel_id=1, source_target_pairs={{0,8},{8,0},{16,24},{24,16},{1,9},{9,1},{17,25},{25,17},{2,10},{10... | collective-permute-start | bytes 393224 | tf_op jit(solution)/shard_map/ppermute | solution.py:23
  195.7 7.7 %collective-permute-start.29 = (bf16[32,2048]{1,0:T(8,128)(2,1)S(1)}, bf16[32,2048]{1,0:T(8,128)(2,1)S(1)}, u32[]{:S(2)}, u32[]{:S(2)}) collective-permute-start(bf16[32,2048]{1,0:T(8,128)(2,1)S(1)} %multiply_convert_fusion), channel_id=1, source_target_pairs={{0,8},{8,0},{16,24},{24,16},{1,9},{9,1},{17,25},{25,17},{2,10},{10... | collective-permute-start | bytes 393224 | tf_op jit(solution)/shard_map/ppermute | solution.py:23
  203.5 12.3 %copy-start.8 = (f32[1024,1]{1,0:T(8,128)S(1)}, f32[1024,1]{1,0:T(8,128)}, u32[]{:S(2)}) copy-start(f32[1024,1]{1,0:T(8,128)} %copy-done.7) | copy-start | bytes 12292
  210.7 13.9 %all-to-all-start.4 = ((bf16[8,16,2048]{2,1,0:T(8,128)(2,1)}), bf16[8,16,2048]{2,1,0:T(8,128)(2,1)}, u32[]{:S(2)}, u32[]{:S(2)}) async-start(bf16[8,16,2048]{2,1,0:T(8,128)(2,1)} %bitcast.6), calls=%async_computation.4 | async-start | bytes 1048576 | tf_op jit(solution)/shard_map/all_to_all | solution.py:421
  214.8 15.2 %collective-permute-start.26 = (bf16[256,256]{1,0:T(8,128)(2,1)S(1)}, bf16[256,256]{1,0:T(8,128)(2,1)}, u32[]{:S(2)}, u32[]{:S(2)}) collective-permute-start(bf16[256,256]{1,0:T(8,128)(2,1)S(1)} %add_convert_fusion.3), channel_id=1, source_target_pairs={{0,16},{8,24},{16,0},{24,8},{1,17},{9,25},{17,1},{25,9},{2,18},{10... | collective-permute-start | bytes 393224 | tf_op jit(solution)/shard_map/ppermute | solution.py:23
  216.6 14.7 %collective-permute-start.31 = (bf16[256,256]{1,0:T(8,128)(2,1)S(1)}, bf16[256,256]{1,0:T(8,128)(2,1)}, u32[]{:S(2)}, u32[]{:S(2)}) collective-permute-start(bf16[256,256]{1,0:T(8,128)(2,1)S(1)} %add_convert_fusion.2), channel_id=1, source_target_pairs={{0,16},{8,24},{16,0},{24,8},{1,17},{9,25},{17,1},{25,9},{2,18},{10... | collective-permute-start | bytes 393224 | tf_op jit(solution)/shard_map/ppermute | solution.py:23
  225.4 13.2 %all-to-all-start.6 = ((bf16[8,16,2048]{2,1,0:T(8,128)(2,1)}), bf16[8,16,2048]{2,1,0:T(8,128)(2,1)S(1)}, u32[]{:S(2)}, u32[]{:S(2)}) async-start(bf16[8,16,2048]{2,1,0:T(8,128)(2,1)} %broadcast_in_dim.13), calls=%async_computation.6 | async-start | bytes 1048576 | tf_op jit(solution)/shard_map/all_to_all | solution.py:426
  231.0 6.4 %collective-permute-start.30 = (bf16[256,256]{1,0:T(8,128)(2,1)S(1)}, bf16[256,256]{1,0:T(8,128)(2,1)S(1)}, u32[]{:S(2)}, u32[]{:S(2)}) collective-permute-start(bf16[256,256]{1,0:T(8,128)(2,1)S(1)} %add_convert_fusion.1), channel_id=1, source_target_pairs={{0,8},{8,0},{16,24},{24,16},{1,9},{9,1},{17,25},{25,17},{2,10},{10... | collective-permute-start | bytes 393224 | tf_op jit(solution)/shard_map/ppermute | solution.py:23
  232.3 11.6 %collective-permute-start.32 = (bf16[256,256]{1,0:T(8,128)(2,1)S(1)}, bf16[256,256]{1,0:T(8,128)(2,1)}, u32[]{:S(2)}, u32[]{:S(2)}) collective-permute-start(bf16[256,256]{1,0:T(8,128)(2,1)S(1)} %add_convert_fusion), channel_id=1, source_target_pairs={{0,8},{8,0},{16,24},{24,16},{1,9},{9,1},{17,25},{25,17},{2,10},{10... | collective-permute-start | bytes 393224 | tf_op jit(solution)/shard_map/ppermute | solution.py:23
  239.4 13.2 %all-to-all-start.7 = ((bf16[8,16,2048]{2,1,0:T(8,128)(2,1)}), bf16[8,16,2048]{2,1,0:T(8,128)(2,1)S(1)}, u32[]{:S(2)}, u32[]{:S(2)}) async-start(bf16[8,16,2048]{2,1,0:T(8,128)(2,1)} %broadcast_in_dim.14), calls=%async_computation.7 | async-start | bytes 1048576 | tf_op jit(solution)/shard_map/all_to_all | solution.py:426
  (19 other events, 26.5 us)

commit v6 on v4

--- a/solution.py
+++ b/solution.py
@@ -11,6 +11,7 @@
 PARTS = 4
 BLOCK = 256
 VOCAB_SCALE = 128.0
+PRE_SCALE = 64.0
 F32 = jnp.float32
 BF16 = jnp.bfloat16
 F16 = jnp.float16
@@ -109,6 +110,82 @@
         cost_estimate=cost(4 * rows * cols, 4 * rows * cols, rows * cols),
         name="target_sums",
     )(target, target, incoming)
+
+
+def target_pass(target, incoming):
+    rows, cols = target.shape
+    block = min(BLOCK, rows)
+
+    def body(target_ref, next_ref, incoming_ref, prob_ref, entropy_ref, window):
+        shifted = shift_in(target_ref, next_ref, incoming_ref, window)
+        first = lax.axis_index("grp") * rows + pl.program_id(0) * block
+        count = lax.axis_size("grp") * rows
+        row = first + lax.broadcasted_iota(jnp.int32, (block, 1), 0)
+        live = jnp.where(row < count - HEAD, 1.0, 0.0)
+        below = shifted - jnp.max(shifted, -1, keepdims=True)
+        raised = jnp.exp(below)
+        total = jnp.sum(raised, -1, keepdims=True)
+        scale = live / total
+        prob_ref[...] = raised * scale
+        entropy_ref[...] = scale * jnp.sum(raised * below, -1, keepdims=True) - live * jnp.log(total)
+
+    per = block // 8
+    return pl.pallas_call(
+        body,
+        grid=(rows // block,),
+        in_specs=[
+            row_spec(block, cols),
+            pl.BlockSpec((8, cols), lambda i: (jnp.minimum((i + 1) * per, rows // 8 - 1), 0)),
+            whole_spec(8, cols),
+        ],
+        out_specs=[row_spec(block, cols), row_spec(block, 1)],
+        out_shape=[
+            jax.ShapeDtypeStruct((rows, cols), F32),
+            jax.ShapeDtypeStruct((rows, 1), F32),
+        ],
+        scratch_shapes=[pltpu.VMEM((block + 8, cols), F32)],
+        compiler_params=params(50),
+        cost_estimate=cost(6 * rows * cols, 8 * rows * cols, rows * cols),
+        name="target_pass",
+    )(target, target, incoming)
+
+
+def target_probs(target, incoming, top, total):
+    rows, cols = target.shape
+    block = min(BLOCK, rows)
+
+    def body(target_ref, next_ref, incoming_ref, top_ref, sum_ref, prob_ref, entropy_ref, window):
+        shifted = shift_in(target_ref, next_ref, incoming_ref, window)
+        first = lax.axis_index("grp") * rows + pl.program_id(0) * block
+        count = lax.axis_size("grp") * rows
+        row = first + lax.broadcasted_iota(jnp.int32, (block, 1), 0)
+        live = jnp.where(row < count - HEAD, 1.0, 0.0)
+        log_target = shifted - (top_ref[...] + jnp.log(sum_ref[...]))
+        prob = jnp.exp(log_target) * live
+        prob_ref[...] = prob
+        entropy_ref[...] = jnp.sum(prob * log_target, -1, keepdims=True)
+
+    per = block // 8
+    return pl.pallas_call(
+        body,
+        grid=(rows // block,),
+        in_specs=[
+            row_spec(block, cols),
+            pl.BlockSpec((8, cols), lambda i: (jnp.minimum((i + 1) * per, rows // 8 - 1), 0)),
+            whole_spec(8, cols),
+            row_spec(block, 1),
+            row_spec(block, 1),
+        ],
+        out_specs=[row_spec(block, cols), row_spec(block, 1)],
+        out_shape=[
+            jax.ShapeDtypeStruct((rows, cols), F32),
+            jax.ShapeDtypeStruct((rows, 1), F32),
+        ],
+        scratch_shapes=[pltpu.VMEM((block + 8, cols), F32)],
+        compiler_params=params(50),
+        cost_estimate=cost(6 * rows * cols, 8 * rows * cols, rows * cols),
+        name="target_probs",
+    )(target, target, incoming, top, total)
 
 
 def vocab_parts(up_weight, head_weight, width):
@@ -160,7 +237,7 @@
             pltpu.VMEM((rank, cols), F32),
             pltpu.SemaphoreType.DMA((PARTS,)),
         ],
-        compiler_params=pltpu.CompilerParams(vmem_limit_bytes=24 << 20),
+        compiler_params=pltpu.CompilerParams(vmem_limit_bytes=56 << 20),
         cost_estimate=cost(2 * rank * depth * cols, 2 * depth * cols, 0),
         name="vocab_parts",
     )(up_weight, head_weight)
@@ -173,7 +250,7 @@
     block = min(BLOCK, rows)
 
     def body(target_ref, acts_ref, own_ref, other_ref, *rest):
-        draft_ref, proj_ref, most_ref, top_ref, sum_ref = rest[-5:]
+        draft_ref, proj_ref, top_ref, sum_ref = rest[-4:]
 
         @pl.when(pl.program_id(0) == 0)
         def _():
@@ -182,10 +259,7 @@
             proj_ref[
                 pl.ds(pl.multiple_of((1 - mine) * half_rank, half_rank), half_rank), :
             ] = other_ref[...]
-            most_ref[...] = jnp.zeros_like(most_ref)
-
-        size = jnp.max(jnp.abs(acts_ref[...].astype(F32)), 0, keepdims=True)
-        most_ref[...] = jnp.maximum(most_ref[...], jnp.max(size, -1, keepdims=True))
+
         draft = target_ref[...] + jnp.dot(
             acts_ref[...], proj_ref[...], preferred_element_type=F32
         )
@@ -200,7 +274,7 @@
         sum_ref[...] = total
 
     carried = () if sums is None else tuple(sums)
-    draft, proj, most, top, total = pl.pallas_call(
+    draft, proj, top, total = pl.pallas_call(
         body,
         grid=(rows // block,),
         in_specs=[
@@ -213,48 +287,40 @@
         out_specs=[
             row_spec(block, width),
             whole_spec(rank, width),
-            whole_spec(8, 128),
             row_spec(block, 1),
             row_spec(block, 1),
         ],
         out_shape=[
             jax.ShapeDtypeStruct((rows, width), F32),
             jax.ShapeDtypeStruct((rank, width), BF16),
-            jax.ShapeDtypeStruct((8, 128), F32),
             jax.ShapeDtypeStruct((rows, 1), F32),
             jax.ShapeDtypeStruct((rows, 1), F32),
         ],
-        compiler_params=params(24),
+        compiler_params=params(54),
         cost_estimate=cost(2 * rows * rank * width, 8 * rows * width, rows * width),
         name="draft_chunk",
     )(target, acts, *pieces, *carried)
-    return draft, proj, most, (top, total)
-
-
-def grad_chunk(draft, target, incoming, label, acts, vocab_proj, column, sums, sizes, carried):
+    return draft, proj, (top, total)
+
+
+def grad_chunk(draft, prob, label, acts, vocab_proj, column, sums, carried):
     rows, width = draft.shape
     rank = acts.shape[1]
     half_rank = rank // 2
     block = min(BLOCK, rows)
-    bounds = sizes.shape[0]
-
-    def body(
-        draft_ref, target_ref, next_ref, incoming_ref, label_ref, acts_ref, proj_ref,
-        top_ref, sum_ref, target_top_ref, target_sum_ref, sizes_ref, *rest
-    ):
-        away_ref, kept_ref, scale_ref, act_ref, loss_ref, totals, window = rest[-7:]
+
+    def body(draft_ref, prob_ref, label_ref, acts_ref, proj_ref, top_ref, sum_ref, *rest):
+        away_ref, kept_ref, act_ref, loss_ref, totals = rest[-5:]
         step = pl.program_id(0)
+        first = lax.axis_index("grp") * rows + step * block
         count = lax.axis_size("grp") * rows
-        row = lax.axis_index("grp") * rows + step * block
-        row = row + lax.broadcasted_iota(jnp.int32, (block, 1), 0)
+        row = first + lax.broadcasted_iota(jnp.int32, (block, 1), 0)
         live = jnp.where(row < count - HEAD, 1.0, 0.0)
-        shifted = shift_in(target_ref, next_ref, incoming_ref, window)
-        log_target = shifted - (target_top_ref[...] + jnp.log(target_sum_ref[...]))
         log_draft = draft_ref[...] - (top_ref[...] + jnp.log(sum_ref[...]))
-        prob = live * jnp.exp(log_target)
+        prob = prob_ref[...]
         place = lax.broadcasted_iota(jnp.int32, (block, width), 1) + column * width
         hit = jnp.where(place == label_ref[...], LAM, 0.0)
-        loss = jnp.sum(prob * (log_target - log_draft) - hit * log_draft, -1, keepdims=True)
+        loss = -jnp.sum((prob + hit) * log_draft, -1, keepdims=True)
         grad = ((live + LAM) * jnp.exp(log_draft) - prob - hit).astype(BF16)
         act = inner_cols(grad, proj_ref[...])
         if carried is not None:
@@ -274,50 +340,38 @@
 
         @pl.when(step == pl.num_programs(0) - 1)
         def _():
-            size = jnp.max(jnp.max(sizes_ref[...], 0), (0, 1), keepdims=True)
-            most = jnp.maximum(size * (1.1 * count), 1e-30)
-            scale = jnp.exp2(jnp.floor(15.0 - jnp.log(most) * 1.4426950408889634))
-            scale_ref[...] = jnp.broadcast_to(scale, (8, 128))
             mine = lax.axis_index("grp") & 1
             away = totals[pl.ds(pl.multiple_of((1 - mine) * half_rank, half_rank), half_rank), :]
-            kept = totals[pl.ds(pl.multiple_of(mine * half_rank, half_rank), half_rank), :]
-            away_ref[...] = away * scale
-            kept_ref[...] = kept * scale
-
-    per = block // 8
+            away_ref[...] = away.astype(BF16)
+            kept_ref[...] = totals[pl.ds(pl.multiple_of(mine * half_rank, half_rank), half_rank), :]
+
     extra = () if carried is None else tuple(carried)
-    away, kept, scale, act, loss = pl.pallas_call(
+    away, kept, act, loss = pl.pallas_call(
         body,
         grid=(rows // block,),
         in_specs=[
             row_spec(block, width),
             row_spec(block, width, column),
-            pl.BlockSpec(
-                (8, width), lambda i: (jnp.minimum((i + 1) * per, rows // 8 - 1), column)
-            ),
-            pl.BlockSpec((8, width), lambda i: (0, column)),
             row_spec(block, 1),
             row_spec(block, rank),
             whole_spec(rank, width),
+            row_spec(block, 1),
+            row_spec(block, 1),
         ]
-        + [row_spec(block, 1)] * 4
-        + [pl.BlockSpec((bounds, 8, 128), lambda i: (0, 0, 0))]
         + ([row_spec(block, rank), row_spec(block, 1)] if extra else []),
-        out_specs=[whole_spec(half_rank, width)] * 2
-        + [whole_spec(8, 128), row_spec(block, rank), row_spec(block, 1)],
+        out_specs=[whole_spec(half_rank, width)] * 2 + [row_spec(block, rank), row_spec(block, 1)],
         out_shape=[
+            jax.ShapeDtypeStruct((half_rank, width), BF16),
             jax.ShapeDtypeStruct((half_rank, width), F32),
-            jax.ShapeDtypeStruct((half_rank, width), F32),
-            jax.ShapeDtypeStruct((8, 128), F32),
             jax.ShapeDtypeStruct((rows, rank), F32),
             jax.ShapeDtypeStruct((rows, 1), F32),
         ],
-        scratch_shapes=[pltpu.VMEM((rank, width), F32), pltpu.VMEM((block + 8, width), F32)],
-        compiler_params=params(24),
+        scratch_shapes=[pltpu.VMEM((rank, width), F32)],
+        compiler_params=params(54),
         cost_estimate=cost(4 * rows * rank * width, 8 * rows * width, rows * width),
         name="grad_chunk",
-    )(draft, target, target, incoming, label, acts, vocab_proj, *sums, sizes, *extra)
-    return (away, kept), scale[0, 0], (act, loss)
+    )(draft, prob, label, acts, vocab_proj, *sums, *extra)
+    return (away, kept), (act, loss)
 
 
 class Line:
@@ -361,7 +415,7 @@
     return line.after(arrived)
 
 
-def reduce_steps(line, pair, axis, bits, wires):
+def reduce_steps(line, pair, axis, bits, wires, alike):
     away, part = pair
     for index, (bit, wire) in enumerate(zip(bits[:-1], wires)):
         mine = own_bit(axis, bit)
@@ -371,7 +425,7 @@
         part = part + arrived.astype(F32)
     sent = part.astype(wires[-1])
     arrived = yield from sent_over(line, sent, axis, bits[-1])
-    return sent.astype(F32) + arrived.astype(F32)
+    return (sent.astype(F32) if alike else part) + arrived.astype(F32)
 
 
 def joined(axis, bit, own, other):
@@ -393,9 +447,9 @@
     return half(part, 1 - mine), half(part, mine)
 
 
-def summed(line, pair, axis, bits, wires, between, pieces):
+def summed(line, pair, axis, bits, wires, between, pieces, alike=False):
     def steps():
-        total = yield from reduce_steps(line, pair, axis, bits, wires)
+        total = yield from reduce_steps(line, pair, axis, bits, wires, alike)
         own = yield from gather_steps(line, between(total), axis, bits)
         pieces.append(own)
         other = yield from sent_over(line, own, axis, bits[0])
@@ -410,22 +464,36 @@
     return pieces[0]
 
 
-def scattered(line, part, wire):
-    count = lax.axis_size("voc")
-    blocks = part.astype(wire).reshape(count, part.shape[0] // count, part.shape[1])
-    blocks = line.put(line.after(blocks))
-    arrived = lax.all_to_all(blocks, "voc", 0, 0)
-    yield
-    return jnp.sum(line.after(arrived).astype(F32), 0)
-
-
-def over_voc(line, part, wire, between):
+def all_to_all(blocks, groups):
+    return lax.all_to_all(blocks, "voc", 0, 0, axis_index_groups=groups)
+
+
+def over_voc(line, part, wire, between, paired=False):
     def steps():
-        total = yield from scattered(line, part, wire)
-        rows = line.put(line.after(between(total)))
-        whole = lax.all_gather(rows, "voc", axis=0, tiled=True)
+        count = lax.axis_size("voc")
+        rows = part
+        groups = None
+        if paired:
+            count = count // 2
+            groups = [list(range(parity, 2 * count, 2)) for parity in range(2)]
+            mine = own_bit("voc", 0)
+            away, kept = half(part, 1 - mine), half(part, mine)
+            arrived = yield from sent_over(line, away.astype(wire), "voc", 0)
+            rows = kept + arrived.astype(F32)
+        blocks = rows.astype(wire).reshape(count, rows.shape[0] // count, rows.shape[1])
+        blocks = line.put(line.after(blocks))
+        arrived = all_to_all(blocks, groups)
         yield
-        return line.after(whole)
+        total = jnp.sum(line.after(arrived).astype(F32), 0)
+        own = line.put(line.after(between(total)))
+        copies = jnp.broadcast_to(own[None], (count, *own.shape))
+        arrived = all_to_all(copies, groups)
+        yield
+        whole = line.after(arrived).reshape(rows.shape)
+        if paired:
+            other = yield from sent_over(line, whole, "voc", 0)
+            return joined("voc", 0, whole, other)
+        return whole
 
     return Chain(steps())
 
@@ -442,68 +510,67 @@
     width = slice_cols // CHUNKS
     chunks = range(CHUNKS)
     z_bits = list(range(group_count.bit_length() - 1))
-    half_wires = [F16] * len(z_bits)
     line = Line()
 
     vocab_pieces = [[] for c in chunks]
     vocab = [
         summed(
-            line, pair, "grp", z_bits, half_wires,
+            line, pair, "grp", z_bits, [F16] * len(z_bits),
             lambda total: (total * (1.0 / VOCAB_SCALE)).astype(BF16), vocab_pieces[c],
         )
         for c, pair in enumerate(vocab_parts(up_weight, head_weight, width))
     ]
-    for c in chunks:
-        vocab[c].step()
+    vocab[0].step()
+    devices = range(group_count)
+    top_rows = line.put(line.after(target_logits[:8]))
+    incoming = lax.ppermute(top_rows, "grp", [(i + 1, i) for i in devices if i + 1 in devices])
+    vocab[1].step()
     pre_part = line.put(
         jnp.dot(line.after(hidden_states), down_weight, preferred_element_type=F32)
     )
     kept_pre = []
 
     def activate(total):
-        kept_pre.append(total)
-        return jax.nn.silu(total).astype(BF16)
-
-    pre = over_voc(line, pre_part, F32, activate)
-    devices = range(group_count)
-    top_rows = line.put(line.after(target_logits[:8]))
-    incoming = lax.ppermute(top_rows, "grp", [(i + 1, i) for i in devices if i + 1 in devices])
+        kept_pre.append(total * (1.0 / PRE_SCALE))
+        return jax.nn.silu(kept_pre[0]).astype(BF16)
+
+    pre = over_voc(line, pre_part * PRE_SCALE, F16, activate)
     vocab[0].step()
     pre.step()
-    target = tuple(target_sums(target_logits, line.after(incoming)))
-    line.put(target[0])
-    target = over_books(target, merge_sums, per_book)
+    vocab[1].step()
+    if per_book == 1:
+        prob, entropy = target_pass(target_logits, line.after(incoming))
+    else:
+        top, total = target_sums(target_logits, incoming)
+        top, total = over_books((top, total), merge_sums, per_book)
+        prob, entropy = target_probs(target_logits, incoming, top, total)
+    line.put(entropy)
     label = lax.dynamic_slice_in_dim(labels, book_index, 1, 1) - book_part * slice_cols
-    vocab[1].step()
     pre.step()
     vocab[0].step()
+    acts = line.put(pre.result())
     vocab[1].step()
-    acts = line.put(pre.result())
 
     drafts, vocab_proj, sums = [], [], None
     for c in chunks:
         vocab[c].result()
         pieces = vocab_pieces[c]
         line.put(pieces[1])
-        draft, proj, size, sums = draft_chunk(target_logits, acts, pieces, c, sums)
+        draft, proj, sums = draft_chunk(target_logits, acts, pieces, c, sums)
         drafts.append(line.put(draft))
         vocab_proj.append(proj)
-        if c == 0:
-            sizes = lax.all_gather(size, "grp", axis=0)
     sums = over_books(tuple(sums), merge_sums, per_book)
 
     grads, carried, grad_pieces = [], None, [[] for c in chunks]
     for c in chunks:
-        pair, scale, carried = grad_chunk(
-            line.after(drafts[c]), target_logits, incoming, label, acts, vocab_proj[c], c,
-            (*sums, *target), sizes, carried,
+        pair, carried = grad_chunk(
+            line.after(drafts[c]), prob, label, acts, vocab_proj[c], c, sums, carried
         )
         line.put(pair)
-        unscale = 1.0 / scale
         grads.append(
             summed(
-                line, pair, "grp", z_bits, half_wires,
-                lambda total, unscale=unscale: (total * unscale).astype(BF16), grad_pieces[c],
+                line, pair, "grp", z_bits, [BF16] * len(z_bits),
+                lambda total: total.astype(BF16), grad_pieces[c],
             )
         )
         grads[c].step()
@@ -512,9 +579,9 @@
         line, act_part, F32, lambda total: (total * silu_slope(kept_pre[0])).astype(BF16)
     )
     grads[0].step()
+    grads[1].step()
     act.step()
-    grads[1].step()
-    loss = over_books(loss, jnp.add, per_book)
+    loss = over_books(loss + entropy, jnp.add, per_book)
     frame_loss = lax.dynamic_slice_in_dim(loss, book_part * block_rows, block_rows, 0)
     frame_loss = frame_loss.reshape(1, 1, block_rows)
 
@@ -524,36 +591,37 @@
     def times_head(before, piece, c):
         return line.put(before + inner_cols(line.after(piece), columns(c)))
 
+    own_up = times_head(0.0, first_of(grads[0], grad_pieces[0]), 0)
     act.step()
-    grads[0].step()
-    own_up = times_head(0.0, first_of(grads[0], grad_pieces[0]), 0)
+    grads[0].result()
+    other_up = times_head(0.0, grad_pieces[0][1], 0)
     pre_grad = line.put(act.result())
     down_part = line.put(inner_rows(line.after(hidden_states), pre_grad))
-    grads[0].result()
-    other_up = times_head(0.0, grad_pieces[0][1], 0)
-    grads[1].step()
+    own = first_of(grads[1], grad_pieces[1])
     rows = down_part.shape[0] // 2
     down_pieces = [[], []]
     downs = [
         summed(
             line, split_pair(part, "grp", z_bits), "grp", z_bits, [BF16] * len(z_bits),
-            lambda total: total.astype(BF16), down_pieces[i],
+            lambda total: total.astype(BF16), down_pieces[i], True,
         )
         for i, part in enumerate((down_part[:rows], down_part[rows:]))
     ]
     downs[0].step()
     downs[1].step()
-    own_up = times_head(own_up, first_of(grads[1], grad_pieces[1]), 1)
+    own_up = times_head(own_up, own, 1)
     grads[1].result()
     other_up = times_head(other_up, grad_pieces[1][1], 1)
     up_part = joined("grp", 0, own_up, other_up)
-    ups = over_voc(line, up_part, BF16, lambda total: total.astype(BF16))
+    ups = over_voc(line, up_part, BF16, lambda total: total.astype(BF16), True)
     ups.step()
     downs[0].step()
     downs[1].step()
     ups.step()
+    ups.step()
     downs[0].step()
     downs[1].step()
+    ups.step()
     grad_b = ups.result().astype(F32)
     for chain in downs:
         chain.result()

time: 223 us -> 209 us (0.937)
  blocking collectives: 31.8 us -> 0 us
  Pallas kernels: 30.6 us -> 48.1 us
  between operations: 15.8 us -> 0.97 us
  starting transfers between devices: 35 us -> 48.2 us
  local copies, waits for them, and re-layouts: 15.9 us -> 6.31 us
  other arithmetic: 18.3 us -> 27.4 us
  matrix products: 10.7 us -> 18.1 us
  waiting for transfers between devices: 63.8 us -> 58.4 us
    all_gather x3 -> x0, blocking collectives: 31.8 us -> none  [the longest x2 18.7 us: steps(): whole = lax.all_gather(rows, 'voc', axis=0, tiled=True)]
    all_to_all x3 -> x6, starting transfers between devices: 12.7 us -> 24.1 us  [all_to_all(): return lax.all_to_all(blocks, 'voc', 0, 0, axis_index_groups=groups)]
    unnamed x37 -> x41, local copies, waits for them, and re-layouts: 12.4 us -> 2.08 us
    ppermute x1, waiting for transfers between devices: 7.71 us -> 0.59 us  [on_device(): lax.ppermute(top_rows, 'grp', [(i + 1, i) for i in devices if i + 1 in de...]
    dot_general x4, matrix products: 8.26 us -> 14.7 us  [inner_cols(): lax.dot_general(left, right, (((1,), (1,)), ((), ())), preferred_element_...]
    pallas_call x2, Pallas kernels: 7.59 us -> 12.8 us  [draft_chunk(): pl.pallas_call(body, grid=(rows // block,), in_specs=[row_spec(block, wid...]
    convert_element_type x2 -> x4, other arithmetic: 0.07 us -> 4.65 us  [on_device(): total.astype(BF16)]
    pallas_call x2, Pallas kernels: 12.2 us -> 16.8 us  [grad_chunk(): pl.pallas_call(body, grid=(rows // block,), in_specs=[row_spec(block, wid...]
  transfers between devices with their start and end apart: 23 -> 27, of which waited for: 15 -> 15; matrix products, arithmetic and copies ran while one was open for 11% -> 21% of each run, Pallas kernels for 7% -> 12%
where the time goes in v6:
time: 209 us; the launch traced here: 208 us
  waiting for transfers between devices  58.4 us (28%)
  starting transfers between devices  48.2 us (23%)
  Pallas kernels  48.1 us (23%)
  other arithmetic  27.4 us (13%)
  matrix products  18.1 us (9%)
  local copies, waits for them, and re-layouts  6.31 us (3%)
    ppermute x20, waiting for transfers between devices, swap(): return lax.ppermute(value, axis, pairs)  44.3 us
    all_to_all x6, starting transfers between devices, all_to_all(): return lax.all_to_all(blocks, 'voc', 0, 0, axis_index_groups=groups)  24.1 us
    ppermute x20, starting transfers between devices, swap(): return lax.ppermute(value, axis, pairs)  22.8 us
    pallas_call x2, Pallas kernels, grad_chunk(): pl.pallas_call(body, grid=(rows // block,), in_specs=[row_spec(block, wid...  16.8 us
    dot_general x4, matrix products, inner_cols(): lax.dot_general(left, right, (((1,), (1,)), ((), ())), preferred_element_...  14.7 us
    all_to_all x6, waiting for transfers between devices, all_to_all(): return lax.all_to_all(blocks, 'voc', 0, 0, axis_index_groups=groups)  13.6 us
    pallas_call x2, Pallas kernels, draft_chunk(): pl.pallas_call(body, grid=(rows // block,), in_specs=[row_spec(block, wid...  12.8 us
    pallas_call x1, Pallas kernels, vocab_parts(): pl.pallas_call(body, in_specs=[pl.BlockSpec(memory_space=pltpu.VMEM), pl....  9.45 us
  transfers between devices with their start and end apart: 27, of which 15 were waited for; matrix products, arithmetic and copies ran while one was open for 21% of the time, Pallas kernels for 12%

profile of v6, /device:TPU:0, one launch (start us, length us, event | category | flops | bytes accessed | tf_op | source)
XLA Modules:
  0.0 207.6 jit_solution(6173841660755299575)
XLA Ops:
  0.7 9.4 %vocab_parts.1 = (f32[128,1024]{1,0:T(8,128)}, f32[128,1024]{1,0:T(8,128)}, f32[128,1024]{1,0:T(8,128)}, f32[128,1024]{1,0:T(8,128)}) custom-call(bf16[256,2048]{1,0:T(8,128)(2,1)} %up_ref.1, bf16[2048,2048]{1,0:T(8,128)(2,1)} %head_ref.1), custom_call_target="tpu_custom_call" | custom-call | flops 524288 | bytes 2048 | tf_op jit(solution)/shard_map/vocab_parts/pallas_call | solution.py:230
  11.3 3.1 %collective-permute-start = (f16[128,1024]{1,0:T(8,128)(2,1)S(1)}, f16[128,1024]{1,0:T(8,128)(2,1)S(1)}, u32[]{:S(2)}, u32[]{:S(2)}) collective-permute-start(f16[128,1024]{1,0:T(8,128)(2,1)S(1)} %convert_element_type.119), channel_id=1, source_target_pairs={{0,8},{8,0},{16,24},{24,16},{1,9},{9,1},{17,25},{25,17},{2,10},{10... | collective-permute-start | bytes 786440 | tf_op jit(solution)/shard_map/ppermute | solution.py:23
  15.2 1.8 convert_element_type.118
  17.0 1.5 multiply_convert_fusion
  18.5 3.0 %collective-permute-done = f16[128,1024]{1,0:T(8,128)(2,1)S(1)} collective-permute-done((f16[128,1024]{1,0:T(8,128)(2,1)S(1)}, f16[128,1024]{1,0:T(8,128)(2,1)S(1)}, u32[]{:S(2)}, u32[]{:S(2)}) %collective-permute-start) | collective-permute-done | bytes 262176 | tf_op jit(solution)/shard_map/ppermute | solution.py:23
  22.3 4.2 %all-to-all-start = ((f16[8,128,256]{2,1,0:T(8,128)(2,1)}), f16[8,128,256]{2,1,0:T(8,128)(2,1)S(1)}, u32[]{:S(2)}, u32[]{:S(2)}) async-start(f16[8,128,256]{2,1,0:T(8,128)(2,1)} %bitcast.26), calls=%async_computation | async-start | bytes 1048576 | tf_op jit(solution)/shard_map/all_to_all | solution.py:468
  26.5 1.3 collective-permute-start.1
  27.8 3.7 %collective-permute-start.3 = (f16[128,1024]{1,0:T(8,128)(2,1)}, f16[128,1024]{1,0:T(8,128)(2,1)}, u32[]{:S(2)}, u32[]{:S(2)}) collective-permute-start(f16[128,1024]{1,0:T(8,128)(2,1)} %fusion.19), channel_id=1, source_target_pairs={{0,16},{8,24},{16,0},{24,8},{1,17},{9,25},{17,1},{25,9},{2,18},{10... | collective-permute-start | bytes 786440 | tf_op jit(solution)/shard_map/ppermute | solution.py:23
  32.9 9.1 %target_pass.1 = (f32[1024,2048]{1,0:T(8,128)}, f32[1024,1]{1,0:T(8,128)S(1)}) custom-call(f32[1024,2048]{1,0:T(8,128)} %target_ref.5, f32[1024,2048]{1,0:T(8,128)} %target_ref.5, f32[8,2048]{1,0:T(8,128)S(1)} %collective-permute-done.1.incoming_ref), custom_call_target="tpu_custom_call" | custom-call | flops 3072 | bytes 4096 | tf_op jit(solution)/shard_map/target_pass/pallas_call | solution.py:133
  43.0 4.0 %all-to-all-start.1 = ((bf16[8,128,256]{2,1,0:T(8,128)(2,1)}), bf16[8,128,256]{2,1,0:T(8,128)(2,1)S(1)}, u32[]{:S(2)}, u32[]{:S(2)}) async-start(bf16[8,128,256]{2,1,0:T(8,128)(2,1)} %broadcast_in_dim.6), calls=%async_computation.1 | async-start | bytes 1048576 | tf_op jit(solution)/shard_map/all_to_all | solution.py:468
  46.9 3.3 %collective-permute-start.4 = (f16[128,1024]{1,0:T(8,128)(2,1)}, f16[128,1024]{1,0:T(8,128)(2,1)}, u32[]{:S(2)}, u32[]{:S(2)}) collective-permute-start(f16[128,1024]{1,0:T(8,128)(2,1)} %fusion.20), channel_id=1, source_target_pairs={{0,16},{8,24},{16,0},{24,8},{1,17},{9,25},{17,1},{25,9},{2,18},{10... | collective-permute-start | bytes 786440 | tf_op jit(solution)/shard_map/ppermute | solution.py:23
  50.2 1.3 multiply_convert_fusion.2.own_ref
  51.6 5.1 %all-to-all-done.1 = bf16[8,128,256]{2,1,0:T(8,128)(2,1)S(1)} async-done(((bf16[8,128,256]{2,1,0:T(8,128)(2,1)}), bf16[8,128,256]{2,1,0:T(8,128)(2,1)S(1)}, u32[]{:S(2)}, u32[]{:S(2)}) %all-to-all-start.1) | async-done | bytes 524320 | tf_op jit(solution)/shard_map/all_to_all | solution.py:468
  56.7 6.5 %collective-permute-done.4 = f16[128,1024]{1,0:T(8,128)(2,1)} collective-permute-done((f16[128,1024]{1,0:T(8,128)(2,1)}, f16[128,1024]{1,0:T(8,128)(2,1)}, u32[]{:S(2)}, u32[]{:S(2)}) %collective-permute-start.4) | collective-permute-done | bytes 262176 | tf_op jit(solution)/shard_map/ppermute | solution.py:23
  63.2 2.0 multiply_convert_fusion.1.own_ref
  67.0 6.2 %draft_chunk.2 = (f32[1024,1024]{1,0:T(8,128)}, bf16[256,1024]{1,0:T(8,128)(2,1)}, f32[1024,1]{1,0:T(8,128)}, f32[1024,1]{1,0:T(8,128)}) custom-call(f32[1024,2048]{1,0:T(8,128)} %target_ref.5, bf16[1024,256]{1,0:T(8,128)(2,1)} %bitcast.19, bf16[128,1024]{1,0:T(8,128)(2,1)} %copy-done.13, bf16[128,1024]{1,0:T(8,128)(2,1)} %collective-permute-done.6.other_ref), custom_call_target="tpu_custom_call" | custom-call | flops 131072 | bytes 2048 | tf_op jit(solution)/shard_map/draft_chunk/pallas_call | solution.py:277
  73.6 6.7 %draft_chunk.3 = (f32[1024,1024]{1,0:T(8,128)}, bf16[256,1024]{1,0:T(8,128)(2,1)}, f32[1024,1]{1,0:T(8,128)}, f32[1024,1]{1,0:T(8,128)}) custom-call(f32[1024,2048]{1,0:T(8,128)} %target_ref.5, bf16[1024,256]{1,0:T(8,128)(2,1)} %bitcast.20, bf16[128,1024]{1,0:T(8,128)(2,1)} %multiply_convert_fusion.1.own_ref, ...), custom_call_target="tpu_custom_call" | custom-call | flops 131072 | bytes 2048 | tf_op jit(solution)/shard_map/draft_chunk/pallas_call | solution.py:277
  80.3 8.1 %grad_chunk.2 = (bf16[128,1024]{1,0:T(8,128)(2,1)}, f32[128,1024]{1,0:T(8,128)}, f32[1024,256]{1,0:T(8,128)}, f32[1024,1]{1,0:T(8,128)}) custom-call(f32[1024,1024]{1,0:T(8,128)} %get-tuple-element.111.draft_ref, f32[1024,2048]{1,0:T(8,128)} %get-tuple-element.112.prob_ref, s32[1024,1]{1,0:T(8,128)} %copy.11.label_ref, bf16[1024,256]{1,0:T(8,128)(2,1)} %bitcast.21, ...), custom_call_target="tpu_custom_call" | custom-call | flops 262144 | bytes 2048 | tf_op jit(solution)/shard_map/grad_chunk/pallas_call | solution.py:349
  88.3 1.7 collective-permute-start.8
  90.0 8.7 %grad_chunk.3 = (bf16[128,1024]{1,0:T(8,128)(2,1)}, f32[128,1024]{1,0:T(8,128)}, f32[1024,256]{1,0:T(8,128)}, f32[1024,1]{1,0:T(8,128)}) custom-call(f32[1024,1024]{1,0:T(8,128)} %get-tuple-element.117.draft_ref, f32[1024,2048]{1,0:T(8,128)} %get-tuple-element.112.prob_ref, s32[1024,1]{1,0:T(8,128)} %copy.11.label_ref, bf16[1024,256]{1,0:T(8,128)(2,1)} %bitcast.22, ...), custom_call_target="tpu_custom_call" | custom-call | flops 262144 | bytes 2048 | tf_op jit(solution)/shard_map/grad_chunk/pallas_call | solution.py:349
  100.0 6.5 %collective-permute-done.7 = bf16[128,1024]{1,0:T(8,128)(2,1)S(1)} collective-permute-done((bf16[128,1024]{1,0:T(8,128)(2,1)}, bf16[128,1024]{1,0:T(8,128)(2,1)S(1)}, u32[]{:S(2)}, u32[]{:S(2)}) %collective-permute-start.7) | collective-permute-done | bytes 262176 | tf_op jit(solution)/shard_map/ppermute | solution.py:23
  106.5 1.8 fusion.22
  108.3 4.3 %all-to-all-start.2 = ((f32[8,128,256]{2,1,0:T(8,128)}), f32[8,128,256]{2,1,0:T(8,128)}, u32[]{:S(2)}, u32[]{:S(2)}) async-start(f32[8,128,256]{2,1,0:T(8,128)} %bitcast.25), calls=%async_computation.2 | async-start | bytes 2097152 | tf_op jit(solution)/shard_map/all_to_all | solution.py:468
  113.4 14.2 %collective-permute-done.9 = bf16[128,1024]{1,0:T(8,128)(2,1)S(1)} collective-permute-done((bf16[128,1024]{1,0:T(8,128)(2,1)}, bf16[128,1024]{1,0:T(8,128)(2,1)S(1)}, u32[]{:S(2)}, u32[]{:S(2)}) %collective-permute-start.9) | collective-permute-done | bytes 262176 | tf_op jit(solution)/shard_map/ppermute | solution.py:23
  127.6 1.7 add_convert_fusion.1
  129.4 4.7 %fusion.6 = f32[128,2048]{1,0:T(8,128)} fusion(bf16[128,1024]{1,0:T(8,128)(2,1)} %add_convert_fusion.1, bf16[2048,2048]{1,0:T(8,128)(2,1)} %head_ref.1), kind=kOutput, calls=%fused_computation.6 | convolution fusion | flops 536870912 | bytes 5505024 | tf_op jit(solution)/shard_map/dot_general | solution.py:45
  134.1 1.3 reduce_sum.31
  136.3 4.3 %all-to-all-start.3 = ((bf16[8,128,256]{2,1,0:T(8,128)(2,1)}), bf16[8,128,256]{2,1,0:T(8,128)(2,1)}, u32[]{:S(2)}, u32[]{:S(2)}) async-start(bf16[8,128,256]{2,1,0:T(8,128)(2,1)} %broadcast_in_dim.7), calls=%async_computation.3 | async-start | bytes 1048576 | tf_op jit(solution)/shard_map/all_to_all | solution.py:468
  140.7 2.6 %collective-permute-start.11 = (bf16[128,1024]{1,0:T(8,128)(2,1)}, bf16[128,1024]{1,0:T(8,128)(2,1)}, u32[]{:S(2)}, u32[]{:S(2)}) collective-permute-start(bf16[128,1024]{1,0:T(8,128)(2,1)} %fusion.22), channel_id=1, source_target_pairs={{0,16},{8,24},{16,0},{24,8},{1,17},{9,25},{17,1},{25,9},{2,18},{10... | collective-permute-start | bytes 786440 | tf_op jit(solution)/shard_map/ppermute | solution.py:23
  143.2 4.7 %fusion.4 = f32[128,2048]{1,0:T(8,128)} fusion(bf16[128,1024]{1,0:T(8,128)(2,1)S(1)} %collective-permute-done.10, bf16[2048,2048]{1,0:T(8,128)(2,1)} %head_ref.1), kind=kOutput, calls=%fused_computation.4 | convolution fusion | flops 536870912 | bytes 5505024 | tf_op jit(solution)/shard_map/dot_general | solution.py:45
  147.9 2.3 %all-to-all-done.3 = bf16[8,128,256]{2,1,0:T(8,128)(2,1)} async-done(((bf16[8,128,256]{2,1,0:T(8,128)(2,1)}), bf16[8,128,256]{2,1,0:T(8,128)(2,1)}, u32[]{:S(2)}, u32[]{:S(2)}) %all-to-all-start.3) | async-done | bytes 524320 | tf_op jit(solution)/shard_map/all_to_all | solution.py:468
  150.2 1.9 fusion.24
  152.3 3.6 %collective-permute-done.11 = bf16[128,1024]{1,0:T(8,128)(2,1)} collective-permute-done((bf16[128,1024]{1,0:T(8,128)(2,1)}, bf16[128,1024]{1,0:T(8,128)(2,1)}, u32[]{:S(2)}, u32[]{:S(2)}) %collective-permute-start.11) | collective-permute-done | bytes 262176 | tf_op jit(solution)/shard_map/ppermute | solution.py:23
  157.1 2.1 collective-permute-start.12
  159.2 3.7 %fusion.8 = f32[128,2048]{1,0:T(8,128)S(1)} fusion(f32[128,2048]{1,0:T(8,128)S(1)} %copy-done.11, bf16[128,1024]{1,0:T(8,128)(2,1)S(1)} %add_convert_fusion, bf16[2048,2048]{1,0:T(8,128)(2,1)} %head_ref.1), kind=kOutput, calls=%fused_computation.12 | convolution fusion | flops 537133056 | bytes 6553600 | tf_op jit(solution)/shard_map/dot_general | solution.py:45
  162.9 3.1 %collective-permute-done.13 = bf16[128,1024]{1,0:T(8,128)(2,1)S(1)} collective-permute-done((bf16[128,1024]{1,0:T(8,128)(2,1)S(1)}, bf16[128,1024]{1,0:T(8,128)(2,1)S(1)}, u32[]{:S(2)}, u32[]{:S(2)}) %collective-permute-start.13) | collective-permute-done | bytes 262176 | tf_op jit(solution)/shard_map/ppermute | solution.py:23
  166.0 1.5 broadcast_select_fusion.2
  170.7 4.6 %collective-permute-done.16 = bf16[256,256]{1,0:T(8,128)(2,1)S(1)} collective-permute-done((bf16[256,256]{1,0:T(8,128)(2,1)S(1)}, bf16[256,256]{1,0:T(8,128)(2,1)S(1)}, u32[]{:S(2)}, u32[]{:S(2)}) %collective-permute-start.16) | collective-permute-done | bytes 131104 | tf_op jit(solution)/shard_map/ppermute | solution.py:23
  175.4 2.4 %fusion.16 = bf16[128,2048]{1,0:T(8,128)(2,1)} fusion(s32[]{:T(128)S(6)} %select_n.77, f32[128,2048]{1,0:T(8,128)} %copy-done.3, f32[128,2048]{1,0:T(8,128)} %copy-done.2, bf16[128,2048]{1,0:T(8,128)(2,1)} %collective-permute-done.15), kind=kLoop, calls=%fused_computation.16 | loop fusion | flops 1048576 | bytes 3145732 | tf_op jit(solution)/shard_map/convert_element_type | solution.py:483
  177.9 3.9 %all-to-all-start.4 = ((bf16[4,32,2048]{2,1,0:T(8,128)(2,1)}), bf16[4,32,2048]{2,1,0:T(8,128)(2,1)S(1)}, u32[]{:S(2)}, u32[]{:S(2)}) async-start(bf16[4,32,2048]{2,1,0:T(8,128)(2,1)} %bitcast.24), calls=%async_computation.4 | async-start | bytes 1048576 | tf_op jit(solution)/shard_map/all_to_all | solution.py:468
  182.5 2.2 %collective-permute-start.18 = (bf16[256,256]{1,0:T(8,128)(2,1)S(1)}, bf16[256,256]{1,0:T(8,128)(2,1)}, u32[]{:S(2)}, u32[]{:S(2)}) collective-permute-start(bf16[256,256]{1,0:T(8,128)(2,1)S(1)} %add_convert_fusion.4), channel_id=1, source_target_pairs={{0,16},{8,24},{16,0},{24,8},{1,17},{9,25},{17,1},{25,9},{2,18},{10... | collective-permute-start | bytes 393224 | tf_op jit(solution)/shard_map/ppermute | solution.py:23
  184.7 5.0 %all-to-all-done.4 = bf16[4,32,2048]{2,1,0:T(8,128)(2,1)S(1)} async-done(((bf16[4,32,2048]{2,1,0:T(8,128)(2,1)}), bf16[4,32,2048]{2,1,0:T(8,128)(2,1)S(1)}, u32[]{:S(2)}, u32[]{:S(2)}) %all-to-all-start.4) | async-done | bytes 524320 | tf_op jit(solution)/shard_map/all_to_all | solution.py:468
  190.6 3.5 %all-to-all-start.5 = ((bf16[4,32,2048]{2,1,0:T(8,128)(2,1)}), bf16[4,32,2048]{2,1,0:T(8,128)(2,1)S(1)}, u32[]{:S(2)}, u32[]{:S(2)}) async-start(bf16[4,32,2048]{2,1,0:T(8,128)(2,1)} %broadcast_in_dim.8), calls=%async_computation.5 | async-start | bytes 1048576 | tf_op jit(solution)/shard_map/all_to_all | solution.py:468
  196.7 1.4 collective-permute-start.19
  198.1 1.8 add_reduce_fusion
  200.0 1.1 all-to-all-done.5
  201.1 1.9 collective-permute-done.19
  206.0 1.6 maximum_convert_fusion
  (94 shorter events, 22.3 us)
Async XLA Ops:
  0.6 16.4 %copy-start = (bf16[1024,1024]{1,0:T(8,128)(2,1)S(1)}, bf16[1024,1024]{1,0:T(8,128)(2,1)}, u32[]{:S(2)}) copy-start(bf16[1024,1024]{1,0:T(8,128)(2,1)} %param.6) | copy-start | bytes 6291460
  0.6 16.4 %copy-start.17 = (bf16[1024,256]{1,0:T(8,128)(2,1)S(1)}, bf16[1024,256]{1,0:T(8,128)(2,1)}, u32[]{:S(2)}) copy-start(bf16[1024,256]{1,0:T(8,128)(2,1)} %param.9) | copy-start | bytes 1572868
  10.1 11.4 %copy-start.6 = (f32[128,1024]{1,0:T(8,128)S(1)}, f32[128,1024]{1,0:T(8,128)}, u32[]{:S(2)}) copy-start(f32[128,1024]{1,0:T(8,128)} %get-tuple-element.89) | copy-start | bytes 1572868
  11.3 10.2 %collective-permute-start = (f16[128,1024]{1,0:T(8,128)(2,1)S(1)}, f16[128,1024]{1,0:T(8,128)(2,1)S(1)}, u32[]{:S(2)}, u32[]{:S(2)}) collective-permute-start(f16[128,1024]{1,0:T(8,128)(2,1)S(1)} %convert_element_type.119), channel_id=1, source_target_pairs={{0,8},{8,0},{16,24},{24,16},{1,9},{9,1},{17,25},{25,17},{2,10},{10... | collective-permute-start | bytes 786440 | tf_op jit(solution)/shard_map/ppermute | solution.py:23
  17.0 14.6 %copy-start.5 = (f32[128,1024]{1,0:T(8,128)S(1)}, f32[128,1024]{1,0:T(8,128)}, u32[]{:S(2)}) copy-start(f32[128,1024]{1,0:T(8,128)} %get-tuple-element.93) | copy-start | bytes 1572868
  17.0 14.6 %collective-permute-start.2 = (f16[128,1024]{1,0:T(8,128)(2,1)}, f16[128,1024]{1,0:T(8,128)(2,1)S(1)}, u32[]{:S(2)}, u32[]{:S(2)}) collective-permute-start(f16[128,1024]{1,0:T(8,128)(2,1)} %convert_element_type.118), channel_id=1, source_target_pairs={{0,8},{8,0},{16,24},{24,16},{1,9},{9,1},{17,25},{25,17},{2,10},{10... | collective-permute-start | bytes 786440 | tf_op jit(solution)/shard_map/ppermute | solution.py:23
  21.5 0.8 copy-start.15
  22.3 19.7 %all-to-all-start = ((f16[8,128,256]{2,1,0:T(8,128)(2,1)}), f16[8,128,256]{2,1,0:T(8,128)(2,1)S(1)}, u32[]{:S(2)}, u32[]{:S(2)}) async-start(f16[8,128,256]{2,1,0:T(8,128)(2,1)} %bitcast.26), calls=%async_computation | async-start | bytes 1048576 | tf_op jit(solution)/shard_map/all_to_all | solution.py:468
  26.5 6.4 %collective-permute-start.1 = (f32[8,2048]{1,0:T(8,128)S(1)}, f32[8,2048]{1,0:T(8,128)S(1)}, u32[]{:S(2)}, u32[]{:S(2)}) collective-permute-start(f32[8,2048]{1,0:T(8,128)S(1)} %slice.17), channel_id=1, source_target_pairs={{8,0},{16,8},{24,16},{9,1},{17,9},{25,17},{10,2},{18,10},{26,18},{... | collective-permute-start | bytes 196616 | tf_op jit(solution)/shard_map/ppermute | solution.py:526
  27.8 22.4 %collective-permute-start.3 = (f16[128,1024]{1,0:T(8,128)(2,1)}, f16[128,1024]{1,0:T(8,128)(2,1)}, u32[]{:S(2)}, u32[]{:S(2)}) collective-permute-start(f16[128,1024]{1,0:T(8,128)(2,1)} %fusion.19), channel_id=1, source_target_pairs={{0,16},{8,24},{16,0},{24,8},{1,17},{9,25},{17,1},{25,9},{2,18},{10... | collective-permute-start | bytes 786440 | tf_op jit(solution)/shard_map/ppermute | solution.py:23
  31.5 10.5 %copy-start.14 = (f16[128,1024]{1,0:T(8,128)(2,1)}, f16[128,1024]{1,0:T(8,128)(2,1)S(1)}, u32[]{:S(2)}) copy-start(f16[128,1024]{1,0:T(8,128)(2,1)S(1)} %collective-permute-done.2) | copy-start | bytes 786436
  43.0 13.7 %all-to-all-start.1 = ((bf16[8,128,256]{2,1,0:T(8,128)(2,1)}), bf16[8,128,256]{2,1,0:T(8,128)(2,1)S(1)}, u32[]{:S(2)}, u32[]{:S(2)}) async-start(bf16[8,128,256]{2,1,0:T(8,128)(2,1)} %broadcast_in_dim.6), calls=%async_computation.1 | async-start | bytes 1048576 | tf_op jit(solution)/shard_map/all_to_all | solution.py:468
  46.9 16.3 %collective-permute-start.4 = (f16[128,1024]{1,0:T(8,128)(2,1)}, f16[128,1024]{1,0:T(8,128)(2,1)}, u32[]{:S(2)}, u32[]{:S(2)}) collective-permute-start(f16[128,1024]{1,0:T(8,128)(2,1)} %fusion.20), channel_id=1, source_target_pairs={{0,16},{8,24},{16,0},{24,8},{1,17},{9,25},{17,1},{25,9},{2,18},{10... | collective-permute-start | bytes 786440 | tf_op jit(solution)/shard_map/ppermute | solution.py:23
  51.5 15.5 %copy-start.13 = (bf16[128,1024]{1,0:T(8,128)(2,1)}, bf16[128,1024]{1,0:T(8,128)(2,1)S(1)}, u32[]{:S(2)}) copy-start(bf16[128,1024]{1,0:T(8,128)(2,1)S(1)} %multiply_convert_fusion.2.own_ref) | copy-start | bytes 786436
  51.5 15.5 %collective-permute-start.6 = (bf16[128,1024]{1,0:T(8,128)(2,1)S(1)}, bf16[128,1024]{1,0:T(8,128)(2,1)}, u32[]{:S(2)}, u32[]{:S(2)}) collective-permute-start(bf16[128,1024]{1,0:T(8,128)(2,1)S(1)} %multiply_convert_fusion.2.own_ref), channel_id=1, source_target_pairs={{0,8},{8,0},{16,24},{24,16},{1,9},{9,1},{17,25},{25,17},{2,10},{10... | collective-permute-start | bytes 786440 | tf_op jit(solution)/shard_map/ppermute | solution.py:23
  56.7 10.3 %copy-start.1 = (bf16[8,128,256]{2,1,0:T(8,128)(2,1)}, bf16[8,128,256]{2,1,0:T(8,128)(2,1)S(1)}, u32[]{:S(2)}) copy-start(bf16[8,128,256]{2,1,0:T(8,128)(2,1)S(1)} %all-to-all-done.1) | copy-start | bytes 1572868
  65.2 8.4 %collective-permute-start.5 = (bf16[128,1024]{1,0:T(8,128)(2,1)}, bf16[128,1024]{1,0:T(8,128)(2,1)}, u32[]{:S(2)}, u32[]{:S(2)}) collective-permute-start(bf16[128,1024]{1,0:T(8,128)(2,1)} %multiply_convert_fusion.1.own_ref), channel_id=1, source_target_pairs={{0,8},{8,0},{16,24},{24,16},{1,9},{9,1},{17,25},{25,17},{2,10},{10... | collective-permute-start | bytes 786440 | tf_op jit(solution)/shard_map/ppermute | solution.py:23
  88.3 10.9 %collective-permute-start.8 = (bf16[128,1024]{1,0:T(8,128)(2,1)}, bf16[128,1024]{1,0:T(8,128)(2,1)S(1)}, u32[]{:S(2)}, u32[]{:S(2)}) collective-permute-start(bf16[128,1024]{1,0:T(8,128)(2,1)} %get-tuple-element.116), channel_id=1, source_target_pairs={{0,8},{8,0},{16,24},{24,16},{1,9},{9,1},{17,25},{25,17},{2,10},{10... | collective-permute-start | bytes 786440 | tf_op jit(solution)/shard_map/ppermute | solution.py:23
  90.0 9.2 %copy-start.7 = (f32[128,1024]{1,0:T(8,128)S(1)}, f32[128,1024]{1,0:T(8,128)}, u32[]{:S(2)}) copy-start(f32[128,1024]{1,0:T(8,128)} %get-tuple-element.125) | copy-start | bytes 1572868
  98.7 7.8 %collective-permute-start.7 = (bf16[128,1024]{1,0:T(8,128)(2,1)}, bf16[128,1024]{1,0:T(8,128)(2,1)S(1)}, u32[]{:S(2)}, u32[]{:S(2)}) collective-permute-start(bf16[128,1024]{1,0:T(8,128)(2,1)} %get-tuple-element.124), channel_id=1, source_target_pairs={{0,8},{8,0},{16,24},{24,16},{1,9},{9,1},{17,25},{25,17},{2,10},{10... | collective-permute-start | bytes 786440 | tf_op jit(solution)/shard_map/ppermute | solution.py:23
  99.2 7.3 %copy-start.16 = (bf16[128,1024]{1,0:T(8,128)(2,1)}, bf16[128,1024]{1,0:T(8,128)(2,1)S(1)}, u32[]{:S(2)}) copy-start(bf16[128,1024]{1,0:T(8,128)(2,1)S(1)} %collective-permute-done.8) | copy-start | bytes 786436
  108.3 25.8 %all-to-all-start.2 = ((f32[8,128,256]{2,1,0:T(8,128)}), f32[8,128,256]{2,1,0:T(8,128)}, u32[]{:S(2)}, u32[]{:S(2)}) async-start(f32[8,128,256]{2,1,0:T(8,128)} %bitcast.25), calls=%async_computation.2 | async-start | bytes 2097152 | tf_op jit(solution)/shard_map/all_to_all | solution.py:468
  112.6 15.1 %collective-permute-start.9 = (bf16[128,1024]{1,0:T(8,128)(2,1)}, bf16[128,1024]{1,0:T(8,128)(2,1)S(1)}, u32[]{:S(2)}, u32[]{:S(2)}) collective-permute-start(bf16[128,1024]{1,0:T(8,128)(2,1)} %fusion.21), channel_id=1, source_target_pairs={{0,16},{8,24},{16,0},{24,8},{1,17},{9,25},{17,1},{25,9},{2,18},{10... | collective-permute-start | bytes 786440 | tf_op jit(solution)/shard_map/ppermute | solution.py:23
  129.4 13.9 %collective-permute-start.10 = (bf16[128,1024]{1,0:T(8,128)(2,1)}, bf16[128,1024]{1,0:T(8,128)(2,1)S(1)}, u32[]{:S(2)}, u32[]{:S(2)}) collective-permute-start(bf16[128,1024]{1,0:T(8,128)(2,1)} %add_convert_fusion.1), channel_id=1, source_target_pairs={{0,8},{8,0},{16,24},{24,16},{1,9},{9,1},{17,25},{25,17},{2,10},{10... | collective-permute-start | bytes 786440 | tf_op jit(solution)/shard_map/ppermute | solution.py:23
  136.3 13.9 %all-to-all-start.3 = ((bf16[8,128,256]{2,1,0:T(8,128)(2,1)}), bf16[8,128,256]{2,1,0:T(8,128)(2,1)}, u32[]{:S(2)}, u32[]{:S(2)}) async-start(bf16[8,128,256]{2,1,0:T(8,128)(2,1)} %broadcast_in_dim.7), calls=%async_computation.3 | async-start | bytes 1048576 | tf_op jit(solution)/shard_map/all_to_all | solution.py:468
  140.7 15.2 %collective-permute-start.11 = (bf16[128,1024]{1,0:T(8,128)(2,1)}, bf16[128,1024]{1,0:T(8,128)(2,1)}, u32[]{:S(2)}, u32[]{:S(2)}) collective-permute-start(bf16[128,1024]{1,0:T(8,128)(2,1)} %fusion.22), channel_id=1, source_target_pairs={{0,16},{8,24},{16,0},{24,8},{1,17},{9,25},{17,1},{25,9},{2,18},{10... | collective-permute-start | bytes 786440 | tf_op jit(solution)/shard_map/ppermute | solution.py:23
  147.9 8.0 %copy-start.4 = (f32[128,1024]{1,0:T(8,128)S(1)}, f32[128,1024]{1,0:T(8,128)}, u32[]{:S(2)}) copy-start(f32[128,1024]{1,0:T(8,128)} %get-tuple-element.123) | copy-start | bytes 1572868
  150.2 8.9 %copy-start.11 = (f32[128,2048]{1,0:T(8,128)S(1)}, f32[128,2048]{1,0:T(8,128)}, u32[]{:S(2)}) copy-start(f32[128,2048]{1,0:T(8,128)} %fusion.6) | copy-start | bytes 3145732
  150.2 15.7 %slice-start = ((s8[8388608]{0:T(1024)(128)(4,1)}), s8[4194304]{0:T(1024)(128)(4,1)S(1)}, s32[]{:S(2)}) async-start(s8[8388608]{0:T(1024)(128)(4,1)} %bitcast.17), calls=%async_computation.6 | async-start | bytes 8388608
  152.3 6.9 %copy-start.8 = (f32[512,256]{1,0:T(8,128)}, f32[512,256]{1,0:T(8,128)S(1)}, u32[]{:S(2)}) copy-start(f32[512,256]{1,0:T(8,128)S(1)} %get-tuple-element.170) | copy-start | bytes 1572868
  152.3 6.9 %copy-start.10 = (f32[512,256]{1,0:T(8,128)}, f32[512,256]{1,0:T(8,128)S(1)}, u32[]{:S(2)}) copy-start(f32[512,256]{1,0:T(8,128)S(1)} %get-tuple-element.169) | copy-start | bytes 1572868
  152.3 13.7 %slice-start.1 = ((s8[8388608]{0:T(1024)(128)(4,1)}), s8[4194304]{0:T(1024)(128)(4,1)S(1)}, s32[]{:S(2)}) async-start(s8[8388608]{0:T(1024)(128)(4,1)} %bitcast.17), calls=%async_computation.7 | async-start | bytes 8388608
  152.3 13.7 %copy-start.12 = (f32[128,2048]{1,0:T(8,128)S(1)}, f32[128,2048]{1,0:T(8,128)}, u32[]{:S(2)}) copy-start(f32[128,2048]{1,0:T(8,128)} %fusion.4) | copy-start | bytes 3145732
  157.0 9.0 %collective-permute-start.13 = (bf16[128,1024]{1,0:T(8,128)(2,1)S(1)}, bf16[128,1024]{1,0:T(8,128)(2,1)S(1)}, u32[]{:S(2)}, u32[]{:S(2)}) collective-permute-start(bf16[128,1024]{1,0:T(8,128)(2,1)S(1)} %add_convert_fusion), channel_id=1, source_target_pairs={{0,8},{8,0},{16,24},{24,16},{1,9},{9,1},{17,25},{25,17},{2,10},{10... | collective-permute-start | bytes 786440 | tf_op jit(solution)/shard_map/ppermute | solution.py:23
  157.1 12.7 %collective-permute-start.12 = (bf16[256,256]{1,0:T(8,128)(2,1)S(1)}, bf16[256,256]{1,0:T(8,128)(2,1)S(1)}, u32[]{:S(2)}, u32[]{:S(2)}) collective-permute-start(bf16[256,256]{1,0:T(8,128)(2,1)S(1)} %get-tuple-element.142), channel_id=1, source_target_pairs={{0,8},{8,0},{16,24},{24,16},{1,9},{9,1},{17,25},{25,17},{2,10},{10... | collective-permute-start | bytes 393224 | tf_op jit(solution)/shard_map/ppermute | solution.py:23
  162.9 12.5 %copy-start.9 = (f32[512,256]{1,0:T(8,128)S(1)}, f32[512,256]{1,0:T(8,128)}, u32[]{:S(2)}) copy-start(f32[512,256]{1,0:T(8,128)} %copy-done.8) | copy-start | bytes 1572868
  167.5 1.0 copy-start.2
  167.5 2.0 copy-start.3
  169.5 6.0 %collective-permute-start.15 = (bf16[128,2048]{1,0:T(8,128)(2,1)}, bf16[128,2048]{1,0:T(8,128)(2,1)}, u32[]{:S(2)}, u32[]{:S(2)}) collective-permute-start(bf16[128,2048]{1,0:T(8,128)(2,1)} %fusion.18), channel_id=1, source_target_pairs={{0,1},{1,0},{2,3},{3,2},{4,5},{5,4},{6,7},{7,6},{8,9},{9,8},{10,11... | collective-permute-start | bytes 1572872 | tf_op jit(solution)/shard_map/ppermute | solution.py:23
  169.5 5.9 %collective-permute-start.16 = (bf16[256,256]{1,0:T(8,128)(2,1)S(1)}, bf16[256,256]{1,0:T(8,128)(2,1)S(1)}, u32[]{:S(2)}, u32[]{:S(2)}) collective-permute-start(bf16[256,256]{1,0:T(8,128)(2,1)S(1)} %get-tuple-element.143), channel_id=1, source_target_pairs={{0,8},{8,0},{16,24},{24,16},{1,9},{9,1},{17,25},{25,17},{2,10},{10... | collective-permute-start | bytes 393224 | tf_op jit(solution)/shard_map/ppermute | solution.py:23
  177.9 11.8 %all-to-all-start.4 = ((bf16[4,32,2048]{2,1,0:T(8,128)(2,1)}), bf16[4,32,2048]{2,1,0:T(8,128)(2,1)S(1)}, u32[]{:S(2)}, u32[]{:S(2)}) async-start(bf16[4,32,2048]{2,1,0:T(8,128)(2,1)} %bitcast.24), calls=%async_computation.4 | async-start | bytes 1048576 | tf_op jit(solution)/shard_map/all_to_all | solution.py:468
  181.8 12.3 %collective-permute-start.14 = (bf16[256,256]{1,0:T(8,128)(2,1)S(1)}, bf16[256,256]{1,0:T(8,128)(2,1)}, u32[]{:S(2)}, u32[]{:S(2)}) collective-permute-start(bf16[256,256]{1,0:T(8,128)(2,1)S(1)} %add_convert_fusion.5), channel_id=1, source_target_pairs={{0,16},{8,24},{16,0},{24,8},{1,17},{9,25},{17,1},{25,9},{2,18},{10... | collective-permute-start | bytes 393224 | tf_op jit(solution)/shard_map/ppermute | solution.py:23
  182.5 13.3 %collective-permute-start.18 = (bf16[256,256]{1,0:T(8,128)(2,1)S(1)}, bf16[256,256]{1,0:T(8,128)(2,1)}, u32[]{:S(2)}, u32[]{:S(2)}) collective-permute-start(bf16[256,256]{1,0:T(8,128)(2,1)S(1)} %add_convert_fusion.4), channel_id=1, source_target_pairs={{0,16},{8,24},{16,0},{24,8},{1,17},{9,25},{17,1},{25,9},{2,18},{10... | collective-permute-start | bytes 393224 | tf_op jit(solution)/shard_map/ppermute | solution.py:23
  190.6 10.5 %all-to-all-start.5 = ((bf16[4,32,2048]{2,1,0:T(8,128)(2,1)}), bf16[4,32,2048]{2,1,0:T(8,128)(2,1)S(1)}, u32[]{:S(2)}, u32[]{:S(2)}) async-start(bf16[4,32,2048]{2,1,0:T(8,128)(2,1)} %broadcast_in_dim.8), calls=%async_computation.5 | async-start | bytes 1048576 | tf_op jit(solution)/shard_map/all_to_all | solution.py:468
  195.0 6.1 %collective-permute-start.17 = (bf16[256,256]{1,0:T(8,128)(2,1)S(1)}, bf16[256,256]{1,0:T(8,128)(2,1)}, u32[]{:S(2)}, u32[]{:S(2)}) collective-permute-start(bf16[256,256]{1,0:T(8,128)(2,1)S(1)} %add_convert_fusion.3), channel_id=1, source_target_pairs={{0,8},{8,0},{16,24},{24,16},{1,9},{9,1},{17,25},{25,17},{2,10},{10... | collective-permute-start | bytes 393224 | tf_op jit(solution)/shard_map/ppermute | solution.py:23
  196.7 6.3 %collective-permute-start.19 = (bf16[256,256]{1,0:T(8,128)(2,1)S(1)}, bf16[256,256]{1,0:T(8,128)(2,1)}, u32[]{:S(2)}, u32[]{:S(2)}) collective-permute-start(bf16[256,256]{1,0:T(8,128)(2,1)S(1)} %add_convert_fusion.2), channel_id=1, source_target_pairs={{0,8},{8,0},{16,24},{24,16},{1,9},{9,1},{17,25},{25,17},{2,10},{10... | collective-permute-start | bytes 393224 | tf_op jit(solution)/shard_map/ppermute | solution.py:23
  201.1 4.8 %collective-permute-start.20 = (bf16[128,2048]{1,0:T(8,128)(2,1)S(1)}, bf16[128,2048]{1,0:T(8,128)(2,1)S(1)}, u32[]{:S(2)}, u32[]{:S(2)}) collective-permute-start(bf16[128,2048]{1,0:T(8,128)(2,1)S(1)} %bitcast.23), channel_id=1, source_target_pairs={{0,1},{1,0},{2,3},{3,2},{4,5},{5,4},{6,7},{7,6},{8,9},{9,8},{10,11... | collective-permute-start | bytes 1572872 | tf_op jit(solution)/shard_map/ppermute | solution.py:23

commit v7 on v6

--- a/solution.py
+++ b/solution.py
@@ -8,7 +8,6 @@
 HEAD = 2
 LAM = 0.1
 CHUNKS = 2
-PARTS = 4
 BLOCK = 256
 VOCAB_SCALE = 128.0
 PRE_SCALE = 64.0
@@ -186,62 +185,6 @@
         cost_estimate=cost(6 * rows * cols, 8 * rows * cols, rows * cols),
         name="target_probs",
     )(target, target, incoming, top, total)
-
-
-def vocab_parts(up_weight, head_weight, width):
-    rank, depth = up_weight.shape
-    cols = head_weight.shape[1]
-    rows = rank // 2
-    block = depth // PARTS
-    count = cols // width
-
-    def body(up_ref, head_ref, *rest):
-        outs, (buffer, totals, arrived) = rest[: 2 * count], rest[2 * count :]
-        copies = [
-            pltpu.make_async_copy(
-                head_ref.at[pl.ds(k * block, block), :], buffer.at[k], arrived.at[k]
-            )
-            for k in range(PARTS)
-        ]
-        for copy in copies:
-            copy.start()
-        tile = min(512, cols)
-        for k in range(PARTS):
-            copies[k].wait()
-            left = up_ref[:, k * block : (k + 1) * block]
-
-            @pl.loop(0, cols // tile)
-            def _(t):
-                place = pl.ds(pl.multiple_of(t * tile, tile), tile)
-                term = jnp.dot(left, buffer[k, :, place], preferred_element_type=F32)
-                if k == 0:
-                    totals[:, place] = term
-                else:
-                    totals[:, place] += term
-
-        mine = lax.axis_index("grp") & 1
-        for c in range(count):
-            here = slice(c * width, (c + 1) * width)
-            away = totals[pl.ds(pl.multiple_of((1 - mine) * rows, rows), rows), here]
-            kept = totals[pl.ds(pl.multiple_of(mine * rows, rows), rows), here]
-            outs[2 * c][...] = away * VOCAB_SCALE
-            outs[2 * c + 1][...] = kept * VOCAB_SCALE
-
-    outs = pl.pallas_call(
-        body,
-        in_specs=[pl.BlockSpec(memory_space=pltpu.VMEM), pl.BlockSpec(memory_space=pltpu.HBM)],
-        out_specs=[pl.BlockSpec(memory_space=pltpu.VMEM)] * (2 * count),
-        out_shape=[jax.ShapeDtypeStruct((rows, width), F32)] * (2 * count),
-        scratch_shapes=[
-            pltpu.VMEM((PARTS, block, cols), BF16),
-            pltpu.VMEM((rank, cols), F32),
-            pltpu.SemaphoreType.DMA((PARTS,)),
-        ],
-        compiler_params=pltpu.CompilerParams(vmem_limit_bytes=56 << 20),
-        cost_estimate=cost(2 * rank * depth * cols, 2 * depth * cols, 0),
-        name="vocab_parts",
-    )(up_weight, head_weight)
-    return [(outs[2 * c], outs[2 * c + 1]) for c in range(count)]
 
 
 def draft_chunk(target, acts, pieces, column, sums):
@@ -296,7 +239,7 @@
             jax.ShapeDtypeStruct((rows, 1), F32),
             jax.ShapeDtypeStruct((rows, 1), F32),
         ],
-        compiler_params=params(54),
+        compiler_params=params(16),
         cost_estimate=cost(2 * rows * rank * width, 8 * rows * width, rows * width),
         name="draft_chunk",
     )(target, acts, *pieces, *carried)
@@ -367,7 +310,7 @@
             jax.ShapeDtypeStruct((rows, 1), F32),
         ],
         scratch_shapes=[pltpu.VMEM((rank, width), F32)],
-        compiler_params=params(54),
+        compiler_params=params(16),
         cost_estimate=cost(4 * rows * rank * width, 8 * rows * width, rows * width),
         name="grad_chunk",
     )(draft, prob, label, acts, vocab_proj, *sums, *extra)
@@ -464,38 +407,10 @@
     return pieces[0]
 
 
-def all_to_all(blocks, groups):
-    return lax.all_to_all(blocks, "voc", 0, 0, axis_index_groups=groups)
-
-
-def over_voc(line, part, wire, between, paired=False):
-    def steps():
-        count = lax.axis_size("voc")
-        rows = part
-        groups = None
-        if paired:
-            count = count // 2
-            groups = [list(range(parity, 2 * count, 2)) for parity in range(2)]
-            mine = own_bit("voc", 0)
-            away, kept = half(part, 1 - mine), half(part, mine)
-            arrived = yield from sent_over(line, away.astype(wire), "voc", 0)
-            rows = kept + arrived.astype(F32)
-        blocks = rows.astype(wire).reshape(count, rows.shape[0] // count, rows.shape[1])
-        blocks = line.put(line.after(blocks))
-        arrived = all_to_all(blocks, groups)
-        yield
-        total = jnp.sum(line.after(arrived).astype(F32), 0)
-        own = line.put(line.after(between(total)))
-        copies = jnp.broadcast_to(own[None], (count, *own.shape))
-        arrived = all_to_all(copies, groups)
-        yield
-        whole = line.after(arrived).reshape(rows.shape)
-        if paired:
-            other = yield from sent_over(line, whole, "voc", 0)
-            return joined("voc", 0, whole, other)
-        return whole
-
-    return Chain(steps())
+def over_voc(line, part, bits, wires, between, alike=False):
+    pieces = []
+    chain = summed(line, split_pair(part, "voc", bits), "voc", bits, wires, between, pieces, alike)
+    return chain, lambda: (chain.result(), joined("voc", bits[0], *pieces))[1]
 
 
 def on_device(hidden_states, target_logits, labels, down_weight, up_weight, head_weight):
@@ -510,16 +425,28 @@
     width = slice_cols // CHUNKS
     chunks = range(CHUNKS)
     z_bits = list(range(group_count.bit_length() - 1))
+    v_bits = list(range(lax.axis_size("voc").bit_length() - 1))
+    v_other = v_bits[:1] + v_bits[:0:-1]
     line = Line()
 
+    def columns(c):
+        return head_weight[:, c * width : (c + 1) * width]
+
+    mine = own_bit("grp", z_bits[0])
+    up_away, up_kept = half(up_weight, 1 - mine), half(up_weight, mine)
     vocab_pieces = [[] for c in chunks]
-    vocab = [
-        summed(
-            line, pair, "grp", z_bits, [F16] * len(z_bits),
-            lambda total: (total * (1.0 / VOCAB_SCALE)).astype(BF16), vocab_pieces[c],
+    vocab = []
+    for c in chunks:
+        away, kept = [
+            jnp.dot(part, columns(c), preferred_element_type=F32) * VOCAB_SCALE
+            for part in (up_away, up_kept)
+        ]
+        vocab.append(
+            summed(
+                line, (away, kept), "grp", z_bits, [F16] * len(z_bits),
+                lambda total: (total * (1.0 / VOCAB_SCALE)).astype(BF16), vocab_pieces[c],
+            )
         )
-        for c, pair in enumerate(vocab_parts(up_weight, head_weight, width))
-    ]
     vocab[0].step()
     devices = range(group_count)
     top_rows = line.put(line.after(target_logits[:8]))
@@ -534,10 +461,16 @@
         kept_pre.append(total * (1.0 / PRE_SCALE))
         return jax.nn.silu(kept_pre[0]).astype(BF16)
 
-    pre = over_voc(line, pre_part * PRE_SCALE, F16, activate)
+    pre, all_acts = over_voc(
+        line, pre_part * PRE_SCALE, v_bits, [F16] * len(v_bits), activate
+    )
+    pre.step()
+    incoming = line.put(line.after(incoming))
     vocab[0].step()
     pre.step()
     vocab[1].step()
+    pre.step()
+    vocab[0].step()
     if per_book == 1:
         prob, entropy = target_pass(target_logits, line.after(incoming))
     else:
@@ -547,9 +480,11 @@
     line.put(entropy)
     label = lax.dynamic_slice_in_dim(labels, book_index, 1, 1) - book_part * slice_cols
     pre.step()
-    vocab[0].step()
-    acts = line.put(pre.result())
+    vocab[0].result()
+    line.put(vocab_pieces[0][1])
     vocab[1].step()
+    pre.step()
+    acts = line.put(all_acts())
 
     drafts, vocab_proj, sums = [], [], None
     for c in chunks:
@@ -575,29 +510,30 @@
         )
         grads[c].step()
     act_part, loss = carried
-    act = over_voc(
-        line, act_part, F32, lambda total: (total * silu_slope(kept_pre[0])).astype(BF16)
+    act, all_pre_grad = over_voc(
+        line, act_part, v_bits, [F32] + [BF16] * len(v_bits),
+        lambda total: (total * silu_slope(kept_pre[0])).astype(BF16),
     )
     grads[0].step()
+    act.step()
+    act.step()
     grads[1].step()
     act.step()
     loss = over_books(loss + entropy, jnp.add, per_book)
     frame_loss = lax.dynamic_slice_in_dim(loss, book_part * block_rows, block_rows, 0)
     frame_loss = frame_loss.reshape(1, 1, block_rows)
 
-    def columns(c):
-        return head_weight[:, c * width : (c + 1) * width]
-
     def times_head(before, piece, c):
         return line.put(before + inner_cols(line.after(piece), columns(c)))
 
     own_up = times_head(0.0, first_of(grads[0], grad_pieces[0]), 0)
+    act.step()
+    own = first_of(grads[1], grad_pieces[1])
     act.step()
     grads[0].result()
     other_up = times_head(0.0, grad_pieces[0][1], 0)
-    pre_grad = line.put(act.result())
+    pre_grad = line.put(all_pre_grad())
     down_part = line.put(inner_rows(line.after(hidden_states), pre_grad))
-    own = first_of(grads[1], grad_pieces[1])
     rows = down_part.shape[0] // 2
     down_pieces = [[], []]
     downs = [
@@ -612,17 +548,18 @@
     own_up = times_head(own_up, own, 1)
     grads[1].result()
     other_up = times_head(other_up, grad_pieces[1][1], 1)
-    up_part = joined("grp", 0, own_up, other_up)
-    ups = over_voc(line, up_part, BF16, lambda total: total.astype(BF16), True)
-    ups.step()
-    downs[0].step()
-    downs[1].step()
-    ups.step()
-    ups.step()
-    downs[0].step()
-    downs[1].step()
-    ups.step()
-    grad_b = ups.result().astype(F32)
+    up_part = joined("grp", z_bits[0], own_up, other_up)
+    rank = up_part.shape[0] // 2
+    ups = [
+        over_voc(
+            line, part, bits, [F32] + [BF16] * len(v_bits), lambda total: total.astype(BF16), True
+        )
+        for part, bits in ((up_part[:rank], v_bits), (up_part[rank:], v_other))
+    ]
+    for _ in range(2 * len(v_bits)):
+        for chain in (ups[0][0], ups[1][0], downs[0], downs[1]):
+            chain.step()
+    grad_b = jnp.concatenate([result().astype(F32) for _, result in ups], 0)
     for chain in downs:
         chain.result()
     grad_a = jnp.concatenate(

time: 209 us -> 158 us (0.76)
  Pallas kernels: 48.1 us -> 24 us
  waiting for transfers between devices: 58.4 us -> 39.3 us
  other arithmetic: 27.4 us -> 14 us
  matrix products: 18.1 us -> 26.7 us
  starting transfers between devices: 48.2 us -> 44 us
    all_to_all x6 -> x0, starting transfers between devices: 24.1 us -> none  [all_to_all(): return lax.all_to_all(blocks, 'voc', 0, 0, axis_index_groups=groups)]
    ppermute x20 -> x38, starting transfers between devices: 22.8 us -> 42.7 us  [swap(): return lax.ppermute(value, axis, pairs)]
    dot_general x0 -> x4, matrix products: none -> 14.7 us  [on_device(): jnp.dot(part, columns(c), preferred_element_type=F32) * VOCAB_SCALE]
    all_to_all x6 -> x0, waiting for transfers between devices: 13.6 us -> none  [all_to_all(): return lax.all_to_all(blocks, 'voc', 0, 0, axis_index_groups=groups)]
    pallas_call x1 -> x0, Pallas kernels: 9.45 us -> none  [vocab_parts(): pl.pallas_call(body, in_specs=[pl.BlockSpec(memory_space=pltpu.VMEM), pl....]
    pallas_call x2, Pallas kernels: 16.8 us -> 8.26 us  [grad_chunk(): pl.pallas_call(body, grid=(rows // block,), in_specs=[row_spec(block, wid...]
    pallas_call x2, Pallas kernels: 12.8 us -> 6.57 us  [draft_chunk(): pl.pallas_call(body, grid=(rows // block,), in_specs=[row_spec(block, wid...]
    ppermute x20 -> x38, waiting for transfers between devices: 44.3 us -> 39.3 us  [swap(): return lax.ppermute(value, axis, pairs)]
  transfers between devices with their start and end apart: 27 -> 39, of which waited for: 15 -> 18; matrix products, arithmetic and copies ran while one was open for 21% -> 24% of each run, Pallas kernels for 12% -> 10%
where the time goes in v7:
time: 158 us
  starting transfers between devices  44 us (28%)
  waiting for transfers between devices  39.3 us (25%)
  matrix products  26.7 us (17%)
  Pallas kernels  24 us (15%)
  other arithmetic  14 us (9%)
  local copies, waits for them, and re-layouts  8.2 us (5%)
    ppermute x38, starting transfers between devices, swap(): return lax.ppermute(value, axis, pairs)  42.7 us
    ppermute x38, waiting for transfers between devices, swap(): return lax.ppermute(value, axis, pairs)  39.3 us
    dot_general x4, matrix products, on_device(): jnp.dot(part, columns(c), preferred_element_type=F32) * VOCAB_SCALE  14.7 us
    dot_general x4, matrix products, inner_cols(): lax.dot_general(left, right, (((1,), (1,)), ((), ())), preferred_element_...  10.6 us
    pallas_call x1, Pallas kernels, target_pass(): pl.pallas_call(body, grid=(rows // block,), in_specs=[row_spec(block, col...  9.17 us
    pallas_call x2, Pallas kernels, grad_chunk(): pl.pallas_call(body, grid=(rows // block,), in_specs=[row_spec(block, wid...  8.26 us
    pallas_call x2, Pallas kernels, draft_chunk(): pl.pallas_call(body, grid=(rows // block,), in_specs=[row_spec(block, wid...  6.57 us
    unnamed x63, local copies, waits for them, and re-layouts  5.47 us
  transfers between devices with their start and end apart: 39, of which 18 were waited for; matrix products, arithmetic and copies ran while one was open for 24% of the time, Pallas kernels for 10%

profile of v7, /device:TPU:0, one launch (start us, length us, event | category | flops | bytes accessed | tf_op | source)
XLA Modules:
  0.0 157.6 jit_solution(11387323791067379630)
XLA Ops:
  0.7 3.9 %fusion.34 = f16[128,1024]{1,0:T(8,128)(2,1)} fusion(bf16[2048,2048]{1,0:T(8,128)(2,1)} %param.11, bf16[256,2048]{1,0:T(8,128)(2,1)} %param.10, s32[]{:T(128)S(6)} %select_n.175), kind=kOutput, calls=%fused_computation.22 | convolution fusion | flops 537133056 | bytes 4980740 | tf_op jit(solution)/shard_map/dot_general | solution.py:441
  4.6 3.0 %collective-permute-start.1 = (f16[128,1024]{1,0:T(8,128)(2,1)}, f16[128,1024]{1,0:T(8,128)(2,1)S(1)}, u32[]{:S(2)}, u32[]{:S(2)}) collective-permute-start(f16[128,1024]{1,0:T(8,128)(2,1)} %fusion.34), channel_id=1, source_target_pairs={{0,8},{8,0},{16,24},{24,16},{1,9},{9,1},{17,25},{25,17},{2,10},{10... | collective-permute-start | bytes 786440 | tf_op jit(solution)/shard_map/ppermute | solution.py:22
  8.5 1.3 collective-permute-start.2
  9.8 3.6 %fusion.37 = f16[128,1024]{1,0:T(8,128)(2,1)} fusion(bf16[2048,2048]{1,0:T(8,128)(2,1)} %param.11, bf16[256,2048]{1,0:T(8,128)(2,1)S(1)} %copy-done.24, s32[]{:T(128)S(6)} %select_n.175), kind=kOutput, calls=%fused_computation.23 | convolution fusion | flops 537133056 | bytes 4980740 | tf_op jit(solution)/shard_map/dot_general | solution.py:441
  13.4 2.6 %collective-permute-start.4 = (f16[128,1024]{1,0:T(8,128)(2,1)}, f16[128,1024]{1,0:T(8,128)(2,1)}, u32[]{:S(2)}, u32[]{:S(2)}) collective-permute-start(f16[128,1024]{1,0:T(8,128)(2,1)} %fusion.37), channel_id=1, source_target_pairs={{0,8},{8,0},{16,24},{24,16},{1,9},{9,1},{17,25},{25,17},{2,10},{10... | collective-permute-start | bytes 786440 | tf_op jit(solution)/shard_map/ppermute | solution.py:22
  17.6 3.2 %fusion.44 = (f16[128,1024]{1,0:T(8,128)(2,1)S(1)}, f32[128,1024]{1,0:T(8,128)S(1)}) fusion(f16[128,1024]{1,0:T(8,128)(2,1)S(1)} %collective-permute-done.1, bf16[2048,2048]{1,0:T(8,128)(2,1)} %param.11, bf16[256,2048]{1,0:T(8,128)(2,1)} %param.10, s32[]{:T(128)S(6)} %select_n.178), kind=kOutput, calls=%fused_computation.49 | convolution fusion | flops 537395200 | bytes 5767172 | tf_op jit(solution)/shard_map/dot_general | solution.py:441
  20.9 2.7 %collective-permute-start.6 = (f16[128,1024]{1,0:T(8,128)(2,1)S(1)}, f16[128,1024]{1,0:T(8,128)(2,1)S(1)}, u32[]{:S(2)}, u32[]{:S(2)}) collective-permute-start(f16[128,1024]{1,0:T(8,128)(2,1)S(1)} %get-tuple-element.111), channel_id=1, source_target_pairs={{0,16},{8,24},{16,0},{24,8},{1,17},{9,25},{17,1},{25,9},{2,18},{10... | collective-permute-start | bytes 786440 | tf_op jit(solution)/shard_map/ppermute | solution.py:22
  24.8 1.6 collective-permute-start.3
  26.3 3.9 %fusion.45 = (f16[128,1024]{1,0:T(8,128)(2,1)}, f32[128,1024]{1,0:T(8,128)}) fusion(f16[128,1024]{1,0:T(8,128)(2,1)} %collective-permute-done.4, bf16[2048,2048]{1,0:T(8,128)(2,1)} %param.11, bf16[256,2048]{1,0:T(8,128)(2,1)S(1)} %copy-done.25, s32[]{:T(128)S(6)} %select_n.178), kind=kOutput, calls=%fused_computation.50 | convolution fusion | flops 537395200 | bytes 5767172 | tf_op jit(solution)/shard_map/dot_general | solution.py:441
  31.2 1.5 collective-permute-start.5
  32.7 2.9 %collective-permute-done.6 = f16[128,1024]{1,0:T(8,128)(2,1)S(1)} collective-permute-done((f16[128,1024]{1,0:T(8,128)(2,1)S(1)}, f16[128,1024]{1,0:T(8,128)(2,1)S(1)}, u32[]{:S(2)}, u32[]{:S(2)}) %collective-permute-start.6) | collective-permute-done | bytes 262176 | tf_op jit(solution)/shard_map/ppermute | solution.py:22
  35.8 3.1 %collective-permute-start.8 = (f16[128,1024]{1,0:T(8,128)(2,1)}, f16[128,1024]{1,0:T(8,128)(2,1)}, u32[]{:S(2)}, u32[]{:S(2)}) collective-permute-start(f16[128,1024]{1,0:T(8,128)(2,1)} %get-tuple-element.115), channel_id=1, source_target_pairs={{0,16},{8,24},{16,0},{24,8},{1,17},{9,25},{17,1},{25,9},{2,18},{10... | collective-permute-start | bytes 786440 | tf_op jit(solution)/shard_map/ppermute | solution.py:22
  39.0 9.2 %target_pass.1 = (f32[1024,2048]{1,0:T(8,128)}, f32[1024,1]{1,0:T(8,128)S(1)}) custom-call(f32[1024,2048]{1,0:T(8,128)} %target_ref.5, f32[1024,2048]{1,0:T(8,128)} %target_ref.5, f32[8,2048]{1,0:T(8,128)S(1)} %collective-permute-done.2.incoming_ref), custom_call_target="tpu_custom_call" | custom-call | flops 3072 | bytes 4096 | tf_op jit(solution)/shard_map/target_pass/pallas_call | solution.py:132
  48.3 1.6 collective-permute-start.7
  51.1 1.9 %multiply_convert_fusion.own_ref = bf16[128,1024]{1,0:T(8,128)(2,1)} fusion(f16[128,1024]{1,0:T(8,128)(2,1)} %collective-permute-done.8, f32[128,1024]{1,0:T(8,128)S(1)} %copy-done.19, f16[128,1024]{1,0:T(8,128)(2,1)} %collective-permute-done.4), kind=kLoop, calls=%fused_computation.36 | loop fusion | flops 786432 | bytes 1310720 | tf_op jit(solution)/shard_map/convert_element_type | solution.py:447
  56.5 3.4 %copy-done.1 = f32[1024,2048]{1,0:T(8,128)S(1)} copy-done((f32[1024,2048]{1,0:T(8,128)S(1)}, f32[1024,2048]{1,0:T(8,128)}, u32[]{:S(2)}) %copy-start.1) | copy-done | bytes 8388632
  60.8 2.5 %draft_chunk.2 = (f32[1024,1024]{1,0:T(8,128)S(1)}, bf16[256,1024]{1,0:T(8,128)(2,1)S(1)}, f32[1024,1]{1,0:T(8,128)S(1)}, f32[1024,1]{1,0:T(8,128)S(1)}) custom-call(f32[1024,2048]{1,0:T(8,128)S(1)} %copy-done.1, bf16[1024,256]{1,0:T(8,128)(2,1)S(1)} %pad_maximum_fusion.acts_ref, bf16[128,1024]{1,0:T(8,128)(2,1)S(1)} %multiply_convert_fusion.1.own_ref, ...), custom_call_target="tpu_custom_call" | custom-call | flops 131072 | bytes 2048 | tf_op jit(solution)/shard_map/draft_chunk/pallas_call | solution.py:220
  63.3 4.1 %draft_chunk.3 = (f32[1024,1024]{1,0:T(8,128)S(1)}, bf16[256,1024]{1,0:T(8,128)(2,1)S(1)}, f32[1024,1]{1,0:T(8,128)S(1)}, f32[1024,1]{1,0:T(8,128)S(1)}) custom-call(f32[1024,2048]{1,0:T(8,128)S(1)} %copy-done.1, bf16[1024,256]{1,0:T(8,128)(2,1)S(1)} %pad_maximum_fusion.acts_ref, bf16[128,1024]{1,0:T(8,128)(2,1)} %multiply_convert_fusion.own_ref, ...), custom_call_target="tpu_custom_call" | custom-call | flops 131072 | bytes 2048 | tf_op jit(solution)/shard_map/draft_chunk/pallas_call | solution.py:220
  67.4 4.1 %grad_chunk.2 = (bf16[128,1024]{1,0:T(8,128)(2,1)S(1)}, f32[128,1024]{1,0:T(8,128)S(1)}, f32[1024,256]{1,0:T(8,128)S(1)}, f32[1024,1]{1,0:T(8,128)S(1)}) custom-call(f32[1024,1024]{1,0:T(8,128)S(1)} %get-tuple-element.135.draft_ref, f32[1024,2048]{1,0:T(8,128)S(1)} %bitcast.9, s32[1024,1]{1,0:T(8,128)S(1)} %copy.11.label_ref, ...), custom_call_target="tpu_custom_call" | custom-call | flops 262144 | bytes 2048 | tf_op jit(solution)/shard_map/grad_chunk/pallas_call | solution.py:292
  72.8 4.2 %grad_chunk.3 = (bf16[128,1024]{1,0:T(8,128)(2,1)S(1)}, f32[128,1024]{1,0:T(8,128)S(1)}, f32[1024,256]{1,0:T(8,128)S(1)}, f32[1024,1]{1,0:T(8,128)S(1)}) custom-call(f32[1024,1024]{1,0:T(8,128)S(1)} %get-tuple-element.141.draft_ref, f32[1024,2048]{1,0:T(8,128)S(1)} %bitcast.9, s32[1024,1]{1,0:T(8,128)S(1)} %copy.11.label_ref, ...), custom_call_target="tpu_custom_call" | custom-call | flops 262144 | bytes 2048 | tf_op jit(solution)/shard_map/grad_chunk/pallas_call | solution.py:292
  78.6 1.3 collective-permute-done.12
  80.9 1.3 collective-permute-start.15
  82.2 2.0 %add_reduce_fusion = f32[1024]{0:T(1024)} fusion(f32[1024,1]{1,0:T(8,128)} %copy-done.8, f32[1024,1]{1,0:T(8,128)} %copy-done.7), kind=kLoop, calls=%fused_computation.35 | loop fusion | flops 1024 | bytes 12288 | tf_op jit(solution)/shard_map/add | solution.py:522
  85.4 1.3 dynamic-slice_add_fusion.2
  86.7 1.6 collective-permute-start.14
  88.2 4.4 %collective-permute-done.15 = bf16[128,1024]{1,0:T(8,128)(2,1)S(1)} collective-permute-done((bf16[128,1024]{1,0:T(8,128)(2,1)}, bf16[128,1024]{1,0:T(8,128)(2,1)S(1)}, u32[]{:S(2)}, u32[]{:S(2)}) %collective-permute-start.15) | collective-permute-done | bytes 262176 | tf_op jit(solution)/shard_map/ppermute | solution.py:22
  93.0 1.6 %collective-permute-start.16 = (bf16[256,256]{1,0:T(8,128)(2,1)S(1)}, bf16[256,256]{1,0:T(8,128)(2,1)S(1)}, u32[]{:S(2)}, u32[]{:S(2)}) collective-permute-start(bf16[256,256]{1,0:T(8,128)(2,1)S(1)} %fusion.48), channel_id=1, source_target_pairs={{0,4},{1,5},{2,6},{3,7},{4,0},{5,1},{6,2},{7,3},{8,12},{9,13},{10,... | collective-permute-start | bytes 393224 | tf_op jit(solution)/shard_map/ppermute | solution.py:22
  94.6 11.2 %collective-permute-done.17 = bf16[128,1024]{1,0:T(8,128)(2,1)S(1)} collective-permute-done((bf16[128,1024]{1,0:T(8,128)(2,1)}, bf16[128,1024]{1,0:T(8,128)(2,1)S(1)}, u32[]{:S(2)}, u32[]{:S(2)}) %collective-permute-start.17) | collective-permute-done | bytes 262176 | tf_op jit(solution)/shard_map/ppermute | solution.py:22
  106.0 3.7 %fusion.2 = f32[128,2048]{1,0:T(8,128)S(1)} fusion(bf16[128,1024]{1,0:T(8,128)(2,1)S(1)} %add_convert_fusion.1, bf16[2048,2048]{1,0:T(8,128)(2,1)} %param.11), kind=kOutput, calls=%fused_computation.2 | convolution fusion | flops 536870912 | bytes 5505024 | tf_op jit(solution)/shard_map/dot_general | solution.py:44
  109.9 1.6 collective-permute-start.18
  111.6 2.1 %collective-permute-start.23 = (bf16[128,1024]{1,0:T(8,128)(2,1)S(1)}, bf16[128,1024]{1,0:T(8,128)(2,1)S(1)}, u32[]{:S(2)}, u32[]{:S(2)}) collective-permute-start(bf16[128,1024]{1,0:T(8,128)(2,1)S(1)} %add_convert_fusion), channel_id=1, source_target_pairs={{0,8},{8,0},{16,24},{24,16},{1,9},{9,1},{17,25},{25,17},{2,10},{10... | collective-permute-start | bytes 786440 | tf_op jit(solution)/shard_map/ppermute | solution.py:22
  113.6 1.3 collective-permute-done.18
  116.2 3.8 %fusion = f32[128,2048]{1,0:T(8,128)S(1)} fusion(bf16[128,1024]{1,0:T(8,128)(2,1)S(1)} %collective-permute-done.21, bf16[2048,2048]{1,0:T(8,128)(2,1)} %param.11), kind=kOutput, calls=%fused_computation | convolution fusion | flops 536870912 | bytes 5505024 | tf_op jit(solution)/shard_map/dot_general | solution.py:44
  123.2 1.5 fusion.16
  124.7 1.5 broadcast_select_fusion
  129.3 1.8 %collective-permute-start.31 = (bf16[256,256]{1,0:T(8,128)(2,1)S(1)}, bf16[256,256]{1,0:T(8,128)(2,1)S(1)}, u32[]{:S(2)}, u32[]{:S(2)}) collective-permute-start(bf16[256,256]{1,0:T(8,128)(2,1)S(1)} %add_convert_fusion.8), channel_id=1, source_target_pairs={{0,16},{8,24},{16,0},{24,8},{1,17},{9,25},{17,1},{25,9},{2,18},{10... | collective-permute-start | bytes 393224 | tf_op jit(solution)/shard_map/ppermute | solution.py:22
  131.3 1.6 collective-permute-start.30
  133.0 1.6 %collective-permute-start.29 = (bf16[32,2048]{1,0:T(8,128)(2,1)S(1)}, bf16[32,2048]{1,0:T(8,128)(2,1)S(1)}, u32[]{:S(2)}, u32[]{:S(2)}) collective-permute-start(bf16[32,2048]{1,0:T(8,128)(2,1)S(1)} %dynamic-slice_convert_fusion.1), channel_id=1, source_target_pairs={{0,4},{1,5},{2,6},{3,7},{4,0},{5,1},{6,2},{7,3},{8,12},{9,13},{10,... | collective-permute-start | bytes 393224 | tf_op jit(solution)/shard_map/ppermute | solution.py:22
  134.5 5.0 %collective-permute-done.24 = bf16[256,256]{1,0:T(8,128)(2,1)S(1)} collective-permute-done((bf16[256,256]{1,0:T(8,128)(2,1)S(1)}, bf16[256,256]{1,0:T(8,128)(2,1)S(1)}, u32[]{:S(2)}, u32[]{:S(2)}) %collective-permute-start.24) | collective-permute-done | bytes 131104 | tf_op jit(solution)/shard_map/ppermute | solution.py:22
  139.6 2.3 %collective-permute-done.31 = bf16[256,256]{1,0:T(8,128)(2,1)S(1)} collective-permute-done((bf16[256,256]{1,0:T(8,128)(2,1)S(1)}, bf16[256,256]{1,0:T(8,128)(2,1)S(1)}, u32[]{:S(2)}, u32[]{:S(2)}) %collective-permute-start.31) | collective-permute-done | bytes 131104 | tf_op jit(solution)/shard_map/ppermute | solution.py:22
  142.1 1.6 %collective-permute-start.33 = (bf16[32,2048]{1,0:T(8,128)(2,1)S(1)}, bf16[32,2048]{1,0:T(8,128)(2,1)S(1)}, u32[]{:S(2)}, u32[]{:S(2)}) collective-permute-start(bf16[32,2048]{1,0:T(8,128)(2,1)S(1)} %add_convert_fusion.5), channel_id=1, source_target_pairs={{0,4},{1,5},{2,6},{3,7},{4,0},{5,1},{6,2},{7,3},{8,12},{9,13},{10,... | collective-permute-start | bytes 393224 | tf_op jit(solution)/shard_map/ppermute | solution.py:22
  143.7 1.6 collective-permute-start.35
  145.2 2.2 %collective-permute-done.32 = bf16[256,256]{1,0:T(8,128)(2,1)S(1)} collective-permute-done((bf16[256,256]{1,0:T(8,128)(2,1)S(1)}, bf16[256,256]{1,0:T(8,128)(2,1)S(1)}, u32[]{:S(2)}, u32[]{:S(2)}) %collective-permute-start.32) | collective-permute-done | bytes 131104 | tf_op jit(solution)/shard_map/ppermute | solution.py:22
  147.5 1.6 collective-permute-start.34
  149.1 1.6 %collective-permute-start.37 = (bf16[32,2048]{1,0:T(8,128)(2,1)S(1)}, bf16[32,2048]{1,0:T(8,128)(2,1)S(1)}, u32[]{:S(2)}, u32[]{:S(2)}) collective-permute-start(bf16[32,2048]{1,0:T(8,128)(2,1)S(1)} %add_convert_fusion.2), channel_id=1, source_target_pairs={{0,4},{1,5},{2,6},{3,7},{4,0},{5,1},{6,2},{7,3},{8,12},{9,13},{10,... | collective-permute-start | bytes 393224 | tf_op jit(solution)/shard_map/ppermute | solution.py:22
  150.7 1.9 %collective-permute-done.34 = bf16[32,2048]{1,0:T(8,128)(2,1)S(1)} collective-permute-done((bf16[32,2048]{1,0:T(8,128)(2,1)S(1)}, bf16[32,2048]{1,0:T(8,128)(2,1)S(1)}, u32[]{:S(2)}, u32[]{:S(2)}) %collective-permute-start.34) | collective-permute-done | bytes 131104 | tf_op jit(solution)/shard_map/ppermute | solution.py:22
  152.7 1.5 collective-permute-done.37
  156.0 1.6 maximum_convert_fusion
  (161 shorter events, 26.2 us)
Async XLA Ops:
  0.6 15.4 %copy-start = (bf16[1024,1024]{1,0:T(8,128)(2,1)S(1)}, bf16[1024,1024]{1,0:T(8,128)(2,1)}, u32[]{:S(2)}) copy-start(bf16[1024,1024]{1,0:T(8,128)(2,1)} %param.6) | copy-start | bytes 6291460
  4.6 13.0 %collective-permute-start.1 = (f16[128,1024]{1,0:T(8,128)(2,1)}, f16[128,1024]{1,0:T(8,128)(2,1)S(1)}, u32[]{:S(2)}, u32[]{:S(2)}) collective-permute-start(f16[128,1024]{1,0:T(8,128)(2,1)} %fusion.34), channel_id=1, source_target_pairs={{0,8},{8,0},{16,24},{24,16},{1,9},{9,1},{17,25},{25,17},{2,10},{10... | collective-permute-start | bytes 786440 | tf_op jit(solution)/shard_map/ppermute | solution.py:22
  8.5 9.1 %collective-permute-start.2 = (f32[8,2048]{1,0:T(8,128)S(1)}, f32[8,2048]{1,0:T(8,128)S(1)}, u32[]{:S(2)}, u32[]{:S(2)}) collective-permute-start(f32[8,2048]{1,0:T(8,128)S(1)} %slice.22), channel_id=1, source_target_pairs={{8,0},{16,8},{24,16},{9,1},{17,9},{25,17},{10,2},{18,10},{26,18},{... | collective-permute-start | bytes 196616 | tf_op jit(solution)/shard_map/ppermute | solution.py:453
  13.4 12.9 %collective-permute-start.4 = (f16[128,1024]{1,0:T(8,128)(2,1)}, f16[128,1024]{1,0:T(8,128)(2,1)}, u32[]{:S(2)}, u32[]{:S(2)}) collective-permute-start(f16[128,1024]{1,0:T(8,128)(2,1)} %fusion.37), channel_id=1, source_target_pairs={{0,8},{8,0},{16,24},{24,16},{1,9},{9,1},{17,25},{25,17},{2,10},{10... | collective-permute-start | bytes 786440 | tf_op jit(solution)/shard_map/ppermute | solution.py:22
  17.6 5.9 %collective-permute-start = (f16[512,256]{1,0:T(8,128)(2,1)}, f16[512,256]{1,0:T(8,128)(2,1)}, u32[]{:S(2)}, u32[]{:S(2)}) collective-permute-start(f16[512,256]{1,0:T(8,128)(2,1)} %dynamic-slice_convert_fusion), channel_id=1, source_target_pairs={{0,1},{1,0},{2,3},{3,2},{4,5},{5,4},{6,7},{7,6},{8,9},{9,8},{10,11... | collective-permute-start | bytes 786440 | tf_op jit(solution)/shard_map/ppermute | solution.py:22
  20.9 14.7 %collective-permute-start.6 = (f16[128,1024]{1,0:T(8,128)(2,1)S(1)}, f16[128,1024]{1,0:T(8,128)(2,1)S(1)}, u32[]{:S(2)}, u32[]{:S(2)}) collective-permute-start(f16[128,1024]{1,0:T(8,128)(2,1)S(1)} %get-tuple-element.111), channel_id=1, source_target_pairs={{0,16},{8,24},{16,0},{24,8},{1,17},{9,25},{17,1},{25,9},{2,18},{10... | collective-permute-start | bytes 786440 | tf_op jit(solution)/shard_map/ppermute | solution.py:22
  24.7 23.4 %copy-start.12 = (f32[512,256]{1,0:T(8,128)}, f32[512,256]{1,0:T(8,128)S(1)}, u32[]{:S(2)}) copy-start(f32[512,256]{1,0:T(8,128)S(1)} %convert_add_fusion.3) | copy-start | bytes 1572868
  24.8 5.7 %collective-permute-start.3 = (f16[256,256]{1,0:T(8,128)(2,1)S(1)}, f16[256,256]{1,0:T(8,128)(2,1)S(1)}, u32[]{:S(2)}, u32[]{:S(2)}) collective-permute-start(f16[256,256]{1,0:T(8,128)(2,1)S(1)} %dynamic-slice_convert_fusion.6), channel_id=1, source_target_pairs={{0,2},{1,3},{2,0},{3,1},{4,6},{5,7},{6,4},{7,5},{8,10},{9,11},{10,... | collective-permute-start | bytes 393224 | tf_op jit(solution)/shard_map/ppermute | solution.py:22
  30.5 17.7 %copy-start.14 = (f16[256,256]{1,0:T(8,128)(2,1)}, f16[256,256]{1,0:T(8,128)(2,1)S(1)}, u32[]{:S(2)}) copy-start(f16[256,256]{1,0:T(8,128)(2,1)S(1)} %collective-permute-done.3) | copy-start | bytes 393220
  31.2 17.0 %collective-permute-start.5 = (f16[256,256]{1,0:T(8,128)(2,1)}, f16[256,256]{1,0:T(8,128)(2,1)S(1)}, u32[]{:S(2)}, u32[]{:S(2)}) collective-permute-start(f16[256,256]{1,0:T(8,128)(2,1)} %fusion.49), channel_id=1, source_target_pairs={{0,4},{1,5},{2,6},{3,7},{4,0},{5,1},{6,2},{7,3},{8,12},{9,13},{10,... | collective-permute-start | bytes 393224 | tf_op jit(solution)/shard_map/ppermute | solution.py:22
  35.8 14.1 %collective-permute-start.9 = (bf16[128,1024]{1,0:T(8,128)(2,1)S(1)}, bf16[128,1024]{1,0:T(8,128)(2,1)S(1)}, u32[]{:S(2)}, u32[]{:S(2)}) collective-permute-start(bf16[128,1024]{1,0:T(8,128)(2,1)S(1)} %multiply_convert_fusion.1.own_ref), channel_id=1, source_target_pairs={{0,8},{8,0},{16,24},{24,16},{1,9},{9,1},{17,25},{25,17},{2,10},{10... | collective-permute-start | bytes 786440 | tf_op jit(solution)/shard_map/ppermute | solution.py:22
  35.8 15.2 %collective-permute-start.8 = (f16[128,1024]{1,0:T(8,128)(2,1)}, f16[128,1024]{1,0:T(8,128)(2,1)}, u32[]{:S(2)}, u32[]{:S(2)}) collective-permute-start(f16[128,1024]{1,0:T(8,128)(2,1)} %get-tuple-element.115), channel_id=1, source_target_pairs={{0,16},{8,24},{16,0},{24,8},{1,17},{9,25},{17,1},{25,9},{2,18},{10... | collective-permute-start | bytes 786440 | tf_op jit(solution)/shard_map/ppermute | solution.py:22
  48.3 5.0 %collective-permute-start.7 = (bf16[256,256]{1,0:T(8,128)(2,1)S(1)}, bf16[256,256]{1,0:T(8,128)(2,1)S(1)}, u32[]{:S(2)}, u32[]{:S(2)}) collective-permute-start(bf16[256,256]{1,0:T(8,128)(2,1)S(1)} %multiply_convert_fusion.3), channel_id=1, source_target_pairs={{0,2},{1,3},{2,0},{3,1},{4,6},{5,7},{6,4},{7,5},{8,10},{9,11},{10,... | collective-permute-start | bytes 393224 | tf_op jit(solution)/shard_map/ppermute | solution.py:22
  53.4 1.7 %collective-permute-start.10 = (bf16[512,256]{1,0:T(8,128)(2,1)S(1)}, bf16[512,256]{1,0:T(8,128)(2,1)}, u32[]{:S(2)}, u32[]{:S(2)}) collective-permute-start(bf16[512,256]{1,0:T(8,128)(2,1)S(1)} %pad_maximum_fusion.2), channel_id=1, source_target_pairs={{0,1},{1,0},{2,3},{3,2},{4,5},{5,4},{6,7},{7,6},{8,9},{9,8},{10,11... | collective-permute-start | bytes 786440 | tf_op jit(solution)/shard_map/ppermute | solution.py:22
  54.2 9.1 %collective-permute-start.11 = (bf16[128,1024]{1,0:T(8,128)(2,1)}, bf16[128,1024]{1,0:T(8,128)(2,1)}, u32[]{:S(2)}, u32[]{:S(2)}) collective-permute-start(bf16[128,1024]{1,0:T(8,128)(2,1)} %multiply_convert_fusion.own_ref), channel_id=1, source_target_pairs={{0,8},{8,0},{16,24},{24,16},{1,9},{9,1},{17,25},{25,17},{2,10},{10... | collective-permute-start | bytes 786440 | tf_op jit(solution)/shard_map/ppermute | solution.py:22
  71.5 8.4 %collective-permute-start.12 = (bf16[128,1024]{1,0:T(8,128)(2,1)S(1)}, bf16[128,1024]{1,0:T(8,128)(2,1)S(1)}, u32[]{:S(2)}, u32[]{:S(2)}) collective-permute-start(bf16[128,1024]{1,0:T(8,128)(2,1)S(1)} %get-tuple-element.140), channel_id=1, source_target_pairs={{0,8},{8,0},{16,24},{24,16},{1,9},{9,1},{17,25},{25,17},{2,10},{10... | collective-permute-start | bytes 786440 | tf_op jit(solution)/shard_map/ppermute | solution.py:22
  77.8 14.9 %copy-start.3 = (f32[128,1024]{1,0:T(8,128)S(1)}, f32[128,1024]{1,0:T(8,128)}, u32[]{:S(2)}) copy-start(f32[128,1024]{1,0:T(8,128)} %copy-done.2) | copy-start | bytes 1572868
  80.8 25.0 %copy-start.5 = (f32[128,1024]{1,0:T(8,128)S(1)}, f32[128,1024]{1,0:T(8,128)}, u32[]{:S(2)}) copy-start(f32[128,1024]{1,0:T(8,128)} %copy-done.4) | copy-start | bytes 1572868
  80.8 4.6 %collective-permute-start.13 = (f32[512,256]{1,0:T(8,128)}, f32[512,256]{1,0:T(8,128)}, u32[]{:S(2)}, u32[]{:S(2)}) collective-permute-start(f32[512,256]{1,0:T(8,128)} %constant_dynamic-slice_fusion.2), channel_id=1, source_target_pairs={{0,1},{1,0},{2,3},{3,2},{4,5},{5,4},{6,7},{7,6},{8,9},{9,8},{10,11... | collective-permute-start | bytes 1572872 | tf_op jit(solution)/shard_map/ppermute | solution.py:22
  80.8 24.9 %copy-start.18 = (bf16[128,1024]{1,0:T(8,128)(2,1)S(1)}, bf16[128,1024]{1,0:T(8,128)(2,1)}, u32[]{:S(2)}) copy-start(bf16[128,1024]{1,0:T(8,128)(2,1)} %copy-done.17) | copy-start | bytes 786436
  80.9 11.7 %collective-permute-start.15 = (bf16[128,1024]{1,0:T(8,128)(2,1)}, bf16[128,1024]{1,0:T(8,128)(2,1)S(1)}, u32[]{:S(2)}, u32[]{:S(2)}) collective-permute-start(bf16[128,1024]{1,0:T(8,128)(2,1)} %copy-done.11), channel_id=1, source_target_pairs={{0,8},{8,0},{16,24},{24,16},{1,9},{9,1},{17,25},{25,17},{2,10},{10... | collective-permute-start | bytes 786440 | tf_op jit(solution)/shard_map/ppermute | solution.py:22
  84.2 21.6 %collective-permute-start.17 = (bf16[128,1024]{1,0:T(8,128)(2,1)}, bf16[128,1024]{1,0:T(8,128)(2,1)S(1)}, u32[]{:S(2)}, u32[]{:S(2)}) collective-permute-start(bf16[128,1024]{1,0:T(8,128)(2,1)} %fusion.46), channel_id=1, source_target_pairs={{0,16},{8,24},{16,0},{24,8},{1,17},{9,25},{17,1},{25,9},{2,18},{10... | collective-permute-start | bytes 786440 | tf_op jit(solution)/shard_map/ppermute | solution.py:22
  86.7 6.3 %collective-permute-start.14 = (bf16[256,256]{1,0:T(8,128)(2,1)S(1)}, bf16[256,256]{1,0:T(8,128)(2,1)S(1)}, u32[]{:S(2)}, u32[]{:S(2)}) collective-permute-start(bf16[256,256]{1,0:T(8,128)(2,1)S(1)} %dynamic-slice_convert_fusion.5), channel_id=1, source_target_pairs={{0,2},{1,3},{2,0},{3,1},{4,6},{5,7},{6,4},{7,5},{8,10},{9,11},{10,... | collective-permute-start | bytes 393224 | tf_op jit(solution)/shard_map/ppermute | solution.py:22
  92.6 17.0 %copy-start.13 = (f32[512,256]{1,0:T(8,128)S(1)}, f32[512,256]{1,0:T(8,128)}, u32[]{:S(2)}) copy-start(f32[512,256]{1,0:T(8,128)} %copy-done.12) | copy-start | bytes 1572868
  92.6 17.0 %copy-start.15 = (f16[256,256]{1,0:T(8,128)(2,1)S(1)}, f16[256,256]{1,0:T(8,128)(2,1)}, u32[]{:S(2)}) copy-start(f16[256,256]{1,0:T(8,128)(2,1)} %copy-done.14) | copy-start | bytes 393220
  92.6 17.1 %copy-start.21 = (f16[256,256]{1,0:T(8,128)(2,1)S(1)}, f16[256,256]{1,0:T(8,128)(2,1)}, u32[]{:S(2)}) copy-start(f16[256,256]{1,0:T(8,128)(2,1)} %copy-done.20) | copy-start | bytes 393220
  92.7 18.7 %collective-permute-start.19 = (bf16[128,1024]{1,0:T(8,128)(2,1)S(1)}, bf16[128,1024]{1,0:T(8,128)(2,1)S(1)}, u32[]{:S(2)}, u32[]{:S(2)}) collective-permute-start(bf16[128,1024]{1,0:T(8,128)(2,1)S(1)} %fusion.47), channel_id=1, source_target_pairs={{0,16},{8,24},{16,0},{24,8},{1,17},{9,25},{17,1},{25,9},{2,18},{10... | collective-permute-start | bytes 786440 | tf_op jit(solution)/shard_map/ppermute | solution.py:22
  93.0 16.7 %collective-permute-start.16 = (bf16[256,256]{1,0:T(8,128)(2,1)S(1)}, bf16[256,256]{1,0:T(8,128)(2,1)S(1)}, u32[]{:S(2)}, u32[]{:S(2)}) collective-permute-start(bf16[256,256]{1,0:T(8,128)(2,1)S(1)} %fusion.48), channel_id=1, source_target_pairs={{0,4},{1,5},{2,6},{3,7},{4,0},{5,1},{6,2},{7,3},{8,12},{9,13},{10,... | collective-permute-start | bytes 393224 | tf_op jit(solution)/shard_map/ppermute | solution.py:22
  105.9 10.3 %collective-permute-start.21 = (bf16[128,1024]{1,0:T(8,128)(2,1)S(1)}, bf16[128,1024]{1,0:T(8,128)(2,1)S(1)}, u32[]{:S(2)}, u32[]{:S(2)}) collective-permute-start(bf16[128,1024]{1,0:T(8,128)(2,1)S(1)} %add_convert_fusion.1), channel_id=1, source_target_pairs={{0,8},{8,0},{16,24},{24,16},{1,9},{9,1},{17,25},{25,17},{2,10},{10... | collective-permute-start | bytes 786440 | tf_op jit(solution)/shard_map/ppermute | solution.py:22
  109.9 5.0 %collective-permute-start.18 = (bf16[256,256]{1,0:T(8,128)(2,1)S(1)}, bf16[256,256]{1,0:T(8,128)(2,1)S(1)}, u32[]{:S(2)}, u32[]{:S(2)}) collective-permute-start(bf16[256,256]{1,0:T(8,128)(2,1)S(1)} %multiply_convert_fusion.2), channel_id=1, source_target_pairs={{0,2},{1,3},{2,0},{3,1},{4,6},{5,7},{6,4},{7,5},{8,10},{9,11},{10,... | collective-permute-start | bytes 393224 | tf_op jit(solution)/shard_map/ppermute | solution.py:22
  111.6 13.1 %collective-permute-start.23 = (bf16[128,1024]{1,0:T(8,128)(2,1)S(1)}, bf16[128,1024]{1,0:T(8,128)(2,1)S(1)}, u32[]{:S(2)}, u32[]{:S(2)}) collective-permute-start(bf16[128,1024]{1,0:T(8,128)(2,1)S(1)} %add_convert_fusion), channel_id=1, source_target_pairs={{0,8},{8,0},{16,24},{24,16},{1,9},{9,1},{17,25},{25,17},{2,10},{10... | collective-permute-start | bytes 786440 | tf_op jit(solution)/shard_map/ppermute | solution.py:22
  115.0 5.1 %collective-permute-start.20 = (bf16[512,256]{1,0:T(8,128)(2,1)S(1)}, bf16[512,256]{1,0:T(8,128)(2,1)S(1)}, u32[]{:S(2)}, u32[]{:S(2)}) collective-permute-start(bf16[512,256]{1,0:T(8,128)(2,1)S(1)} %pad_maximum_fusion.3), channel_id=1, source_target_pairs={{0,1},{1,0},{2,3},{3,2},{4,5},{5,4},{6,7},{7,6},{8,9},{9,8},{10,11... | collective-permute-start | bytes 786440 | tf_op jit(solution)/shard_map/ppermute | solution.py:22
  121.1 6.4 %collective-permute-start.22 = (bf16[256,256]{1,0:T(8,128)(2,1)S(1)}, bf16[256,256]{1,0:T(8,128)(2,1)S(1)}, u32[]{:S(2)}, u32[]{:S(2)}) collective-permute-start(bf16[256,256]{1,0:T(8,128)(2,1)S(1)} %dynamic-slice_convert_fusion.4), channel_id=1, source_target_pairs={{0,8},{8,0},{16,24},{24,16},{1,9},{9,1},{17,25},{25,17},{2,10},{10... | collective-permute-start | bytes 393224 | tf_op jit(solution)/shard_map/ppermute | solution.py:22
  122.0 7.3 %collective-permute-start.27 = (bf16[256,256]{1,0:T(8,128)(2,1)S(1)}, bf16[256,256]{1,0:T(8,128)(2,1)S(1)}, u32[]{:S(2)}, u32[]{:S(2)}) collective-permute-start(bf16[256,256]{1,0:T(8,128)(2,1)S(1)} %dynamic-slice_convert_fusion.3), channel_id=1, source_target_pairs={{0,8},{8,0},{16,24},{24,16},{1,9},{9,1},{17,25},{25,17},{2,10},{10... | collective-permute-start | bytes 393224 | tf_op jit(solution)/shard_map/ppermute | solution.py:22
  126.3 4.9 %collective-permute-start.26 = (f32[64,2048]{1,0:T(8,128)S(1)}, f32[64,2048]{1,0:T(8,128)S(1)}, u32[]{:S(2)}, u32[]{:S(2)}) collective-permute-start(f32[64,2048]{1,0:T(8,128)S(1)} %constant_dynamic-slice_fusion), channel_id=1, source_target_pairs={{0,1},{1,0},{2,3},{3,2},{4,5},{5,4},{6,7},{7,6},{8,9},{9,8},{10,11... | collective-permute-start | bytes 1572872 | tf_op jit(solution)/shard_map/ppermute | solution.py:22
  126.4 6.4 %collective-permute-start.25 = (f32[64,2048]{1,0:T(8,128)S(1)}, f32[64,2048]{1,0:T(8,128)S(1)}, u32[]{:S(2)}, u32[]{:S(2)}) collective-permute-start(f32[64,2048]{1,0:T(8,128)S(1)} %constant_dynamic-slice_fusion.1), channel_id=1, source_target_pairs={{0,1},{1,0},{2,3},{3,2},{4,5},{5,4},{6,7},{7,6},{8,9},{9,8},{10,11... | collective-permute-start | bytes 1572872 | tf_op jit(solution)/shard_map/ppermute | solution.py:22
  127.6 11.9 %collective-permute-start.24 = (bf16[256,256]{1,0:T(8,128)(2,1)S(1)}, bf16[256,256]{1,0:T(8,128)(2,1)S(1)}, u32[]{:S(2)}, u32[]{:S(2)}) collective-permute-start(bf16[256,256]{1,0:T(8,128)(2,1)S(1)} %add_convert_fusion.9), channel_id=1, source_target_pairs={{0,16},{8,24},{16,0},{24,8},{1,17},{9,25},{17,1},{25,9},{2,18},{10... | collective-permute-start | bytes 393224 | tf_op jit(solution)/shard_map/ppermute | solution.py:22
  129.3 12.6 %collective-permute-start.31 = (bf16[256,256]{1,0:T(8,128)(2,1)S(1)}, bf16[256,256]{1,0:T(8,128)(2,1)S(1)}, u32[]{:S(2)}, u32[]{:S(2)}) collective-permute-start(bf16[256,256]{1,0:T(8,128)(2,1)S(1)} %add_convert_fusion.8), channel_id=1, source_target_pairs={{0,16},{8,24},{16,0},{24,8},{1,17},{9,25},{17,1},{25,9},{2,18},{10... | collective-permute-start | bytes 393224 | tf_op jit(solution)/shard_map/ppermute | solution.py:22
  131.3 10.7 %collective-permute-start.30 = (bf16[32,2048]{1,0:T(8,128)(2,1)S(1)}, bf16[32,2048]{1,0:T(8,128)(2,1)S(1)}, u32[]{:S(2)}, u32[]{:S(2)}) collective-permute-start(bf16[32,2048]{1,0:T(8,128)(2,1)S(1)} %dynamic-slice_convert_fusion.2), channel_id=1, source_target_pairs={{0,2},{1,3},{2,0},{3,1},{4,6},{5,7},{6,4},{7,5},{8,10},{9,11},{10,... | collective-permute-start | bytes 393224 | tf_op jit(solution)/shard_map/ppermute | solution.py:22
  133.0 10.7 %collective-permute-start.29 = (bf16[32,2048]{1,0:T(8,128)(2,1)S(1)}, bf16[32,2048]{1,0:T(8,128)(2,1)S(1)}, u32[]{:S(2)}, u32[]{:S(2)}) collective-permute-start(bf16[32,2048]{1,0:T(8,128)(2,1)S(1)} %dynamic-slice_convert_fusion.1), channel_id=1, source_target_pairs={{0,4},{1,5},{2,6},{3,7},{4,0},{5,1},{6,2},{7,3},{8,12},{9,13},{10,... | collective-permute-start | bytes 393224 | tf_op jit(solution)/shard_map/ppermute | solution.py:22
  139.5 5.7 %collective-permute-start.28 = (bf16[256,256]{1,0:T(8,128)(2,1)S(1)}, bf16[256,256]{1,0:T(8,128)(2,1)S(1)}, u32[]{:S(2)}, u32[]{:S(2)}) collective-permute-start(bf16[256,256]{1,0:T(8,128)(2,1)S(1)} %add_convert_fusion.7), channel_id=1, source_target_pairs={{0,8},{8,0},{16,24},{24,16},{1,9},{9,1},{17,25},{25,17},{2,10},{10... | collective-permute-start | bytes 393224 | tf_op jit(solution)/shard_map/ppermute | solution.py:22
  141.9 5.5 %collective-permute-start.32 = (bf16[256,256]{1,0:T(8,128)(2,1)S(1)}, bf16[256,256]{1,0:T(8,128)(2,1)S(1)}, u32[]{:S(2)}, u32[]{:S(2)}) collective-permute-start(bf16[256,256]{1,0:T(8,128)(2,1)S(1)} %add_convert_fusion.6), channel_id=1, source_target_pairs={{0,8},{8,0},{16,24},{24,16},{1,9},{9,1},{17,25},{25,17},{2,10},{10... | collective-permute-start | bytes 393224 | tf_op jit(solution)/shard_map/ppermute | solution.py:22
  142.1 5.4 %collective-permute-start.33 = (bf16[32,2048]{1,0:T(8,128)(2,1)S(1)}, bf16[32,2048]{1,0:T(8,128)(2,1)S(1)}, u32[]{:S(2)}, u32[]{:S(2)}) collective-permute-start(bf16[32,2048]{1,0:T(8,128)(2,1)S(1)} %add_convert_fusion.5), channel_id=1, source_target_pairs={{0,4},{1,5},{2,6},{3,7},{4,0},{5,1},{6,2},{7,3},{8,12},{9,13},{10,... | collective-permute-start | bytes 393224 | tf_op jit(solution)/shard_map/ppermute | solution.py:22
  143.7 5.4 %collective-permute-start.35 = (bf16[32,2048]{1,0:T(8,128)(2,1)S(1)}, bf16[32,2048]{1,0:T(8,128)(2,1)S(1)}, u32[]{:S(2)}, u32[]{:S(2)}) collective-permute-start(bf16[32,2048]{1,0:T(8,128)(2,1)S(1)} %add_convert_fusion.4), channel_id=1, source_target_pairs={{0,2},{1,3},{2,0},{3,1},{4,6},{5,7},{6,4},{7,5},{8,10},{9,11},{10,... | collective-permute-start | bytes 393224 | tf_op jit(solution)/shard_map/ppermute | solution.py:22
  147.5 5.0 %collective-permute-start.34 = (bf16[32,2048]{1,0:T(8,128)(2,1)S(1)}, bf16[32,2048]{1,0:T(8,128)(2,1)S(1)}, u32[]{:S(2)}, u32[]{:S(2)}) collective-permute-start(bf16[32,2048]{1,0:T(8,128)(2,1)S(1)} %add_convert_fusion.3), channel_id=1, source_target_pairs={{0,2},{1,3},{2,0},{3,1},{4,6},{5,7},{6,4},{7,5},{8,10},{9,11},{10,... | collective-permute-start | bytes 393224 | tf_op jit(solution)/shard_map/ppermute | solution.py:22
  149.1 5.0 %collective-permute-start.37 = (bf16[32,2048]{1,0:T(8,128)(2,1)S(1)}, bf16[32,2048]{1,0:T(8,128)(2,1)S(1)}, u32[]{:S(2)}, u32[]{:S(2)}) collective-permute-start(bf16[32,2048]{1,0:T(8,128)(2,1)S(1)} %add_convert_fusion.2), channel_id=1, source_target_pairs={{0,4},{1,5},{2,6},{3,7},{4,0},{5,1},{6,2},{7,3},{8,12},{9,13},{10,... | collective-permute-start | bytes 393224 | tf_op jit(solution)/shard_map/ppermute | solution.py:22
  152.6 2.8 %collective-permute-start.36 = (bf16[64,2048]{1,0:T(8,128)(2,1)S(1)}, bf16[64,2048]{1,0:T(8,128)(2,1)S(1)}, u32[]{:S(2)}, u32[]{:S(2)}) collective-permute-start(bf16[64,2048]{1,0:T(8,128)(2,1)S(1)} %pad_maximum_fusion.4), channel_id=1, source_target_pairs={{0,1},{1,0},{2,3},{3,2},{4,5},{5,4},{6,7},{7,6},{8,9},{9,8},{10,11... | collective-permute-start | bytes 786440 | tf_op jit(solution)/shard_map/ppermute | solution.py:22
  154.2 1.6 %collective-permute-start.38 = (bf16[64,2048]{1,0:T(8,128)(2,1)S(1)}, bf16[64,2048]{1,0:T(8,128)(2,1)S(1)}, u32[]{:S(2)}, u32[]{:S(2)}) collective-permute-start(bf16[64,2048]{1,0:T(8,128)(2,1)S(1)} %pad_maximum_fusion.5), channel_id=1, source_target_pairs={{0,1},{1,0},{2,3},{3,2},{4,5},{5,4},{6,7},{7,6},{8,9},{9,8},{10,11... | collective-permute-start | bytes 786440 | tf_op jit(solution)/shard_map/ppermute | solution.py:22
  (22 other events, 126.2 us)

commit v8 on v7

--- a/solution.py
+++ b/solution.py
@@ -105,7 +105,7 @@
         out_specs=[row_spec(block, 1)] * 2,
         out_shape=[jax.ShapeDtypeStruct((rows, 1), F32)] * 2,
         scratch_shapes=[pltpu.VMEM((block + 8, cols), F32)],
-        compiler_params=params(50),
+        compiler_params=params(24),
         cost_estimate=cost(4 * rows * cols, 4 * rows * cols, rows * cols),
         name="target_sums",
     )(target, target, incoming)
@@ -143,7 +143,7 @@
             jax.ShapeDtypeStruct((rows, 1), F32),
         ],
         scratch_shapes=[pltpu.VMEM((block + 8, cols), F32)],
-        compiler_params=params(50),
+        compiler_params=params(24),
         cost_estimate=cost(6 * rows * cols, 8 * rows * cols, rows * cols),
         name="target_pass",
     )(target, target, incoming)
@@ -181,7 +181,7 @@
             jax.ShapeDtypeStruct((rows, 1), F32),
         ],
         scratch_shapes=[pltpu.VMEM((block + 8, cols), F32)],
-        compiler_params=params(50),
+        compiler_params=params(24),
         cost_estimate=cost(6 * rows * cols, 8 * rows * cols, rows * cols),
         name="target_probs",
     )(target, target, incoming, top, total)
@@ -435,15 +435,16 @@
     mine = own_bit("grp", z_bits[0])
     up_away, up_kept = half(up_weight, 1 - mine), half(up_weight, mine)
     vocab_pieces = [[] for c in chunks]
-    vocab = []
+    vocab, sent = [], []
     for c in chunks:
         away, kept = [
             jnp.dot(part, columns(c), preferred_element_type=F32) * VOCAB_SCALE
             for part in (up_away, up_kept)
         ]
+        sent.append(away.astype(F16))
         vocab.append(
             summed(
-                line, (away, kept), "grp", z_bits, [F16] * len(z_bits),
+                line, (sent[c], kept), "grp", z_bits, [F16] * len(z_bits),
                 lambda total: (total * (1.0 / VOCAB_SCALE)).astype(BF16), vocab_pieces[c],
             )
         )
@@ -451,7 +452,6 @@
     devices = range(group_count)
     top_rows = line.put(line.after(target_logits[:8]))
     incoming = lax.ppermute(top_rows, "grp", [(i + 1, i) for i in devices if i + 1 in devices])
-    vocab[1].step()
     pre_part = line.put(
         jnp.dot(line.after(hidden_states), down_weight, preferred_element_type=F32)
     )
@@ -465,8 +465,10 @@
         line, pre_part * PRE_SCALE, v_bits, [F16] * len(v_bits), activate
     )
     pre.step()
+    line.put(sent[1])
     incoming = line.put(line.after(incoming))
     vocab[0].step()
+    vocab[1].step()
     pre.step()
     vocab[1].step()
     pre.step()
@@ -480,9 +482,9 @@
     line.put(entropy)
     label = lax.dynamic_slice_in_dim(labels, book_index, 1, 1) - book_part * slice_cols
     pre.step()
+    vocab[1].step()
     vocab[0].result()
     line.put(vocab_pieces[0][1])
-    vocab[1].step()
     pre.step()
     acts = line.put(all_acts())
 
@@ -519,10 +521,6 @@
     act.step()
     grads[1].step()
     act.step()
-    loss = over_books(loss + entropy, jnp.add, per_book)
-    frame_loss = lax.dynamic_slice_in_dim(loss, book_part * block_rows, block_rows, 0)
-    frame_loss = frame_loss.reshape(1, 1, block_rows)
-
     def times_head(before, piece, c):
         return line.put(before + inner_cols(line.after(piece), columns(c)))
 
@@ -556,8 +554,12 @@
         )
         for part, bits in ((up_part[:rank], v_bits), (up_part[rank:], v_other))
     ]
-    for _ in range(2 * len(v_bits)):
-        for chain in (ups[0][0], ups[1][0], downs[0], downs[1]):
+    swaps = [chain for chain, _ in ups]
+    loss = over_books(line.after(loss) + entropy, jnp.add, per_book)
+    frame_loss = lax.dynamic_slice_in_dim(loss, book_part * block_rows, block_rows, 0)
+    frame_loss = frame_loss.reshape(1, 1, block_rows)
+    for turn in (swaps, downs, swaps, swaps, swaps, downs, swaps):
+        for chain in turn:
             chain.step()
     grad_b = jnp.concatenate([result().astype(F32) for _, result in ups], 0)
     for chain in downs:

time: 158 us -> 152 us (0.962)
  Pallas kernels: 24 us -> 18.8 us
  local copies, waits for them, and re-layouts: 8.2 us -> 12.9 us
  other arithmetic: 14 us -> 10.1 us
  waiting for transfers between devices: 39.3 us -> 37.4 us
    pallas_call x1, Pallas kernels: 9.17 us -> 4.03 us  [target_pass(): pl.pallas_call(body, grid=(rows // block,), in_specs=[row_spec(block, col...]
    unnamed x63 -> x59, local copies, waits for them, and re-layouts: 5.47 us -> 10.1 us
    ppermute x38, waiting for transfers between devices: 39.3 us -> 37.4 us  [swap(): return lax.ppermute(value, axis, pairs)]
  transfers between devices with their start and end apart: 39 -> 39, of which waited for: 18 -> 17; matrix products, arithmetic and copies ran while one was open for 24% -> 23% of each run, Pallas kernels for 10% -> 7%
where the time goes in v8:
time: 152 us; the launch traced here: 151 us
  starting transfers between devices  43.6 us (29%)
  waiting for transfers between devices  37.4 us (25%)
  matrix products  27.1 us (18%)
  Pallas kernels  18.8 us (12%)
  local copies, waits for them, and re-layouts  12.9 us (8%)
  other arithmetic  10.1 us (7%)
    ppermute x38, starting transfers between devices, swap(): return lax.ppermute(value, axis, pairs)  42.3 us
    ppermute x38, waiting for transfers between devices, swap(): return lax.ppermute(value, axis, pairs)  37.4 us
    dot_general x4, matrix products, on_device(): jnp.dot(part, columns(c), preferred_element_type=F32) * VOCAB_SCALE  13.9 us
    dot_general x4, matrix products, inner_cols(): lax.dot_general(left, right, (((1,), (1,)), ((), ())), preferred_element_...  10.6 us
    unnamed x59, local copies, waits for them, and re-layouts  10.1 us
    pallas_call x2, Pallas kernels, grad_chunk(): pl.pallas_call(body, grid=(rows // block,), in_specs=[row_spec(block, wid...  8.26 us
    pallas_call x2, Pallas kernels, draft_chunk(): pl.pallas_call(body, grid=(rows // block,), in_specs=[row_spec(block, wid...  6.55 us
    pallas_call x1, Pallas kernels, target_pass(): pl.pallas_call(body, grid=(rows // block,), in_specs=[row_spec(block, col...  4.03 us
  transfers between devices with their start and end apart: 39, of which 17 were waited for; matrix products, arithmetic and copies ran while one was open for 23% of the time, Pallas kernels for 7%

profile of v8, /device:TPU:0, one launch (start us, length us, event | category | flops | bytes accessed | tf_op | source)
XLA Modules:
  0.0 151.3 jit_solution(9724220928450411124)
XLA Ops:
  0.7 3.9 %fusion.37 = f16[128,1024]{1,0:T(8,128)(2,1)} fusion(bf16[2048,2048]{1,0:T(8,128)(2,1)} %param.11, bf16[256,2048]{1,0:T(8,128)(2,1)} %param.10, s32[]{:T(128)S(6)} %select_n.175), kind=kOutput, calls=%fused_computation.23 | convolution fusion | flops 537133056 | bytes 4980740 | tf_op jit(solution)/shard_map/dot_general | solution.py:441
  4.6 3.0 %collective-permute-start.1 = (f16[128,1024]{1,0:T(8,128)(2,1)}, f16[128,1024]{1,0:T(8,128)(2,1)S(1)}, u32[]{:S(2)}, u32[]{:S(2)}) collective-permute-start(f16[128,1024]{1,0:T(8,128)(2,1)} %fusion.37), channel_id=1, source_target_pairs={{0,8},{8,0},{16,24},{24,16},{1,9},{9,1},{17,25},{25,17},{2,10},{10... | collective-permute-start | bytes 786440 | tf_op jit(solution)/shard_map/ppermute | solution.py:22
  8.4 1.3 collective-permute-start.2
  9.7 1.8 %broadcast_multiply_fusion = f32[1024,256]{1,0:T(8,128)S(1)} fusion(bf16[1024,1024]{1,0:T(8,128)(2,1)S(1)} %copy-done, bf16[1024,256]{1,0:T(8,128)(2,1)} %param.9), kind=kOutput, calls=%fused_computation.42 | convolution fusion | flops 537133056 | bytes 3670016 | tf_op jit(solution)/shard_map/dot_general | solution.py:456
  12.3 3.8 %fusion.34 = f16[128,1024]{1,0:T(8,128)(2,1)} fusion(bf16[2048,2048]{1,0:T(8,128)(2,1)} %param.11, bf16[256,2048]{1,0:T(8,128)(2,1)} %param.10, s32[]{:T(128)S(6)} %select_n.175), kind=kOutput, calls=%fused_computation.22 | convolution fusion | flops 537133056 | bytes 4980740 | tf_op jit(solution)/shard_map/dot_general | solution.py:441
  16.1 3.3 %fusion.44 = (f16[128,1024]{1,0:T(8,128)(2,1)S(1)}, f32[128,1024]{1,0:T(8,128)S(1)}) fusion(f16[128,1024]{1,0:T(8,128)(2,1)S(1)} %collective-permute-done.1, bf16[2048,2048]{1,0:T(8,128)(2,1)} %param.11, bf16[256,2048]{1,0:T(8,128)(2,1)} %param.10, s32[]{:T(128)S(6)} %select_n.178), kind=kOutput, calls=%fused_computation.49 | convolution fusion | flops 537395200 | bytes 5767172 | tf_op jit(solution)/shard_map/dot_general | solution.py:441
  19.3 3.3 %collective-permute-start.6 = (f16[128,1024]{1,0:T(8,128)(2,1)S(1)}, f16[128,1024]{1,0:T(8,128)(2,1)S(1)}, u32[]{:S(2)}, u32[]{:S(2)}) collective-permute-start(f16[128,1024]{1,0:T(8,128)(2,1)S(1)} %get-tuple-element.111), channel_id=1, source_target_pairs={{0,16},{8,24},{16,0},{24,8},{1,17},{9,25},{17,1},{25,9},{2,18},{10... | collective-permute-start | bytes 786440 | tf_op jit(solution)/shard_map/ppermute | solution.py:22
  22.6 2.0 %collective-permute-start.4 = (f16[128,1024]{1,0:T(8,128)(2,1)S(1)}, f16[128,1024]{1,0:T(8,128)(2,1)S(1)}, u32[]{:S(2)}, u32[]{:S(2)}) collective-permute-start(f16[128,1024]{1,0:T(8,128)(2,1)S(1)} %copy-done.22), channel_id=1, source_target_pairs={{0,8},{8,0},{16,24},{24,16},{1,9},{9,1},{17,25},{25,17},{2,10},{10... | collective-permute-start | bytes 786440 | tf_op jit(solution)/shard_map/ppermute | solution.py:22
  25.7 1.6 %collective-permute-start.3 = (f16[256,256]{1,0:T(8,128)(2,1)S(1)}, f16[256,256]{1,0:T(8,128)(2,1)S(1)}, u32[]{:S(2)}, u32[]{:S(2)}) collective-permute-start(f16[256,256]{1,0:T(8,128)(2,1)S(1)} %dynamic-slice_convert_fusion.6), channel_id=1, source_target_pairs={{0,2},{1,3},{2,0},{3,1},{4,6},{5,7},{6,4},{7,5},{8,10},{9,11},{10,... | collective-permute-start | bytes 393224 | tf_op jit(solution)/shard_map/ppermute | solution.py:22
  27.3 8.1 %collective-permute-done.4 = f16[128,1024]{1,0:T(8,128)(2,1)S(1)} collective-permute-done((f16[128,1024]{1,0:T(8,128)(2,1)S(1)}, f16[128,1024]{1,0:T(8,128)(2,1)S(1)}, u32[]{:S(2)}, u32[]{:S(2)}) %collective-permute-start.4) | collective-permute-done | bytes 262176 | tf_op jit(solution)/shard_map/ppermute | solution.py:22
  35.4 3.0 %fusion.45 = (f16[128,1024]{1,0:T(8,128)(2,1)S(1)}, f32[128,1024]{1,0:T(8,128)S(1)}) fusion(f16[128,1024]{1,0:T(8,128)(2,1)S(1)} %collective-permute-done.4, bf16[2048,2048]{1,0:T(8,128)(2,1)} %param.11, bf16[256,2048]{1,0:T(8,128)(2,1)S(1)} %copy-done.21, s32[]{:T(128)S(6)} %select_n.178), kind=kOutput, calls=%fused_computation.50 | convolution fusion | flops 537395200 | bytes 5767172 | tf_op jit(solution)/shard_map/dot_general | solution.py:441
  38.3 2.0 %collective-permute-start.9 = (f16[128,1024]{1,0:T(8,128)(2,1)S(1)}, f16[128,1024]{1,0:T(8,128)(2,1)S(1)}, u32[]{:S(2)}, u32[]{:S(2)}) collective-permute-start(f16[128,1024]{1,0:T(8,128)(2,1)S(1)} %get-tuple-element.116), channel_id=1, source_target_pairs={{0,16},{8,24},{16,0},{24,8},{1,17},{9,25},{17,1},{25,9},{2,18},{10... | collective-permute-start | bytes 786440 | tf_op jit(solution)/shard_map/ppermute | solution.py:22
  40.4 1.6 %collective-permute-start.5 = (f16[256,256]{1,0:T(8,128)(2,1)S(1)}, f16[256,256]{1,0:T(8,128)(2,1)S(1)}, u32[]{:S(2)}, u32[]{:S(2)}) collective-permute-start(f16[256,256]{1,0:T(8,128)(2,1)S(1)} %fusion.49), channel_id=1, source_target_pairs={{0,4},{1,5},{2,6},{3,7},{4,0},{5,1},{6,2},{7,3},{8,12},{9,13},{10,... | collective-permute-start | bytes 393224 | tf_op jit(solution)/shard_map/ppermute | solution.py:22
  42.3 4.0 %target_pass.1 = (f32[1024,2048]{1,0:T(8,128)S(1)}, f32[1024,1]{1,0:T(8,128)S(1)}) custom-call(f32[1024,2048]{1,0:T(8,128)S(1)} %bitcast.9, f32[1024,2048]{1,0:T(8,128)S(1)} %bitcast.9, f32[8,2048]{1,0:T(8,128)S(1)} %collective-permute-done.2.incoming_ref), custom_call_target="tpu_custom_call" | custom-call | flops 3072 | bytes 4096 | tf_op jit(solution)/shard_map/target_pass/pallas_call | solution.py:132
  46.3 3.4 %copy-done.2 = f32[1024,2048]{1,0:T(8,128)} copy-done((f32[1024,2048]{1,0:T(8,128)}, f32[1024,2048]{1,0:T(8,128)S(1)}, u32[]{:S(2)}) %copy-start.2) | copy-done | bytes 8388632
  49.8 1.6 %collective-permute-start.7 = (bf16[256,256]{1,0:T(8,128)(2,1)S(1)}, bf16[256,256]{1,0:T(8,128)(2,1)S(1)}, u32[]{:S(2)}, u32[]{:S(2)}) collective-permute-start(bf16[256,256]{1,0:T(8,128)(2,1)S(1)} %multiply_convert_fusion.3), channel_id=1, source_target_pairs={{0,2},{1,3},{2,0},{3,1},{4,6},{5,7},{6,4},{7,5},{8,10},{9,11},{10,... | collective-permute-start | bytes 393224 | tf_op jit(solution)/shard_map/ppermute | solution.py:22
  55.8 2.0 %collective-permute-start.11 = (bf16[128,1024]{1,0:T(8,128)(2,1)}, bf16[128,1024]{1,0:T(8,128)(2,1)}, u32[]{:S(2)}, u32[]{:S(2)}) collective-permute-start(bf16[128,1024]{1,0:T(8,128)(2,1)} %multiply_convert_fusion.own_ref), channel_id=1, source_target_pairs={{0,8},{8,0},{16,24},{24,16},{1,9},{9,1},{17,25},{25,17},{2,10},{10... | collective-permute-start | bytes 786440 | tf_op jit(solution)/shard_map/ppermute | solution.py:22
  58.1 3.4 %copy-done.1 = f32[1024,2048]{1,0:T(8,128)S(1)} copy-done((f32[1024,2048]{1,0:T(8,128)S(1)}, f32[1024,2048]{1,0:T(8,128)}, u32[]{:S(2)}) %copy-start.1) | copy-done | bytes 8388632
  62.4 2.5 %draft_chunk.2 = (f32[1024,1024]{1,0:T(8,128)S(1)}, bf16[256,1024]{1,0:T(8,128)(2,1)S(1)}, f32[1024,1]{1,0:T(8,128)S(1)}, f32[1024,1]{1,0:T(8,128)S(1)}) custom-call(f32[1024,2048]{1,0:T(8,128)S(1)} %copy-done.1, bf16[1024,256]{1,0:T(8,128)(2,1)S(1)} %pad_maximum_fusion.acts_ref, bf16[128,1024]{1,0:T(8,128)(2,1)S(1)} %multiply_convert_fusion.1.own_ref, ...), custom_call_target="tpu_custom_call" | custom-call | flops 131072 | bytes 2048 | tf_op jit(solution)/shard_map/draft_chunk/pallas_call | solution.py:220
  65.0 4.0 %draft_chunk.3 = (f32[1024,1024]{1,0:T(8,128)S(1)}, bf16[256,1024]{1,0:T(8,128)(2,1)S(1)}, f32[1024,1]{1,0:T(8,128)S(1)}, f32[1024,1]{1,0:T(8,128)S(1)}) custom-call(f32[1024,2048]{1,0:T(8,128)S(1)} %copy-done.1, bf16[1024,256]{1,0:T(8,128)(2,1)S(1)} %pad_maximum_fusion.acts_ref, bf16[128,1024]{1,0:T(8,128)(2,1)} %multiply_convert_fusion.own_ref, ...), custom_call_target="tpu_custom_call" | custom-call | flops 131072 | bytes 2048 | tf_op jit(solution)/shard_map/draft_chunk/pallas_call | solution.py:220
  69.1 4.1 %grad_chunk.2 = (bf16[128,1024]{1,0:T(8,128)(2,1)S(1)}, f32[128,1024]{1,0:T(8,128)S(1)}, f32[1024,256]{1,0:T(8,128)S(1)}, f32[1024,1]{1,0:T(8,128)S(1)}) custom-call(f32[1024,1024]{1,0:T(8,128)S(1)} %get-tuple-element.136.draft_ref, f32[1024,2048]{1,0:T(8,128)S(1)} %bitcast.11, s32[1024,1]{1,0:T(8,128)S(1)} %copy.11.label_ref, ...), custom_call_target="tpu_custom_call" | custom-call | flops 262144 | bytes 2048 | tf_op jit(solution)/shard_map/grad_chunk/pallas_call | solution.py:292
  73.2 1.8 %collective-permute-start.12 = (bf16[128,1024]{1,0:T(8,128)(2,1)S(1)}, bf16[128,1024]{1,0:T(8,128)(2,1)S(1)}, u32[]{:S(2)}, u32[]{:S(2)}) collective-permute-start(bf16[128,1024]{1,0:T(8,128)(2,1)S(1)} %get-tuple-element.141), channel_id=1, source_target_pairs={{0,8},{8,0},{16,24},{24,16},{1,9},{9,1},{17,25},{25,17},{2,10},{10... | collective-permute-start | bytes 786440 | tf_op jit(solution)/shard_map/ppermute | solution.py:22
  75.0 4.2 %grad_chunk.3 = (bf16[128,1024]{1,0:T(8,128)(2,1)S(1)}, f32[128,1024]{1,0:T(8,128)S(1)}, f32[1024,256]{1,0:T(8,128)S(1)}, f32[1024,1]{1,0:T(8,128)S(1)}) custom-call(f32[1024,1024]{1,0:T(8,128)S(1)} %get-tuple-element.142.draft_ref, f32[1024,2048]{1,0:T(8,128)S(1)} %bitcast.11, s32[1024,1]{1,0:T(8,128)S(1)} %copy.11.label_ref, ...), custom_call_target="tpu_custom_call" | custom-call | flops 262144 | bytes 2048 | tf_op jit(solution)/shard_map/grad_chunk/pallas_call | solution.py:292
  83.6 1.4 collective-permute-start.13
  86.1 1.6 %collective-permute-start.15 = (bf16[256,256]{1,0:T(8,128)(2,1)S(1)}, bf16[256,256]{1,0:T(8,128)(2,1)S(1)}, u32[]{:S(2)}, u32[]{:S(2)}) collective-permute-start(bf16[256,256]{1,0:T(8,128)(2,1)S(1)} %dynamic-slice_convert_fusion.5), channel_id=1, source_target_pairs={{0,2},{1,3},{2,0},{3,1},{4,6},{5,7},{6,4},{7,5},{8,10},{9,11},{10,... | collective-permute-start | bytes 393224 | tf_op jit(solution)/shard_map/ppermute | solution.py:22
  87.7 8.9 %collective-permute-done.16 = bf16[128,1024]{1,0:T(8,128)(2,1)S(1)} collective-permute-done((bf16[128,1024]{1,0:T(8,128)(2,1)}, bf16[128,1024]{1,0:T(8,128)(2,1)S(1)}, u32[]{:S(2)}, u32[]{:S(2)}) %collective-permute-start.16) | collective-permute-done | bytes 262176 | tf_op jit(solution)/shard_map/ppermute | solution.py:22
  97.4 1.3 collective-permute-done.13
  101.0 3.7 %fusion.10 = f32[128,2048]{1,0:T(8,128)S(1)} fusion(bf16[128,1024]{1,0:T(8,128)(2,1)S(1)} %add_convert_fusion.1, bf16[2048,2048]{1,0:T(8,128)(2,1)} %param.11), kind=kOutput, calls=%fused_computation.10 | convolution fusion | flops 536870912 | bytes 5505024 | tf_op jit(solution)/shard_map/dot_general | solution.py:44
  104.9 1.6 %collective-permute-start.19 = (bf16[256,256]{1,0:T(8,128)(2,1)S(1)}, bf16[256,256]{1,0:T(8,128)(2,1)S(1)}, u32[]{:S(2)}, u32[]{:S(2)}) collective-permute-start(bf16[256,256]{1,0:T(8,128)(2,1)S(1)} %multiply_convert_fusion.2), channel_id=1, source_target_pairs={{0,2},{1,3},{2,0},{3,1},{4,6},{5,7},{6,4},{7,5},{8,10},{9,11},{10,... | collective-permute-start | bytes 393224 | tf_op jit(solution)/shard_map/ppermute | solution.py:22
  106.5 3.9 %collective-permute-done.20 = bf16[128,1024]{1,0:T(8,128)(2,1)S(1)} collective-permute-done((bf16[128,1024]{1,0:T(8,128)(2,1)S(1)}, bf16[128,1024]{1,0:T(8,128)(2,1)S(1)}, u32[]{:S(2)}, u32[]{:S(2)}) %collective-permute-start.20) | collective-permute-done | bytes 262176 | tf_op jit(solution)/shard_map/ppermute | solution.py:22
  110.8 1.4 collective-permute-done.17
  112.1 3.8 %fusion.8 = f32[128,2048]{1,0:T(8,128)S(1)} fusion(bf16[128,1024]{1,0:T(8,128)(2,1)S(1)} %collective-permute-done.17, bf16[2048,2048]{1,0:T(8,128)(2,1)} %param.11), kind=kOutput, calls=%fused_computation.8 | convolution fusion | flops 536870912 | bytes 5505024 | tf_op jit(solution)/shard_map/dot_general | solution.py:44
  117.7 1.4 collective-permute-start.27
  119.1 1.5 %fusion.16 = f32[128,2048]{1,0:T(8,128)S(1)} fusion(f32[128,2048]{1,0:T(8,128)S(1)} %fusion.10, bf16[128,1024]{1,0:T(8,128)(2,1)S(1)} %add_convert_fusion, bf16[2048,2048]{1,0:T(8,128)(2,1)S(1)} %bitcast.13), kind=kOutput, calls=%fused_computation.16 | convolution fusion | flops 537133056 | bytes 6553600 | tf_op jit(solution)/shard_map/dot_general | solution.py:44
  120.7 1.5 %broadcast_select_fusion = (f32[128,2048]{1,0:T(8,128)S(1)}, f32[128,2048]{1,0:T(8,128)S(1)}) fusion(f32[128,2048]{1,0:T(8,128)S(1)} %fusion.16, pred[]{:T(512)S(6)} %eq.12, f32[128,2048]{1,0:T(8,128)S(1)} %fusion.8, bf16[128,1024]{1,0:T(8,128)(2,1)S(1)} %collective-permute-done.21, bf16[2048,2048]{1,0:T(8,128)(2,1)S(1)} %bitcast.13), kind=kOutput, calls=%fused_computation.43 | convolution fusion | flops 537657344 | bytes 8650753 | tf_op jit(solution)/shard_map/dot_general | solution.py:44
  123.8 1.3 collective-permute-start.24
  125.2 1.9 %collective-permute-start.35 = (bf16[256,256]{1,0:T(8,128)(2,1)S(1)}, bf16[256,256]{1,0:T(8,128)(2,1)S(1)}, u32[]{:S(2)}, u32[]{:S(2)}) collective-permute-start(bf16[256,256]{1,0:T(8,128)(2,1)S(1)} %add_convert_fusion.8), channel_id=1, source_target_pairs={{0,16},{8,24},{16,0},{24,8},{1,17},{9,25},{17,1},{25,9},{2,18},{10... | collective-permute-start | bytes 393224 | tf_op jit(solution)/shard_map/ppermute | solution.py:22
  127.2 1.6 %collective-permute-start.29 = (bf16[32,2048]{1,0:T(8,128)(2,1)S(1)}, bf16[32,2048]{1,0:T(8,128)(2,1)S(1)}, u32[]{:S(2)}, u32[]{:S(2)}) collective-permute-start(bf16[32,2048]{1,0:T(8,128)(2,1)S(1)} %dynamic-slice_convert_fusion.2), channel_id=1, source_target_pairs={{0,2},{1,3},{2,0},{3,1},{4,6},{5,7},{6,4},{7,5},{8,10},{9,11},{10,... | collective-permute-start | bytes 393224 | tf_op jit(solution)/shard_map/ppermute | solution.py:22
  128.9 1.4 collective-permute-start.28
  130.3 2.0 %collective-permute-done.29 = bf16[32,2048]{1,0:T(8,128)(2,1)S(1)} collective-permute-done((bf16[32,2048]{1,0:T(8,128)(2,1)S(1)}, bf16[32,2048]{1,0:T(8,128)(2,1)S(1)}, u32[]{:S(2)}, u32[]{:S(2)}) %collective-permute-start.29) | collective-permute-done | bytes 131104 | tf_op jit(solution)/shard_map/ppermute | solution.py:22
  132.3 1.4 collective-permute-start.31
  135.3 2.1 %collective-permute-done.31 = bf16[32,2048]{1,0:T(8,128)(2,1)S(1)} collective-permute-done((bf16[32,2048]{1,0:T(8,128)(2,1)S(1)}, bf16[32,2048]{1,0:T(8,128)(2,1)S(1)}, u32[]{:S(2)}, u32[]{:S(2)}) %collective-permute-start.31) | collective-permute-done | bytes 131104 | tf_op jit(solution)/shard_map/ppermute | solution.py:22
  137.4 1.6 %collective-permute-start.34 = (bf16[32,2048]{1,0:T(8,128)(2,1)S(1)}, bf16[32,2048]{1,0:T(8,128)(2,1)S(1)}, u32[]{:S(2)}, u32[]{:S(2)}) collective-permute-start(bf16[32,2048]{1,0:T(8,128)(2,1)S(1)} %add_convert_fusion.5), channel_id=1, source_target_pairs={{0,2},{1,3},{2,0},{3,1},{4,6},{5,7},{6,4},{7,5},{8,10},{9,11},{10,... | collective-permute-start | bytes 393224 | tf_op jit(solution)/shard_map/ppermute | solution.py:22
  138.9 2.0 %collective-permute-done.30 = bf16[32,2048]{1,0:T(8,128)(2,1)S(1)} collective-permute-done((bf16[32,2048]{1,0:T(8,128)(2,1)S(1)}, bf16[32,2048]{1,0:T(8,128)(2,1)S(1)}, u32[]{:S(2)}, u32[]{:S(2)}) %collective-permute-start.30) | collective-permute-done | bytes 131104 | tf_op jit(solution)/shard_map/ppermute | solution.py:22
  142.3 1.9 %collective-permute-start.36 = (bf16[256,256]{1,0:T(8,128)(2,1)S(1)}, bf16[256,256]{1,0:T(8,128)(2,1)S(1)}, u32[]{:S(2)}, u32[]{:S(2)}) collective-permute-start(bf16[256,256]{1,0:T(8,128)(2,1)S(1)} %add_convert_fusion.2), channel_id=1, source_target_pairs={{0,8},{8,0},{16,24},{24,16},{1,9},{9,1},{17,25},{25,17},{2,10},{10... | collective-permute-start | bytes 393224 | tf_op jit(solution)/shard_map/ppermute | solution.py:22
  144.3 1.7 %collective-permute-done.33 = bf16[32,2048]{1,0:T(8,128)(2,1)S(1)} collective-permute-done((bf16[32,2048]{1,0:T(8,128)(2,1)S(1)}, bf16[32,2048]{1,0:T(8,128)(2,1)S(1)}, u32[]{:S(2)}, u32[]{:S(2)}) %collective-permute-start.33) | collective-permute-done | bytes 131104 | tf_op jit(solution)/shard_map/ppermute | solution.py:22
  147.0 1.4 collective-permute-done.36
  149.7 1.6 %maximum_convert_fusion = f32[256,2048]{1,0:T(8,128)} fusion(bf16[64,2048]{1,0:T(8,128)(2,1)S(1)} %get-tuple-element.216, bf16[64,2048]{1,0:T(8,128)(2,1)S(1)} %get-tuple-element.215, bf16[64,2048]{1,0:T(8,128)(2,1)S(1)} %get-tuple-element.240, bf16[64,2048]{1,0:T(8,128)(2,1)S(1)} %get-tuple-element.241), kind=kLoop, calls=%fused_computation.24 | loop fusion | flops 4194304 | bytes 3145728 | tf_op jit(solution)/shard_map/concatenate | solution.py:564
  (158 shorter events, 26.7 us)
Async XLA Ops:
  0.6 9.1 %copy-start = (bf16[1024,1024]{1,0:T(8,128)(2,1)S(1)}, bf16[1024,1024]{1,0:T(8,128)(2,1)}, u32[]{:S(2)}) copy-start(bf16[1024,1024]{1,0:T(8,128)(2,1)} %param.6) | copy-start | bytes 6291460
  4.6 11.5 %collective-permute-start.1 = (f16[128,1024]{1,0:T(8,128)(2,1)}, f16[128,1024]{1,0:T(8,128)(2,1)S(1)}, u32[]{:S(2)}, u32[]{:S(2)}) collective-permute-start(f16[128,1024]{1,0:T(8,128)(2,1)} %fusion.37), channel_id=1, source_target_pairs={{0,8},{8,0},{16,24},{24,16},{1,9},{9,1},{17,25},{25,17},{2,10},{10... | collective-permute-start | bytes 786440 | tf_op jit(solution)/shard_map/ppermute | solution.py:22
  8.4 7.6 %collective-permute-start.2 = (f32[8,2048]{1,0:T(8,128)S(1)}, f32[8,2048]{1,0:T(8,128)S(1)}, u32[]{:S(2)}, u32[]{:S(2)}) collective-permute-start(f32[8,2048]{1,0:T(8,128)S(1)} %slice.10), channel_id=1, source_target_pairs={{8,0},{16,8},{24,16},{9,1},{17,9},{25,17},{10,2},{18,10},{26,18},{... | collective-permute-start | bytes 196616 | tf_op jit(solution)/shard_map/ppermute | solution.py:454
  12.2 12.4 %collective-permute-start = (f16[512,256]{1,0:T(8,128)(2,1)}, f16[512,256]{1,0:T(8,128)(2,1)}, u32[]{:S(2)}, u32[]{:S(2)}) collective-permute-start(f16[512,256]{1,0:T(8,128)(2,1)} %dynamic-slice_convert_fusion), channel_id=1, source_target_pairs={{0,1},{1,0},{2,3},{3,2},{4,5},{5,4},{6,7},{7,6},{8,9},{9,8},{10,11... | collective-permute-start | bytes 786440 | tf_op jit(solution)/shard_map/ppermute | solution.py:22
  16.0 19.3 %copy-start.21 = (bf16[256,2048]{1,0:T(8,128)(2,1)S(1)}, bf16[256,2048]{1,0:T(8,128)(2,1)}, u32[]{:S(2)}) copy-start(bf16[256,2048]{1,0:T(8,128)(2,1)} %param.10) | copy-start | bytes 3145732
  16.1 26.2 %slice-start = ((s8[8388608]{0:T(1024)(128)(4,1)}), s8[4194304]{0:T(1024)(128)(4,1)S(1)}, s32[]{:S(2)}) async-start(s8[8388608]{0:T(1024)(128)(4,1)} %bitcast.8), calls=%async_computation | async-start | bytes 8388608
  19.3 22.7 %collective-permute-start.6 = (f16[128,1024]{1,0:T(8,128)(2,1)S(1)}, f16[128,1024]{1,0:T(8,128)(2,1)S(1)}, u32[]{:S(2)}, u32[]{:S(2)}) collective-permute-start(f16[128,1024]{1,0:T(8,128)(2,1)S(1)} %get-tuple-element.111), channel_id=1, source_target_pairs={{0,16},{8,24},{16,0},{24,8},{1,17},{9,25},{17,1},{25,9},{2,18},{10... | collective-permute-start | bytes 786440 | tf_op jit(solution)/shard_map/ppermute | solution.py:22
  22.6 12.7 %collective-permute-start.4 = (f16[128,1024]{1,0:T(8,128)(2,1)S(1)}, f16[128,1024]{1,0:T(8,128)(2,1)S(1)}, u32[]{:S(2)}, u32[]{:S(2)}) collective-permute-start(f16[128,1024]{1,0:T(8,128)(2,1)S(1)} %copy-done.22), channel_id=1, source_target_pairs={{0,8},{8,0},{16,24},{24,16},{1,9},{9,1},{17,25},{25,17},{2,10},{10... | collective-permute-start | bytes 786440 | tf_op jit(solution)/shard_map/ppermute | solution.py:22
  25.7 24.0 %copy-start.14 = (f32[512,256]{1,0:T(8,128)}, f32[512,256]{1,0:T(8,128)S(1)}, u32[]{:S(2)}) copy-start(f32[512,256]{1,0:T(8,128)S(1)} %convert_add_fusion.3) | copy-start | bytes 1572868
  25.7 16.5 %slice-start.1 = ((s8[8388608]{0:T(1024)(128)(4,1)}), s8[4194304]{0:T(1024)(128)(4,1)S(1)}, s32[]{:S(2)}) async-start(s8[8388608]{0:T(1024)(128)(4,1)} %bitcast.8), calls=%async_computation.1 | async-start | bytes 8388608
  25.7 14.7 %collective-permute-start.3 = (f16[256,256]{1,0:T(8,128)(2,1)S(1)}, f16[256,256]{1,0:T(8,128)(2,1)S(1)}, u32[]{:S(2)}, u32[]{:S(2)}) collective-permute-start(f16[256,256]{1,0:T(8,128)(2,1)S(1)} %dynamic-slice_convert_fusion.6), channel_id=1, source_target_pairs={{0,2},{1,3},{2,0},{3,1},{4,6},{5,7},{6,4},{7,5},{8,10},{9,11},{10,... | collective-permute-start | bytes 393224 | tf_op jit(solution)/shard_map/ppermute | solution.py:22
  38.3 14.0 %collective-permute-start.9 = (f16[128,1024]{1,0:T(8,128)(2,1)S(1)}, f16[128,1024]{1,0:T(8,128)(2,1)S(1)}, u32[]{:S(2)}, u32[]{:S(2)}) collective-permute-start(f16[128,1024]{1,0:T(8,128)(2,1)S(1)} %get-tuple-element.116), channel_id=1, source_target_pairs={{0,16},{8,24},{16,0},{24,8},{1,17},{9,25},{17,1},{25,9},{2,18},{10... | collective-permute-start | bytes 786440 | tf_op jit(solution)/shard_map/ppermute | solution.py:22
  40.4 9.3 %copy-start.16 = (f16[256,256]{1,0:T(8,128)(2,1)}, f16[256,256]{1,0:T(8,128)(2,1)S(1)}, u32[]{:S(2)}) copy-start(f16[256,256]{1,0:T(8,128)(2,1)S(1)} %collective-permute-done.3) | copy-start | bytes 393220
  40.4 9.2 %collective-permute-start.5 = (f16[256,256]{1,0:T(8,128)(2,1)S(1)}, f16[256,256]{1,0:T(8,128)(2,1)S(1)}, u32[]{:S(2)}, u32[]{:S(2)}) collective-permute-start(f16[256,256]{1,0:T(8,128)(2,1)S(1)} %fusion.49), channel_id=1, source_target_pairs={{0,4},{1,5},{2,6},{3,7},{4,0},{5,1},{6,2},{7,3},{8,12},{9,13},{10,... | collective-permute-start | bytes 393224 | tf_op jit(solution)/shard_map/ppermute | solution.py:22
  42.1 11.2 %collective-permute-start.8 = (bf16[128,1024]{1,0:T(8,128)(2,1)S(1)}, bf16[128,1024]{1,0:T(8,128)(2,1)S(1)}, u32[]{:S(2)}, u32[]{:S(2)}) collective-permute-start(bf16[128,1024]{1,0:T(8,128)(2,1)S(1)} %multiply_convert_fusion.1.own_ref), channel_id=1, source_target_pairs={{0,8},{8,0},{16,24},{24,16},{1,9},{9,1},{17,25},{25,17},{2,10},{10... | collective-permute-start | bytes 786440 | tf_op jit(solution)/shard_map/ppermute | solution.py:22
  49.8 5.0 %collective-permute-start.7 = (bf16[256,256]{1,0:T(8,128)(2,1)S(1)}, bf16[256,256]{1,0:T(8,128)(2,1)S(1)}, u32[]{:S(2)}, u32[]{:S(2)}) collective-permute-start(bf16[256,256]{1,0:T(8,128)(2,1)S(1)} %multiply_convert_fusion.3), channel_id=1, source_target_pairs={{0,2},{1,3},{2,0},{3,1},{4,6},{5,7},{6,4},{7,5},{8,10},{9,11},{10,... | collective-permute-start | bytes 393224 | tf_op jit(solution)/shard_map/ppermute | solution.py:22
  54.9 2.8 %collective-permute-start.10 = (bf16[512,256]{1,0:T(8,128)(2,1)S(1)}, bf16[512,256]{1,0:T(8,128)(2,1)S(1)}, u32[]{:S(2)}, u32[]{:S(2)}) collective-permute-start(bf16[512,256]{1,0:T(8,128)(2,1)S(1)} %pad_maximum_fusion.2), channel_id=1, source_target_pairs={{0,1},{1,0},{2,3},{3,2},{4,5},{5,4},{6,7},{7,6},{8,9},{9,8},{10,11... | collective-permute-start | bytes 786440 | tf_op jit(solution)/shard_map/ppermute | solution.py:22
  55.8 9.2 %collective-permute-start.11 = (bf16[128,1024]{1,0:T(8,128)(2,1)}, bf16[128,1024]{1,0:T(8,128)(2,1)}, u32[]{:S(2)}, u32[]{:S(2)}) collective-permute-start(bf16[128,1024]{1,0:T(8,128)(2,1)} %multiply_convert_fusion.own_ref), channel_id=1, source_target_pairs={{0,8},{8,0},{16,24},{24,16},{1,9},{9,1},{17,25},{25,17},{2,10},{10... | collective-permute-start | bytes 786440 | tf_op jit(solution)/shard_map/ppermute | solution.py:22
  73.2 8.5 %copy-start.5 = (f32[128,1024]{1,0:T(8,128)}, f32[128,1024]{1,0:T(8,128)S(1)}, u32[]{:S(2)}) copy-start(f32[128,1024]{1,0:T(8,128)S(1)} %get-tuple-element.147) | copy-start | bytes 1572868
  73.2 8.5 %collective-permute-start.12 = (bf16[128,1024]{1,0:T(8,128)(2,1)S(1)}, bf16[128,1024]{1,0:T(8,128)(2,1)S(1)}, u32[]{:S(2)}, u32[]{:S(2)}) collective-permute-start(bf16[128,1024]{1,0:T(8,128)(2,1)S(1)} %get-tuple-element.141), channel_id=1, source_target_pairs={{0,8},{8,0},{16,24},{24,16},{1,9},{9,1},{17,25},{25,17},{2,10},{10... | collective-permute-start | bytes 786440 | tf_op jit(solution)/shard_map/ppermute | solution.py:22
  80.0 16.6 %copy-start.4 = (f32[128,1024]{1,0:T(8,128)S(1)}, f32[128,1024]{1,0:T(8,128)}, u32[]{:S(2)}) copy-start(f32[128,1024]{1,0:T(8,128)} %copy-done.3) | copy-start | bytes 1572868
  82.4 2.6 %collective-permute-start.14 = (f32[512,256]{1,0:T(8,128)}, f32[512,256]{1,0:T(8,128)S(1)}, u32[]{:S(2)}, u32[]{:S(2)}) collective-permute-start(f32[512,256]{1,0:T(8,128)} %constant_dynamic-slice_fusion.2), channel_id=1, source_target_pairs={{0,1},{1,0},{2,3},{3,2},{4,5},{5,4},{6,7},{7,6},{8,9},{9,8},{10,11... | collective-permute-start | bytes 1572872 | tf_op jit(solution)/shard_map/ppermute | solution.py:22
  82.4 14.2 %collective-permute-start.16 = (bf16[128,1024]{1,0:T(8,128)(2,1)}, bf16[128,1024]{1,0:T(8,128)(2,1)S(1)}, u32[]{:S(2)}, u32[]{:S(2)}) collective-permute-start(bf16[128,1024]{1,0:T(8,128)(2,1)} %copy-done.13), channel_id=1, source_target_pairs={{0,8},{8,0},{16,24},{24,16},{1,9},{9,1},{17,25},{25,17},{2,10},{10... | collective-permute-start | bytes 786440 | tf_op jit(solution)/shard_map/ppermute | solution.py:22
  83.6 15.0 %collective-permute-start.13 = (bf16[128,1024]{1,0:T(8,128)(2,1)S(1)}, bf16[128,1024]{1,0:T(8,128)(2,1)S(1)}, u32[]{:S(2)}, u32[]{:S(2)}) collective-permute-start(bf16[128,1024]{1,0:T(8,128)(2,1)S(1)} %fusion.46), channel_id=1, source_target_pairs={{0,16},{8,24},{16,0},{24,8},{1,17},{9,25},{17,1},{25,9},{2,18},{10... | collective-permute-start | bytes 786440 | tf_op jit(solution)/shard_map/ppermute | solution.py:22
  86.1 10.6 %collective-permute-start.15 = (bf16[256,256]{1,0:T(8,128)(2,1)S(1)}, bf16[256,256]{1,0:T(8,128)(2,1)S(1)}, u32[]{:S(2)}, u32[]{:S(2)}) collective-permute-start(bf16[256,256]{1,0:T(8,128)(2,1)S(1)} %dynamic-slice_convert_fusion.5), channel_id=1, source_target_pairs={{0,2},{1,3},{2,0},{3,1},{4,6},{5,7},{6,4},{7,5},{8,10},{9,11},{10,... | collective-permute-start | bytes 393224 | tf_op jit(solution)/shard_map/ppermute | solution.py:22
  96.6 8.1 %copy-start.20 = (f16[256,256]{1,0:T(8,128)(2,1)S(1)}, f16[256,256]{1,0:T(8,128)(2,1)}, u32[]{:S(2)}) copy-start(f16[256,256]{1,0:T(8,128)(2,1)} %copy-done.19) | copy-start | bytes 393220
  96.7 13.8 %collective-permute-start.20 = (bf16[128,1024]{1,0:T(8,128)(2,1)S(1)}, bf16[128,1024]{1,0:T(8,128)(2,1)S(1)}, u32[]{:S(2)}, u32[]{:S(2)}) collective-permute-start(bf16[128,1024]{1,0:T(8,128)(2,1)S(1)} %fusion.47), channel_id=1, source_target_pairs={{0,16},{8,24},{16,0},{24,8},{1,17},{9,25},{17,1},{25,9},{2,18},{10... | collective-permute-start | bytes 786440 | tf_op jit(solution)/shard_map/ppermute | solution.py:22
  96.8 7.9 %collective-permute-start.18 = (bf16[256,256]{1,0:T(8,128)(2,1)S(1)}, bf16[256,256]{1,0:T(8,128)(2,1)S(1)}, u32[]{:S(2)}, u32[]{:S(2)}) collective-permute-start(bf16[256,256]{1,0:T(8,128)(2,1)S(1)} %fusion.48), channel_id=1, source_target_pairs={{0,4},{1,5},{2,6},{3,7},{4,0},{5,1},{6,2},{7,3},{8,12},{9,13},{10,... | collective-permute-start | bytes 393224 | tf_op jit(solution)/shard_map/ppermute | solution.py:22
  99.8 12.3 %collective-permute-start.17 = (bf16[128,1024]{1,0:T(8,128)(2,1)S(1)}, bf16[128,1024]{1,0:T(8,128)(2,1)S(1)}, u32[]{:S(2)}, u32[]{:S(2)}) collective-permute-start(bf16[128,1024]{1,0:T(8,128)(2,1)S(1)} %add_convert_fusion.1), channel_id=1, source_target_pairs={{0,8},{8,0},{16,24},{24,16},{1,9},{9,1},{17,25},{25,17},{2,10},{10... | collective-permute-start | bytes 786440 | tf_op jit(solution)/shard_map/ppermute | solution.py:22
  104.9 5.7 %collective-permute-start.19 = (bf16[256,256]{1,0:T(8,128)(2,1)S(1)}, bf16[256,256]{1,0:T(8,128)(2,1)S(1)}, u32[]{:S(2)}, u32[]{:S(2)}) collective-permute-start(bf16[256,256]{1,0:T(8,128)(2,1)S(1)} %multiply_convert_fusion.2), channel_id=1, source_target_pairs={{0,2},{1,3},{2,0},{3,1},{4,6},{5,7},{6,4},{7,5},{8,10},{9,11},{10,... | collective-permute-start | bytes 393224 | tf_op jit(solution)/shard_map/ppermute | solution.py:22
  110.5 10.1 %collective-permute-start.21 = (bf16[128,1024]{1,0:T(8,128)(2,1)S(1)}, bf16[128,1024]{1,0:T(8,128)(2,1)S(1)}, u32[]{:S(2)}, u32[]{:S(2)}) collective-permute-start(bf16[128,1024]{1,0:T(8,128)(2,1)S(1)} %add_convert_fusion), channel_id=1, source_target_pairs={{0,8},{8,0},{16,24},{24,16},{1,9},{9,1},{17,25},{25,17},{2,10},{10... | collective-permute-start | bytes 786440 | tf_op jit(solution)/shard_map/ppermute | solution.py:22
  110.7 5.3 %collective-permute-start.22 = (bf16[512,256]{1,0:T(8,128)(2,1)S(1)}, bf16[512,256]{1,0:T(8,128)(2,1)S(1)}, u32[]{:S(2)}, u32[]{:S(2)}) collective-permute-start(bf16[512,256]{1,0:T(8,128)(2,1)S(1)} %pad_maximum_fusion.3), channel_id=1, source_target_pairs={{0,1},{1,0},{2,3},{3,2},{4,5},{5,4},{6,7},{7,6},{8,9},{9,8},{10,11... | collective-permute-start | bytes 786440 | tf_op jit(solution)/shard_map/ppermute | solution.py:22
  117.0 6.8 %collective-permute-start.23 = (bf16[256,256]{1,0:T(8,128)(2,1)S(1)}, bf16[256,256]{1,0:T(8,128)(2,1)S(1)}, u32[]{:S(2)}, u32[]{:S(2)}) collective-permute-start(bf16[256,256]{1,0:T(8,128)(2,1)S(1)} %dynamic-slice_convert_fusion.3), channel_id=1, source_target_pairs={{0,8},{8,0},{16,24},{24,16},{1,9},{9,1},{17,25},{25,17},{2,10},{10... | collective-permute-start | bytes 393224 | tf_op jit(solution)/shard_map/ppermute | solution.py:22
  117.7 7.4 %collective-permute-start.27 = (bf16[256,256]{1,0:T(8,128)(2,1)S(1)}, bf16[256,256]{1,0:T(8,128)(2,1)S(1)}, u32[]{:S(2)}, u32[]{:S(2)}) collective-permute-start(bf16[256,256]{1,0:T(8,128)(2,1)S(1)} %dynamic-slice_convert_fusion.4), channel_id=1, source_target_pairs={{0,8},{8,0},{16,24},{24,16},{1,9},{9,1},{17,25},{25,17},{2,10},{10... | collective-permute-start | bytes 393224 | tf_op jit(solution)/shard_map/ppermute | solution.py:22
  122.3 4.8 %collective-permute-start.26 = (f32[64,2048]{1,0:T(8,128)S(1)}, f32[64,2048]{1,0:T(8,128)S(1)}, u32[]{:S(2)}, u32[]{:S(2)}) collective-permute-start(f32[64,2048]{1,0:T(8,128)S(1)} %constant_dynamic-slice_fusion), channel_id=1, source_target_pairs={{0,1},{1,0},{2,3},{3,2},{4,5},{5,4},{6,7},{7,6},{8,9},{9,8},{10,11... | collective-permute-start | bytes 1572872 | tf_op jit(solution)/shard_map/ppermute | solution.py:22
  122.4 6.4 %collective-permute-start.25 = (f32[64,2048]{1,0:T(8,128)S(1)}, f32[64,2048]{1,0:T(8,128)S(1)}, u32[]{:S(2)}, u32[]{:S(2)}) collective-permute-start(f32[64,2048]{1,0:T(8,128)S(1)} %constant_dynamic-slice_fusion.1), channel_id=1, source_target_pairs={{0,1},{1,0},{2,3},{3,2},{4,5},{5,4},{6,7},{7,6},{8,9},{9,8},{10,11... | collective-permute-start | bytes 1572872 | tf_op jit(solution)/shard_map/ppermute | solution.py:22
  123.8 18.1 %collective-permute-start.24 = (bf16[256,256]{1,0:T(8,128)(2,1)S(1)}, bf16[256,256]{1,0:T(8,128)(2,1)S(1)}, u32[]{:S(2)}, u32[]{:S(2)}) collective-permute-start(bf16[256,256]{1,0:T(8,128)(2,1)S(1)} %add_convert_fusion.9), channel_id=1, source_target_pairs={{0,16},{8,24},{16,0},{24,8},{1,17},{9,25},{17,1},{25,9},{2,18},{10... | collective-permute-start | bytes 393224 | tf_op jit(solution)/shard_map/ppermute | solution.py:22
  125.2 17.1 %collective-permute-start.35 = (bf16[256,256]{1,0:T(8,128)(2,1)S(1)}, bf16[256,256]{1,0:T(8,128)(2,1)S(1)}, u32[]{:S(2)}, u32[]{:S(2)}) collective-permute-start(bf16[256,256]{1,0:T(8,128)(2,1)S(1)} %add_convert_fusion.8), channel_id=1, source_target_pairs={{0,16},{8,24},{16,0},{24,8},{1,17},{9,25},{17,1},{25,9},{2,18},{10... | collective-permute-start | bytes 393224 | tf_op jit(solution)/shard_map/ppermute | solution.py:22
  127.2 5.0 %collective-permute-start.29 = (bf16[32,2048]{1,0:T(8,128)(2,1)S(1)}, bf16[32,2048]{1,0:T(8,128)(2,1)S(1)}, u32[]{:S(2)}, u32[]{:S(2)}) collective-permute-start(bf16[32,2048]{1,0:T(8,128)(2,1)S(1)} %dynamic-slice_convert_fusion.2), channel_id=1, source_target_pairs={{0,2},{1,3},{2,0},{3,1},{4,6},{5,7},{6,4},{7,5},{8,10},{9,11},{10,... | collective-permute-start | bytes 393224 | tf_op jit(solution)/shard_map/ppermute | solution.py:22
  128.9 5.8 %collective-permute-start.28 = (bf16[32,2048]{1,0:T(8,128)(2,1)S(1)}, bf16[32,2048]{1,0:T(8,128)(2,1)S(1)}, u32[]{:S(2)}, u32[]{:S(2)}) collective-permute-start(bf16[32,2048]{1,0:T(8,128)(2,1)S(1)} %dynamic-slice_convert_fusion.1), channel_id=1, source_target_pairs={{0,4},{1,5},{2,6},{3,7},{4,0},{5,1},{6,2},{7,3},{8,12},{9,13},{10,... | collective-permute-start | bytes 393224 | tf_op jit(solution)/shard_map/ppermute | solution.py:22
  132.3 5.0 %collective-permute-start.31 = (bf16[32,2048]{1,0:T(8,128)(2,1)S(1)}, bf16[32,2048]{1,0:T(8,128)(2,1)S(1)}, u32[]{:S(2)}, u32[]{:S(2)}) collective-permute-start(bf16[32,2048]{1,0:T(8,128)(2,1)S(1)} %add_convert_fusion.7), channel_id=1, source_target_pairs={{0,4},{1,5},{2,6},{3,7},{4,0},{5,1},{6,2},{7,3},{8,12},{9,13},{10,... | collective-permute-start | bytes 393224 | tf_op jit(solution)/shard_map/ppermute | solution.py:22
  134.7 6.3 %collective-permute-start.30 = (bf16[32,2048]{1,0:T(8,128)(2,1)S(1)}, bf16[32,2048]{1,0:T(8,128)(2,1)S(1)}, u32[]{:S(2)}, u32[]{:S(2)}) collective-permute-start(bf16[32,2048]{1,0:T(8,128)(2,1)S(1)} %add_convert_fusion.6), channel_id=1, source_target_pairs={{0,2},{1,3},{2,0},{3,1},{4,6},{5,7},{6,4},{7,5},{8,10},{9,11},{10,... | collective-permute-start | bytes 393224 | tf_op jit(solution)/shard_map/ppermute | solution.py:22
  137.4 6.8 %collective-permute-start.34 = (bf16[32,2048]{1,0:T(8,128)(2,1)S(1)}, bf16[32,2048]{1,0:T(8,128)(2,1)S(1)}, u32[]{:S(2)}, u32[]{:S(2)}) collective-permute-start(bf16[32,2048]{1,0:T(8,128)(2,1)S(1)} %add_convert_fusion.5), channel_id=1, source_target_pairs={{0,2},{1,3},{2,0},{3,1},{4,6},{5,7},{6,4},{7,5},{8,10},{9,11},{10,... | collective-permute-start | bytes 393224 | tf_op jit(solution)/shard_map/ppermute | solution.py:22
  141.0 5.0 %collective-permute-start.33 = (bf16[32,2048]{1,0:T(8,128)(2,1)S(1)}, bf16[32,2048]{1,0:T(8,128)(2,1)S(1)}, u32[]{:S(2)}, u32[]{:S(2)}) collective-permute-start(bf16[32,2048]{1,0:T(8,128)(2,1)S(1)} %add_convert_fusion.4), channel_id=1, source_target_pairs={{0,4},{1,5},{2,6},{3,7},{4,0},{5,1},{6,2},{7,3},{8,12},{9,13},{10,... | collective-permute-start | bytes 393224 | tf_op jit(solution)/shard_map/ppermute | solution.py:22
  142.0 5.0 %collective-permute-start.32 = (bf16[256,256]{1,0:T(8,128)(2,1)S(1)}, bf16[256,256]{1,0:T(8,128)(2,1)S(1)}, u32[]{:S(2)}, u32[]{:S(2)}) collective-permute-start(bf16[256,256]{1,0:T(8,128)(2,1)S(1)} %add_convert_fusion.3), channel_id=1, source_target_pairs={{0,8},{8,0},{16,24},{24,16},{1,9},{9,1},{17,25},{25,17},{2,10},{10... | collective-permute-start | bytes 393224 | tf_op jit(solution)/shard_map/ppermute | solution.py:22
  142.3 6.1 %collective-permute-start.36 = (bf16[256,256]{1,0:T(8,128)(2,1)S(1)}, bf16[256,256]{1,0:T(8,128)(2,1)S(1)}, u32[]{:S(2)}, u32[]{:S(2)}) collective-permute-start(bf16[256,256]{1,0:T(8,128)(2,1)S(1)} %add_convert_fusion.2), channel_id=1, source_target_pairs={{0,8},{8,0},{16,24},{24,16},{1,9},{9,1},{17,25},{25,17},{2,10},{10... | collective-permute-start | bytes 393224 | tf_op jit(solution)/shard_map/ppermute | solution.py:22
  144.2 5.3 %collective-permute-start.37 = (bf16[64,2048]{1,0:T(8,128)(2,1)S(1)}, bf16[64,2048]{1,0:T(8,128)(2,1)S(1)}, u32[]{:S(2)}, u32[]{:S(2)}) collective-permute-start(bf16[64,2048]{1,0:T(8,128)(2,1)S(1)} %pad_maximum_fusion.4), channel_id=1, source_target_pairs={{0,1},{1,0},{2,3},{3,2},{4,5},{5,4},{6,7},{7,6},{8,9},{9,8},{10,11... | collective-permute-start | bytes 786440 | tf_op jit(solution)/shard_map/ppermute | solution.py:22
  146.1 3.4 %collective-permute-start.38 = (bf16[64,2048]{1,0:T(8,128)(2,1)S(1)}, bf16[64,2048]{1,0:T(8,128)(2,1)S(1)}, u32[]{:S(2)}, u32[]{:S(2)}) collective-permute-start(bf16[64,2048]{1,0:T(8,128)(2,1)S(1)} %pad_maximum_fusion.5), channel_id=1, source_target_pairs={{0,1},{1,0},{2,3},{3,2},{4,5},{5,4},{6,7},{7,6},{8,9},{9,8},{10,11... | collective-permute-start | bytes 786440 | tf_op jit(solution)/shard_map/ppermute | solution.py:22
  (20 other events, 72.2 us)

commit v9 on v8

--- a/solution.py
+++ b/solution.py
@@ -452,6 +452,7 @@
     devices = range(group_count)
     top_rows = line.put(line.after(target_logits[:8]))
     incoming = lax.ppermute(top_rows, "grp", [(i + 1, i) for i in devices if i + 1 in devices])
+    vocab[1].step()
     pre_part = line.put(
         jnp.dot(line.after(hidden_states), down_weight, preferred_element_type=F32)
     )
@@ -465,28 +466,27 @@
         line, pre_part * PRE_SCALE, v_bits, [F16] * len(v_bits), activate
     )
     pre.step()
-    line.put(sent[1])
     incoming = line.put(line.after(incoming))
     vocab[0].step()
-    vocab[1].step()
     pre.step()
     vocab[1].step()
     pre.step()
     vocab[0].step()
-    if per_book == 1:
-        prob, entropy = target_pass(target_logits, line.after(incoming))
-    else:
-        top, total = target_sums(target_logits, incoming)
-        top, total = over_books((top, total), merge_sums, per_book)
-        prob, entropy = target_probs(target_logits, incoming, top, total)
-    line.put(entropy)
-    label = lax.dynamic_slice_in_dim(labels, book_index, 1, 1) - book_part * slice_cols
     pre.step()
     vocab[1].step()
     vocab[0].result()
     line.put(vocab_pieces[0][1])
     pre.step()
     acts = line.put(all_acts())
+    if per_book == 1:
+        prob, entropy = target_pass(line.after(target_logits), incoming)
+    else:
+        top, total = target_sums(target_logits, incoming)
+        top, total = over_books((top, total), merge_sums, per_book)
+        prob, entropy = target_probs(target_logits, incoming, top, total)
+    line.put(entropy)
+    acts = line.after(acts)
+    label = lax.dynamic_slice_in_dim(labels, book_index, 1, 1) - book_part * slice_cols
 
     drafts, vocab_proj, sums = [], [], None
     for c in chunks:

time: 152 us -> 163 us (1.072)
  waiting for transfers between devices: 37.4 us -> 46.8 us
  starting transfers between devices: 43.6 us -> 46.5 us
  other arithmetic: 10.1 us -> 12.9 us
    ppermute x38, waiting for transfers between devices: 37.4 us -> 46.8 us  [swap(): return lax.ppermute(value, axis, pairs)]
    ppermute x38, starting transfers between devices: 42.3 us -> 45.3 us  [swap(): return lax.ppermute(value, axis, pairs)]
    unnamed x59 -> x47, local copies, waits for them, and re-layouts: 10.1 us -> 8.52 us
  transfers between devices with their start and end apart: 39 -> 39, of which waited for: 17 -> 16; matrix products, arithmetic and copies ran while one was open for 23% -> 21% of each run, Pallas kernels for 7% -> 7%
where the time goes in v9:
time: 163 us; the launch traced here: 162 us
  waiting for transfers between devices  46.8 us (29%)
  starting transfers between devices  46.5 us (29%)
  matrix products  25.8 us (16%)
  Pallas kernels  17.7 us (11%)
  other arithmetic  12.9 us (8%)
  local copies, waits for them, and re-layouts  11.3 us (7%)
    ppermute x38, waiting for transfers between devices, swap(): return lax.ppermute(value, axis, pairs)  46.8 us
    ppermute x38, starting transfers between devices, swap(): return lax.ppermute(value, axis, pairs)  45.3 us
    dot_general x4, matrix products, on_device(): jnp.dot(part, columns(c), preferred_element_type=F32) * VOCAB_SCALE  13.8 us
    dot_general x4, matrix products, inner_cols(): lax.dot_general(left, right, (((1,), (1,)), ((), ())), preferred_element_...  10.6 us
    unnamed x47, local copies, waits for them, and re-layouts  8.52 us
    pallas_call x2, Pallas kernels, grad_chunk(): pl.pallas_call(body, grid=(rows // block,), in_specs=[row_spec(block, wid...  8.27 us
    pallas_call x2, Pallas kernels, draft_chunk(): pl.pallas_call(body, grid=(rows // block,), in_specs=[row_spec(block, wid...  5.45 us
    pallas_call x1, Pallas kernels, target_pass(): pl.pallas_call(body, grid=(rows // block,), in_specs=[row_spec(block, col...  4.01 us
  transfers between devices with their start and end apart: 39, of which 16 were waited for; matrix products, arithmetic and copies ran while one was open for 21% of the time, Pallas kernels for 7%

profile of v9, /device:TPU:0, one launch (start us, length us, event | category | flops | bytes accessed | tf_op | source)
XLA Modules:
  0.0 162.4 jit_solution(5027863420715110840)
XLA Ops:
  0.7 4.0 %fusion.34 = f16[128,1024]{1,0:T(8,128)(2,1)} fusion(bf16[2048,2048]{1,0:T(8,128)(2,1)} %param.11, bf16[256,2048]{1,0:T(8,128)(2,1)} %param.10, s32[]{:T(128)S(6)} %select_n.175), kind=kOutput, calls=%fused_computation.22 | convolution fusion | flops 537133056 | bytes 4980740 | tf_op jit(solution)/shard_map/dot_general | solution.py:441
  4.6 3.0 %collective-permute-start.1 = (f16[128,1024]{1,0:T(8,128)(2,1)}, f16[128,1024]{1,0:T(8,128)(2,1)}, u32[]{:S(2)}, u32[]{:S(2)}) collective-permute-start(f16[128,1024]{1,0:T(8,128)(2,1)} %fusion.34), channel_id=1, source_target_pairs={{0,8},{8,0},{16,24},{24,16},{1,9},{9,1},{17,25},{25,17},{2,10},{10... | collective-permute-start | bytes 786440 | tf_op jit(solution)/shard_map/ppermute | solution.py:22
  9.8 3.6 %fusion.37 = f16[128,1024]{1,0:T(8,128)(2,1)} fusion(bf16[2048,2048]{1,0:T(8,128)(2,1)} %param.11, bf16[256,2048]{1,0:T(8,128)(2,1)S(1)} %copy-done.18, s32[]{:T(128)S(6)} %select_n.175), kind=kOutput, calls=%fused_computation.23 | convolution fusion | flops 537133056 | bytes 4980740 | tf_op jit(solution)/shard_map/dot_general | solution.py:441
  13.4 2.6 %collective-permute-start.4 = (f16[128,1024]{1,0:T(8,128)(2,1)}, f16[128,1024]{1,0:T(8,128)(2,1)S(1)}, u32[]{:S(2)}, u32[]{:S(2)}) collective-permute-start(f16[128,1024]{1,0:T(8,128)(2,1)} %fusion.37), channel_id=1, source_target_pairs={{0,8},{8,0},{16,24},{24,16},{1,9},{9,1},{17,25},{25,17},{2,10},{10... | collective-permute-start | bytes 786440 | tf_op jit(solution)/shard_map/ppermute | solution.py:22
  17.6 3.2 %fusion.44 = (f16[128,1024]{1,0:T(8,128)(2,1)S(1)}, f32[128,1024]{1,0:T(8,128)S(1)}) fusion(f16[128,1024]{1,0:T(8,128)(2,1)} %collective-permute-done.1, bf16[2048,2048]{1,0:T(8,128)(2,1)} %param.11, bf16[256,2048]{1,0:T(8,128)(2,1)} %param.10, s32[]{:T(128)S(6)} %select_n.178), kind=kOutput, calls=%fused_computation.49 | convolution fusion | flops 537395200 | bytes 5767172 | tf_op jit(solution)/shard_map/dot_general | solution.py:441
  20.8 2.7 %collective-permute-start.6 = (f16[128,1024]{1,0:T(8,128)(2,1)S(1)}, f16[128,1024]{1,0:T(8,128)(2,1)S(1)}, u32[]{:S(2)}, u32[]{:S(2)}) collective-permute-start(f16[128,1024]{1,0:T(8,128)(2,1)S(1)} %get-tuple-element.113), channel_id=1, source_target_pairs={{0,16},{8,24},{16,0},{24,8},{1,17},{9,25},{17,1},{25,9},{2,18},{10... | collective-permute-start | bytes 786440 | tf_op jit(solution)/shard_map/ppermute | solution.py:22
  24.5 1.5 collective-permute-start.3
  26.1 3.0 %fusion.45 = (f16[128,1024]{1,0:T(8,128)(2,1)S(1)}, f32[128,1024]{1,0:T(8,128)S(1)}) fusion(f16[128,1024]{1,0:T(8,128)(2,1)S(1)} %collective-permute-done.4, bf16[2048,2048]{1,0:T(8,128)(2,1)} %param.11, bf16[256,2048]{1,0:T(8,128)(2,1)S(1)} %copy-done.19, s32[]{:T(128)S(6)} %select_n.178), kind=kOutput, calls=%fused_computation.50 | convolution fusion | flops 537395200 | bytes 5767172 | tf_op jit(solution)/shard_map/dot_general | solution.py:441
  30.2 1.6 collective-permute-start.5
  31.8 9.4 %collective-permute-done.6 = f16[128,1024]{1,0:T(8,128)(2,1)S(1)} collective-permute-done((f16[128,1024]{1,0:T(8,128)(2,1)S(1)}, f16[128,1024]{1,0:T(8,128)(2,1)S(1)}, u32[]{:S(2)}, u32[]{:S(2)}) %collective-permute-start.6) | collective-permute-done | bytes 262176 | tf_op jit(solution)/shard_map/ppermute | solution.py:22
  42.6 1.6 collective-permute-start.7
  44.2 2.7 %collective-permute-done.9 = f16[128,1024]{1,0:T(8,128)(2,1)S(1)} collective-permute-done((f16[128,1024]{1,0:T(8,128)(2,1)S(1)}, f16[128,1024]{1,0:T(8,128)(2,1)S(1)}, u32[]{:S(2)}, u32[]{:S(2)}) %collective-permute-start.9) | collective-permute-done | bytes 262176 | tf_op jit(solution)/shard_map/ppermute | solution.py:22
  47.0 5.4 %collective-permute-done.8.other_ref = bf16[128,1024]{1,0:T(8,128)(2,1)S(1)} collective-permute-done((bf16[128,1024]{1,0:T(8,128)(2,1)S(1)}, bf16[128,1024]{1,0:T(8,128)(2,1)S(1)}, u32[]{:S(2)}, u32[]{:S(2)}) %collective-permute-start.8) | collective-permute-done | bytes 262176 | tf_op jit(solution)/shard_map/ppermute | solution.py:22
  56.9 3.4 %copy-done.1 = f32[1024,2048]{1,0:T(8,128)S(1)} copy-done((f32[1024,2048]{1,0:T(8,128)S(1)}, f32[1024,2048]{1,0:T(8,128)}, u32[]{:S(2)}) %copy-start.1) | copy-done | bytes 8388632
  60.3 4.0 %target_pass.1 = (f32[1024,2048]{1,0:T(8,128)S(1)}, f32[1024,1]{1,0:T(8,128)S(1)}) custom-call(f32[1024,2048]{1,0:T(8,128)S(1)} %copy-done.1, f32[1024,2048]{1,0:T(8,128)S(1)} %copy-done.1, f32[8,2048]{1,0:T(8,128)S(1)} %collective-permute-done.2.incoming_ref), custom_call_target="tpu_custom_call" | custom-call | flops 3072 | bytes 4096 | tf_op jit(solution)/shard_map/target_pass/pallas_call | solution.py:132
  65.1 3.4 %copy-done.2 = f32[1024,2048]{1,0:T(8,128)S(1)} copy-done((f32[1024,2048]{1,0:T(8,128)S(1)}, f32[1024,2048]{1,0:T(8,128)}, u32[]{:S(2)}) %copy-start.2) | copy-done | bytes 8388632
  68.5 2.5 %draft_chunk.2 = (f32[1024,1024]{1,0:T(8,128)S(1)}, bf16[256,1024]{1,0:T(8,128)(2,1)S(1)}, f32[1024,1]{1,0:T(8,128)S(1)}, f32[1024,1]{1,0:T(8,128)S(1)}) custom-call(f32[1024,2048]{1,0:T(8,128)S(1)} %copy-done.2, bf16[1024,256]{1,0:T(8,128)(2,1)S(1)} %pad_maximum_fusion.acts_ref, bf16[128,1024]{1,0:T(8,128)(2,1)S(1)} %multiply_convert_fusion.1.own_ref, ...), custom_call_target="tpu_custom_call" | custom-call | flops 131072 | bytes 2048 | tf_op jit(solution)/shard_map/draft_chunk/pallas_call | solution.py:220
  71.0 3.0 %draft_chunk.3 = (f32[1024,1024]{1,0:T(8,128)S(1)}, bf16[256,1024]{1,0:T(8,128)(2,1)S(1)}, f32[1024,1]{1,0:T(8,128)S(1)}, f32[1024,1]{1,0:T(8,128)S(1)}) custom-call(f32[1024,2048]{1,0:T(8,128)S(1)} %copy-done.2, bf16[1024,256]{1,0:T(8,128)(2,1)S(1)} %pad_maximum_fusion.acts_ref, bf16[128,1024]{1,0:T(8,128)(2,1)S(1)} %multiply_convert_fusion.own_ref, ...), custom_call_target="tpu_custom_call" | custom-call | flops 131072 | bytes 2048 | tf_op jit(solution)/shard_map/draft_chunk/pallas_call | solution.py:220
  74.0 4.1 %grad_chunk.2 = (bf16[128,1024]{1,0:T(8,128)(2,1)S(1)}, f32[128,1024]{1,0:T(8,128)S(1)}, f32[1024,256]{1,0:T(8,128)S(1)}, f32[1024,1]{1,0:T(8,128)S(1)}) custom-call(f32[1024,1024]{1,0:T(8,128)S(1)} %get-tuple-element.138.draft_ref, f32[1024,2048]{1,0:T(8,128)S(1)} %get-tuple-element.139.prob_ref, s32[1024,1]{1,0:T(8,128)S(1)} %copy.11.label_ref, ...), custom_call_target="tpu_custom_call" | custom-call | flops 262144 | bytes 2048 | tf_op jit(solution)/shard_map/grad_chunk/pallas_call | solution.py:292
  79.4 4.2 %grad_chunk.3 = (bf16[128,1024]{1,0:T(8,128)(2,1)S(1)}, f32[128,1024]{1,0:T(8,128)S(1)}, f32[1024,256]{1,0:T(8,128)S(1)}, f32[1024,1]{1,0:T(8,128)S(1)}) custom-call(f32[1024,1024]{1,0:T(8,128)S(1)} %get-tuple-element.144.draft_ref, f32[1024,2048]{1,0:T(8,128)S(1)} %get-tuple-element.139.prob_ref, s32[1024,1]{1,0:T(8,128)S(1)} %copy.11.label_ref, ...), custom_call_target="tpu_custom_call" | custom-call | flops 262144 | bytes 2048 | tf_op jit(solution)/shard_map/grad_chunk/pallas_call | solution.py:292
  84.5 2.0 %collective-permute-done.12 = bf16[128,1024]{1,0:T(8,128)(2,1)S(1)} collective-permute-done((bf16[128,1024]{1,0:T(8,128)(2,1)S(1)}, bf16[128,1024]{1,0:T(8,128)(2,1)S(1)}, u32[]{:S(2)}, u32[]{:S(2)}) %collective-permute-start.12) | collective-permute-done | bytes 262176 | tf_op jit(solution)/shard_map/ppermute | solution.py:22
  88.8 1.9 %collective-permute-start.13 = (bf16[128,1024]{1,0:T(8,128)(2,1)}, bf16[128,1024]{1,0:T(8,128)(2,1)S(1)}, u32[]{:S(2)}, u32[]{:S(2)}) collective-permute-start(bf16[128,1024]{1,0:T(8,128)(2,1)} %fusion.46), channel_id=1, source_target_pairs={{0,16},{8,24},{16,0},{24,8},{1,17},{9,25},{17,1},{25,9},{2,18},{10... | collective-permute-start | bytes 786440 | tf_op jit(solution)/shard_map/ppermute | solution.py:22
  91.8 1.6 collective-permute-start.15
  93.3 8.2 %collective-permute-done.16 = bf16[128,1024]{1,0:T(8,128)(2,1)S(1)} collective-permute-done((bf16[128,1024]{1,0:T(8,128)(2,1)S(1)}, bf16[128,1024]{1,0:T(8,128)(2,1)S(1)}, u32[]{:S(2)}, u32[]{:S(2)}) %collective-permute-start.16) | collective-permute-done | bytes 262176 | tf_op jit(solution)/shard_map/ppermute | solution.py:22
  101.7 1.6 collective-permute-start.18
  103.3 5.7 %collective-permute-done.13 = bf16[128,1024]{1,0:T(8,128)(2,1)S(1)} collective-permute-done((bf16[128,1024]{1,0:T(8,128)(2,1)}, bf16[128,1024]{1,0:T(8,128)(2,1)S(1)}, u32[]{:S(2)}, u32[]{:S(2)}) %collective-permute-start.13) | collective-permute-done | bytes 262176 | tf_op jit(solution)/shard_map/ppermute | solution.py:22
  110.5 3.7 %fusion.2 = f32[128,2048]{1,0:T(8,128)S(1)} fusion(bf16[128,1024]{1,0:T(8,128)(2,1)S(1)} %add_convert_fusion.1, bf16[2048,2048]{1,0:T(8,128)(2,1)} %param.11), kind=kOutput, calls=%fused_computation.2 | convolution fusion | flops 536870912 | bytes 5505024 | tf_op jit(solution)/shard_map/dot_general | solution.py:44
  114.5 1.5 collective-permute-start.19
  116.2 1.9 %collective-permute-start.21 = (bf16[128,1024]{1,0:T(8,128)(2,1)S(1)}, bf16[128,1024]{1,0:T(8,128)(2,1)S(1)}, u32[]{:S(2)}, u32[]{:S(2)}) collective-permute-start(bf16[128,1024]{1,0:T(8,128)(2,1)S(1)} %add_convert_fusion), channel_id=1, source_target_pairs={{0,8},{8,0},{16,24},{24,16},{1,9},{9,1},{17,25},{25,17},{2,10},{10... | collective-permute-start | bytes 786440 | tf_op jit(solution)/shard_map/ppermute | solution.py:22
  118.0 1.5 collective-permute-done.19
  119.7 3.9 %fusion = f32[128,2048]{1,0:T(8,128)S(1)} fusion(bf16[128,1024]{1,0:T(8,128)(2,1)S(1)} %collective-permute-done.17, bf16[2048,2048]{1,0:T(8,128)(2,1)} %param.11), kind=kOutput, calls=%fused_computation | convolution fusion | flops 536870912 | bytes 5505024 | tf_op jit(solution)/shard_map/dot_general | solution.py:44
  124.6 1.9 %collective-permute-start.23 = (bf16[256,256]{1,0:T(8,128)(2,1)S(1)}, bf16[256,256]{1,0:T(8,128)(2,1)S(1)}, u32[]{:S(2)}, u32[]{:S(2)}) collective-permute-start(bf16[256,256]{1,0:T(8,128)(2,1)S(1)} %dynamic-slice_convert_fusion.3), channel_id=1, source_target_pairs={{0,8},{8,0},{16,24},{24,16},{1,9},{9,1},{17,25},{25,17},{2,10},{10... | collective-permute-start | bytes 393224 | tf_op jit(solution)/shard_map/ppermute | solution.py:22
  126.7 1.5 fusion.16
  128.2 1.5 broadcast_select_fusion
  131.3 3.8 %collective-permute-start.24 = (bf16[256,256]{1,0:T(8,128)(2,1)S(1)}, bf16[256,256]{1,0:T(8,128)(2,1)S(1)}, u32[]{:S(2)}, u32[]{:S(2)}) collective-permute-start(bf16[256,256]{1,0:T(8,128)(2,1)S(1)} %add_convert_fusion.9), channel_id=1, source_target_pairs={{0,16},{8,24},{16,0},{24,8},{1,17},{9,25},{17,1},{25,9},{2,18},{10... | collective-permute-start | bytes 393224 | tf_op jit(solution)/shard_map/ppermute | solution.py:22
  135.2 2.4 %collective-permute-start.35 = (bf16[256,256]{1,0:T(8,128)(2,1)S(1)}, bf16[256,256]{1,0:T(8,128)(2,1)S(1)}, u32[]{:S(2)}, u32[]{:S(2)}) collective-permute-start(bf16[256,256]{1,0:T(8,128)(2,1)S(1)} %add_convert_fusion.8), channel_id=1, source_target_pairs={{0,16},{8,24},{16,0},{24,8},{1,17},{9,25},{17,1},{25,9},{2,18},{10... | collective-permute-start | bytes 393224 | tf_op jit(solution)/shard_map/ppermute | solution.py:22
  137.7 1.5 collective-permute-start.29
  139.3 1.7 %collective-permute-start.28 = (bf16[32,2048]{1,0:T(8,128)(2,1)S(1)}, bf16[32,2048]{1,0:T(8,128)(2,1)S(1)}, u32[]{:S(2)}, u32[]{:S(2)}) collective-permute-start(bf16[32,2048]{1,0:T(8,128)(2,1)S(1)} %dynamic-slice_convert_fusion.1), channel_id=1, source_target_pairs={{0,4},{1,5},{2,6},{3,7},{4,0},{5,1},{6,2},{7,3},{8,12},{9,13},{10,... | collective-permute-start | bytes 393224 | tf_op jit(solution)/shard_map/ppermute | solution.py:22
  140.9 1.8 %collective-permute-done.29 = bf16[32,2048]{1,0:T(8,128)(2,1)S(1)} collective-permute-done((bf16[32,2048]{1,0:T(8,128)(2,1)S(1)}, bf16[32,2048]{1,0:T(8,128)(2,1)S(1)}, u32[]{:S(2)}, u32[]{:S(2)}) %collective-permute-start.29) | collective-permute-done | bytes 131104 | tf_op jit(solution)/shard_map/ppermute | solution.py:22
  142.8 1.6 collective-permute-start.31
  145.9 1.9 %collective-permute-done.31 = bf16[32,2048]{1,0:T(8,128)(2,1)S(1)} collective-permute-done((bf16[32,2048]{1,0:T(8,128)(2,1)S(1)}, bf16[32,2048]{1,0:T(8,128)(2,1)S(1)}, u32[]{:S(2)}, u32[]{:S(2)}) %collective-permute-start.31) | collective-permute-done | bytes 131104 | tf_op jit(solution)/shard_map/ppermute | solution.py:22
  147.9 1.5 collective-permute-start.34
  149.3 2.0 %collective-permute-done.30 = bf16[32,2048]{1,0:T(8,128)(2,1)S(1)} collective-permute-done((bf16[32,2048]{1,0:T(8,128)(2,1)S(1)}, bf16[32,2048]{1,0:T(8,128)(2,1)S(1)}, u32[]{:S(2)}, u32[]{:S(2)}) %collective-permute-start.30) | collective-permute-done | bytes 131104 | tf_op jit(solution)/shard_map/ppermute | solution.py:22
  151.4 1.7 %collective-permute-start.33 = (bf16[32,2048]{1,0:T(8,128)(2,1)S(1)}, bf16[32,2048]{1,0:T(8,128)(2,1)S(1)}, u32[]{:S(2)}, u32[]{:S(2)}) collective-permute-start(bf16[32,2048]{1,0:T(8,128)(2,1)S(1)} %add_convert_fusion.4), channel_id=1, source_target_pairs={{0,4},{1,5},{2,6},{3,7},{4,0},{5,1},{6,2},{7,3},{8,12},{9,13},{10,... | collective-permute-start | bytes 393224 | tf_op jit(solution)/shard_map/ppermute | solution.py:22
  153.2 2.1 %collective-permute-start.36 = (bf16[256,256]{1,0:T(8,128)(2,1)S(1)}, bf16[256,256]{1,0:T(8,128)(2,1)S(1)}, u32[]{:S(2)}, u32[]{:S(2)}) collective-permute-start(bf16[256,256]{1,0:T(8,128)(2,1)S(1)} %add_convert_fusion.2), channel_id=1, source_target_pairs={{0,8},{8,0},{16,24},{24,16},{1,9},{9,1},{17,25},{25,17},{2,10},{10... | collective-permute-start | bytes 393224 | tf_op jit(solution)/shard_map/ppermute | solution.py:22
  156.5 1.6 collective-permute-done.32
  158.1 1.4 collective-permute-done.36
  160.8 1.6 maximum_convert_fusion
  (144 shorter events, 27.7 us)
Async XLA Ops:
  0.6 15.4 %copy-start = (bf16[1024,1024]{1,0:T(8,128)(2,1)S(1)}, bf16[1024,1024]{1,0:T(8,128)(2,1)}, u32[]{:S(2)}) copy-start(bf16[1024,1024]{1,0:T(8,128)(2,1)} %param.6) | copy-start | bytes 6291460
  0.6 9.1 %copy-start.18 = (bf16[256,2048]{1,0:T(8,128)(2,1)S(1)}, bf16[256,2048]{1,0:T(8,128)(2,1)}, u32[]{:S(2)}) copy-start(bf16[256,2048]{1,0:T(8,128)(2,1)} %param.10) | copy-start | bytes 3145732
  4.6 11.4 %copy-start.20 = (bf16[1024,256]{1,0:T(8,128)(2,1)S(1)}, bf16[1024,256]{1,0:T(8,128)(2,1)}, u32[]{:S(2)}) copy-start(bf16[1024,256]{1,0:T(8,128)(2,1)} %param.9) | copy-start | bytes 1572868
  4.6 12.9 %collective-permute-start.1 = (f16[128,1024]{1,0:T(8,128)(2,1)}, f16[128,1024]{1,0:T(8,128)(2,1)}, u32[]{:S(2)}, u32[]{:S(2)}) collective-permute-start(f16[128,1024]{1,0:T(8,128)(2,1)} %fusion.34), channel_id=1, source_target_pairs={{0,8},{8,0},{16,24},{24,16},{1,9},{9,1},{17,25},{25,17},{2,10},{10... | collective-permute-start | bytes 786440 | tf_op jit(solution)/shard_map/ppermute | solution.py:22
  8.5 9.0 %collective-permute-start.2 = (f32[8,2048]{1,0:T(8,128)S(1)}, f32[8,2048]{1,0:T(8,128)S(1)}, u32[]{:S(2)}, u32[]{:S(2)}) collective-permute-start(f32[8,2048]{1,0:T(8,128)S(1)} %slice.22), channel_id=1, source_target_pairs={{8,0},{16,8},{24,16},{9,1},{17,9},{25,17},{10,2},{18,10},{26,18},{... | collective-permute-start | bytes 196616 | tf_op jit(solution)/shard_map/ppermute | solution.py:454
  13.4 12.7 %collective-permute-start.4 = (f16[128,1024]{1,0:T(8,128)(2,1)}, f16[128,1024]{1,0:T(8,128)(2,1)S(1)}, u32[]{:S(2)}, u32[]{:S(2)}) collective-permute-start(f16[128,1024]{1,0:T(8,128)(2,1)} %fusion.37), channel_id=1, source_target_pairs={{0,8},{8,0},{16,24},{24,16},{1,9},{9,1},{17,25},{25,17},{2,10},{10... | collective-permute-start | bytes 786440 | tf_op jit(solution)/shard_map/ppermute | solution.py:22
  17.5 5.9 %collective-permute-start = (f16[512,256]{1,0:T(8,128)(2,1)}, f16[512,256]{1,0:T(8,128)(2,1)}, u32[]{:S(2)}, u32[]{:S(2)}) collective-permute-start(f16[512,256]{1,0:T(8,128)(2,1)} %dynamic-slice_convert_fusion), channel_id=1, source_target_pairs={{0,1},{1,0},{2,3},{3,2},{4,5},{5,4},{6,7},{7,6},{8,9},{9,8},{10,11... | collective-permute-start | bytes 786440 | tf_op jit(solution)/shard_map/ppermute | solution.py:22
  20.8 20.4 %collective-permute-start.6 = (f16[128,1024]{1,0:T(8,128)(2,1)S(1)}, f16[128,1024]{1,0:T(8,128)(2,1)S(1)}, u32[]{:S(2)}, u32[]{:S(2)}) collective-permute-start(f16[128,1024]{1,0:T(8,128)(2,1)S(1)} %get-tuple-element.113), channel_id=1, source_target_pairs={{0,16},{8,24},{16,0},{24,8},{1,17},{9,25},{17,1},{25,9},{2,18},{10... | collective-permute-start | bytes 786440 | tf_op jit(solution)/shard_map/ppermute | solution.py:22
  24.5 18.0 %copy-start.9 = (f32[512,256]{1,0:T(8,128)}, f32[512,256]{1,0:T(8,128)S(1)}, u32[]{:S(2)}) copy-start(f32[512,256]{1,0:T(8,128)S(1)} %convert_add_fusion.3) | copy-start | bytes 1572868
  24.5 5.7 %collective-permute-start.3 = (f16[256,256]{1,0:T(8,128)(2,1)S(1)}, f16[256,256]{1,0:T(8,128)(2,1)S(1)}, u32[]{:S(2)}, u32[]{:S(2)}) collective-permute-start(f16[256,256]{1,0:T(8,128)(2,1)S(1)} %dynamic-slice_convert_fusion.6), channel_id=1, source_target_pairs={{0,2},{1,3},{2,0},{3,1},{4,6},{5,7},{6,4},{7,5},{8,10},{9,11},{10,... | collective-permute-start | bytes 393224 | tf_op jit(solution)/shard_map/ppermute | solution.py:22
  29.0 17.8 %collective-permute-start.9 = (f16[128,1024]{1,0:T(8,128)(2,1)S(1)}, f16[128,1024]{1,0:T(8,128)(2,1)S(1)}, u32[]{:S(2)}, u32[]{:S(2)}) collective-permute-start(f16[128,1024]{1,0:T(8,128)(2,1)S(1)} %get-tuple-element.117), channel_id=1, source_target_pairs={{0,16},{8,24},{16,0},{24,8},{1,17},{9,25},{17,1},{25,9},{2,18},{10... | collective-permute-start | bytes 786440 | tf_op jit(solution)/shard_map/ppermute | solution.py:22
  30.2 22.2 %copy-start.11 = (f16[256,256]{1,0:T(8,128)(2,1)}, f16[256,256]{1,0:T(8,128)(2,1)S(1)}, u32[]{:S(2)}) copy-start(f16[256,256]{1,0:T(8,128)(2,1)S(1)} %collective-permute-done.3) | copy-start | bytes 393220
  30.2 12.2 %collective-permute-start.5 = (f16[256,256]{1,0:T(8,128)(2,1)S(1)}, f16[256,256]{1,0:T(8,128)(2,1)S(1)}, u32[]{:S(2)}, u32[]{:S(2)}) collective-permute-start(f16[256,256]{1,0:T(8,128)(2,1)S(1)} %fusion.49), channel_id=1, source_target_pairs={{0,4},{1,5},{2,6},{3,7},{4,0},{5,1},{6,2},{7,3},{8,12},{9,13},{10,... | collective-permute-start | bytes 393224 | tf_op jit(solution)/shard_map/ppermute | solution.py:22
  42.3 10.1 %collective-permute-start.8 = (bf16[128,1024]{1,0:T(8,128)(2,1)S(1)}, bf16[128,1024]{1,0:T(8,128)(2,1)S(1)}, u32[]{:S(2)}, u32[]{:S(2)}) collective-permute-start(bf16[128,1024]{1,0:T(8,128)(2,1)S(1)} %multiply_convert_fusion.1.own_ref), channel_id=1, source_target_pairs={{0,8},{8,0},{16,24},{24,16},{1,9},{9,1},{17,25},{25,17},{2,10},{10... | collective-permute-start | bytes 786440 | tf_op jit(solution)/shard_map/ppermute | solution.py:22
  42.5 9.9 %copy-start.16 = (f16[256,256]{1,0:T(8,128)(2,1)}, f16[256,256]{1,0:T(8,128)(2,1)S(1)}, u32[]{:S(2)}) copy-start(f16[256,256]{1,0:T(8,128)(2,1)S(1)} %collective-permute-done.5) | copy-start | bytes 393220
  42.6 9.8 %collective-permute-start.7 = (bf16[256,256]{1,0:T(8,128)(2,1)S(1)}, bf16[256,256]{1,0:T(8,128)(2,1)S(1)}, u32[]{:S(2)}, u32[]{:S(2)}) collective-permute-start(bf16[256,256]{1,0:T(8,128)(2,1)S(1)} %multiply_convert_fusion.3), channel_id=1, source_target_pairs={{0,2},{1,3},{2,0},{3,1},{4,6},{5,7},{6,4},{7,5},{8,10},{9,11},{10,... | collective-permute-start | bytes 393224 | tf_op jit(solution)/shard_map/ppermute | solution.py:22
  53.8 1.9 %collective-permute-start.10 = (bf16[512,256]{1,0:T(8,128)(2,1)}, bf16[512,256]{1,0:T(8,128)(2,1)}, u32[]{:S(2)}, u32[]{:S(2)}) collective-permute-start(bf16[512,256]{1,0:T(8,128)(2,1)} %pad_maximum_fusion.2), channel_id=1, source_target_pairs={{0,1},{1,0},{2,3},{3,2},{4,5},{5,4},{6,7},{7,6},{8,9},{9,8},{10,11... | collective-permute-start | bytes 786440 | tf_op jit(solution)/shard_map/ppermute | solution.py:22
  54.8 16.1 %collective-permute-start.11 = (bf16[128,1024]{1,0:T(8,128)(2,1)S(1)}, bf16[128,1024]{1,0:T(8,128)(2,1)S(1)}, u32[]{:S(2)}, u32[]{:S(2)}) collective-permute-start(bf16[128,1024]{1,0:T(8,128)(2,1)S(1)} %multiply_convert_fusion.own_ref), channel_id=1, source_target_pairs={{0,8},{8,0},{16,24},{24,16},{1,9},{9,1},{17,25},{25,17},{2,10},{10... | collective-permute-start | bytes 786440 | tf_op jit(solution)/shard_map/ppermute | solution.py:22
  78.1 8.4 %collective-permute-start.12 = (bf16[128,1024]{1,0:T(8,128)(2,1)S(1)}, bf16[128,1024]{1,0:T(8,128)(2,1)S(1)}, u32[]{:S(2)}, u32[]{:S(2)}) collective-permute-start(bf16[128,1024]{1,0:T(8,128)(2,1)S(1)} %get-tuple-element.143), channel_id=1, source_target_pairs={{0,8},{8,0},{16,24},{24,16},{1,9},{9,1},{17,25},{25,17},{2,10},{10... | collective-permute-start | bytes 786440 | tf_op jit(solution)/shard_map/ppermute | solution.py:22
  87.3 3.3 %collective-permute-start.14 = (f32[512,256]{1,0:T(8,128)}, f32[512,256]{1,0:T(8,128)S(1)}, u32[]{:S(2)}, u32[]{:S(2)}) collective-permute-start(f32[512,256]{1,0:T(8,128)} %constant_dynamic-slice_fusion.2), channel_id=1, source_target_pairs={{0,1},{1,0},{2,3},{3,2},{4,5},{5,4},{6,7},{7,6},{8,9},{9,8},{10,11... | collective-permute-start | bytes 1572872 | tf_op jit(solution)/shard_map/ppermute | solution.py:22
  87.4 14.1 %collective-permute-start.16 = (bf16[128,1024]{1,0:T(8,128)(2,1)S(1)}, bf16[128,1024]{1,0:T(8,128)(2,1)S(1)}, u32[]{:S(2)}, u32[]{:S(2)}) collective-permute-start(bf16[128,1024]{1,0:T(8,128)(2,1)S(1)} %get-tuple-element.150), channel_id=1, source_target_pairs={{0,8},{8,0},{16,24},{24,16},{1,9},{9,1},{17,25},{25,17},{2,10},{10... | collective-permute-start | bytes 786440 | tf_op jit(solution)/shard_map/ppermute | solution.py:22
  88.8 20.3 %collective-permute-start.13 = (bf16[128,1024]{1,0:T(8,128)(2,1)}, bf16[128,1024]{1,0:T(8,128)(2,1)S(1)}, u32[]{:S(2)}, u32[]{:S(2)}) collective-permute-start(bf16[128,1024]{1,0:T(8,128)(2,1)} %fusion.46), channel_id=1, source_target_pairs={{0,16},{8,24},{16,0},{24,8},{1,17},{9,25},{17,1},{25,9},{2,18},{10... | collective-permute-start | bytes 786440 | tf_op jit(solution)/shard_map/ppermute | solution.py:22
  91.8 9.9 %collective-permute-start.15 = (bf16[256,256]{1,0:T(8,128)(2,1)S(1)}, bf16[256,256]{1,0:T(8,128)(2,1)S(1)}, u32[]{:S(2)}, u32[]{:S(2)}) collective-permute-start(bf16[256,256]{1,0:T(8,128)(2,1)S(1)} %dynamic-slice_convert_fusion.5), channel_id=1, source_target_pairs={{0,2},{1,3},{2,0},{3,1},{4,6},{5,7},{6,4},{7,5},{8,10},{9,11},{10,... | collective-permute-start | bytes 393224 | tf_op jit(solution)/shard_map/ppermute | solution.py:22
  101.5 12.8 %copy-start.10 = (f32[512,256]{1,0:T(8,128)S(1)}, f32[512,256]{1,0:T(8,128)}, u32[]{:S(2)}) copy-start(f32[512,256]{1,0:T(8,128)} %copy-done.9) | copy-start | bytes 1572868
  101.5 12.8 %copy-start.12 = (f16[256,256]{1,0:T(8,128)(2,1)S(1)}, f16[256,256]{1,0:T(8,128)(2,1)}, u32[]{:S(2)}) copy-start(f16[256,256]{1,0:T(8,128)(2,1)} %copy-done.11) | copy-start | bytes 393220
  101.5 12.8 %copy-start.17 = (f16[256,256]{1,0:T(8,128)(2,1)S(1)}, f16[256,256]{1,0:T(8,128)(2,1)}, u32[]{:S(2)}) copy-start(f16[256,256]{1,0:T(8,128)(2,1)} %copy-done.16) | copy-start | bytes 393220
  101.6 14.5 %collective-permute-start.20 = (bf16[128,1024]{1,0:T(8,128)(2,1)S(1)}, bf16[128,1024]{1,0:T(8,128)(2,1)S(1)}, u32[]{:S(2)}, u32[]{:S(2)}) collective-permute-start(bf16[128,1024]{1,0:T(8,128)(2,1)S(1)} %fusion.47), channel_id=1, source_target_pairs={{0,16},{8,24},{16,0},{24,8},{1,17},{9,25},{17,1},{25,9},{2,18},{10... | collective-permute-start | bytes 786440 | tf_op jit(solution)/shard_map/ppermute | solution.py:22
  101.7 12.6 %collective-permute-start.18 = (bf16[256,256]{1,0:T(8,128)(2,1)S(1)}, bf16[256,256]{1,0:T(8,128)(2,1)S(1)}, u32[]{:S(2)}, u32[]{:S(2)}) collective-permute-start(bf16[256,256]{1,0:T(8,128)(2,1)S(1)} %fusion.48), channel_id=1, source_target_pairs={{0,4},{1,5},{2,6},{3,7},{4,0},{5,1},{6,2},{7,3},{8,12},{9,13},{10,... | collective-permute-start | bytes 393224 | tf_op jit(solution)/shard_map/ppermute | solution.py:22
  110.2 9.4 %collective-permute-start.17 = (bf16[128,1024]{1,0:T(8,128)(2,1)S(1)}, bf16[128,1024]{1,0:T(8,128)(2,1)S(1)}, u32[]{:S(2)}, u32[]{:S(2)}) collective-permute-start(bf16[128,1024]{1,0:T(8,128)(2,1)S(1)} %add_convert_fusion.1), channel_id=1, source_target_pairs={{0,8},{8,0},{16,24},{24,16},{1,9},{9,1},{17,25},{25,17},{2,10},{10... | collective-permute-start | bytes 786440 | tf_op jit(solution)/shard_map/ppermute | solution.py:22
  114.5 5.0 %collective-permute-start.19 = (bf16[256,256]{1,0:T(8,128)(2,1)S(1)}, bf16[256,256]{1,0:T(8,128)(2,1)S(1)}, u32[]{:S(2)}, u32[]{:S(2)}) collective-permute-start(bf16[256,256]{1,0:T(8,128)(2,1)S(1)} %multiply_convert_fusion.2), channel_id=1, source_target_pairs={{0,2},{1,3},{2,0},{3,1},{4,6},{5,7},{6,4},{7,5},{8,10},{9,11},{10,... | collective-permute-start | bytes 393224 | tf_op jit(solution)/shard_map/ppermute | solution.py:22
  116.2 12.1 %collective-permute-start.21 = (bf16[128,1024]{1,0:T(8,128)(2,1)S(1)}, bf16[128,1024]{1,0:T(8,128)(2,1)S(1)}, u32[]{:S(2)}, u32[]{:S(2)}) collective-permute-start(bf16[128,1024]{1,0:T(8,128)(2,1)S(1)} %add_convert_fusion), channel_id=1, source_target_pairs={{0,8},{8,0},{16,24},{24,16},{1,9},{9,1},{17,25},{25,17},{2,10},{10... | collective-permute-start | bytes 786440 | tf_op jit(solution)/shard_map/ppermute | solution.py:22
  119.6 4.0 %collective-permute-start.22 = (bf16[512,256]{1,0:T(8,128)(2,1)S(1)}, bf16[512,256]{1,0:T(8,128)(2,1)S(1)}, u32[]{:S(2)}, u32[]{:S(2)}) collective-permute-start(bf16[512,256]{1,0:T(8,128)(2,1)S(1)} %pad_maximum_fusion.3), channel_id=1, source_target_pairs={{0,1},{1,0},{2,3},{3,2},{4,5},{5,4},{6,7},{7,6},{8,9},{9,8},{10,11... | collective-permute-start | bytes 786440 | tf_op jit(solution)/shard_map/ppermute | solution.py:22
  124.6 6.7 %collective-permute-start.23 = (bf16[256,256]{1,0:T(8,128)(2,1)S(1)}, bf16[256,256]{1,0:T(8,128)(2,1)S(1)}, u32[]{:S(2)}, u32[]{:S(2)}) collective-permute-start(bf16[256,256]{1,0:T(8,128)(2,1)S(1)} %dynamic-slice_convert_fusion.3), channel_id=1, source_target_pairs={{0,8},{8,0},{16,24},{24,16},{1,9},{9,1},{17,25},{25,17},{2,10},{10... | collective-permute-start | bytes 393224 | tf_op jit(solution)/shard_map/ppermute | solution.py:22
  126.4 8.8 %collective-permute-start.27 = (bf16[256,256]{1,0:T(8,128)(2,1)S(1)}, bf16[256,256]{1,0:T(8,128)(2,1)S(1)}, u32[]{:S(2)}, u32[]{:S(2)}) collective-permute-start(bf16[256,256]{1,0:T(8,128)(2,1)S(1)} %dynamic-slice_convert_fusion.4), channel_id=1, source_target_pairs={{0,8},{8,0},{16,24},{24,16},{1,9},{9,1},{17,25},{25,17},{2,10},{10... | collective-permute-start | bytes 393224 | tf_op jit(solution)/shard_map/ppermute | solution.py:22
  129.8 7.8 %collective-permute-start.26 = (f32[64,2048]{1,0:T(8,128)S(1)}, f32[64,2048]{1,0:T(8,128)S(1)}, u32[]{:S(2)}, u32[]{:S(2)}) collective-permute-start(f32[64,2048]{1,0:T(8,128)S(1)} %constant_dynamic-slice_fusion), channel_id=1, source_target_pairs={{0,1},{1,0},{2,3},{3,2},{4,5},{5,4},{6,7},{7,6},{8,9},{9,8},{10,11... | collective-permute-start | bytes 1572872 | tf_op jit(solution)/shard_map/ppermute | solution.py:22
  129.9 9.2 %collective-permute-start.25 = (f32[64,2048]{1,0:T(8,128)S(1)}, f32[64,2048]{1,0:T(8,128)S(1)}, u32[]{:S(2)}, u32[]{:S(2)}) collective-permute-start(f32[64,2048]{1,0:T(8,128)S(1)} %constant_dynamic-slice_fusion.1), channel_id=1, source_target_pairs={{0,1},{1,0},{2,3},{3,2},{4,5},{5,4},{6,7},{7,6},{8,9},{9,8},{10,11... | collective-permute-start | bytes 1572872 | tf_op jit(solution)/shard_map/ppermute | solution.py:22
  131.3 21.7 %collective-permute-start.24 = (bf16[256,256]{1,0:T(8,128)(2,1)S(1)}, bf16[256,256]{1,0:T(8,128)(2,1)S(1)}, u32[]{:S(2)}, u32[]{:S(2)}) collective-permute-start(bf16[256,256]{1,0:T(8,128)(2,1)S(1)} %add_convert_fusion.9), channel_id=1, source_target_pairs={{0,16},{8,24},{16,0},{24,8},{1,17},{9,25},{17,1},{25,9},{2,18},{10... | collective-permute-start | bytes 393224 | tf_op jit(solution)/shard_map/ppermute | solution.py:22
  135.2 17.9 %collective-permute-start.35 = (bf16[256,256]{1,0:T(8,128)(2,1)S(1)}, bf16[256,256]{1,0:T(8,128)(2,1)S(1)}, u32[]{:S(2)}, u32[]{:S(2)}) collective-permute-start(bf16[256,256]{1,0:T(8,128)(2,1)S(1)} %add_convert_fusion.8), channel_id=1, source_target_pairs={{0,16},{8,24},{16,0},{24,8},{1,17},{9,25},{17,1},{25,9},{2,18},{10... | collective-permute-start | bytes 393224 | tf_op jit(solution)/shard_map/ppermute | solution.py:22
  137.7 5.0 %collective-permute-start.29 = (bf16[32,2048]{1,0:T(8,128)(2,1)S(1)}, bf16[32,2048]{1,0:T(8,128)(2,1)S(1)}, u32[]{:S(2)}, u32[]{:S(2)}) collective-permute-start(bf16[32,2048]{1,0:T(8,128)(2,1)S(1)} %dynamic-slice_convert_fusion.2), channel_id=1, source_target_pairs={{0,2},{1,3},{2,0},{3,1},{4,6},{5,7},{6,4},{7,5},{8,10},{9,11},{10,... | collective-permute-start | bytes 393224 | tf_op jit(solution)/shard_map/ppermute | solution.py:22
  139.3 5.7 %collective-permute-start.28 = (bf16[32,2048]{1,0:T(8,128)(2,1)S(1)}, bf16[32,2048]{1,0:T(8,128)(2,1)S(1)}, u32[]{:S(2)}, u32[]{:S(2)}) collective-permute-start(bf16[32,2048]{1,0:T(8,128)(2,1)S(1)} %dynamic-slice_convert_fusion.1), channel_id=1, source_target_pairs={{0,4},{1,5},{2,6},{3,7},{4,0},{5,1},{6,2},{7,3},{8,12},{9,13},{10,... | collective-permute-start | bytes 393224 | tf_op jit(solution)/shard_map/ppermute | solution.py:22
  142.8 5.0 %collective-permute-start.31 = (bf16[32,2048]{1,0:T(8,128)(2,1)S(1)}, bf16[32,2048]{1,0:T(8,128)(2,1)S(1)}, u32[]{:S(2)}, u32[]{:S(2)}) collective-permute-start(bf16[32,2048]{1,0:T(8,128)(2,1)S(1)} %add_convert_fusion.7), channel_id=1, source_target_pairs={{0,4},{1,5},{2,6},{3,7},{4,0},{5,1},{6,2},{7,3},{8,12},{9,13},{10,... | collective-permute-start | bytes 393224 | tf_op jit(solution)/shard_map/ppermute | solution.py:22
  145.0 6.3 %collective-permute-start.30 = (bf16[32,2048]{1,0:T(8,128)(2,1)S(1)}, bf16[32,2048]{1,0:T(8,128)(2,1)S(1)}, u32[]{:S(2)}, u32[]{:S(2)}) collective-permute-start(bf16[32,2048]{1,0:T(8,128)(2,1)S(1)} %add_convert_fusion.6), channel_id=1, source_target_pairs={{0,2},{1,3},{2,0},{3,1},{4,6},{5,7},{6,4},{7,5},{8,10},{9,11},{10,... | collective-permute-start | bytes 393224 | tf_op jit(solution)/shard_map/ppermute | solution.py:22
  147.9 7.4 %collective-permute-start.34 = (bf16[32,2048]{1,0:T(8,128)(2,1)S(1)}, bf16[32,2048]{1,0:T(8,128)(2,1)S(1)}, u32[]{:S(2)}, u32[]{:S(2)}) collective-permute-start(bf16[32,2048]{1,0:T(8,128)(2,1)S(1)} %add_convert_fusion.5), channel_id=1, source_target_pairs={{0,2},{1,3},{2,0},{3,1},{4,6},{5,7},{6,4},{7,5},{8,10},{9,11},{10,... | collective-permute-start | bytes 393224 | tf_op jit(solution)/shard_map/ppermute | solution.py:22
  151.4 5.0 %collective-permute-start.33 = (bf16[32,2048]{1,0:T(8,128)(2,1)S(1)}, bf16[32,2048]{1,0:T(8,128)(2,1)S(1)}, u32[]{:S(2)}, u32[]{:S(2)}) collective-permute-start(bf16[32,2048]{1,0:T(8,128)(2,1)S(1)} %add_convert_fusion.4), channel_id=1, source_target_pairs={{0,4},{1,5},{2,6},{3,7},{4,0},{5,1},{6,2},{7,3},{8,12},{9,13},{10,... | collective-permute-start | bytes 393224 | tf_op jit(solution)/shard_map/ppermute | solution.py:22
  153.1 5.0 %collective-permute-start.32 = (bf16[256,256]{1,0:T(8,128)(2,1)S(1)}, bf16[256,256]{1,0:T(8,128)(2,1)S(1)}, u32[]{:S(2)}, u32[]{:S(2)}) collective-permute-start(bf16[256,256]{1,0:T(8,128)(2,1)S(1)} %add_convert_fusion.3), channel_id=1, source_target_pairs={{0,8},{8,0},{16,24},{24,16},{1,9},{9,1},{17,25},{25,17},{2,10},{10... | collective-permute-start | bytes 393224 | tf_op jit(solution)/shard_map/ppermute | solution.py:22
  153.2 6.3 %collective-permute-start.36 = (bf16[256,256]{1,0:T(8,128)(2,1)S(1)}, bf16[256,256]{1,0:T(8,128)(2,1)S(1)}, u32[]{:S(2)}, u32[]{:S(2)}) collective-permute-start(bf16[256,256]{1,0:T(8,128)(2,1)S(1)} %add_convert_fusion.2), channel_id=1, source_target_pairs={{0,8},{8,0},{16,24},{24,16},{1,9},{9,1},{17,25},{25,17},{2,10},{10... | collective-permute-start | bytes 393224 | tf_op jit(solution)/shard_map/ppermute | solution.py:22
  155.3 5.3 %collective-permute-start.37 = (bf16[64,2048]{1,0:T(8,128)(2,1)S(1)}, bf16[64,2048]{1,0:T(8,128)(2,1)S(1)}, u32[]{:S(2)}, u32[]{:S(2)}) collective-permute-start(bf16[64,2048]{1,0:T(8,128)(2,1)S(1)} %pad_maximum_fusion.4), channel_id=1, source_target_pairs={{0,1},{1,0},{2,3},{3,2},{4,5},{5,4},{6,7},{7,6},{8,9},{9,8},{10,11... | collective-permute-start | bytes 786440 | tf_op jit(solution)/shard_map/ppermute | solution.py:22
  156.5 4.1 %collective-permute-start.38 = (bf16[64,2048]{1,0:T(8,128)(2,1)S(1)}, bf16[64,2048]{1,0:T(8,128)(2,1)S(1)}, u32[]{:S(2)}, u32[]{:S(2)}) collective-permute-start(bf16[64,2048]{1,0:T(8,128)(2,1)S(1)} %pad_maximum_fusion.5), channel_id=1, source_target_pairs={{0,1},{1,0},{2,3},{3,2},{4,5},{5,4},{6,7},{7,6},{8,9},{9,8},{10,11... | collective-permute-start | bytes 786440 | tf_op jit(solution)/shard_map/ppermute | solution.py:22
  (14 other events, 49.4 us)

commit v10 on v8

--- a/solution.py
+++ b/solution.py
@@ -452,6 +452,7 @@
     devices = range(group_count)
     top_rows = line.put(line.after(target_logits[:8]))
     incoming = lax.ppermute(top_rows, "grp", [(i + 1, i) for i in devices if i + 1 in devices])
+    vocab[1].step()
     pre_part = line.put(
         jnp.dot(line.after(hidden_states), down_weight, preferred_element_type=F32)
     )
@@ -465,27 +466,25 @@
         line, pre_part * PRE_SCALE, v_bits, [F16] * len(v_bits), activate
     )
     pre.step()
-    line.put(sent[1])
     incoming = line.put(line.after(incoming))
     vocab[0].step()
-    vocab[1].step()
     pre.step()
     vocab[1].step()
     pre.step()
-    vocab[0].step()
     if per_book == 1:
-        prob, entropy = target_pass(target_logits, line.after(incoming))
+        prob, entropy = target_pass(line.after(target_logits), incoming)
     else:
         top, total = target_sums(target_logits, incoming)
         top, total = over_books((top, total), merge_sums, per_book)
         prob, entropy = target_probs(target_logits, incoming, top, total)
     line.put(entropy)
     label = lax.dynamic_slice_in_dim(labels, book_index, 1, 1) - book_part * slice_cols
+    vocab[0].step()
     pre.step()
     vocab[1].step()
+    pre.step()
     vocab[0].result()
     line.put(vocab_pieces[0][1])
-    pre.step()
     acts = line.put(all_acts())
 
     drafts, vocab_proj, sums = [], [], None

time: 152 us -> 148 us (0.974)
  waiting for transfers between devices: 37.4 us -> 33.8 us
  other arithmetic: 10.1 us -> 12 us
  starting transfers between devices: 43.6 us -> 41.9 us
    ppermute x38, waiting for transfers between devices: 37.4 us -> 33.8 us  [swap(): return lax.ppermute(value, axis, pairs)]
    convert_element_type x2, other arithmetic: 0.95 us -> 2.84 us  [on_device(): (total * (1.0 / VOCAB_SCALE)).astype(BF16)]
    ppermute x38, starting transfers between devices: 42.3 us -> 40.6 us  [swap(): return lax.ppermute(value, axis, pairs)]
    unnamed x59 -> x57, local copies, waits for them, and re-layouts: 10.1 us -> 10.8 us
  transfers between devices with their start and end apart: 39 -> 39, of which waited for: 17 -> 16; matrix products, arithmetic and copies ran while one was open for 23% -> 24% of each run, Pallas kernels for 7% -> 7%
where the time goes in v10:
time: 148 us; the launch traced here: 147 us
  starting transfers between devices  41.9 us (28%)
  waiting for transfers between devices  33.8 us (23%)
  matrix products  25.9 us (18%)
  Pallas kernels  18.9 us (13%)
  local copies, waits for them, and re-layouts  13.5 us (9%)
  other arithmetic  12 us (8%)
    ppermute x38, starting transfers between devices, swap(): return lax.ppermute(value, axis, pairs)  40.6 us
    ppermute x38, waiting for transfers between devices, swap(): return lax.ppermute(value, axis, pairs)  33.8 us
    dot_general x4, matrix products, on_device(): jnp.dot(part, columns(c), preferred_element_type=F32) * VOCAB_SCALE  13.8 us
    unnamed x57, local copies, waits for them, and re-layouts  10.8 us
    dot_general x4, matrix products, inner_cols(): lax.dot_general(left, right, (((1,), (1,)), ((), ())), preferred_element_...  10.6 us
    pallas_call x2, Pallas kernels, grad_chunk(): pl.pallas_call(body, grid=(rows // block,), in_specs=[row_spec(block, wid...  8.28 us
    pallas_call x2, Pallas kernels, draft_chunk(): pl.pallas_call(body, grid=(rows // block,), in_specs=[row_spec(block, wid...  6.57 us
    pallas_call x1, Pallas kernels, target_pass(): pl.pallas_call(body, grid=(rows // block,), in_specs=[row_spec(block, col...  4.01 us
  transfers between devices with their start and end apart: 39, of which 16 were waited for; matrix products, arithmetic and copies ran while one was open for 24% of the time, Pallas kernels for 7%

profile of v10, /device:TPU:0, one launch (start us, length us, event | category | flops | bytes accessed | tf_op | source)
XLA Modules:
  0.0 147.4 jit_solution(2225110483595473106)
XLA Ops:
  0.7 3.9 %fusion.34 = f16[128,1024]{1,0:T(8,128)(2,1)} fusion(bf16[2048,2048]{1,0:T(8,128)(2,1)} %param.11, bf16[256,2048]{1,0:T(8,128)(2,1)} %param.10, s32[]{:T(128)S(6)} %select_n.175), kind=kOutput, calls=%fused_computation.22 | convolution fusion | flops 537133056 | bytes 4980740 | tf_op jit(solution)/shard_map/dot_general | solution.py:441
  4.6 3.0 %collective-permute-start.1 = (f16[128,1024]{1,0:T(8,128)(2,1)}, f16[128,1024]{1,0:T(8,128)(2,1)}, u32[]{:S(2)}, u32[]{:S(2)}) collective-permute-start(f16[128,1024]{1,0:T(8,128)(2,1)} %fusion.34), channel_id=1, source_target_pairs={{0,8},{8,0},{16,24},{24,16},{1,9},{9,1},{17,25},{25,17},{2,10},{10... | collective-permute-start | bytes 786440 | tf_op jit(solution)/shard_map/ppermute | solution.py:22
  8.5 1.3 collective-permute-start.2
  9.8 3.6 %fusion.37 = f16[128,1024]{1,0:T(8,128)(2,1)} fusion(bf16[2048,2048]{1,0:T(8,128)(2,1)} %param.11, bf16[256,2048]{1,0:T(8,128)(2,1)S(1)} %copy-done.19, s32[]{:T(128)S(6)} %select_n.175), kind=kOutput, calls=%fused_computation.23 | convolution fusion | flops 537133056 | bytes 4980740 | tf_op jit(solution)/shard_map/dot_general | solution.py:441
  13.4 2.6 %collective-permute-start.4 = (f16[128,1024]{1,0:T(8,128)(2,1)}, f16[128,1024]{1,0:T(8,128)(2,1)}, u32[]{:S(2)}, u32[]{:S(2)}) collective-permute-start(f16[128,1024]{1,0:T(8,128)(2,1)} %fusion.37), channel_id=1, source_target_pairs={{0,8},{8,0},{16,24},{24,16},{1,9},{9,1},{17,25},{25,17},{2,10},{10... | collective-permute-start | bytes 786440 | tf_op jit(solution)/shard_map/ppermute | solution.py:22
  17.5 3.3 %fusion.44 = (f16[128,1024]{1,0:T(8,128)(2,1)S(1)}, f32[128,1024]{1,0:T(8,128)S(1)}) fusion(f16[128,1024]{1,0:T(8,128)(2,1)} %collective-permute-done.1, bf16[2048,2048]{1,0:T(8,128)(2,1)} %param.11, bf16[256,2048]{1,0:T(8,128)(2,1)} %param.10, s32[]{:T(128)S(6)} %select_n.178), kind=kOutput, calls=%fused_computation.49 | convolution fusion | flops 537395200 | bytes 5767172 | tf_op jit(solution)/shard_map/dot_general | solution.py:441
  20.9 2.7 %collective-permute-start.6 = (f16[128,1024]{1,0:T(8,128)(2,1)S(1)}, f16[128,1024]{1,0:T(8,128)(2,1)S(1)}, u32[]{:S(2)}, u32[]{:S(2)}) collective-permute-start(f16[128,1024]{1,0:T(8,128)(2,1)S(1)} %get-tuple-element.112), channel_id=1, source_target_pairs={{0,16},{8,24},{16,0},{24,8},{1,17},{9,25},{17,1},{25,9},{2,18},{10... | collective-permute-start | bytes 786440 | tf_op jit(solution)/shard_map/ppermute | solution.py:22
  24.6 1.6 %collective-permute-start.3 = (f16[256,256]{1,0:T(8,128)(2,1)S(1)}, f16[256,256]{1,0:T(8,128)(2,1)S(1)}, u32[]{:S(2)}, u32[]{:S(2)}) collective-permute-start(f16[256,256]{1,0:T(8,128)(2,1)S(1)} %dynamic-slice_convert_fusion.6), channel_id=1, source_target_pairs={{0,2},{1,3},{2,0},{3,1},{4,6},{5,7},{6,4},{7,5},{8,10},{9,11},{10,... | collective-permute-start | bytes 393224 | tf_op jit(solution)/shard_map/ppermute | solution.py:22
  26.1 3.0 %fusion.45 = (f16[128,1024]{1,0:T(8,128)(2,1)S(1)}, f32[128,1024]{1,0:T(8,128)S(1)}) fusion(f16[128,1024]{1,0:T(8,128)(2,1)} %collective-permute-done.4, bf16[2048,2048]{1,0:T(8,128)(2,1)} %param.11, bf16[256,2048]{1,0:T(8,128)(2,1)S(1)} %copy-done.20, s32[]{:T(128)S(6)} %select_n.178), kind=kOutput, calls=%fused_computation.50 | convolution fusion | flops 537395200 | bytes 5767172 | tf_op jit(solution)/shard_map/dot_general | solution.py:441
  30.3 1.6 %collective-permute-start.5 = (f16[256,256]{1,0:T(8,128)(2,1)S(1)}, f16[256,256]{1,0:T(8,128)(2,1)S(1)}, u32[]{:S(2)}, u32[]{:S(2)}) collective-permute-start(f16[256,256]{1,0:T(8,128)(2,1)S(1)} %fusion.49), channel_id=1, source_target_pairs={{0,4},{1,5},{2,6},{3,7},{4,0},{5,1},{6,2},{7,3},{8,12},{9,13},{10,... | collective-permute-start | bytes 393224 | tf_op jit(solution)/shard_map/ppermute | solution.py:22
  31.9 4.0 %target_pass.1 = (f32[1024,2048]{1,0:T(8,128)S(1)}, f32[1024,1]{1,0:T(8,128)S(1)}) custom-call(f32[1024,2048]{1,0:T(8,128)S(1)} %bitcast.9, f32[1024,2048]{1,0:T(8,128)S(1)} %bitcast.9, f32[8,2048]{1,0:T(8,128)S(1)} %collective-permute-done.2.incoming_ref), custom_call_target="tpu_custom_call" | custom-call | flops 3072 | bytes 4096 | tf_op jit(solution)/shard_map/target_pass/pallas_call | solution.py:132
  35.9 3.3 %copy-done.2 = f32[1024,2048]{1,0:T(8,128)} copy-done((f32[1024,2048]{1,0:T(8,128)}, f32[1024,2048]{1,0:T(8,128)S(1)}, u32[]{:S(2)}) %copy-start.2) | copy-done | bytes 8388632
  40.1 1.2 collective-permute-done.6
  42.6 1.6 %collective-permute-start.7 = (bf16[256,256]{1,0:T(8,128)(2,1)S(1)}, bf16[256,256]{1,0:T(8,128)(2,1)S(1)}, u32[]{:S(2)}, u32[]{:S(2)}) collective-permute-start(bf16[256,256]{1,0:T(8,128)(2,1)S(1)} %multiply_convert_fusion.3), channel_id=1, source_target_pairs={{0,2},{1,3},{2,0},{3,1},{4,6},{5,7},{6,4},{7,5},{8,10},{9,11},{10,... | collective-permute-start | bytes 393224 | tf_op jit(solution)/shard_map/ppermute | solution.py:22
  44.2 2.7 %collective-permute-done.8 = f16[128,1024]{1,0:T(8,128)(2,1)S(1)} collective-permute-done((f16[128,1024]{1,0:T(8,128)(2,1)S(1)}, f16[128,1024]{1,0:T(8,128)(2,1)S(1)}, u32[]{:S(2)}, u32[]{:S(2)}) %collective-permute-start.8) | collective-permute-done | bytes 262176 | tf_op jit(solution)/shard_map/ppermute | solution.py:22
  46.9 1.8 %multiply_convert_fusion.own_ref = bf16[128,1024]{1,0:T(8,128)(2,1)} fusion(f16[128,1024]{1,0:T(8,128)(2,1)S(1)} %collective-permute-done.8, f32[128,1024]{1,0:T(8,128)S(1)} %get-tuple-element.238, f16[128,1024]{1,0:T(8,128)(2,1)} %collective-permute-done.4), kind=kLoop, calls=%fused_computation.36 | loop fusion | flops 786432 | bytes 1310720 | tf_op jit(solution)/shard_map/convert_element_type | solution.py:448
  50.7 1.8 %collective-permute-done.10.other_ref = bf16[128,1024]{1,0:T(8,128)(2,1)S(1)} collective-permute-done((bf16[128,1024]{1,0:T(8,128)(2,1)S(1)}, bf16[128,1024]{1,0:T(8,128)(2,1)S(1)}, u32[]{:S(2)}, u32[]{:S(2)}) %collective-permute-start.10) | collective-permute-done | bytes 262176 | tf_op jit(solution)/shard_map/ppermute | solution.py:22
  53.4 3.4 %copy-done.1 = f32[1024,2048]{1,0:T(8,128)S(1)} copy-done((f32[1024,2048]{1,0:T(8,128)S(1)}, f32[1024,2048]{1,0:T(8,128)}, u32[]{:S(2)}) %copy-start.1) | copy-done | bytes 8388632
  57.8 2.5 %draft_chunk.2 = (f32[1024,1024]{1,0:T(8,128)S(1)}, bf16[256,1024]{1,0:T(8,128)(2,1)S(1)}, f32[1024,1]{1,0:T(8,128)S(1)}, f32[1024,1]{1,0:T(8,128)S(1)}) custom-call(f32[1024,2048]{1,0:T(8,128)S(1)} %copy-done.1, bf16[1024,256]{1,0:T(8,128)(2,1)S(1)} %pad_maximum_fusion.acts_ref, bf16[128,1024]{1,0:T(8,128)(2,1)S(1)} %multiply_convert_fusion.1.own_ref, ...), custom_call_target="tpu_custom_call" | custom-call | flops 131072 | bytes 2048 | tf_op jit(solution)/shard_map/draft_chunk/pallas_call | solution.py:220
  60.3 4.1 %draft_chunk.3 = (f32[1024,1024]{1,0:T(8,128)S(1)}, bf16[256,1024]{1,0:T(8,128)(2,1)S(1)}, f32[1024,1]{1,0:T(8,128)S(1)}, f32[1024,1]{1,0:T(8,128)S(1)}) custom-call(f32[1024,2048]{1,0:T(8,128)S(1)} %copy-done.1, bf16[1024,256]{1,0:T(8,128)(2,1)S(1)} %pad_maximum_fusion.acts_ref, bf16[128,1024]{1,0:T(8,128)(2,1)} %multiply_convert_fusion.own_ref, ...), custom_call_target="tpu_custom_call" | custom-call | flops 131072 | bytes 2048 | tf_op jit(solution)/shard_map/draft_chunk/pallas_call | solution.py:220
  64.4 4.1 %grad_chunk.2 = (bf16[128,1024]{1,0:T(8,128)(2,1)S(1)}, f32[128,1024]{1,0:T(8,128)S(1)}, f32[1024,256]{1,0:T(8,128)S(1)}, f32[1024,1]{1,0:T(8,128)S(1)}) custom-call(f32[1024,1024]{1,0:T(8,128)S(1)} %get-tuple-element.136.draft_ref, f32[1024,2048]{1,0:T(8,128)S(1)} %bitcast.11, s32[1024,1]{1,0:T(8,128)S(1)} %copy.11.label_ref, ...), custom_call_target="tpu_custom_call" | custom-call | flops 262144 | bytes 2048 | tf_op jit(solution)/shard_map/grad_chunk/pallas_call | solution.py:292
  68.6 4.2 %grad_chunk.3 = (bf16[128,1024]{1,0:T(8,128)(2,1)S(1)}, f32[128,1024]{1,0:T(8,128)S(1)}, f32[1024,256]{1,0:T(8,128)S(1)}, f32[1024,1]{1,0:T(8,128)S(1)}) custom-call(f32[1024,1024]{1,0:T(8,128)S(1)} %get-tuple-element.142.draft_ref, f32[1024,2048]{1,0:T(8,128)S(1)} %bitcast.11, s32[1024,1]{1,0:T(8,128)S(1)} %copy.11.label_ref, ...), custom_call_target="tpu_custom_call" | custom-call | flops 262144 | bytes 2048 | tf_op jit(solution)/shard_map/grad_chunk/pallas_call | solution.py:292
  74.4 2.4 %collective-permute-done.12 = bf16[128,1024]{1,0:T(8,128)(2,1)S(1)} collective-permute-done((bf16[128,1024]{1,0:T(8,128)(2,1)S(1)}, bf16[128,1024]{1,0:T(8,128)(2,1)S(1)}, u32[]{:S(2)}, u32[]{:S(2)}) %collective-permute-start.12) | collective-permute-done | bytes 262176 | tf_op jit(solution)/shard_map/ppermute | solution.py:22
  77.8 2.9 %collective-permute-start.13 = (bf16[128,1024]{1,0:T(8,128)(2,1)S(1)}, bf16[128,1024]{1,0:T(8,128)(2,1)S(1)}, u32[]{:S(2)}, u32[]{:S(2)}) collective-permute-start(bf16[128,1024]{1,0:T(8,128)(2,1)S(1)} %fusion.46), channel_id=1, source_target_pairs={{0,16},{8,24},{16,0},{24,8},{1,17},{9,25},{17,1},{25,9},{2,18},{10... | collective-permute-start | bytes 786440 | tf_op jit(solution)/shard_map/ppermute | solution.py:22
  81.8 1.6 %collective-permute-start.15 = (bf16[256,256]{1,0:T(8,128)(2,1)S(1)}, bf16[256,256]{1,0:T(8,128)(2,1)S(1)}, u32[]{:S(2)}, u32[]{:S(2)}) collective-permute-start(bf16[256,256]{1,0:T(8,128)(2,1)S(1)} %dynamic-slice_convert_fusion.5), channel_id=1, source_target_pairs={{0,2},{1,3},{2,0},{3,1},{4,6},{5,7},{6,4},{7,5},{8,10},{9,11},{10,... | collective-permute-start | bytes 393224 | tf_op jit(solution)/shard_map/ppermute | solution.py:22
  83.4 8.7 %collective-permute-done.16 = bf16[128,1024]{1,0:T(8,128)(2,1)S(1)} collective-permute-done((bf16[128,1024]{1,0:T(8,128)(2,1)}, bf16[128,1024]{1,0:T(8,128)(2,1)S(1)}, u32[]{:S(2)}, u32[]{:S(2)}) %collective-permute-start.16) | collective-permute-done | bytes 262176 | tf_op jit(solution)/shard_map/ppermute | solution.py:22
  92.3 1.6 %collective-permute-start.18 = (bf16[256,256]{1,0:T(8,128)(2,1)S(1)}, bf16[256,256]{1,0:T(8,128)(2,1)S(1)}, u32[]{:S(2)}, u32[]{:S(2)}) collective-permute-start(bf16[256,256]{1,0:T(8,128)(2,1)S(1)} %fusion.48), channel_id=1, source_target_pairs={{0,4},{1,5},{2,6},{3,7},{4,0},{5,1},{6,2},{7,3},{8,12},{9,13},{10,... | collective-permute-start | bytes 393224 | tf_op jit(solution)/shard_map/ppermute | solution.py:22
  93.8 1.2 add_convert_fusion.1
  95.1 2.1 %collective-permute-start.17 = (bf16[128,1024]{1,0:T(8,128)(2,1)S(1)}, bf16[128,1024]{1,0:T(8,128)(2,1)S(1)}, u32[]{:S(2)}, u32[]{:S(2)}) collective-permute-start(bf16[128,1024]{1,0:T(8,128)(2,1)S(1)} %add_convert_fusion.1), channel_id=1, source_target_pairs={{0,8},{8,0},{16,24},{24,16},{1,9},{9,1},{17,25},{25,17},{2,10},{10... | collective-permute-start | bytes 786440 | tf_op jit(solution)/shard_map/ppermute | solution.py:22
  97.1 3.7 %fusion.2 = f32[128,2048]{1,0:T(8,128)S(1)} fusion(bf16[128,1024]{1,0:T(8,128)(2,1)S(1)} %add_convert_fusion.1, bf16[2048,2048]{1,0:T(8,128)(2,1)} %param.11), kind=kOutput, calls=%fused_computation.2 | convolution fusion | flops 536870912 | bytes 5505024 | tf_op jit(solution)/shard_map/dot_general | solution.py:44
  101.1 1.6 %collective-permute-start.19 = (bf16[256,256]{1,0:T(8,128)(2,1)S(1)}, bf16[256,256]{1,0:T(8,128)(2,1)S(1)}, u32[]{:S(2)}, u32[]{:S(2)}) collective-permute-start(bf16[256,256]{1,0:T(8,128)(2,1)S(1)} %multiply_convert_fusion.2), channel_id=1, source_target_pairs={{0,2},{1,3},{2,0},{3,1},{4,6},{5,7},{6,4},{7,5},{8,10},{9,11},{10,... | collective-permute-start | bytes 393224 | tf_op jit(solution)/shard_map/ppermute | solution.py:22
  102.6 3.2 %collective-permute-done.20 = bf16[128,1024]{1,0:T(8,128)(2,1)S(1)} collective-permute-done((bf16[128,1024]{1,0:T(8,128)(2,1)S(1)}, bf16[128,1024]{1,0:T(8,128)(2,1)S(1)}, u32[]{:S(2)}, u32[]{:S(2)}) %collective-permute-start.20) | collective-permute-done | bytes 262176 | tf_op jit(solution)/shard_map/ppermute | solution.py:22
  106.2 2.1 %collective-permute-done.17 = bf16[128,1024]{1,0:T(8,128)(2,1)S(1)} collective-permute-done((bf16[128,1024]{1,0:T(8,128)(2,1)S(1)}, bf16[128,1024]{1,0:T(8,128)(2,1)S(1)}, u32[]{:S(2)}, u32[]{:S(2)}) %collective-permute-start.17) | collective-permute-done | bytes 262176 | tf_op jit(solution)/shard_map/ppermute | solution.py:22
  108.3 3.8 %fusion = f32[128,2048]{1,0:T(8,128)S(1)} fusion(bf16[128,1024]{1,0:T(8,128)(2,1)S(1)} %collective-permute-done.17, bf16[2048,2048]{1,0:T(8,128)(2,1)} %param.11), kind=kOutput, calls=%fused_computation | convolution fusion | flops 536870912 | bytes 5505024 | tf_op jit(solution)/shard_map/dot_general | solution.py:44
  113.3 2.0 %collective-permute-start.27 = (bf16[256,256]{1,0:T(8,128)(2,1)S(1)}, bf16[256,256]{1,0:T(8,128)(2,1)S(1)}, u32[]{:S(2)}, u32[]{:S(2)}) collective-permute-start(bf16[256,256]{1,0:T(8,128)(2,1)S(1)} %dynamic-slice_convert_fusion.4), channel_id=1, source_target_pairs={{0,8},{8,0},{16,24},{24,16},{1,9},{9,1},{17,25},{25,17},{2,10},{10... | collective-permute-start | bytes 393224 | tf_op jit(solution)/shard_map/ppermute | solution.py:22
  115.3 1.5 %fusion.16 = f32[128,2048]{1,0:T(8,128)S(1)} fusion(f32[128,2048]{1,0:T(8,128)S(1)} %fusion.2, bf16[128,1024]{1,0:T(8,128)(2,1)S(1)} %add_convert_fusion, bf16[2048,2048]{1,0:T(8,128)(2,1)S(1)} %bitcast.13), kind=kOutput, calls=%fused_computation.16 | convolution fusion | flops 537133056 | bytes 6553600 | tf_op jit(solution)/shard_map/dot_general | solution.py:44
  116.9 1.5 %broadcast_select_fusion = (f32[128,2048]{1,0:T(8,128)S(1)}, f32[128,2048]{1,0:T(8,128)S(1)}) fusion(f32[128,2048]{1,0:T(8,128)S(1)} %fusion.16, pred[]{:T(512)S(6)} %eq.12, f32[128,2048]{1,0:T(8,128)S(1)} %fusion, bf16[128,1024]{1,0:T(8,128)(2,1)S(1)} %collective-permute-done.21, bf16[2048,2048]{1,0:T(8,128)(2,1)S(1)} %bitcast.13), kind=kOutput, calls=%fused_computation.43 | convolution fusion | flops 537657344 | bytes 8650753 | tf_op jit(solution)/shard_map/dot_general | solution.py:44
  121.1 2.0 %collective-permute-start.35 = (bf16[256,256]{1,0:T(8,128)(2,1)S(1)}, bf16[256,256]{1,0:T(8,128)(2,1)S(1)}, u32[]{:S(2)}, u32[]{:S(2)}) collective-permute-start(bf16[256,256]{1,0:T(8,128)(2,1)S(1)} %add_convert_fusion.8), channel_id=1, source_target_pairs={{0,16},{8,24},{16,0},{24,8},{1,17},{9,25},{17,1},{25,9},{2,18},{10... | collective-permute-start | bytes 393224 | tf_op jit(solution)/shard_map/ppermute | solution.py:22
  123.2 1.6 %collective-permute-start.29 = (bf16[32,2048]{1,0:T(8,128)(2,1)S(1)}, bf16[32,2048]{1,0:T(8,128)(2,1)S(1)}, u32[]{:S(2)}, u32[]{:S(2)}) collective-permute-start(bf16[32,2048]{1,0:T(8,128)(2,1)S(1)} %dynamic-slice_convert_fusion.2), channel_id=1, source_target_pairs={{0,2},{1,3},{2,0},{3,1},{4,6},{5,7},{6,4},{7,5},{8,10},{9,11},{10,... | collective-permute-start | bytes 393224 | tf_op jit(solution)/shard_map/ppermute | solution.py:22
  125.9 2.3 %collective-permute-done.29 = bf16[32,2048]{1,0:T(8,128)(2,1)S(1)} collective-permute-done((bf16[32,2048]{1,0:T(8,128)(2,1)S(1)}, bf16[32,2048]{1,0:T(8,128)(2,1)S(1)}, u32[]{:S(2)}, u32[]{:S(2)}) %collective-permute-start.29) | collective-permute-done | bytes 131104 | tf_op jit(solution)/shard_map/ppermute | solution.py:22
  130.9 2.4 %collective-permute-done.31 = bf16[32,2048]{1,0:T(8,128)(2,1)S(1)} collective-permute-done((bf16[32,2048]{1,0:T(8,128)(2,1)S(1)}, bf16[32,2048]{1,0:T(8,128)(2,1)S(1)}, u32[]{:S(2)}, u32[]{:S(2)}) %collective-permute-start.31) | collective-permute-done | bytes 131104 | tf_op jit(solution)/shard_map/ppermute | solution.py:22
  133.3 1.6 %collective-permute-start.34 = (bf16[32,2048]{1,0:T(8,128)(2,1)S(1)}, bf16[32,2048]{1,0:T(8,128)(2,1)S(1)}, u32[]{:S(2)}, u32[]{:S(2)}) collective-permute-start(bf16[32,2048]{1,0:T(8,128)(2,1)S(1)} %add_convert_fusion.5), channel_id=1, source_target_pairs={{0,2},{1,3},{2,0},{3,1},{4,6},{5,7},{6,4},{7,5},{8,10},{9,11},{10,... | collective-permute-start | bytes 393224 | tf_op jit(solution)/shard_map/ppermute | solution.py:22
  134.9 1.6 %collective-permute-done.30 = bf16[32,2048]{1,0:T(8,128)(2,1)S(1)} collective-permute-done((bf16[32,2048]{1,0:T(8,128)(2,1)S(1)}, bf16[32,2048]{1,0:T(8,128)(2,1)S(1)}, u32[]{:S(2)}, u32[]{:S(2)}) %collective-permute-start.30) | collective-permute-done | bytes 131104 | tf_op jit(solution)/shard_map/ppermute | solution.py:22
  136.5 1.5 %collective-permute-start.33 = (bf16[32,2048]{1,0:T(8,128)(2,1)S(1)}, bf16[32,2048]{1,0:T(8,128)(2,1)S(1)}, u32[]{:S(2)}, u32[]{:S(2)}) collective-permute-start(bf16[32,2048]{1,0:T(8,128)(2,1)S(1)} %add_convert_fusion.4), channel_id=1, source_target_pairs={{0,4},{1,5},{2,6},{3,7},{4,0},{5,1},{6,2},{7,3},{8,12},{9,13},{10,... | collective-permute-start | bytes 393224 | tf_op jit(solution)/shard_map/ppermute | solution.py:22
  138.3 2.0 %collective-permute-start.36 = (bf16[256,256]{1,0:T(8,128)(2,1)S(1)}, bf16[256,256]{1,0:T(8,128)(2,1)S(1)}, u32[]{:S(2)}, u32[]{:S(2)}) collective-permute-start(bf16[256,256]{1,0:T(8,128)(2,1)S(1)} %add_convert_fusion.2), channel_id=1, source_target_pairs={{0,8},{8,0},{16,24},{24,16},{1,9},{9,1},{17,25},{25,17},{2,10},{10... | collective-permute-start | bytes 393224 | tf_op jit(solution)/shard_map/ppermute | solution.py:22
  141.7 1.4 collective-permute-done.32
  143.1 1.4 collective-permute-done.36
  145.8 1.6 %maximum_convert_fusion = f32[256,2048]{1,0:T(8,128)} fusion(bf16[64,2048]{1,0:T(8,128)(2,1)S(1)} %get-tuple-element.216, bf16[64,2048]{1,0:T(8,128)(2,1)S(1)} %get-tuple-element.215, bf16[64,2048]{1,0:T(8,128)(2,1)S(1)} %get-tuple-element.240, bf16[64,2048]{1,0:T(8,128)(2,1)S(1)} %get-tuple-element.241), kind=kLoop, calls=%fused_computation.24 | loop fusion | flops 4194304 | bytes 3145728 | tf_op jit(solution)/shard_map/concatenate | solution.py:563
  (156 shorter events, 25.8 us)
Async XLA Ops:
  0.6 15.4 %copy-start = (bf16[1024,1024]{1,0:T(8,128)(2,1)S(1)}, bf16[1024,1024]{1,0:T(8,128)(2,1)}, u32[]{:S(2)}) copy-start(bf16[1024,1024]{1,0:T(8,128)(2,1)} %param.6) | copy-start | bytes 6291460
  0.6 9.1 %copy-start.19 = (bf16[256,2048]{1,0:T(8,128)(2,1)S(1)}, bf16[256,2048]{1,0:T(8,128)(2,1)}, u32[]{:S(2)}) copy-start(bf16[256,2048]{1,0:T(8,128)(2,1)} %param.10) | copy-start | bytes 3145732
  4.6 11.4 %copy-start.21 = (bf16[1024,256]{1,0:T(8,128)(2,1)S(1)}, bf16[1024,256]{1,0:T(8,128)(2,1)}, u32[]{:S(2)}) copy-start(bf16[1024,256]{1,0:T(8,128)(2,1)} %param.9) | copy-start | bytes 1572868
  4.6 12.9 %collective-permute-start.1 = (f16[128,1024]{1,0:T(8,128)(2,1)}, f16[128,1024]{1,0:T(8,128)(2,1)}, u32[]{:S(2)}, u32[]{:S(2)}) collective-permute-start(f16[128,1024]{1,0:T(8,128)(2,1)} %fusion.34), channel_id=1, source_target_pairs={{0,8},{8,0},{16,24},{24,16},{1,9},{9,1},{17,25},{25,17},{2,10},{10... | collective-permute-start | bytes 786440 | tf_op jit(solution)/shard_map/ppermute | solution.py:22
  8.5 9.0 %collective-permute-start.2 = (f32[8,2048]{1,0:T(8,128)S(1)}, f32[8,2048]{1,0:T(8,128)S(1)}, u32[]{:S(2)}, u32[]{:S(2)}) collective-permute-start(f32[8,2048]{1,0:T(8,128)S(1)} %slice.22), channel_id=1, source_target_pairs={{8,0},{16,8},{24,16},{9,1},{17,9},{25,17},{10,2},{18,10},{26,18},{... | collective-permute-start | bytes 196616 | tf_op jit(solution)/shard_map/ppermute | solution.py:454
  13.4 12.8 %collective-permute-start.4 = (f16[128,1024]{1,0:T(8,128)(2,1)}, f16[128,1024]{1,0:T(8,128)(2,1)}, u32[]{:S(2)}, u32[]{:S(2)}) collective-permute-start(f16[128,1024]{1,0:T(8,128)(2,1)} %fusion.37), channel_id=1, source_target_pairs={{0,8},{8,0},{16,24},{24,16},{1,9},{9,1},{17,25},{25,17},{2,10},{10... | collective-permute-start | bytes 786440 | tf_op jit(solution)/shard_map/ppermute | solution.py:22
  17.5 6.0 %collective-permute-start = (f16[512,256]{1,0:T(8,128)(2,1)}, f16[512,256]{1,0:T(8,128)(2,1)}, u32[]{:S(2)}, u32[]{:S(2)}) collective-permute-start(f16[512,256]{1,0:T(8,128)(2,1)} %dynamic-slice_convert_fusion), channel_id=1, source_target_pairs={{0,1},{1,0},{2,3},{3,2},{4,5},{5,4},{6,7},{7,6},{8,9},{9,8},{10,11... | collective-permute-start | bytes 786440 | tf_op jit(solution)/shard_map/ppermute | solution.py:22
  17.5 14.4 %slice-start = ((s8[8388608]{0:T(1024)(128)(4,1)}), s8[4194304]{0:T(1024)(128)(4,1)S(1)}, s32[]{:S(2)}) async-start(s8[8388608]{0:T(1024)(128)(4,1)} %bitcast.8), calls=%async_computation | async-start | bytes 8388608
  20.8 11.0 %slice-start.1 = ((s8[8388608]{0:T(1024)(128)(4,1)}), s8[4194304]{0:T(1024)(128)(4,1)S(1)}, s32[]{:S(2)}) async-start(s8[8388608]{0:T(1024)(128)(4,1)} %bitcast.8), calls=%async_computation.1 | async-start | bytes 8388608
  20.9 20.4 %collective-permute-start.6 = (f16[128,1024]{1,0:T(8,128)(2,1)S(1)}, f16[128,1024]{1,0:T(8,128)(2,1)S(1)}, u32[]{:S(2)}, u32[]{:S(2)}) collective-permute-start(f16[128,1024]{1,0:T(8,128)(2,1)S(1)} %get-tuple-element.112), channel_id=1, source_target_pairs={{0,16},{8,24},{16,0},{24,8},{1,17},{9,25},{17,1},{25,9},{2,18},{10... | collective-permute-start | bytes 786440 | tf_op jit(solution)/shard_map/ppermute | solution.py:22
  24.5 18.0 %copy-start.14 = (f32[512,256]{1,0:T(8,128)}, f32[512,256]{1,0:T(8,128)S(1)}, u32[]{:S(2)}) copy-start(f32[512,256]{1,0:T(8,128)S(1)} %convert_add_fusion.3) | copy-start | bytes 1572868
  24.6 5.7 %collective-permute-start.3 = (f16[256,256]{1,0:T(8,128)(2,1)S(1)}, f16[256,256]{1,0:T(8,128)(2,1)S(1)}, u32[]{:S(2)}, u32[]{:S(2)}) collective-permute-start(f16[256,256]{1,0:T(8,128)(2,1)S(1)} %dynamic-slice_convert_fusion.6), channel_id=1, source_target_pairs={{0,2},{1,3},{2,0},{3,1},{4,6},{5,7},{6,4},{7,5},{8,10},{9,11},{10,... | collective-permute-start | bytes 393224 | tf_op jit(solution)/shard_map/ppermute | solution.py:22
  29.1 17.8 %collective-permute-start.8 = (f16[128,1024]{1,0:T(8,128)(2,1)S(1)}, f16[128,1024]{1,0:T(8,128)(2,1)S(1)}, u32[]{:S(2)}, u32[]{:S(2)}) collective-permute-start(f16[128,1024]{1,0:T(8,128)(2,1)S(1)} %get-tuple-element.116), channel_id=1, source_target_pairs={{0,16},{8,24},{16,0},{24,8},{1,17},{9,25},{17,1},{25,9},{2,18},{10... | collective-permute-start | bytes 786440 | tf_op jit(solution)/shard_map/ppermute | solution.py:22
  30.3 12.2 %collective-permute-start.5 = (f16[256,256]{1,0:T(8,128)(2,1)S(1)}, f16[256,256]{1,0:T(8,128)(2,1)S(1)}, u32[]{:S(2)}, u32[]{:S(2)}) collective-permute-start(f16[256,256]{1,0:T(8,128)(2,1)S(1)} %fusion.49), channel_id=1, source_target_pairs={{0,4},{1,5},{2,6},{3,7},{4,0},{5,1},{6,2},{7,3},{8,12},{9,13},{10,... | collective-permute-start | bytes 393224 | tf_op jit(solution)/shard_map/ppermute | solution.py:22
  42.3 10.1 %collective-permute-start.10 = (bf16[128,1024]{1,0:T(8,128)(2,1)S(1)}, bf16[128,1024]{1,0:T(8,128)(2,1)S(1)}, u32[]{:S(2)}, u32[]{:S(2)}) collective-permute-start(bf16[128,1024]{1,0:T(8,128)(2,1)S(1)} %multiply_convert_fusion.1.own_ref), channel_id=1, source_target_pairs={{0,8},{8,0},{16,24},{24,16},{1,9},{9,1},{17,25},{25,17},{2,10},{10... | collective-permute-start | bytes 786440 | tf_op jit(solution)/shard_map/ppermute | solution.py:22
  42.6 6.1 %collective-permute-start.7 = (bf16[256,256]{1,0:T(8,128)(2,1)S(1)}, bf16[256,256]{1,0:T(8,128)(2,1)S(1)}, u32[]{:S(2)}, u32[]{:S(2)}) collective-permute-start(bf16[256,256]{1,0:T(8,128)(2,1)S(1)} %multiply_convert_fusion.3), channel_id=1, source_target_pairs={{0,2},{1,3},{2,0},{3,1},{4,6},{5,7},{6,4},{7,5},{8,10},{9,11},{10,... | collective-permute-start | bytes 393224 | tf_op jit(solution)/shard_map/ppermute | solution.py:22
  48.8 3.7 %collective-permute-start.9 = (bf16[512,256]{1,0:T(8,128)(2,1)S(1)}, bf16[512,256]{1,0:T(8,128)(2,1)S(1)}, u32[]{:S(2)}, u32[]{:S(2)}) collective-permute-start(bf16[512,256]{1,0:T(8,128)(2,1)S(1)} %pad_maximum_fusion.2), channel_id=1, source_target_pairs={{0,1},{1,0},{2,3},{3,2},{4,5},{5,4},{6,7},{7,6},{8,9},{9,8},{10,11... | collective-permute-start | bytes 786440 | tf_op jit(solution)/shard_map/ppermute | solution.py:22
  49.6 10.6 %collective-permute-start.11 = (bf16[128,1024]{1,0:T(8,128)(2,1)}, bf16[128,1024]{1,0:T(8,128)(2,1)}, u32[]{:S(2)}, u32[]{:S(2)}) collective-permute-start(bf16[128,1024]{1,0:T(8,128)(2,1)} %multiply_convert_fusion.own_ref), channel_id=1, source_target_pairs={{0,8},{8,0},{16,24},{24,16},{1,9},{9,1},{17,25},{25,17},{2,10},{10... | collective-permute-start | bytes 786440 | tf_op jit(solution)/shard_map/ppermute | solution.py:22
  68.5 8.3 %collective-permute-start.12 = (bf16[128,1024]{1,0:T(8,128)(2,1)S(1)}, bf16[128,1024]{1,0:T(8,128)(2,1)S(1)}, u32[]{:S(2)}, u32[]{:S(2)}) collective-permute-start(bf16[128,1024]{1,0:T(8,128)(2,1)S(1)} %get-tuple-element.141), channel_id=1, source_target_pairs={{0,8},{8,0},{16,24},{24,16},{1,9},{9,1},{17,25},{25,17},{2,10},{10... | collective-permute-start | bytes 786440 | tf_op jit(solution)/shard_map/ppermute | solution.py:22
  73.6 18.4 %copy-start.4 = (f32[128,1024]{1,0:T(8,128)S(1)}, f32[128,1024]{1,0:T(8,128)}, u32[]{:S(2)}) copy-start(f32[128,1024]{1,0:T(8,128)} %copy-done.3) | copy-start | bytes 1572868
  77.5 3.2 %collective-permute-start.14 = (f32[512,256]{1,0:T(8,128)}, f32[512,256]{1,0:T(8,128)S(1)}, u32[]{:S(2)}, u32[]{:S(2)}) collective-permute-start(f32[512,256]{1,0:T(8,128)} %constant_dynamic-slice_fusion.2), channel_id=1, source_target_pairs={{0,1},{1,0},{2,3},{3,2},{4,5},{5,4},{6,7},{7,6},{8,9},{9,8},{10,11... | collective-permute-start | bytes 1572872 | tf_op jit(solution)/shard_map/ppermute | solution.py:22
  77.5 14.5 %collective-permute-start.16 = (bf16[128,1024]{1,0:T(8,128)(2,1)}, bf16[128,1024]{1,0:T(8,128)(2,1)S(1)}, u32[]{:S(2)}, u32[]{:S(2)}) collective-permute-start(bf16[128,1024]{1,0:T(8,128)(2,1)} %copy-done.13), channel_id=1, source_target_pairs={{0,8},{8,0},{16,24},{24,16},{1,9},{9,1},{17,25},{25,17},{2,10},{10... | collective-permute-start | bytes 786440 | tf_op jit(solution)/shard_map/ppermute | solution.py:22
  77.8 16.0 %collective-permute-start.13 = (bf16[128,1024]{1,0:T(8,128)(2,1)S(1)}, bf16[128,1024]{1,0:T(8,128)(2,1)S(1)}, u32[]{:S(2)}, u32[]{:S(2)}) collective-permute-start(bf16[128,1024]{1,0:T(8,128)(2,1)S(1)} %fusion.46), channel_id=1, source_target_pairs={{0,16},{8,24},{16,0},{24,8},{1,17},{9,25},{17,1},{25,9},{2,18},{10... | collective-permute-start | bytes 786440 | tf_op jit(solution)/shard_map/ppermute | solution.py:22
  81.8 10.4 %collective-permute-start.15 = (bf16[256,256]{1,0:T(8,128)(2,1)S(1)}, bf16[256,256]{1,0:T(8,128)(2,1)S(1)}, u32[]{:S(2)}, u32[]{:S(2)}) collective-permute-start(bf16[256,256]{1,0:T(8,128)(2,1)S(1)} %dynamic-slice_convert_fusion.5), channel_id=1, source_target_pairs={{0,2},{1,3},{2,0},{3,1},{4,6},{5,7},{6,4},{7,5},{8,10},{9,11},{10,... | collective-permute-start | bytes 393224 | tf_op jit(solution)/shard_map/ppermute | solution.py:22
  92.0 8.8 %copy-start.15 = (f32[512,256]{1,0:T(8,128)S(1)}, f32[512,256]{1,0:T(8,128)}, u32[]{:S(2)}) copy-start(f32[512,256]{1,0:T(8,128)} %copy-done.14) | copy-start | bytes 1572868
  92.1 8.8 %copy-start.18 = (f16[256,256]{1,0:T(8,128)(2,1)S(1)}, f16[256,256]{1,0:T(8,128)(2,1)}, u32[]{:S(2)}) copy-start(f16[256,256]{1,0:T(8,128)(2,1)} %copy-done.17) | copy-start | bytes 393220
  92.1 13.7 %collective-permute-start.20 = (bf16[128,1024]{1,0:T(8,128)(2,1)S(1)}, bf16[128,1024]{1,0:T(8,128)(2,1)S(1)}, u32[]{:S(2)}, u32[]{:S(2)}) collective-permute-start(bf16[128,1024]{1,0:T(8,128)(2,1)S(1)} %fusion.47), channel_id=1, source_target_pairs={{0,16},{8,24},{16,0},{24,8},{1,17},{9,25},{17,1},{25,9},{2,18},{10... | collective-permute-start | bytes 786440 | tf_op jit(solution)/shard_map/ppermute | solution.py:22
  92.3 8.6 %collective-permute-start.18 = (bf16[256,256]{1,0:T(8,128)(2,1)S(1)}, bf16[256,256]{1,0:T(8,128)(2,1)S(1)}, u32[]{:S(2)}, u32[]{:S(2)}) collective-permute-start(bf16[256,256]{1,0:T(8,128)(2,1)S(1)} %fusion.48), channel_id=1, source_target_pairs={{0,4},{1,5},{2,6},{3,7},{4,0},{5,1},{6,2},{7,3},{8,12},{9,13},{10,... | collective-permute-start | bytes 393224 | tf_op jit(solution)/shard_map/ppermute | solution.py:22
  95.1 13.2 %collective-permute-start.17 = (bf16[128,1024]{1,0:T(8,128)(2,1)S(1)}, bf16[128,1024]{1,0:T(8,128)(2,1)S(1)}, u32[]{:S(2)}, u32[]{:S(2)}) collective-permute-start(bf16[128,1024]{1,0:T(8,128)(2,1)S(1)} %add_convert_fusion.1), channel_id=1, source_target_pairs={{0,8},{8,0},{16,24},{24,16},{1,9},{9,1},{17,25},{25,17},{2,10},{10... | collective-permute-start | bytes 786440 | tf_op jit(solution)/shard_map/ppermute | solution.py:22
  101.1 5.0 %collective-permute-start.19 = (bf16[256,256]{1,0:T(8,128)(2,1)S(1)}, bf16[256,256]{1,0:T(8,128)(2,1)S(1)}, u32[]{:S(2)}, u32[]{:S(2)}) collective-permute-start(bf16[256,256]{1,0:T(8,128)(2,1)S(1)} %multiply_convert_fusion.2), channel_id=1, source_target_pairs={{0,2},{1,3},{2,0},{3,1},{4,6},{5,7},{6,4},{7,5},{8,10},{9,11},{10,... | collective-permute-start | bytes 393224 | tf_op jit(solution)/shard_map/ppermute | solution.py:22
  106.0 10.9 %collective-permute-start.21 = (bf16[128,1024]{1,0:T(8,128)(2,1)S(1)}, bf16[128,1024]{1,0:T(8,128)(2,1)S(1)}, u32[]{:S(2)}, u32[]{:S(2)}) collective-permute-start(bf16[128,1024]{1,0:T(8,128)(2,1)S(1)} %add_convert_fusion), channel_id=1, source_target_pairs={{0,8},{8,0},{16,24},{24,16},{1,9},{9,1},{17,25},{25,17},{2,10},{10... | collective-permute-start | bytes 786440 | tf_op jit(solution)/shard_map/ppermute | solution.py:22
  106.2 6.0 %collective-permute-start.22 = (bf16[512,256]{1,0:T(8,128)(2,1)S(1)}, bf16[512,256]{1,0:T(8,128)(2,1)S(1)}, u32[]{:S(2)}, u32[]{:S(2)}) collective-permute-start(bf16[512,256]{1,0:T(8,128)(2,1)S(1)} %pad_maximum_fusion.3), channel_id=1, source_target_pairs={{0,1},{1,0},{2,3},{3,2},{4,5},{5,4},{6,7},{7,6},{8,9},{9,8},{10,11... | collective-permute-start | bytes 786440 | tf_op jit(solution)/shard_map/ppermute | solution.py:22
  113.2 6.8 %collective-permute-start.23 = (bf16[256,256]{1,0:T(8,128)(2,1)S(1)}, bf16[256,256]{1,0:T(8,128)(2,1)S(1)}, u32[]{:S(2)}, u32[]{:S(2)}) collective-permute-start(bf16[256,256]{1,0:T(8,128)(2,1)S(1)} %dynamic-slice_convert_fusion.3), channel_id=1, source_target_pairs={{0,8},{8,0},{16,24},{24,16},{1,9},{9,1},{17,25},{25,17},{2,10},{10... | collective-permute-start | bytes 393224 | tf_op jit(solution)/shard_map/ppermute | solution.py:22
  113.3 7.8 %collective-permute-start.27 = (bf16[256,256]{1,0:T(8,128)(2,1)S(1)}, bf16[256,256]{1,0:T(8,128)(2,1)S(1)}, u32[]{:S(2)}, u32[]{:S(2)}) collective-permute-start(bf16[256,256]{1,0:T(8,128)(2,1)S(1)} %dynamic-slice_convert_fusion.4), channel_id=1, source_target_pairs={{0,8},{8,0},{16,24},{24,16},{1,9},{9,1},{17,25},{25,17},{2,10},{10... | collective-permute-start | bytes 393224 | tf_op jit(solution)/shard_map/ppermute | solution.py:22
  118.5 4.6 %collective-permute-start.26 = (f32[64,2048]{1,0:T(8,128)S(1)}, f32[64,2048]{1,0:T(8,128)S(1)}, u32[]{:S(2)}, u32[]{:S(2)}) collective-permute-start(f32[64,2048]{1,0:T(8,128)S(1)} %constant_dynamic-slice_fusion), channel_id=1, source_target_pairs={{0,1},{1,0},{2,3},{3,2},{4,5},{5,4},{6,7},{7,6},{8,9},{9,8},{10,11... | collective-permute-start | bytes 1572872 | tf_op jit(solution)/shard_map/ppermute | solution.py:22
  118.6 6.2 %collective-permute-start.25 = (f32[64,2048]{1,0:T(8,128)S(1)}, f32[64,2048]{1,0:T(8,128)S(1)}, u32[]{:S(2)}, u32[]{:S(2)}) collective-permute-start(f32[64,2048]{1,0:T(8,128)S(1)} %constant_dynamic-slice_fusion.1), channel_id=1, source_target_pairs={{0,1},{1,0},{2,3},{3,2},{4,5},{5,4},{6,7},{7,6},{8,9},{9,8},{10,11... | collective-permute-start | bytes 1572872 | tf_op jit(solution)/shard_map/ppermute | solution.py:22
  120.0 18.0 %collective-permute-start.24 = (bf16[256,256]{1,0:T(8,128)(2,1)S(1)}, bf16[256,256]{1,0:T(8,128)(2,1)S(1)}, u32[]{:S(2)}, u32[]{:S(2)}) collective-permute-start(bf16[256,256]{1,0:T(8,128)(2,1)S(1)} %add_convert_fusion.9), channel_id=1, source_target_pairs={{0,16},{8,24},{16,0},{24,8},{1,17},{9,25},{17,1},{25,9},{2,18},{10... | collective-permute-start | bytes 393224 | tf_op jit(solution)/shard_map/ppermute | solution.py:22
  121.1 17.2 %collective-permute-start.35 = (bf16[256,256]{1,0:T(8,128)(2,1)S(1)}, bf16[256,256]{1,0:T(8,128)(2,1)S(1)}, u32[]{:S(2)}, u32[]{:S(2)}) collective-permute-start(bf16[256,256]{1,0:T(8,128)(2,1)S(1)} %add_convert_fusion.8), channel_id=1, source_target_pairs={{0,16},{8,24},{16,0},{24,8},{1,17},{9,25},{17,1},{25,9},{2,18},{10... | collective-permute-start | bytes 393224 | tf_op jit(solution)/shard_map/ppermute | solution.py:22
  123.2 5.0 %collective-permute-start.29 = (bf16[32,2048]{1,0:T(8,128)(2,1)S(1)}, bf16[32,2048]{1,0:T(8,128)(2,1)S(1)}, u32[]{:S(2)}, u32[]{:S(2)}) collective-permute-start(bf16[32,2048]{1,0:T(8,128)(2,1)S(1)} %dynamic-slice_convert_fusion.2), channel_id=1, source_target_pairs={{0,2},{1,3},{2,0},{3,1},{4,6},{5,7},{6,4},{7,5},{8,10},{9,11},{10,... | collective-permute-start | bytes 393224 | tf_op jit(solution)/shard_map/ppermute | solution.py:22
  124.9 5.4 %collective-permute-start.28 = (bf16[32,2048]{1,0:T(8,128)(2,1)S(1)}, bf16[32,2048]{1,0:T(8,128)(2,1)S(1)}, u32[]{:S(2)}, u32[]{:S(2)}) collective-permute-start(bf16[32,2048]{1,0:T(8,128)(2,1)S(1)} %dynamic-slice_convert_fusion.1), channel_id=1, source_target_pairs={{0,4},{1,5},{2,6},{3,7},{4,0},{5,1},{6,2},{7,3},{8,12},{9,13},{10,... | collective-permute-start | bytes 393224 | tf_op jit(solution)/shard_map/ppermute | solution.py:22
  128.3 5.0 %collective-permute-start.31 = (bf16[32,2048]{1,0:T(8,128)(2,1)S(1)}, bf16[32,2048]{1,0:T(8,128)(2,1)S(1)}, u32[]{:S(2)}, u32[]{:S(2)}) collective-permute-start(bf16[32,2048]{1,0:T(8,128)(2,1)S(1)} %add_convert_fusion.7), channel_id=1, source_target_pairs={{0,4},{1,5},{2,6},{3,7},{4,0},{5,1},{6,2},{7,3},{8,12},{9,13},{10,... | collective-permute-start | bytes 393224 | tf_op jit(solution)/shard_map/ppermute | solution.py:22
  130.3 6.2 %collective-permute-start.30 = (bf16[32,2048]{1,0:T(8,128)(2,1)S(1)}, bf16[32,2048]{1,0:T(8,128)(2,1)S(1)}, u32[]{:S(2)}, u32[]{:S(2)}) collective-permute-start(bf16[32,2048]{1,0:T(8,128)(2,1)S(1)} %add_convert_fusion.6), channel_id=1, source_target_pairs={{0,2},{1,3},{2,0},{3,1},{4,6},{5,7},{6,4},{7,5},{8,10},{9,11},{10,... | collective-permute-start | bytes 393224 | tf_op jit(solution)/shard_map/ppermute | solution.py:22
  133.3 6.9 %collective-permute-start.34 = (bf16[32,2048]{1,0:T(8,128)(2,1)S(1)}, bf16[32,2048]{1,0:T(8,128)(2,1)S(1)}, u32[]{:S(2)}, u32[]{:S(2)}) collective-permute-start(bf16[32,2048]{1,0:T(8,128)(2,1)S(1)} %add_convert_fusion.5), channel_id=1, source_target_pairs={{0,2},{1,3},{2,0},{3,1},{4,6},{5,7},{6,4},{7,5},{8,10},{9,11},{10,... | collective-permute-start | bytes 393224 | tf_op jit(solution)/shard_map/ppermute | solution.py:22
  136.5 5.0 %collective-permute-start.33 = (bf16[32,2048]{1,0:T(8,128)(2,1)S(1)}, bf16[32,2048]{1,0:T(8,128)(2,1)S(1)}, u32[]{:S(2)}, u32[]{:S(2)}) collective-permute-start(bf16[32,2048]{1,0:T(8,128)(2,1)S(1)} %add_convert_fusion.4), channel_id=1, source_target_pairs={{0,4},{1,5},{2,6},{3,7},{4,0},{5,1},{6,2},{7,3},{8,12},{9,13},{10,... | collective-permute-start | bytes 393224 | tf_op jit(solution)/shard_map/ppermute | solution.py:22
  138.1 5.0 %collective-permute-start.32 = (bf16[256,256]{1,0:T(8,128)(2,1)S(1)}, bf16[256,256]{1,0:T(8,128)(2,1)S(1)}, u32[]{:S(2)}, u32[]{:S(2)}) collective-permute-start(bf16[256,256]{1,0:T(8,128)(2,1)S(1)} %add_convert_fusion.3), channel_id=1, source_target_pairs={{0,8},{8,0},{16,24},{24,16},{1,9},{9,1},{17,25},{25,17},{2,10},{10... | collective-permute-start | bytes 393224 | tf_op jit(solution)/shard_map/ppermute | solution.py:22
  138.3 6.2 %collective-permute-start.36 = (bf16[256,256]{1,0:T(8,128)(2,1)S(1)}, bf16[256,256]{1,0:T(8,128)(2,1)S(1)}, u32[]{:S(2)}, u32[]{:S(2)}) collective-permute-start(bf16[256,256]{1,0:T(8,128)(2,1)S(1)} %add_convert_fusion.2), channel_id=1, source_target_pairs={{0,8},{8,0},{16,24},{24,16},{1,9},{9,1},{17,25},{25,17},{2,10},{10... | collective-permute-start | bytes 393224 | tf_op jit(solution)/shard_map/ppermute | solution.py:22
  140.3 5.3 %collective-permute-start.37 = (bf16[64,2048]{1,0:T(8,128)(2,1)S(1)}, bf16[64,2048]{1,0:T(8,128)(2,1)S(1)}, u32[]{:S(2)}, u32[]{:S(2)}) collective-permute-start(bf16[64,2048]{1,0:T(8,128)(2,1)S(1)} %pad_maximum_fusion.4), channel_id=1, source_target_pairs={{0,1},{1,0},{2,3},{3,2},{4,5},{5,4},{6,7},{7,6},{8,9},{9,8},{10,11... | collective-permute-start | bytes 786440 | tf_op jit(solution)/shard_map/ppermute | solution.py:22
  141.6 4.0 %collective-permute-start.38 = (bf16[64,2048]{1,0:T(8,128)(2,1)S(1)}, bf16[64,2048]{1,0:T(8,128)(2,1)S(1)}, u32[]{:S(2)}, u32[]{:S(2)}) collective-permute-start(bf16[64,2048]{1,0:T(8,128)(2,1)S(1)} %pad_maximum_fusion.5), channel_id=1, source_target_pairs={{0,1},{1,0},{2,3},{3,2},{4,5},{5,4},{6,7},{7,6},{8,9},{9,8},{10,11... | collective-permute-start | bytes 786440 | tf_op jit(solution)/shard_map/ppermute | solution.py:22
  (19 other events, 69.0 us)

commit v11 on v10

--- a/solution.py
+++ b/solution.py
@@ -64,7 +64,7 @@
 
 
 def cost(flops, read, exps):
-    return pl.CostEstimate(flops=flops // 4096, bytes_accessed=read // 4096, transcendentals=0)
+    return pl.CostEstimate(flops=flops // 4096, bytes_accessed=read, transcendentals=0)
 
 
 def row_spec(block, cols, column=0):
@@ -528,7 +528,7 @@
     own = first_of(grads[1], grad_pieces[1])
     act.step()
     grads[0].result()
-    other_up = times_head(0.0, grad_pieces[0][1], 0)
+    line.put(grad_pieces[0][1])
     pre_grad = line.put(all_pre_grad())
     down_part = line.put(inner_rows(line.after(hidden_states), pre_grad))
     rows = down_part.shape[0] // 2
@@ -543,6 +543,7 @@
     downs[0].step()
     downs[1].step()
     own_up = times_head(own_up, own, 1)
+    other_up = times_head(0.0, grad_pieces[0][1], 0)
     grads[1].result()
     other_up = times_head(other_up, grad_pieces[1][1], 1)
     up_part = joined("grp", z_bits[0], own_up, other_up)

time: 148 us -> 150 us (1.014)
  local copies, waits for them, and re-layouts: 13.5 us -> 11.3 us
  waiting for transfers between devices: 33.8 us -> 35.7 us
  starting transfers between devices: 41.9 us -> 43.4 us
    ppermute x38, waiting for transfers between devices: 33.8 us -> 35.7 us  [swap(): return lax.ppermute(value, axis, pairs)]
    unnamed x57 -> x51, local copies, waits for them, and re-layouts: 10.8 us -> 9.41 us
  transfers between devices with their start and end apart: 39 -> 39, of which waited for: 16 -> 16; matrix products, arithmetic and copies ran while one was open for 24% -> 23% of each run, Pallas kernels for 7% -> 7%
where the time goes in v11:
time: 150 us; the launch traced here: 149 us
  starting transfers between devices  43.4 us (29%)
  waiting for transfers between devices  35.7 us (24%)
  matrix products  25.5 us (17%)
  Pallas kernels  18.9 us (13%)
  other arithmetic  12.9 us (9%)
  local copies, waits for them, and re-layouts  11.3 us (8%)
    ppermute x38, starting transfers between devices, swap(): return lax.ppermute(value, axis, pairs)  42.1 us
    ppermute x38, waiting for transfers between devices, swap(): return lax.ppermute(value, axis, pairs)  35.7 us
    dot_general x4, matrix products, on_device(): jnp.dot(part, columns(c), preferred_element_type=F32) * VOCAB_SCALE  13.9 us
    dot_general x4, matrix products, inner_cols(): lax.dot_general(left, right, (((1,), (1,)), ((), ())), preferred_element_...  10.2 us
    unnamed x51, local copies, waits for them, and re-layouts  9.41 us
    pallas_call x2, Pallas kernels, grad_chunk(): pl.pallas_call(body, grid=(rows // block,), in_specs=[row_spec(block, wid...  8.31 us
    pallas_call x2, Pallas kernels, draft_chunk(): pl.pallas_call(body, grid=(rows // block,), in_specs=[row_spec(block, wid...  6.57 us
    pallas_call x1, Pallas kernels, target_pass(): pl.pallas_call(body, grid=(rows // block,), in_specs=[row_spec(block, col...  4.01 us
  transfers between devices with their start and end apart: 39, of which 16 were waited for; matrix products, arithmetic and copies ran while one was open for 23% of the time, Pallas kernels for 7%

profile of v11, /device:TPU:0, one launch (start us, length us, event | category | flops | bytes accessed | tf_op | source)
XLA Modules:
  0.0 149.0 jit_solution(9332635827022316208)
XLA Ops:
  0.7 3.9 %fusion.34 = f16[128,1024]{1,0:T(8,128)(2,1)} fusion(bf16[2048,2048]{1,0:T(8,128)(2,1)} %param.11, bf16[256,2048]{1,0:T(8,128)(2,1)} %param.10, s32[]{:T(128)S(6)} %select_n.175), kind=kOutput, calls=%fused_computation.22 | convolution fusion | flops 537133056 | bytes 4980740 | tf_op jit(solution)/shard_map/dot_general | solution.py:441
  4.6 3.0 %collective-permute-start.1 = (f16[128,1024]{1,0:T(8,128)(2,1)}, f16[128,1024]{1,0:T(8,128)(2,1)}, u32[]{:S(2)}, u32[]{:S(2)}) collective-permute-start(f16[128,1024]{1,0:T(8,128)(2,1)} %fusion.34), channel_id=1, source_target_pairs={{0,8},{8,0},{16,24},{24,16},{1,9},{9,1},{17,25},{25,17},{2,10},{10... | collective-permute-start | bytes 786440 | tf_op jit(solution)/shard_map/ppermute | solution.py:22
  8.5 1.3 collective-permute-start.2
  9.8 3.6 %fusion.37 = f16[128,1024]{1,0:T(8,128)(2,1)} fusion(bf16[2048,2048]{1,0:T(8,128)(2,1)} %param.11, bf16[256,2048]{1,0:T(8,128)(2,1)S(1)} %copy-done.14, s32[]{:T(128)S(6)} %select_n.175), kind=kOutput, calls=%fused_computation.23 | convolution fusion | flops 537133056 | bytes 4980740 | tf_op jit(solution)/shard_map/dot_general | solution.py:441
  13.4 2.6 %collective-permute-start.4 = (f16[128,1024]{1,0:T(8,128)(2,1)}, f16[128,1024]{1,0:T(8,128)(2,1)}, u32[]{:S(2)}, u32[]{:S(2)}) collective-permute-start(f16[128,1024]{1,0:T(8,128)(2,1)} %fusion.37), channel_id=1, source_target_pairs={{0,8},{8,0},{16,24},{24,16},{1,9},{9,1},{17,25},{25,17},{2,10},{10... | collective-permute-start | bytes 786440 | tf_op jit(solution)/shard_map/ppermute | solution.py:22
  17.5 3.3 %fusion.44 = (f16[128,1024]{1,0:T(8,128)(2,1)S(1)}, f32[128,1024]{1,0:T(8,128)S(1)}) fusion(f16[128,1024]{1,0:T(8,128)(2,1)} %collective-permute-done.1, bf16[2048,2048]{1,0:T(8,128)(2,1)} %param.11, bf16[256,2048]{1,0:T(8,128)(2,1)} %param.10, s32[]{:T(128)S(6)} %select_n.178), kind=kOutput, calls=%fused_computation.49 | convolution fusion | flops 537395200 | bytes 5767172 | tf_op jit(solution)/shard_map/dot_general | solution.py:441
  20.9 2.7 %collective-permute-start.6 = (f16[128,1024]{1,0:T(8,128)(2,1)S(1)}, f16[128,1024]{1,0:T(8,128)(2,1)S(1)}, u32[]{:S(2)}, u32[]{:S(2)}) collective-permute-start(f16[128,1024]{1,0:T(8,128)(2,1)S(1)} %get-tuple-element.112), channel_id=1, source_target_pairs={{0,16},{8,24},{16,0},{24,8},{1,17},{9,25},{17,1},{25,9},{2,18},{10... | collective-permute-start | bytes 786440 | tf_op jit(solution)/shard_map/ppermute | solution.py:22
  24.6 1.6 %collective-permute-start.3 = (f16[256,256]{1,0:T(8,128)(2,1)S(1)}, f16[256,256]{1,0:T(8,128)(2,1)S(1)}, u32[]{:S(2)}, u32[]{:S(2)}) collective-permute-start(f16[256,256]{1,0:T(8,128)(2,1)S(1)} %dynamic-slice_convert_fusion.6), channel_id=1, source_target_pairs={{0,2},{1,3},{2,0},{3,1},{4,6},{5,7},{6,4},{7,5},{8,10},{9,11},{10,... | collective-permute-start | bytes 393224 | tf_op jit(solution)/shard_map/ppermute | solution.py:22
  26.1 3.0 %fusion.45 = (f16[128,1024]{1,0:T(8,128)(2,1)S(1)}, f32[128,1024]{1,0:T(8,128)S(1)}) fusion(f16[128,1024]{1,0:T(8,128)(2,1)} %collective-permute-done.4, bf16[2048,2048]{1,0:T(8,128)(2,1)} %param.11, bf16[256,2048]{1,0:T(8,128)(2,1)S(1)} %copy-done.15, s32[]{:T(128)S(6)} %select_n.178), kind=kOutput, calls=%fused_computation.50 | convolution fusion | flops 537395200 | bytes 5767172 | tf_op jit(solution)/shard_map/dot_general | solution.py:441
  30.3 1.6 %collective-permute-start.5 = (f16[256,256]{1,0:T(8,128)(2,1)S(1)}, f16[256,256]{1,0:T(8,128)(2,1)S(1)}, u32[]{:S(2)}, u32[]{:S(2)}) collective-permute-start(f16[256,256]{1,0:T(8,128)(2,1)S(1)} %fusion.49), channel_id=1, source_target_pairs={{0,4},{1,5},{2,6},{3,7},{4,0},{5,1},{6,2},{7,3},{8,12},{9,13},{10,... | collective-permute-start | bytes 393224 | tf_op jit(solution)/shard_map/ppermute | solution.py:22
  31.9 4.0 %target_pass.1 = (f32[1024,2048]{1,0:T(8,128)S(1)}, f32[1024,1]{1,0:T(8,128)S(1)}) custom-call(f32[1024,2048]{1,0:T(8,128)S(1)} %bitcast.9, f32[1024,2048]{1,0:T(8,128)S(1)} %bitcast.9, f32[8,2048]{1,0:T(8,128)S(1)} %collective-permute-done.2.incoming_ref), custom_call_target="tpu_custom_call" | custom-call | flops 3072 | bytes 16777216 | tf_op jit(solution)/shard_map/target_pass/pallas_call | solution.py:132
  35.9 3.4 %copy-done.2 = f32[1024,2048]{1,0:T(8,128)} copy-done((f32[1024,2048]{1,0:T(8,128)}, f32[1024,2048]{1,0:T(8,128)S(1)}, u32[]{:S(2)}) %copy-start.2) | copy-done | bytes 8388632
  40.1 1.2 collective-permute-done.6
  42.6 1.6 %collective-permute-start.7 = (bf16[256,256]{1,0:T(8,128)(2,1)S(1)}, bf16[256,256]{1,0:T(8,128)(2,1)S(1)}, u32[]{:S(2)}, u32[]{:S(2)}) collective-permute-start(bf16[256,256]{1,0:T(8,128)(2,1)S(1)} %multiply_convert_fusion.3), channel_id=1, source_target_pairs={{0,2},{1,3},{2,0},{3,1},{4,6},{5,7},{6,4},{7,5},{8,10},{9,11},{10,... | collective-permute-start | bytes 393224 | tf_op jit(solution)/shard_map/ppermute | solution.py:22
  44.2 2.7 %collective-permute-done.8 = f16[128,1024]{1,0:T(8,128)(2,1)S(1)} collective-permute-done((f16[128,1024]{1,0:T(8,128)(2,1)S(1)}, f16[128,1024]{1,0:T(8,128)(2,1)S(1)}, u32[]{:S(2)}, u32[]{:S(2)}) %collective-permute-start.8) | collective-permute-done | bytes 262176 | tf_op jit(solution)/shard_map/ppermute | solution.py:22
  46.9 1.8 %multiply_convert_fusion.own_ref = bf16[128,1024]{1,0:T(8,128)(2,1)} fusion(f16[128,1024]{1,0:T(8,128)(2,1)S(1)} %collective-permute-done.8, f32[128,1024]{1,0:T(8,128)S(1)} %get-tuple-element.238, f16[128,1024]{1,0:T(8,128)(2,1)} %collective-permute-done.4), kind=kLoop, calls=%fused_computation.36 | loop fusion | flops 786432 | bytes 1310720 | tf_op jit(solution)/shard_map/convert_element_type | solution.py:448
  50.7 1.8 %collective-permute-done.10.other_ref = bf16[128,1024]{1,0:T(8,128)(2,1)S(1)} collective-permute-done((bf16[128,1024]{1,0:T(8,128)(2,1)S(1)}, bf16[128,1024]{1,0:T(8,128)(2,1)S(1)}, u32[]{:S(2)}, u32[]{:S(2)}) %collective-permute-start.10) | collective-permute-done | bytes 262176 | tf_op jit(solution)/shard_map/ppermute | solution.py:22
  53.4 3.4 %copy-done.1 = f32[1024,2048]{1,0:T(8,128)S(1)} copy-done((f32[1024,2048]{1,0:T(8,128)S(1)}, f32[1024,2048]{1,0:T(8,128)}, u32[]{:S(2)}) %copy-start.1) | copy-done | bytes 8388632
  57.8 2.5 %draft_chunk.2 = (f32[1024,1024]{1,0:T(8,128)S(1)}, bf16[256,1024]{1,0:T(8,128)(2,1)S(1)}, f32[1024,1]{1,0:T(8,128)S(1)}, f32[1024,1]{1,0:T(8,128)S(1)}) custom-call(f32[1024,2048]{1,0:T(8,128)S(1)} %copy-done.1, bf16[1024,256]{1,0:T(8,128)(2,1)S(1)} %pad_maximum_fusion.acts_ref, bf16[128,1024]{1,0:T(8,128)(2,1)S(1)} %multiply_convert_fusion.1.own_ref, ...), custom_call_target="tpu_custom_call" | custom-call | flops 131072 | bytes 8388608 | tf_op jit(solution)/shard_map/draft_chunk/pallas_call | solution.py:220
  60.3 4.1 %draft_chunk.3 = (f32[1024,1024]{1,0:T(8,128)S(1)}, bf16[256,1024]{1,0:T(8,128)(2,1)S(1)}, f32[1024,1]{1,0:T(8,128)S(1)}, f32[1024,1]{1,0:T(8,128)S(1)}) custom-call(f32[1024,2048]{1,0:T(8,128)S(1)} %copy-done.1, bf16[1024,256]{1,0:T(8,128)(2,1)S(1)} %pad_maximum_fusion.acts_ref, bf16[128,1024]{1,0:T(8,128)(2,1)} %multiply_convert_fusion.own_ref, ...), custom_call_target="tpu_custom_call" | custom-call | flops 131072 | bytes 8388608 | tf_op jit(solution)/shard_map/draft_chunk/pallas_call | solution.py:220
  64.4 4.1 %grad_chunk.2 = (bf16[128,1024]{1,0:T(8,128)(2,1)S(1)}, f32[128,1024]{1,0:T(8,128)S(1)}, f32[1024,256]{1,0:T(8,128)S(1)}, f32[1024,1]{1,0:T(8,128)S(1)}) custom-call(f32[1024,1024]{1,0:T(8,128)S(1)} %get-tuple-element.136.draft_ref, f32[1024,2048]{1,0:T(8,128)S(1)} %bitcast.11, s32[1024,1]{1,0:T(8,128)S(1)} %copy.11.label_ref, ...), custom_call_target="tpu_custom_call" | custom-call | flops 262144 | bytes 8388608 | tf_op jit(solution)/shard_map/grad_chunk/pallas_call | solution.py:292
  68.6 4.2 %grad_chunk.3 = (bf16[128,1024]{1,0:T(8,128)(2,1)S(1)}, f32[128,1024]{1,0:T(8,128)S(1)}, f32[1024,256]{1,0:T(8,128)S(1)}, f32[1024,1]{1,0:T(8,128)S(1)}) custom-call(f32[1024,1024]{1,0:T(8,128)S(1)} %get-tuple-element.142.draft_ref, f32[1024,2048]{1,0:T(8,128)S(1)} %bitcast.11, s32[1024,1]{1,0:T(8,128)S(1)} %copy.11.label_ref, ...), custom_call_target="tpu_custom_call" | custom-call | flops 262144 | bytes 8388608 | tf_op jit(solution)/shard_map/grad_chunk/pallas_call | solution.py:292
  72.9 3.9 %collective-permute-done.12 = bf16[128,1024]{1,0:T(8,128)(2,1)S(1)} collective-permute-done((bf16[128,1024]{1,0:T(8,128)(2,1)S(1)}, bf16[128,1024]{1,0:T(8,128)(2,1)S(1)}, u32[]{:S(2)}, u32[]{:S(2)}) %collective-permute-start.12) | collective-permute-done | bytes 262176 | tf_op jit(solution)/shard_map/ppermute | solution.py:22
  77.3 2.9 %collective-permute-start.13 = (bf16[128,1024]{1,0:T(8,128)(2,1)S(1)}, bf16[128,1024]{1,0:T(8,128)(2,1)S(1)}, u32[]{:S(2)}, u32[]{:S(2)}) collective-permute-start(bf16[128,1024]{1,0:T(8,128)(2,1)S(1)} %fusion.46), channel_id=1, source_target_pairs={{0,16},{8,24},{16,0},{24,8},{1,17},{9,25},{17,1},{25,9},{2,18},{10... | collective-permute-start | bytes 786440 | tf_op jit(solution)/shard_map/ppermute | solution.py:22
  80.3 1.6 %collective-permute-start.15 = (bf16[256,256]{1,0:T(8,128)(2,1)S(1)}, bf16[256,256]{1,0:T(8,128)(2,1)S(1)}, u32[]{:S(2)}, u32[]{:S(2)}) collective-permute-start(bf16[256,256]{1,0:T(8,128)(2,1)S(1)} %dynamic-slice_convert_fusion.5), channel_id=1, source_target_pairs={{0,2},{1,3},{2,0},{3,1},{4,6},{5,7},{6,4},{7,5},{8,10},{9,11},{10,... | collective-permute-start | bytes 393224 | tf_op jit(solution)/shard_map/ppermute | solution.py:22
  81.8 9.2 %collective-permute-done.16 = bf16[128,1024]{1,0:T(8,128)(2,1)S(1)} collective-permute-done((bf16[128,1024]{1,0:T(8,128)(2,1)S(1)}, bf16[128,1024]{1,0:T(8,128)(2,1)S(1)}, u32[]{:S(2)}, u32[]{:S(2)}) %collective-permute-start.16) | collective-permute-done | bytes 262176 | tf_op jit(solution)/shard_map/ppermute | solution.py:22
  91.2 1.6 %collective-permute-start.18 = (bf16[256,256]{1,0:T(8,128)(2,1)S(1)}, bf16[256,256]{1,0:T(8,128)(2,1)S(1)}, u32[]{:S(2)}, u32[]{:S(2)}) collective-permute-start(bf16[256,256]{1,0:T(8,128)(2,1)S(1)} %fusion.48), channel_id=1, source_target_pairs={{0,4},{1,5},{2,6},{3,7},{4,0},{5,1},{6,2},{7,3},{8,12},{9,13},{10,... | collective-permute-start | bytes 393224 | tf_op jit(solution)/shard_map/ppermute | solution.py:22
  93.6 2.0 %collective-permute-start.17 = (bf16[128,1024]{1,0:T(8,128)(2,1)}, bf16[128,1024]{1,0:T(8,128)(2,1)}, u32[]{:S(2)}, u32[]{:S(2)}) collective-permute-start(bf16[128,1024]{1,0:T(8,128)(2,1)} %add_convert_fusion.1), channel_id=1, source_target_pairs={{0,8},{8,0},{16,24},{24,16},{1,9},{9,1},{17,25},{25,17},{2,10},{10... | collective-permute-start | bytes 786440 | tf_op jit(solution)/shard_map/ppermute | solution.py:22
  95.6 2.5 %fusion.2 = f32[128,2048]{1,0:T(8,128)S(1)} fusion(bf16[128,1024]{1,0:T(8,128)(2,1)} %add_convert_fusion.1, bf16[2048,2048]{1,0:T(8,128)(2,1)S(1)} %bitcast.13), kind=kOutput, calls=%fused_computation.2 | convolution fusion | flops 536870912 | bytes 5505024 | tf_op jit(solution)/shard_map/dot_general | solution.py:44
  98.4 1.6 %collective-permute-start.19 = (bf16[256,256]{1,0:T(8,128)(2,1)S(1)}, bf16[256,256]{1,0:T(8,128)(2,1)S(1)}, u32[]{:S(2)}, u32[]{:S(2)}) collective-permute-start(bf16[256,256]{1,0:T(8,128)(2,1)S(1)} %multiply_convert_fusion.2), channel_id=1, source_target_pairs={{0,2},{1,3},{2,0},{3,1},{4,6},{5,7},{6,4},{7,5},{8,10},{9,11},{10,... | collective-permute-start | bytes 393224 | tf_op jit(solution)/shard_map/ppermute | solution.py:22
  99.9 4.7 %collective-permute-done.20 = bf16[128,1024]{1,0:T(8,128)(2,1)S(1)} collective-permute-done((bf16[128,1024]{1,0:T(8,128)(2,1)S(1)}, bf16[128,1024]{1,0:T(8,128)(2,1)S(1)}, u32[]{:S(2)}, u32[]{:S(2)}) %collective-permute-start.20) | collective-permute-done | bytes 262176 | tf_op jit(solution)/shard_map/ppermute | solution.py:22
  110.3 1.9 %collective-permute-start.27 = (bf16[256,256]{1,0:T(8,128)(2,1)S(1)}, bf16[256,256]{1,0:T(8,128)(2,1)S(1)}, u32[]{:S(2)}, u32[]{:S(2)}) collective-permute-start(bf16[256,256]{1,0:T(8,128)(2,1)S(1)} %dynamic-slice_convert_fusion.4), channel_id=1, source_target_pairs={{0,8},{8,0},{16,24},{24,16},{1,9},{9,1},{17,25},{25,17},{2,10},{10... | collective-permute-start | bytes 393224 | tf_op jit(solution)/shard_map/ppermute | solution.py:22
  112.1 3.7 %fusion.16 = f32[128,2048]{1,0:T(8,128)S(1)} fusion(f32[128,2048]{1,0:T(8,128)S(1)} %fusion.2, bf16[128,1024]{1,0:T(8,128)(2,1)S(1)} %copy-done.11, bf16[2048,2048]{1,0:T(8,128)(2,1)} %param.11), kind=kOutput, calls=%fused_computation.16 | convolution fusion | flops 537133056 | bytes 6553600 | tf_op jit(solution)/shard_map/dot_general | solution.py:44
  115.9 2.5 %fusion = f32[128,2048]{1,0:T(8,128)S(1)} fusion(bf16[128,1024]{1,0:T(8,128)(2,1)} %collective-permute-done.17, bf16[2048,2048]{1,0:T(8,128)(2,1)S(1)} %bitcast.15), kind=kOutput, calls=%fused_computation | convolution fusion | flops 536870912 | bytes 5505024 | tf_op jit(solution)/shard_map/dot_general | solution.py:44
  118.4 1.5 %broadcast_select_fusion = (f32[128,2048]{1,0:T(8,128)S(1)}, f32[128,2048]{1,0:T(8,128)S(1)}) fusion(f32[128,2048]{1,0:T(8,128)S(1)} %fusion.16, pred[]{:T(512)S(6)} %eq.12, f32[128,2048]{1,0:T(8,128)S(1)} %fusion, bf16[128,1024]{1,0:T(8,128)(2,1)S(1)} %collective-permute-done.22, bf16[2048,2048]{1,0:T(8,128)(2,1)S(1)} %bitcast.15), kind=kOutput, calls=%fused_computation.43 | convolution fusion | flops 537657344 | bytes 8650753 | tf_op jit(solution)/shard_map/dot_general | solution.py:44
  122.5 2.1 %collective-permute-start.35 = (bf16[256,256]{1,0:T(8,128)(2,1)S(1)}, bf16[256,256]{1,0:T(8,128)(2,1)S(1)}, u32[]{:S(2)}, u32[]{:S(2)}) collective-permute-start(bf16[256,256]{1,0:T(8,128)(2,1)S(1)} %add_convert_fusion.8), channel_id=1, source_target_pairs={{0,16},{8,24},{16,0},{24,8},{1,17},{9,25},{17,1},{25,9},{2,18},{10... | collective-permute-start | bytes 393224 | tf_op jit(solution)/shard_map/ppermute | solution.py:22
  124.7 1.6 %collective-permute-start.29 = (bf16[32,2048]{1,0:T(8,128)(2,1)S(1)}, bf16[32,2048]{1,0:T(8,128)(2,1)S(1)}, u32[]{:S(2)}, u32[]{:S(2)}) collective-permute-start(bf16[32,2048]{1,0:T(8,128)(2,1)S(1)} %dynamic-slice_convert_fusion.2), channel_id=1, source_target_pairs={{0,2},{1,3},{2,0},{3,1},{4,6},{5,7},{6,4},{7,5},{8,10},{9,11},{10,... | collective-permute-start | bytes 393224 | tf_op jit(solution)/shard_map/ppermute | solution.py:22
  126.4 1.6 %collective-permute-start.28 = (bf16[32,2048]{1,0:T(8,128)(2,1)S(1)}, bf16[32,2048]{1,0:T(8,128)(2,1)S(1)}, u32[]{:S(2)}, u32[]{:S(2)}) collective-permute-start(bf16[32,2048]{1,0:T(8,128)(2,1)S(1)} %dynamic-slice_convert_fusion.1), channel_id=1, source_target_pairs={{0,4},{1,5},{2,6},{3,7},{4,0},{5,1},{6,2},{7,3},{8,12},{9,13},{10,... | collective-permute-start | bytes 393224 | tf_op jit(solution)/shard_map/ppermute | solution.py:22
  128.0 1.8 %collective-permute-done.29 = bf16[32,2048]{1,0:T(8,128)(2,1)S(1)} collective-permute-done((bf16[32,2048]{1,0:T(8,128)(2,1)S(1)}, bf16[32,2048]{1,0:T(8,128)(2,1)S(1)}, u32[]{:S(2)}, u32[]{:S(2)}) %collective-permute-start.29) | collective-permute-done | bytes 131104 | tf_op jit(solution)/shard_map/ppermute | solution.py:22
  129.8 1.6 %collective-permute-start.31 = (bf16[32,2048]{1,0:T(8,128)(2,1)S(1)}, bf16[32,2048]{1,0:T(8,128)(2,1)S(1)}, u32[]{:S(2)}, u32[]{:S(2)}) collective-permute-start(bf16[32,2048]{1,0:T(8,128)(2,1)S(1)} %add_convert_fusion.7), channel_id=1, source_target_pairs={{0,4},{1,5},{2,6},{3,7},{4,0},{5,1},{6,2},{7,3},{8,12},{9,13},{10,... | collective-permute-start | bytes 393224 | tf_op jit(solution)/shard_map/ppermute | solution.py:22
  133.0 1.9 %collective-permute-done.31 = bf16[32,2048]{1,0:T(8,128)(2,1)S(1)} collective-permute-done((bf16[32,2048]{1,0:T(8,128)(2,1)S(1)}, bf16[32,2048]{1,0:T(8,128)(2,1)S(1)}, u32[]{:S(2)}, u32[]{:S(2)}) %collective-permute-start.31) | collective-permute-done | bytes 131104 | tf_op jit(solution)/shard_map/ppermute | solution.py:22
  134.9 1.6 %collective-permute-start.34 = (bf16[32,2048]{1,0:T(8,128)(2,1)S(1)}, bf16[32,2048]{1,0:T(8,128)(2,1)S(1)}, u32[]{:S(2)}, u32[]{:S(2)}) collective-permute-start(bf16[32,2048]{1,0:T(8,128)(2,1)S(1)} %add_convert_fusion.5), channel_id=1, source_target_pairs={{0,2},{1,3},{2,0},{3,1},{4,6},{5,7},{6,4},{7,5},{8,10},{9,11},{10,... | collective-permute-start | bytes 393224 | tf_op jit(solution)/shard_map/ppermute | solution.py:22
  136.4 1.7 %collective-permute-done.30 = bf16[32,2048]{1,0:T(8,128)(2,1)S(1)} collective-permute-done((bf16[32,2048]{1,0:T(8,128)(2,1)S(1)}, bf16[32,2048]{1,0:T(8,128)(2,1)S(1)}, u32[]{:S(2)}, u32[]{:S(2)}) %collective-permute-start.30) | collective-permute-done | bytes 131104 | tf_op jit(solution)/shard_map/ppermute | solution.py:22
  138.1 1.5 %collective-permute-start.33 = (bf16[32,2048]{1,0:T(8,128)(2,1)S(1)}, bf16[32,2048]{1,0:T(8,128)(2,1)S(1)}, u32[]{:S(2)}, u32[]{:S(2)}) collective-permute-start(bf16[32,2048]{1,0:T(8,128)(2,1)S(1)} %add_convert_fusion.4), channel_id=1, source_target_pairs={{0,4},{1,5},{2,6},{3,7},{4,0},{5,1},{6,2},{7,3},{8,12},{9,13},{10,... | collective-permute-start | bytes 393224 | tf_op jit(solution)/shard_map/ppermute | solution.py:22
  140.1 1.8 %collective-permute-start.36 = (bf16[256,256]{1,0:T(8,128)(2,1)S(1)}, bf16[256,256]{1,0:T(8,128)(2,1)S(1)}, u32[]{:S(2)}, u32[]{:S(2)}) collective-permute-start(bf16[256,256]{1,0:T(8,128)(2,1)S(1)} %add_convert_fusion.2), channel_id=1, source_target_pairs={{0,8},{8,0},{16,24},{24,16},{1,9},{9,1},{17,25},{25,17},{2,10},{10... | collective-permute-start | bytes 393224 | tf_op jit(solution)/shard_map/ppermute | solution.py:22
  143.3 1.4 collective-permute-done.32
  144.7 1.4 collective-permute-done.36
  147.5 1.6 %maximum_convert_fusion = f32[256,2048]{1,0:T(8,128)} fusion(bf16[64,2048]{1,0:T(8,128)(2,1)S(1)} %get-tuple-element.216, bf16[64,2048]{1,0:T(8,128)(2,1)S(1)} %get-tuple-element.215, bf16[64,2048]{1,0:T(8,128)(2,1)S(1)} %get-tuple-element.240, bf16[64,2048]{1,0:T(8,128)(2,1)S(1)} %get-tuple-element.241), kind=kLoop, calls=%fused_computation.24 | loop fusion | flops 4194304 | bytes 3145728 | tf_op jit(solution)/shard_map/concatenate | solution.py:564
  (151 shorter events, 25.5 us)
Async XLA Ops:
  0.6 15.4 %copy-start = (bf16[1024,1024]{1,0:T(8,128)(2,1)S(1)}, bf16[1024,1024]{1,0:T(8,128)(2,1)}, u32[]{:S(2)}) copy-start(bf16[1024,1024]{1,0:T(8,128)(2,1)} %param.6) | copy-start | bytes 6291460
  0.6 9.1 %copy-start.14 = (bf16[256,2048]{1,0:T(8,128)(2,1)S(1)}, bf16[256,2048]{1,0:T(8,128)(2,1)}, u32[]{:S(2)}) copy-start(bf16[256,2048]{1,0:T(8,128)(2,1)} %param.10) | copy-start | bytes 3145732
  4.6 11.4 %copy-start.16 = (bf16[1024,256]{1,0:T(8,128)(2,1)S(1)}, bf16[1024,256]{1,0:T(8,128)(2,1)}, u32[]{:S(2)}) copy-start(bf16[1024,256]{1,0:T(8,128)(2,1)} %param.9) | copy-start | bytes 1572868
  4.6 12.9 %collective-permute-start.1 = (f16[128,1024]{1,0:T(8,128)(2,1)}, f16[128,1024]{1,0:T(8,128)(2,1)}, u32[]{:S(2)}, u32[]{:S(2)}) collective-permute-start(f16[128,1024]{1,0:T(8,128)(2,1)} %fusion.34), channel_id=1, source_target_pairs={{0,8},{8,0},{16,24},{24,16},{1,9},{9,1},{17,25},{25,17},{2,10},{10... | collective-permute-start | bytes 786440 | tf_op jit(solution)/shard_map/ppermute | solution.py:22
  8.5 9.0 %collective-permute-start.2 = (f32[8,2048]{1,0:T(8,128)S(1)}, f32[8,2048]{1,0:T(8,128)S(1)}, u32[]{:S(2)}, u32[]{:S(2)}) collective-permute-start(f32[8,2048]{1,0:T(8,128)S(1)} %slice.22), channel_id=1, source_target_pairs={{8,0},{16,8},{24,16},{9,1},{17,9},{25,17},{10,2},{18,10},{26,18},{... | collective-permute-start | bytes 196616 | tf_op jit(solution)/shard_map/ppermute | solution.py:454
  13.4 12.8 %collective-permute-start.4 = (f16[128,1024]{1,0:T(8,128)(2,1)}, f16[128,1024]{1,0:T(8,128)(2,1)}, u32[]{:S(2)}, u32[]{:S(2)}) collective-permute-start(f16[128,1024]{1,0:T(8,128)(2,1)} %fusion.37), channel_id=1, source_target_pairs={{0,8},{8,0},{16,24},{24,16},{1,9},{9,1},{17,25},{25,17},{2,10},{10... | collective-permute-start | bytes 786440 | tf_op jit(solution)/shard_map/ppermute | solution.py:22
  17.5 6.0 %collective-permute-start = (f16[512,256]{1,0:T(8,128)(2,1)}, f16[512,256]{1,0:T(8,128)(2,1)}, u32[]{:S(2)}, u32[]{:S(2)}) collective-permute-start(f16[512,256]{1,0:T(8,128)(2,1)} %dynamic-slice_convert_fusion), channel_id=1, source_target_pairs={{0,1},{1,0},{2,3},{3,2},{4,5},{5,4},{6,7},{7,6},{8,9},{9,8},{10,11... | collective-permute-start | bytes 786440 | tf_op jit(solution)/shard_map/ppermute | solution.py:22
  17.5 14.4 %slice-start = ((s8[8388608]{0:T(1024)(128)(4,1)}), s8[4194304]{0:T(1024)(128)(4,1)S(1)}, s32[]{:S(2)}) async-start(s8[8388608]{0:T(1024)(128)(4,1)} %bitcast.8), calls=%async_computation | async-start | bytes 8388608
  20.9 11.0 %slice-start.1 = ((s8[8388608]{0:T(1024)(128)(4,1)}), s8[4194304]{0:T(1024)(128)(4,1)S(1)}, s32[]{:S(2)}) async-start(s8[8388608]{0:T(1024)(128)(4,1)} %bitcast.8), calls=%async_computation.1 | async-start | bytes 8388608
  20.9 20.4 %collective-permute-start.6 = (f16[128,1024]{1,0:T(8,128)(2,1)S(1)}, f16[128,1024]{1,0:T(8,128)(2,1)S(1)}, u32[]{:S(2)}, u32[]{:S(2)}) collective-permute-start(f16[128,1024]{1,0:T(8,128)(2,1)S(1)} %get-tuple-element.112), channel_id=1, source_target_pairs={{0,16},{8,24},{16,0},{24,8},{1,17},{9,25},{17,1},{25,9},{2,18},{10... | collective-permute-start | bytes 786440 | tf_op jit(solution)/shard_map/ppermute | solution.py:22
  24.5 18.0 %copy-start.9 = (f32[512,256]{1,0:T(8,128)}, f32[512,256]{1,0:T(8,128)S(1)}, u32[]{:S(2)}) copy-start(f32[512,256]{1,0:T(8,128)S(1)} %convert_add_fusion.3) | copy-start | bytes 1572868
  24.6 5.7 %collective-permute-start.3 = (f16[256,256]{1,0:T(8,128)(2,1)S(1)}, f16[256,256]{1,0:T(8,128)(2,1)S(1)}, u32[]{:S(2)}, u32[]{:S(2)}) collective-permute-start(f16[256,256]{1,0:T(8,128)(2,1)S(1)} %dynamic-slice_convert_fusion.6), channel_id=1, source_target_pairs={{0,2},{1,3},{2,0},{3,1},{4,6},{5,7},{6,4},{7,5},{8,10},{9,11},{10,... | collective-permute-start | bytes 393224 | tf_op jit(solution)/shard_map/ppermute | solution.py:22
  29.1 17.8 %collective-permute-start.8 = (f16[128,1024]{1,0:T(8,128)(2,1)S(1)}, f16[128,1024]{1,0:T(8,128)(2,1)S(1)}, u32[]{:S(2)}, u32[]{:S(2)}) collective-permute-start(f16[128,1024]{1,0:T(8,128)(2,1)S(1)} %get-tuple-element.116), channel_id=1, source_target_pairs={{0,16},{8,24},{16,0},{24,8},{1,17},{9,25},{17,1},{25,9},{2,18},{10... | collective-permute-start | bytes 786440 | tf_op jit(solution)/shard_map/ppermute | solution.py:22
  30.3 12.2 %collective-permute-start.5 = (f16[256,256]{1,0:T(8,128)(2,1)S(1)}, f16[256,256]{1,0:T(8,128)(2,1)S(1)}, u32[]{:S(2)}, u32[]{:S(2)}) collective-permute-start(f16[256,256]{1,0:T(8,128)(2,1)S(1)} %fusion.49), channel_id=1, source_target_pairs={{0,4},{1,5},{2,6},{3,7},{4,0},{5,1},{6,2},{7,3},{8,12},{9,13},{10,... | collective-permute-start | bytes 393224 | tf_op jit(solution)/shard_map/ppermute | solution.py:22
  42.3 10.1 %collective-permute-start.10 = (bf16[128,1024]{1,0:T(8,128)(2,1)S(1)}, bf16[128,1024]{1,0:T(8,128)(2,1)S(1)}, u32[]{:S(2)}, u32[]{:S(2)}) collective-permute-start(bf16[128,1024]{1,0:T(8,128)(2,1)S(1)} %multiply_convert_fusion.1.own_ref), channel_id=1, source_target_pairs={{0,8},{8,0},{16,24},{24,16},{1,9},{9,1},{17,25},{25,17},{2,10},{10... | collective-permute-start | bytes 786440 | tf_op jit(solution)/shard_map/ppermute | solution.py:22
  42.6 6.1 %collective-permute-start.7 = (bf16[256,256]{1,0:T(8,128)(2,1)S(1)}, bf16[256,256]{1,0:T(8,128)(2,1)S(1)}, u32[]{:S(2)}, u32[]{:S(2)}) collective-permute-start(bf16[256,256]{1,0:T(8,128)(2,1)S(1)} %multiply_convert_fusion.3), channel_id=1, source_target_pairs={{0,2},{1,3},{2,0},{3,1},{4,6},{5,7},{6,4},{7,5},{8,10},{9,11},{10,... | collective-permute-start | bytes 393224 | tf_op jit(solution)/shard_map/ppermute | solution.py:22
  48.8 3.7 %collective-permute-start.9 = (bf16[512,256]{1,0:T(8,128)(2,1)S(1)}, bf16[512,256]{1,0:T(8,128)(2,1)S(1)}, u32[]{:S(2)}, u32[]{:S(2)}) collective-permute-start(bf16[512,256]{1,0:T(8,128)(2,1)S(1)} %pad_maximum_fusion.2), channel_id=1, source_target_pairs={{0,1},{1,0},{2,3},{3,2},{4,5},{5,4},{6,7},{7,6},{8,9},{9,8},{10,11... | collective-permute-start | bytes 786440 | tf_op jit(solution)/shard_map/ppermute | solution.py:22
  49.6 10.6 %collective-permute-start.11 = (bf16[128,1024]{1,0:T(8,128)(2,1)}, bf16[128,1024]{1,0:T(8,128)(2,1)}, u32[]{:S(2)}, u32[]{:S(2)}) collective-permute-start(bf16[128,1024]{1,0:T(8,128)(2,1)} %multiply_convert_fusion.own_ref), channel_id=1, source_target_pairs={{0,8},{8,0},{16,24},{24,16},{1,9},{9,1},{17,25},{25,17},{2,10},{10... | collective-permute-start | bytes 786440 | tf_op jit(solution)/shard_map/ppermute | solution.py:22
  68.5 8.3 %collective-permute-start.12 = (bf16[128,1024]{1,0:T(8,128)(2,1)S(1)}, bf16[128,1024]{1,0:T(8,128)(2,1)S(1)}, u32[]{:S(2)}, u32[]{:S(2)}) collective-permute-start(bf16[128,1024]{1,0:T(8,128)(2,1)S(1)} %get-tuple-element.141), channel_id=1, source_target_pairs={{0,8},{8,0},{16,24},{24,16},{1,9},{9,1},{17,25},{25,17},{2,10},{10... | collective-permute-start | bytes 786440 | tf_op jit(solution)/shard_map/ppermute | solution.py:22
  68.6 27.1 %slice-start.4 = ((s8[8388608]{0:T(1024)(128)(4,1)}), s8[4194304]{0:T(1024)(128)(4,1)S(1)}, s32[]{:S(2)}) async-start(s8[8388608]{0:T(1024)(128)(4,1)} %bitcast.12), calls=%async_computation.4 | async-start | bytes 8388608
  68.6 27.0 %slice-start.5 = ((s8[8388608]{0:T(1024)(128)(4,1)}), s8[4194304]{0:T(1024)(128)(4,1)S(1)}, s32[]{:S(2)}) async-start(s8[8388608]{0:T(1024)(128)(4,1)} %bitcast.12), calls=%async_computation.5 | async-start | bytes 8388608
  72.8 25.3 %copy-start.5 = (f32[1024,1]{1,0:T(8,128)}, f32[1024,1]{1,0:T(8,128)S(1)}, u32[]{:S(2)}) copy-start(f32[1024,1]{1,0:T(8,128)S(1)} %get-tuple-element.178) | copy-start | bytes 12292
  76.8 3.3 %collective-permute-start.14 = (f32[512,256]{1,0:T(8,128)S(1)}, f32[512,256]{1,0:T(8,128)S(1)}, u32[]{:S(2)}, u32[]{:S(2)}) collective-permute-start(f32[512,256]{1,0:T(8,128)S(1)} %constant_dynamic-slice_fusion.2), channel_id=1, source_target_pairs={{0,1},{1,0},{2,3},{3,2},{4,5},{5,4},{6,7},{7,6},{8,9},{9,8},{10,11... | collective-permute-start | bytes 1572872 | tf_op jit(solution)/shard_map/ppermute | solution.py:22
  76.9 14.1 %collective-permute-start.16 = (bf16[128,1024]{1,0:T(8,128)(2,1)S(1)}, bf16[128,1024]{1,0:T(8,128)(2,1)S(1)}, u32[]{:S(2)}, u32[]{:S(2)}) collective-permute-start(bf16[128,1024]{1,0:T(8,128)(2,1)S(1)} %get-tuple-element.148), channel_id=1, source_target_pairs={{0,8},{8,0},{16,24},{24,16},{1,9},{9,1},{17,25},{25,17},{2,10},{10... | collective-permute-start | bytes 786440 | tf_op jit(solution)/shard_map/ppermute | solution.py:22
  77.3 15.6 %collective-permute-start.13 = (bf16[128,1024]{1,0:T(8,128)(2,1)S(1)}, bf16[128,1024]{1,0:T(8,128)(2,1)S(1)}, u32[]{:S(2)}, u32[]{:S(2)}) collective-permute-start(bf16[128,1024]{1,0:T(8,128)(2,1)S(1)} %fusion.46), channel_id=1, source_target_pairs={{0,16},{8,24},{16,0},{24,8},{1,17},{9,25},{17,1},{25,9},{2,18},{10... | collective-permute-start | bytes 786440 | tf_op jit(solution)/shard_map/ppermute | solution.py:22
  80.3 10.9 %collective-permute-start.15 = (bf16[256,256]{1,0:T(8,128)(2,1)S(1)}, bf16[256,256]{1,0:T(8,128)(2,1)S(1)}, u32[]{:S(2)}, u32[]{:S(2)}) collective-permute-start(bf16[256,256]{1,0:T(8,128)(2,1)S(1)} %dynamic-slice_convert_fusion.5), channel_id=1, source_target_pairs={{0,2},{1,3},{2,0},{3,1},{4,6},{5,7},{6,4},{7,5},{8,10},{9,11},{10,... | collective-permute-start | bytes 393224 | tf_op jit(solution)/shard_map/ppermute | solution.py:22
  91.1 13.5 %collective-permute-start.20 = (bf16[128,1024]{1,0:T(8,128)(2,1)S(1)}, bf16[128,1024]{1,0:T(8,128)(2,1)S(1)}, u32[]{:S(2)}, u32[]{:S(2)}) collective-permute-start(bf16[128,1024]{1,0:T(8,128)(2,1)S(1)} %fusion.47), channel_id=1, source_target_pairs={{0,16},{8,24},{16,0},{24,8},{1,17},{9,25},{17,1},{25,9},{2,18},{10... | collective-permute-start | bytes 786440 | tf_op jit(solution)/shard_map/ppermute | solution.py:22
  91.2 6.9 %collective-permute-start.18 = (bf16[256,256]{1,0:T(8,128)(2,1)S(1)}, bf16[256,256]{1,0:T(8,128)(2,1)S(1)}, u32[]{:S(2)}, u32[]{:S(2)}) collective-permute-start(bf16[256,256]{1,0:T(8,128)(2,1)S(1)} %fusion.48), channel_id=1, source_target_pairs={{0,4},{1,5},{2,6},{3,7},{4,0},{5,1},{6,2},{7,3},{8,12},{9,13},{10,... | collective-permute-start | bytes 393224 | tf_op jit(solution)/shard_map/ppermute | solution.py:22
  93.6 13.4 %collective-permute-start.17 = (bf16[128,1024]{1,0:T(8,128)(2,1)}, bf16[128,1024]{1,0:T(8,128)(2,1)}, u32[]{:S(2)}, u32[]{:S(2)}) collective-permute-start(bf16[128,1024]{1,0:T(8,128)(2,1)} %add_convert_fusion.1), channel_id=1, source_target_pairs={{0,8},{8,0},{16,24},{24,16},{1,9},{9,1},{17,25},{25,17},{2,10},{10... | collective-permute-start | bytes 786440 | tf_op jit(solution)/shard_map/ppermute | solution.py:22
  98.4 7.1 %collective-permute-start.19 = (bf16[256,256]{1,0:T(8,128)(2,1)S(1)}, bf16[256,256]{1,0:T(8,128)(2,1)S(1)}, u32[]{:S(2)}, u32[]{:S(2)}) collective-permute-start(bf16[256,256]{1,0:T(8,128)(2,1)S(1)} %multiply_convert_fusion.2), channel_id=1, source_target_pairs={{0,2},{1,3},{2,0},{3,1},{4,6},{5,7},{6,4},{7,5},{8,10},{9,11},{10,... | collective-permute-start | bytes 393224 | tf_op jit(solution)/shard_map/ppermute | solution.py:22
  106.2 1.9 %collective-permute-start.21 = (bf16[512,256]{1,0:T(8,128)(2,1)}, bf16[512,256]{1,0:T(8,128)(2,1)}, u32[]{:S(2)}, u32[]{:S(2)}) collective-permute-start(bf16[512,256]{1,0:T(8,128)(2,1)} %pad_maximum_fusion.3), channel_id=1, source_target_pairs={{0,1},{1,0},{2,3},{3,2},{4,5},{5,4},{6,7},{7,6},{8,9},{9,8},{10,11... | collective-permute-start | bytes 786440 | tf_op jit(solution)/shard_map/ppermute | solution.py:22
  106.2 12.2 %collective-permute-start.22 = (bf16[128,1024]{1,0:T(8,128)(2,1)}, bf16[128,1024]{1,0:T(8,128)(2,1)S(1)}, u32[]{:S(2)}, u32[]{:S(2)}) collective-permute-start(bf16[128,1024]{1,0:T(8,128)(2,1)} %add_convert_fusion), channel_id=1, source_target_pairs={{0,8},{8,0},{16,24},{24,16},{1,9},{9,1},{17,25},{25,17},{2,10},{10... | collective-permute-start | bytes 786440 | tf_op jit(solution)/shard_map/ppermute | solution.py:22
  110.1 11.4 %collective-permute-start.23 = (bf16[256,256]{1,0:T(8,128)(2,1)S(1)}, bf16[256,256]{1,0:T(8,128)(2,1)S(1)}, u32[]{:S(2)}, u32[]{:S(2)}) collective-permute-start(bf16[256,256]{1,0:T(8,128)(2,1)S(1)} %dynamic-slice_convert_fusion.3), channel_id=1, source_target_pairs={{0,8},{8,0},{16,24},{24,16},{1,9},{9,1},{17,25},{25,17},{2,10},{10... | collective-permute-start | bytes 393224 | tf_op jit(solution)/shard_map/ppermute | solution.py:22
  110.3 12.2 %collective-permute-start.27 = (bf16[256,256]{1,0:T(8,128)(2,1)S(1)}, bf16[256,256]{1,0:T(8,128)(2,1)S(1)}, u32[]{:S(2)}, u32[]{:S(2)}) collective-permute-start(bf16[256,256]{1,0:T(8,128)(2,1)S(1)} %dynamic-slice_convert_fusion.4), channel_id=1, source_target_pairs={{0,8},{8,0},{16,24},{24,16},{1,9},{9,1},{17,25},{25,17},{2,10},{10... | collective-permute-start | bytes 393224 | tf_op jit(solution)/shard_map/ppermute | solution.py:22
  120.0 4.6 %collective-permute-start.26 = (f32[64,2048]{1,0:T(8,128)S(1)}, f32[64,2048]{1,0:T(8,128)S(1)}, u32[]{:S(2)}, u32[]{:S(2)}) collective-permute-start(f32[64,2048]{1,0:T(8,128)S(1)} %constant_dynamic-slice_fusion), channel_id=1, source_target_pairs={{0,1},{1,0},{2,3},{3,2},{4,5},{5,4},{6,7},{7,6},{8,9},{9,8},{10,11... | collective-permute-start | bytes 1572872 | tf_op jit(solution)/shard_map/ppermute | solution.py:22
  120.1 6.2 %collective-permute-start.25 = (f32[64,2048]{1,0:T(8,128)S(1)}, f32[64,2048]{1,0:T(8,128)S(1)}, u32[]{:S(2)}, u32[]{:S(2)}) collective-permute-start(f32[64,2048]{1,0:T(8,128)S(1)} %constant_dynamic-slice_fusion.1), channel_id=1, source_target_pairs={{0,1},{1,0},{2,3},{3,2},{4,5},{5,4},{6,7},{7,6},{8,9},{9,8},{10,11... | collective-permute-start | bytes 1572872 | tf_op jit(solution)/shard_map/ppermute | solution.py:22
  121.5 18.1 %collective-permute-start.24 = (bf16[256,256]{1,0:T(8,128)(2,1)S(1)}, bf16[256,256]{1,0:T(8,128)(2,1)S(1)}, u32[]{:S(2)}, u32[]{:S(2)}) collective-permute-start(bf16[256,256]{1,0:T(8,128)(2,1)S(1)} %add_convert_fusion.9), channel_id=1, source_target_pairs={{0,16},{8,24},{16,0},{24,8},{1,17},{9,25},{17,1},{25,9},{2,18},{10... | collective-permute-start | bytes 393224 | tf_op jit(solution)/shard_map/ppermute | solution.py:22
  122.5 17.5 %collective-permute-start.35 = (bf16[256,256]{1,0:T(8,128)(2,1)S(1)}, bf16[256,256]{1,0:T(8,128)(2,1)S(1)}, u32[]{:S(2)}, u32[]{:S(2)}) collective-permute-start(bf16[256,256]{1,0:T(8,128)(2,1)S(1)} %add_convert_fusion.8), channel_id=1, source_target_pairs={{0,16},{8,24},{16,0},{24,8},{1,17},{9,25},{17,1},{25,9},{2,18},{10... | collective-permute-start | bytes 393224 | tf_op jit(solution)/shard_map/ppermute | solution.py:22
  124.7 5.0 %collective-permute-start.29 = (bf16[32,2048]{1,0:T(8,128)(2,1)S(1)}, bf16[32,2048]{1,0:T(8,128)(2,1)S(1)}, u32[]{:S(2)}, u32[]{:S(2)}) collective-permute-start(bf16[32,2048]{1,0:T(8,128)(2,1)S(1)} %dynamic-slice_convert_fusion.2), channel_id=1, source_target_pairs={{0,2},{1,3},{2,0},{3,1},{4,6},{5,7},{6,4},{7,5},{8,10},{9,11},{10,... | collective-permute-start | bytes 393224 | tf_op jit(solution)/shard_map/ppermute | solution.py:22
  126.4 5.4 %collective-permute-start.28 = (bf16[32,2048]{1,0:T(8,128)(2,1)S(1)}, bf16[32,2048]{1,0:T(8,128)(2,1)S(1)}, u32[]{:S(2)}, u32[]{:S(2)}) collective-permute-start(bf16[32,2048]{1,0:T(8,128)(2,1)S(1)} %dynamic-slice_convert_fusion.1), channel_id=1, source_target_pairs={{0,4},{1,5},{2,6},{3,7},{4,0},{5,1},{6,2},{7,3},{8,12},{9,13},{10,... | collective-permute-start | bytes 393224 | tf_op jit(solution)/shard_map/ppermute | solution.py:22
  129.8 5.0 %collective-permute-start.31 = (bf16[32,2048]{1,0:T(8,128)(2,1)S(1)}, bf16[32,2048]{1,0:T(8,128)(2,1)S(1)}, u32[]{:S(2)}, u32[]{:S(2)}) collective-permute-start(bf16[32,2048]{1,0:T(8,128)(2,1)S(1)} %add_convert_fusion.7), channel_id=1, source_target_pairs={{0,4},{1,5},{2,6},{3,7},{4,0},{5,1},{6,2},{7,3},{8,12},{9,13},{10,... | collective-permute-start | bytes 393224 | tf_op jit(solution)/shard_map/ppermute | solution.py:22
  131.8 6.3 %collective-permute-start.30 = (bf16[32,2048]{1,0:T(8,128)(2,1)S(1)}, bf16[32,2048]{1,0:T(8,128)(2,1)S(1)}, u32[]{:S(2)}, u32[]{:S(2)}) collective-permute-start(bf16[32,2048]{1,0:T(8,128)(2,1)S(1)} %add_convert_fusion.6), channel_id=1, source_target_pairs={{0,2},{1,3},{2,0},{3,1},{4,6},{5,7},{6,4},{7,5},{8,10},{9,11},{10,... | collective-permute-start | bytes 393224 | tf_op jit(solution)/shard_map/ppermute | solution.py:22
  134.9 7.0 %collective-permute-start.34 = (bf16[32,2048]{1,0:T(8,128)(2,1)S(1)}, bf16[32,2048]{1,0:T(8,128)(2,1)S(1)}, u32[]{:S(2)}, u32[]{:S(2)}) collective-permute-start(bf16[32,2048]{1,0:T(8,128)(2,1)S(1)} %add_convert_fusion.5), channel_id=1, source_target_pairs={{0,2},{1,3},{2,0},{3,1},{4,6},{5,7},{6,4},{7,5},{8,10},{9,11},{10,... | collective-permute-start | bytes 393224 | tf_op jit(solution)/shard_map/ppermute | solution.py:22
  138.1 5.0 %collective-permute-start.33 = (bf16[32,2048]{1,0:T(8,128)(2,1)S(1)}, bf16[32,2048]{1,0:T(8,128)(2,1)S(1)}, u32[]{:S(2)}, u32[]{:S(2)}) collective-permute-start(bf16[32,2048]{1,0:T(8,128)(2,1)S(1)} %add_convert_fusion.4), channel_id=1, source_target_pairs={{0,4},{1,5},{2,6},{3,7},{4,0},{5,1},{6,2},{7,3},{8,12},{9,13},{10,... | collective-permute-start | bytes 393224 | tf_op jit(solution)/shard_map/ppermute | solution.py:22
  139.7 5.0 %collective-permute-start.32 = (bf16[256,256]{1,0:T(8,128)(2,1)S(1)}, bf16[256,256]{1,0:T(8,128)(2,1)S(1)}, u32[]{:S(2)}, u32[]{:S(2)}) collective-permute-start(bf16[256,256]{1,0:T(8,128)(2,1)S(1)} %add_convert_fusion.3), channel_id=1, source_target_pairs={{0,8},{8,0},{16,24},{24,16},{1,9},{9,1},{17,25},{25,17},{2,10},{10... | collective-permute-start | bytes 393224 | tf_op jit(solution)/shard_map/ppermute | solution.py:22
  140.1 6.0 %collective-permute-start.36 = (bf16[256,256]{1,0:T(8,128)(2,1)S(1)}, bf16[256,256]{1,0:T(8,128)(2,1)S(1)}, u32[]{:S(2)}, u32[]{:S(2)}) collective-permute-start(bf16[256,256]{1,0:T(8,128)(2,1)S(1)} %add_convert_fusion.2), channel_id=1, source_target_pairs={{0,8},{8,0},{16,24},{24,16},{1,9},{9,1},{17,25},{25,17},{2,10},{10... | collective-permute-start | bytes 393224 | tf_op jit(solution)/shard_map/ppermute | solution.py:22
  141.9 5.3 %collective-permute-start.37 = (bf16[64,2048]{1,0:T(8,128)(2,1)S(1)}, bf16[64,2048]{1,0:T(8,128)(2,1)S(1)}, u32[]{:S(2)}, u32[]{:S(2)}) collective-permute-start(bf16[64,2048]{1,0:T(8,128)(2,1)S(1)} %pad_maximum_fusion.4), channel_id=1, source_target_pairs={{0,1},{1,0},{2,3},{3,2},{4,5},{5,4},{6,7},{7,6},{8,9},{9,8},{10,11... | collective-permute-start | bytes 786440 | tf_op jit(solution)/shard_map/ppermute | solution.py:22
  143.2 4.0 %collective-permute-start.38 = (bf16[64,2048]{1,0:T(8,128)(2,1)S(1)}, bf16[64,2048]{1,0:T(8,128)(2,1)S(1)}, u32[]{:S(2)}, u32[]{:S(2)}) collective-permute-start(bf16[64,2048]{1,0:T(8,128)(2,1)S(1)} %pad_maximum_fusion.5), channel_id=1, source_target_pairs={{0,1},{1,0},{2,3},{3,2},{4,5},{5,4},{6,7},{7,6},{8,9},{9,8},{10,11... | collective-permute-start | bytes 786440 | tf_op jit(solution)/shard_map/ppermute | solution.py:22
  (16 other events, 69.3 us)

commit v12 on v10

--- a/solution.py
+++ b/solution.py
@@ -85,7 +85,7 @@
 
 def target_sums(target, incoming):
     rows, cols = target.shape
-    block = min(BLOCK, rows)
+    block = min(BLOCK // 2, rows)
 
     def body(target_ref, next_ref, incoming_ref, top_ref, sum_ref, window):
         shifted = shift_in(target_ref, next_ref, incoming_ref, window)
@@ -105,7 +105,7 @@
         out_specs=[row_spec(block, 1)] * 2,
         out_shape=[jax.ShapeDtypeStruct((rows, 1), F32)] * 2,
         scratch_shapes=[pltpu.VMEM((block + 8, cols), F32)],
-        compiler_params=params(24),
+        compiler_params=params(12),
         cost_estimate=cost(4 * rows * cols, 4 * rows * cols, rows * cols),
         name="target_sums",
     )(target, target, incoming)
@@ -113,7 +113,7 @@
 
 def target_pass(target, incoming):
     rows, cols = target.shape
-    block = min(BLOCK, rows)
+    block = min(BLOCK // 2, rows)
 
     def body(target_ref, next_ref, incoming_ref, prob_ref, entropy_ref, window):
         shifted = shift_in(target_ref, next_ref, incoming_ref, window)
@@ -143,7 +143,7 @@
             jax.ShapeDtypeStruct((rows, 1), F32),
         ],
         scratch_shapes=[pltpu.VMEM((block + 8, cols), F32)],
-        compiler_params=params(24),
+        compiler_params=params(12),
         cost_estimate=cost(6 * rows * cols, 8 * rows * cols, rows * cols),
         name="target_pass",
     )(target, target, incoming)
@@ -151,7 +151,7 @@
 
 def target_probs(target, incoming, top, total):
     rows, cols = target.shape
-    block = min(BLOCK, rows)
+    block = min(BLOCK // 2, rows)
 
     def body(target_ref, next_ref, incoming_ref, top_ref, sum_ref, prob_ref, entropy_ref, window):
         shifted = shift_in(target_ref, next_ref, incoming_ref, window)
@@ -181,7 +181,7 @@
             jax.ShapeDtypeStruct((rows, 1), F32),
         ],
         scratch_shapes=[pltpu.VMEM((block + 8, cols), F32)],
-        compiler_params=params(24),
+        compiler_params=params(12),
         cost_estimate=cost(6 * rows * cols, 8 * rows * cols, rows * cols),
         name="target_probs",
     )(target, target, incoming, top, total)
@@ -239,7 +239,7 @@
             jax.ShapeDtypeStruct((rows, 1), F32),
             jax.ShapeDtypeStruct((rows, 1), F32),
         ],
-        compiler_params=params(16),
+        compiler_params=params(14),
         cost_estimate=cost(2 * rows * rank * width, 8 * rows * width, rows * width),
         name="draft_chunk",
     )(target, acts, *pieces, *carried)
@@ -310,7 +310,7 @@
             jax.ShapeDtypeStruct((rows, 1), F32),
         ],
         scratch_shapes=[pltpu.VMEM((rank, width), F32)],
-        compiler_params=params(16),
+        compiler_params=params(14),
         cost_estimate=cost(4 * rows * rank * width, 8 * rows * width, rows * width),
         name="grad_chunk",
     )(draft, prob, label, acts, vocab_proj, *sums, *extra)

time: 148 us -> 148 us (level)
  transfers between devices with their start and end apart: 39 -> 39, of which waited for: 16 -> 16; matrix products, arithmetic and copies ran while one was open for 24% -> 24% of each run, Pallas kernels for 7% -> 8%
where the time goes in v12:
time: 148 us; the launch traced here: 147 us
  starting transfers between devices  41.8 us (28%)
  waiting for transfers between devices  33.1 us (22%)
  matrix products  26 us (18%)
  Pallas kernels  19.6 us (13%)
  local copies, waits for them, and re-layouts  13.5 us (9%)
  other arithmetic  12 us (8%)
    ppermute x38, starting transfers between devices, swap(): return lax.ppermute(value, axis, pairs)  40.5 us
    ppermute x38, waiting for transfers between devices, swap(): return lax.ppermute(value, axis, pairs)  33.1 us
    dot_general x4, matrix products, on_device(): jnp.dot(part, columns(c), preferred_element_type=F32) * VOCAB_SCALE  13.8 us
    unnamed x57, local copies, waits for them, and re-layouts  10.8 us
    dot_general x4, matrix products, inner_cols(): lax.dot_general(left, right, (((1,), (1,)), ((), ())), preferred_element_...  10.6 us
    pallas_call x2, Pallas kernels, grad_chunk(): pl.pallas_call(body, grid=(rows // block,), in_specs=[row_spec(block, wid...  8.28 us
    pallas_call x2, Pallas kernels, draft_chunk(): pl.pallas_call(body, grid=(rows // block,), in_specs=[row_spec(block, wid...  6.57 us
    pallas_call x1, Pallas kernels, target_pass(): pl.pallas_call(body, grid=(rows // block,), in_specs=[row_spec(block, col...  4.7 us
  transfers between devices with their start and end apart: 39, of which 16 were waited for; matrix products, arithmetic and copies ran while one was open for 24% of the time, Pallas kernels for 8%

profile of v12, /device:TPU:0, one launch (start us, length us, event | category | flops | bytes accessed | tf_op | source)
XLA Modules:
  0.0 147.4 jit_solution(2926424217241920616)
XLA Ops:
  0.7 3.9 %fusion.34 = f16[128,1024]{1,0:T(8,128)(2,1)} fusion(bf16[2048,2048]{1,0:T(8,128)(2,1)} %param.11, bf16[256,2048]{1,0:T(8,128)(2,1)} %param.10, s32[]{:T(128)S(6)} %select_n.175), kind=kOutput, calls=%fused_computation.22 | convolution fusion | flops 537133056 | bytes 4980740 | tf_op jit(solution)/shard_map/dot_general | solution.py:441
  4.6 3.0 %collective-permute-start.1 = (f16[128,1024]{1,0:T(8,128)(2,1)}, f16[128,1024]{1,0:T(8,128)(2,1)}, u32[]{:S(2)}, u32[]{:S(2)}) collective-permute-start(f16[128,1024]{1,0:T(8,128)(2,1)} %fusion.34), channel_id=1, source_target_pairs={{0,8},{8,0},{16,24},{24,16},{1,9},{9,1},{17,25},{25,17},{2,10},{10... | collective-permute-start | bytes 786440 | tf_op jit(solution)/shard_map/ppermute | solution.py:22
  8.5 1.3 collective-permute-start.2
  9.8 3.6 %fusion.37 = f16[128,1024]{1,0:T(8,128)(2,1)} fusion(bf16[2048,2048]{1,0:T(8,128)(2,1)} %param.11, bf16[256,2048]{1,0:T(8,128)(2,1)S(1)} %copy-done.19, s32[]{:T(128)S(6)} %select_n.175), kind=kOutput, calls=%fused_computation.23 | convolution fusion | flops 537133056 | bytes 4980740 | tf_op jit(solution)/shard_map/dot_general | solution.py:441
  13.4 2.6 %collective-permute-start.4 = (f16[128,1024]{1,0:T(8,128)(2,1)}, f16[128,1024]{1,0:T(8,128)(2,1)}, u32[]{:S(2)}, u32[]{:S(2)}) collective-permute-start(f16[128,1024]{1,0:T(8,128)(2,1)} %fusion.37), channel_id=1, source_target_pairs={{0,8},{8,0},{16,24},{24,16},{1,9},{9,1},{17,25},{25,17},{2,10},{10... | collective-permute-start | bytes 786440 | tf_op jit(solution)/shard_map/ppermute | solution.py:22
  17.5 3.3 %fusion.44 = (f16[128,1024]{1,0:T(8,128)(2,1)S(1)}, f32[128,1024]{1,0:T(8,128)S(1)}) fusion(f16[128,1024]{1,0:T(8,128)(2,1)} %collective-permute-done.1, bf16[2048,2048]{1,0:T(8,128)(2,1)} %param.11, bf16[256,2048]{1,0:T(8,128)(2,1)} %param.10, s32[]{:T(128)S(6)} %select_n.178), kind=kOutput, calls=%fused_computation.49 | convolution fusion | flops 537395200 | bytes 5767172 | tf_op jit(solution)/shard_map/dot_general | solution.py:441
  20.9 2.7 %collective-permute-start.6 = (f16[128,1024]{1,0:T(8,128)(2,1)S(1)}, f16[128,1024]{1,0:T(8,128)(2,1)S(1)}, u32[]{:S(2)}, u32[]{:S(2)}) collective-permute-start(f16[128,1024]{1,0:T(8,128)(2,1)S(1)} %get-tuple-element.112), channel_id=1, source_target_pairs={{0,16},{8,24},{16,0},{24,8},{1,17},{9,25},{17,1},{25,9},{2,18},{10... | collective-permute-start | bytes 786440 | tf_op jit(solution)/shard_map/ppermute | solution.py:22
  24.6 1.6 %collective-permute-start.3 = (f16[256,256]{1,0:T(8,128)(2,1)S(1)}, f16[256,256]{1,0:T(8,128)(2,1)S(1)}, u32[]{:S(2)}, u32[]{:S(2)}) collective-permute-start(f16[256,256]{1,0:T(8,128)(2,1)S(1)} %dynamic-slice_convert_fusion.6), channel_id=1, source_target_pairs={{0,2},{1,3},{2,0},{3,1},{4,6},{5,7},{6,4},{7,5},{8,10},{9,11},{10,... | collective-permute-start | bytes 393224 | tf_op jit(solution)/shard_map/ppermute | solution.py:22
  26.1 3.0 %fusion.45 = (f16[128,1024]{1,0:T(8,128)(2,1)S(1)}, f32[128,1024]{1,0:T(8,128)S(1)}) fusion(f16[128,1024]{1,0:T(8,128)(2,1)} %collective-permute-done.4, bf16[2048,2048]{1,0:T(8,128)(2,1)} %param.11, bf16[256,2048]{1,0:T(8,128)(2,1)S(1)} %copy-done.20, s32[]{:T(128)S(6)} %select_n.178), kind=kOutput, calls=%fused_computation.50 | convolution fusion | flops 537395200 | bytes 5767172 | tf_op jit(solution)/shard_map/dot_general | solution.py:441
  30.3 1.6 %collective-permute-start.5 = (f16[256,256]{1,0:T(8,128)(2,1)S(1)}, f16[256,256]{1,0:T(8,128)(2,1)S(1)}, u32[]{:S(2)}, u32[]{:S(2)}) collective-permute-start(f16[256,256]{1,0:T(8,128)(2,1)S(1)} %fusion.49), channel_id=1, source_target_pairs={{0,4},{1,5},{2,6},{3,7},{4,0},{5,1},{6,2},{7,3},{8,12},{9,13},{10,... | collective-permute-start | bytes 393224 | tf_op jit(solution)/shard_map/ppermute | solution.py:22
  31.9 4.7 %target_pass.1 = (f32[1024,2048]{1,0:T(8,128)S(1)}, f32[1024,1]{1,0:T(8,128)S(1)}) custom-call(f32[1024,2048]{1,0:T(8,128)S(1)} %bitcast.9, f32[1024,2048]{1,0:T(8,128)S(1)} %bitcast.9, f32[8,2048]{1,0:T(8,128)S(1)} %collective-permute-done.2.incoming_ref), custom_call_target="tpu_custom_call" | custom-call | flops 3072 | bytes 4096 | tf_op jit(solution)/shard_map/target_pass/pallas_call | solution.py:132
  36.6 3.3 %copy-done.2 = f32[1024,2048]{1,0:T(8,128)} copy-done((f32[1024,2048]{1,0:T(8,128)}, f32[1024,2048]{1,0:T(8,128)S(1)}, u32[]{:S(2)}) %copy-start.2) | copy-done | bytes 8388632
  42.7 1.6 %collective-permute-start.7 = (bf16[256,256]{1,0:T(8,128)(2,1)S(1)}, bf16[256,256]{1,0:T(8,128)(2,1)S(1)}, u32[]{:S(2)}, u32[]{:S(2)}) collective-permute-start(bf16[256,256]{1,0:T(8,128)(2,1)S(1)} %multiply_convert_fusion.3), channel_id=1, source_target_pairs={{0,2},{1,3},{2,0},{3,1},{4,6},{5,7},{6,4},{7,5},{8,10},{9,11},{10,... | collective-permute-start | bytes 393224 | tf_op jit(solution)/shard_map/ppermute | solution.py:22
  44.2 2.7 %collective-permute-done.8 = f16[128,1024]{1,0:T(8,128)(2,1)S(1)} collective-permute-done((f16[128,1024]{1,0:T(8,128)(2,1)S(1)}, f16[128,1024]{1,0:T(8,128)(2,1)S(1)}, u32[]{:S(2)}, u32[]{:S(2)}) %collective-permute-start.8) | collective-permute-done | bytes 262176 | tf_op jit(solution)/shard_map/ppermute | solution.py:22
  46.9 1.8 %multiply_convert_fusion.own_ref = bf16[128,1024]{1,0:T(8,128)(2,1)} fusion(f16[128,1024]{1,0:T(8,128)(2,1)S(1)} %collective-permute-done.8, f32[128,1024]{1,0:T(8,128)S(1)} %get-tuple-element.238, f16[128,1024]{1,0:T(8,128)(2,1)} %collective-permute-done.4), kind=kLoop, calls=%fused_computation.36 | loop fusion | flops 786432 | bytes 1310720 | tf_op jit(solution)/shard_map/convert_element_type | solution.py:448
  50.7 1.8 %collective-permute-done.10.other_ref = bf16[128,1024]{1,0:T(8,128)(2,1)S(1)} collective-permute-done((bf16[128,1024]{1,0:T(8,128)(2,1)S(1)}, bf16[128,1024]{1,0:T(8,128)(2,1)S(1)}, u32[]{:S(2)}, u32[]{:S(2)}) %collective-permute-start.10) | collective-permute-done | bytes 262176 | tf_op jit(solution)/shard_map/ppermute | solution.py:22
  53.4 3.4 %copy-done.1 = f32[1024,2048]{1,0:T(8,128)S(1)} copy-done((f32[1024,2048]{1,0:T(8,128)S(1)}, f32[1024,2048]{1,0:T(8,128)}, u32[]{:S(2)}) %copy-start.1) | copy-done | bytes 8388632
  57.8 2.5 %draft_chunk.2 = (f32[1024,1024]{1,0:T(8,128)S(1)}, bf16[256,1024]{1,0:T(8,128)(2,1)S(1)}, f32[1024,1]{1,0:T(8,128)S(1)}, f32[1024,1]{1,0:T(8,128)S(1)}) custom-call(f32[1024,2048]{1,0:T(8,128)S(1)} %copy-done.1, bf16[1024,256]{1,0:T(8,128)(2,1)S(1)} %pad_maximum_fusion.acts_ref, bf16[128,1024]{1,0:T(8,128)(2,1)S(1)} %multiply_convert_fusion.1.own_ref, ...), custom_call_target="tpu_custom_call" | custom-call | flops 131072 | bytes 2048 | tf_op jit(solution)/shard_map/draft_chunk/pallas_call | solution.py:220
  60.3 4.1 %draft_chunk.3 = (f32[1024,1024]{1,0:T(8,128)S(1)}, bf16[256,1024]{1,0:T(8,128)(2,1)S(1)}, f32[1024,1]{1,0:T(8,128)S(1)}, f32[1024,1]{1,0:T(8,128)S(1)}) custom-call(f32[1024,2048]{1,0:T(8,128)S(1)} %copy-done.1, bf16[1024,256]{1,0:T(8,128)(2,1)S(1)} %pad_maximum_fusion.acts_ref, bf16[128,1024]{1,0:T(8,128)(2,1)} %multiply_convert_fusion.own_ref, ...), custom_call_target="tpu_custom_call" | custom-call | flops 131072 | bytes 2048 | tf_op jit(solution)/shard_map/draft_chunk/pallas_call | solution.py:220
  64.4 4.1 %grad_chunk.2 = (bf16[128,1024]{1,0:T(8,128)(2,1)S(1)}, f32[128,1024]{1,0:T(8,128)S(1)}, f32[1024,256]{1,0:T(8,128)S(1)}, f32[1024,1]{1,0:T(8,128)S(1)}) custom-call(f32[1024,1024]{1,0:T(8,128)S(1)} %get-tuple-element.136.draft_ref, f32[1024,2048]{1,0:T(8,128)S(1)} %bitcast.11, s32[1024,1]{1,0:T(8,128)S(1)} %copy.11.label_ref, ...), custom_call_target="tpu_custom_call" | custom-call | flops 262144 | bytes 2048 | tf_op jit(solution)/shard_map/grad_chunk/pallas_call | solution.py:292
  68.6 4.2 %grad_chunk.3 = (bf16[128,1024]{1,0:T(8,128)(2,1)S(1)}, f32[128,1024]{1,0:T(8,128)S(1)}, f32[1024,256]{1,0:T(8,128)S(1)}, f32[1024,1]{1,0:T(8,128)S(1)}) custom-call(f32[1024,1024]{1,0:T(8,128)S(1)} %get-tuple-element.142.draft_ref, f32[1024,2048]{1,0:T(8,128)S(1)} %bitcast.11, s32[1024,1]{1,0:T(8,128)S(1)} %copy.11.label_ref, ...), custom_call_target="tpu_custom_call" | custom-call | flops 262144 | bytes 2048 | tf_op jit(solution)/shard_map/grad_chunk/pallas_call | solution.py:292
  74.4 2.4 %collective-permute-done.12 = bf16[128,1024]{1,0:T(8,128)(2,1)S(1)} collective-permute-done((bf16[128,1024]{1,0:T(8,128)(2,1)S(1)}, bf16[128,1024]{1,0:T(8,128)(2,1)S(1)}, u32[]{:S(2)}, u32[]{:S(2)}) %collective-permute-start.12) | collective-permute-done | bytes 262176 | tf_op jit(solution)/shard_map/ppermute | solution.py:22
  77.8 2.9 %collective-permute-start.13 = (bf16[128,1024]{1,0:T(8,128)(2,1)S(1)}, bf16[128,1024]{1,0:T(8,128)(2,1)S(1)}, u32[]{:S(2)}, u32[]{:S(2)}) collective-permute-start(bf16[128,1024]{1,0:T(8,128)(2,1)S(1)} %fusion.46), channel_id=1, source_target_pairs={{0,16},{8,24},{16,0},{24,8},{1,17},{9,25},{17,1},{25,9},{2,18},{10... | collective-permute-start | bytes 786440 | tf_op jit(solution)/shard_map/ppermute | solution.py:22
  81.8 1.6 %collective-permute-start.15 = (bf16[256,256]{1,0:T(8,128)(2,1)S(1)}, bf16[256,256]{1,0:T(8,128)(2,1)S(1)}, u32[]{:S(2)}, u32[]{:S(2)}) collective-permute-start(bf16[256,256]{1,0:T(8,128)(2,1)S(1)} %dynamic-slice_convert_fusion.5), channel_id=1, source_target_pairs={{0,2},{1,3},{2,0},{3,1},{4,6},{5,7},{6,4},{7,5},{8,10},{9,11},{10,... | collective-permute-start | bytes 393224 | tf_op jit(solution)/shard_map/ppermute | solution.py:22
  83.4 8.7 %collective-permute-done.16 = bf16[128,1024]{1,0:T(8,128)(2,1)S(1)} collective-permute-done((bf16[128,1024]{1,0:T(8,128)(2,1)}, bf16[128,1024]{1,0:T(8,128)(2,1)S(1)}, u32[]{:S(2)}, u32[]{:S(2)}) %collective-permute-start.16) | collective-permute-done | bytes 262176 | tf_op jit(solution)/shard_map/ppermute | solution.py:22
  92.3 1.6 %collective-permute-start.18 = (bf16[256,256]{1,0:T(8,128)(2,1)S(1)}, bf16[256,256]{1,0:T(8,128)(2,1)S(1)}, u32[]{:S(2)}, u32[]{:S(2)}) collective-permute-start(bf16[256,256]{1,0:T(8,128)(2,1)S(1)} %fusion.48), channel_id=1, source_target_pairs={{0,4},{1,5},{2,6},{3,7},{4,0},{5,1},{6,2},{7,3},{8,12},{9,13},{10,... | collective-permute-start | bytes 393224 | tf_op jit(solution)/shard_map/ppermute | solution.py:22
  93.8 1.2 add_convert_fusion.1
  95.1 2.1 %collective-permute-start.17 = (bf16[128,1024]{1,0:T(8,128)(2,1)S(1)}, bf16[128,1024]{1,0:T(8,128)(2,1)S(1)}, u32[]{:S(2)}, u32[]{:S(2)}) collective-permute-start(bf16[128,1024]{1,0:T(8,128)(2,1)S(1)} %add_convert_fusion.1), channel_id=1, source_target_pairs={{0,8},{8,0},{16,24},{24,16},{1,9},{9,1},{17,25},{25,17},{2,10},{10... | collective-permute-start | bytes 786440 | tf_op jit(solution)/shard_map/ppermute | solution.py:22
  97.1 3.7 %fusion.2 = f32[128,2048]{1,0:T(8,128)S(1)} fusion(bf16[128,1024]{1,0:T(8,128)(2,1)S(1)} %add_convert_fusion.1, bf16[2048,2048]{1,0:T(8,128)(2,1)} %param.11), kind=kOutput, calls=%fused_computation.2 | convolution fusion | flops 536870912 | bytes 5505024 | tf_op jit(solution)/shard_map/dot_general | solution.py:44
  101.1 1.6 %collective-permute-start.19 = (bf16[256,256]{1,0:T(8,128)(2,1)S(1)}, bf16[256,256]{1,0:T(8,128)(2,1)S(1)}, u32[]{:S(2)}, u32[]{:S(2)}) collective-permute-start(bf16[256,256]{1,0:T(8,128)(2,1)S(1)} %multiply_convert_fusion.2), channel_id=1, source_target_pairs={{0,2},{1,3},{2,0},{3,1},{4,6},{5,7},{6,4},{7,5},{8,10},{9,11},{10,... | collective-permute-start | bytes 393224 | tf_op jit(solution)/shard_map/ppermute | solution.py:22
  102.6 3.2 %collective-permute-done.20 = bf16[128,1024]{1,0:T(8,128)(2,1)S(1)} collective-permute-done((bf16[128,1024]{1,0:T(8,128)(2,1)S(1)}, bf16[128,1024]{1,0:T(8,128)(2,1)S(1)}, u32[]{:S(2)}, u32[]{:S(2)}) %collective-permute-start.20) | collective-permute-done | bytes 262176 | tf_op jit(solution)/shard_map/ppermute | solution.py:22
  106.2 2.1 %collective-permute-done.17 = bf16[128,1024]{1,0:T(8,128)(2,1)S(1)} collective-permute-done((bf16[128,1024]{1,0:T(8,128)(2,1)S(1)}, bf16[128,1024]{1,0:T(8,128)(2,1)S(1)}, u32[]{:S(2)}, u32[]{:S(2)}) %collective-permute-start.17) | collective-permute-done | bytes 262176 | tf_op jit(solution)/shard_map/ppermute | solution.py:22
  108.3 3.8 %fusion = f32[128,2048]{1,0:T(8,128)S(1)} fusion(bf16[128,1024]{1,0:T(8,128)(2,1)S(1)} %collective-permute-done.17, bf16[2048,2048]{1,0:T(8,128)(2,1)} %param.11), kind=kOutput, calls=%fused_computation | convolution fusion | flops 536870912 | bytes 5505024 | tf_op jit(solution)/shard_map/dot_general | solution.py:44
  113.3 2.0 %collective-permute-start.27 = (bf16[256,256]{1,0:T(8,128)(2,1)S(1)}, bf16[256,256]{1,0:T(8,128)(2,1)S(1)}, u32[]{:S(2)}, u32[]{:S(2)}) collective-permute-start(bf16[256,256]{1,0:T(8,128)(2,1)S(1)} %dynamic-slice_convert_fusion.4), channel_id=1, source_target_pairs={{0,8},{8,0},{16,24},{24,16},{1,9},{9,1},{17,25},{25,17},{2,10},{10... | collective-permute-start | bytes 393224 | tf_op jit(solution)/shard_map/ppermute | solution.py:22
  115.3 1.5 %fusion.16 = f32[128,2048]{1,0:T(8,128)S(1)} fusion(f32[128,2048]{1,0:T(8,128)S(1)} %fusion.2, bf16[128,1024]{1,0:T(8,128)(2,1)S(1)} %add_convert_fusion, bf16[2048,2048]{1,0:T(8,128)(2,1)S(1)} %bitcast.13), kind=kOutput, calls=%fused_computation.16 | convolution fusion | flops 537133056 | bytes 6553600 | tf_op jit(solution)/shard_map/dot_general | solution.py:44
  116.9 1.5 %broadcast_select_fusion = (f32[128,2048]{1,0:T(8,128)S(1)}, f32[128,2048]{1,0:T(8,128)S(1)}) fusion(f32[128,2048]{1,0:T(8,128)S(1)} %fusion.16, pred[]{:T(512)S(6)} %eq.12, f32[128,2048]{1,0:T(8,128)S(1)} %fusion, bf16[128,1024]{1,0:T(8,128)(2,1)S(1)} %collective-permute-done.21, bf16[2048,2048]{1,0:T(8,128)(2,1)S(1)} %bitcast.13), kind=kOutput, calls=%fused_computation.43 | convolution fusion | flops 537657344 | bytes 8650753 | tf_op jit(solution)/shard_map/dot_general | solution.py:44
  121.1 2.0 %collective-permute-start.35 = (bf16[256,256]{1,0:T(8,128)(2,1)S(1)}, bf16[256,256]{1,0:T(8,128)(2,1)S(1)}, u32[]{:S(2)}, u32[]{:S(2)}) collective-permute-start(bf16[256,256]{1,0:T(8,128)(2,1)S(1)} %add_convert_fusion.8), channel_id=1, source_target_pairs={{0,16},{8,24},{16,0},{24,8},{1,17},{9,25},{17,1},{25,9},{2,18},{10... | collective-permute-start | bytes 393224 | tf_op jit(solution)/shard_map/ppermute | solution.py:22
  123.2 1.6 %collective-permute-start.29 = (bf16[32,2048]{1,0:T(8,128)(2,1)S(1)}, bf16[32,2048]{1,0:T(8,128)(2,1)S(1)}, u32[]{:S(2)}, u32[]{:S(2)}) collective-permute-start(bf16[32,2048]{1,0:T(8,128)(2,1)S(1)} %dynamic-slice_convert_fusion.2), channel_id=1, source_target_pairs={{0,2},{1,3},{2,0},{3,1},{4,6},{5,7},{6,4},{7,5},{8,10},{9,11},{10,... | collective-permute-start | bytes 393224 | tf_op jit(solution)/shard_map/ppermute | solution.py:22
  125.9 2.3 %collective-permute-done.29 = bf16[32,2048]{1,0:T(8,128)(2,1)S(1)} collective-permute-done((bf16[32,2048]{1,0:T(8,128)(2,1)S(1)}, bf16[32,2048]{1,0:T(8,128)(2,1)S(1)}, u32[]{:S(2)}, u32[]{:S(2)}) %collective-permute-start.29) | collective-permute-done | bytes 131104 | tf_op jit(solution)/shard_map/ppermute | solution.py:22
  130.9 2.4 %collective-permute-done.31 = bf16[32,2048]{1,0:T(8,128)(2,1)S(1)} collective-permute-done((bf16[32,2048]{1,0:T(8,128)(2,1)S(1)}, bf16[32,2048]{1,0:T(8,128)(2,1)S(1)}, u32[]{:S(2)}, u32[]{:S(2)}) %collective-permute-start.31) | collective-permute-done | bytes 131104 | tf_op jit(solution)/shard_map/ppermute | solution.py:22
  133.3 1.6 %collective-permute-start.34 = (bf16[32,2048]{1,0:T(8,128)(2,1)S(1)}, bf16[32,2048]{1,0:T(8,128)(2,1)S(1)}, u32[]{:S(2)}, u32[]{:S(2)}) collective-permute-start(bf16[32,2048]{1,0:T(8,128)(2,1)S(1)} %add_convert_fusion.5), channel_id=1, source_target_pairs={{0,2},{1,3},{2,0},{3,1},{4,6},{5,7},{6,4},{7,5},{8,10},{9,11},{10,... | collective-permute-start | bytes 393224 | tf_op jit(solution)/shard_map/ppermute | solution.py:22
  134.9 1.6 %collective-permute-done.30 = bf16[32,2048]{1,0:T(8,128)(2,1)S(1)} collective-permute-done((bf16[32,2048]{1,0:T(8,128)(2,1)S(1)}, bf16[32,2048]{1,0:T(8,128)(2,1)S(1)}, u32[]{:S(2)}, u32[]{:S(2)}) %collective-permute-start.30) | collective-permute-done | bytes 131104 | tf_op jit(solution)/shard_map/ppermute | solution.py:22
  136.5 1.5 %collective-permute-start.33 = (bf16[32,2048]{1,0:T(8,128)(2,1)S(1)}, bf16[32,2048]{1,0:T(8,128)(2,1)S(1)}, u32[]{:S(2)}, u32[]{:S(2)}) collective-permute-start(bf16[32,2048]{1,0:T(8,128)(2,1)S(1)} %add_convert_fusion.4), channel_id=1, source_target_pairs={{0,4},{1,5},{2,6},{3,7},{4,0},{5,1},{6,2},{7,3},{8,12},{9,13},{10,... | collective-permute-start | bytes 393224 | tf_op jit(solution)/shard_map/ppermute | solution.py:22
  138.3 2.0 %collective-permute-start.36 = (bf16[256,256]{1,0:T(8,128)(2,1)S(1)}, bf16[256,256]{1,0:T(8,128)(2,1)S(1)}, u32[]{:S(2)}, u32[]{:S(2)}) collective-permute-start(bf16[256,256]{1,0:T(8,128)(2,1)S(1)} %add_convert_fusion.2), channel_id=1, source_target_pairs={{0,8},{8,0},{16,24},{24,16},{1,9},{9,1},{17,25},{25,17},{2,10},{10... | collective-permute-start | bytes 393224 | tf_op jit(solution)/shard_map/ppermute | solution.py:22
  140.4 1.2 collective-permute-done.33
  141.7 1.4 collective-permute-done.32
  143.1 1.4 collective-permute-done.36
  145.8 1.6 %maximum_convert_fusion = f32[256,2048]{1,0:T(8,128)} fusion(bf16[64,2048]{1,0:T(8,128)(2,1)S(1)} %get-tuple-element.216, bf16[64,2048]{1,0:T(8,128)(2,1)S(1)} %get-tuple-element.215, bf16[64,2048]{1,0:T(8,128)(2,1)S(1)} %get-tuple-element.240, bf16[64,2048]{1,0:T(8,128)(2,1)S(1)} %get-tuple-element.241), kind=kLoop, calls=%fused_computation.24 | loop fusion | flops 4194304 | bytes 3145728 | tf_op jit(solution)/shard_map/concatenate | solution.py:563
  (156 shorter events, 25.1 us)
Async XLA Ops:
  0.6 15.4 %copy-start = (bf16[1024,1024]{1,0:T(8,128)(2,1)S(1)}, bf16[1024,1024]{1,0:T(8,128)(2,1)}, u32[]{:S(2)}) copy-start(bf16[1024,1024]{1,0:T(8,128)(2,1)} %param.6) | copy-start | bytes 6291460
  0.6 9.1 %copy-start.19 = (bf16[256,2048]{1,0:T(8,128)(2,1)S(1)}, bf16[256,2048]{1,0:T(8,128)(2,1)}, u32[]{:S(2)}) copy-start(bf16[256,2048]{1,0:T(8,128)(2,1)} %param.10) | copy-start | bytes 3145732
  4.6 11.4 %copy-start.21 = (bf16[1024,256]{1,0:T(8,128)(2,1)S(1)}, bf16[1024,256]{1,0:T(8,128)(2,1)}, u32[]{:S(2)}) copy-start(bf16[1024,256]{1,0:T(8,128)(2,1)} %param.9) | copy-start | bytes 1572868
  4.6 12.9 %collective-permute-start.1 = (f16[128,1024]{1,0:T(8,128)(2,1)}, f16[128,1024]{1,0:T(8,128)(2,1)}, u32[]{:S(2)}, u32[]{:S(2)}) collective-permute-start(f16[128,1024]{1,0:T(8,128)(2,1)} %fusion.34), channel_id=1, source_target_pairs={{0,8},{8,0},{16,24},{24,16},{1,9},{9,1},{17,25},{25,17},{2,10},{10... | collective-permute-start | bytes 786440 | tf_op jit(solution)/shard_map/ppermute | solution.py:22
  8.5 9.0 %collective-permute-start.2 = (f32[8,2048]{1,0:T(8,128)S(1)}, f32[8,2048]{1,0:T(8,128)S(1)}, u32[]{:S(2)}, u32[]{:S(2)}) collective-permute-start(f32[8,2048]{1,0:T(8,128)S(1)} %slice.22), channel_id=1, source_target_pairs={{8,0},{16,8},{24,16},{9,1},{17,9},{25,17},{10,2},{18,10},{26,18},{... | collective-permute-start | bytes 196616 | tf_op jit(solution)/shard_map/ppermute | solution.py:454
  13.4 12.8 %collective-permute-start.4 = (f16[128,1024]{1,0:T(8,128)(2,1)}, f16[128,1024]{1,0:T(8,128)(2,1)}, u32[]{:S(2)}, u32[]{:S(2)}) collective-permute-start(f16[128,1024]{1,0:T(8,128)(2,1)} %fusion.37), channel_id=1, source_target_pairs={{0,8},{8,0},{16,24},{24,16},{1,9},{9,1},{17,25},{25,17},{2,10},{10... | collective-permute-start | bytes 786440 | tf_op jit(solution)/shard_map/ppermute | solution.py:22
  17.5 6.0 %collective-permute-start = (f16[512,256]{1,0:T(8,128)(2,1)}, f16[512,256]{1,0:T(8,128)(2,1)}, u32[]{:S(2)}, u32[]{:S(2)}) collective-permute-start(f16[512,256]{1,0:T(8,128)(2,1)} %dynamic-slice_convert_fusion), channel_id=1, source_target_pairs={{0,1},{1,0},{2,3},{3,2},{4,5},{5,4},{6,7},{7,6},{8,9},{9,8},{10,11... | collective-permute-start | bytes 786440 | tf_op jit(solution)/shard_map/ppermute | solution.py:22
  17.5 14.4 %slice-start = ((s8[8388608]{0:T(1024)(128)(4,1)}), s8[4194304]{0:T(1024)(128)(4,1)S(1)}, s32[]{:S(2)}) async-start(s8[8388608]{0:T(1024)(128)(4,1)} %bitcast.8), calls=%async_computation | async-start | bytes 8388608
  20.8 11.0 %slice-start.1 = ((s8[8388608]{0:T(1024)(128)(4,1)}), s8[4194304]{0:T(1024)(128)(4,1)S(1)}, s32[]{:S(2)}) async-start(s8[8388608]{0:T(1024)(128)(4,1)} %bitcast.8), calls=%async_computation.1 | async-start | bytes 8388608
  20.9 20.4 %collective-permute-start.6 = (f16[128,1024]{1,0:T(8,128)(2,1)S(1)}, f16[128,1024]{1,0:T(8,128)(2,1)S(1)}, u32[]{:S(2)}, u32[]{:S(2)}) collective-permute-start(f16[128,1024]{1,0:T(8,128)(2,1)S(1)} %get-tuple-element.112), channel_id=1, source_target_pairs={{0,16},{8,24},{16,0},{24,8},{1,17},{9,25},{17,1},{25,9},{2,18},{10... | collective-permute-start | bytes 786440 | tf_op jit(solution)/shard_map/ppermute | solution.py:22
  24.5 18.0 %copy-start.14 = (f32[512,256]{1,0:T(8,128)}, f32[512,256]{1,0:T(8,128)S(1)}, u32[]{:S(2)}) copy-start(f32[512,256]{1,0:T(8,128)S(1)} %convert_add_fusion.3) | copy-start | bytes 1572868
  24.6 5.7 %collective-permute-start.3 = (f16[256,256]{1,0:T(8,128)(2,1)S(1)}, f16[256,256]{1,0:T(8,128)(2,1)S(1)}, u32[]{:S(2)}, u32[]{:S(2)}) collective-permute-start(f16[256,256]{1,0:T(8,128)(2,1)S(1)} %dynamic-slice_convert_fusion.6), channel_id=1, source_target_pairs={{0,2},{1,3},{2,0},{3,1},{4,6},{5,7},{6,4},{7,5},{8,10},{9,11},{10,... | collective-permute-start | bytes 393224 | tf_op jit(solution)/shard_map/ppermute | solution.py:22
  29.1 17.8 %collective-permute-start.8 = (f16[128,1024]{1,0:T(8,128)(2,1)S(1)}, f16[128,1024]{1,0:T(8,128)(2,1)S(1)}, u32[]{:S(2)}, u32[]{:S(2)}) collective-permute-start(f16[128,1024]{1,0:T(8,128)(2,1)S(1)} %get-tuple-element.116), channel_id=1, source_target_pairs={{0,16},{8,24},{16,0},{24,8},{1,17},{9,25},{17,1},{25,9},{2,18},{10... | collective-permute-start | bytes 786440 | tf_op jit(solution)/shard_map/ppermute | solution.py:22
  30.3 12.2 %collective-permute-start.5 = (f16[256,256]{1,0:T(8,128)(2,1)S(1)}, f16[256,256]{1,0:T(8,128)(2,1)S(1)}, u32[]{:S(2)}, u32[]{:S(2)}) collective-permute-start(f16[256,256]{1,0:T(8,128)(2,1)S(1)} %fusion.49), channel_id=1, source_target_pairs={{0,4},{1,5},{2,6},{3,7},{4,0},{5,1},{6,2},{7,3},{8,12},{9,13},{10,... | collective-permute-start | bytes 393224 | tf_op jit(solution)/shard_map/ppermute | solution.py:22
  42.3 10.1 %collective-permute-start.10 = (bf16[128,1024]{1,0:T(8,128)(2,1)S(1)}, bf16[128,1024]{1,0:T(8,128)(2,1)S(1)}, u32[]{:S(2)}, u32[]{:S(2)}) collective-permute-start(bf16[128,1024]{1,0:T(8,128)(2,1)S(1)} %multiply_convert_fusion.1.own_ref), channel_id=1, source_target_pairs={{0,8},{8,0},{16,24},{24,16},{1,9},{9,1},{17,25},{25,17},{2,10},{10... | collective-permute-start | bytes 786440 | tf_op jit(solution)/shard_map/ppermute | solution.py:22
  42.7 6.1 %collective-permute-start.7 = (bf16[256,256]{1,0:T(8,128)(2,1)S(1)}, bf16[256,256]{1,0:T(8,128)(2,1)S(1)}, u32[]{:S(2)}, u32[]{:S(2)}) collective-permute-start(bf16[256,256]{1,0:T(8,128)(2,1)S(1)} %multiply_convert_fusion.3), channel_id=1, source_target_pairs={{0,2},{1,3},{2,0},{3,1},{4,6},{5,7},{6,4},{7,5},{8,10},{9,11},{10,... | collective-permute-start | bytes 393224 | tf_op jit(solution)/shard_map/ppermute | solution.py:22
  48.8 3.7 %collective-permute-start.9 = (bf16[512,256]{1,0:T(8,128)(2,1)S(1)}, bf16[512,256]{1,0:T(8,128)(2,1)S(1)}, u32[]{:S(2)}, u32[]{:S(2)}) collective-permute-start(bf16[512,256]{1,0:T(8,128)(2,1)S(1)} %pad_maximum_fusion.2), channel_id=1, source_target_pairs={{0,1},{1,0},{2,3},{3,2},{4,5},{5,4},{6,7},{7,6},{8,9},{9,8},{10,11... | collective-permute-start | bytes 786440 | tf_op jit(solution)/shard_map/ppermute | solution.py:22
  49.6 10.6 %collective-permute-start.11 = (bf16[128,1024]{1,0:T(8,128)(2,1)}, bf16[128,1024]{1,0:T(8,128)(2,1)}, u32[]{:S(2)}, u32[]{:S(2)}) collective-permute-start(bf16[128,1024]{1,0:T(8,128)(2,1)} %multiply_convert_fusion.own_ref), channel_id=1, source_target_pairs={{0,8},{8,0},{16,24},{24,16},{1,9},{9,1},{17,25},{25,17},{2,10},{10... | collective-permute-start | bytes 786440 | tf_op jit(solution)/shard_map/ppermute | solution.py:22
  68.5 8.3 %collective-permute-start.12 = (bf16[128,1024]{1,0:T(8,128)(2,1)S(1)}, bf16[128,1024]{1,0:T(8,128)(2,1)S(1)}, u32[]{:S(2)}, u32[]{:S(2)}) collective-permute-start(bf16[128,1024]{1,0:T(8,128)(2,1)S(1)} %get-tuple-element.141), channel_id=1, source_target_pairs={{0,8},{8,0},{16,24},{24,16},{1,9},{9,1},{17,25},{25,17},{2,10},{10... | collective-permute-start | bytes 786440 | tf_op jit(solution)/shard_map/ppermute | solution.py:22
  73.6 18.5 %copy-start.4 = (f32[128,1024]{1,0:T(8,128)S(1)}, f32[128,1024]{1,0:T(8,128)}, u32[]{:S(2)}) copy-start(f32[128,1024]{1,0:T(8,128)} %copy-done.3) | copy-start | bytes 1572868
  77.5 3.2 %collective-permute-start.14 = (f32[512,256]{1,0:T(8,128)}, f32[512,256]{1,0:T(8,128)S(1)}, u32[]{:S(2)}, u32[]{:S(2)}) collective-permute-start(f32[512,256]{1,0:T(8,128)} %constant_dynamic-slice_fusion.2), channel_id=1, source_target_pairs={{0,1},{1,0},{2,3},{3,2},{4,5},{5,4},{6,7},{7,6},{8,9},{9,8},{10,11... | collective-permute-start | bytes 1572872 | tf_op jit(solution)/shard_map/ppermute | solution.py:22
  77.5 14.5 %collective-permute-start.16 = (bf16[128,1024]{1,0:T(8,128)(2,1)}, bf16[128,1024]{1,0:T(8,128)(2,1)S(1)}, u32[]{:S(2)}, u32[]{:S(2)}) collective-permute-start(bf16[128,1024]{1,0:T(8,128)(2,1)} %copy-done.13), channel_id=1, source_target_pairs={{0,8},{8,0},{16,24},{24,16},{1,9},{9,1},{17,25},{25,17},{2,10},{10... | collective-permute-start | bytes 786440 | tf_op jit(solution)/shard_map/ppermute | solution.py:22
  77.8 16.0 %collective-permute-start.13 = (bf16[128,1024]{1,0:T(8,128)(2,1)S(1)}, bf16[128,1024]{1,0:T(8,128)(2,1)S(1)}, u32[]{:S(2)}, u32[]{:S(2)}) collective-permute-start(bf16[128,1024]{1,0:T(8,128)(2,1)S(1)} %fusion.46), channel_id=1, source_target_pairs={{0,16},{8,24},{16,0},{24,8},{1,17},{9,25},{17,1},{25,9},{2,18},{10... | collective-permute-start | bytes 786440 | tf_op jit(solution)/shard_map/ppermute | solution.py:22
  81.8 10.4 %collective-permute-start.15 = (bf16[256,256]{1,0:T(8,128)(2,1)S(1)}, bf16[256,256]{1,0:T(8,128)(2,1)S(1)}, u32[]{:S(2)}, u32[]{:S(2)}) collective-permute-start(bf16[256,256]{1,0:T(8,128)(2,1)S(1)} %dynamic-slice_convert_fusion.5), channel_id=1, source_target_pairs={{0,2},{1,3},{2,0},{3,1},{4,6},{5,7},{6,4},{7,5},{8,10},{9,11},{10,... | collective-permute-start | bytes 393224 | tf_op jit(solution)/shard_map/ppermute | solution.py:22
  92.1 8.8 %copy-start.15 = (f32[512,256]{1,0:T(8,128)S(1)}, f32[512,256]{1,0:T(8,128)}, u32[]{:S(2)}) copy-start(f32[512,256]{1,0:T(8,128)} %copy-done.14) | copy-start | bytes 1572868
  92.1 8.8 %copy-start.18 = (f16[256,256]{1,0:T(8,128)(2,1)S(1)}, f16[256,256]{1,0:T(8,128)(2,1)}, u32[]{:S(2)}) copy-start(f16[256,256]{1,0:T(8,128)(2,1)} %copy-done.17) | copy-start | bytes 393220
  92.1 13.7 %collective-permute-start.20 = (bf16[128,1024]{1,0:T(8,128)(2,1)S(1)}, bf16[128,1024]{1,0:T(8,128)(2,1)S(1)}, u32[]{:S(2)}, u32[]{:S(2)}) collective-permute-start(bf16[128,1024]{1,0:T(8,128)(2,1)S(1)} %fusion.47), channel_id=1, source_target_pairs={{0,16},{8,24},{16,0},{24,8},{1,17},{9,25},{17,1},{25,9},{2,18},{10... | collective-permute-start | bytes 786440 | tf_op jit(solution)/shard_map/ppermute | solution.py:22
  92.3 8.6 %collective-permute-start.18 = (bf16[256,256]{1,0:T(8,128)(2,1)S(1)}, bf16[256,256]{1,0:T(8,128)(2,1)S(1)}, u32[]{:S(2)}, u32[]{:S(2)}) collective-permute-start(bf16[256,256]{1,0:T(8,128)(2,1)S(1)} %fusion.48), channel_id=1, source_target_pairs={{0,4},{1,5},{2,6},{3,7},{4,0},{5,1},{6,2},{7,3},{8,12},{9,13},{10,... | collective-permute-start | bytes 393224 | tf_op jit(solution)/shard_map/ppermute | solution.py:22
  95.1 13.2 %collective-permute-start.17 = (bf16[128,1024]{1,0:T(8,128)(2,1)S(1)}, bf16[128,1024]{1,0:T(8,128)(2,1)S(1)}, u32[]{:S(2)}, u32[]{:S(2)}) collective-permute-start(bf16[128,1024]{1,0:T(8,128)(2,1)S(1)} %add_convert_fusion.1), channel_id=1, source_target_pairs={{0,8},{8,0},{16,24},{24,16},{1,9},{9,1},{17,25},{25,17},{2,10},{10... | collective-permute-start | bytes 786440 | tf_op jit(solution)/shard_map/ppermute | solution.py:22
  101.1 5.0 %collective-permute-start.19 = (bf16[256,256]{1,0:T(8,128)(2,1)S(1)}, bf16[256,256]{1,0:T(8,128)(2,1)S(1)}, u32[]{:S(2)}, u32[]{:S(2)}) collective-permute-start(bf16[256,256]{1,0:T(8,128)(2,1)S(1)} %multiply_convert_fusion.2), channel_id=1, source_target_pairs={{0,2},{1,3},{2,0},{3,1},{4,6},{5,7},{6,4},{7,5},{8,10},{9,11},{10,... | collective-permute-start | bytes 393224 | tf_op jit(solution)/shard_map/ppermute | solution.py:22
  106.0 10.9 %collective-permute-start.21 = (bf16[128,1024]{1,0:T(8,128)(2,1)S(1)}, bf16[128,1024]{1,0:T(8,128)(2,1)S(1)}, u32[]{:S(2)}, u32[]{:S(2)}) collective-permute-start(bf16[128,1024]{1,0:T(8,128)(2,1)S(1)} %add_convert_fusion), channel_id=1, source_target_pairs={{0,8},{8,0},{16,24},{24,16},{1,9},{9,1},{17,25},{25,17},{2,10},{10... | collective-permute-start | bytes 786440 | tf_op jit(solution)/shard_map/ppermute | solution.py:22
  106.2 6.0 %collective-permute-start.22 = (bf16[512,256]{1,0:T(8,128)(2,1)S(1)}, bf16[512,256]{1,0:T(8,128)(2,1)S(1)}, u32[]{:S(2)}, u32[]{:S(2)}) collective-permute-start(bf16[512,256]{1,0:T(8,128)(2,1)S(1)} %pad_maximum_fusion.3), channel_id=1, source_target_pairs={{0,1},{1,0},{2,3},{3,2},{4,5},{5,4},{6,7},{7,6},{8,9},{9,8},{10,11... | collective-permute-start | bytes 786440 | tf_op jit(solution)/shard_map/ppermute | solution.py:22
  113.2 6.8 %collective-permute-start.23 = (bf16[256,256]{1,0:T(8,128)(2,1)S(1)}, bf16[256,256]{1,0:T(8,128)(2,1)S(1)}, u32[]{:S(2)}, u32[]{:S(2)}) collective-permute-start(bf16[256,256]{1,0:T(8,128)(2,1)S(1)} %dynamic-slice_convert_fusion.3), channel_id=1, source_target_pairs={{0,8},{8,0},{16,24},{24,16},{1,9},{9,1},{17,25},{25,17},{2,10},{10... | collective-permute-start | bytes 393224 | tf_op jit(solution)/shard_map/ppermute | solution.py:22
  113.3 7.7 %collective-permute-start.27 = (bf16[256,256]{1,0:T(8,128)(2,1)S(1)}, bf16[256,256]{1,0:T(8,128)(2,1)S(1)}, u32[]{:S(2)}, u32[]{:S(2)}) collective-permute-start(bf16[256,256]{1,0:T(8,128)(2,1)S(1)} %dynamic-slice_convert_fusion.4), channel_id=1, source_target_pairs={{0,8},{8,0},{16,24},{24,16},{1,9},{9,1},{17,25},{25,17},{2,10},{10... | collective-permute-start | bytes 393224 | tf_op jit(solution)/shard_map/ppermute | solution.py:22
  118.5 4.6 %collective-permute-start.26 = (f32[64,2048]{1,0:T(8,128)S(1)}, f32[64,2048]{1,0:T(8,128)S(1)}, u32[]{:S(2)}, u32[]{:S(2)}) collective-permute-start(f32[64,2048]{1,0:T(8,128)S(1)} %constant_dynamic-slice_fusion), channel_id=1, source_target_pairs={{0,1},{1,0},{2,3},{3,2},{4,5},{5,4},{6,7},{7,6},{8,9},{9,8},{10,11... | collective-permute-start | bytes 1572872 | tf_op jit(solution)/shard_map/ppermute | solution.py:22
  118.6 6.2 %collective-permute-start.25 = (f32[64,2048]{1,0:T(8,128)S(1)}, f32[64,2048]{1,0:T(8,128)S(1)}, u32[]{:S(2)}, u32[]{:S(2)}) collective-permute-start(f32[64,2048]{1,0:T(8,128)S(1)} %constant_dynamic-slice_fusion.1), channel_id=1, source_target_pairs={{0,1},{1,0},{2,3},{3,2},{4,5},{5,4},{6,7},{7,6},{8,9},{9,8},{10,11... | collective-permute-start | bytes 1572872 | tf_op jit(solution)/shard_map/ppermute | solution.py:22
  120.0 18.0 %collective-permute-start.24 = (bf16[256,256]{1,0:T(8,128)(2,1)S(1)}, bf16[256,256]{1,0:T(8,128)(2,1)S(1)}, u32[]{:S(2)}, u32[]{:S(2)}) collective-permute-start(bf16[256,256]{1,0:T(8,128)(2,1)S(1)} %add_convert_fusion.9), channel_id=1, source_target_pairs={{0,16},{8,24},{16,0},{24,8},{1,17},{9,25},{17,1},{25,9},{2,18},{10... | collective-permute-start | bytes 393224 | tf_op jit(solution)/shard_map/ppermute | solution.py:22
  121.1 17.2 %collective-permute-start.35 = (bf16[256,256]{1,0:T(8,128)(2,1)S(1)}, bf16[256,256]{1,0:T(8,128)(2,1)S(1)}, u32[]{:S(2)}, u32[]{:S(2)}) collective-permute-start(bf16[256,256]{1,0:T(8,128)(2,1)S(1)} %add_convert_fusion.8), channel_id=1, source_target_pairs={{0,16},{8,24},{16,0},{24,8},{1,17},{9,25},{17,1},{25,9},{2,18},{10... | collective-permute-start | bytes 393224 | tf_op jit(solution)/shard_map/ppermute | solution.py:22
  123.2 5.0 %collective-permute-start.29 = (bf16[32,2048]{1,0:T(8,128)(2,1)S(1)}, bf16[32,2048]{1,0:T(8,128)(2,1)S(1)}, u32[]{:S(2)}, u32[]{:S(2)}) collective-permute-start(bf16[32,2048]{1,0:T(8,128)(2,1)S(1)} %dynamic-slice_convert_fusion.2), channel_id=1, source_target_pairs={{0,2},{1,3},{2,0},{3,1},{4,6},{5,7},{6,4},{7,5},{8,10},{9,11},{10,... | collective-permute-start | bytes 393224 | tf_op jit(solution)/shard_map/ppermute | solution.py:22
  124.9 5.4 %collective-permute-start.28 = (bf16[32,2048]{1,0:T(8,128)(2,1)S(1)}, bf16[32,2048]{1,0:T(8,128)(2,1)S(1)}, u32[]{:S(2)}, u32[]{:S(2)}) collective-permute-start(bf16[32,2048]{1,0:T(8,128)(2,1)S(1)} %dynamic-slice_convert_fusion.1), channel_id=1, source_target_pairs={{0,4},{1,5},{2,6},{3,7},{4,0},{5,1},{6,2},{7,3},{8,12},{9,13},{10,... | collective-permute-start | bytes 393224 | tf_op jit(solution)/shard_map/ppermute | solution.py:22
  128.3 5.0 %collective-permute-start.31 = (bf16[32,2048]{1,0:T(8,128)(2,1)S(1)}, bf16[32,2048]{1,0:T(8,128)(2,1)S(1)}, u32[]{:S(2)}, u32[]{:S(2)}) collective-permute-start(bf16[32,2048]{1,0:T(8,128)(2,1)S(1)} %add_convert_fusion.7), channel_id=1, source_target_pairs={{0,4},{1,5},{2,6},{3,7},{4,0},{5,1},{6,2},{7,3},{8,12},{9,13},{10,... | collective-permute-start | bytes 393224 | tf_op jit(solution)/shard_map/ppermute | solution.py:22
  130.3 6.2 %collective-permute-start.30 = (bf16[32,2048]{1,0:T(8,128)(2,1)S(1)}, bf16[32,2048]{1,0:T(8,128)(2,1)S(1)}, u32[]{:S(2)}, u32[]{:S(2)}) collective-permute-start(bf16[32,2048]{1,0:T(8,128)(2,1)S(1)} %add_convert_fusion.6), channel_id=1, source_target_pairs={{0,2},{1,3},{2,0},{3,1},{4,6},{5,7},{6,4},{7,5},{8,10},{9,11},{10,... | collective-permute-start | bytes 393224 | tf_op jit(solution)/shard_map/ppermute | solution.py:22
  133.3 6.9 %collective-permute-start.34 = (bf16[32,2048]{1,0:T(8,128)(2,1)S(1)}, bf16[32,2048]{1,0:T(8,128)(2,1)S(1)}, u32[]{:S(2)}, u32[]{:S(2)}) collective-permute-start(bf16[32,2048]{1,0:T(8,128)(2,1)S(1)} %add_convert_fusion.5), channel_id=1, source_target_pairs={{0,2},{1,3},{2,0},{3,1},{4,6},{5,7},{6,4},{7,5},{8,10},{9,11},{10,... | collective-permute-start | bytes 393224 | tf_op jit(solution)/shard_map/ppermute | solution.py:22
  136.5 5.0 %collective-permute-start.33 = (bf16[32,2048]{1,0:T(8,128)(2,1)S(1)}, bf16[32,2048]{1,0:T(8,128)(2,1)S(1)}, u32[]{:S(2)}, u32[]{:S(2)}) collective-permute-start(bf16[32,2048]{1,0:T(8,128)(2,1)S(1)} %add_convert_fusion.4), channel_id=1, source_target_pairs={{0,4},{1,5},{2,6},{3,7},{4,0},{5,1},{6,2},{7,3},{8,12},{9,13},{10,... | collective-permute-start | bytes 393224 | tf_op jit(solution)/shard_map/ppermute | solution.py:22
  138.1 5.0 %collective-permute-start.32 = (bf16[256,256]{1,0:T(8,128)(2,1)S(1)}, bf16[256,256]{1,0:T(8,128)(2,1)S(1)}, u32[]{:S(2)}, u32[]{:S(2)}) collective-permute-start(bf16[256,256]{1,0:T(8,128)(2,1)S(1)} %add_convert_fusion.3), channel_id=1, source_target_pairs={{0,8},{8,0},{16,24},{24,16},{1,9},{9,1},{17,25},{25,17},{2,10},{10... | collective-permute-start | bytes 393224 | tf_op jit(solution)/shard_map/ppermute | solution.py:22
  138.3 6.2 %collective-permute-start.36 = (bf16[256,256]{1,0:T(8,128)(2,1)S(1)}, bf16[256,256]{1,0:T(8,128)(2,1)S(1)}, u32[]{:S(2)}, u32[]{:S(2)}) collective-permute-start(bf16[256,256]{1,0:T(8,128)(2,1)S(1)} %add_convert_fusion.2), channel_id=1, source_target_pairs={{0,8},{8,0},{16,24},{24,16},{1,9},{9,1},{17,25},{25,17},{2,10},{10... | collective-permute-start | bytes 393224 | tf_op jit(solution)/shard_map/ppermute | solution.py:22
  140.3 5.3 %collective-permute-start.37 = (bf16[64,2048]{1,0:T(8,128)(2,1)S(1)}, bf16[64,2048]{1,0:T(8,128)(2,1)S(1)}, u32[]{:S(2)}, u32[]{:S(2)}) collective-permute-start(bf16[64,2048]{1,0:T(8,128)(2,1)S(1)} %pad_maximum_fusion.4), channel_id=1, source_target_pairs={{0,1},{1,0},{2,3},{3,2},{4,5},{5,4},{6,7},{7,6},{8,9},{9,8},{10,11... | collective-permute-start | bytes 786440 | tf_op jit(solution)/shard_map/ppermute | solution.py:22
  141.6 4.0 %collective-permute-start.38 = (bf16[64,2048]{1,0:T(8,128)(2,1)S(1)}, bf16[64,2048]{1,0:T(8,128)(2,1)S(1)}, u32[]{:S(2)}, u32[]{:S(2)}) collective-permute-start(bf16[64,2048]{1,0:T(8,128)(2,1)S(1)} %pad_maximum_fusion.5), channel_id=1, source_target_pairs={{0,1},{1,0},{2,3},{3,2},{4,5},{5,4},{6,7},{7,6},{8,9},{9,8},{10,11... | collective-permute-start | bytes 786440 | tf_op jit(solution)/shard_map/ppermute | solution.py:22
  (19 other events, 69.0 us)

commit v13 on v10

--- a/solution.py
+++ b/solution.py
@@ -546,21 +546,43 @@
     grads[1].result()
     other_up = times_head(other_up, grad_pieces[1][1], 1)
     up_part = joined("grp", z_bits[0], own_up, other_up)
-    rank = up_part.shape[0] // 2
-    ups = [
-        over_voc(
-            line, part, bits, [F32] + [BF16] * len(v_bits), lambda total: total.astype(BF16), True
-        )
-        for part, bits in ((up_part[:rank], v_bits), (up_part[rank:], v_other))
-    ]
-    swaps = [chain for chain, _ in ups]
+    def core_steps():
+        away, kept = split_pair(up_part, "voc", v_bits)
+        arrived = yield from sent_over(line, away, "voc", v_bits[0])
+        return kept + arrived
+
+    core = Chain(core_steps())
+    downs[0].step()
+    core.step()
     loss = over_books(line.after(loss) + entropy, jnp.add, per_book)
     frame_loss = lax.dynamic_slice_in_dim(loss, book_part * block_rows, block_rows, 0)
     frame_loss = frame_loss.reshape(1, 1, block_rows)
-    for turn in (swaps, downs, swaps, swaps, swaps, downs, swaps):
+    downs[1].step()
+    part = core.result()
+    rank = part.shape[0] // 2
+    routes = (v_bits[1:], v_bits[:0:-1])
+    up_pieces = [[] for _ in routes]
+    ups = [
+        summed(
+            line, split_pair(piece, "voc", bits), "voc", bits, [BF16] * len(bits),
+            lambda total: total.astype(BF16), pieces, True,
+        )
+        for piece, bits, pieces in zip((part[:rank], part[rank:]), routes, up_pieces)
+    ]
+    for turn in (ups, ups, ups, downs):
         for chain in turn:
             chain.step()
-    grad_b = jnp.concatenate([result().astype(F32) for _, result in ups], 0)
+    for chain in ups:
+        chain.result()
+    whole = jnp.concatenate(
+        [joined("voc", bits[0], *pieces) for bits, pieces in zip(routes, up_pieces)], 0
+    )
+
+    def last_steps():
+        other = yield from sent_over(line, whole, "voc", v_bits[0])
+        return joined("voc", v_bits[0], whole, other)
+
+    grad_b = Chain(last_steps()).result().astype(F32)
     for chain in downs:
         chain.result()
     grad_a = jnp.concatenate(

time: 148 us -> 158 us (1.068)
  waiting for transfers between devices: 33.8 us -> 41.4 us
  other arithmetic: 12 us -> 16.7 us
  starting transfers between devices: 41.9 us -> 38.3 us
    ppermute x38 -> x36, waiting for transfers between devices: 33.8 us -> 41.4 us  [swap(): return lax.ppermute(value, axis, pairs)]
    ppermute x38 -> x36, starting transfers between devices: 40.6 us -> 37 us  [swap(): return lax.ppermute(value, axis, pairs)]
    add x0 -> x1, other arithmetic: none -> 1.83 us  [core_steps(): return kept + arrived]
    convert_element_type x8, other arithmetic: 0.3 us -> 2 us  [reduce_steps(): sent = part.astype(wires[-1])]
    unnamed x57 -> x67, local copies, waits for them, and re-layouts: 10.8 us -> 11.9 us
  transfers between devices with their start and end apart: 39 -> 37, of which waited for: 16 -> 17; matrix products, arithmetic and copies ran while one was open for 24% -> 25% of each run, Pallas kernels for 7% -> 7%
where the time goes in v13:
time: 158 us; the launch traced here: 157 us
  waiting for transfers between devices  41.4 us (26%)
  starting transfers between devices  38.3 us (24%)
  matrix products  25.9 us (16%)
  Pallas kernels  18.9 us (12%)
  other arithmetic  16.7 us (11%)
  local copies, waits for them, and re-layouts  14.6 us (9%)
    ppermute x36, waiting for transfers between devices, swap(): return lax.ppermute(value, axis, pairs)  41.4 us
    ppermute x36, starting transfers between devices, swap(): return lax.ppermute(value, axis, pairs)  37 us
    dot_general x4, matrix products, on_device(): jnp.dot(part, columns(c), preferred_element_type=F32) * VOCAB_SCALE  13.8 us
    unnamed x67, local copies, waits for them, and re-layouts  11.9 us
    dot_general x4, matrix products, inner_cols(): lax.dot_general(left, right, (((1,), (1,)), ((), ())), preferred_element_...  10.6 us
    pallas_call x2, Pallas kernels, grad_chunk(): pl.pallas_call(body, grid=(rows // block,), in_specs=[row_spec(block, wid...  8.28 us
    pallas_call x2, Pallas kernels, draft_chunk(): pl.pallas_call(body, grid=(rows // block,), in_specs=[row_spec(block, wid...  6.57 us
    pallas_call x1, Pallas kernels, target_pass(): pl.pallas_call(body, grid=(rows // block,), in_specs=[row_spec(block, col...  4.01 us
  transfers between devices with their start and end apart: 37, of which 17 were waited for; matrix products, arithmetic and copies ran while one was open for 25% of the time, Pallas kernels for 7%

profile of v13, /device:TPU:0, one launch (start us, length us, event | category | flops | bytes accessed | tf_op | source)
XLA Modules:
  0.0 157.1 jit_solution(4531417312182364939)
XLA Ops:
  0.7 3.9 %fusion.34 = f16[128,1024]{1,0:T(8,128)(2,1)} fusion(bf16[2048,2048]{1,0:T(8,128)(2,1)} %param.11, bf16[256,2048]{1,0:T(8,128)(2,1)} %param.10, s32[]{:T(128)S(6)} %select_n.165), kind=kOutput, calls=%fused_computation.26 | convolution fusion | flops 537133056 | bytes 4980740 | tf_op jit(solution)/shard_map/dot_general | solution.py:441
  4.6 3.0 %collective-permute-start.1 = (f16[128,1024]{1,0:T(8,128)(2,1)}, f16[128,1024]{1,0:T(8,128)(2,1)S(1)}, u32[]{:S(2)}, u32[]{:S(2)}) collective-permute-start(f16[128,1024]{1,0:T(8,128)(2,1)} %fusion.34), channel_id=1, source_target_pairs={{0,8},{8,0},{16,24},{24,16},{1,9},{9,1},{17,25},{25,17},{2,10},{10... | collective-permute-start | bytes 786440 | tf_op jit(solution)/shard_map/ppermute | solution.py:22
  8.5 1.3 collective-permute-start.2
  9.8 3.6 %fusion.37 = f16[128,1024]{1,0:T(8,128)(2,1)} fusion(bf16[2048,2048]{1,0:T(8,128)(2,1)} %param.11, bf16[256,2048]{1,0:T(8,128)(2,1)S(1)} %copy-done.24, s32[]{:T(128)S(6)} %select_n.165), kind=kOutput, calls=%fused_computation.27 | convolution fusion | flops 537133056 | bytes 4980740 | tf_op jit(solution)/shard_map/dot_general | solution.py:441
  13.4 2.6 %collective-permute-start.4 = (f16[128,1024]{1,0:T(8,128)(2,1)}, f16[128,1024]{1,0:T(8,128)(2,1)}, u32[]{:S(2)}, u32[]{:S(2)}) collective-permute-start(f16[128,1024]{1,0:T(8,128)(2,1)} %fusion.37), channel_id=1, source_target_pairs={{0,8},{8,0},{16,24},{24,16},{1,9},{9,1},{17,25},{25,17},{2,10},{10... | collective-permute-start | bytes 786440 | tf_op jit(solution)/shard_map/ppermute | solution.py:22
  17.6 3.3 %fusion.47 = (f16[128,1024]{1,0:T(8,128)(2,1)S(1)}, f32[128,1024]{1,0:T(8,128)S(1)}) fusion(f16[128,1024]{1,0:T(8,128)(2,1)S(1)} %collective-permute-done.1, bf16[2048,2048]{1,0:T(8,128)(2,1)} %param.11, bf16[256,2048]{1,0:T(8,128)(2,1)} %param.10, s32[]{:T(128)S(6)} %select_n.168), kind=kOutput, calls=%fused_computation.57 | convolution fusion | flops 537395200 | bytes 5767172 | tf_op jit(solution)/shard_map/dot_general | solution.py:441
  20.9 2.7 %collective-permute-start.6 = (f16[128,1024]{1,0:T(8,128)(2,1)S(1)}, f16[128,1024]{1,0:T(8,128)(2,1)S(1)}, u32[]{:S(2)}, u32[]{:S(2)}) collective-permute-start(f16[128,1024]{1,0:T(8,128)(2,1)S(1)} %get-tuple-element.108), channel_id=1, source_target_pairs={{0,16},{8,24},{16,0},{24,8},{1,17},{9,25},{17,1},{25,9},{2,18},{10... | collective-permute-start | bytes 786440 | tf_op jit(solution)/shard_map/ppermute | solution.py:22
  24.6 1.6 collective-permute-start.3
  26.1 3.0 %fusion.48 = (f16[128,1024]{1,0:T(8,128)(2,1)S(1)}, f32[128,1024]{1,0:T(8,128)S(1)}) fusion(f16[128,1024]{1,0:T(8,128)(2,1)} %collective-permute-done.4, bf16[2048,2048]{1,0:T(8,128)(2,1)} %param.11, bf16[256,2048]{1,0:T(8,128)(2,1)S(1)} %copy-done.25, s32[]{:T(128)S(6)} %select_n.168), kind=kOutput, calls=%fused_computation.58 | convolution fusion | flops 537395200 | bytes 5767172 | tf_op jit(solution)/shard_map/dot_general | solution.py:441
  30.3 1.6 %collective-permute-start.5 = (f16[256,256]{1,0:T(8,128)(2,1)S(1)}, f16[256,256]{1,0:T(8,128)(2,1)S(1)}, u32[]{:S(2)}, u32[]{:S(2)}) collective-permute-start(f16[256,256]{1,0:T(8,128)(2,1)S(1)} %fusion.52), channel_id=1, source_target_pairs={{0,4},{1,5},{2,6},{3,7},{4,0},{5,1},{6,2},{7,3},{8,12},{9,13},{10,... | collective-permute-start | bytes 393224 | tf_op jit(solution)/shard_map/ppermute | solution.py:22
  31.9 4.0 %target_pass.1 = (f32[1024,2048]{1,0:T(8,128)S(1)}, f32[1024,1]{1,0:T(8,128)S(1)}) custom-call(f32[1024,2048]{1,0:T(8,128)S(1)} %bitcast.9, f32[1024,2048]{1,0:T(8,128)S(1)} %bitcast.9, f32[8,2048]{1,0:T(8,128)S(1)} %collective-permute-done.2.incoming_ref), custom_call_target="tpu_custom_call" | custom-call | flops 3072 | bytes 4096 | tf_op jit(solution)/shard_map/target_pass/pallas_call | solution.py:132
  35.9 3.3 %copy-done.2 = f32[1024,2048]{1,0:T(8,128)} copy-done((f32[1024,2048]{1,0:T(8,128)}, f32[1024,2048]{1,0:T(8,128)S(1)}, u32[]{:S(2)}) %copy-start.2) | copy-done | bytes 8388632
  40.1 1.2 collective-permute-done.6
  41.7 1.6 collective-permute-start.7
  43.2 3.7 %collective-permute-done.8 = f16[128,1024]{1,0:T(8,128)(2,1)S(1)} collective-permute-done((f16[128,1024]{1,0:T(8,128)(2,1)S(1)}, f16[128,1024]{1,0:T(8,128)(2,1)S(1)}, u32[]{:S(2)}, u32[]{:S(2)}) %collective-permute-start.8) | collective-permute-done | bytes 262176 | tf_op jit(solution)/shard_map/ppermute | solution.py:22
  46.9 1.8 %multiply_convert_fusion.own_ref = bf16[128,1024]{1,0:T(8,128)(2,1)} fusion(f16[128,1024]{1,0:T(8,128)(2,1)S(1)} %collective-permute-done.8, f32[128,1024]{1,0:T(8,128)S(1)} %get-tuple-element.230, f16[128,1024]{1,0:T(8,128)(2,1)} %collective-permute-done.4), kind=kLoop, calls=%fused_computation.42 | loop fusion | flops 786432 | bytes 1310720 | tf_op jit(solution)/shard_map/convert_element_type | solution.py:448
  49.7 2.7 %collective-permute-done.10.other_ref = bf16[128,1024]{1,0:T(8,128)(2,1)S(1)} collective-permute-done((bf16[128,1024]{1,0:T(8,128)(2,1)S(1)}, bf16[128,1024]{1,0:T(8,128)(2,1)S(1)}, u32[]{:S(2)}, u32[]{:S(2)}) %collective-permute-start.10) | collective-permute-done | bytes 262176 | tf_op jit(solution)/shard_map/ppermute | solution.py:22
  53.9 3.4 %copy-done.1 = f32[1024,2048]{1,0:T(8,128)S(1)} copy-done((f32[1024,2048]{1,0:T(8,128)S(1)}, f32[1024,2048]{1,0:T(8,128)}, u32[]{:S(2)}) %copy-start.1) | copy-done | bytes 8388632
  58.2 2.5 %draft_chunk.2 = (f32[1024,1024]{1,0:T(8,128)S(1)}, bf16[256,1024]{1,0:T(8,128)(2,1)S(1)}, f32[1024,1]{1,0:T(8,128)S(1)}, f32[1024,1]{1,0:T(8,128)S(1)}) custom-call(f32[1024,2048]{1,0:T(8,128)S(1)} %copy-done.1, bf16[1024,256]{1,0:T(8,128)(2,1)S(1)} %pad_maximum_fusion.acts_ref, bf16[128,1024]{1,0:T(8,128)(2,1)S(1)} %multiply_convert_fusion.1.own_ref, ...), custom_call_target="tpu_custom_call" | custom-call | flops 131072 | bytes 2048 | tf_op jit(solution)/shard_map/draft_chunk/pallas_call | solution.py:220
  60.7 4.1 %draft_chunk.3 = (f32[1024,1024]{1,0:T(8,128)S(1)}, bf16[256,1024]{1,0:T(8,128)(2,1)S(1)}, f32[1024,1]{1,0:T(8,128)S(1)}, f32[1024,1]{1,0:T(8,128)S(1)}) custom-call(f32[1024,2048]{1,0:T(8,128)S(1)} %copy-done.1, bf16[1024,256]{1,0:T(8,128)(2,1)S(1)} %pad_maximum_fusion.acts_ref, bf16[128,1024]{1,0:T(8,128)(2,1)} %multiply_convert_fusion.own_ref, ...), custom_call_target="tpu_custom_call" | custom-call | flops 131072 | bytes 2048 | tf_op jit(solution)/shard_map/draft_chunk/pallas_call | solution.py:220
  64.9 4.1 %grad_chunk.2 = (bf16[128,1024]{1,0:T(8,128)(2,1)S(1)}, f32[128,1024]{1,0:T(8,128)S(1)}, f32[1024,256]{1,0:T(8,128)S(1)}, f32[1024,1]{1,0:T(8,128)S(1)}) custom-call(f32[1024,1024]{1,0:T(8,128)S(1)} %get-tuple-element.132.draft_ref, f32[1024,2048]{1,0:T(8,128)S(1)} %bitcast.11, s32[1024,1]{1,0:T(8,128)S(1)} %copy.11.label_ref, ...), custom_call_target="tpu_custom_call" | custom-call | flops 262144 | bytes 2048 | tf_op jit(solution)/shard_map/grad_chunk/pallas_call | solution.py:292
  69.0 4.2 %grad_chunk.3 = (bf16[128,1024]{1,0:T(8,128)(2,1)S(1)}, f32[128,1024]{1,0:T(8,128)S(1)}, f32[1024,256]{1,0:T(8,128)S(1)}, f32[1024,1]{1,0:T(8,128)S(1)}) custom-call(f32[1024,1024]{1,0:T(8,128)S(1)} %get-tuple-element.138.draft_ref, f32[1024,2048]{1,0:T(8,128)S(1)} %bitcast.11, s32[1024,1]{1,0:T(8,128)S(1)} %copy.11.label_ref, ...), custom_call_target="tpu_custom_call" | custom-call | flops 262144 | bytes 2048 | tf_op jit(solution)/shard_map/grad_chunk/pallas_call | solution.py:292
  74.9 2.4 %collective-permute-done.12 = bf16[128,1024]{1,0:T(8,128)(2,1)S(1)} collective-permute-done((bf16[128,1024]{1,0:T(8,128)(2,1)S(1)}, bf16[128,1024]{1,0:T(8,128)(2,1)S(1)}, u32[]{:S(2)}, u32[]{:S(2)}) %collective-permute-start.12) | collective-permute-done | bytes 262176 | tf_op jit(solution)/shard_map/ppermute | solution.py:22
  78.5 2.9 %collective-permute-start.13 = (bf16[128,1024]{1,0:T(8,128)(2,1)}, bf16[128,1024]{1,0:T(8,128)(2,1)S(1)}, u32[]{:S(2)}, u32[]{:S(2)}) collective-permute-start(bf16[128,1024]{1,0:T(8,128)(2,1)} %fusion.49), channel_id=1, source_target_pairs={{0,16},{8,24},{16,0},{24,8},{1,17},{9,25},{17,1},{25,9},{2,18},{10... | collective-permute-start | bytes 786440 | tf_op jit(solution)/shard_map/ppermute | solution.py:22
  82.5 1.6 collective-permute-start.15
  84.1 8.4 %collective-permute-done.16 = bf16[128,1024]{1,0:T(8,128)(2,1)S(1)} collective-permute-done((bf16[128,1024]{1,0:T(8,128)(2,1)}, bf16[128,1024]{1,0:T(8,128)(2,1)S(1)}, u32[]{:S(2)}, u32[]{:S(2)}) %collective-permute-start.16) | collective-permute-done | bytes 262176 | tf_op jit(solution)/shard_map/ppermute | solution.py:22
  92.7 1.6 %collective-permute-start.18 = (bf16[256,256]{1,0:T(8,128)(2,1)S(1)}, bf16[256,256]{1,0:T(8,128)(2,1)S(1)}, u32[]{:S(2)}, u32[]{:S(2)}) collective-permute-start(bf16[256,256]{1,0:T(8,128)(2,1)S(1)} %fusion.51), channel_id=1, source_target_pairs={{0,4},{1,5},{2,6},{3,7},{4,0},{5,1},{6,2},{7,3},{8,12},{9,13},{10,... | collective-permute-start | bytes 393224 | tf_op jit(solution)/shard_map/ppermute | solution.py:22
  94.3 1.2 add_convert_fusion.1
  95.5 2.1 %collective-permute-start.21 = (bf16[128,1024]{1,0:T(8,128)(2,1)S(1)}, bf16[128,1024]{1,0:T(8,128)(2,1)S(1)}, u32[]{:S(2)}, u32[]{:S(2)}) collective-permute-start(bf16[128,1024]{1,0:T(8,128)(2,1)S(1)} %add_convert_fusion.1), channel_id=1, source_target_pairs={{0,8},{8,0},{16,24},{24,16},{1,9},{9,1},{17,25},{25,17},{2,10},{10... | collective-permute-start | bytes 786440 | tf_op jit(solution)/shard_map/ppermute | solution.py:22
  97.6 3.7 %fusion.2 = f32[128,2048]{1,0:T(8,128)S(1)} fusion(bf16[128,1024]{1,0:T(8,128)(2,1)S(1)} %add_convert_fusion.1, bf16[2048,2048]{1,0:T(8,128)(2,1)} %param.11), kind=kOutput, calls=%fused_computation.2 | convolution fusion | flops 536870912 | bytes 5505024 | tf_op jit(solution)/shard_map/dot_general | solution.py:44
  101.5 1.6 collective-permute-start.19
  103.0 3.1 %collective-permute-done.17 = bf16[128,1024]{1,0:T(8,128)(2,1)S(1)} collective-permute-done((bf16[128,1024]{1,0:T(8,128)(2,1)S(1)}, bf16[128,1024]{1,0:T(8,128)(2,1)S(1)}, u32[]{:S(2)}, u32[]{:S(2)}) %collective-permute-start.17) | collective-permute-done | bytes 262176 | tf_op jit(solution)/shard_map/ppermute | solution.py:22
  106.6 2.0 %collective-permute-done.21 = bf16[128,1024]{1,0:T(8,128)(2,1)S(1)} collective-permute-done((bf16[128,1024]{1,0:T(8,128)(2,1)S(1)}, bf16[128,1024]{1,0:T(8,128)(2,1)S(1)}, u32[]{:S(2)}, u32[]{:S(2)}) %collective-permute-start.21) | collective-permute-done | bytes 262176 | tf_op jit(solution)/shard_map/ppermute | solution.py:22
  108.7 3.9 %fusion = f32[128,2048]{1,0:T(8,128)S(1)} fusion(bf16[128,1024]{1,0:T(8,128)(2,1)S(1)} %collective-permute-done.21, bf16[2048,2048]{1,0:T(8,128)(2,1)} %param.11), kind=kOutput, calls=%fused_computation | convolution fusion | flops 536870912 | bytes 5505024 | tf_op jit(solution)/shard_map/dot_general | solution.py:44
  115.0 1.5 fusion.16
  116.6 1.5 broadcast_select_fusion.2
  121.1 2.3 %collective-permute-start.24 = (bf16[256,256]{1,0:T(8,128)(2,1)S(1)}, bf16[256,256]{1,0:T(8,128)(2,1)S(1)}, u32[]{:S(2)}, u32[]{:S(2)}) collective-permute-start(bf16[256,256]{1,0:T(8,128)(2,1)S(1)} %add_convert_fusion.9), channel_id=1, source_target_pairs={{0,16},{8,24},{16,0},{24,8},{1,17},{9,25},{17,1},{25,9},{2,18},{10... | collective-permute-start | bytes 393224 | tf_op jit(solution)/shard_map/ppermute | solution.py:22
  123.4 5.5 %collective-permute-done.26 = bf16[256,256]{1,0:T(8,128)(2,1)S(1)} collective-permute-done((bf16[256,256]{1,0:T(8,128)(2,1)S(1)}, bf16[256,256]{1,0:T(8,128)(2,1)S(1)}, u32[]{:S(2)}, u32[]{:S(2)}) %collective-permute-start.26) | collective-permute-done | bytes 131104 | tf_op jit(solution)/shard_map/ppermute | solution.py:22
  130.8 1.8 %fusion.41 = f32[128,2048]{1,0:T(8,128)S(1)} fusion(f32[128,2048]{1,0:T(8,128)} %collective-permute-done.25, s32[]{:T(128)S(6)} %select_n.187, f32[128,2048]{1,0:T(8,128)} %copy-done.15, f32[128,2048]{1,0:T(8,128)} %copy-done.14), kind=kLoop, calls=%fused_computation.29 | loop fusion | flops 524288 | bytes 4194308 | tf_op jit(solution)/shard_map/add | solution.py:552
  132.7 1.6 collective-permute-start.28
  135.1 2.7 %collective-permute-done.28 = bf16[32,2048]{1,0:T(8,128)(2,1)S(1)} collective-permute-done((bf16[32,2048]{1,0:T(8,128)(2,1)S(1)}, bf16[32,2048]{1,0:T(8,128)(2,1)S(1)}, u32[]{:S(2)}, u32[]{:S(2)}) %collective-permute-start.28) | collective-permute-done | bytes 131104 | tf_op jit(solution)/shard_map/ppermute | solution.py:22
  140.3 2.6 %collective-permute-done.30 = bf16[32,2048]{1,0:T(8,128)(2,1)S(1)} collective-permute-done((bf16[32,2048]{1,0:T(8,128)(2,1)S(1)}, bf16[32,2048]{1,0:T(8,128)(2,1)S(1)}, u32[]{:S(2)}, u32[]{:S(2)}) %collective-permute-start.30) | collective-permute-done | bytes 131104 | tf_op jit(solution)/shard_map/ppermute | solution.py:22
  142.9 1.6 collective-permute-start.32
  146.5 2.7 %collective-permute-start.31 = (bf16[256,256]{1,0:T(8,128)(2,1)S(1)}, bf16[256,256]{1,0:T(8,128)(2,1)S(1)}, u32[]{:S(2)}, u32[]{:S(2)}) collective-permute-start(bf16[256,256]{1,0:T(8,128)(2,1)S(1)} %add_convert_fusion.3), channel_id=1, source_target_pairs={{0,8},{8,0},{16,24},{24,16},{1,9},{9,1},{17,25},{25,17},{2,10},{10... | collective-permute-start | bytes 393224 | tf_op jit(solution)/shard_map/ppermute | solution.py:22
  149.3 1.3 collective-permute-done.34
  150.8 1.3 collective-permute-done.31
  152.1 2.1 %collective-permute-done.35 = bf16[256,256]{1,0:T(8,128)(2,1)S(1)} collective-permute-done((bf16[256,256]{1,0:T(8,128)(2,1)S(1)}, bf16[256,256]{1,0:T(8,128)(2,1)S(1)}, u32[]{:S(2)}, u32[]{:S(2)}) %collective-permute-start.35) | collective-permute-done | bytes 131104 | tf_op jit(solution)/shard_map/ppermute | solution.py:22
  155.6 1.6 maximum_convert_fusion
  (160 shorter events, 28.3 us)
Async XLA Ops:
  0.6 15.4 %copy-start = (bf16[1024,1024]{1,0:T(8,128)(2,1)S(1)}, bf16[1024,1024]{1,0:T(8,128)(2,1)}, u32[]{:S(2)}) copy-start(bf16[1024,1024]{1,0:T(8,128)(2,1)} %param.6) | copy-start | bytes 6291460
  0.6 9.1 %copy-start.24 = (bf16[256,2048]{1,0:T(8,128)(2,1)S(1)}, bf16[256,2048]{1,0:T(8,128)(2,1)}, u32[]{:S(2)}) copy-start(bf16[256,2048]{1,0:T(8,128)(2,1)} %param.10) | copy-start | bytes 3145732
  4.6 11.4 %copy-start.26 = (bf16[1024,256]{1,0:T(8,128)(2,1)S(1)}, bf16[1024,256]{1,0:T(8,128)(2,1)}, u32[]{:S(2)}) copy-start(bf16[1024,256]{1,0:T(8,128)(2,1)} %param.9) | copy-start | bytes 1572868
  4.6 12.9 %collective-permute-start.1 = (f16[128,1024]{1,0:T(8,128)(2,1)}, f16[128,1024]{1,0:T(8,128)(2,1)S(1)}, u32[]{:S(2)}, u32[]{:S(2)}) collective-permute-start(f16[128,1024]{1,0:T(8,128)(2,1)} %fusion.34), channel_id=1, source_target_pairs={{0,8},{8,0},{16,24},{24,16},{1,9},{9,1},{17,25},{25,17},{2,10},{10... | collective-permute-start | bytes 786440 | tf_op jit(solution)/shard_map/ppermute | solution.py:22
  8.5 9.0 %collective-permute-start.2 = (f32[8,2048]{1,0:T(8,128)S(1)}, f32[8,2048]{1,0:T(8,128)S(1)}, u32[]{:S(2)}, u32[]{:S(2)}) collective-permute-start(f32[8,2048]{1,0:T(8,128)S(1)} %slice.28), channel_id=1, source_target_pairs={{8,0},{16,8},{24,16},{9,1},{17,9},{25,17},{10,2},{18,10},{26,18},{... | collective-permute-start | bytes 196616 | tf_op jit(solution)/shard_map/ppermute | solution.py:454
  13.4 12.7 %collective-permute-start.4 = (f16[128,1024]{1,0:T(8,128)(2,1)}, f16[128,1024]{1,0:T(8,128)(2,1)}, u32[]{:S(2)}, u32[]{:S(2)}) collective-permute-start(f16[128,1024]{1,0:T(8,128)(2,1)} %fusion.37), channel_id=1, source_target_pairs={{0,8},{8,0},{16,24},{24,16},{1,9},{9,1},{17,25},{25,17},{2,10},{10... | collective-permute-start | bytes 786440 | tf_op jit(solution)/shard_map/ppermute | solution.py:22
  17.5 6.0 %collective-permute-start = (f16[512,256]{1,0:T(8,128)(2,1)}, f16[512,256]{1,0:T(8,128)(2,1)}, u32[]{:S(2)}, u32[]{:S(2)}) collective-permute-start(f16[512,256]{1,0:T(8,128)(2,1)} %dynamic-slice_convert_fusion), channel_id=1, source_target_pairs={{0,1},{1,0},{2,3},{3,2},{4,5},{5,4},{6,7},{7,6},{8,9},{9,8},{10,11... | collective-permute-start | bytes 786440 | tf_op jit(solution)/shard_map/ppermute | solution.py:22
  17.5 14.4 %slice-start = ((s8[8388608]{0:T(1024)(128)(4,1)}), s8[4194304]{0:T(1024)(128)(4,1)S(1)}, s32[]{:S(2)}) async-start(s8[8388608]{0:T(1024)(128)(4,1)} %bitcast.8), calls=%async_computation | async-start | bytes 8388608
  20.8 11.1 %slice-start.1 = ((s8[8388608]{0:T(1024)(128)(4,1)}), s8[4194304]{0:T(1024)(128)(4,1)S(1)}, s32[]{:S(2)}) async-start(s8[8388608]{0:T(1024)(128)(4,1)} %bitcast.8), calls=%async_computation.1 | async-start | bytes 8388608
  20.9 20.4 %collective-permute-start.6 = (f16[128,1024]{1,0:T(8,128)(2,1)S(1)}, f16[128,1024]{1,0:T(8,128)(2,1)S(1)}, u32[]{:S(2)}, u32[]{:S(2)}) collective-permute-start(f16[128,1024]{1,0:T(8,128)(2,1)S(1)} %get-tuple-element.108), channel_id=1, source_target_pairs={{0,16},{8,24},{16,0},{24,8},{1,17},{9,25},{17,1},{25,9},{2,18},{10... | collective-permute-start | bytes 786440 | tf_op jit(solution)/shard_map/ppermute | solution.py:22
  24.5 17.0 %copy-start.16 = (f32[512,256]{1,0:T(8,128)}, f32[512,256]{1,0:T(8,128)S(1)}, u32[]{:S(2)}) copy-start(f32[512,256]{1,0:T(8,128)S(1)} %convert_add_fusion.3) | copy-start | bytes 1572868
  24.6 5.7 %collective-permute-start.3 = (f16[256,256]{1,0:T(8,128)(2,1)S(1)}, f16[256,256]{1,0:T(8,128)(2,1)S(1)}, u32[]{:S(2)}, u32[]{:S(2)}) collective-permute-start(f16[256,256]{1,0:T(8,128)(2,1)S(1)} %dynamic-slice_convert_fusion.6), channel_id=1, source_target_pairs={{0,2},{1,3},{2,0},{3,1},{4,6},{5,7},{6,4},{7,5},{8,10},{9,11},{10,... | collective-permute-start | bytes 393224 | tf_op jit(solution)/shard_map/ppermute | solution.py:22
  29.1 17.8 %collective-permute-start.8 = (f16[128,1024]{1,0:T(8,128)(2,1)S(1)}, f16[128,1024]{1,0:T(8,128)(2,1)S(1)}, u32[]{:S(2)}, u32[]{:S(2)}) collective-permute-start(f16[128,1024]{1,0:T(8,128)(2,1)S(1)} %get-tuple-element.112), channel_id=1, source_target_pairs={{0,16},{8,24},{16,0},{24,8},{1,17},{9,25},{17,1},{25,9},{2,18},{10... | collective-permute-start | bytes 786440 | tf_op jit(solution)/shard_map/ppermute | solution.py:22
  30.3 10.9 %copy-start.23 = (f16[128,1024]{1,0:T(8,128)(2,1)S(1)}, f16[128,1024]{1,0:T(8,128)(2,1)}, u32[]{:S(2)}) copy-start(f16[128,1024]{1,0:T(8,128)(2,1)} %copy-done.22) | copy-start | bytes 786436
  30.3 11.3 %collective-permute-start.5 = (f16[256,256]{1,0:T(8,128)(2,1)S(1)}, f16[256,256]{1,0:T(8,128)(2,1)S(1)}, u32[]{:S(2)}, u32[]{:S(2)}) collective-permute-start(f16[256,256]{1,0:T(8,128)(2,1)S(1)} %fusion.52), channel_id=1, source_target_pairs={{0,4},{1,5},{2,6},{3,7},{4,0},{5,1},{6,2},{7,3},{8,12},{9,13},{10,... | collective-permute-start | bytes 393224 | tf_op jit(solution)/shard_map/ppermute | solution.py:22
  41.4 11.1 %collective-permute-start.10 = (bf16[128,1024]{1,0:T(8,128)(2,1)S(1)}, bf16[128,1024]{1,0:T(8,128)(2,1)S(1)}, u32[]{:S(2)}, u32[]{:S(2)}) collective-permute-start(bf16[128,1024]{1,0:T(8,128)(2,1)S(1)} %multiply_convert_fusion.1.own_ref), channel_id=1, source_target_pairs={{0,8},{8,0},{16,24},{24,16},{1,9},{9,1},{17,25},{25,17},{2,10},{10... | collective-permute-start | bytes 786440 | tf_op jit(solution)/shard_map/ppermute | solution.py:22
  41.6 10.9 %copy-start.20 = (f16[256,256]{1,0:T(8,128)(2,1)}, f16[256,256]{1,0:T(8,128)(2,1)S(1)}, u32[]{:S(2)}) copy-start(f16[256,256]{1,0:T(8,128)(2,1)S(1)} %collective-permute-done.5) | copy-start | bytes 393220
  41.7 7.0 %collective-permute-start.7 = (bf16[256,256]{1,0:T(8,128)(2,1)S(1)}, bf16[256,256]{1,0:T(8,128)(2,1)S(1)}, u32[]{:S(2)}, u32[]{:S(2)}) collective-permute-start(bf16[256,256]{1,0:T(8,128)(2,1)S(1)} %multiply_convert_fusion.3), channel_id=1, source_target_pairs={{0,2},{1,3},{2,0},{3,1},{4,6},{5,7},{6,4},{7,5},{8,10},{9,11},{10,... | collective-permute-start | bytes 393224 | tf_op jit(solution)/shard_map/ppermute | solution.py:22
  48.8 3.7 %collective-permute-start.9 = (bf16[512,256]{1,0:T(8,128)(2,1)S(1)}, bf16[512,256]{1,0:T(8,128)(2,1)}, u32[]{:S(2)}, u32[]{:S(2)}) collective-permute-start(bf16[512,256]{1,0:T(8,128)(2,1)S(1)} %pad_maximum_fusion.3), channel_id=1, source_target_pairs={{0,1},{1,0},{2,3},{3,2},{4,5},{5,4},{6,7},{7,6},{8,9},{9,8},{10,11... | collective-permute-start | bytes 786440 | tf_op jit(solution)/shard_map/ppermute | solution.py:22
  49.6 11.1 %collective-permute-start.11 = (bf16[128,1024]{1,0:T(8,128)(2,1)}, bf16[128,1024]{1,0:T(8,128)(2,1)}, u32[]{:S(2)}, u32[]{:S(2)}) collective-permute-start(bf16[128,1024]{1,0:T(8,128)(2,1)} %multiply_convert_fusion.own_ref), channel_id=1, source_target_pairs={{0,8},{8,0},{16,24},{24,16},{1,9},{9,1},{17,25},{25,17},{2,10},{10... | collective-permute-start | bytes 786440 | tf_op jit(solution)/shard_map/ppermute | solution.py:22
  69.0 8.3 %collective-permute-start.12 = (bf16[128,1024]{1,0:T(8,128)(2,1)S(1)}, bf16[128,1024]{1,0:T(8,128)(2,1)S(1)}, u32[]{:S(2)}, u32[]{:S(2)}) collective-permute-start(bf16[128,1024]{1,0:T(8,128)(2,1)S(1)} %get-tuple-element.137), channel_id=1, source_target_pairs={{0,8},{8,0},{16,24},{24,16},{1,9},{9,1},{17,25},{25,17},{2,10},{10... | collective-permute-start | bytes 786440 | tf_op jit(solution)/shard_map/ppermute | solution.py:22
  74.0 18.4 %copy-start.4 = (f32[128,1024]{1,0:T(8,128)S(1)}, f32[128,1024]{1,0:T(8,128)}, u32[]{:S(2)}) copy-start(f32[128,1024]{1,0:T(8,128)} %copy-done.3) | copy-start | bytes 1572868
  78.1 3.3 %collective-permute-start.14 = (f32[512,256]{1,0:T(8,128)}, f32[512,256]{1,0:T(8,128)S(1)}, u32[]{:S(2)}, u32[]{:S(2)}) collective-permute-start(f32[512,256]{1,0:T(8,128)} %constant_dynamic-slice_fusion), channel_id=1, source_target_pairs={{0,1},{1,0},{2,3},{3,2},{4,5},{5,4},{6,7},{7,6},{8,9},{9,8},{10,11... | collective-permute-start | bytes 1572872 | tf_op jit(solution)/shard_map/ppermute | solution.py:22
  78.2 14.3 %collective-permute-start.16 = (bf16[128,1024]{1,0:T(8,128)(2,1)}, bf16[128,1024]{1,0:T(8,128)(2,1)S(1)}, u32[]{:S(2)}, u32[]{:S(2)}) collective-permute-start(bf16[128,1024]{1,0:T(8,128)(2,1)} %copy-done.13), channel_id=1, source_target_pairs={{0,8},{8,0},{16,24},{24,16},{1,9},{9,1},{17,25},{25,17},{2,10},{10... | collective-permute-start | bytes 786440 | tf_op jit(solution)/shard_map/ppermute | solution.py:22
  78.5 15.8 %collective-permute-start.13 = (bf16[128,1024]{1,0:T(8,128)(2,1)}, bf16[128,1024]{1,0:T(8,128)(2,1)S(1)}, u32[]{:S(2)}, u32[]{:S(2)}) collective-permute-start(bf16[128,1024]{1,0:T(8,128)(2,1)} %fusion.49), channel_id=1, source_target_pairs={{0,16},{8,24},{16,0},{24,8},{1,17},{9,25},{17,1},{25,9},{2,18},{10... | collective-permute-start | bytes 786440 | tf_op jit(solution)/shard_map/ppermute | solution.py:22
  82.5 10.1 %collective-permute-start.15 = (bf16[256,256]{1,0:T(8,128)(2,1)S(1)}, bf16[256,256]{1,0:T(8,128)(2,1)S(1)}, u32[]{:S(2)}, u32[]{:S(2)}) collective-permute-start(bf16[256,256]{1,0:T(8,128)(2,1)S(1)} %dynamic-slice_convert_fusion.5), channel_id=1, source_target_pairs={{0,2},{1,3},{2,0},{3,1},{4,6},{5,7},{6,4},{7,5},{8,10},{9,11},{10,... | collective-permute-start | bytes 393224 | tf_op jit(solution)/shard_map/ppermute | solution.py:22
  92.6 13.6 %collective-permute-start.17 = (bf16[128,1024]{1,0:T(8,128)(2,1)S(1)}, bf16[128,1024]{1,0:T(8,128)(2,1)S(1)}, u32[]{:S(2)}, u32[]{:S(2)}) collective-permute-start(bf16[128,1024]{1,0:T(8,128)(2,1)S(1)} %fusion.50), channel_id=1, source_target_pairs={{0,16},{8,24},{16,0},{24,8},{1,17},{9,25},{17,1},{25,9},{2,18},{10... | collective-permute-start | bytes 786440 | tf_op jit(solution)/shard_map/ppermute | solution.py:22
  92.7 8.6 %collective-permute-start.18 = (bf16[256,256]{1,0:T(8,128)(2,1)S(1)}, bf16[256,256]{1,0:T(8,128)(2,1)S(1)}, u32[]{:S(2)}, u32[]{:S(2)}) collective-permute-start(bf16[256,256]{1,0:T(8,128)(2,1)S(1)} %fusion.51), channel_id=1, source_target_pairs={{0,4},{1,5},{2,6},{3,7},{4,0},{5,1},{6,2},{7,3},{8,12},{9,13},{10,... | collective-permute-start | bytes 393224 | tf_op jit(solution)/shard_map/ppermute | solution.py:22
  95.5 13.2 %collective-permute-start.21 = (bf16[128,1024]{1,0:T(8,128)(2,1)S(1)}, bf16[128,1024]{1,0:T(8,128)(2,1)S(1)}, u32[]{:S(2)}, u32[]{:S(2)}) collective-permute-start(bf16[128,1024]{1,0:T(8,128)(2,1)S(1)} %add_convert_fusion.1), channel_id=1, source_target_pairs={{0,8},{8,0},{16,24},{24,16},{1,9},{9,1},{17,25},{25,17},{2,10},{10... | collective-permute-start | bytes 786440 | tf_op jit(solution)/shard_map/ppermute | solution.py:22
  101.5 5.0 %collective-permute-start.19 = (bf16[256,256]{1,0:T(8,128)(2,1)S(1)}, bf16[256,256]{1,0:T(8,128)(2,1)S(1)}, u32[]{:S(2)}, u32[]{:S(2)}) collective-permute-start(bf16[256,256]{1,0:T(8,128)(2,1)S(1)} %multiply_convert_fusion.2), channel_id=1, source_target_pairs={{0,2},{1,3},{2,0},{3,1},{4,6},{5,7},{6,4},{7,5},{8,10},{9,11},{10,... | collective-permute-start | bytes 393224 | tf_op jit(solution)/shard_map/ppermute | solution.py:22
  106.3 10.3 %collective-permute-start.22 = (bf16[128,1024]{1,0:T(8,128)(2,1)S(1)}, bf16[128,1024]{1,0:T(8,128)(2,1)S(1)}, u32[]{:S(2)}, u32[]{:S(2)}) collective-permute-start(bf16[128,1024]{1,0:T(8,128)(2,1)S(1)} %add_convert_fusion), channel_id=1, source_target_pairs={{0,8},{8,0},{16,24},{24,16},{1,9},{9,1},{17,25},{25,17},{2,10},{10... | collective-permute-start | bytes 786440 | tf_op jit(solution)/shard_map/ppermute | solution.py:22
  106.6 6.0 %collective-permute-start.20 = (bf16[512,256]{1,0:T(8,128)(2,1)S(1)}, bf16[512,256]{1,0:T(8,128)(2,1)S(1)}, u32[]{:S(2)}, u32[]{:S(2)}) collective-permute-start(bf16[512,256]{1,0:T(8,128)(2,1)S(1)} %pad_maximum_fusion.4), channel_id=1, source_target_pairs={{0,1},{1,0},{2,3},{3,2},{4,5},{5,4},{6,7},{7,6},{8,9},{9,8},{10,11... | collective-permute-start | bytes 786440 | tf_op jit(solution)/shard_map/ppermute | solution.py:22
  113.5 6.7 %collective-permute-start.23 = (bf16[256,256]{1,0:T(8,128)(2,1)S(1)}, bf16[256,256]{1,0:T(8,128)(2,1)S(1)}, u32[]{:S(2)}, u32[]{:S(2)}) collective-permute-start(bf16[256,256]{1,0:T(8,128)(2,1)S(1)} %get-tuple-element.169), channel_id=1, source_target_pairs={{0,8},{8,0},{16,24},{24,16},{1,9},{9,1},{17,25},{25,17},{2,10},{10... | collective-permute-start | bytes 393224 | tf_op jit(solution)/shard_map/ppermute | solution.py:22
  118.1 11.8 %copy-start.8 = (f32[1024,1]{1,0:T(8,128)S(1)}, f32[1024,1]{1,0:T(8,128)}, u32[]{:S(2)}) copy-start(f32[1024,1]{1,0:T(8,128)} %copy-done.7) | copy-start | bytes 12292
  118.2 11.8 %copy-start.10 = (f32[1024,1]{1,0:T(8,128)S(1)}, f32[1024,1]{1,0:T(8,128)}, u32[]{:S(2)}) copy-start(f32[1024,1]{1,0:T(8,128)} %copy-done.9) | copy-start | bytes 12292
  120.3 10.4 %collective-permute-start.25 = (f32[128,2048]{1,0:T(8,128)}, f32[128,2048]{1,0:T(8,128)}, u32[]{:S(2)}, u32[]{:S(2)}) collective-permute-start(f32[128,2048]{1,0:T(8,128)} %fusion.42), channel_id=1, source_target_pairs={{0,1},{1,0},{2,3},{3,2},{4,5},{5,4},{6,7},{7,6},{8,9},{9,8},{10,11... | collective-permute-start | bytes 3145736 | tf_op jit(solution)/shard_map/ppermute | solution.py:22
  120.4 8.5 %collective-permute-start.26 = (bf16[256,256]{1,0:T(8,128)(2,1)S(1)}, bf16[256,256]{1,0:T(8,128)(2,1)S(1)}, u32[]{:S(2)}, u32[]{:S(2)}) collective-permute-start(bf16[256,256]{1,0:T(8,128)(2,1)S(1)} %get-tuple-element.170), channel_id=1, source_target_pairs={{0,8},{8,0},{16,24},{24,16},{1,9},{9,1},{17,25},{25,17},{2,10},{10... | collective-permute-start | bytes 393224 | tf_op jit(solution)/shard_map/ppermute | solution.py:22
  121.1 25.3 %collective-permute-start.24 = (bf16[256,256]{1,0:T(8,128)(2,1)S(1)}, bf16[256,256]{1,0:T(8,128)(2,1)S(1)}, u32[]{:S(2)}, u32[]{:S(2)}) collective-permute-start(bf16[256,256]{1,0:T(8,128)(2,1)S(1)} %add_convert_fusion.9), channel_id=1, source_target_pairs={{0,16},{8,24},{16,0},{24,8},{1,17},{9,25},{17,1},{25,9},{2,18},{10... | collective-permute-start | bytes 393224 | tf_op jit(solution)/shard_map/ppermute | solution.py:22
  129.9 19.3 %collective-permute-start.33 = (bf16[256,256]{1,0:T(8,128)(2,1)S(1)}, bf16[256,256]{1,0:T(8,128)(2,1)S(1)}, u32[]{:S(2)}, u32[]{:S(2)}) collective-permute-start(bf16[256,256]{1,0:T(8,128)(2,1)S(1)} %add_convert_fusion.8), channel_id=1, source_target_pairs={{0,16},{8,24},{16,0},{24,8},{1,17},{9,25},{17,1},{25,9},{2,18},{10... | collective-permute-start | bytes 393224 | tf_op jit(solution)/shard_map/ppermute | solution.py:22
  132.7 5.1 %collective-permute-start.28 = (bf16[32,2048]{1,0:T(8,128)(2,1)S(1)}, bf16[32,2048]{1,0:T(8,128)(2,1)S(1)}, u32[]{:S(2)}, u32[]{:S(2)}) collective-permute-start(bf16[32,2048]{1,0:T(8,128)(2,1)S(1)} %dynamic-slice_convert_fusion.1), channel_id=1, source_target_pairs={{0,2},{1,3},{2,0},{3,1},{4,6},{5,7},{6,4},{7,5},{8,10},{9,11},{10,... | collective-permute-start | bytes 393224 | tf_op jit(solution)/shard_map/ppermute | solution.py:22
  134.3 5.0 %collective-permute-start.27 = (bf16[32,2048]{1,0:T(8,128)(2,1)S(1)}, bf16[32,2048]{1,0:T(8,128)(2,1)S(1)}, u32[]{:S(2)}, u32[]{:S(2)}) collective-permute-start(bf16[32,2048]{1,0:T(8,128)(2,1)S(1)} %dynamic-slice_convert_fusion.2), channel_id=1, source_target_pairs={{0,4},{1,5},{2,6},{3,7},{4,0},{5,1},{6,2},{7,3},{8,12},{9,13},{10,... | collective-permute-start | bytes 393224 | tf_op jit(solution)/shard_map/ppermute | solution.py:22
  137.9 5.0 %collective-permute-start.30 = (bf16[32,2048]{1,0:T(8,128)(2,1)S(1)}, bf16[32,2048]{1,0:T(8,128)(2,1)S(1)}, u32[]{:S(2)}, u32[]{:S(2)}) collective-permute-start(bf16[32,2048]{1,0:T(8,128)(2,1)S(1)} %add_convert_fusion.7), channel_id=1, source_target_pairs={{0,4},{1,5},{2,6},{3,7},{4,0},{5,1},{6,2},{7,3},{8,12},{9,13},{10,... | collective-permute-start | bytes 393224 | tf_op jit(solution)/shard_map/ppermute | solution.py:22
  139.4 6.2 %collective-permute-start.29 = (bf16[32,2048]{1,0:T(8,128)(2,1)S(1)}, bf16[32,2048]{1,0:T(8,128)(2,1)S(1)}, u32[]{:S(2)}, u32[]{:S(2)}) collective-permute-start(bf16[32,2048]{1,0:T(8,128)(2,1)S(1)} %add_convert_fusion.6), channel_id=1, source_target_pairs={{0,2},{1,3},{2,0},{3,1},{4,6},{5,7},{6,4},{7,5},{8,10},{9,11},{10,... | collective-permute-start | bytes 393224 | tf_op jit(solution)/shard_map/ppermute | solution.py:22
  142.9 6.3 %collective-permute-start.32 = (bf16[32,2048]{1,0:T(8,128)(2,1)S(1)}, bf16[32,2048]{1,0:T(8,128)(2,1)S(1)}, u32[]{:S(2)}, u32[]{:S(2)}) collective-permute-start(bf16[32,2048]{1,0:T(8,128)(2,1)S(1)} %add_convert_fusion.5), channel_id=1, source_target_pairs={{0,2},{1,3},{2,0},{3,1},{4,6},{5,7},{6,4},{7,5},{8,10},{9,11},{10,... | collective-permute-start | bytes 393224 | tf_op jit(solution)/shard_map/ppermute | solution.py:22
  145.6 5.0 %collective-permute-start.34 = (bf16[32,2048]{1,0:T(8,128)(2,1)S(1)}, bf16[32,2048]{1,0:T(8,128)(2,1)S(1)}, u32[]{:S(2)}, u32[]{:S(2)}) collective-permute-start(bf16[32,2048]{1,0:T(8,128)(2,1)S(1)} %add_convert_fusion.4), channel_id=1, source_target_pairs={{0,4},{1,5},{2,6},{3,7},{4,0},{5,1},{6,2},{7,3},{8,12},{9,13},{10,... | collective-permute-start | bytes 393224 | tf_op jit(solution)/shard_map/ppermute | solution.py:22
  146.5 5.6 %collective-permute-start.31 = (bf16[256,256]{1,0:T(8,128)(2,1)S(1)}, bf16[256,256]{1,0:T(8,128)(2,1)S(1)}, u32[]{:S(2)}, u32[]{:S(2)}) collective-permute-start(bf16[256,256]{1,0:T(8,128)(2,1)S(1)} %add_convert_fusion.3), channel_id=1, source_target_pairs={{0,8},{8,0},{16,24},{24,16},{1,9},{9,1},{17,25},{25,17},{2,10},{10... | collective-permute-start | bytes 393224 | tf_op jit(solution)/shard_map/ppermute | solution.py:22
  149.2 5.0 %collective-permute-start.35 = (bf16[256,256]{1,0:T(8,128)(2,1)S(1)}, bf16[256,256]{1,0:T(8,128)(2,1)S(1)}, u32[]{:S(2)}, u32[]{:S(2)}) collective-permute-start(bf16[256,256]{1,0:T(8,128)(2,1)S(1)} %add_convert_fusion.2), channel_id=1, source_target_pairs={{0,8},{8,0},{16,24},{24,16},{1,9},{9,1},{17,25},{25,17},{2,10},{10... | collective-permute-start | bytes 393224 | tf_op jit(solution)/shard_map/ppermute | solution.py:22
  150.7 4.7 %collective-permute-start.36 = (bf16[128,2048]{1,0:T(8,128)(2,1)S(1)}, bf16[128,2048]{1,0:T(8,128)(2,1)S(1)}, u32[]{:S(2)}, u32[]{:S(2)}) collective-permute-start(bf16[128,2048]{1,0:T(8,128)(2,1)S(1)} %pad_maximum_fusion.2), channel_id=1, source_target_pairs={{0,1},{1,0},{2,3},{3,2},{4,5},{5,4},{6,7},{7,6},{8,9},{9,8},{10,11... | collective-permute-start | bytes 1572872 | tf_op jit(solution)/shard_map/ppermute | solution.py:22
  (22 other events, 87.5 us)

commit v14 on v10

--- a/solution.py
+++ b/solution.py
@@ -10,7 +10,7 @@
 CHUNKS = 2
 BLOCK = 256
 VOCAB_SCALE = 128.0
-PRE_SCALE = 64.0
+PRE_SCALE = 32.0
 F32 = jnp.float32
 BF16 = jnp.bfloat16
 F16 = jnp.float16

time: 148 us -> 148 us (level)
  no operation moved by 1% of the time
where the time goes in v14:
time: 148 us; the launch traced here: 147 us
  starting transfers between devices  41.9 us (28%)
  waiting for transfers between devices  33.8 us (23%)
  matrix products  25.9 us (18%)
  Pallas kernels  18.9 us (13%)
  local copies, waits for them, and re-layouts  13.5 us (9%)
  other arithmetic  12 us (8%)
    ppermute x38, starting transfers between devices, swap(): return lax.ppermute(value, axis, pairs)  40.6 us
    ppermute x38, waiting for transfers between devices, swap(): return lax.ppermute(value, axis, pairs)  33.8 us
    dot_general x4, matrix products, on_device(): jnp.dot(part, columns(c), preferred_element_type=F32) * VOCAB_SCALE  13.8 us
    unnamed x57, local copies, waits for them, and re-layouts  10.8 us
    dot_general x4, matrix products, inner_cols(): lax.dot_general(left, right, (((1,), (1,)), ((), ())), preferred_element_...  10.6 us
    pallas_call x2, Pallas kernels, grad_chunk(): pl.pallas_call(body, grid=(rows // block,), in_specs=[row_spec(block, wid...  8.28 us
    pallas_call x2, Pallas kernels, draft_chunk(): pl.pallas_call(body, grid=(rows // block,), in_specs=[row_spec(block, wid...  6.57 us
    pallas_call x1, Pallas kernels, target_pass(): pl.pallas_call(body, grid=(rows // block,), in_specs=[row_spec(block, col...  4.01 us
  transfers between devices with their start and end apart: 39, of which 16 were waited for; matrix products, arithmetic and copies ran while one was open for 24% of the time, Pallas kernels for 7%

profile of v14, /device:TPU:0, one launch (start us, length us, event | category | flops | bytes accessed | tf_op | source)
XLA Modules:
  0.0 147.4 jit_solution(15562161272968499505)
XLA Ops:
  0.7 3.9 %fusion.34 = f16[128,1024]{1,0:T(8,128)(2,1)} fusion(bf16[2048,2048]{1,0:T(8,128)(2,1)} %param.11, bf16[256,2048]{1,0:T(8,128)(2,1)} %param.10, s32[]{:T(128)S(6)} %select_n.175), kind=kOutput, calls=%fused_computation.22 | convolution fusion | flops 537133056 | bytes 4980740 | tf_op jit(solution)/shard_map/dot_general | solution.py:441
  4.6 3.0 %collective-permute-start.1 = (f16[128,1024]{1,0:T(8,128)(2,1)}, f16[128,1024]{1,0:T(8,128)(2,1)}, u32[]{:S(2)}, u32[]{:S(2)}) collective-permute-start(f16[128,1024]{1,0:T(8,128)(2,1)} %fusion.34), channel_id=1, source_target_pairs={{0,8},{8,0},{16,24},{24,16},{1,9},{9,1},{17,25},{25,17},{2,10},{10... | collective-permute-start | bytes 786440 | tf_op jit(solution)/shard_map/ppermute | solution.py:22
  8.5 1.3 collective-permute-start.2
  9.8 3.6 %fusion.37 = f16[128,1024]{1,0:T(8,128)(2,1)} fusion(bf16[2048,2048]{1,0:T(8,128)(2,1)} %param.11, bf16[256,2048]{1,0:T(8,128)(2,1)S(1)} %copy-done.19, s32[]{:T(128)S(6)} %select_n.175), kind=kOutput, calls=%fused_computation.23 | convolution fusion | flops 537133056 | bytes 4980740 | tf_op jit(solution)/shard_map/dot_general | solution.py:441
  13.4 2.6 %collective-permute-start.4 = (f16[128,1024]{1,0:T(8,128)(2,1)}, f16[128,1024]{1,0:T(8,128)(2,1)}, u32[]{:S(2)}, u32[]{:S(2)}) collective-permute-start(f16[128,1024]{1,0:T(8,128)(2,1)} %fusion.37), channel_id=1, source_target_pairs={{0,8},{8,0},{16,24},{24,16},{1,9},{9,1},{17,25},{25,17},{2,10},{10... | collective-permute-start | bytes 786440 | tf_op jit(solution)/shard_map/ppermute | solution.py:22
  17.5 3.3 %fusion.44 = (f16[128,1024]{1,0:T(8,128)(2,1)S(1)}, f32[128,1024]{1,0:T(8,128)S(1)}) fusion(f16[128,1024]{1,0:T(8,128)(2,1)} %collective-permute-done.1, bf16[2048,2048]{1,0:T(8,128)(2,1)} %param.11, bf16[256,2048]{1,0:T(8,128)(2,1)} %param.10, s32[]{:T(128)S(6)} %select_n.178), kind=kOutput, calls=%fused_computation.49 | convolution fusion | flops 537395200 | bytes 5767172 | tf_op jit(solution)/shard_map/dot_general | solution.py:441
  20.9 2.7 %collective-permute-start.6 = (f16[128,1024]{1,0:T(8,128)(2,1)S(1)}, f16[128,1024]{1,0:T(8,128)(2,1)S(1)}, u32[]{:S(2)}, u32[]{:S(2)}) collective-permute-start(f16[128,1024]{1,0:T(8,128)(2,1)S(1)} %get-tuple-element.112), channel_id=1, source_target_pairs={{0,16},{8,24},{16,0},{24,8},{1,17},{9,25},{17,1},{25,9},{2,18},{10... | collective-permute-start | bytes 786440 | tf_op jit(solution)/shard_map/ppermute | solution.py:22
  24.6 1.6 %collective-permute-start.3 = (f16[256,256]{1,0:T(8,128)(2,1)S(1)}, f16[256,256]{1,0:T(8,128)(2,1)S(1)}, u32[]{:S(2)}, u32[]{:S(2)}) collective-permute-start(f16[256,256]{1,0:T(8,128)(2,1)S(1)} %dynamic-slice_convert_fusion.6), channel_id=1, source_target_pairs={{0,2},{1,3},{2,0},{3,1},{4,6},{5,7},{6,4},{7,5},{8,10},{9,11},{10,... | collective-permute-start | bytes 393224 | tf_op jit(solution)/shard_map/ppermute | solution.py:22
  26.1 3.0 %fusion.45 = (f16[128,1024]{1,0:T(8,128)(2,1)S(1)}, f32[128,1024]{1,0:T(8,128)S(1)}) fusion(f16[128,1024]{1,0:T(8,128)(2,1)} %collective-permute-done.4, bf16[2048,2048]{1,0:T(8,128)(2,1)} %param.11, bf16[256,2048]{1,0:T(8,128)(2,1)S(1)} %copy-done.20, s32[]{:T(128)S(6)} %select_n.178), kind=kOutput, calls=%fused_computation.50 | convolution fusion | flops 537395200 | bytes 5767172 | tf_op jit(solution)/shard_map/dot_general | solution.py:441
  30.3 1.6 %collective-permute-start.5 = (f16[256,256]{1,0:T(8,128)(2,1)S(1)}, f16[256,256]{1,0:T(8,128)(2,1)S(1)}, u32[]{:S(2)}, u32[]{:S(2)}) collective-permute-start(f16[256,256]{1,0:T(8,128)(2,1)S(1)} %fusion.49), channel_id=1, source_target_pairs={{0,4},{1,5},{2,6},{3,7},{4,0},{5,1},{6,2},{7,3},{8,12},{9,13},{10,... | collective-permute-start | bytes 393224 | tf_op jit(solution)/shard_map/ppermute | solution.py:22
  31.9 4.0 %target_pass.1 = (f32[1024,2048]{1,0:T(8,128)S(1)}, f32[1024,1]{1,0:T(8,128)S(1)}) custom-call(f32[1024,2048]{1,0:T(8,128)S(1)} %bitcast.9, f32[1024,2048]{1,0:T(8,128)S(1)} %bitcast.9, f32[8,2048]{1,0:T(8,128)S(1)} %collective-permute-done.2.incoming_ref), custom_call_target="tpu_custom_call" | custom-call | flops 3072 | bytes 4096 | tf_op jit(solution)/shard_map/target_pass/pallas_call | solution.py:132
  35.9 3.3 %copy-done.2 = f32[1024,2048]{1,0:T(8,128)} copy-done((f32[1024,2048]{1,0:T(8,128)}, f32[1024,2048]{1,0:T(8,128)S(1)}, u32[]{:S(2)}) %copy-start.2) | copy-done | bytes 8388632
  40.1 1.2 collective-permute-done.6
  42.6 1.6 %collective-permute-start.7 = (bf16[256,256]{1,0:T(8,128)(2,1)S(1)}, bf16[256,256]{1,0:T(8,128)(2,1)S(1)}, u32[]{:S(2)}, u32[]{:S(2)}) collective-permute-start(bf16[256,256]{1,0:T(8,128)(2,1)S(1)} %multiply_convert_fusion.3), channel_id=1, source_target_pairs={{0,2},{1,3},{2,0},{3,1},{4,6},{5,7},{6,4},{7,5},{8,10},{9,11},{10,... | collective-permute-start | bytes 393224 | tf_op jit(solution)/shard_map/ppermute | solution.py:22
  44.2 2.7 %collective-permute-done.8 = f16[128,1024]{1,0:T(8,128)(2,1)S(1)} collective-permute-done((f16[128,1024]{1,0:T(8,128)(2,1)S(1)}, f16[128,1024]{1,0:T(8,128)(2,1)S(1)}, u32[]{:S(2)}, u32[]{:S(2)}) %collective-permute-start.8) | collective-permute-done | bytes 262176 | tf_op jit(solution)/shard_map/ppermute | solution.py:22
  46.9 1.8 %multiply_convert_fusion.own_ref = bf16[128,1024]{1,0:T(8,128)(2,1)} fusion(f16[128,1024]{1,0:T(8,128)(2,1)S(1)} %collective-permute-done.8, f32[128,1024]{1,0:T(8,128)S(1)} %get-tuple-element.238, f16[128,1024]{1,0:T(8,128)(2,1)} %collective-permute-done.4), kind=kLoop, calls=%fused_computation.36 | loop fusion | flops 786432 | bytes 1310720 | tf_op jit(solution)/shard_map/convert_element_type | solution.py:448
  50.7 1.8 %collective-permute-done.10.other_ref = bf16[128,1024]{1,0:T(8,128)(2,1)S(1)} collective-permute-done((bf16[128,1024]{1,0:T(8,128)(2,1)S(1)}, bf16[128,1024]{1,0:T(8,128)(2,1)S(1)}, u32[]{:S(2)}, u32[]{:S(2)}) %collective-permute-start.10) | collective-permute-done | bytes 262176 | tf_op jit(solution)/shard_map/ppermute | solution.py:22
  53.4 3.4 %copy-done.1 = f32[1024,2048]{1,0:T(8,128)S(1)} copy-done((f32[1024,2048]{1,0:T(8,128)S(1)}, f32[1024,2048]{1,0:T(8,128)}, u32[]{:S(2)}) %copy-start.1) | copy-done | bytes 8388632
  57.8 2.5 %draft_chunk.2 = (f32[1024,1024]{1,0:T(8,128)S(1)}, bf16[256,1024]{1,0:T(8,128)(2,1)S(1)}, f32[1024,1]{1,0:T(8,128)S(1)}, f32[1024,1]{1,0:T(8,128)S(1)}) custom-call(f32[1024,2048]{1,0:T(8,128)S(1)} %copy-done.1, bf16[1024,256]{1,0:T(8,128)(2,1)S(1)} %pad_maximum_fusion.acts_ref, bf16[128,1024]{1,0:T(8,128)(2,1)S(1)} %multiply_convert_fusion.1.own_ref, ...), custom_call_target="tpu_custom_call" | custom-call | flops 131072 | bytes 2048 | tf_op jit(solution)/shard_map/draft_chunk/pallas_call | solution.py:220
  60.3 4.1 %draft_chunk.3 = (f32[1024,1024]{1,0:T(8,128)S(1)}, bf16[256,1024]{1,0:T(8,128)(2,1)S(1)}, f32[1024,1]{1,0:T(8,128)S(1)}, f32[1024,1]{1,0:T(8,128)S(1)}) custom-call(f32[1024,2048]{1,0:T(8,128)S(1)} %copy-done.1, bf16[1024,256]{1,0:T(8,128)(2,1)S(1)} %pad_maximum_fusion.acts_ref, bf16[128,1024]{1,0:T(8,128)(2,1)} %multiply_convert_fusion.own_ref, ...), custom_call_target="tpu_custom_call" | custom-call | flops 131072 | bytes 2048 | tf_op jit(solution)/shard_map/draft_chunk/pallas_call | solution.py:220
  64.4 4.1 %grad_chunk.2 = (bf16[128,1024]{1,0:T(8,128)(2,1)S(1)}, f32[128,1024]{1,0:T(8,128)S(1)}, f32[1024,256]{1,0:T(8,128)S(1)}, f32[1024,1]{1,0:T(8,128)S(1)}) custom-call(f32[1024,1024]{1,0:T(8,128)S(1)} %get-tuple-element.136.draft_ref, f32[1024,2048]{1,0:T(8,128)S(1)} %bitcast.11, s32[1024,1]{1,0:T(8,128)S(1)} %copy.11.label_ref, ...), custom_call_target="tpu_custom_call" | custom-call | flops 262144 | bytes 2048 | tf_op jit(solution)/shard_map/grad_chunk/pallas_call | solution.py:292
  68.6 4.2 %grad_chunk.3 = (bf16[128,1024]{1,0:T(8,128)(2,1)S(1)}, f32[128,1024]{1,0:T(8,128)S(1)}, f32[1024,256]{1,0:T(8,128)S(1)}, f32[1024,1]{1,0:T(8,128)S(1)}) custom-call(f32[1024,1024]{1,0:T(8,128)S(1)} %get-tuple-element.142.draft_ref, f32[1024,2048]{1,0:T(8,128)S(1)} %bitcast.11, s32[1024,1]{1,0:T(8,128)S(1)} %copy.11.label_ref, ...), custom_call_target="tpu_custom_call" | custom-call | flops 262144 | bytes 2048 | tf_op jit(solution)/shard_map/grad_chunk/pallas_call | solution.py:292
  74.4 2.4 %collective-permute-done.12 = bf16[128,1024]{1,0:T(8,128)(2,1)S(1)} collective-permute-done((bf16[128,1024]{1,0:T(8,128)(2,1)S(1)}, bf16[128,1024]{1,0:T(8,128)(2,1)S(1)}, u32[]{:S(2)}, u32[]{:S(2)}) %collective-permute-start.12) | collective-permute-done | bytes 262176 | tf_op jit(solution)/shard_map/ppermute | solution.py:22
  77.8 2.9 %collective-permute-start.13 = (bf16[128,1024]{1,0:T(8,128)(2,1)S(1)}, bf16[128,1024]{1,0:T(8,128)(2,1)S(1)}, u32[]{:S(2)}, u32[]{:S(2)}) collective-permute-start(bf16[128,1024]{1,0:T(8,128)(2,1)S(1)} %fusion.46), channel_id=1, source_target_pairs={{0,16},{8,24},{16,0},{24,8},{1,17},{9,25},{17,1},{25,9},{2,18},{10... | collective-permute-start | bytes 786440 | tf_op jit(solution)/shard_map/ppermute | solution.py:22
  81.8 1.6 %collective-permute-start.15 = (bf16[256,256]{1,0:T(8,128)(2,1)S(1)}, bf16[256,256]{1,0:T(8,128)(2,1)S(1)}, u32[]{:S(2)}, u32[]{:S(2)}) collective-permute-start(bf16[256,256]{1,0:T(8,128)(2,1)S(1)} %dynamic-slice_convert_fusion.5), channel_id=1, source_target_pairs={{0,2},{1,3},{2,0},{3,1},{4,6},{5,7},{6,4},{7,5},{8,10},{9,11},{10,... | collective-permute-start | bytes 393224 | tf_op jit(solution)/shard_map/ppermute | solution.py:22
  83.4 8.7 %collective-permute-done.16 = bf16[128,1024]{1,0:T(8,128)(2,1)S(1)} collective-permute-done((bf16[128,1024]{1,0:T(8,128)(2,1)}, bf16[128,1024]{1,0:T(8,128)(2,1)S(1)}, u32[]{:S(2)}, u32[]{:S(2)}) %collective-permute-start.16) | collective-permute-done | bytes 262176 | tf_op jit(solution)/shard_map/ppermute | solution.py:22
  92.3 1.6 %collective-permute-start.18 = (bf16[256,256]{1,0:T(8,128)(2,1)S(1)}, bf16[256,256]{1,0:T(8,128)(2,1)S(1)}, u32[]{:S(2)}, u32[]{:S(2)}) collective-permute-start(bf16[256,256]{1,0:T(8,128)(2,1)S(1)} %fusion.48), channel_id=1, source_target_pairs={{0,4},{1,5},{2,6},{3,7},{4,0},{5,1},{6,2},{7,3},{8,12},{9,13},{10,... | collective-permute-start | bytes 393224 | tf_op jit(solution)/shard_map/ppermute | solution.py:22
  93.8 1.2 add_convert_fusion.1
  95.1 2.1 %collective-permute-start.17 = (bf16[128,1024]{1,0:T(8,128)(2,1)S(1)}, bf16[128,1024]{1,0:T(8,128)(2,1)S(1)}, u32[]{:S(2)}, u32[]{:S(2)}) collective-permute-start(bf16[128,1024]{1,0:T(8,128)(2,1)S(1)} %add_convert_fusion.1), channel_id=1, source_target_pairs={{0,8},{8,0},{16,24},{24,16},{1,9},{9,1},{17,25},{25,17},{2,10},{10... | collective-permute-start | bytes 786440 | tf_op jit(solution)/shard_map/ppermute | solution.py:22
  97.1 3.7 %fusion.2 = f32[128,2048]{1,0:T(8,128)S(1)} fusion(bf16[128,1024]{1,0:T(8,128)(2,1)S(1)} %add_convert_fusion.1, bf16[2048,2048]{1,0:T(8,128)(2,1)} %param.11), kind=kOutput, calls=%fused_computation.2 | convolution fusion | flops 536870912 | bytes 5505024 | tf_op jit(solution)/shard_map/dot_general | solution.py:44
  101.1 1.6 %collective-permute-start.19 = (bf16[256,256]{1,0:T(8,128)(2,1)S(1)}, bf16[256,256]{1,0:T(8,128)(2,1)S(1)}, u32[]{:S(2)}, u32[]{:S(2)}) collective-permute-start(bf16[256,256]{1,0:T(8,128)(2,1)S(1)} %multiply_convert_fusion.2), channel_id=1, source_target_pairs={{0,2},{1,3},{2,0},{3,1},{4,6},{5,7},{6,4},{7,5},{8,10},{9,11},{10,... | collective-permute-start | bytes 393224 | tf_op jit(solution)/shard_map/ppermute | solution.py:22
  102.6 3.2 %collective-permute-done.20 = bf16[128,1024]{1,0:T(8,128)(2,1)S(1)} collective-permute-done((bf16[128,1024]{1,0:T(8,128)(2,1)S(1)}, bf16[128,1024]{1,0:T(8,128)(2,1)S(1)}, u32[]{:S(2)}, u32[]{:S(2)}) %collective-permute-start.20) | collective-permute-done | bytes 262176 | tf_op jit(solution)/shard_map/ppermute | solution.py:22
  106.2 2.1 %collective-permute-done.17 = bf16[128,1024]{1,0:T(8,128)(2,1)S(1)} collective-permute-done((bf16[128,1024]{1,0:T(8,128)(2,1)S(1)}, bf16[128,1024]{1,0:T(8,128)(2,1)S(1)}, u32[]{:S(2)}, u32[]{:S(2)}) %collective-permute-start.17) | collective-permute-done | bytes 262176 | tf_op jit(solution)/shard_map/ppermute | solution.py:22
  108.3 3.8 %fusion = f32[128,2048]{1,0:T(8,128)S(1)} fusion(bf16[128,1024]{1,0:T(8,128)(2,1)S(1)} %collective-permute-done.17, bf16[2048,2048]{1,0:T(8,128)(2,1)} %param.11), kind=kOutput, calls=%fused_computation | convolution fusion | flops 536870912 | bytes 5505024 | tf_op jit(solution)/shard_map/dot_general | solution.py:44
  113.3 2.0 %collective-permute-start.27 = (bf16[256,256]{1,0:T(8,128)(2,1)S(1)}, bf16[256,256]{1,0:T(8,128)(2,1)S(1)}, u32[]{:S(2)}, u32[]{:S(2)}) collective-permute-start(bf16[256,256]{1,0:T(8,128)(2,1)S(1)} %dynamic-slice_convert_fusion.4), channel_id=1, source_target_pairs={{0,8},{8,0},{16,24},{24,16},{1,9},{9,1},{17,25},{25,17},{2,10},{10... | collective-permute-start | bytes 393224 | tf_op jit(solution)/shard_map/ppermute | solution.py:22
  115.3 1.5 %fusion.16 = f32[128,2048]{1,0:T(8,128)S(1)} fusion(f32[128,2048]{1,0:T(8,128)S(1)} %fusion.2, bf16[128,1024]{1,0:T(8,128)(2,1)S(1)} %add_convert_fusion, bf16[2048,2048]{1,0:T(8,128)(2,1)S(1)} %bitcast.13), kind=kOutput, calls=%fused_computation.16 | convolution fusion | flops 537133056 | bytes 6553600 | tf_op jit(solution)/shard_map/dot_general | solution.py:44
  116.9 1.5 %broadcast_select_fusion = (f32[128,2048]{1,0:T(8,128)S(1)}, f32[128,2048]{1,0:T(8,128)S(1)}) fusion(f32[128,2048]{1,0:T(8,128)S(1)} %fusion.16, pred[]{:T(512)S(6)} %eq.12, f32[128,2048]{1,0:T(8,128)S(1)} %fusion, bf16[128,1024]{1,0:T(8,128)(2,1)S(1)} %collective-permute-done.21, bf16[2048,2048]{1,0:T(8,128)(2,1)S(1)} %bitcast.13), kind=kOutput, calls=%fused_computation.43 | convolution fusion | flops 537657344 | bytes 8650753 | tf_op jit(solution)/shard_map/dot_general | solution.py:44
  121.1 2.0 %collective-permute-start.35 = (bf16[256,256]{1,0:T(8,128)(2,1)S(1)}, bf16[256,256]{1,0:T(8,128)(2,1)S(1)}, u32[]{:S(2)}, u32[]{:S(2)}) collective-permute-start(bf16[256,256]{1,0:T(8,128)(2,1)S(1)} %add_convert_fusion.8), channel_id=1, source_target_pairs={{0,16},{8,24},{16,0},{24,8},{1,17},{9,25},{17,1},{25,9},{2,18},{10... | collective-permute-start | bytes 393224 | tf_op jit(solution)/shard_map/ppermute | solution.py:22
  123.2 1.6 %collective-permute-start.29 = (bf16[32,2048]{1,0:T(8,128)(2,1)S(1)}, bf16[32,2048]{1,0:T(8,128)(2,1)S(1)}, u32[]{:S(2)}, u32[]{:S(2)}) collective-permute-start(bf16[32,2048]{1,0:T(8,128)(2,1)S(1)} %dynamic-slice_convert_fusion.2), channel_id=1, source_target_pairs={{0,2},{1,3},{2,0},{3,1},{4,6},{5,7},{6,4},{7,5},{8,10},{9,11},{10,... | collective-permute-start | bytes 393224 | tf_op jit(solution)/shard_map/ppermute | solution.py:22
  125.9 2.3 %collective-permute-done.29 = bf16[32,2048]{1,0:T(8,128)(2,1)S(1)} collective-permute-done((bf16[32,2048]{1,0:T(8,128)(2,1)S(1)}, bf16[32,2048]{1,0:T(8,128)(2,1)S(1)}, u32[]{:S(2)}, u32[]{:S(2)}) %collective-permute-start.29) | collective-permute-done | bytes 131104 | tf_op jit(solution)/shard_map/ppermute | solution.py:22
  130.9 2.4 %collective-permute-done.31 = bf16[32,2048]{1,0:T(8,128)(2,1)S(1)} collective-permute-done((bf16[32,2048]{1,0:T(8,128)(2,1)S(1)}, bf16[32,2048]{1,0:T(8,128)(2,1)S(1)}, u32[]{:S(2)}, u32[]{:S(2)}) %collective-permute-start.31) | collective-permute-done | bytes 131104 | tf_op jit(solution)/shard_map/ppermute | solution.py:22
  133.3 1.6 %collective-permute-start.34 = (bf16[32,2048]{1,0:T(8,128)(2,1)S(1)}, bf16[32,2048]{1,0:T(8,128)(2,1)S(1)}, u32[]{:S(2)}, u32[]{:S(2)}) collective-permute-start(bf16[32,2048]{1,0:T(8,128)(2,1)S(1)} %add_convert_fusion.5), channel_id=1, source_target_pairs={{0,2},{1,3},{2,0},{3,1},{4,6},{5,7},{6,4},{7,5},{8,10},{9,11},{10,... | collective-permute-start | bytes 393224 | tf_op jit(solution)/shard_map/ppermute | solution.py:22
  134.9 1.6 %collective-permute-done.30 = bf16[32,2048]{1,0:T(8,128)(2,1)S(1)} collective-permute-done((bf16[32,2048]{1,0:T(8,128)(2,1)S(1)}, bf16[32,2048]{1,0:T(8,128)(2,1)S(1)}, u32[]{:S(2)}, u32[]{:S(2)}) %collective-permute-start.30) | collective-permute-done | bytes 131104 | tf_op jit(solution)/shard_map/ppermute | solution.py:22
  136.5 1.5 %collective-permute-start.33 = (bf16[32,2048]{1,0:T(8,128)(2,1)S(1)}, bf16[32,2048]{1,0:T(8,128)(2,1)S(1)}, u32[]{:S(2)}, u32[]{:S(2)}) collective-permute-start(bf16[32,2048]{1,0:T(8,128)(2,1)S(1)} %add_convert_fusion.4), channel_id=1, source_target_pairs={{0,4},{1,5},{2,6},{3,7},{4,0},{5,1},{6,2},{7,3},{8,12},{9,13},{10,... | collective-permute-start | bytes 393224 | tf_op jit(solution)/shard_map/ppermute | solution.py:22
  138.3 2.0 %collective-permute-start.36 = (bf16[256,256]{1,0:T(8,128)(2,1)S(1)}, bf16[256,256]{1,0:T(8,128)(2,1)S(1)}, u32[]{:S(2)}, u32[]{:S(2)}) collective-permute-start(bf16[256,256]{1,0:T(8,128)(2,1)S(1)} %add_convert_fusion.2), channel_id=1, source_target_pairs={{0,8},{8,0},{16,24},{24,16},{1,9},{9,1},{17,25},{25,17},{2,10},{10... | collective-permute-start | bytes 393224 | tf_op jit(solution)/shard_map/ppermute | solution.py:22
  141.7 1.4 collective-permute-done.32
  143.1 1.4 collective-permute-done.36
  145.8 1.6 %maximum_convert_fusion = f32[256,2048]{1,0:T(8,128)} fusion(bf16[64,2048]{1,0:T(8,128)(2,1)S(1)} %get-tuple-element.216, bf16[64,2048]{1,0:T(8,128)(2,1)S(1)} %get-tuple-element.215, bf16[64,2048]{1,0:T(8,128)(2,1)S(1)} %get-tuple-element.240, bf16[64,2048]{1,0:T(8,128)(2,1)S(1)} %get-tuple-element.241), kind=kLoop, calls=%fused_computation.24 | loop fusion | flops 4194304 | bytes 3145728 | tf_op jit(solution)/shard_map/concatenate | solution.py:563
  (156 shorter events, 25.8 us)
Async XLA Ops:
  0.6 15.4 %copy-start = (bf16[1024,1024]{1,0:T(8,128)(2,1)S(1)}, bf16[1024,1024]{1,0:T(8,128)(2,1)}, u32[]{:S(2)}) copy-start(bf16[1024,1024]{1,0:T(8,128)(2,1)} %param.6) | copy-start | bytes 6291460
  0.6 9.1 %copy-start.19 = (bf16[256,2048]{1,0:T(8,128)(2,1)S(1)}, bf16[256,2048]{1,0:T(8,128)(2,1)}, u32[]{:S(2)}) copy-start(bf16[256,2048]{1,0:T(8,128)(2,1)} %param.10) | copy-start | bytes 3145732
  4.6 11.4 %copy-start.21 = (bf16[1024,256]{1,0:T(8,128)(2,1)S(1)}, bf16[1024,256]{1,0:T(8,128)(2,1)}, u32[]{:S(2)}) copy-start(bf16[1024,256]{1,0:T(8,128)(2,1)} %param.9) | copy-start | bytes 1572868
  4.6 12.9 %collective-permute-start.1 = (f16[128,1024]{1,0:T(8,128)(2,1)}, f16[128,1024]{1,0:T(8,128)(2,1)}, u32[]{:S(2)}, u32[]{:S(2)}) collective-permute-start(f16[128,1024]{1,0:T(8,128)(2,1)} %fusion.34), channel_id=1, source_target_pairs={{0,8},{8,0},{16,24},{24,16},{1,9},{9,1},{17,25},{25,17},{2,10},{10... | collective-permute-start | bytes 786440 | tf_op jit(solution)/shard_map/ppermute | solution.py:22
  8.5 9.0 %collective-permute-start.2 = (f32[8,2048]{1,0:T(8,128)S(1)}, f32[8,2048]{1,0:T(8,128)S(1)}, u32[]{:S(2)}, u32[]{:S(2)}) collective-permute-start(f32[8,2048]{1,0:T(8,128)S(1)} %slice.22), channel_id=1, source_target_pairs={{8,0},{16,8},{24,16},{9,1},{17,9},{25,17},{10,2},{18,10},{26,18},{... | collective-permute-start | bytes 196616 | tf_op jit(solution)/shard_map/ppermute | solution.py:454
  13.4 12.8 %collective-permute-start.4 = (f16[128,1024]{1,0:T(8,128)(2,1)}, f16[128,1024]{1,0:T(8,128)(2,1)}, u32[]{:S(2)}, u32[]{:S(2)}) collective-permute-start(f16[128,1024]{1,0:T(8,128)(2,1)} %fusion.37), channel_id=1, source_target_pairs={{0,8},{8,0},{16,24},{24,16},{1,9},{9,1},{17,25},{25,17},{2,10},{10... | collective-permute-start | bytes 786440 | tf_op jit(solution)/shard_map/ppermute | solution.py:22
  17.5 6.0 %collective-permute-start = (f16[512,256]{1,0:T(8,128)(2,1)}, f16[512,256]{1,0:T(8,128)(2,1)}, u32[]{:S(2)}, u32[]{:S(2)}) collective-permute-start(f16[512,256]{1,0:T(8,128)(2,1)} %dynamic-slice_convert_fusion), channel_id=1, source_target_pairs={{0,1},{1,0},{2,3},{3,2},{4,5},{5,4},{6,7},{7,6},{8,9},{9,8},{10,11... | collective-permute-start | bytes 786440 | tf_op jit(solution)/shard_map/ppermute | solution.py:22
  17.5 14.4 %slice-start = ((s8[8388608]{0:T(1024)(128)(4,1)}), s8[4194304]{0:T(1024)(128)(4,1)S(1)}, s32[]{:S(2)}) async-start(s8[8388608]{0:T(1024)(128)(4,1)} %bitcast.8), calls=%async_computation | async-start | bytes 8388608
  20.8 11.0 %slice-start.1 = ((s8[8388608]{0:T(1024)(128)(4,1)}), s8[4194304]{0:T(1024)(128)(4,1)S(1)}, s32[]{:S(2)}) async-start(s8[8388608]{0:T(1024)(128)(4,1)} %bitcast.8), calls=%async_computation.1 | async-start | bytes 8388608
  20.9 20.4 %collective-permute-start.6 = (f16[128,1024]{1,0:T(8,128)(2,1)S(1)}, f16[128,1024]{1,0:T(8,128)(2,1)S(1)}, u32[]{:S(2)}, u32[]{:S(2)}) collective-permute-start(f16[128,1024]{1,0:T(8,128)(2,1)S(1)} %get-tuple-element.112), channel_id=1, source_target_pairs={{0,16},{8,24},{16,0},{24,8},{1,17},{9,25},{17,1},{25,9},{2,18},{10... | collective-permute-start | bytes 786440 | tf_op jit(solution)/shard_map/ppermute | solution.py:22
  24.5 18.0 %copy-start.14 = (f32[512,256]{1,0:T(8,128)}, f32[512,256]{1,0:T(8,128)S(1)}, u32[]{:S(2)}) copy-start(f32[512,256]{1,0:T(8,128)S(1)} %convert_add_fusion.3) | copy-start | bytes 1572868
  24.6 5.7 %collective-permute-start.3 = (f16[256,256]{1,0:T(8,128)(2,1)S(1)}, f16[256,256]{1,0:T(8,128)(2,1)S(1)}, u32[]{:S(2)}, u32[]{:S(2)}) collective-permute-start(f16[256,256]{1,0:T(8,128)(2,1)S(1)} %dynamic-slice_convert_fusion.6), channel_id=1, source_target_pairs={{0,2},{1,3},{2,0},{3,1},{4,6},{5,7},{6,4},{7,5},{8,10},{9,11},{10,... | collective-permute-start | bytes 393224 | tf_op jit(solution)/shard_map/ppermute | solution.py:22
  29.1 17.8 %collective-permute-start.8 = (f16[128,1024]{1,0:T(8,128)(2,1)S(1)}, f16[128,1024]{1,0:T(8,128)(2,1)S(1)}, u32[]{:S(2)}, u32[]{:S(2)}) collective-permute-start(f16[128,1024]{1,0:T(8,128)(2,1)S(1)} %get-tuple-element.116), channel_id=1, source_target_pairs={{0,16},{8,24},{16,0},{24,8},{1,17},{9,25},{17,1},{25,9},{2,18},{10... | collective-permute-start | bytes 786440 | tf_op jit(solution)/shard_map/ppermute | solution.py:22
  30.3 12.2 %collective-permute-start.5 = (f16[256,256]{1,0:T(8,128)(2,1)S(1)}, f16[256,256]{1,0:T(8,128)(2,1)S(1)}, u32[]{:S(2)}, u32[]{:S(2)}) collective-permute-start(f16[256,256]{1,0:T(8,128)(2,1)S(1)} %fusion.49), channel_id=1, source_target_pairs={{0,4},{1,5},{2,6},{3,7},{4,0},{5,1},{6,2},{7,3},{8,12},{9,13},{10,... | collective-permute-start | bytes 393224 | tf_op jit(solution)/shard_map/ppermute | solution.py:22
  42.3 10.1 %collective-permute-start.10 = (bf16[128,1024]{1,0:T(8,128)(2,1)S(1)}, bf16[128,1024]{1,0:T(8,128)(2,1)S(1)}, u32[]{:S(2)}, u32[]{:S(2)}) collective-permute-start(bf16[128,1024]{1,0:T(8,128)(2,1)S(1)} %multiply_convert_fusion.1.own_ref), channel_id=1, source_target_pairs={{0,8},{8,0},{16,24},{24,16},{1,9},{9,1},{17,25},{25,17},{2,10},{10... | collective-permute-start | bytes 786440 | tf_op jit(solution)/shard_map/ppermute | solution.py:22
  42.6 6.1 %collective-permute-start.7 = (bf16[256,256]{1,0:T(8,128)(2,1)S(1)}, bf16[256,256]{1,0:T(8,128)(2,1)S(1)}, u32[]{:S(2)}, u32[]{:S(2)}) collective-permute-start(bf16[256,256]{1,0:T(8,128)(2,1)S(1)} %multiply_convert_fusion.3), channel_id=1, source_target_pairs={{0,2},{1,3},{2,0},{3,1},{4,6},{5,7},{6,4},{7,5},{8,10},{9,11},{10,... | collective-permute-start | bytes 393224 | tf_op jit(solution)/shard_map/ppermute | solution.py:22
  48.8 3.7 %collective-permute-start.9 = (bf16[512,256]{1,0:T(8,128)(2,1)S(1)}, bf16[512,256]{1,0:T(8,128)(2,1)S(1)}, u32[]{:S(2)}, u32[]{:S(2)}) collective-permute-start(bf16[512,256]{1,0:T(8,128)(2,1)S(1)} %pad_maximum_fusion.2), channel_id=1, source_target_pairs={{0,1},{1,0},{2,3},{3,2},{4,5},{5,4},{6,7},{7,6},{8,9},{9,8},{10,11... | collective-permute-start | bytes 786440 | tf_op jit(solution)/shard_map/ppermute | solution.py:22
  49.6 10.6 %collective-permute-start.11 = (bf16[128,1024]{1,0:T(8,128)(2,1)}, bf16[128,1024]{1,0:T(8,128)(2,1)}, u32[]{:S(2)}, u32[]{:S(2)}) collective-permute-start(bf16[128,1024]{1,0:T(8,128)(2,1)} %multiply_convert_fusion.own_ref), channel_id=1, source_target_pairs={{0,8},{8,0},{16,24},{24,16},{1,9},{9,1},{17,25},{25,17},{2,10},{10... | collective-permute-start | bytes 786440 | tf_op jit(solution)/shard_map/ppermute | solution.py:22
  68.5 8.3 %collective-permute-start.12 = (bf16[128,1024]{1,0:T(8,128)(2,1)S(1)}, bf16[128,1024]{1,0:T(8,128)(2,1)S(1)}, u32[]{:S(2)}, u32[]{:S(2)}) collective-permute-start(bf16[128,1024]{1,0:T(8,128)(2,1)S(1)} %get-tuple-element.141), channel_id=1, source_target_pairs={{0,8},{8,0},{16,24},{24,16},{1,9},{9,1},{17,25},{25,17},{2,10},{10... | collective-permute-start | bytes 786440 | tf_op jit(solution)/shard_map/ppermute | solution.py:22
  73.6 18.4 %copy-start.4 = (f32[128,1024]{1,0:T(8,128)S(1)}, f32[128,1024]{1,0:T(8,128)}, u32[]{:S(2)}) copy-start(f32[128,1024]{1,0:T(8,128)} %copy-done.3) | copy-start | bytes 1572868
  77.5 3.2 %collective-permute-start.14 = (f32[512,256]{1,0:T(8,128)}, f32[512,256]{1,0:T(8,128)S(1)}, u32[]{:S(2)}, u32[]{:S(2)}) collective-permute-start(f32[512,256]{1,0:T(8,128)} %constant_dynamic-slice_fusion.2), channel_id=1, source_target_pairs={{0,1},{1,0},{2,3},{3,2},{4,5},{5,4},{6,7},{7,6},{8,9},{9,8},{10,11... | collective-permute-start | bytes 1572872 | tf_op jit(solution)/shard_map/ppermute | solution.py:22
  77.5 14.5 %collective-permute-start.16 = (bf16[128,1024]{1,0:T(8,128)(2,1)}, bf16[128,1024]{1,0:T(8,128)(2,1)S(1)}, u32[]{:S(2)}, u32[]{:S(2)}) collective-permute-start(bf16[128,1024]{1,0:T(8,128)(2,1)} %copy-done.13), channel_id=1, source_target_pairs={{0,8},{8,0},{16,24},{24,16},{1,9},{9,1},{17,25},{25,17},{2,10},{10... | collective-permute-start | bytes 786440 | tf_op jit(solution)/shard_map/ppermute | solution.py:22
  77.8 16.0 %collective-permute-start.13 = (bf16[128,1024]{1,0:T(8,128)(2,1)S(1)}, bf16[128,1024]{1,0:T(8,128)(2,1)S(1)}, u32[]{:S(2)}, u32[]{:S(2)}) collective-permute-start(bf16[128,1024]{1,0:T(8,128)(2,1)S(1)} %fusion.46), channel_id=1, source_target_pairs={{0,16},{8,24},{16,0},{24,8},{1,17},{9,25},{17,1},{25,9},{2,18},{10... | collective-permute-start | bytes 786440 | tf_op jit(solution)/shard_map/ppermute | solution.py:22
  81.8 10.4 %collective-permute-start.15 = (bf16[256,256]{1,0:T(8,128)(2,1)S(1)}, bf16[256,256]{1,0:T(8,128)(2,1)S(1)}, u32[]{:S(2)}, u32[]{:S(2)}) collective-permute-start(bf16[256,256]{1,0:T(8,128)(2,1)S(1)} %dynamic-slice_convert_fusion.5), channel_id=1, source_target_pairs={{0,2},{1,3},{2,0},{3,1},{4,6},{5,7},{6,4},{7,5},{8,10},{9,11},{10,... | collective-permute-start | bytes 393224 | tf_op jit(solution)/shard_map/ppermute | solution.py:22
  92.0 8.8 %copy-start.15 = (f32[512,256]{1,0:T(8,128)S(1)}, f32[512,256]{1,0:T(8,128)}, u32[]{:S(2)}) copy-start(f32[512,256]{1,0:T(8,128)} %copy-done.14) | copy-start | bytes 1572868
  92.1 8.8 %copy-start.18 = (f16[256,256]{1,0:T(8,128)(2,1)S(1)}, f16[256,256]{1,0:T(8,128)(2,1)}, u32[]{:S(2)}) copy-start(f16[256,256]{1,0:T(8,128)(2,1)} %copy-done.17) | copy-start | bytes 393220
  92.1 13.7 %collective-permute-start.20 = (bf16[128,1024]{1,0:T(8,128)(2,1)S(1)}, bf16[128,1024]{1,0:T(8,128)(2,1)S(1)}, u32[]{:S(2)}, u32[]{:S(2)}) collective-permute-start(bf16[128,1024]{1,0:T(8,128)(2,1)S(1)} %fusion.47), channel_id=1, source_target_pairs={{0,16},{8,24},{16,0},{24,8},{1,17},{9,25},{17,1},{25,9},{2,18},{10... | collective-permute-start | bytes 786440 | tf_op jit(solution)/shard_map/ppermute | solution.py:22
  92.3 8.6 %collective-permute-start.18 = (bf16[256,256]{1,0:T(8,128)(2,1)S(1)}, bf16[256,256]{1,0:T(8,128)(2,1)S(1)}, u32[]{:S(2)}, u32[]{:S(2)}) collective-permute-start(bf16[256,256]{1,0:T(8,128)(2,1)S(1)} %fusion.48), channel_id=1, source_target_pairs={{0,4},{1,5},{2,6},{3,7},{4,0},{5,1},{6,2},{7,3},{8,12},{9,13},{10,... | collective-permute-start | bytes 393224 | tf_op jit(solution)/shard_map/ppermute | solution.py:22
  95.1 13.2 %collective-permute-start.17 = (bf16[128,1024]{1,0:T(8,128)(2,1)S(1)}, bf16[128,1024]{1,0:T(8,128)(2,1)S(1)}, u32[]{:S(2)}, u32[]{:S(2)}) collective-permute-start(bf16[128,1024]{1,0:T(8,128)(2,1)S(1)} %add_convert_fusion.1), channel_id=1, source_target_pairs={{0,8},{8,0},{16,24},{24,16},{1,9},{9,1},{17,25},{25,17},{2,10},{10... | collective-permute-start | bytes 786440 | tf_op jit(solution)/shard_map/ppermute | solution.py:22
  101.1 5.0 %collective-permute-start.19 = (bf16[256,256]{1,0:T(8,128)(2,1)S(1)}, bf16[256,256]{1,0:T(8,128)(2,1)S(1)}, u32[]{:S(2)}, u32[]{:S(2)}) collective-permute-start(bf16[256,256]{1,0:T(8,128)(2,1)S(1)} %multiply_convert_fusion.2), channel_id=1, source_target_pairs={{0,2},{1,3},{2,0},{3,1},{4,6},{5,7},{6,4},{7,5},{8,10},{9,11},{10,... | collective-permute-start | bytes 393224 | tf_op jit(solution)/shard_map/ppermute | solution.py:22
  106.0 10.9 %collective-permute-start.21 = (bf16[128,1024]{1,0:T(8,128)(2,1)S(1)}, bf16[128,1024]{1,0:T(8,128)(2,1)S(1)}, u32[]{:S(2)}, u32[]{:S(2)}) collective-permute-start(bf16[128,1024]{1,0:T(8,128)(2,1)S(1)} %add_convert_fusion), channel_id=1, source_target_pairs={{0,8},{8,0},{16,24},{24,16},{1,9},{9,1},{17,25},{25,17},{2,10},{10... | collective-permute-start | bytes 786440 | tf_op jit(solution)/shard_map/ppermute | solution.py:22
  106.2 6.0 %collective-permute-start.22 = (bf16[512,256]{1,0:T(8,128)(2,1)S(1)}, bf16[512,256]{1,0:T(8,128)(2,1)S(1)}, u32[]{:S(2)}, u32[]{:S(2)}) collective-permute-start(bf16[512,256]{1,0:T(8,128)(2,1)S(1)} %pad_maximum_fusion.3), channel_id=1, source_target_pairs={{0,1},{1,0},{2,3},{3,2},{4,5},{5,4},{6,7},{7,6},{8,9},{9,8},{10,11... | collective-permute-start | bytes 786440 | tf_op jit(solution)/shard_map/ppermute | solution.py:22
  113.2 6.8 %collective-permute-start.23 = (bf16[256,256]{1,0:T(8,128)(2,1)S(1)}, bf16[256,256]{1,0:T(8,128)(2,1)S(1)}, u32[]{:S(2)}, u32[]{:S(2)}) collective-permute-start(bf16[256,256]{1,0:T(8,128)(2,1)S(1)} %dynamic-slice_convert_fusion.3), channel_id=1, source_target_pairs={{0,8},{8,0},{16,24},{24,16},{1,9},{9,1},{17,25},{25,17},{2,10},{10... | collective-permute-start | bytes 393224 | tf_op jit(solution)/shard_map/ppermute | solution.py:22
  113.3 7.8 %collective-permute-start.27 = (bf16[256,256]{1,0:T(8,128)(2,1)S(1)}, bf16[256,256]{1,0:T(8,128)(2,1)S(1)}, u32[]{:S(2)}, u32[]{:S(2)}) collective-permute-start(bf16[256,256]{1,0:T(8,128)(2,1)S(1)} %dynamic-slice_convert_fusion.4), channel_id=1, source_target_pairs={{0,8},{8,0},{16,24},{24,16},{1,9},{9,1},{17,25},{25,17},{2,10},{10... | collective-permute-start | bytes 393224 | tf_op jit(solution)/shard_map/ppermute | solution.py:22
  118.5 4.6 %collective-permute-start.26 = (f32[64,2048]{1,0:T(8,128)S(1)}, f32[64,2048]{1,0:T(8,128)S(1)}, u32[]{:S(2)}, u32[]{:S(2)}) collective-permute-start(f32[64,2048]{1,0:T(8,128)S(1)} %constant_dynamic-slice_fusion), channel_id=1, source_target_pairs={{0,1},{1,0},{2,3},{3,2},{4,5},{5,4},{6,7},{7,6},{8,9},{9,8},{10,11... | collective-permute-start | bytes 1572872 | tf_op jit(solution)/shard_map/ppermute | solution.py:22
  118.6 6.2 %collective-permute-start.25 = (f32[64,2048]{1,0:T(8,128)S(1)}, f32[64,2048]{1,0:T(8,128)S(1)}, u32[]{:S(2)}, u32[]{:S(2)}) collective-permute-start(f32[64,2048]{1,0:T(8,128)S(1)} %constant_dynamic-slice_fusion.1), channel_id=1, source_target_pairs={{0,1},{1,0},{2,3},{3,2},{4,5},{5,4},{6,7},{7,6},{8,9},{9,8},{10,11... | collective-permute-start | bytes 1572872 | tf_op jit(solution)/shard_map/ppermute | solution.py:22
  120.0 18.0 %collective-permute-start.24 = (bf16[256,256]{1,0:T(8,128)(2,1)S(1)}, bf16[256,256]{1,0:T(8,128)(2,1)S(1)}, u32[]{:S(2)}, u32[]{:S(2)}) collective-permute-start(bf16[256,256]{1,0:T(8,128)(2,1)S(1)} %add_convert_fusion.9), channel_id=1, source_target_pairs={{0,16},{8,24},{16,0},{24,8},{1,17},{9,25},{17,1},{25,9},{2,18},{10... | collective-permute-start | bytes 393224 | tf_op jit(solution)/shard_map/ppermute | solution.py:22
  121.1 17.2 %collective-permute-start.35 = (bf16[256,256]{1,0:T(8,128)(2,1)S(1)}, bf16[256,256]{1,0:T(8,128)(2,1)S(1)}, u32[]{:S(2)}, u32[]{:S(2)}) collective-permute-start(bf16[256,256]{1,0:T(8,128)(2,1)S(1)} %add_convert_fusion.8), channel_id=1, source_target_pairs={{0,16},{8,24},{16,0},{24,8},{1,17},{9,25},{17,1},{25,9},{2,18},{10... | collective-permute-start | bytes 393224 | tf_op jit(solution)/shard_map/ppermute | solution.py:22
  123.2 5.0 %collective-permute-start.29 = (bf16[32,2048]{1,0:T(8,128)(2,1)S(1)}, bf16[32,2048]{1,0:T(8,128)(2,1)S(1)}, u32[]{:S(2)}, u32[]{:S(2)}) collective-permute-start(bf16[32,2048]{1,0:T(8,128)(2,1)S(1)} %dynamic-slice_convert_fusion.2), channel_id=1, source_target_pairs={{0,2},{1,3},{2,0},{3,1},{4,6},{5,7},{6,4},{7,5},{8,10},{9,11},{10,... | collective-permute-start | bytes 393224 | tf_op jit(solution)/shard_map/ppermute | solution.py:22
  124.9 5.4 %collective-permute-start.28 = (bf16[32,2048]{1,0:T(8,128)(2,1)S(1)}, bf16[32,2048]{1,0:T(8,128)(2,1)S(1)}, u32[]{:S(2)}, u32[]{:S(2)}) collective-permute-start(bf16[32,2048]{1,0:T(8,128)(2,1)S(1)} %dynamic-slice_convert_fusion.1), channel_id=1, source_target_pairs={{0,4},{1,5},{2,6},{3,7},{4,0},{5,1},{6,2},{7,3},{8,12},{9,13},{10,... | collective-permute-start | bytes 393224 | tf_op jit(solution)/shard_map/ppermute | solution.py:22
  128.3 5.0 %collective-permute-start.31 = (bf16[32,2048]{1,0:T(8,128)(2,1)S(1)}, bf16[32,2048]{1,0:T(8,128)(2,1)S(1)}, u32[]{:S(2)}, u32[]{:S(2)}) collective-permute-start(bf16[32,2048]{1,0:T(8,128)(2,1)S(1)} %add_convert_fusion.7), channel_id=1, source_target_pairs={{0,4},{1,5},{2,6},{3,7},{4,0},{5,1},{6,2},{7,3},{8,12},{9,13},{10,... | collective-permute-start | bytes 393224 | tf_op jit(solution)/shard_map/ppermute | solution.py:22
  130.3 6.2 %collective-permute-start.30 = (bf16[32,2048]{1,0:T(8,128)(2,1)S(1)}, bf16[32,2048]{1,0:T(8,128)(2,1)S(1)}, u32[]{:S(2)}, u32[]{:S(2)}) collective-permute-start(bf16[32,2048]{1,0:T(8,128)(2,1)S(1)} %add_convert_fusion.6), channel_id=1, source_target_pairs={{0,2},{1,3},{2,0},{3,1},{4,6},{5,7},{6,4},{7,5},{8,10},{9,11},{10,... | collective-permute-start | bytes 393224 | tf_op jit(solution)/shard_map/ppermute | solution.py:22
  133.3 6.9 %collective-permute-start.34 = (bf16[32,2048]{1,0:T(8,128)(2,1)S(1)}, bf16[32,2048]{1,0:T(8,128)(2,1)S(1)}, u32[]{:S(2)}, u32[]{:S(2)}) collective-permute-start(bf16[32,2048]{1,0:T(8,128)(2,1)S(1)} %add_convert_fusion.5), channel_id=1, source_target_pairs={{0,2},{1,3},{2,0},{3,1},{4,6},{5,7},{6,4},{7,5},{8,10},{9,11},{10,... | collective-permute-start | bytes 393224 | tf_op jit(solution)/shard_map/ppermute | solution.py:22
  136.5 5.0 %collective-permute-start.33 = (bf16[32,2048]{1,0:T(8,128)(2,1)S(1)}, bf16[32,2048]{1,0:T(8,128)(2,1)S(1)}, u32[]{:S(2)}, u32[]{:S(2)}) collective-permute-start(bf16[32,2048]{1,0:T(8,128)(2,1)S(1)} %add_convert_fusion.4), channel_id=1, source_target_pairs={{0,4},{1,5},{2,6},{3,7},{4,0},{5,1},{6,2},{7,3},{8,12},{9,13},{10,... | collective-permute-start | bytes 393224 | tf_op jit(solution)/shard_map/ppermute | solution.py:22
  138.1 5.0 %collective-permute-start.32 = (bf16[256,256]{1,0:T(8,128)(2,1)S(1)}, bf16[256,256]{1,0:T(8,128)(2,1)S(1)}, u32[]{:S(2)}, u32[]{:S(2)}) collective-permute-start(bf16[256,256]{1,0:T(8,128)(2,1)S(1)} %add_convert_fusion.3), channel_id=1, source_target_pairs={{0,8},{8,0},{16,24},{24,16},{1,9},{9,1},{17,25},{25,17},{2,10},{10... | collective-permute-start | bytes 393224 | tf_op jit(solution)/shard_map/ppermute | solution.py:22
  138.3 6.2 %collective-permute-start.36 = (bf16[256,256]{1,0:T(8,128)(2,1)S(1)}, bf16[256,256]{1,0:T(8,128)(2,1)S(1)}, u32[]{:S(2)}, u32[]{:S(2)}) collective-permute-start(bf16[256,256]{1,0:T(8,128)(2,1)S(1)} %add_convert_fusion.2), channel_id=1, source_target_pairs={{0,8},{8,0},{16,24},{24,16},{1,9},{9,1},{17,25},{25,17},{2,10},{10... | collective-permute-start | bytes 393224 | tf_op jit(solution)/shard_map/ppermute | solution.py:22
  140.3 5.3 %collective-permute-start.37 = (bf16[64,2048]{1,0:T(8,128)(2,1)S(1)}, bf16[64,2048]{1,0:T(8,128)(2,1)S(1)}, u32[]{:S(2)}, u32[]{:S(2)}) collective-permute-start(bf16[64,2048]{1,0:T(8,128)(2,1)S(1)} %pad_maximum_fusion.4), channel_id=1, source_target_pairs={{0,1},{1,0},{2,3},{3,2},{4,5},{5,4},{6,7},{7,6},{8,9},{9,8},{10,11... | collective-permute-start | bytes 786440 | tf_op jit(solution)/shard_map/ppermute | solution.py:22
  141.6 4.0 %collective-permute-start.38 = (bf16[64,2048]{1,0:T(8,128)(2,1)S(1)}, bf16[64,2048]{1,0:T(8,128)(2,1)S(1)}, u32[]{:S(2)}, u32[]{:S(2)}) collective-permute-start(bf16[64,2048]{1,0:T(8,128)(2,1)S(1)} %pad_maximum_fusion.5), channel_id=1, source_target_pairs={{0,1},{1,0},{2,3},{3,2},{4,5},{5,4},{6,7},{7,6},{8,9},{9,8},{10,11... | collective-permute-start | bytes 786440 | tf_op jit(solution)/shard_map/ppermute | solution.py:22
  (19 other events, 69.0 us)
